TPU v7x, 32 devices: a whole 2x2x4 slice. The times are simulated.
32 devices in a mesh: section: 4 (over x, core), seq: 2 (over y), dp: 4 (over z).
Axes of the slice: x: 2, y: 2, z: 4, core: 2. Of those that a mesh axis runs over, the one named last changes fastest.
Arguments:
- tile_feats: bfloat16 [4, 1024, 1536], P('dp', 'seq', 'section'), may hold values from -6 to 6
- tile_gain: float32 [1536], replicated, may hold values from 0.25 to 1.75
- w_gate: bfloat16 [1536, 4096], P(('seq', 'dp'), 'section'), may hold values from -0.15625 to 0.15625
- w_up: bfloat16 [1536, 4096], P(('seq', 'dp'), 'section'), may hold values from -0.15625 to 0.15625
- w_down: bfloat16 [4096, 1536], P('section', ('seq', 'dp')), may hold values from -0.09375 to 0.09375
- w_proj: bfloat16 [1536, 768], P('section'), may hold values from -0.15625 to 0.15625
- slide_gain: float32 [768], replicated, may hold values from 0.25 to 1.75
- w_qkv: bfloat16 [3, 768, 768], P(None, None, 'section'), may hold values from -0.7647408 to 0.7647408
- w_out: bfloat16 [768, 768], P('section'), may hold values from -0.21875 to 0.21875
- lengths: int32 [4, 3], P('dp'), may hold values from 1 to 768, 1024 in all within a row
- seg_len: int32 [16], P('section'), may hold values from 512 to 1024
- rate: int32 [16], P('section'), may hold values from 1 to 4
Outputs:
- slide_out: bfloat16 [4, 1024, 768], P('dp', 'seq', 'section')
Inputs may be any that keep to these rules, and one draw needn't show every extreme that they name: Each row of lengths sums to 1024, and one slide of each pack has 768 tiles.
All inputs are finite; a program needn't handle non-finite values.
Results may differ from a plain program's by a relative error of at most 0.0087.
Values may be sent and summed in bfloat16 or wider, within the bound.
No kernel may reach another device: no remote copies, remote signals or barrier semaphores. Data moves between devices by JAX's collectives and lax.ppermute only.
A program may use at most 192 MiB of HBM per device.

v0:
```python
import math

import jax
import jax.numpy as jnp
from jax import lax
from jax.sharding import PartitionSpec as P


def layer_norm(rows, gain):
    mean = jnp.mean(rows, axis=-1, keepdims=True)
    centered = rows - mean
    var = jnp.mean(centered * centered, axis=-1, keepdims=True)
    return centered * lax.rsqrt(var + 1e-06) * gain


def slide_place(lengths_row, index):
    ends = jnp.cumsum(lengths_row, dtype=jnp.int32)
    after = index[:, None] >= ends[None, :]
    slide = jnp.sum(after.astype(jnp.int32), axis=1, dtype=jnp.int32)
    before = jnp.sum(jnp.where(after, lengths_row[None, :], 0), axis=1, dtype=jnp.int32)
    return (slide, index - before)


def allowed(q_slide, q_pos, q_idx, k_slide, k_pos, k_idx, seg, rate, heads):
    width = seg[:, None, None]
    step = rate[:, None, None]
    offset = (heads % rate)[:, None, None]
    same = (q_slide[:, None] == k_slide[None, :])[None]
    block = q_pos[None, :, None] // width == k_pos[None, None, :] // width
    pick = (k_pos[None, None, :] % step == offset) | (q_idx[:, None] == k_idx[None, :])[None]
    return same & block & pick


def per_device(
    tile_feats,
    tile_gain,
    w_gate,
    w_up,
    w_down,
    w_proj,
    slide_gain,
    w_qkv,
    w_out,
    lengths,
    seg_len,
    rate,
):
    mine = tile_feats[0]
    tok_rows = mine.shape[0]
    whole = lax.all_gather(mine, "section", axis=1, tiled=True)
    normed = layer_norm(whole.astype(jnp.float32), tile_gain).astype(jnp.bfloat16)
    gate = jnp.dot(
        normed,
        lax.all_gather(w_gate, ("seq", "dp"), axis=0, tiled=True),
        preferred_element_type=jnp.float32,
    )
    up = jnp.dot(
        normed,
        lax.all_gather(w_up, ("seq", "dp"), axis=0, tiled=True),
        preferred_element_type=jnp.float32,
    )
    hidden = (jax.nn.silu(gate) * up).astype(jnp.bfloat16)
    terms = jnp.dot(
        hidden,
        lax.all_gather(w_down, ("seq", "dp"), axis=1, tiled=True),
        preferred_element_type=jnp.float32,
    )
    tile_part = lax.psum_scatter(terms, "section", scatter_dimension=1, tiled=True)
    tile_out = (mine.astype(jnp.float32) + tile_part).astype(jnp.bfloat16)
    part_emb = jnp.dot(tile_out, w_proj, preferred_element_type=jnp.float32)
    share_width = w_qkv.shape[2]
    section_at = lax.axis_index("section")
    emb = lax.psum(part_emb, "section")
    slide_normed = layer_norm(emb, slide_gain).astype(jnp.bfloat16)
    emb_mine = lax.dynamic_slice_in_dim(emb, section_at * share_width, share_width, 1)
    projected = jnp.einsum(
        "rd,cde->cre", slide_normed, w_qkv, preferred_element_type=jnp.float32
    ).astype(jnp.bfloat16)
    local_heads = seg_len.shape[0]
    head_size = share_width // local_heads
    query = projected[0].reshape(tok_rows, local_heads, head_size)
    heads = section_at * local_heads + jnp.arange(local_heads, dtype=jnp.int32)
    lengths_row = lengths[0]
    q_idx = lax.axis_index("seq") * tok_rows + jnp.arange(tok_rows, dtype=jnp.int32)
    q_slide, q_pos = slide_place(lengths_row, q_idx)
    scale = 1.0 / math.sqrt(head_size)
    key_piece = lax.all_gather(projected[1], "seq", axis=0, tiled=True)
    value_piece = lax.all_gather(projected[2], "seq", axis=0, tiled=True)
    count = key_piece.shape[0]
    k_idx = jnp.arange(count, dtype=jnp.int32)
    k_slide, k_pos = slide_place(lengths_row, k_idx)
    mask = allowed(q_slide, q_pos, q_idx, k_slide, k_pos, k_idx, seg_len, rate, heads)
    running = jnp.full((local_heads, tok_rows), -1e30, jnp.float32)
    scores = (
        jnp.einsum(
            "qhd,khd->hqk",
            query,
            key_piece.reshape(count, local_heads, head_size),
            preferred_element_type=jnp.float32,
        )
        * scale
    )
    scores = jnp.where(mask, scores, -1e30)
    fresh = jnp.maximum(running, jnp.max(scores, axis=-1))
    weights = jnp.where(mask, jnp.exp(scores - fresh[..., None]), 0.0)
    total = jnp.sum(weights, axis=-1)
    values = value_piece.reshape(count, local_heads, head_size).astype(jnp.float32)
    acc = jnp.einsum("hqk,khd->hqd", weights, values)
    running, total, acc = (fresh, total, acc)
    att = (
        (acc / total[..., None])
        .transpose(1, 0, 2)
        .reshape(tok_rows, share_width)
        .astype(jnp.bfloat16)
    )
    out_part = jnp.dot(att, w_out, preferred_element_type=jnp.float32)
    out_share = lax.psum_scatter(out_part, "section", scatter_dimension=1, tiled=True)
    return (emb_mine + out_share).astype(jnp.bfloat16).reshape(1, tok_rows, share_width)


def solution(mesh):
    placed = (
        P("dp", "seq", "section"),
        P(),
        P(("seq", "dp"), "section"),
        P(("seq", "dp"), "section"),
        P("section", ("seq", "dp")),
        P("section", None),
        P(),
        P(None, None, "section"),
        P("section", None),
        P("dp", None),
        P("section"),
        P("section"),
    )
    return jax.shard_map(
        per_device, mesh=mesh, in_specs=placed, out_specs=P("dp", "seq", "section"), check_vma=False
    )
```

profile of v0, /device:TPU:0, one launch (start us, length us, event | category | flops | bytes accessed | tf_op | source)
XLA Modules:
  0.0 375.5 jit_solution(13758225857818873409)
XLA Ops:
  6.5 0.7 all-gather.14.cloned.1.call-update
  7.3 0.0 all-gather.8.cloned.1.call-start
  7.3 0.7 all-gather.8.cloned.1.call-update
  8.0 0.0 all-gather.10.cloned.1.call-start
  8.1 0.7 all-gather.10.cloned.1.call-update
  8.8 0.0 all-gather.12.cloned.1.call-start
  8.8 0.5 all-gather.12.cloned.1.call-update
  9.3 0.0 reduce-scatter.5.cloned.1.call-start
  9.4 21.9 %all-gather.14.cloned.1.call-done = bf16[1,512,1536]{2,1,0:T(8,128)(2,1)} async-done(((bf16[1,512,384]{2,1,0:T(8,128)(2,1)}), bf16[1,512,1536]{2,1,0:T(8,128)(2,1)}) %all-gather.14.cloned.1.call-update) | async-done | bytes 1572880 | tf_op jit(solution)/shard_map/all_gather | solution.py:50
  31.3 1.8 convert_reduce_fusion
  33.1 0.1 copy-done.2
  33.2 0.5 fusion.10
  33.7 60.1 %all-gather.8.cloned.1.call-done = bf16[1536,1024]{1,0:T(8,128)(2,1)} async-done(((bf16[192,1024]{1,0:T(8,128)(2,1)}), bf16[1536,1024]{1,0:T(8,128)(2,1)}) %all-gather.8.cloned.1.call-update) | async-done | bytes 3145744 | tf_op jit(solution)/shard_map/all_gather | solution.py:54
  93.9 5.1 %fusion.41 = f32[512,1024]{1,0:T(8,128)} fusion(bf16[1536,1024]{1,0:T(8,128)(2,1)} %all-gather.8.cloned.1.call-done, bf16[1,512,1536]{2,1,0:T(8,128)(2,1)S(1)} %copy-done.2, f32[1536]{0:T(1024)S(1)} %copy-done.10, f32[512]{0:T(512)S(1)} %add_rsqrt_fusion.1, f32[512]{0:T(512)S(1)} %broadcast_multiply_fusion.1), kind=kOutput, calls=%fused_computation.75 | convolution fusion | flops 1614544896 | bytes 6825984 | tf_op jit(solution)/shard_map/dot_general | solution.py:52
  98.9 56.1 %all-gather.10.cloned.1.call-done = bf16[1536,1024]{1,0:T(8,128)(2,1)} async-done(((bf16[192,1024]{1,0:T(8,128)(2,1)}), bf16[1536,1024]{1,0:T(8,128)(2,1)}) %all-gather.10.cloned.1.call-update) | async-done | bytes 3145744 | tf_op jit(solution)/shard_map/all_gather | solution.py:59
  155.1 61.1 %all-gather.12.cloned.1.call-done = bf16[1024,1536]{0,1:T(8,128)(2,1)} async-done(((bf16[1024,192]{0,1:T(8,128)(2,1)}), bf16[1024,1536]{0,1:T(8,128)(2,1)}) %all-gather.12.cloned.1.call-update) | async-done | bytes 3145744 | tf_op jit(solution)/shard_map/all_gather | solution.py:65
  216.1 8.7 %fusion.16 = f32[512,1536]{1,0:T(8,128)} fusion(bf16[1024,1536]{0,1:T(8,128)(2,1)} %all-gather.12.cloned.1.call-done, f32[512,1024]{1,0:T(8,128)} %fusion.41, bf16[1536,1024]{1,0:T(8,128)(2,1)} %all-gather.10.cloned.1.call-done, bf16[1,512,1536]{2,1,0:T(8,128)(2,1)S(1)} %copy-done.2, f32[1536]{0:T(1024)S(1)} %copy-done.10, f32[512]{0:T(512)S(1)} %add_rsqrt_fusion.1, ...), kind=kOutput, calls=%fused_computation.27 | convolution fusion | flops 3228303360 | bytes 13117440 | tf_op jit(solution)/shard_map/dot_general | solution.py:63
  224.9 0.0 reduce-scatter.5.cloned.1.call-update
  224.9 0.0 all-reduce.2.cloned.1.call-start
  224.9 0.6 copy-done.7
  225.5 0.2 reduce-window.8
  225.7 0.1 convert_reduce_fusion.1
  225.8 0.1 fusion.30
  225.9 0.1 compare_select_fusion.1
  226.0 0.4 fusion.26
  226.5 35.1 %reduce-scatter.5.cloned.1.call-done = f32[512,384]{1,0:T(8,128)} async-done(((f32[512,1536]{1,0:T(8,128)}), f32[512,384]{1,0:T(8,128)}) %reduce-scatter.5.cloned.1.call-update) | async-done | bytes 786448 | tf_op jit(solution)/shard_map/reduce_scatter | solution.py:68
  261.6 2.9 fusion.22
  264.5 0.0 all-reduce.2.cloned.1.call-update
  264.5 0.0 reduce-scatter.7.cloned.1.call-start
  264.6 0.3 add_select_fusion.1
  264.9 0.4 add_select_fusion
  265.3 0.7 iota_compare_fusion
  266.0 41.5 %all-reduce.2.cloned.1.call-done = f32[512,768]{1,0:T(8,128)} async-done(((f32[512,768]{1,0:T(8,128)}), f32[512,768]{1,0:T(8,128)}) %all-reduce.2.cloned.1.call-update) | async-done | bytes 1572880 | tf_op jit(solution)/shard_map/psum | solution.py:73
  307.5 1.7 reduce_sum.87
  309.2 0.2 copy-done.1
  309.4 0.3 multiply_reduce_fusion
  309.7 0.8 fusion.17
  310.5 0.1 convert_bitcast_fusion.1
  310.7 7.4 %all-gather.1 = bf16[1,1024,192]{1,2,0:T(8,128)(2,1)S(1)} all-gather(bf16[1,512,192]{1,2,0:T(8,128)(2,1)S(1)} %get-tuple-element.11), channel_id=3, replica_groups=mesh['section'=4,'seq'=2,'dp'=4] {'seq'}, dimensions={1}, use_global_device_ids=true | all-gather | bytes 589824 | tf_op jit(solution)/shard_map/all_gather | solution.py:87
  318.0 3.3 fusion
  321.3 6.3 %all-gather.2 = bf16[1,1024,192]{1,2,0:T(8,128)(2,1)S(1)} all-gather(bf16[1,512,192]{1,2,0:T(8,128)(2,1)S(1)} %get-tuple-element.12), channel_id=4, replica_groups=mesh['section'=4,'seq'=2,'dp'=4] {'seq'}, dimensions={1}, use_global_device_ids=true | all-gather | bytes 589824 | tf_op jit(solution)/shard_map/all_gather | solution.py:88
  327.7 4.4 %fusion.1 = f32[4,512]{1,0:T(4,128)S(1)} fusion(f32[4,512,1024]{2,1,0:T(8,128)S(1)} %get-tuple-element.19, f32[4,512]{1,0:T(4,128)S(1)} %broadcast_maximum_fusion, pred[512,1024]{1,0:T(8,128)(4,1)S(1)} %get-tuple-element.20, pred[4,1024]{1,0:T(4,128)(4,1)S(1)} %fusion.26, s32[4,1024]{1,0:T(4,128)S(1)} %add_select_fusion, s32[4,512]{1,0:T(4,128)S(1)} %add_select_fusion.1, ...), kind=kLoop, calls=%fused_computation.4 | loop fusion | flops 18872320 | bytes 9482240 | tf_op jit(solution)/shard_map/reduce_sum | solution.py:106
  332.1 3.8 %fusion.15 = bf16[512,4,48]{0,2,1:T(8,128)(2,1)S(1)} fusion(bf16[1024,4,48]{0,2,1:T(8,128)(2,1)S(1)} %bitcast.61, f32[4,512,1024]{2,1,0:T(8,128)S(1)} %get-tuple-element.19, f32[4,512]{1,0:T(4,128)S(1)} %broadcast_maximum_fusion, f32[512,4]{0,1:T(4,128)S(1)} %bitcast.65, s32[4,1024]{1,0:T(4,128)S(1)} %add_select_fusion, s32[4,512]{1,0:T(4,128)S(1)} %add_select_fusion.1, ...), kind=kOutput, calls=%fused_computation.26 | convolution fusion | flops 218300416 | bytes 10072064 | tf_op jit(solution)/shard_map/hqk,khd->hqd/dot_general | solution.py:108
  335.9 1.6 convolution_bitcast_fusion
  337.5 28.9 %reduce-scatter.7.cloned.1.call-done = f32[192,512]{1,0:T(8,128)} async-done(((f32[768,512]{1,0:T(8,128)}), f32[192,512]{1,0:T(8,128)}) %reduce-scatter.7.cloned.1.call-update) | async-done | bytes 393232
  366.4 1.2 copy.21
  367.6 0.2 fusion.25
  367.8 0.8 copy.18
  (32 shorter events, 0.2 us)
Async XLA Ops:
  6.5 303.2 %copy-start = (bf16[3,768,192]{1,2,0:T(8,128)(2,1)S(1)}, bf16[3,768,192]{1,2,0:T(8,128)(2,1)}, u32[]{:S(2)}) copy-start(bf16[3,768,192]{1,2,0:T(8,128)(2,1)} %param.19) | copy-start | bytes 2654212
  6.5 24.8 %all-gather.14.cloned.1.call-start = ((), (), s32[]{:S(2)}) async-start(), calls=%async_computation.7 | async-start | bytes 1966080 | tf_op jit(solution)/shard_map/all_gather | solution.py:50
  7.3 86.6 %copy-start.10 = (f32[1536]{0:T(1024)S(1)}, f32[1536]{0:T(1024)}, u32[]{:S(2)}) copy-start(f32[1536]{0:T(1024)} %param.13) | copy-start | bytes 18436
  7.3 86.6 %all-gather.8.cloned.1.call-start = ((), (), s32[]{:S(2)}) async-start(), calls=%async_computation.2 | async-start | bytes 3538944 | tf_op jit(solution)/shard_map/all_gather | solution.py:54
  8.0 147.1 %all-gather.10.cloned.1.call-start = ((), (), s32[]{:S(2)}) async-start(), calls=%async_computation.3 | async-start | bytes 3538944 | tf_op jit(solution)/shard_map/all_gather | solution.py:59
  8.8 207.4 %all-gather.12.cloned.1.call-start = ((), (), s32[]{:S(2)}) async-start(), calls=%async_computation.4 | async-start | bytes 3538944 | tf_op jit(solution)/shard_map/all_gather | solution.py:65
  9.3 252.3 %reduce-scatter.5.cloned.1.call-start = ((), (), s32[]{:S(2)}) async-start(), calls=%async_computation.5 | async-start | bytes 3932160 | tf_op jit(solution)/shard_map/reduce_scatter | solution.py:68
  31.3 1.9 copy-start.2
  224.9 0.7 copy-start.7
  224.9 1.0 copy-start.9
  224.9 36.8 %copy-start.3 = (bf16[1,512,384]{2,1,0:T(8,128)(2,1)S(1)}, bf16[1,512,384]{2,1,0:T(8,128)(2,1)}, u32[]{:S(2)}) copy-start(bf16[1,512,384]{2,1,0:T(8,128)(2,1)} %param.12) | copy-start | bytes 1179652
  224.9 36.8 %copy-start.4 = (bf16[384,768]{1,0:T(8,128)(2,1)S(1)}, bf16[384,768]{1,0:T(8,128)(2,1)}, u32[]{:S(2)}) copy-start(bf16[384,768]{1,0:T(8,128)(2,1)} %param.17) | copy-start | bytes 1769476
  224.9 82.6 %all-reduce.2.cloned.1.call-start = ((), (), s32[]{:S(2)}) async-start(), calls=%async_computation.6 | async-start | bytes 3145728 | tf_op jit(solution)/shard_map/psum | solution.py:73
  226.5 38.1 %copy-start.8 = (s32[4]{0:T(128)S(1)}, s32[4]{0:T(128)}, u32[]{:S(2)}) copy-start(s32[4]{0:T(128)} %param.22) | copy-start | bytes 52
  264.5 101.9 %reduce-scatter.7.cloned.1.call-start = ((), (), s32[]{:S(2)}) async-start(), calls=%async_computation.8 | async-start | bytes 1966080
  265.3 44.4 %copy-start.6 = (f32[768]{0:T(1024)S(1)}, f32[768]{0:T(1024)}, u32[]{:S(2)}) copy-start(f32[768]{0:T(1024)} %param.18) | copy-start | bytes 9220
  307.5 1.9 copy-start.1
  332.1 3.8 %copy-start.5 = (bf16[192,768]{1,0:T(8,128)(2,1)S(1)}, bf16[192,768]{1,0:T(8,128)(2,1)}, u32[]{:S(2)}) copy-start(bf16[192,768]{1,0:T(8,128)(2,1)} %param.20) | copy-start | bytes 884740
Sparse Core Ops, SparseCore 0:
  8.9 22.3 all-gather.13
  33.4 60.4 all-gather.7
  96.0 59.0 all-gather.9
  157.0 59.0 all-gather.11
  225.0 36.5 reduce-scatter.4
  264.6 42.8 all-reduce.1
  337.6 28.7 reduce-scatter.6
where the time goes:
time: 376 us; the launch traced here: 375 us
  waiting for transfers between devices  307 us (82%)
  matrix products  26.1 us (7%)
  blocking collectives  13.7 us (4%)
  between operations  13.7 us (4%)
  other arithmetic  11.4 us (3%)
    all_gather x1, waiting for transfers between devices, per_device(): lax.all_gather(w_down, ('seq', 'dp'), axis=1, tiled=True)  61.1 us
    all_gather x1, waiting for transfers between devices, per_device(): lax.all_gather(w_gate, ('seq', 'dp'), axis=0, tiled=True)  60.1 us
    all_gather x1, waiting for transfers between devices, per_device(): lax.all_gather(w_up, ('seq', 'dp'), axis=0, tiled=True)  56.1 us
    psum x1, waiting for transfers between devices, per_device(): emb = lax.psum(part_emb, 'section')  41.5 us
    reduce_scatter x1, waiting for transfers between devices, per_device(): lax.psum_scatter(terms, 'section', scatter_dimension=1, tiled=True)  35.1 us
    unnamed x8, waiting for transfers between devices  31.6 us
    all_gather x1, waiting for transfers between devices, per_device(): whole = lax.all_gather(mine, 'section', axis=1, tiled=True)  21.9 us
    dot_general x1, matrix products, per_device(): jnp.dot(hidden, lax.all_gather(w_down, ('seq', 'dp'), axis=1, tiled=True)...  8.71 us
  transfers between devices with their start and end apart: 7, of which 7 were waited for; matrix products, arithmetic and copies ran while one was open for 3% of the time, Pallas kernels for 0%

commit v1 on v0

v1 whole, which is shorter than its diff:
```python
import math

import jax
import jax.numpy as jnp
from jax import lax
from jax.experimental import pallas as pl
from jax.experimental.pallas import tpu as pltpu
from jax.sharding import PartitionSpec as P

NEG = -1e30
AXES = ("section", "seq", "dp")


def layer_norm(rows, gain):
    mean = jnp.mean(rows, axis=-1, keepdims=True)
    centered = rows - mean
    var = jnp.mean(centered * centered, axis=-1, keepdims=True)
    return centered * lax.rsqrt(var + 1e-06) * gain


def slide_place(lengths_row, index):
    ends = jnp.cumsum(lengths_row, dtype=jnp.int32)
    after = index[:, None] >= ends[None, :]
    slide = jnp.sum(after.astype(jnp.int32), axis=1, dtype=jnp.int32)
    before = jnp.sum(jnp.where(after, lengths_row[None, :], 0), axis=1, dtype=jnp.int32)
    return (slide, index - before)


def attend_block(sec, mine, keys, weights, out_weights, emb, q_code, k_code, heads):
    rows, count = mine.shape[0], keys.shape[0]
    width = weights[0].shape[2]
    size = width // heads
    scale = math.log2(math.e) / math.sqrt(size)
    lane_head = lax.broadcasted_iota(jnp.int32, (rows, width), 1) // size
    diag = lax.broadcasted_iota(jnp.int32, (rows, count), 0) == lax.broadcasted_iota(
        jnp.int32, (rows, count), 1
    )
    total = emb[...]
    for m in range(len(weights)):
        query = jnp.dot(mine, weights[m][0], preferred_element_type=jnp.float32).astype(jnp.bfloat16)
        key = jnp.dot(keys, weights[m][1], preferred_element_type=jnp.float32).astype(jnp.bfloat16)
        value = jnp.dot(keys, weights[m][2], preferred_element_type=jnp.float32).astype(jnp.bfloat16)
        split = jnp.concatenate(
            [jnp.where(lane_head == h, query, jnp.zeros_like(query)) for h in range(heads)], axis=0
        )
        scores = lax.dot_general(
            split, key, (((1,), (1,)), ((), ())), preferred_element_type=jnp.float32
        )
        parts, sums = [], []
        for h in range(heads):
            at = m * heads + h
            ok = (q_code[:, at : at + 1] == k_code[at : at + 1, :]) | diag
            own = jnp.where(ok, scores[h * rows : (h + 1) * rows], NEG)
            top = jnp.max(own, axis=1, keepdims=True)
            weight = jnp.exp2((own - top) * scale)
            sums.append(jnp.sum(weight, axis=1, keepdims=True))
            parts.append(weight.astype(jnp.bfloat16))
        mixed = jnp.dot(jnp.concatenate(parts, axis=0), value, preferred_element_type=jnp.float32)
        att = jnp.zeros((rows, width), jnp.float32)
        for h in range(heads):
            att = jnp.where(lane_head == h, mixed[h * rows : (h + 1) * rows] / sums[h], att)
        total = total + jnp.dot(
            att.astype(jnp.bfloat16), out_weights[m][...], preferred_element_type=jnp.float32
        )
    return total


def attend_kernel(sec_ref, mine_ref, near_ref, far_ref, *refs, heads, parts):
    weights, out_weights = refs[:parts], refs[parts : 2 * parts]
    emb_ref, q_ref, k_ref, out_ref = refs[2 * parts :]
    mine = mine_ref[...]
    keys = jnp.concatenate(
        [mine]
        + [near_ref[i] for i in range(near_ref.shape[0])]
        + [far_ref[i] for i in range(far_ref.shape[0])],
        axis=0,
    )
    total = attend_block(
        sec_ref[0], mine, keys, weights, out_weights, emb_ref, q_ref[...], k_ref, heads
    )
    width = out_ref.shape[2]
    for j in range(parts):
        out_ref[j ^ sec_ref[0]] = total[:, j * width : (j + 1) * width].astype(out_ref.dtype)


def build(n_sec, n_seq, n_dp):
    sizes = {"section": n_sec, "seq": n_seq, "dp": n_dp}

    def flip(x, **masks):
        names = tuple(a for a in AXES if masks.get(a))
        pairs = []
        total = math.prod(sizes[a] for a in names)
        for source in range(total):
            rest, coords = source, []
            for a in reversed(names):
                coords.append(rest % sizes[a])
                rest //= sizes[a]
            target = 0
            for a, c in zip(names, reversed(coords)):
                target = target * sizes[a] + (c ^ masks[a])
            pairs.append((source, target))
        return lax.ppermute(x, names if len(names) > 1 else names[0], pairs)

    def rotate(x, k):
        return lax.ppermute(x, "dp", [(i, (i + k) % n_dp) for i in range(n_dp)])

    def gather_section(x):
        across = flip(x, section=2)
        return [x, flip(x, section=1), across, flip(across, section=1)]

    def gather_rows(same, other, seq_at, dp_at):
        got = [same] + [rotate(other if k % 2 else same, k) for k in range(1, n_dp)]
        mats, rows, units = same.shape
        if n_seq == 2:
            whole = jnp.zeros((mats, n_seq * n_dp * rows, units), same.dtype)
            for k, block in enumerate(got):
                z = (dp_at - k) % n_dp
                theirs = flip(block, seq=1)
                whole = lax.dynamic_update_slice(whole, block, (0, (seq_at * n_dp + z) * rows, 0))
                whole = lax.dynamic_update_slice(
                    whole, theirs, (0, ((1 - seq_at) * n_dp + z) * rows, 0)
                )
            return whole
        part = jnp.zeros((mats, n_dp * rows, units), same.dtype)
        for k, block in enumerate(got):
            part = lax.dynamic_update_slice(part, block, (0, ((dp_at - k) % n_dp) * rows, 0))
        return lax.all_gather(part, "seq", axis=1, tiled=True)

    def per_device(
        tile_feats,
        tile_gain,
        w_gate,
        w_up,
        w_down,
        w_proj,
        slide_gain,
        w_qkv,
        w_out,
        lengths,
        seg_len,
        rate,
    ):
        sec = lax.axis_index("section")
        seq_at = lax.axis_index("seq")
        dp_at = lax.axis_index("dp")
        core, side, odd = sec % 2, sec // 2, dp_at % 2
        mine = tile_feats[0]
        tokens, feats = mine.shape
        own_rows = tokens // n_sec
        half = w_gate.shape[1] // 2

        def absolute(blocks):
            stacked = jnp.stack(blocks)
            return [lax.dynamic_index_in_dim(stacked, sec ^ j, 0, False) for j in range(n_sec)]

        both = jnp.concatenate([mine, flip(mine, dp=1)], axis=0)
        rows = jnp.concatenate(absolute(gather_section(both)), axis=1)

        down = w_down.T

        def halves(x, which):
            return lax.dynamic_slice_in_dim(x, which * half, half, x.ndim - 1)

        pair = jnp.stack([w_gate, w_up])
        gate_up = gather_rows(halves(pair, odd), halves(pair, 1 - odd), seq_at, dp_at)
        down_all = gather_rows(halves(down[None], odd), halves(down[None], 1 - odd), seq_at, dp_at)[0]

        proj = jnp.concatenate(absolute(gather_section(w_proj)), axis=0)
        qkv = gather_section(w_qkv)
        outs = gather_section(w_out)
        head_info = gather_section(jnp.stack([seg_len, rate]))

        normed = layer_norm(rows.astype(jnp.float32), tile_gain).astype(jnp.bfloat16)
        gate = jnp.dot(normed, gate_up[0], preferred_element_type=jnp.float32)
        up = jnp.dot(normed, gate_up[1], preferred_element_type=jnp.float32)
        hidden = (jax.nn.silu(gate) * up).astype(jnp.bfloat16)
        hidden = hidden.reshape(2, n_sec // 2, 2, own_rows, half)
        folded = lax.dot_general(
            proj, down_all, (((0,), (0,)), ((), ())), preferred_element_type=jnp.float32
        ).astype(jnp.bfloat16)

        def project(units):
            return lax.dot_general(
                units, folded, (((4 - 1,), (1,)), ((), ())), preferred_element_type=jnp.float32
            )

        send = project(lax.dynamic_index_in_dim(hidden, 1 - core, 2, False)).astype(jnp.bfloat16)
        got = flip(send, section=1)
        kept = project(lax.dynamic_index_in_dim(hidden, core, 2, False)) + got.astype(jnp.float32)
        here = lax.dynamic_index_in_dim(kept, side, 1, False)
        there = lax.dynamic_index_in_dim(kept, 1 - side, 1, False).astype(jnp.bfloat16)
        from_x = flip(there[0], section=2)
        from_z = flip(here[1].astype(jnp.bfloat16), dp=1)
        from_xz = flip(there[1], section=2, dp=1)
        residual = jnp.dot(
            lax.dynamic_slice_in_dim(rows[:tokens], sec * own_rows, own_rows, 0),
            proj,
            preferred_element_type=jnp.float32,
        )
        emb = (
            residual
            + here[0]
            + from_x.astype(jnp.float32)
            + from_z.astype(jnp.float32)
            + from_xz.astype(jnp.float32)
        )
        slide_normed = layer_norm(emb, slide_gain).astype(jnp.bfloat16)

        my_start = seq_at * tokens + sec * own_rows
        span = jnp.arange(own_rows, dtype=jnp.int32)
        if n_seq == 2:
            near = jnp.stack(
                [
                    flip(slide_normed, section=2),
                    flip(slide_normed, seq=1),
                    flip(slide_normed, section=2, seq=1),
                ]
            )
            far = flip(jnp.concatenate([slide_normed[None], near]), section=1)
            order = [(s, q) for s in (0, 1) for q in ((0, 0), (2, 0), (0, 1), (2, 1))]
            starts = [(seq_at ^ q[1]) * tokens + (sec ^ q[0] ^ s) * own_rows for s, q in order]
            k_idx = jnp.concatenate([start + span for start in starts])
        else:
            every = lax.all_gather(slide_normed, ("seq", "section"), axis=0, tiled=True)
            count = every.shape[0]
            keys = jnp.concatenate([slide_normed, jnp.roll(every, -my_start, axis=0)[own_rows:]])
            k_idx = (my_start + jnp.arange(count, dtype=jnp.int32)) % count
        count = k_idx.shape[0]

        local_heads = seg_len.shape[0]
        heads = jnp.concatenate(
            [(sec ^ m) * local_heads + jnp.arange(local_heads, dtype=jnp.int32) for m in range(n_sec)]
        )
        seg_all = jnp.concatenate([info[0] for info in head_info])
        rate_all = jnp.concatenate([info[1] for info in head_info])
        slide, pos = slide_place(lengths[0], k_idx)
        block = slide[None, :] * count + pos[None, :] // seg_all[:, None]
        picked = pos[None, :] % rate_all[:, None] == (heads % rate_all)[:, None]
        k_code = jnp.where(picked, block, -1)
        q_code = block[:, :own_rows].T

        width = w_qkv.shape[2]
        if n_seq == 2:
            params = dict(
                compiler_params=pltpu.CompilerParams(vmem_limit_bytes=48 * 2**20),
                cost_estimate=pl.CostEstimate(
                    flops=2 * n_sec * count * width * (2 * 768 + 2 * local_heads * own_rows),
                    bytes_accessed=8 * 2**20,
                    transcendentals=n_sec * local_heads * own_rows * count,
                ),
            )
            vmem = pl.BlockSpec(memory_space=pltpu.VMEM)
            final = pl.pallas_call(
                lambda *refs: attend_kernel(*refs, heads=local_heads, parts=n_sec),
                out_shape=jax.ShapeDtypeStruct((n_sec, own_rows, width), jnp.bfloat16),
                in_specs=[pl.BlockSpec(memory_space=pltpu.SMEM)] + [vmem] * (6 + 2 * n_sec),
                out_specs=vmem,
                **params,
            )(sec[None], slide_normed, near, far, *qkv, *outs, emb, q_code, k_code)
        else:
            total = emb
            for m in range(n_sec):
                query = jnp.dot(slide_normed, qkv[m][0], preferred_element_type=jnp.float32)
                key = jnp.dot(keys, qkv[m][1], preferred_element_type=jnp.float32)
                value = jnp.dot(keys, qkv[m][2], preferred_element_type=jnp.float32)
                size = width // local_heads

                def one_head(args):
                    q, k, v, q_row, k_row = args
                    scores = jnp.dot(q, k.T, preferred_element_type=jnp.float32) / math.sqrt(size)
                    diag = jnp.arange(own_rows)[:, None] == jnp.arange(count)[None, :]
                    ok = (q_row[:, None] == k_row[None, :]) | diag
                    weight = jax.nn.softmax(jnp.where(ok, scores, NEG), axis=-1)
                    return jnp.dot(weight, v, preferred_element_type=jnp.float32)

                def by_head(x):
                    return x.astype(jnp.bfloat16).reshape(-1, local_heads, size).transpose(1, 0, 2)

                at = slice(m * local_heads, (m + 1) * local_heads)
                att = lax.map(
                    one_head,
                    (by_head(query), by_head(key), by_head(value), q_code.T[at], k_code[at]),
                )
                att = att.transpose(1, 0, 2).reshape(own_rows, width).astype(jnp.bfloat16)
                total = total + jnp.dot(att, outs[m], preferred_element_type=jnp.float32)
            cut = total.astype(jnp.bfloat16).reshape(own_rows, n_sec, width).transpose(1, 0, 2)
            final = jnp.stack(
                [lax.dynamic_index_in_dim(cut, sec ^ m, 0, False) for m in range(n_sec)]
            )

        pieces = [final[0]] + [flip(final[m], section=m) for m in range(1, n_sec)]
        return jnp.concatenate(absolute(pieces), axis=0)[None]

    return per_device


def solution(mesh):
    placed = (
        P("dp", "seq", "section"),
        P(),
        P(("seq", "dp"), "section"),
        P(("seq", "dp"), "section"),
        P("section", ("seq", "dp")),
        P("section", None),
        P(),
        P(None, None, "section"),
        P("section", None),
        P("dp", None),
        P("section"),
        P("section"),
    )
    shape = mesh.shape
    return jax.shard_map(
        build(shape["section"], shape["seq"], shape["dp"]),
        mesh=mesh,
        in_specs=placed,
        out_specs=P("dp", "seq", "section"),
        check_vma=False,
    )
```

time: 376 us -> 169 us (0.45)
  waiting for transfers between devices: 307 us -> 69.5 us
  starting transfers between devices: 0.24 us -> 47.6 us
  matrix products: 26.1 us -> 9.83 us
  blocking collectives: 13.7 us -> 0 us
  local copies, waits for them, and re-layouts: 2.89 us -> 16.3 us
  between operations: 13.7 us -> 0.83 us
  Pallas kernels: 0 us -> 11.3 us
    all_gather x4 -> x0, waiting for transfers between devices: 199 us -> none  [the longest x1 61.1 us: per_device(): lax.all_gather(w_down, ('seq', 'dp'), axis=1, tiled=True)]
    ppermute x0 -> x41, waiting for transfers between devices: none -> 69.5 us  [the longest x35 51.7 us: flip(): return lax.ppermute(x, names if len(names) > 1 else names[0], pairs)]
    ppermute x0 -> x41, starting transfers between devices: none -> 47.6 us  [the longest x35 29.4 us: flip(): return lax.ppermute(x, names if len(names) > 1 else names[0], pairs)]
    psum x1 -> x0, waiting for transfers between devices: 41.5 us -> none  [per_device(): emb = lax.psum(part_emb, 'section')]
    reduce_scatter x1 -> x0, waiting for transfers between devices: 35.1 us -> none  [per_device(): lax.psum_scatter(terms, 'section', scatter_dimension=1, tiled=True)]
    unnamed x8 -> x0, waiting for transfers between devices: 31.6 us -> none
    dot_general x5 -> x6, matrix products: 23.7 us -> 9.83 us  [the longest x2 3.61 us: project(): lax.dot_general(units, folded, (((4 - 1,), (1,)), ((), ())), preferred_el...]
    all_gather x2 -> x0, blocking collectives: 13.7 us -> none  [the longest x1 7.36 us: per_device(): key_piece = lax.all_gather(projected[1], 'seq', axis=0, tiled=True)]
  transfers between devices with their start and end apart: 7 -> 41, of which waited for: 7 -> 19; matrix products, arithmetic and copies ran while one was open for 3% -> 21% of each run, Pallas kernels for 0% -> 0%
where the time goes in v1:
time: 169 us; the launch traced here: 168 us
  waiting for transfers between devices  69.5 us (41%)
  starting transfers between devices  47.6 us (28%)
  local copies, waits for them, and re-layouts  16.3 us (10%)
  other arithmetic  12.9 us (8%)
  Pallas kernels  11.3 us (7%)
  matrix products  9.83 us (6%)
    ppermute x35, waiting for transfers between devices, flip(): return lax.ppermute(x, names if len(names) > 1 else names[0], pairs)  51.7 us
    ppermute x35, starting transfers between devices, flip(): return lax.ppermute(x, names if len(names) > 1 else names[0], pairs)  29.4 us
    ppermute x6, starting transfers between devices, rotate(): return lax.ppermute(x, 'dp', [(i, (i + k) % n_dp) for i in range(n_dp)])  18.1 us
    ppermute x6, waiting for transfers between devices, rotate(): return lax.ppermute(x, 'dp', [(i, (i + k) % n_dp) for i in range(n_dp)])  17.8 us
    pallas_call x1, Pallas kernels, per_device(): pl.pallas_call(lambda *refs: attend_kernel(*refs, heads=local_heads, part...  11.3 us
    ppermute x3, local copies, waits for them, and re-layouts, flip(): return lax.ppermute(x, names if len(names) > 1 else names[0], pairs)  6.22 us
    dot_general x2, matrix products, project(): lax.dot_general(units, folded, (((4 - 1,), (1,)), ((), ())), preferred_el...  3.61 us
  transfers between devices with their start and end apart: 41, of which 19 were waited for; matrix products, arithmetic and copies ran while one was open for 21% of the time, Pallas kernels for 0%

profile of v1, /device:TPU:0, one launch (start us, length us, event | category | flops | bytes accessed | tf_op | source)
XLA Modules:
  0.0 168.2 jit_solution(7117277278868441199)
XLA Ops:
  1.2 1.0 constant_dynamic-update-slice_fusion.7
  2.2 3.0 %collective-permute-start.7 = (bf16[2,192,512]{2,1,0:T(8,128)(2,1)}, bf16[2,192,512]{2,1,0:T(8,128)(2,1)}, u32[]{:S(2)}, u32[]{:S(2)}) collective-permute-start(bf16[2,192,512]{2,1,0:T(8,128)(2,1)} %get-tuple-element.14), channel_id=1, source_target_pairs={{0,4},{4,0},{1,5},{5,1},{2,6},{6,2},{3,7},{7,3},{8,12},{12,8},{9,1... | collective-permute-start | bytes 1179656 | tf_op jit(solution)/shard_map/ppermute | solution.py:102
  5.2 2.6 %collective-permute-start.10 = (bf16[2,192,512]{2,1,0:T(8,128)(2,1)}, bf16[2,192,512]{2,1,0:T(8,128)(2,1)}, u32[]{:S(2)}, u32[]{:S(2)}) collective-permute-start(bf16[2,192,512]{2,1,0:T(8,128)(2,1)} %get-tuple-element.14), channel_id=1, source_target_pairs={{0,2},{1,3},{2,0},{3,1},{4,6},{5,7},{6,4},{7,5},{8,10},{9,11},{10,... | collective-permute-start | bytes 1179656 | tf_op jit(solution)/shard_map/ppermute | solution.py:105
  9.1 1.9 %collective-permute-start.15 = (bf16[1,192,512]{2,1,0:T(8,128)(2,1)}, bf16[1,192,512]{2,1,0:T(8,128)(2,1)}, u32[]{:S(2)}, u32[]{:S(2)}) collective-permute-start(bf16[1,192,512]{2,1,0:T(8,128)(2,1)} %get-tuple-element.30), channel_id=1, source_target_pairs={{0,1},{1,2},{2,3},{3,0},{4,5},{5,6},{6,7},{7,4},{8,9},{9,10},{10,1... | collective-permute-start | bytes 589832 | tf_op jit(solution)/shard_map/ppermute | solution.py:105
  14.4 4.4 %collective-permute-done.14 = bf16[1,192,512]{2,1,0:T(8,128)(2,1)} collective-permute-done((bf16[1,192,512]{2,1,0:T(8,128)(2,1)}, bf16[1,192,512]{2,1,0:T(8,128)(2,1)}, u32[]{:S(2)}, u32[]{:S(2)}) %collective-permute-start.14) | collective-permute-done | bytes 196640 | tf_op jit(solution)/shard_map/ppermute | solution.py:102
  18.8 3.8 %collective-permute-start.19 = (bf16[1,192,512]{2,1,0:T(8,128)(2,1)}, bf16[1,192,512]{2,1,0:T(8,128)(2,1)S(1)}, u32[]{:S(2)}, u32[]{:S(2)}) collective-permute-start(bf16[1,192,512]{2,1,0:T(8,128)(2,1)} %get-tuple-element.30), channel_id=1, source_target_pairs={{0,3},{1,0},{2,1},{3,2},{4,7},{5,4},{6,5},{7,6},{8,11},{9,8},{10,9... | collective-permute-start | bytes 589832 | tf_op jit(solution)/shard_map/ppermute | solution.py:105
  22.7 5.3 %collective-permute-done.15 = bf16[1,192,512]{2,1,0:T(8,128)(2,1)} collective-permute-done((bf16[1,192,512]{2,1,0:T(8,128)(2,1)}, bf16[1,192,512]{2,1,0:T(8,128)(2,1)}, u32[]{:S(2)}, u32[]{:S(2)}) %collective-permute-start.15) | collective-permute-done | bytes 196640 | tf_op jit(solution)/shard_map/ppermute | solution.py:105
  30.4 8.9 %collective-permute-done.17 = bf16[1,192,512]{2,1,0:T(8,128)(2,1)} collective-permute-done((bf16[1,192,512]{2,1,0:T(8,128)(2,1)}, bf16[1,192,512]{2,1,0:T(8,128)(2,1)}, u32[]{:S(2)}, u32[]{:S(2)}) %collective-permute-start.17) | collective-permute-done | bytes 196640 | tf_op jit(solution)/shard_map/ppermute | solution.py:105
  39.3 6.1 %collective-permute-start.8 = (bf16[2,192,512]{2,1,0:T(8,128)(2,1)}, bf16[2,192,512]{2,1,0:T(8,128)(2,1)S(1)}, u32[]{:S(2)}, u32[]{:S(2)}) collective-permute-start(bf16[2,192,512]{2,1,0:T(8,128)(2,1)} %get-tuple-element.25), channel_id=1, source_target_pairs={{0,1},{1,2},{2,3},{3,0},{4,5},{5,6},{6,7},{7,4},{8,9},{9,10},{10,1... | collective-permute-start | bytes 1179656 | tf_op jit(solution)/shard_map/ppermute | solution.py:105
  45.4 1.5 collective-permute-start.18
  47.9 3.6 %collective-permute-start = (bf16[512,384]{1,0:T(8,128)(2,1)S(1)}, bf16[512,384]{1,0:T(8,128)(2,1)S(1)}, u32[]{:S(2)}, u32[]{:S(2)}) collective-permute-start(bf16[512,384]{1,0:T(8,128)(2,1)S(1)} %bitcast.140), channel_id=1, source_target_pairs={{0,1},{1,0},{2,3},{3,2},{4,5},{5,4},{6,7},{7,6},{8,9},{9,8},{10,11... | collective-permute-start | bytes 1179656 | tf_op jit(solution)/shard_map/ppermute | solution.py:102
  51.9 1.5 collective-permute-start.20
  53.5 1.8 %collective-permute-done.8 = bf16[2,192,512]{2,1,0:T(8,128)(2,1)S(1)} collective-permute-done((bf16[2,192,512]{2,1,0:T(8,128)(2,1)}, bf16[2,192,512]{2,1,0:T(8,128)(2,1)S(1)}, u32[]{:S(2)}, u32[]{:S(2)}) %collective-permute-start.8) | collective-permute-done | bytes 393248 | tf_op jit(solution)/shard_map/ppermute | solution.py:105
  55.3 3.7 %collective-permute-start.12 = (bf16[2,192,512]{2,1,0:T(8,128)(2,1)S(1)}, bf16[2,192,512]{2,1,0:T(8,128)(2,1)S(1)}, u32[]{:S(2)}, u32[]{:S(2)}) collective-permute-start(bf16[2,192,512]{2,1,0:T(8,128)(2,1)S(1)} %copy-done.20), channel_id=1, source_target_pairs={{0,3},{1,0},{2,1},{3,2},{4,7},{5,4},{6,5},{7,6},{8,11},{9,8},{10,9... | collective-permute-start | bytes 1179656 | tf_op jit(solution)/shard_map/ppermute | solution.py:105
  59.0 4.6 %collective-permute-done = bf16[512,384]{1,0:T(8,128)(2,1)S(1)} collective-permute-done((bf16[512,384]{1,0:T(8,128)(2,1)S(1)}, bf16[512,384]{1,0:T(8,128)(2,1)S(1)}, u32[]{:S(2)}, u32[]{:S(2)}) %collective-permute-start) | collective-permute-done | bytes 393248 | tf_op jit(solution)/shard_map/ppermute | solution.py:102
  63.6 1.5 collective-permute-start.5
  65.1 1.5 collective-permute-start.9
  67.9 1.0 constant_dynamic-update-slice_fusion.6
  69.0 1.8 %collective-permute-done.12 = bf16[2,192,512]{2,1,0:T(8,128)(2,1)S(1)} collective-permute-done((bf16[2,192,512]{2,1,0:T(8,128)(2,1)S(1)}, bf16[2,192,512]{2,1,0:T(8,128)(2,1)S(1)}, u32[]{:S(2)}, u32[]{:S(2)}) %collective-permute-start.12) | collective-permute-done | bytes 393248 | tf_op jit(solution)/shard_map/ppermute | solution.py:105
  70.8 9.1 %collective-permute-done.5 = bf16[384,768]{1,0:T(8,128)(2,1)S(1)} collective-permute-done((bf16[384,768]{1,0:T(8,128)(2,1)S(1)}, bf16[384,768]{1,0:T(8,128)(2,1)S(1)}, u32[]{:S(2)}, u32[]{:S(2)}) %collective-permute-start.5) | collective-permute-done | bytes 589856 | tf_op jit(solution)/shard_map/ppermute | solution.py:102
  79.9 1.5 collective-permute-start.13
  81.4 1.0 constant_dynamic-update-slice_fusion.3
  82.5 3.1 %collective-permute-done.11 = bf16[2,192,512]{2,1,0:T(8,128)(2,1)S(1)} collective-permute-done((bf16[2,192,512]{2,1,0:T(8,128)(2,1)}, bf16[2,192,512]{2,1,0:T(8,128)(2,1)S(1)}, u32[]{:S(2)}, u32[]{:S(2)}) %collective-permute-start.11) | collective-permute-done | bytes 393248 | tf_op jit(solution)/shard_map/ppermute | solution.py:102
  86.2 4.1 %collective-permute-done.13 = bf16[2,192,512]{2,1,0:T(8,128)(2,1)S(1)} collective-permute-done((bf16[2,192,512]{2,1,0:T(8,128)(2,1)S(1)}, bf16[2,192,512]{2,1,0:T(8,128)(2,1)S(1)}, u32[]{:S(2)}, u32[]{:S(2)}) %collective-permute-start.13) | collective-permute-done | bytes 393248 | tf_op jit(solution)/shard_map/ppermute | solution.py:102
  90.9 2.4 %collective-permute-done.2 = bf16[1024,384]{1,0:T(8,128)(2,1)S(1)} collective-permute-done((bf16[1024,384]{1,0:T(8,128)(2,1)S(1)}, bf16[1024,384]{1,0:T(8,128)(2,1)S(1)}, u32[]{:S(2)}, u32[]{:S(2)}) %collective-permute-start.2) | collective-permute-done | bytes 786464 | tf_op jit(solution)/shard_map/ppermute | solution.py:102
  94.3 1.4 fusion.7
  100.3 1.8 %fusion.6 = f32[1024,512]{1,0:T(8,128)S(1)} fusion(bf16[1024,1536]{1,0:T(8,128)(2,1)S(1)} %fusion.4, bf16[2,1536,512]{2,1,0:T(8,128)(2,1)S(1)} %constant_dynamic-update-slice_fusion), kind=kOutput, calls=%fused_computation.15 | convolution fusion | flops 1610612736 | bytes 6815744 | tf_op jit(solution)/shard_map/dot_general | solution.py:174
  102.1 2.0 %multiply_convert_fusion = bf16[1024,512]{1,0:T(8,128)(2,1)S(1)} fusion(f32[1024,512]{1,0:T(8,128)S(1)} %fusion.6, bf16[1024,1536]{1,0:T(8,128)(2,1)S(1)} %fusion.4, bf16[2,1536,512]{2,1,0:T(8,128)(2,1)S(1)} %constant_dynamic-update-slice_fusion), kind=kOutput, calls=%fused_computation.11 | convolution fusion | flops 1613758464 | bytes 7864320 | tf_op jit(solution)/shard_map/dot_general | solution.py:175
  104.1 1.6 convolution_convert_fusion
  105.9 1.5 copy.34.refs_4_
  108.2 2.0 %convert_add_fusion = f32[2,2,128,768]{3,2,1,0:T(8,128)S(1)} fusion(bf16[2,2,128,768]{3,2,1,0:T(8,128)(2,1)S(1)} %collective-permute-done.21, bf16[768,512,1,1]{1,0,3,2:T(8,128)(2,1)} %copy-done.7, bf16[2,2,2,128,512]{4,3,2,1,0:T(8,128)(2,1)} %bitcast.145, s32[]{:T(128)S(6)} %select_n.184), kind=kOutput, calls=%fused_computation.16 | convolution fusion | flops 403439616 | bytes 3670020 | tf_op jit(solution)/shard_map/dot_general | solution.py:183
  110.4 2.0 %collective-permute-start.22 = (bf16[128,768]{1,0:T(8,128)(2,1)S(1)}, bf16[128,768]{1,0:T(8,128)(2,1)S(1)}, u32[]{:S(2)}, u32[]{:S(2)}) collective-permute-start(bf16[128,768]{1,0:T(8,128)(2,1)S(1)} %get-tuple-element.28), channel_id=1, source_target_pairs={{0,16},{8,24},{16,0},{24,8},{1,17},{9,25},{17,1},{25,9},{2,18},{10... | collective-permute-start | bytes 589832 | tf_op jit(solution)/shard_map/ppermute | solution.py:102
  112.4 2.0 %collective-permute-start.24 = (bf16[128,768]{1,0:T(8,128)(2,1)S(1)}, bf16[128,768]{1,0:T(8,128)(2,1)S(1)}, u32[]{:S(2)}, u32[]{:S(2)}) collective-permute-start(bf16[128,768]{1,0:T(8,128)(2,1)S(1)} %get-tuple-element.29), channel_id=1, source_target_pairs={{0,17},{1,16},{2,19},{3,18},{8,25},{9,24},{10,27},{11,26},{16,1},{... | collective-permute-start | bytes 589832 | tf_op jit(solution)/shard_map/ppermute | solution.py:102
  115.3 6.7 %collective-permute-done.22 = bf16[128,768]{1,0:T(8,128)(2,1)S(1)} collective-permute-done((bf16[128,768]{1,0:T(8,128)(2,1)S(1)}, bf16[128,768]{1,0:T(8,128)(2,1)S(1)}, u32[]{:S(2)}, u32[]{:S(2)}) %collective-permute-start.22) | collective-permute-done | bytes 196640 | tf_op jit(solution)/shard_map/ppermute | solution.py:102
  122.0 2.3 %collective-permute-done.23 = bf16[128,768]{1,0:T(8,128)(2,1)S(1)} collective-permute-done((bf16[128,768]{1,0:T(8,128)(2,1)S(1)}, bf16[128,768]{1,0:T(8,128)(2,1)S(1)}, u32[]{:S(2)}, u32[]{:S(2)}) %collective-permute-start.23) | collective-permute-done | bytes 196640 | tf_op jit(solution)/shard_map/ppermute | solution.py:102
  126.4 1.5 collective-permute-start.26
  128.0 1.2 collective-permute-start.27
  129.3 4.2 %collective-permute-done.25 = bf16[128,768]{1,0:T(8,128)(2,1)S(1)} collective-permute-done((bf16[128,768]{1,0:T(8,128)(2,1)S(1)}, bf16[128,768]{1,0:T(8,128)(2,1)S(1)}, u32[]{:S(2)}, u32[]{:S(2)}) %collective-permute-start.25) | collective-permute-done | bytes 196640 | tf_op jit(solution)/shard_map/ppermute | solution.py:102
  134.1 4.6 %collective-permute-done.27 = bf16[128,768]{1,0:T(8,128)(2,1)S(1)} collective-permute-done((bf16[128,768]{1,0:T(8,128)(2,1)S(1)}, bf16[128,768]{1,0:T(8,128)(2,1)S(1)}, u32[]{:S(2)}, u32[]{:S(2)}) %collective-permute-start.27) | collective-permute-done | bytes 196640 | tf_op jit(solution)/shard_map/ppermute | solution.py:102
  139.9 1.4 fusion.26
  141.3 1.4 collective-permute-done.33.refs_10_
  142.8 2.4 %copy.36.refs_6_ = bf16[3,768,192]{2,1,0:T(8,128)(2,1)} copy(bf16[3,768,192]{1,2,0:T(8,128)(2,1)} %collective-permute-done.30) | data formatting | bytes 1769472 | tf_op jit(solution)/shard_map/ppermute | solution.py:102
  145.2 1.5 copy.35.refs_5_
  146.7 2.3 %copy.37.refs_7_ = bf16[3,768,192]{2,1,0:T(8,128)(2,1)} copy(bf16[3,768,192]{1,2,0:T(8,128)(2,1)} %collective-permute-done.31) | data formatting | bytes 1769472 | tf_op jit(solution)/shard_map/ppermute | solution.py:102
  149.1 1.2 pad_maximum_fusion.6.refs_2_
  150.3 11.3 %shard_map.118 = bf16[4,128,192]{2,1,0:T(8,128)(2,1)S(1)} custom-call(s32[1]{0:T(128)} %bitcast.refs_0_, bf16[128,768]{1,0:T(8,128)(2,1)S(1)} %multiply_convert_fusion.1.refs_1_, bf16[3,128,768]{2,1,0:T(8,128)(2,1)S(1)} %pad_maximum_fusion.6.refs_2_, bf16[4,128,768]{2,1,0:T(8,128)(2,1)} %collective-permute-done.28.refs_3_, ...), custom_call_target="tpu_custom_call" | custom-call | flops 4026531840 | bytes 8388608 | tf_op jit(solution)/shard_map/pallas_call | solution.py:253
  162.5 1.1 collective-permute-start.40
  163.6 3.3 %collective-permute-done.39 = bf16[128,192]{1,0:T(8,128)(2,1)S(1)} collective-permute-done((bf16[128,192]{1,0:T(8,128)(2,1)S(1)}, bf16[128,192]{1,0:T(8,128)(2,1)S(1)}, u32[]{:S(2)}, u32[]{:S(2)}) %collective-permute-start.39) | collective-permute-done | bytes 49184 | tf_op jit(solution)/shard_map/ppermute | solution.py:102
  (178 shorter events, 25.8 us)
Async XLA Ops:
  2.2 64.6 %collective-permute-start.7 = (bf16[2,192,512]{2,1,0:T(8,128)(2,1)}, bf16[2,192,512]{2,1,0:T(8,128)(2,1)}, u32[]{:S(2)}, u32[]{:S(2)}) collective-permute-start(bf16[2,192,512]{2,1,0:T(8,128)(2,1)} %get-tuple-element.14), channel_id=1, source_target_pairs={{0,4},{4,0},{1,5},{5,1},{2,6},{6,2},{3,7},{7,3},{8,12},{12,8},{9,1... | collective-permute-start | bytes 1179656 | tf_op jit(solution)/shard_map/ppermute | solution.py:102
  5.2 62.2 %collective-permute-start.10 = (bf16[2,192,512]{2,1,0:T(8,128)(2,1)}, bf16[2,192,512]{2,1,0:T(8,128)(2,1)}, u32[]{:S(2)}, u32[]{:S(2)}) collective-permute-start(bf16[2,192,512]{2,1,0:T(8,128)(2,1)} %get-tuple-element.14), channel_id=1, source_target_pairs={{0,2},{1,3},{2,0},{3,1},{4,6},{5,7},{6,4},{7,5},{8,10},{9,11},{10,... | collective-permute-start | bytes 1179656 | tf_op jit(solution)/shard_map/ppermute | solution.py:105
  8.6 10.3 %collective-permute-start.14 = (bf16[1,192,512]{2,1,0:T(8,128)(2,1)}, bf16[1,192,512]{2,1,0:T(8,128)(2,1)}, u32[]{:S(2)}, u32[]{:S(2)}) collective-permute-start(bf16[1,192,512]{2,1,0:T(8,128)(2,1)} %get-tuple-element.31), channel_id=1, source_target_pairs={{0,4},{4,0},{1,5},{5,1},{2,6},{6,2},{3,7},{7,3},{8,12},{12,8},{9,1... | collective-permute-start | bytes 589832 | tf_op jit(solution)/shard_map/ppermute | solution.py:102
  9.1 30.2 %collective-permute-start.17 = (bf16[1,192,512]{2,1,0:T(8,128)(2,1)}, bf16[1,192,512]{2,1,0:T(8,128)(2,1)}, u32[]{:S(2)}, u32[]{:S(2)}) collective-permute-start(bf16[1,192,512]{2,1,0:T(8,128)(2,1)} %get-tuple-element.31), channel_id=1, source_target_pairs={{0,2},{1,3},{2,0},{3,1},{4,6},{5,7},{6,4},{7,5},{8,10},{9,11},{10,... | collective-permute-start | bytes 589832 | tf_op jit(solution)/shard_map/ppermute | solution.py:105
  9.1 18.9 %collective-permute-start.15 = (bf16[1,192,512]{2,1,0:T(8,128)(2,1)}, bf16[1,192,512]{2,1,0:T(8,128)(2,1)}, u32[]{:S(2)}, u32[]{:S(2)}) collective-permute-start(bf16[1,192,512]{2,1,0:T(8,128)(2,1)} %get-tuple-element.30), channel_id=1, source_target_pairs={{0,1},{1,2},{2,3},{3,0},{4,5},{5,6},{6,7},{7,4},{8,9},{9,10},{10,1... | collective-permute-start | bytes 589832 | tf_op jit(solution)/shard_map/ppermute | solution.py:105
  12.3 35.6 %copy-start.17 = (bf16[1,512,384]{2,1,0:T(8,128)(2,1)S(1)}, bf16[1,512,384]{2,1,0:T(8,128)(2,1)}, u32[]{:S(2)}) copy-start(bf16[1,512,384]{2,1,0:T(8,128)(2,1)} %param.12) | copy-start | bytes 1179652
  12.3 43.0 %copy-start.20 = (bf16[2,192,512]{2,1,0:T(8,128)(2,1)S(1)}, bf16[2,192,512]{2,1,0:T(8,128)(2,1)}, u32[]{:S(2)}) copy-start(bf16[2,192,512]{2,1,0:T(8,128)(2,1)} %get-tuple-element.25) | copy-start | bytes 1179652
  12.3 51.3 %copy-start.8 = (bf16[384,768]{1,0:T(8,128)(2,1)S(1)}, bf16[384,768]{1,0:T(8,128)(2,1)}, u32[]{:S(2)}) copy-start(bf16[384,768]{1,0:T(8,128)(2,1)} %param.17) | copy-start | bytes 1769476
  18.8 29.1 %collective-permute-start.19 = (bf16[1,192,512]{2,1,0:T(8,128)(2,1)}, bf16[1,192,512]{2,1,0:T(8,128)(2,1)S(1)}, u32[]{:S(2)}, u32[]{:S(2)}) collective-permute-start(bf16[1,192,512]{2,1,0:T(8,128)(2,1)} %get-tuple-element.30), channel_id=1, source_target_pairs={{0,3},{1,0},{2,1},{3,2},{4,7},{5,4},{6,5},{7,6},{8,11},{9,8},{10,9... | collective-permute-start | bytes 589832 | tf_op jit(solution)/shard_map/ppermute | solution.py:105
  28.0 17.5 %collective-permute-start.16 = (bf16[1,192,512]{2,1,0:T(8,128)(2,1)}, bf16[1,192,512]{2,1,0:T(8,128)(2,1)S(1)}, u32[]{:S(2)}, u32[]{:S(2)}) collective-permute-start(bf16[1,192,512]{2,1,0:T(8,128)(2,1)} %collective-permute-done.15), channel_id=1, source_target_pairs={{0,4},{4,0},{1,5},{5,1},{2,6},{6,2},{3,7},{7,3},{8,12},{12,8},{9,1... | collective-permute-start | bytes 589832 | tf_op jit(solution)/shard_map/ppermute | solution.py:102
  39.3 16.0 %collective-permute-start.8 = (bf16[2,192,512]{2,1,0:T(8,128)(2,1)}, bf16[2,192,512]{2,1,0:T(8,128)(2,1)S(1)}, u32[]{:S(2)}, u32[]{:S(2)}) collective-permute-start(bf16[2,192,512]{2,1,0:T(8,128)(2,1)} %get-tuple-element.25), channel_id=1, source_target_pairs={{0,1},{1,2},{2,3},{3,0},{4,5},{5,6},{6,7},{7,4},{8,9},{9,10},{10,1... | collective-permute-start | bytes 1179656 | tf_op jit(solution)/shard_map/ppermute | solution.py:105
  45.4 6.5 %collective-permute-start.18 = (bf16[1,192,512]{2,1,0:T(8,128)(2,1)}, bf16[1,192,512]{2,1,0:T(8,128)(2,1)S(1)}, u32[]{:S(2)}, u32[]{:S(2)}) collective-permute-start(bf16[1,192,512]{2,1,0:T(8,128)(2,1)} %collective-permute-done.17), channel_id=1, source_target_pairs={{0,4},{4,0},{1,5},{5,1},{2,6},{6,2},{3,7},{7,3},{8,12},{12,8},{9,1... | collective-permute-start | bytes 589832 | tf_op jit(solution)/shard_map/ppermute | solution.py:102
  47.9 15.7 %collective-permute-start = (bf16[512,384]{1,0:T(8,128)(2,1)S(1)}, bf16[512,384]{1,0:T(8,128)(2,1)S(1)}, u32[]{:S(2)}, u32[]{:S(2)}) collective-permute-start(bf16[512,384]{1,0:T(8,128)(2,1)S(1)} %bitcast.140), channel_id=1, source_target_pairs={{0,1},{1,0},{2,3},{3,2},{4,5},{5,4},{6,7},{7,6},{8,9},{9,8},{10,11... | collective-permute-start | bytes 1179656 | tf_op jit(solution)/shard_map/ppermute | solution.py:102
  51.9 13.2 %collective-permute-start.20 = (bf16[1,192,512]{2,1,0:T(8,128)(2,1)S(1)}, bf16[1,192,512]{2,1,0:T(8,128)(2,1)S(1)}, u32[]{:S(2)}, u32[]{:S(2)}) collective-permute-start(bf16[1,192,512]{2,1,0:T(8,128)(2,1)S(1)} %collective-permute-done.19), channel_id=1, source_target_pairs={{0,4},{4,0},{1,5},{5,1},{2,6},{6,2},{3,7},{7,3},{8,12},{12,8},{9,1... | collective-permute-start | bytes 589832 | tf_op jit(solution)/shard_map/ppermute | solution.py:102
  55.3 15.5 %collective-permute-start.12 = (bf16[2,192,512]{2,1,0:T(8,128)(2,1)S(1)}, bf16[2,192,512]{2,1,0:T(8,128)(2,1)S(1)}, u32[]{:S(2)}, u32[]{:S(2)}) collective-permute-start(bf16[2,192,512]{2,1,0:T(8,128)(2,1)S(1)} %copy-done.20), channel_id=1, source_target_pairs={{0,3},{1,0},{2,1},{3,2},{4,7},{5,4},{6,5},{7,6},{8,11},{9,8},{10,9... | collective-permute-start | bytes 1179656 | tf_op jit(solution)/shard_map/ppermute | solution.py:105
  63.6 16.3 %collective-permute-start.5 = (bf16[384,768]{1,0:T(8,128)(2,1)S(1)}, bf16[384,768]{1,0:T(8,128)(2,1)S(1)}, u32[]{:S(2)}, u32[]{:S(2)}) collective-permute-start(bf16[384,768]{1,0:T(8,128)(2,1)S(1)} %copy-done.8), channel_id=1, source_target_pairs={{0,16},{8,24},{16,0},{24,8},{1,17},{9,25},{17,1},{25,9},{2,18},{10... | collective-permute-start | bytes 1769480 | tf_op jit(solution)/shard_map/ppermute | solution.py:102
  65.1 16.3 %collective-permute-start.9 = (bf16[2,192,512]{2,1,0:T(8,128)(2,1)S(1)}, bf16[2,192,512]{2,1,0:T(8,128)(2,1)S(1)}, u32[]{:S(2)}, u32[]{:S(2)}) collective-permute-start(bf16[2,192,512]{2,1,0:T(8,128)(2,1)S(1)} %collective-permute-done.8), channel_id=1, source_target_pairs={{0,4},{4,0},{1,5},{5,1},{2,6},{6,2},{3,7},{7,3},{8,12},{12,8},{9,1... | collective-permute-start | bytes 1179656 | tf_op jit(solution)/shard_map/ppermute | solution.py:102
  66.8 26.5 %collective-permute-start.2 = (bf16[1024,384]{1,0:T(8,128)(2,1)S(1)}, bf16[1024,384]{1,0:T(8,128)(2,1)S(1)}, u32[]{:S(2)}, u32[]{:S(2)}) collective-permute-start(bf16[1024,384]{1,0:T(8,128)(2,1)S(1)} %get-tuple-element.27), channel_id=1, source_target_pairs={{0,16},{8,24},{16,0},{24,8},{1,17},{9,25},{17,1},{25,9},{2,18},{10... | collective-permute-start | bytes 2359304 | tf_op jit(solution)/shard_map/ppermute | solution.py:102
  67.4 18.2 %collective-permute-start.11 = (bf16[2,192,512]{2,1,0:T(8,128)(2,1)}, bf16[2,192,512]{2,1,0:T(8,128)(2,1)S(1)}, u32[]{:S(2)}, u32[]{:S(2)}) collective-permute-start(bf16[2,192,512]{2,1,0:T(8,128)(2,1)} %collective-permute-done.10), channel_id=1, source_target_pairs={{0,4},{4,0},{1,5},{5,1},{2,6},{6,2},{3,7},{7,3},{8,12},{12,8},{9,1... | collective-permute-start | bytes 1179656 | tf_op jit(solution)/shard_map/ppermute | solution.py:102
  70.7 19.6 %collective-permute-start.4 = (bf16[384,768]{1,0:T(8,128)(2,1)S(1)}, bf16[384,768]{1,0:T(8,128)(2,1)S(1)}, u32[]{:S(2)}, u32[]{:S(2)}) collective-permute-start(bf16[384,768]{1,0:T(8,128)(2,1)S(1)} %copy-done.8), channel_id=1, source_target_pairs={{0,8},{8,0},{16,24},{24,16},{1,9},{9,1},{17,25},{25,17},{2,10},{10... | collective-permute-start | bytes 1769480 | tf_op jit(solution)/shard_map/ppermute | solution.py:102
  79.9 10.4 %collective-permute-start.13 = (bf16[2,192,512]{2,1,0:T(8,128)(2,1)S(1)}, bf16[2,192,512]{2,1,0:T(8,128)(2,1)S(1)}, u32[]{:S(2)}, u32[]{:S(2)}) collective-permute-start(bf16[2,192,512]{2,1,0:T(8,128)(2,1)S(1)} %collective-permute-done.12), channel_id=1, source_target_pairs={{0,4},{4,0},{1,5},{5,1},{2,6},{6,2},{3,7},{7,3},{8,12},{12,8},{9,1... | collective-permute-start | bytes 1179656 | tf_op jit(solution)/shard_map/ppermute | solution.py:102
  81.4 11.9 %collective-permute-start.6 = (bf16[384,768]{1,0:T(8,128)(2,1)S(1)}, bf16[384,768]{1,0:T(8,128)(2,1)S(1)}, u32[]{:S(2)}, u32[]{:S(2)}) collective-permute-start(bf16[384,768]{1,0:T(8,128)(2,1)S(1)} %collective-permute-done.5), channel_id=1, source_target_pairs={{0,8},{8,0},{16,24},{24,16},{1,9},{9,1},{17,25},{25,17},{2,10},{10... | collective-permute-start | bytes 1769480 | tf_op jit(solution)/shard_map/ppermute | solution.py:102
  85.6 21.9 %collective-permute-start.36 = (s32[2,4]{1,0:T(2,128)}, s32[2,4]{1,0:T(2,128)S(1)}, u32[]{:S(2)}, u32[]{:S(2)}) collective-permute-start(s32[2,4]{1,0:T(2,128)} %pad_add_fusion), channel_id=1, source_target_pairs={{0,16},{8,24},{16,0},{24,8},{1,17},{9,25},{17,1},{25,9},{2,18},{10... | collective-permute-start | bytes 104 | tf_op jit(solution)/shard_map/ppermute | solution.py:102
  90.3 17.6 %collective-permute-start.35 = (s32[2,4]{1,0:T(2,128)}, s32[2,4]{1,0:T(2,128)S(1)}, u32[]{:S(2)}, u32[]{:S(2)}) collective-permute-start(s32[2,4]{1,0:T(2,128)} %pad_add_fusion), channel_id=1, source_target_pairs={{0,8},{8,0},{16,24},{24,16},{1,9},{9,1},{17,25},{25,17},{2,10},{10... | collective-permute-start | bytes 104 | tf_op jit(solution)/shard_map/ppermute | solution.py:102
  90.3 24.8 %collective-permute-start.30 = (bf16[3,768,192]{1,2,0:T(8,128)(2,1)}, bf16[3,768,192]{1,2,0:T(8,128)(2,1)}, u32[]{:S(2)}, u32[]{:S(2)}) collective-permute-start(bf16[3,768,192]{1,2,0:T(8,128)(2,1)} %param.19), channel_id=1, source_target_pairs={{0,16},{8,24},{16,0},{24,8},{1,17},{9,25},{17,1},{25,9},{2,18},{10... | collective-permute-start | bytes 2654216 | tf_op jit(solution)/shard_map/ppermute | solution.py:102
  93.3 2.5 %collective-permute-start.1 = (bf16[1024,384]{1,0:T(8,128)(2,1)S(1)}, bf16[1024,384]{1,0:T(8,128)(2,1)S(1)}, u32[]{:S(2)}, u32[]{:S(2)}) collective-permute-start(bf16[1024,384]{1,0:T(8,128)(2,1)S(1)} %get-tuple-element.27), channel_id=1, source_target_pairs={{0,8},{8,0},{16,24},{24,16},{1,9},{9,1},{17,25},{25,17},{2,10},{10... | collective-permute-start | bytes 2359304 | tf_op jit(solution)/shard_map/ppermute | solution.py:102
  93.3 3.4 %collective-permute-start.3 = (bf16[1024,384]{1,0:T(8,128)(2,1)S(1)}, bf16[1024,384]{1,0:T(8,128)(2,1)S(1)}, u32[]{:S(2)}, u32[]{:S(2)}) collective-permute-start(bf16[1024,384]{1,0:T(8,128)(2,1)S(1)} %collective-permute-done.2), channel_id=1, source_target_pairs={{0,8},{8,0},{16,24},{24,16},{1,9},{9,1},{17,25},{25,17},{2,10},{10... | collective-permute-start | bytes 2359304 | tf_op jit(solution)/shard_map/ppermute | solution.py:102
  95.8 49.4 %collective-permute-start.29 = (bf16[3,768,192]{1,2,0:T(8,128)(2,1)}, bf16[3,768,192]{1,2,0:T(8,128)(2,1)}, u32[]{:S(2)}, u32[]{:S(2)}) collective-permute-start(bf16[3,768,192]{1,2,0:T(8,128)(2,1)} %param.19), channel_id=1, source_target_pairs={{0,8},{8,0},{16,24},{24,16},{1,9},{9,1},{17,25},{25,17},{2,10},{10... | collective-permute-start | bytes 2654216 | tf_op jit(solution)/shard_map/ppermute | solution.py:102
  105.7 2.5 %collective-permute-start.21 = (bf16[2,2,128,768]{3,2,1,0:T(8,128)(2,1)}, bf16[2,2,128,768]{3,2,1,0:T(8,128)(2,1)S(1)}, u32[]{:S(2)}, u32[]{:S(2)}) collective-permute-start(bf16[2,2,128,768]{3,2,1,0:T(8,128)(2,1)} %convolution_convert_fusion), channel_id=1, source_target_pairs={{0,8},{8,0},{16,24},{24,16},{1,9},{9,1},{17,25},{25,17},{2,10},{10... | collective-permute-start | bytes 2359304 | tf_op jit(solution)/shard_map/ppermute | solution.py:102
  107.5 7.0 %collective-permute-start.37 = (s32[2,4]{1,0:T(2,128)S(1)}, s32[2,4]{1,0:T(2,128)S(1)}, u32[]{:S(2)}, u32[]{:S(2)}) collective-permute-start(s32[2,4]{1,0:T(2,128)S(1)} %collective-permute-done.36), channel_id=1, source_target_pairs={{0,8},{8,0},{16,24},{24,16},{1,9},{9,1},{17,25},{25,17},{2,10},{10... | collective-permute-start | bytes 104 | tf_op jit(solution)/shard_map/ppermute | solution.py:102
  110.3 14.0 %copy-start.10 = (bf16[384,768]{1,0:T(8,128)(2,1)S(1)}, bf16[384,768]{1,0:T(8,128)(2,1)}, u32[]{:S(2)}) copy-start(bf16[384,768]{1,0:T(8,128)(2,1)} %copy-done.9) | copy-start | bytes 1769476
  110.4 11.6 %collective-permute-start.22 = (bf16[128,768]{1,0:T(8,128)(2,1)S(1)}, bf16[128,768]{1,0:T(8,128)(2,1)S(1)}, u32[]{:S(2)}, u32[]{:S(2)}) collective-permute-start(bf16[128,768]{1,0:T(8,128)(2,1)S(1)} %get-tuple-element.28), channel_id=1, source_target_pairs={{0,16},{8,24},{16,0},{24,8},{1,17},{9,25},{17,1},{25,9},{2,18},{10... | collective-permute-start | bytes 589832 | tf_op jit(solution)/shard_map/ppermute | solution.py:102
  112.4 9.6 %collective-permute-start.24 = (bf16[128,768]{1,0:T(8,128)(2,1)S(1)}, bf16[128,768]{1,0:T(8,128)(2,1)S(1)}, u32[]{:S(2)}, u32[]{:S(2)}) collective-permute-start(bf16[128,768]{1,0:T(8,128)(2,1)S(1)} %get-tuple-element.29), channel_id=1, source_target_pairs={{0,17},{1,16},{2,19},{3,18},{8,25},{9,24},{10,27},{11,26},{16,1},{... | collective-permute-start | bytes 589832 | tf_op jit(solution)/shard_map/ppermute | solution.py:102
  114.4 9.8 %collective-permute-start.23 = (bf16[128,768]{1,0:T(8,128)(2,1)S(1)}, bf16[128,768]{1,0:T(8,128)(2,1)S(1)}, u32[]{:S(2)}, u32[]{:S(2)}) collective-permute-start(bf16[128,768]{1,0:T(8,128)(2,1)S(1)} %fusion.23), channel_id=1, source_target_pairs={{0,1},{1,0},{2,3},{3,2},{4,5},{5,4},{6,7},{7,6},{8,9},{9,8},{10,11... | collective-permute-start | bytes 589832 | tf_op jit(solution)/shard_map/ppermute | solution.py:102
  115.1 31.6 %collective-permute-start.31 = (bf16[3,768,192]{1,2,0:T(8,128)(2,1)}, bf16[3,768,192]{1,2,0:T(8,128)(2,1)}, u32[]{:S(2)}, u32[]{:S(2)}) collective-permute-start(bf16[3,768,192]{1,2,0:T(8,128)(2,1)} %collective-permute-done.30), channel_id=1, source_target_pairs={{0,8},{8,0},{16,24},{24,16},{1,9},{9,1},{17,25},{25,17},{2,10},{10... | collective-permute-start | bytes 2654216 | tf_op jit(solution)/shard_map/ppermute | solution.py:102
  115.3 18.2 %copy-start = (bf16[192,768]{1,0:T(8,128)(2,1)S(1)}, bf16[192,768]{1,0:T(8,128)(2,1)}, u32[]{:S(2)}) copy-start(bf16[192,768]{1,0:T(8,128)(2,1)} %refs_8_.1) | copy-start | bytes 884740
  125.3 14.4 %copy-start.27 = (s32[4]{0:T(128)S(1)}, s32[4]{0:T(128)}, u32[]{:S(2)}) copy-start(s32[4]{0:T(128)} %iota_add_fusion.1) | copy-start | bytes 52
  125.3 14.4 %copy-start.28 = (s32[4]{0:T(128)S(1)}, s32[4]{0:T(128)}, u32[]{:S(2)}) copy-start(s32[4]{0:T(128)} %iota_add_fusion.2) | copy-start | bytes 52
  125.6 7.9 %collective-permute-start.25 = (bf16[128,768]{1,0:T(8,128)(2,1)S(1)}, bf16[128,768]{1,0:T(8,128)(2,1)S(1)}, u32[]{:S(2)}, u32[]{:S(2)}) collective-permute-start(bf16[128,768]{1,0:T(8,128)(2,1)S(1)} %multiply_convert_fusion.1.refs_1_), channel_id=1, source_target_pairs={{0,16},{8,24},{16,0},{24,8},{1,17},{9,25},{17,1},{25,9},{2,18},{10... | collective-permute-start | bytes 589832 | tf_op jit(solution)/shard_map/ppermute | solution.py:102
  126.4 7.7 %collective-permute-start.26 = (bf16[128,768]{1,0:T(8,128)(2,1)S(1)}, bf16[128,768]{1,0:T(8,128)(2,1)S(1)}, u32[]{:S(2)}, u32[]{:S(2)}) collective-permute-start(bf16[128,768]{1,0:T(8,128)(2,1)S(1)} %multiply_convert_fusion.1.refs_1_), channel_id=1, source_target_pairs={{0,4},{4,0},{1,5},{5,1},{2,6},{6,2},{3,7},{7,3},{8,12},{12,8},{9,1... | collective-permute-start | bytes 589832 | tf_op jit(solution)/shard_map/ppermute | solution.py:102
  128.0 10.8 %collective-permute-start.27 = (bf16[128,768]{1,0:T(8,128)(2,1)S(1)}, bf16[128,768]{1,0:T(8,128)(2,1)S(1)}, u32[]{:S(2)}, u32[]{:S(2)}) collective-permute-start(bf16[128,768]{1,0:T(8,128)(2,1)S(1)} %multiply_convert_fusion.1.refs_1_), channel_id=1, source_target_pairs={{0,20},{4,16},{8,28},{12,24},{16,4},{20,0},{24,12},{28,8},{1,21},{... | collective-permute-start | bytes 589832 | tf_op jit(solution)/shard_map/ppermute | solution.py:102
  133.6 9.1 %collective-permute-start.33 = (bf16[192,768]{1,0:T(8,128)(2,1)S(1)}, bf16[192,768]{1,0:T(8,128)(2,1)}, u32[]{:S(2)}, u32[]{:S(2)}) collective-permute-start(bf16[192,768]{1,0:T(8,128)(2,1)S(1)} %copy-done), channel_id=1, source_target_pairs={{0,16},{8,24},{16,0},{24,8},{1,17},{9,25},{17,1},{25,9},{2,18},{10... | collective-permute-start | bytes 884744 | tf_op jit(solution)/shard_map/ppermute | solution.py:102
  134.1 16.1 %collective-permute-start.32 = (bf16[192,768]{1,0:T(8,128)(2,1)S(1)}, bf16[192,768]{1,0:T(8,128)(2,1)}, u32[]{:S(2)}, u32[]{:S(2)}) collective-permute-start(bf16[192,768]{1,0:T(8,128)(2,1)S(1)} %copy-done), channel_id=1, source_target_pairs={{0,8},{8,0},{16,24},{24,16},{1,9},{9,1},{17,25},{25,17},{2,10},{10... | collective-permute-start | bytes 884744 | tf_op jit(solution)/shard_map/ppermute | solution.py:102
  139.7 10.6 %collective-permute-start.28 = (bf16[4,128,768]{2,1,0:T(8,128)(2,1)}, bf16[4,128,768]{2,1,0:T(8,128)(2,1)}, u32[]{:S(2)}, u32[]{:S(2)}) collective-permute-start(bf16[4,128,768]{2,1,0:T(8,128)(2,1)} %pad_maximum_fusion.5), channel_id=1, source_target_pairs={{0,8},{8,0},{16,24},{24,16},{1,9},{9,1},{17,25},{25,17},{2,10},{10... | collective-permute-start | bytes 2359304 | tf_op jit(solution)/shard_map/ppermute | solution.py:102
  142.7 7.6 %collective-permute-start.34 = (bf16[192,768]{1,0:T(8,128)(2,1)}, bf16[192,768]{1,0:T(8,128)(2,1)}, u32[]{:S(2)}, u32[]{:S(2)}) collective-permute-start(bf16[192,768]{1,0:T(8,128)(2,1)} %collective-permute-done.33.refs_10_), channel_id=1, source_target_pairs={{0,8},{8,0},{16,24},{24,16},{1,9},{9,1},{17,25},{25,17},{2,10},{10... | collective-permute-start | bytes 884744 | tf_op jit(solution)/shard_map/ppermute | solution.py:102
  161.6 2.0 %collective-permute-start.38 = (bf16[128,192]{1,0:T(8,128)(2,1)S(1)}, bf16[128,192]{1,0:T(8,128)(2,1)S(1)}, u32[]{:S(2)}, u32[]{:S(2)}) collective-permute-start(bf16[128,192]{1,0:T(8,128)(2,1)S(1)} %get-tuple-element.39), channel_id=1, source_target_pairs={{0,8},{8,0},{16,24},{24,16},{1,9},{9,1},{17,25},{25,17},{2,10},{10... | collective-permute-start | bytes 147464 | tf_op jit(solution)/shard_map/ppermute | solution.py:102
  162.2 4.8 %collective-permute-start.39 = (bf16[128,192]{1,0:T(8,128)(2,1)S(1)}, bf16[128,192]{1,0:T(8,128)(2,1)S(1)}, u32[]{:S(2)}, u32[]{:S(2)}) collective-permute-start(bf16[128,192]{1,0:T(8,128)(2,1)S(1)} %get-tuple-element.38), channel_id=1, source_target_pairs={{0,16},{8,24},{16,0},{24,8},{1,17},{9,25},{17,1},{25,9},{2,18},{10... | collective-permute-start | bytes 147464 | tf_op jit(solution)/shard_map/ppermute | solution.py:102
  162.5 4.4 %collective-permute-start.40 = (bf16[128,192]{1,0:T(8,128)(2,1)S(1)}, bf16[128,192]{1,0:T(8,128)(2,1)S(1)}, u32[]{:S(2)}, u32[]{:S(2)}) collective-permute-start(bf16[128,192]{1,0:T(8,128)(2,1)S(1)} %get-tuple-element.37), channel_id=1, source_target_pairs={{0,24},{8,16},{16,8},{24,0},{1,25},{9,17},{17,9},{25,1},{2,26},{10... | collective-permute-start | bytes 147464 | tf_op jit(solution)/shard_map/ppermute | solution.py:102
  (23 other events, 161.3 us)

commit v2 on v1

v2 whole, which is shorter than its diff:
```python
import math

import jax
import jax.numpy as jnp
from jax import lax
from jax.experimental import pallas as pl
from jax.experimental.pallas import tpu as pltpu
from jax.sharding import PartitionSpec as P

NEG = -1e30
AXES = ("section", "seq", "dp")


def layer_norm(rows, gain):
    mean = jnp.mean(rows, axis=-1, keepdims=True)
    centered = rows - mean
    var = jnp.mean(centered * centered, axis=-1, keepdims=True)
    return centered * lax.rsqrt(var + 1e-06) * gain


def slide_place(lengths_row, index):
    ends = jnp.cumsum(lengths_row, dtype=jnp.int32)
    after = index[:, None] >= ends[None, :]
    slide = jnp.sum(after.astype(jnp.int32), axis=1, dtype=jnp.int32)
    before = jnp.sum(jnp.where(after, lengths_row[None, :], 0), axis=1, dtype=jnp.int32)
    return (slide, index - before)


def attend_kernel(sec_ref, mine_ref, *refs, heads, size):
    near, (far_ref, w_ref, emb_ref, q_ref, k_ref, out_ref) = refs[:-6], refs[-6:]
    parts, _, width, _ = w_ref.shape
    rows = mine_ref.shape[0]
    mine = mine_ref[...]
    keys = jnp.concatenate(
        [mine] + [ref[...] for ref in near] + [far_ref[i] for i in range(far_ref.shape[0])], axis=0
    )
    count = keys.shape[0]
    scale = math.log2(math.e) / math.sqrt(size)

    def project(x, which):
        matrix = jnp.concatenate([w_ref[m, which] for m in range(parts)], axis=0)
        return lax.dot_general(
            x, matrix, (((1,), (1,)), ((), ())), preferred_element_type=jnp.float32
        ).astype(jnp.bfloat16)

    query, key, value = project(mine, 0), project(keys, 1), project(keys, 2)
    out_matrix = jnp.concatenate([w_ref[m, 3] for m in range(parts)], axis=0)
    diag = lax.broadcasted_iota(jnp.int32, (rows, count), 0) == lax.broadcasted_iota(
        jnp.int32, (rows, count), 1
    )
    total = emb_ref[...]
    for m in range(parts):
        lo = m * width // 128 * 128
        hi = -(-(m + 1) * width // 128) * 128
        lane_head = (lax.broadcasted_iota(jnp.int32, (rows, hi - lo), 1) + lo) // size
        q_part = query[:, lo:hi]
        split = jnp.concatenate(
            [
                jnp.where(lane_head == m * heads + h, q_part, jnp.zeros_like(q_part))
                for h in range(heads)
            ],
            axis=0,
        )
        scores = lax.dot_general(
            split, key[:, lo:hi], (((1,), (1,)), ((), ())), preferred_element_type=jnp.float32
        )
        weights, sums = [], []
        for h in range(heads):
            at = m * heads + h
            ok = (q_ref[:, at : at + 1] == k_ref[at : at + 1, :]) | diag
            own = jnp.where(ok, scores[h * rows : (h + 1) * rows], NEG)
            top = jnp.max(own, axis=1, keepdims=True)
            weight = jnp.exp2((own - top) * scale)
            sums.append(jnp.sum(weight, axis=1, keepdims=True))
            weights.append(weight.astype(jnp.bfloat16))
        mixed = jnp.dot(
            jnp.concatenate(weights, axis=0), value[:, lo:hi], preferred_element_type=jnp.float32
        )
        att = jnp.zeros((rows, hi - lo), jnp.float32)
        for h in range(heads):
            att = jnp.where(
                lane_head == m * heads + h, mixed[h * rows : (h + 1) * rows] / sums[h], att
            )
        total = total + jnp.dot(
            att.astype(jnp.bfloat16), out_matrix[lo:hi], preferred_element_type=jnp.float32
        )
    for j in range(parts):
        out_ref[j ^ sec_ref[0]] = total[:, j * width : (j + 1) * width].astype(out_ref.dtype)


def build(n_sec, n_seq, n_dp):
    sizes = {"section": n_sec, "seq": n_seq, "dp": n_dp}

    def flip(x, **masks):
        names = tuple(a for a in AXES if masks.get(a))
        pairs = []
        total = math.prod(sizes[a] for a in names)
        for source in range(total):
            rest, coords = source, []
            for a in reversed(names):
                coords.append(rest % sizes[a])
                rest //= sizes[a]
            target = 0
            for a, c in zip(names, reversed(coords)):
                target = target * sizes[a] + (c ^ masks[a])
            pairs.append((source, target))
        return lax.ppermute(x, names if len(names) > 1 else names[0], pairs)

    def rotate(x, k):
        return lax.ppermute(x, "dp", [(i, (i + k) % n_dp) for i in range(n_dp)])

    def gather_section(x):
        across = flip(x, section=2)
        return [x, flip(x, section=1), across, flip(across, section=1)]

    def gather_rows(same, other, seq_at, dp_at):
        got = {0: same}
        mats, rows, units = same.shape
        last = n_dp // 2
        for k in [k for k in range(1, n_dp) if k != last] + [last]:
            block = other if k % 2 else same
            if k == last and n_dp > 2:
                block, got[1] = lax.optimization_barrier((block, got[1]))
            got[k] = rotate(block, k)
        if n_seq == 2:
            whole = jnp.zeros((mats, n_seq * n_dp * rows, units), same.dtype)
            for k, block in got.items():
                z = (dp_at - k) % n_dp
                theirs = flip(block, seq=1)
                whole = lax.dynamic_update_slice(whole, block, (0, (seq_at * n_dp + z) * rows, 0))
                whole = lax.dynamic_update_slice(
                    whole, theirs, (0, ((1 - seq_at) * n_dp + z) * rows, 0)
                )
            return whole
        part = jnp.zeros((mats, n_dp * rows, units), same.dtype)
        for k, block in got.items():
            part = lax.dynamic_update_slice(part, block, (0, ((dp_at - k) % n_dp) * rows, 0))
        return lax.all_gather(part, "seq", axis=1, tiled=True)

    def per_device(
        tile_feats,
        tile_gain,
        w_gate,
        w_up,
        w_down,
        w_proj,
        slide_gain,
        w_qkv,
        w_out,
        lengths,
        seg_len,
        rate,
    ):
        sec = lax.axis_index("section")
        seq_at = lax.axis_index("seq")
        dp_at = lax.axis_index("dp")
        core, side, odd = sec % 2, sec // 2, dp_at % 2
        mine = tile_feats[0]
        tokens, feats = mine.shape
        own_rows = tokens // n_sec
        half = w_gate.shape[1] // 2

        def absolute(blocks):
            stacked = jnp.stack(blocks)
            return [lax.dynamic_index_in_dim(stacked, sec ^ j, 0, False) for j in range(n_sec)]

        both = jnp.concatenate([mine, flip(mine, dp=1)], axis=0)
        rows = jnp.concatenate(absolute(gather_section(both)), axis=1)

        matrices = jnp.stack([w_gate, w_up, w_down.T])

        def halves(which):
            return lax.dynamic_slice_in_dim(matrices, which * half, half, 2)

        units = gather_rows(halves(odd), halves(1 - odd), seq_at, dp_at)

        proj = lax.all_gather(w_proj, "section", axis=0, tiled=True)
        slide_w = jnp.concatenate([jnp.swapaxes(w_qkv, 1, 2), w_out[None]], axis=0)
        slide_w = lax.all_gather(slide_w, "section", axis=0)
        head_info = lax.all_gather(jnp.stack([seg_len, rate]), "section", axis=1, tiled=True)

        normed = layer_norm(rows.astype(jnp.float32), tile_gain).astype(jnp.bfloat16)
        gate = jnp.dot(normed, units[0], preferred_element_type=jnp.float32)
        up = jnp.dot(normed, units[1], preferred_element_type=jnp.float32)
        hidden = (jax.nn.silu(gate) * up).astype(jnp.bfloat16)
        hidden = hidden.reshape(2, n_sec // 2, 2, own_rows, half)
        folded = lax.dot_general(
            proj, units[2], (((0,), (0,)), ((), ())), preferred_element_type=jnp.float32
        ).astype(jnp.bfloat16)

        def project(x):
            return lax.dot_general(
                x, folded, (((x.ndim - 1,), (1,)), ((), ())), preferred_element_type=jnp.float32
            )

        send = project(lax.dynamic_index_in_dim(hidden, 1 - core, 2, False)).astype(jnp.bfloat16)
        got = flip(send, section=1)
        kept = project(lax.dynamic_index_in_dim(hidden, core, 2, False)) + got.astype(jnp.float32)
        here = lax.dynamic_index_in_dim(kept, side, 1, False)
        there = lax.dynamic_index_in_dim(kept, 1 - side, 1, False).astype(jnp.bfloat16)
        from_x = flip(there[0], section=2)
        from_z = flip(here[1].astype(jnp.bfloat16), dp=1)
        from_xz = flip(there[1], section=2, dp=1)
        residual = jnp.dot(
            lax.dynamic_slice_in_dim(rows[:tokens], sec * own_rows, own_rows, 0),
            proj,
            preferred_element_type=jnp.float32,
        )
        emb = (
            residual
            + here[0]
            + from_x.astype(jnp.float32)
            + from_z.astype(jnp.float32)
            + from_xz.astype(jnp.float32)
        )
        slide_normed = layer_norm(emb, slide_gain).astype(jnp.bfloat16)

        my_start = seq_at * tokens + sec * own_rows
        span = jnp.arange(own_rows, dtype=jnp.int32)
        if n_seq == 2:
            near = [
                flip(slide_normed, section=2),
                flip(slide_normed, seq=1),
                flip(slide_normed, section=2, seq=1),
            ]
            far = flip(jnp.stack([slide_normed] + near), section=1)
            order = [(s, q) for s in (0, 1) for q in ((0, 0), (2, 0), (0, 1), (2, 1))]
            starts = [(seq_at ^ q[1]) * tokens + (sec ^ q[0] ^ s) * own_rows for s, q in order]
            k_idx = jnp.concatenate([start + span for start in starts])
        else:
            every = lax.all_gather(slide_normed, ("seq", "section"), axis=0, tiled=True)
            count = every.shape[0]
            keys = jnp.concatenate([slide_normed, jnp.roll(every, -my_start, axis=0)[own_rows:]])
            k_idx = (my_start + jnp.arange(count, dtype=jnp.int32)) % count
        count = k_idx.shape[0]

        local_heads = seg_len.shape[0]
        seg_all, rate_all = head_info[0], head_info[1]
        heads = jnp.arange(n_sec * local_heads, dtype=jnp.int32)
        slide, pos = slide_place(lengths[0], k_idx)
        block = slide[None, :] * count + pos[None, :] // seg_all[:, None]
        picked = pos[None, :] % rate_all[:, None] == (heads % rate_all)[:, None]
        k_code = jnp.where(picked, block, -1)
        q_code = block[:, :own_rows].T

        width = w_qkv.shape[2]
        size = width // local_heads
        if n_seq == 2:
            vmem = pl.BlockSpec(memory_space=pltpu.VMEM)
            final = pl.pallas_call(
                lambda *refs: attend_kernel(*refs, heads=local_heads, size=size),
                out_shape=jax.ShapeDtypeStruct((n_sec, own_rows, width), jnp.bfloat16),
                in_specs=[pl.BlockSpec(memory_space=pltpu.SMEM)] + [vmem] * 9,
                out_specs=vmem,
                compiler_params=pltpu.CompilerParams(vmem_limit_bytes=48 * 2**20),
                cost_estimate=pl.CostEstimate(
                    flops=2 * n_sec * count * width * (2 * 768 + 2 * local_heads * own_rows),
                    bytes_accessed=8 * 2**20,
                    transcendentals=n_sec * local_heads * own_rows * count,
                ),
            )(sec[None], slide_normed, *near, far, slide_w, emb, q_code, k_code)
        else:
            total = emb
            for m in range(n_sec):
                at = slice(m * local_heads, (m + 1) * local_heads)

                def by_head(x, matrix):
                    x = jnp.dot(x, matrix.T, preferred_element_type=jnp.float32)
                    return x.astype(jnp.bfloat16).reshape(-1, local_heads, size).transpose(1, 0, 2)

                def one_head(args):
                    q, k, v, q_row, k_row = args
                    scores = jnp.dot(q, k.T, preferred_element_type=jnp.float32) / math.sqrt(size)
                    diag = jnp.arange(own_rows)[:, None] == jnp.arange(count)[None, :]
                    ok = (q_row[:, None] == k_row[None, :]) | diag
                    weight = jax.nn.softmax(jnp.where(ok, scores, NEG), axis=-1)
                    return jnp.dot(weight, v, preferred_element_type=jnp.float32)

                att = lax.map(
                    one_head,
                    (
                        by_head(slide_normed, slide_w[m, 0]),
                        by_head(keys, slide_w[m, 1]),
                        by_head(keys, slide_w[m, 2]),
                        q_code.T[at],
                        k_code[at],
                    ),
                )
                att = att.transpose(1, 0, 2).reshape(own_rows, width).astype(jnp.bfloat16)
                total = total + jnp.dot(att, slide_w[m, 3], preferred_element_type=jnp.float32)
            cut = total.astype(jnp.bfloat16).reshape(own_rows, n_sec, width).transpose(1, 0, 2)
            final = jnp.stack(
                [lax.dynamic_index_in_dim(cut, sec ^ m, 0, False) for m in range(n_sec)]
            )

        pieces = [final[0]] + [flip(final[m], section=m) for m in range(1, n_sec)]
        return jnp.concatenate(absolute(pieces), axis=0)[None]

    return per_device


def solution(mesh):
    placed = (
        P("dp", "seq", "section"),
        P(),
        P(("seq", "dp"), "section"),
        P(("seq", "dp"), "section"),
        P("section", ("seq", "dp")),
        P("section", None),
        P(),
        P(None, None, "section"),
        P("section", None),
        P("dp", None),
        P("section"),
        P("section"),
    )
    shape = mesh.shape
    return jax.shard_map(
        build(shape["section"], shape["seq"], shape["dp"]),
        mesh=mesh,
        in_specs=placed,
        out_specs=P("dp", "seq", "section"),
        check_vma=False,
    )
```

time: 169 us -> 165 us (0.976)
  starting transfers between devices: 47.6 us -> 24 us
  between operations: 0.83 us -> 14 us
  blocking collectives: 0 us -> 5.25 us
  matrix products: 9.83 us -> 14.9 us
  other arithmetic: 12.9 us -> 10.2 us
    ppermute x6 -> x3, waiting for transfers between devices: 17.8 us -> 36.8 us  [rotate(): return lax.ppermute(x, 'dp', [(i, (i + k) % n_dp) for i in range(n_dp)])]
    ppermute x35 -> x19, waiting for transfers between devices: 51.7 us -> 32.7 us  [flip(): return lax.ppermute(x, names if len(names) > 1 else names[0], pairs)]
    ppermute x6 -> x3, starting transfers between devices: 18.1 us -> 3.83 us  [rotate(): return lax.ppermute(x, 'dp', [(i, (i + k) % n_dp) for i in range(n_dp)])]
    ppermute x35 -> x19, starting transfers between devices: 29.4 us -> 20.1 us  [flip(): return lax.ppermute(x, names if len(names) > 1 else names[0], pairs)]
    ppermute x3 -> x0, local copies, waits for them, and re-layouts: 6.22 us -> none  [flip(): return lax.ppermute(x, names if len(names) > 1 else names[0], pairs)]
    dot_general x5, matrix products: 8.82 us -> 14.4 us  [the longest x1 4.41 us: per_device(): up = jnp.dot(normed, units[1], preferred_element_type=jnp.float32)]
    all_gather x0 -> x1, blocking collectives: none -> 5.25 us  [per_device(): lax.all_gather(jnp.stack([seg_len, rate]), 'section', axis=1, tiled=True)]
    dynamic_update_slice x8 -> x4, local copies, waits for them, and re-layouts: 2.1 us -> 4.52 us  [gather_rows(): lax.dynamic_update_slice(whole, theirs, (0, ((1 - seq_at) * n_dp + z) * r...]
  transfers between devices with their start and end apart: 41 -> 24, of which waited for: 19 -> 12; matrix products, arithmetic and copies ran while one was open for 21% -> 23% of each run, Pallas kernels for 0% -> 0%
where the time goes in v2:
time: 165 us
  waiting for transfers between devices  70.3 us (43%)
  starting transfers between devices  24 us (15%)
  local copies, waits for them, and re-layouts  15.5 us (9%)
  matrix products  14.9 us (9%)
  between operations  14 us (8%)
  Pallas kernels  10.5 us (6%)
  other arithmetic  10.2 us (6%)
  blocking collectives  5.25 us (3%)
    ppermute x3, waiting for transfers between devices, rotate(): return lax.ppermute(x, 'dp', [(i, (i + k) % n_dp) for i in range(n_dp)])  36.8 us
    ppermute x19, waiting for transfers between devices, flip(): return lax.ppermute(x, names if len(names) > 1 else names[0], pairs)  32.7 us
    ppermute x19, starting transfers between devices, flip(): return lax.ppermute(x, names if len(names) > 1 else names[0], pairs)  20.1 us
    pallas_call x1, Pallas kernels, per_device(): pl.pallas_call(lambda *refs: attend_kernel(*refs, heads=local_heads, size...  10.5 us
    all_gather x1, blocking collectives, per_device(): lax.all_gather(jnp.stack([seg_len, rate]), 'section', axis=1, tiled=True)  5.25 us
    dynamic_update_slice x4, local copies, waits for them, and re-layouts, gather_rows(): lax.dynamic_update_slice(whole, block, (0, (seq_at * n_dp + z) * rows, 0))  5.09 us
    dynamic_update_slice x4, local copies, waits for them, and re-layouts, gather_rows(): lax.dynamic_update_slice(whole, theirs, (0, ((1 - seq_at) * n_dp + z) * r...  4.52 us
    dot_general x1, matrix products, per_device(): up = jnp.dot(normed, units[1], preferred_element_type=jnp.float32)  4.41 us
  transfers between devices with their start and end apart: 24, of which 12 were waited for; matrix products, arithmetic and copies ran while one was open for 23% of the time, Pallas kernels for 0%

profile of v2, /device:TPU:0, one launch (start us, length us, event | category | flops | bytes accessed | tf_op | source)
XLA Modules:
  0.0 164.6 jit_solution(10953732961456606689)
XLA Ops:
  7.3 3.1 %collective-permute-start = (bf16[512,384]{1,0:T(8,128)(2,1)}, bf16[512,384]{1,0:T(8,128)(2,1)}, u32[]{:S(2)}, u32[]{:S(2)}) collective-permute-start(bf16[512,384]{1,0:T(8,128)(2,1)} %bitcast.125), channel_id=1, source_target_pairs={{0,1},{1,0},{2,3},{3,2},{4,5},{5,4},{6,7},{7,6},{8,9},{9,8},{10,11... | collective-permute-start | bytes 1179656 | tf_op jit(solution)/shard_map/ppermute | solution.py:107
  10.4 1.4 pad_maximum_fusion.2
  11.8 2.6 %broadcast_in_dim.25 = bf16[3,1536,512]{2,1,0:T(8,128)(2,1)} broadcast(bf16[]{:T(256)} %constant.141.clone.1), dimensions={} | broadcast | bytes 4718594 | tf_op jit(solution)/shard_map/broadcast_in_dim | solution.py:126
  14.4 1.4 constant_dynamic-update-slice_fusion.7
  15.8 3.8 %collective-permute-start.7 = (bf16[3,192,512]{2,1,0:T(8,128)(2,1)}, bf16[3,192,512]{2,1,0:T(8,128)(2,1)S(1)}, u32[]{:S(2)}, u32[]{:S(2)}) collective-permute-start(bf16[3,192,512]{2,1,0:T(8,128)(2,1)} %get-tuple-element.25), channel_id=1, source_target_pairs={{0,3},{1,0},{2,1},{3,2},{4,7},{5,4},{6,5},{7,6},{8,11},{9,8},{10,9... | collective-permute-start | bytes 1769480 | tf_op jit(solution)/shard_map/ppermute | solution.py:110
  19.6 1.5 collective-permute-start.4
  21.1 1.2 pad_maximum_fusion.3
  22.4 1.1 fusion.36
  23.5 1.6 collective-permute-start.2
  25.1 10.6 %collective-permute-done.5 = bf16[3,192,512]{2,1,0:T(8,128)(2,1)S(1)} collective-permute-done((bf16[3,192,512]{2,1,0:T(8,128)(2,1)}, bf16[3,192,512]{2,1,0:T(8,128)(2,1)S(1)}, u32[]{:S(2)}, u32[]{:S(2)}) %collective-permute-start.5) | collective-permute-done | bytes 589856 | tf_op jit(solution)/shard_map/ppermute | solution.py:110
  35.9 1.6 collective-permute-start.6
  37.5 8.1 %collective-permute-done.7 = bf16[3,192,512]{2,1,0:T(8,128)(2,1)S(1)} collective-permute-done((bf16[3,192,512]{2,1,0:T(8,128)(2,1)}, bf16[3,192,512]{2,1,0:T(8,128)(2,1)S(1)}, u32[]{:S(2)}, u32[]{:S(2)}) %collective-permute-start.7) | collective-permute-done | bytes 589856 | tf_op jit(solution)/shard_map/ppermute | solution.py:110
  45.6 1.6 collective-permute-start.8
  47.3 3.7 %collective-permute-done.2 = bf16[1024,384]{1,0:T(8,128)(2,1)S(1)} collective-permute-done((bf16[1024,384]{1,0:T(8,128)(2,1)S(1)}, bf16[1024,384]{1,0:T(8,128)(2,1)S(1)}, u32[]{:S(2)}, u32[]{:S(2)}) %collective-permute-start.2) | collective-permute-done | bytes 786464 | tf_op jit(solution)/shard_map/ppermute | solution.py:107
  51.0 1.9 %constant_dynamic-update-slice_fusion.6 = bf16[3,1536,512]{2,1,0:T(8,128)(2,1)} fusion(bf16[3,1536,512]{2,1,0:T(8,128)(2,1)} %get-tuple-element.19, bf16[3,192,512]{2,1,0:T(8,128)(2,1)} %collective-permute-done.4, s32[]{:T(128)S(6)} %select_n.149), kind=kLoop, calls=%fused_computation.82 | loop fusion | bytes 1179652 | tf_op jit(solution)/shard_map/dynamic_update_slice | solution.py:131
  53.0 18.1 %collective-permute-done.9 = bf16[3,192,512]{2,1,0:T(8,128)(2,1)} collective-permute-done((bf16[3,192,512]{2,1,0:T(8,128)(2,1)}, bf16[3,192,512]{2,1,0:T(8,128)(2,1)}, u32[]{:S(2)}, u32[]{:S(2)}) %collective-permute-start.9) | collective-permute-done | bytes 589856 | tf_op jit(solution)/shard_map/ppermute | solution.py:110
  71.1 1.5 collective-permute-start.10
  72.6 0.9 constant_dynamic-update-slice_fusion.5
  73.5 0.9 constant_dynamic-update-slice_fusion.4
  74.4 0.9 constant_dynamic-update-slice_fusion.3
  75.3 0.8 constant_dynamic-update-slice_fusion.2
  76.1 1.9 %constant_dynamic-update-slice_fusion.1 = bf16[3,1536,512]{2,1,0:T(8,128)(2,1)} fusion(bf16[3,1536,512]{2,1,0:T(8,128)(2,1)} %constant_dynamic-update-slice_fusion.2, bf16[3,192,512]{2,1,0:T(8,128)(2,1)} %collective-permute-done.9, s32[]{:T(128)S(6)} %select_n.158), kind=kLoop, calls=%fused_computation.76 | loop fusion | bytes 1179652 | tf_op jit(solution)/shard_map/dynamic_update_slice | solution.py:130
  78.0 7.6 %collective-permute-done.10 = bf16[3,192,512]{2,1,0:T(8,128)(2,1)S(1)} collective-permute-done((bf16[3,192,512]{2,1,0:T(8,128)(2,1)}, bf16[3,192,512]{2,1,0:T(8,128)(2,1)S(1)}, u32[]{:S(2)}, u32[]{:S(2)}) %collective-permute-start.10) | collective-permute-done | bytes 589856 | tf_op jit(solution)/shard_map/ppermute | solution.py:107
  85.6 0.9 constant_dynamic-update-slice_fusion
  88.1 1.0 fusion.2
  89.0 1.0 fusion.4
  90.1 3.2 %fusion.7 = f32[1024,512]{1,0:T(8,128)S(1)} fusion(bf16[1024,1536]{1,0:T(8,128)(2,1)S(1)} %fusion.4, bf16[3,1536,512]{2,1,0:T(8,128)(2,1)} %constant_dynamic-update-slice_fusion), kind=kOutput, calls=%fused_computation.15 | convolution fusion | flops 1610612736 | bytes 6815744 | tf_op jit(solution)/shard_map/dot_general | solution.py:183
  93.2 4.4 %multiply_convert_fusion = bf16[1024,512]{1,0:T(8,128)(2,1)} fusion(f32[1024,512]{1,0:T(8,128)S(1)} %fusion.7, bf16[1024,1536]{1,0:T(8,128)(2,1)S(1)} %fusion.4, bf16[3,1536,512]{2,1,0:T(8,128)(2,1)} %constant_dynamic-update-slice_fusion), kind=kOutput, calls=%fused_computation.9 | convolution fusion | flops 1613758464 | bytes 7864320 | tf_op jit(solution)/shard_map/dot_general | solution.py:184
  97.7 3.7 %fusion.9 = bf16[512,768,1,1]{1,0,3,2:T(8,128)(2,1)S(1)} fusion(bf16[1536,768]{1,0:T(8,128)(2,1)} %all-gather.5.cloned.1.call-done, bf16[3,1536,512]{2,1,0:T(8,128)(2,1)} %constant_dynamic-update-slice_fusion), kind=kOutput, calls=%fused_computation.19 | convolution fusion | flops 1208352768 | bytes 4718592 | tf_op jit(solution)/shard_map/dot_general | solution.py:187
  101.3 0.9 copy-done.2
  102.2 1.5 convolution_convert_fusion
  103.7 5.3 %all-gather.1 = s32[4,4,2]{1,2,0:T(2,128)S(1)} all-gather(s32[1,4,2]{1,2,0:T(2,128)S(1)} %add_bitcast_fusion), channel_id=1, replica_groups=mesh['section'=4,'seq'=2,'dp'=4] {'section'}, dimensions={0}, use_global_device_ids=true | all-gather | bytes 160 | tf_op jit(solution)/shard_map/all_gather | solution.py:180
  109.5 0.8 copy-done.3
  110.7 1.7 %convert_add_fusion = f32[2,2,128,768]{3,2,1,0:T(8,128)S(1)} fusion(bf16[2,2,128,768]{3,2,1,0:T(8,128)(2,1)} %collective-permute-done.11, bf16[512,768,1,1]{1,0,3,2:T(8,128)(2,1)S(1)} %copy-done.3, bf16[2,2,2,128,512]{4,3,2,1,0:T(8,128)(2,1)S(1)} %bitcast.129, s32[]{:T(128)S(6)} %select_n.161), kind=kOutput, calls=%fused_computation.16 | convolution fusion | flops 403439616 | bytes 3670020 | tf_op jit(solution)/shard_map/dot_general | solution.py:192
  112.5 2.0 %collective-permute-start.14 = (bf16[128,768]{1,0:T(8,128)(2,1)S(1)}, bf16[128,768]{1,0:T(8,128)(2,1)S(1)}, u32[]{:S(2)}, u32[]{:S(2)}) collective-permute-start(bf16[128,768]{1,0:T(8,128)(2,1)S(1)} %get-tuple-element.29), channel_id=1, source_target_pairs={{0,17},{1,16},{2,19},{3,18},{8,25},{9,24},{10,27},{11,26},{16,1},{... | collective-permute-start | bytes 589832 | tf_op jit(solution)/shard_map/ppermute | solution.py:107
  114.6 1.1 collective-permute-start.13
  116.7 4.6 %collective-permute-done.14 = bf16[128,768]{1,0:T(8,128)(2,1)S(1)} collective-permute-done((bf16[128,768]{1,0:T(8,128)(2,1)S(1)}, bf16[128,768]{1,0:T(8,128)(2,1)S(1)}, u32[]{:S(2)}, u32[]{:S(2)}) %collective-permute-start.14) | collective-permute-done | bytes 196640 | tf_op jit(solution)/shard_map/ppermute | solution.py:107
  121.3 3.6 %collective-permute-done.13 = bf16[128,768]{1,0:T(8,128)(2,1)S(1)} collective-permute-done((bf16[128,768]{1,0:T(8,128)(2,1)S(1)}, bf16[128,768]{1,0:T(8,128)(2,1)S(1)}, u32[]{:S(2)}, u32[]{:S(2)}) %collective-permute-start.13) | collective-permute-done | bytes 196640 | tf_op jit(solution)/shard_map/ppermute | solution.py:107
  125.4 1.5 collective-permute-start.15
  126.9 1.5 collective-permute-start.16
  129.1 4.2 %collective-permute-done.15.refs_2_ = bf16[128,768]{1,0:T(8,128)(2,1)S(1)} collective-permute-done((bf16[128,768]{1,0:T(8,128)(2,1)S(1)}, bf16[128,768]{1,0:T(8,128)(2,1)S(1)}, u32[]{:S(2)}, u32[]{:S(2)}) %collective-permute-start.15) | collective-permute-done | bytes 196640 | tf_op jit(solution)/shard_map/ppermute | solution.py:107
  133.3 4.4 %collective-permute-done.16.refs_3_ = bf16[128,768]{1,0:T(8,128)(2,1)S(1)} collective-permute-done((bf16[128,768]{1,0:T(8,128)(2,1)S(1)}, bf16[128,768]{1,0:T(8,128)(2,1)S(1)}, u32[]{:S(2)}, u32[]{:S(2)}) %collective-permute-start.16) | collective-permute-done | bytes 196640 | tf_op jit(solution)/shard_map/ppermute | solution.py:107
  138.0 1.4 fusion.26
  140.1 10.5 %shard_map.118 = bf16[4,128,192]{2,1,0:T(8,128)(2,1)S(1)} custom-call(s32[1]{0:T(128)} %bitcast.refs_0_, bf16[128,768]{1,0:T(8,128)(2,1)S(1)} %multiply_convert_fusion.1.refs_1_, bf16[128,768]{1,0:T(8,128)(2,1)S(1)} %collective-permute-done.15.refs_2_, bf16[128,768]{1,0:T(8,128)(2,1)S(1)} %collective-permute-done.16.refs_3_, ...), custom_call_target="tpu_custom_call" | custom-call | flops 4026531840 | bytes 8388608 | tf_op jit(solution)/shard_map/pallas_call | solution.py:250
  150.6 1.0 collective-permute-start.21
  151.6 0.9 collective-permute-start.20
  152.6 2.2 %collective-permute-done.21 = bf16[128,192]{1,0:T(8,128)(2,1)S(1)} collective-permute-done((bf16[128,192]{1,0:T(8,128)(2,1)S(1)}, bf16[128,192]{1,0:T(8,128)(2,1)S(1)}, u32[]{:S(2)}, u32[]{:S(2)}) %collective-permute-start.21) | collective-permute-done | bytes 49184 | tf_op jit(solution)/shard_map/ppermute | solution.py:107
  154.8 1.7 %collective-permute-done.20 = bf16[128,192]{1,0:T(8,128)(2,1)S(1)} collective-permute-done((bf16[128,192]{1,0:T(8,128)(2,1)S(1)}, bf16[128,192]{1,0:T(8,128)(2,1)S(1)}, u32[]{:S(2)}, u32[]{:S(2)}) %collective-permute-start.20) | collective-permute-done | bytes 49184 | tf_op jit(solution)/shard_map/ppermute | solution.py:107
  (95 shorter events, 8.1 us)
Async XLA Ops:
  6.5 91.1 %all-gather.5.cloned.1.call-start = ((), (), s32[]{:S(2)}) async-start(), calls=%async_computation | async-start | bytes 2949120 | tf_op jit(solution)/shard_map/all_gather | solution.py:177
  7.3 132.9 %all-gather.7.cloned.1.call-start = ((), (), s32[]{:S(2)}) async-start(), calls=%async_computation.1 | async-start | bytes 5898240 | tf_op jit(solution)/shard_map/all_gather | solution.py:179
  7.3 15.1 %collective-permute-start = (bf16[512,384]{1,0:T(8,128)(2,1)}, bf16[512,384]{1,0:T(8,128)(2,1)}, u32[]{:S(2)}, u32[]{:S(2)}) collective-permute-start(bf16[512,384]{1,0:T(8,128)(2,1)} %bitcast.125), channel_id=1, source_target_pairs={{0,1},{1,0},{2,3},{3,2},{4,5},{5,4},{6,7},{7,6},{8,9},{9,8},{10,11... | collective-permute-start | bytes 1179656 | tf_op jit(solution)/shard_map/ppermute | solution.py:107
  11.8 9.3 %copy-start.1 = (bf16[3,768,192]{1,2,0:T(8,128)(2,1)S(1)}, bf16[3,768,192]{1,2,0:T(8,128)(2,1)}, u32[]{:S(2)}) copy-start(bf16[3,768,192]{1,2,0:T(8,128)(2,1)} %param.19) | copy-start | bytes 2654212
  11.8 9.3 %copy-start.5 = (bf16[192,768]{1,0:T(8,128)(2,1)S(1)}, bf16[192,768]{1,0:T(8,128)(2,1)}, u32[]{:S(2)}) copy-start(bf16[192,768]{1,0:T(8,128)(2,1)} %param.20) | copy-start | bytes 884740
  14.4 8.0 %copy-start.4 = (bf16[1,512,384]{2,1,0:T(8,128)(2,1)S(1)}, bf16[1,512,384]{2,1,0:T(8,128)(2,1)}, u32[]{:S(2)}) copy-start(bf16[1,512,384]{2,1,0:T(8,128)(2,1)} %param.12) | copy-start | bytes 1179652
  15.8 21.7 %copy-start.10 = (s32[4]{0:T(128)S(1)}, s32[4]{0:T(128)}, u32[]{:S(2)}) copy-start(s32[4]{0:T(128)} %param.23) | copy-start | bytes 52
  15.8 21.7 %copy-start.11 = (s32[4]{0:T(128)S(1)}, s32[4]{0:T(128)}, u32[]{:S(2)}) copy-start(s32[4]{0:T(128)} %param.22) | copy-start | bytes 52
  15.8 20.0 %collective-permute-start.5 = (bf16[3,192,512]{2,1,0:T(8,128)(2,1)}, bf16[3,192,512]{2,1,0:T(8,128)(2,1)S(1)}, u32[]{:S(2)}, u32[]{:S(2)}) collective-permute-start(bf16[3,192,512]{2,1,0:T(8,128)(2,1)} %get-tuple-element.25), channel_id=1, source_target_pairs={{0,1},{1,2},{2,3},{3,0},{4,5},{5,6},{6,7},{7,4},{8,9},{9,10},{10,1... | collective-permute-start | bytes 1769480 | tf_op jit(solution)/shard_map/ppermute | solution.py:110
  15.8 29.8 %collective-permute-start.7 = (bf16[3,192,512]{2,1,0:T(8,128)(2,1)}, bf16[3,192,512]{2,1,0:T(8,128)(2,1)S(1)}, u32[]{:S(2)}, u32[]{:S(2)}) collective-permute-start(bf16[3,192,512]{2,1,0:T(8,128)(2,1)} %get-tuple-element.25), channel_id=1, source_target_pairs={{0,3},{1,0},{2,1},{3,2},{4,7},{5,4},{6,5},{7,6},{8,11},{9,8},{10,9... | collective-permute-start | bytes 1769480 | tf_op jit(solution)/shard_map/ppermute | solution.py:110
  19.6 27.6 %collective-permute-start.4 = (bf16[3,192,512]{2,1,0:T(8,128)(2,1)}, bf16[3,192,512]{2,1,0:T(8,128)(2,1)}, u32[]{:S(2)}, u32[]{:S(2)}) collective-permute-start(bf16[3,192,512]{2,1,0:T(8,128)(2,1)} %get-tuple-element.8), channel_id=1, source_target_pairs={{0,4},{4,0},{1,5},{5,1},{2,6},{6,2},{3,7},{7,3},{8,12},{12,8},{9,1... | collective-permute-start | bytes 1769480 | tf_op jit(solution)/shard_map/ppermute | solution.py:107
  23.5 27.5 %collective-permute-start.2 = (bf16[1024,384]{1,0:T(8,128)(2,1)S(1)}, bf16[1024,384]{1,0:T(8,128)(2,1)S(1)}, u32[]{:S(2)}, u32[]{:S(2)}) collective-permute-start(bf16[1024,384]{1,0:T(8,128)(2,1)S(1)} %get-tuple-element.27), channel_id=1, source_target_pairs={{0,16},{8,24},{16,0},{24,8},{1,17},{9,25},{17,1},{25,9},{2,18},{10... | collective-permute-start | bytes 2359304 | tf_op jit(solution)/shard_map/ppermute | solution.py:107
  35.7 35.4 %collective-permute-start.9 = (bf16[3,192,512]{2,1,0:T(8,128)(2,1)}, bf16[3,192,512]{2,1,0:T(8,128)(2,1)}, u32[]{:S(2)}, u32[]{:S(2)}) collective-permute-start(bf16[3,192,512]{2,1,0:T(8,128)(2,1)} %get-tuple-element.8), channel_id=1, source_target_pairs={{0,2},{1,3},{2,0},{3,1},{4,6},{5,7},{6,4},{7,5},{8,10},{9,11},{10,... | collective-permute-start | bytes 1769480 | tf_op jit(solution)/shard_map/ppermute | solution.py:110
  35.9 37.6 %collective-permute-start.6 = (bf16[3,192,512]{2,1,0:T(8,128)(2,1)S(1)}, bf16[3,192,512]{2,1,0:T(8,128)(2,1)S(1)}, u32[]{:S(2)}, u32[]{:S(2)}) collective-permute-start(bf16[3,192,512]{2,1,0:T(8,128)(2,1)S(1)} %collective-permute-done.5), channel_id=1, source_target_pairs={{0,4},{4,0},{1,5},{5,1},{2,6},{6,2},{3,7},{7,3},{8,12},{12,8},{9,1... | collective-permute-start | bytes 1769480 | tf_op jit(solution)/shard_map/ppermute | solution.py:107
  45.6 29.7 %collective-permute-start.8 = (bf16[3,192,512]{2,1,0:T(8,128)(2,1)S(1)}, bf16[3,192,512]{2,1,0:T(8,128)(2,1)S(1)}, u32[]{:S(2)}, u32[]{:S(2)}) collective-permute-start(bf16[3,192,512]{2,1,0:T(8,128)(2,1)S(1)} %collective-permute-done.7), channel_id=1, source_target_pairs={{0,4},{4,0},{1,5},{5,1},{2,6},{6,2},{3,7},{7,3},{8,12},{12,8},{9,1... | collective-permute-start | bytes 1769480 | tf_op jit(solution)/shard_map/ppermute | solution.py:107
  47.2 39.2 %collective-permute-start.1 = (bf16[1024,384]{1,0:T(8,128)(2,1)S(1)}, bf16[1024,384]{1,0:T(8,128)(2,1)S(1)}, u32[]{:S(2)}, u32[]{:S(2)}) collective-permute-start(bf16[1024,384]{1,0:T(8,128)(2,1)S(1)} %get-tuple-element.27), channel_id=1, source_target_pairs={{0,8},{8,0},{16,24},{24,16},{1,9},{9,1},{17,25},{25,17},{2,10},{10... | collective-permute-start | bytes 2359304 | tf_op jit(solution)/shard_map/ppermute | solution.py:107
  51.0 35.4 %collective-permute-start.3 = (bf16[1024,384]{1,0:T(8,128)(2,1)S(1)}, bf16[1024,384]{1,0:T(8,128)(2,1)S(1)}, u32[]{:S(2)}, u32[]{:S(2)}) collective-permute-start(bf16[1024,384]{1,0:T(8,128)(2,1)S(1)} %collective-permute-done.2), channel_id=1, source_target_pairs={{0,8},{8,0},{16,24},{24,16},{1,9},{9,1},{17,25},{25,17},{2,10},{10... | collective-permute-start | bytes 2359304 | tf_op jit(solution)/shard_map/ppermute | solution.py:107
  71.1 14.5 %collective-permute-start.10 = (bf16[3,192,512]{2,1,0:T(8,128)(2,1)}, bf16[3,192,512]{2,1,0:T(8,128)(2,1)S(1)}, u32[]{:S(2)}, u32[]{:S(2)}) collective-permute-start(bf16[3,192,512]{2,1,0:T(8,128)(2,1)} %collective-permute-done.9), channel_id=1, source_target_pairs={{0,4},{4,0},{1,5},{5,1},{2,6},{6,2},{3,7},{7,3},{8,12},{12,8},{9,1... | collective-permute-start | bytes 1769480 | tf_op jit(solution)/shard_map/ppermute | solution.py:107
  88.0 1.0 copy-start.9
  97.7 11.4 %copy-start.12 = (s32[1,3]{1,0:T(1,128)S(1)}, s32[1,3]{1,0:T(1,128)}, u32[]{:S(2)}) copy-start(s32[1,3]{1,0:T(1,128)} %param.21) | copy-start | bytes 40
  97.7 4.6 %copy-start.6 = (bf16[1024,512]{1,0:T(8,128)(2,1)S(1)}, bf16[1024,512]{1,0:T(8,128)(2,1)}, u32[]{:S(2)}) copy-start(bf16[1024,512]{1,0:T(8,128)(2,1)} %multiply_convert_fusion) | copy-start | bytes 3145732
  101.3 0.9 copy-start.2
  103.7 5.8 %collective-permute-start.11 = (bf16[2,2,128,768]{3,2,1,0:T(8,128)(2,1)}, bf16[2,2,128,768]{3,2,1,0:T(8,128)(2,1)}, u32[]{:S(2)}, u32[]{:S(2)}) collective-permute-start(bf16[2,2,128,768]{3,2,1,0:T(8,128)(2,1)} %convolution_convert_fusion), channel_id=1, source_target_pairs={{0,8},{8,0},{16,24},{24,16},{1,9},{9,1},{17,25},{25,17},{2,10},{10... | collective-permute-start | bytes 2359304 | tf_op jit(solution)/shard_map/ppermute | solution.py:107
  109.2 1.1 copy-start.3
  109.2 1.5 copy-start.7
  109.5 6.7 %copy-start = (bf16[1536,768]{1,0:T(8,128)(2,1)S(1)}, bf16[1536,768]{1,0:T(8,128)(2,1)}, u32[]{:S(2)}) copy-start(bf16[1536,768]{1,0:T(8,128)(2,1)} %all-gather.5.cloned.1.call-done) | copy-start | bytes 7077892
  112.5 12.8 %copy-start.8 = (f32[768]{0:T(1024)S(1)}, f32[768]{0:T(1024)}, u32[]{:S(2)}) copy-start(f32[768]{0:T(1024)} %param.18) | copy-start | bytes 9220
  112.5 8.7 %collective-permute-start.14 = (bf16[128,768]{1,0:T(8,128)(2,1)S(1)}, bf16[128,768]{1,0:T(8,128)(2,1)S(1)}, u32[]{:S(2)}, u32[]{:S(2)}) collective-permute-start(bf16[128,768]{1,0:T(8,128)(2,1)S(1)} %get-tuple-element.29), channel_id=1, source_target_pairs={{0,17},{1,16},{2,19},{3,18},{8,25},{9,24},{10,27},{11,26},{16,1},{... | collective-permute-start | bytes 589832 | tf_op jit(solution)/shard_map/ppermute | solution.py:107
  114.6 10.3 %collective-permute-start.13 = (bf16[128,768]{1,0:T(8,128)(2,1)S(1)}, bf16[128,768]{1,0:T(8,128)(2,1)S(1)}, u32[]{:S(2)}, u32[]{:S(2)}) collective-permute-start(bf16[128,768]{1,0:T(8,128)(2,1)S(1)} %fusion.23), channel_id=1, source_target_pairs={{0,1},{1,0},{2,3},{3,2},{4,5},{5,4},{6,7},{7,6},{8,9},{9,8},{10,11... | collective-permute-start | bytes 589832 | tf_op jit(solution)/shard_map/ppermute | solution.py:107
  115.6 9.3 %collective-permute-start.12 = (bf16[128,768]{1,0:T(8,128)(2,1)S(1)}, bf16[128,768]{1,0:T(8,128)(2,1)S(1)}, u32[]{:S(2)}, u32[]{:S(2)}) collective-permute-start(bf16[128,768]{1,0:T(8,128)(2,1)S(1)} %get-tuple-element.28), channel_id=1, source_target_pairs={{0,16},{8,24},{16,0},{24,8},{1,17},{9,25},{17,1},{25,9},{2,18},{10... | collective-permute-start | bytes 589832 | tf_op jit(solution)/shard_map/ppermute | solution.py:107
  125.4 7.8 %collective-permute-start.15 = (bf16[128,768]{1,0:T(8,128)(2,1)S(1)}, bf16[128,768]{1,0:T(8,128)(2,1)S(1)}, u32[]{:S(2)}, u32[]{:S(2)}) collective-permute-start(bf16[128,768]{1,0:T(8,128)(2,1)S(1)} %multiply_convert_fusion.1.refs_1_), channel_id=1, source_target_pairs={{0,16},{8,24},{16,0},{24,8},{1,17},{9,25},{17,1},{25,9},{2,18},{10... | collective-permute-start | bytes 589832 | tf_op jit(solution)/shard_map/ppermute | solution.py:107
  126.9 10.8 %collective-permute-start.16 = (bf16[128,768]{1,0:T(8,128)(2,1)S(1)}, bf16[128,768]{1,0:T(8,128)(2,1)S(1)}, u32[]{:S(2)}, u32[]{:S(2)}) collective-permute-start(bf16[128,768]{1,0:T(8,128)(2,1)S(1)} %multiply_convert_fusion.1.refs_1_), channel_id=1, source_target_pairs={{0,4},{4,0},{1,5},{5,1},{2,6},{6,2},{3,7},{7,3},{8,12},{12,8},{9,1... | collective-permute-start | bytes 589832 | tf_op jit(solution)/shard_map/ppermute | solution.py:107
  128.4 9.3 %collective-permute-start.17 = (bf16[128,768]{1,0:T(8,128)(2,1)S(1)}, bf16[128,768]{1,0:T(8,128)(2,1)S(1)}, u32[]{:S(2)}, u32[]{:S(2)}) collective-permute-start(bf16[128,768]{1,0:T(8,128)(2,1)S(1)} %multiply_convert_fusion.1.refs_1_), channel_id=1, source_target_pairs={{0,20},{4,16},{8,28},{12,24},{16,4},{20,0},{24,12},{28,8},{1,21},{... | collective-permute-start | bytes 589832 | tf_op jit(solution)/shard_map/ppermute | solution.py:107
  137.8 2.4 %collective-permute-start.18 = (bf16[4,128,768]{2,1,0:T(8,128)(2,1)S(1)}, bf16[4,128,768]{2,1,0:T(8,128)(2,1)S(1)}, u32[]{:S(2)}, u32[]{:S(2)}) collective-permute-start(bf16[4,128,768]{2,1,0:T(8,128)(2,1)S(1)} %pad_maximum_fusion.5), channel_id=1, source_target_pairs={{0,8},{8,0},{16,24},{24,16},{1,9},{9,1},{17,25},{25,17},{2,10},{10... | collective-permute-start | bytes 2359304 | tf_op jit(solution)/shard_map/ppermute | solution.py:107
  150.6 4.1 %collective-permute-start.21 = (bf16[128,192]{1,0:T(8,128)(2,1)S(1)}, bf16[128,192]{1,0:T(8,128)(2,1)S(1)}, u32[]{:S(2)}, u32[]{:S(2)}) collective-permute-start(bf16[128,192]{1,0:T(8,128)(2,1)S(1)} %get-tuple-element.35), channel_id=1, source_target_pairs={{0,24},{8,16},{16,8},{24,0},{1,25},{9,17},{17,9},{25,1},{2,26},{10... | collective-permute-start | bytes 147464 | tf_op jit(solution)/shard_map/ppermute | solution.py:107
  151.6 4.9 %collective-permute-start.20 = (bf16[128,192]{1,0:T(8,128)(2,1)S(1)}, bf16[128,192]{1,0:T(8,128)(2,1)S(1)}, u32[]{:S(2)}, u32[]{:S(2)}) collective-permute-start(bf16[128,192]{1,0:T(8,128)(2,1)S(1)} %get-tuple-element.36), channel_id=1, source_target_pairs={{0,16},{8,24},{16,0},{24,8},{1,17},{9,25},{17,1},{25,9},{2,18},{10... | collective-permute-start | bytes 147464 | tf_op jit(solution)/shard_map/ppermute | solution.py:107
  152.5 4.0 %collective-permute-start.19 = (bf16[128,192]{1,0:T(8,128)(2,1)S(1)}, bf16[128,192]{1,0:T(8,128)(2,1)S(1)}, u32[]{:S(2)}, u32[]{:S(2)}) collective-permute-start(bf16[128,192]{1,0:T(8,128)(2,1)S(1)} %get-tuple-element.37), channel_id=1, source_target_pairs={{0,8},{8,0},{16,24},{24,16},{1,9},{9,1},{17,25},{25,17},{2,10},{10... | collective-permute-start | bytes 147464 | tf_op jit(solution)/shard_map/ppermute | solution.py:107
Sparse Core Ops, SparseCore 0:
  8.9 35.5 all-gather.4
  46.0 39.0 all-gather.6

commit v3 on v2

--- a/solution.py
+++ b/solution.py
@@ -27,8 +27,16 @@
 
 
 def attend_kernel(sec_ref, mine_ref, *refs, heads, size):
-    near, (far_ref, w_ref, emb_ref, q_ref, k_ref, out_ref) = refs[:-6], refs[-6:]
-    parts, _, width, _ = w_ref.shape
+    near, refs = refs[:-8], refs[-8:]
+    far_ref, w_any, emb_ref, q_ref, k_ref, out_ref, w_ref, w_sem = refs
+    _, parts, width, _ = w_ref.shape
+    copies = {}
+    for which in (1, 0, 2, 3):
+        for m in range(parts):
+            copies[which, m] = pltpu.make_async_copy(
+                w_any.at[m, which], w_ref.at[which, m], w_sem.at[which, m]
+            )
+            copies[which, m].start()
     rows = mine_ref.shape[0]
     mine = mine_ref[...]
     keys = jnp.concatenate(
@@ -37,14 +45,18 @@
     count = keys.shape[0]
     scale = math.log2(math.e) / math.sqrt(size)
 
+    def matrix(which):
+        for m in range(parts):
+            copies[which, m].wait()
+        return jnp.concatenate([w_ref[which, m] for m in range(parts)], axis=0)
+
     def project(x, which):
-        matrix = jnp.concatenate([w_ref[m, which] for m in range(parts)], axis=0)
         return lax.dot_general(
-            x, matrix, (((1,), (1,)), ((), ())), preferred_element_type=jnp.float32
+            x, matrix(which), (((1,), (1,)), ((), ())), preferred_element_type=jnp.float32
         ).astype(jnp.bfloat16)
 
-    query, key, value = project(mine, 0), project(keys, 1), project(keys, 2)
-    out_matrix = jnp.concatenate([w_ref[m, 3] for m in range(parts)], axis=0)
+    key = project(keys, 1)
+    query, value, out_matrix = project(mine, 0), project(keys, 2), matrix(3)
     diag = lax.broadcasted_iota(jnp.int32, (rows, count), 0) == lax.broadcasted_iota(
         jnp.int32, (rows, count), 1
     )
@@ -109,33 +121,29 @@
     def rotate(x, k):
         return lax.ppermute(x, "dp", [(i, (i + k) % n_dp) for i in range(n_dp)])
 
+    def after(x, *others):
+        return lax.optimization_barrier((x,) + others)[0]
+
     def gather_section(x):
         across = flip(x, section=2)
-        return [x, flip(x, section=1), across, flip(across, section=1)]
+        return [x, flip(after(x, across), section=1), across, flip(across, section=1)]
 
     def gather_rows(same, other, seq_at, dp_at):
-        got = {0: same}
         mats, rows, units = same.shape
-        last = n_dp // 2
-        for k in [k for k in range(1, n_dp) if k != last] + [last]:
-            block = other if k % 2 else same
-            if k == last and n_dp > 2:
-                block, got[1] = lax.optimization_barrier((block, got[1]))
-            got[k] = rotate(block, k)
-        if n_seq == 2:
-            whole = jnp.zeros((mats, n_seq * n_dp * rows, units), same.dtype)
-            for k, block in got.items():
-                z = (dp_at - k) % n_dp
-                theirs = flip(block, seq=1)
-                whole = lax.dynamic_update_slice(whole, block, (0, (seq_at * n_dp + z) * rows, 0))
-                whole = lax.dynamic_update_slice(
-                    whole, theirs, (0, ((1 - seq_at) * n_dp + z) * rows, 0)
-                )
-            return whole
         part = jnp.zeros((mats, n_dp * rows, units), same.dtype)
-        for k, block in got.items():
+        for k in range(n_dp):
+            block = rotate(other if k % 2 else same, k) if k else same
             part = lax.dynamic_update_slice(part, block, (0, ((dp_at - k) % n_dp) * rows, 0))
         return lax.all_gather(part, "seq", axis=1, tiled=True)
+
+    def place_rows(blocks):
+        seq_at, dp_at = lax.axis_index("seq"), lax.axis_index("dp")
+        mats, rows, units = blocks[0, 0].shape
+        whole = jnp.zeros((mats, n_seq * n_dp * rows, units), blocks[0, 0].dtype)
+        for (y, k), block in blocks.items():
+            at = ((seq_at ^ y) * n_dp + (dp_at - k) % n_dp) * rows
+            whole = lax.dynamic_update_slice(whole, block, (0, at, 0))
+        return whole
 
     def per_device(
         tile_feats,
@@ -164,29 +172,69 @@
             stacked = jnp.stack(blocks)
             return [lax.dynamic_index_in_dim(stacked, sec ^ j, 0, False) for j in range(n_sec)]
 
-        both = jnp.concatenate([mine, flip(mine, dp=1)], axis=0)
-        rows = jnp.concatenate(absolute(gather_section(both)), axis=1)
-
-        matrices = jnp.stack([w_gate, w_up, w_down.T])
-
-        def halves(which):
-            return lax.dynamic_slice_in_dim(matrices, which * half, half, 2)
-
-        units = gather_rows(halves(odd), halves(1 - odd), seq_at, dp_at)
+        def halves(x, which):
+            return lax.dynamic_slice_in_dim(x, which * half, half, x.ndim - 1)
+
+        pair = jnp.stack([w_gate, w_up])
+        pair_same, pair_other = halves(pair, odd), halves(pair, 1 - odd)
+        down = w_down.T[None]
+        down_same, down_other = halves(down, odd), halves(down, 1 - odd)
+        ordered = n_seq == 2 and n_dp == 4
+
+        local_heads = seg_len.shape[0]
+        info = jnp.concatenate([seg_len // 64, seg_len % 64, rate]).astype(jnp.bfloat16)
+        info = jnp.pad(info[None], ((0, 15), (0, feats - 3 * local_heads)))
+        beside = flip(mine, dp=1)
+        both = jnp.concatenate([mine, beside, info], axis=0)
+        blocks = absolute(gather_section(both))
+        rows = jnp.concatenate([block[: 2 * tokens] for block in blocks], axis=1)
+        info = [
+            block[2 * tokens, : 3 * local_heads].astype(jnp.int32).reshape(3, local_heads)
+            for block in blocks
+        ]
+        seg_all = jnp.concatenate([x[0] * 64 + x[1] for x in info])
+        rate_all = jnp.concatenate([x[2] for x in info])
+        normed = layer_norm(rows.astype(jnp.float32), tile_gain).astype(jnp.bfloat16)
+
+        if ordered:
+            g = {(0, 0): pair_same, (0, 1): rotate(pair_other, 1), (0, 3): rotate(pair_other, 3)}
+            g[0, 2] = rotate(after(pair_same, g[0, 1]), 2)
+            for k in (0, 1, 3, 2):
+                g[1, k] = flip(g[0, k], seq=1)
+            gate_up = place_rows(g)
+            d = {(0, 0): down_same}
+            d[0, 1] = rotate(after(down_other, g[0, 2]), 1)
+            d[0, 3] = rotate(after(down_other, g[0, 2]), 3)
+            d[0, 2] = rotate(after(down_same, d[0, 1], normed), 2)
+            d[1, 0] = flip(after(down_same, beside), seq=1)
+            d[1, 1], d[1, 3] = flip(d[0, 1], seq=1), flip(d[0, 3], seq=1)
+        else:
+            gate_up = gather_rows(pair_same, pair_other, seq_at, dp_at)
+            down_all = gather_rows(down_same, down_other, seq_at, dp_at)[0]
 
         proj = lax.all_gather(w_proj, "section", axis=0, tiled=True)
         slide_w = jnp.concatenate([jnp.swapaxes(w_qkv, 1, 2), w_out[None]], axis=0)
         slide_w = lax.all_gather(slide_w, "section", axis=0)
-        head_info = lax.all_gather(jnp.stack([seg_len, rate]), "section", axis=1, tiled=True)
-
-        normed = layer_norm(rows.astype(jnp.float32), tile_gain).astype(jnp.bfloat16)
-        gate = jnp.dot(normed, units[0], preferred_element_type=jnp.float32)
-        up = jnp.dot(normed, units[1], preferred_element_type=jnp.float32)
+
+        gate = jnp.dot(normed, gate_up[0], preferred_element_type=jnp.float32)
+        up = jnp.dot(normed, gate_up[1], preferred_element_type=jnp.float32)
         hidden = (jax.nn.silu(gate) * up).astype(jnp.bfloat16)
         hidden = hidden.reshape(2, n_sec // 2, 2, own_rows, half)
-        folded = lax.dot_general(
-            proj, units[2], (((0,), (0,)), ((), ())), preferred_element_type=jnp.float32
-        ).astype(jnp.bfloat16)
+
+        def fold(proj_rows, down_rows):
+            return lax.dot_general(
+                proj_rows, down_rows, (((0,), (0,)), ((), ())), preferred_element_type=jnp.float32
+            )
+
+        if ordered:
+            folded = fold(proj, place_rows(d)[0])
+            d[1, 2] = flip(after(d[0, 2], hidden, folded), seq=1)
+            down_rows = d[1, 2].shape[1]
+            at = ((1 - seq_at) * n_dp + (dp_at - 2) % n_dp) * down_rows
+            folded = folded + fold(lax.dynamic_slice_in_dim(proj, at, down_rows, 0), d[1, 2][0])
+        else:
+            folded = fold(proj, down_all)
+        folded = folded.astype(jnp.bfloat16)
 
         def project(x):
             return lax.dot_general(
@@ -234,8 +282,6 @@
             k_idx = (my_start + jnp.arange(count, dtype=jnp.int32)) % count
         count = k_idx.shape[0]
 
-        local_heads = seg_len.shape[0]
-        seg_all, rate_all = head_info[0], head_info[1]
         heads = jnp.arange(n_sec * local_heads, dtype=jnp.int32)
         slide, pos = slide_place(lengths[0], k_idx)
         block = slide[None, :] * count + pos[None, :] // seg_all[:, None]
@@ -250,8 +296,15 @@
             final = pl.pallas_call(
                 lambda *refs: attend_kernel(*refs, heads=local_heads, size=size),
                 out_shape=jax.ShapeDtypeStruct((n_sec, own_rows, width), jnp.bfloat16),
-                in_specs=[pl.BlockSpec(memory_space=pltpu.SMEM)] + [vmem] * 9,
+                in_specs=[pl.BlockSpec(memory_space=pltpu.SMEM)]
+                + [vmem] * 5
+                + [pl.BlockSpec(memory_space=pl.ANY)]
+                + [vmem] * 3,
                 out_specs=vmem,
+                scratch_shapes=[
+                    pltpu.VMEM((4,) + (n_sec,) + slide_w.shape[2:], jnp.bfloat16),
+                    pltpu.SemaphoreType.DMA((4, n_sec)),
+                ],
                 compiler_params=pltpu.CompilerParams(vmem_limit_bytes=48 * 2**20),
                 cost_estimate=pl.CostEstimate(
                     flops=2 * n_sec * count * width * (2 * 768 + 2 * local_heads * own_rows),

time: 165 us -> 180 us (1.091)
  waiting for transfers between devices: 70.3 us -> 85.6 us
  blocking collectives: 5.25 us -> 0 us
  starting transfers between devices: 24 us -> 28.7 us
  other arithmetic: 10.2 us -> 13.4 us
  local copies, waits for them, and re-layouts: 15.5 us -> 13 us
  matrix products: 14.9 us -> 13 us
    ppermute x19 -> x23, waiting for transfers between devices: 32.7 us -> 64.1 us  [flip(): return lax.ppermute(x, names if len(names) > 1 else names[0], pairs)]
    ppermute x3 -> x6, waiting for transfers between devices: 36.8 us -> 20.8 us  [rotate(): return lax.ppermute(x, 'dp', [(i, (i + k) % n_dp) for i in range(n_dp)])]
    all_gather x1 -> x0, blocking collectives: 5.25 us -> none  [per_device(): lax.all_gather(jnp.stack([seg_len, rate]), 'section', axis=1, tiled=True)]
    ppermute x3 -> x6, starting transfers between devices: 3.83 us -> 6.61 us  [rotate(): return lax.ppermute(x, 'dp', [(i, (i + k) % n_dp) for i in range(n_dp)])]
    unnamed x27 -> x36, local copies, waits for them, and re-layouts: 2.21 us -> 0.08 us
    dot_general x2, matrix products: 3.18 us -> 1.16 us  [project(): lax.dot_general(x, folded, (((x.ndim - 1,), (1,)), ((), ())), preferred_e...]
    dynamic_update_slice x8 -> x14, local copies, waits for them, and re-layouts: 9.61 us -> 7.62 us  [place_rows(): whole = lax.dynamic_update_slice(whole, block, (0, at, 0))]
    ppermute x19 -> x23, starting transfers between devices: 20.1 us -> 22 us  [flip(): return lax.ppermute(x, names if len(names) > 1 else names[0], pairs)]
  transfers between devices with their start and end apart: 24 -> 31, of which waited for: 12 -> 15; matrix products, arithmetic and copies ran while one was open for 23% -> 21% of each run, Pallas kernels for 0% -> 0%
where the time goes in v3:
time: 180 us
  waiting for transfers between devices  85.6 us (48%)
  starting transfers between devices  28.7 us (16%)
  between operations  14.2 us (8%)
  other arithmetic  13.4 us (7%)
  local copies, waits for them, and re-layouts  13 us (7%)
  matrix products  13 us (7%)
  Pallas kernels  11.7 us (6%)
    ppermute x23, waiting for transfers between devices, flip(): return lax.ppermute(x, names if len(names) > 1 else names[0], pairs)  64.1 us
    ppermute x23, starting transfers between devices, flip(): return lax.ppermute(x, names if len(names) > 1 else names[0], pairs)  22 us
    ppermute x6, waiting for transfers between devices, rotate(): return lax.ppermute(x, 'dp', [(i, (i + k) % n_dp) for i in range(n_dp)])  20.8 us
    pallas_call x1, Pallas kernels, per_device(): pl.pallas_call(lambda *refs: attend_kernel(*refs, heads=local_heads, size...  11.7 us
    dynamic_update_slice x14, local copies, waits for them, and re-layouts, place_rows(): whole = lax.dynamic_update_slice(whole, block, (0, at, 0))  7.62 us
    ppermute x6, starting transfers between devices, rotate(): return lax.ppermute(x, 'dp', [(i, (i + k) % n_dp) for i in range(n_dp)])  6.61 us
    dot_general x1, matrix products, per_device(): up = jnp.dot(normed, gate_up[1], preferred_element_type=jnp.float32)  4.44 us
    dot_general x2, matrix products, fold(): lax.dot_general(proj_rows, down_rows, (((0,), (0,)), ((), ())), preferred...  3.67 us
  transfers between devices with their start and end apart: 31, of which 15 were waited for; matrix products, arithmetic and copies ran while one was open for 21% of the time, Pallas kernels for 0%

profile of v3, /device:TPU:0, one launch (start us, length us, event | category | flops | bytes accessed | tf_op | source)
XLA Modules:
  0.0 179.5 jit_solution(13388201888115778635)
XLA Ops:
  7.4 1.9 %broadcast_in_dim.24 = bf16[2,1536,512]{2,1,0:T(8,128)(2,1)} broadcast(bf16[]{:T(256)} %constant.193.clone.1), dimensions={} | broadcast | bytes 3145730 | tf_op jit(solution)/shard_map/broadcast_in_dim | solution.py:142
  9.3 1.2 constant_dynamic-update-slice_fusion.7
  10.4 3.0 %collective-permute-start.4 = (bf16[2,192,512]{2,1,0:T(8,128)(2,1)}, bf16[2,192,512]{2,1,0:T(8,128)(2,1)}, u32[]{:S(2)}, u32[]{:S(2)}) collective-permute-start(bf16[2,192,512]{2,1,0:T(8,128)(2,1)} %get-tuple-element.41), channel_id=1, source_target_pairs={{0,1},{1,2},{2,3},{3,0},{4,5},{5,6},{6,7},{7,4},{8,9},{9,10},{10,1... | collective-permute-start | bytes 1179656 | tf_op jit(solution)/shard_map/ppermute | solution.py:122
  13.4 2.0 %collective-permute-start.5 = (bf16[2,192,512]{2,1,0:T(8,128)(2,1)}, bf16[2,192,512]{2,1,0:T(8,128)(2,1)S(1)}, u32[]{:S(2)}, u32[]{:S(2)}) collective-permute-start(bf16[2,192,512]{2,1,0:T(8,128)(2,1)} %get-tuple-element.41), channel_id=1, source_target_pairs={{0,3},{1,0},{2,1},{3,2},{4,7},{5,4},{6,5},{7,6},{8,11},{9,8},{10,9... | collective-permute-start | bytes 1179656 | tf_op jit(solution)/shard_map/ppermute | solution.py:122
  15.5 1.7 collective-permute-start.7
  17.2 1.1 pad_maximum_fusion.2
  18.9 22.1 %collective-permute-done = bf16[512,384]{1,0:T(8,128)(2,1)S(1)} collective-permute-done((bf16[512,384]{1,0:T(8,128)(2,1)S(1)}, bf16[512,384]{1,0:T(8,128)(2,1)S(1)}, u32[]{:S(2)}, u32[]{:S(2)}) %collective-permute-start) | collective-permute-done | bytes 393248 | tf_op jit(solution)/shard_map/ppermute | solution.py:119
  41.1 1.0 fusion.49
  42.1 1.5 collective-permute-start.1
  44.2 1.1 collective-permute-start.6
  45.4 0.8 dynamic-slice_bitcast_fusion.10
  46.5 1.6 collective-permute-start.8
  48.6 1.8 constant_dynamic-update-slice_fusion.6
  50.3 0.8 constant_dynamic-update-slice_fusion.5
  51.1 12.1 %collective-permute-done.6 = bf16[2,192,512]{2,1,0:T(8,128)(2,1)S(1)} collective-permute-done((bf16[2,192,512]{2,1,0:T(8,128)(2,1)}, bf16[2,192,512]{2,1,0:T(8,128)(2,1)S(1)}, u32[]{:S(2)}, u32[]{:S(2)}) %collective-permute-start.6) | collective-permute-done | bytes 393248 | tf_op jit(solution)/shard_map/ppermute | solution.py:122
  63.2 1.5 collective-permute-start.14
  65.5 1.8 constant_dynamic-update-slice_fusion.3
  67.3 9.7 %collective-permute-done.1 = bf16[1040,384]{1,0:T(8,128)(2,1)} collective-permute-done((bf16[1040,384]{1,0:T(8,128)(2,1)}, bf16[1040,384]{1,0:T(8,128)(2,1)}, u32[]{:S(2)}, u32[]{:S(2)}) %collective-permute-start.1) | collective-permute-done | bytes 798752 | tf_op jit(solution)/shard_map/ppermute | solution.py:119
  78.7 0.8 constant_dynamic-update-slice_fusion.1
  79.5 1.6 collective-permute-start.10
  81.1 4.0 %collective-permute-done.12 = bf16[1,192,512]{2,1,0:T(8,128)(2,1)S(1)} collective-permute-done((bf16[1,192,512]{2,1,0:T(8,128)(2,1)S(1)}, bf16[1,192,512]{2,1,0:T(8,128)(2,1)S(1)}, u32[]{:S(2)}, u32[]{:S(2)}) %collective-permute-start.12) | collective-permute-done | bytes 196640 | tf_op jit(solution)/shard_map/ppermute | solution.py:122
  85.1 1.2 collective-permute-start.15
  86.4 5.2 %collective-permute-done.10 = bf16[2,192,512]{2,1,0:T(8,128)(2,1)S(1)} collective-permute-done((bf16[2,192,512]{2,1,0:T(8,128)(2,1)S(1)}, bf16[2,192,512]{2,1,0:T(8,128)(2,1)S(1)}, u32[]{:S(2)}, u32[]{:S(2)}) %collective-permute-start.10) | collective-permute-done | bytes 393248 | tf_op jit(solution)/shard_map/ppermute | solution.py:119
  91.6 1.6 collective-permute-start.16
  93.1 0.8 constant_dynamic-update-slice_fusion
  94.0 1.5 pad_maximum_fusion
  95.5 1.3 dynamic-slice_bitcast_fusion.3
  97.9 0.9 convert_reduce_fusion
  98.9 1.0 fusion.2
  99.9 1.0 fusion.4
  100.9 3.2 %fusion.6 = f32[1024,512]{1,0:T(8,128)S(1)} fusion(bf16[1024,1536]{1,0:T(8,128)(2,1)S(1)} %fusion.4, bf16[2,1536,512]{2,1,0:T(8,128)(2,1)} %constant_dynamic-update-slice_fusion), kind=kOutput, calls=%fused_computation.13 | convolution fusion | flops 1610612736 | bytes 6815744 | tf_op jit(solution)/shard_map/dot_general | solution.py:219
  104.2 4.4 %multiply_convert_fusion = bf16[1024,512]{1,0:T(8,128)(2,1)} fusion(f32[1024,512]{1,0:T(8,128)S(1)} %fusion.6, bf16[1024,1536]{1,0:T(8,128)(2,1)S(1)} %fusion.4, bf16[2,1536,512]{2,1,0:T(8,128)(2,1)} %constant_dynamic-update-slice_fusion), kind=kOutput, calls=%fused_computation.9 | convolution fusion | flops 1613758464 | bytes 7864320 | tf_op jit(solution)/shard_map/dot_general | solution.py:220
  108.6 4.7 %collective-permute-done.13 = bf16[1,192,512]{2,1,0:T(8,128)(2,1)S(1)} collective-permute-done((bf16[1,192,512]{2,1,0:T(8,128)(2,1)S(1)}, bf16[1,192,512]{2,1,0:T(8,128)(2,1)S(1)}, u32[]{:S(2)}, u32[]{:S(2)}) %collective-permute-start.13) | collective-permute-done | bytes 196640 | tf_op jit(solution)/shard_map/ppermute | solution.py:122
  113.5 3.2 %convolution_bitcast_fusion = f32[768,512]{0,1:T(8,128)S(1)} fusion(bf16[1536,512]{1,0:T(8,128)(2,1)S(1)} %bitcast_dynamic-update-slice_fusion, bf16[1536,768]{1,0:T(8,128)(2,1)} %all-gather.4.cloned.1.call-done), kind=kOutput, calls=%fused_computation.16 | convolution fusion | flops 1207959552 | bytes 5505024 | tf_op jit(solution)/shard_map/dot_general | solution.py:225
  117.3 5.2 %collective-permute-done.17 = bf16[1,192,512]{2,1,0:T(8,128)(2,1)S(1)} collective-permute-done((bf16[1,192,512]{2,1,0:T(8,128)(2,1)S(1)}, bf16[1,192,512]{2,1,0:T(8,128)(2,1)S(1)}, u32[]{:S(2)}, u32[]{:S(2)}) %collective-permute-start.17) | collective-permute-done | bytes 196640 | tf_op jit(solution)/shard_map/ppermute | solution.py:119
  124.5 1.4 collective-permute-done.18
  126.6 2.5 %collective-permute-start.19 = (bf16[128,768]{1,0:T(8,128)(2,1)S(1)}, bf16[128,768]{1,0:T(8,128)(2,1)S(1)}, u32[]{:S(2)}, u32[]{:S(2)}) collective-permute-start(bf16[128,768]{1,0:T(8,128)(2,1)S(1)} %get-tuple-element.42), channel_id=1, source_target_pairs={{0,16},{8,24},{16,0},{24,8},{1,17},{9,25},{17,1},{25,9},{2,18},{10... | collective-permute-start | bytes 589832 | tf_op jit(solution)/shard_map/ppermute | solution.py:119
  129.1 1.6 collective-permute-start.20
  131.2 7.3 %collective-permute-done.19 = bf16[128,768]{1,0:T(8,128)(2,1)S(1)} collective-permute-done((bf16[128,768]{1,0:T(8,128)(2,1)S(1)}, bf16[128,768]{1,0:T(8,128)(2,1)S(1)}, u32[]{:S(2)}, u32[]{:S(2)}) %collective-permute-start.19) | collective-permute-done | bytes 196640 | tf_op jit(solution)/shard_map/ppermute | solution.py:119
  138.5 1.3 collective-permute-done.20
  140.3 1.7 collective-permute-start.22
  142.4 1.4 collective-permute-start.24
  144.0 4.2 %collective-permute-done.22.refs_2_ = bf16[128,768]{1,0:T(8,128)(2,1)S(1)} collective-permute-done((bf16[128,768]{1,0:T(8,128)(2,1)S(1)}, bf16[128,768]{1,0:T(8,128)(2,1)S(1)}, u32[]{:S(2)}, u32[]{:S(2)}) %collective-permute-start.22) | collective-permute-done | bytes 196640 | tf_op jit(solution)/shard_map/ppermute | solution.py:119
  148.2 3.6 %collective-permute-done.23.refs_3_ = bf16[128,768]{1,0:T(8,128)(2,1)S(1)} collective-permute-done((bf16[128,768]{1,0:T(8,128)(2,1)S(1)}, bf16[128,768]{1,0:T(8,128)(2,1)S(1)}, u32[]{:S(2)}, u32[]{:S(2)}) %collective-permute-start.23) | collective-permute-done | bytes 196640 | tf_op jit(solution)/shard_map/ppermute | solution.py:119
  152.2 1.4 fusion.28
  154.3 11.7 %shard_map.118 = bf16[4,128,192]{2,1,0:T(8,128)(2,1)S(1)} custom-call(s32[1]{0:T(128)} %bitcast.refs_0_, bf16[128,768]{1,0:T(8,128)(2,1)S(1)} %multiply_convert_fusion.1.refs_1_, bf16[128,768]{1,0:T(8,128)(2,1)S(1)} %collective-permute-done.22.refs_2_, bf16[128,768]{1,0:T(8,128)(2,1)S(1)} %collective-permute-done.23.refs_3_, ...), custom_call_target="tpu_custom_call" | custom-call | flops 4026531840 | bytes 8388608 | tf_op jit(solution)/shard_map/pallas_call | solution.py:296
  166.8 1.1 collective-permute-start.28
  167.9 3.2 %collective-permute-done.27 = bf16[128,192]{1,0:T(8,128)(2,1)S(1)} collective-permute-done((bf16[128,192]{1,0:T(8,128)(2,1)S(1)}, bf16[128,192]{1,0:T(8,128)(2,1)S(1)}, u32[]{:S(2)}, u32[]{:S(2)}) %collective-permute-start.27) | collective-permute-done | bytes 49184 | tf_op jit(solution)/shard_map/ppermute | solution.py:119
  (135 shorter events, 14.5 us)
Async XLA Ops:
  6.5 2.7 %copy-start.5 = (bf16[192,1024]{1,0:T(8,128)(2,1)S(1)}, bf16[192,1024]{1,0:T(8,128)(2,1)}, u32[]{:S(2)}) copy-start(bf16[192,1024]{1,0:T(8,128)(2,1)} %param.14) | copy-start | bytes 1179652
  6.5 2.7 %copy-start.4 = (bf16[192,1024]{1,0:T(8,128)(2,1)S(1)}, bf16[192,1024]{1,0:T(8,128)(2,1)}, u32[]{:S(2)}) copy-start(bf16[192,1024]{1,0:T(8,128)(2,1)} %param.15) | copy-start | bytes 1179652
  6.5 8.9 %copy-start.3 = (bf16[1,512,384]{2,1,0:T(8,128)(2,1)S(1)}, bf16[1,512,384]{2,1,0:T(8,128)(2,1)}, u32[]{:S(2)}) copy-start(bf16[1,512,384]{2,1,0:T(8,128)(2,1)} %param.12) | copy-start | bytes 1179652
  6.5 10.7 %copy-start.1 = (bf16[3,768,192]{1,2,0:T(8,128)(2,1)S(1)}, bf16[3,768,192]{1,2,0:T(8,128)(2,1)}, u32[]{:S(2)}) copy-start(bf16[3,768,192]{1,2,0:T(8,128)(2,1)} %param.19) | copy-start | bytes 2654212
  6.5 10.7 %copy-start.6 = (bf16[192,768]{1,0:T(8,128)(2,1)S(1)}, bf16[192,768]{1,0:T(8,128)(2,1)}, u32[]{:S(2)}) copy-start(bf16[192,768]{1,0:T(8,128)(2,1)} %param.20) | copy-start | bytes 884740
  6.5 106.9 %all-gather.4.cloned.1.call-start = ((), (), s32[]{:S(2)}) async-start(), calls=%async_computation | async-start | bytes 2949120 | tf_op jit(solution)/shard_map/all_gather | solution.py:215
  7.3 147.0 %all-gather.6.cloned.1.call-start = ((), (), s32[]{:S(2)}) async-start(), calls=%async_computation.1 | async-start | bytes 5898240 | tf_op jit(solution)/shard_map/all_gather | solution.py:217
  9.2 9.2 %copy-start.16 = (s32[4]{0:T(128)S(1)}, s32[4]{0:T(128)}, u32[]{:S(2)}) copy-start(s32[4]{0:T(128)} %param.22) | copy-start | bytes 52
  9.3 9.2 %copy-start.17 = (s32[4]{0:T(128)S(1)}, s32[4]{0:T(128)}, u32[]{:S(2)}) copy-start(s32[4]{0:T(128)} %param.23) | copy-start | bytes 52
  9.3 9.3 %copy-start.15 = (s32[1,3]{1,0:T(1,128)S(1)}, s32[1,3]{1,0:T(1,128)}, u32[]{:S(2)}) copy-start(s32[1,3]{1,0:T(1,128)} %param.21) | copy-start | bytes 40
  10.4 34.9 %copy-start.2 = (bf16[1024,192]{0,1:T(8,128)(2,1)S(1)}, bf16[1024,192]{0,1:T(8,128)(2,1)}, u32[]{:S(2)}) copy-start(bf16[1024,192]{0,1:T(8,128)(2,1)} %param.16) | copy-start | bytes 1179652
  10.4 33.8 %collective-permute-start.4 = (bf16[2,192,512]{2,1,0:T(8,128)(2,1)}, bf16[2,192,512]{2,1,0:T(8,128)(2,1)}, u32[]{:S(2)}, u32[]{:S(2)}) collective-permute-start(bf16[2,192,512]{2,1,0:T(8,128)(2,1)} %get-tuple-element.41), channel_id=1, source_target_pairs={{0,1},{1,2},{2,3},{3,0},{4,5},{5,6},{6,7},{7,4},{8,9},{9,10},{10,1... | collective-permute-start | bytes 1179656 | tf_op jit(solution)/shard_map/ppermute | solution.py:122
  13.4 34.7 %collective-permute-start.5 = (bf16[2,192,512]{2,1,0:T(8,128)(2,1)}, bf16[2,192,512]{2,1,0:T(8,128)(2,1)S(1)}, u32[]{:S(2)}, u32[]{:S(2)}) collective-permute-start(bf16[2,192,512]{2,1,0:T(8,128)(2,1)} %get-tuple-element.41), channel_id=1, source_target_pairs={{0,3},{1,0},{2,1},{3,2},{4,7},{5,4},{6,5},{7,6},{8,11},{9,8},{10,9... | collective-permute-start | bytes 1179656 | tf_op jit(solution)/shard_map/ppermute | solution.py:122
  15.4 25.6 %collective-permute-start = (bf16[512,384]{1,0:T(8,128)(2,1)S(1)}, bf16[512,384]{1,0:T(8,128)(2,1)S(1)}, u32[]{:S(2)}, u32[]{:S(2)}) collective-permute-start(bf16[512,384]{1,0:T(8,128)(2,1)S(1)} %bitcast.151), channel_id=1, source_target_pairs={{0,1},{1,0},{2,3},{3,2},{4,5},{5,4},{6,7},{7,6},{8,9},{9,8},{10,11... | collective-permute-start | bytes 1179656 | tf_op jit(solution)/shard_map/ppermute | solution.py:119
  15.5 50.1 %collective-permute-start.7 = (bf16[2,192,512]{2,1,0:T(8,128)(2,1)}, bf16[2,192,512]{2,1,0:T(8,128)(2,1)}, u32[]{:S(2)}, u32[]{:S(2)}) collective-permute-start(bf16[2,192,512]{2,1,0:T(8,128)(2,1)} %get-tuple-element.12), channel_id=1, source_target_pairs={{0,4},{4,0},{1,5},{5,1},{2,6},{6,2},{3,7},{7,3},{8,12},{12,8},{9,1... | collective-permute-start | bytes 1179656 | tf_op jit(solution)/shard_map/ppermute | solution.py:119
  42.1 34.9 %collective-permute-start.1 = (bf16[1040,384]{1,0:T(8,128)(2,1)}, bf16[1040,384]{1,0:T(8,128)(2,1)}, u32[]{:S(2)}, u32[]{:S(2)}) collective-permute-start(bf16[1040,384]{1,0:T(8,128)(2,1)} %get-tuple-element.11), channel_id=1, source_target_pairs={{0,16},{8,24},{16,0},{24,8},{1,17},{9,25},{17,1},{25,9},{2,18},{10... | collective-permute-start | bytes 2396168 | tf_op jit(solution)/shard_map/ppermute | solution.py:119
  44.2 19.0 %collective-permute-start.6 = (bf16[2,192,512]{2,1,0:T(8,128)(2,1)}, bf16[2,192,512]{2,1,0:T(8,128)(2,1)S(1)}, u32[]{:S(2)}, u32[]{:S(2)}) collective-permute-start(bf16[2,192,512]{2,1,0:T(8,128)(2,1)} %get-tuple-element.12), channel_id=1, source_target_pairs={{0,2},{1,3},{2,0},{3,1},{4,6},{5,7},{6,4},{7,5},{8,10},{9,11},{10,... | collective-permute-start | bytes 1179656 | tf_op jit(solution)/shard_map/ppermute | solution.py:122
  46.3 32.0 %copy-start.9 = (bf16[1,192,512]{2,1,0:T(8,128)(2,1)S(1)}, bf16[1,192,512]{2,1,0:T(8,128)(2,1)}, u32[]{:S(2)}) copy-start(bf16[1,192,512]{2,1,0:T(8,128)(2,1)} %get-tuple-element.13) | copy-start | bytes 589828
  46.5 30.6 %collective-permute-start.8 = (bf16[2,192,512]{2,1,0:T(8,128)(2,1)}, bf16[2,192,512]{2,1,0:T(8,128)(2,1)S(1)}, u32[]{:S(2)}, u32[]{:S(2)}) collective-permute-start(bf16[2,192,512]{2,1,0:T(8,128)(2,1)} %collective-permute-done.4), channel_id=1, source_target_pairs={{0,4},{4,0},{1,5},{5,1},{2,6},{6,2},{3,7},{7,3},{8,12},{12,8},{9,1... | collective-permute-start | bytes 1179656 | tf_op jit(solution)/shard_map/ppermute | solution.py:119
  48.1 30.2 %collective-permute-start.9 = (bf16[2,192,512]{2,1,0:T(8,128)(2,1)S(1)}, bf16[2,192,512]{2,1,0:T(8,128)(2,1)S(1)}, u32[]{:S(2)}, u32[]{:S(2)}) collective-permute-start(bf16[2,192,512]{2,1,0:T(8,128)(2,1)S(1)} %collective-permute-done.5), channel_id=1, source_target_pairs={{0,4},{4,0},{1,5},{5,1},{2,6},{6,2},{3,7},{7,3},{8,12},{12,8},{9,1... | collective-permute-start | bytes 1179656 | tf_op jit(solution)/shard_map/ppermute | solution.py:119
  63.2 50.1 %collective-permute-start.14 = (bf16[1,192,512]{2,1,0:T(8,128)(2,1)}, bf16[1,192,512]{2,1,0:T(8,128)(2,1)S(1)}, u32[]{:S(2)}, u32[]{:S(2)}) collective-permute-start(bf16[1,192,512]{2,1,0:T(8,128)(2,1)} %get-tuple-element.15), channel_id=1, source_target_pairs={{0,4},{4,0},{1,5},{5,1},{2,6},{6,2},{3,7},{7,3},{8,12},{12,8},{9,1... | collective-permute-start | bytes 589832 | tf_op jit(solution)/shard_map/ppermute | solution.py:119
  65.5 14.0 %collective-permute-start.11 = (bf16[1,192,512]{2,1,0:T(8,128)(2,1)}, bf16[1,192,512]{2,1,0:T(8,128)(2,1)S(1)}, u32[]{:S(2)}, u32[]{:S(2)}) collective-permute-start(bf16[1,192,512]{2,1,0:T(8,128)(2,1)} %get-tuple-element.13), channel_id=1, source_target_pairs={{0,1},{1,2},{2,3},{3,0},{4,5},{5,6},{6,7},{7,4},{8,9},{9,10},{10,1... | collective-permute-start | bytes 589832 | tf_op jit(solution)/shard_map/ppermute | solution.py:122
  77.0 16.9 %collective-permute-start.2 = (bf16[1040,384]{1,0:T(8,128)(2,1)}, bf16[1040,384]{1,0:T(8,128)(2,1)S(1)}, u32[]{:S(2)}, u32[]{:S(2)}) collective-permute-start(bf16[1040,384]{1,0:T(8,128)(2,1)} %get-tuple-element.11), channel_id=1, source_target_pairs={{0,8},{8,0},{16,24},{24,16},{1,9},{9,1},{17,25},{25,17},{2,10},{10... | collective-permute-start | bytes 2396168 | tf_op jit(solution)/shard_map/ppermute | solution.py:119
  77.0 16.9 %collective-permute-start.3 = (bf16[1040,384]{1,0:T(8,128)(2,1)}, bf16[1040,384]{1,0:T(8,128)(2,1)S(1)}, u32[]{:S(2)}, u32[]{:S(2)}) collective-permute-start(bf16[1040,384]{1,0:T(8,128)(2,1)} %collective-permute-done.1), channel_id=1, source_target_pairs={{0,8},{8,0},{16,24},{24,16},{1,9},{9,1},{17,25},{25,17},{2,10},{10... | collective-permute-start | bytes 2396168 | tf_op jit(solution)/shard_map/ppermute | solution.py:119
  78.3 6.8 %collective-permute-start.12 = (bf16[1,192,512]{2,1,0:T(8,128)(2,1)S(1)}, bf16[1,192,512]{2,1,0:T(8,128)(2,1)S(1)}, u32[]{:S(2)}, u32[]{:S(2)}) collective-permute-start(bf16[1,192,512]{2,1,0:T(8,128)(2,1)S(1)} %copy-done.9), channel_id=1, source_target_pairs={{0,3},{1,0},{2,1},{3,2},{4,7},{5,4},{6,5},{7,6},{8,11},{9,8},{10,9... | collective-permute-start | bytes 589832 | tf_op jit(solution)/shard_map/ppermute | solution.py:122
  79.5 12.0 %collective-permute-start.10 = (bf16[2,192,512]{2,1,0:T(8,128)(2,1)S(1)}, bf16[2,192,512]{2,1,0:T(8,128)(2,1)S(1)}, u32[]{:S(2)}, u32[]{:S(2)}) collective-permute-start(bf16[2,192,512]{2,1,0:T(8,128)(2,1)S(1)} %collective-permute-done.6), channel_id=1, source_target_pairs={{0,4},{4,0},{1,5},{5,1},{2,6},{6,2},{3,7},{7,3},{8,12},{12,8},{9,1... | collective-permute-start | bytes 1179656 | tf_op jit(solution)/shard_map/ppermute | solution.py:119
  85.1 28.2 %collective-permute-start.15 = (bf16[1,192,512]{2,1,0:T(8,128)(2,1)S(1)}, bf16[1,192,512]{2,1,0:T(8,128)(2,1)S(1)}, u32[]{:S(2)}, u32[]{:S(2)}) collective-permute-start(bf16[1,192,512]{2,1,0:T(8,128)(2,1)S(1)} %collective-permute-done.11), channel_id=1, source_target_pairs={{0,4},{4,0},{1,5},{5,1},{2,6},{6,2},{3,7},{7,3},{8,12},{12,8},{9,1... | collective-permute-start | bytes 589832 | tf_op jit(solution)/shard_map/ppermute | solution.py:119
  91.6 21.8 %collective-permute-start.16 = (bf16[1,192,512]{2,1,0:T(8,128)(2,1)S(1)}, bf16[1,192,512]{2,1,0:T(8,128)(2,1)S(1)}, u32[]{:S(2)}, u32[]{:S(2)}) collective-permute-start(bf16[1,192,512]{2,1,0:T(8,128)(2,1)S(1)} %collective-permute-done.12), channel_id=1, source_target_pairs={{0,4},{4,0},{1,5},{5,1},{2,6},{6,2},{3,7},{7,3},{8,12},{12,8},{9,1... | collective-permute-start | bytes 589832 | tf_op jit(solution)/shard_map/ppermute | solution.py:119
  100.9 3.2 %copy-start.8 = (bf16[1,192,512]{2,1,0:T(8,128)(2,1)S(1)}, bf16[1,192,512]{2,1,0:T(8,128)(2,1)}, u32[]{:S(2)}) copy-start(bf16[1,192,512]{2,1,0:T(8,128)(2,1)} %get-tuple-element.15) | copy-start | bytes 589828
  104.1 9.2 %collective-permute-start.13 = (bf16[1,192,512]{2,1,0:T(8,128)(2,1)S(1)}, bf16[1,192,512]{2,1,0:T(8,128)(2,1)S(1)}, u32[]{:S(2)}, u32[]{:S(2)}) collective-permute-start(bf16[1,192,512]{2,1,0:T(8,128)(2,1)S(1)} %copy-done.8), channel_id=1, source_target_pairs={{0,2},{1,3},{2,0},{3,1},{4,6},{5,7},{6,4},{7,5},{8,10},{9,11},{10,... | collective-permute-start | bytes 589832 | tf_op jit(solution)/shard_map/ppermute | solution.py:122
  113.4 3.9 %copy-start.14 = (s32[1,12]{1,0:T(1,128)S(1)}, s32[1,12]{1,0:T(1,128)}, u32[]{:S(2)}) copy-start(s32[1,12]{1,0:T(1,128)} %slice_convert_fusion.3) | copy-start | bytes 148
  113.5 9.0 %copy-start = (bf16[1536,768]{1,0:T(8,128)(2,1)S(1)}, bf16[1536,768]{1,0:T(8,128)(2,1)}, u32[]{:S(2)}) copy-start(bf16[1536,768]{1,0:T(8,128)(2,1)} %all-gather.4.cloned.1.call-done) | copy-start | bytes 7077892
  113.5 9.4 %copy-start.7 = (bf16[1024,512]{1,0:T(8,128)(2,1)S(1)}, bf16[1024,512]{1,0:T(8,128)(2,1)}, u32[]{:S(2)}) copy-start(bf16[1024,512]{1,0:T(8,128)(2,1)} %multiply_convert_fusion) | copy-start | bytes 3145732
  116.8 5.7 %collective-permute-start.17 = (bf16[1,192,512]{2,1,0:T(8,128)(2,1)S(1)}, bf16[1,192,512]{2,1,0:T(8,128)(2,1)S(1)}, u32[]{:S(2)}, u32[]{:S(2)}) collective-permute-start(bf16[1,192,512]{2,1,0:T(8,128)(2,1)S(1)} %collective-permute-done.13), channel_id=1, source_target_pairs={{0,4},{4,0},{1,5},{5,1},{2,6},{6,2},{3,7},{7,3},{8,12},{12,8},{9,1... | collective-permute-start | bytes 589832 | tf_op jit(solution)/shard_map/ppermute | solution.py:119
  123.5 2.4 %collective-permute-start.18 = (bf16[2,2,128,768]{3,2,1,0:T(8,128)(2,1)S(1)}, bf16[2,2,128,768]{3,2,1,0:T(8,128)(2,1)S(1)}, u32[]{:S(2)}, u32[]{:S(2)}) collective-permute-start(bf16[2,2,128,768]{3,2,1,0:T(8,128)(2,1)S(1)} %convolution_convert_fusion), channel_id=1, source_target_pairs={{0,8},{8,0},{16,24},{24,16},{1,9},{9,1},{17,25},{25,17},{2,10},{10... | collective-permute-start | bytes 2359304 | tf_op jit(solution)/shard_map/ppermute | solution.py:119
  126.5 13.7 %copy-start.10 = (f32[768]{0:T(1024)S(1)}, f32[768]{0:T(1024)}, u32[]{:S(2)}) copy-start(f32[768]{0:T(1024)} %param.18) | copy-start | bytes 9220
  126.6 11.9 %collective-permute-start.19 = (bf16[128,768]{1,0:T(8,128)(2,1)S(1)}, bf16[128,768]{1,0:T(8,128)(2,1)S(1)}, u32[]{:S(2)}, u32[]{:S(2)}) collective-permute-start(bf16[128,768]{1,0:T(8,128)(2,1)S(1)} %get-tuple-element.42), channel_id=1, source_target_pairs={{0,16},{8,24},{16,0},{24,8},{1,17},{9,25},{17,1},{25,9},{2,18},{10... | collective-permute-start | bytes 589832 | tf_op jit(solution)/shard_map/ppermute | solution.py:119
  129.0 9.4 %collective-permute-start.21 = (bf16[128,768]{1,0:T(8,128)(2,1)S(1)}, bf16[128,768]{1,0:T(8,128)(2,1)S(1)}, u32[]{:S(2)}, u32[]{:S(2)}) collective-permute-start(bf16[128,768]{1,0:T(8,128)(2,1)S(1)} %get-tuple-element.43), channel_id=1, source_target_pairs={{0,17},{1,16},{2,19},{3,18},{8,25},{9,24},{10,27},{11,26},{16,1},{... | collective-permute-start | bytes 589832 | tf_op jit(solution)/shard_map/ppermute | solution.py:119
  129.1 10.7 %collective-permute-start.20 = (bf16[128,768]{1,0:T(8,128)(2,1)S(1)}, bf16[128,768]{1,0:T(8,128)(2,1)S(1)}, u32[]{:S(2)}, u32[]{:S(2)}) collective-permute-start(bf16[128,768]{1,0:T(8,128)(2,1)S(1)} %fusion.24), channel_id=1, source_target_pairs={{0,1},{1,0},{2,3},{3,2},{4,5},{5,4},{6,7},{7,6},{8,9},{9,8},{10,11... | collective-permute-start | bytes 589832 | tf_op jit(solution)/shard_map/ppermute | solution.py:119
  131.2 21.1 %copy-start.11 = (s32[1024]{0:T(1024)S(1)}, s32[1024]{0:T(1024)}, u32[]{:S(2)}) copy-start(s32[1024]{0:T(1024)} %get-tuple-element.24) | copy-start | bytes 12292
  131.2 21.1 %copy-start.12 = (s32[1024]{0:T(1024)S(1)}, s32[1024]{0:T(1024)}, u32[]{:S(2)}) copy-start(s32[1024]{0:T(1024)} %get-tuple-element.67) | copy-start | bytes 12292
  140.3 7.9 %collective-permute-start.22 = (bf16[128,768]{1,0:T(8,128)(2,1)S(1)}, bf16[128,768]{1,0:T(8,128)(2,1)S(1)}, u32[]{:S(2)}, u32[]{:S(2)}) collective-permute-start(bf16[128,768]{1,0:T(8,128)(2,1)S(1)} %multiply_convert_fusion.1.refs_1_), channel_id=1, source_target_pairs={{0,16},{8,24},{16,0},{24,8},{1,17},{9,25},{17,1},{25,9},{2,18},{10... | collective-permute-start | bytes 589832 | tf_op jit(solution)/shard_map/ppermute | solution.py:119
  142.0 9.8 %collective-permute-start.23 = (bf16[128,768]{1,0:T(8,128)(2,1)S(1)}, bf16[128,768]{1,0:T(8,128)(2,1)S(1)}, u32[]{:S(2)}, u32[]{:S(2)}) collective-permute-start(bf16[128,768]{1,0:T(8,128)(2,1)S(1)} %multiply_convert_fusion.1.refs_1_), channel_id=1, source_target_pairs={{0,4},{4,0},{1,5},{5,1},{2,6},{6,2},{3,7},{7,3},{8,12},{12,8},{9,1... | collective-permute-start | bytes 589832 | tf_op jit(solution)/shard_map/ppermute | solution.py:119
  142.4 9.4 %collective-permute-start.24 = (bf16[128,768]{1,0:T(8,128)(2,1)S(1)}, bf16[128,768]{1,0:T(8,128)(2,1)S(1)}, u32[]{:S(2)}, u32[]{:S(2)}) collective-permute-start(bf16[128,768]{1,0:T(8,128)(2,1)S(1)} %multiply_convert_fusion.1.refs_1_), channel_id=1, source_target_pairs={{0,20},{4,16},{8,28},{12,24},{16,4},{20,0},{24,12},{28,8},{1,21},{... | collective-permute-start | bytes 589832 | tf_op jit(solution)/shard_map/ppermute | solution.py:119
  151.9 2.4 %collective-permute-start.25 = (bf16[4,128,768]{2,1,0:T(8,128)(2,1)S(1)}, bf16[4,128,768]{2,1,0:T(8,128)(2,1)S(1)}, u32[]{:S(2)}, u32[]{:S(2)}) collective-permute-start(bf16[4,128,768]{2,1,0:T(8,128)(2,1)S(1)} %pad_maximum_fusion.4), channel_id=1, source_target_pairs={{0,8},{8,0},{16,24},{24,16},{1,9},{9,1},{17,25},{25,17},{2,10},{10... | collective-permute-start | bytes 2359304 | tf_op jit(solution)/shard_map/ppermute | solution.py:119
  166.0 1.9 %collective-permute-start.26 = (bf16[128,192]{1,0:T(8,128)(2,1)S(1)}, bf16[128,192]{1,0:T(8,128)(2,1)S(1)}, u32[]{:S(2)}, u32[]{:S(2)}) collective-permute-start(bf16[128,192]{1,0:T(8,128)(2,1)S(1)} %get-tuple-element.53), channel_id=1, source_target_pairs={{0,8},{8,0},{16,24},{24,16},{1,9},{9,1},{17,25},{25,17},{2,10},{10... | collective-permute-start | bytes 147464 | tf_op jit(solution)/shard_map/ppermute | solution.py:119
  166.2 4.9 %collective-permute-start.27 = (bf16[128,192]{1,0:T(8,128)(2,1)S(1)}, bf16[128,192]{1,0:T(8,128)(2,1)S(1)}, u32[]{:S(2)}, u32[]{:S(2)}) collective-permute-start(bf16[128,192]{1,0:T(8,128)(2,1)S(1)} %get-tuple-element.52), channel_id=1, source_target_pairs={{0,16},{8,24},{16,0},{24,8},{1,17},{9,25},{17,1},{25,9},{2,18},{10... | collective-permute-start | bytes 147464 | tf_op jit(solution)/shard_map/ppermute | solution.py:119
  166.8 4.6 %collective-permute-start.28 = (bf16[128,192]{1,0:T(8,128)(2,1)S(1)}, bf16[128,192]{1,0:T(8,128)(2,1)S(1)}, u32[]{:S(2)}, u32[]{:S(2)}) collective-permute-start(bf16[128,192]{1,0:T(8,128)(2,1)S(1)} %get-tuple-element.51), channel_id=1, source_target_pairs={{0,24},{8,16},{16,8},{24,0},{1,25},{9,17},{17,9},{25,1},{2,26},{10... | collective-permute-start | bytes 147464 | tf_op jit(solution)/shard_map/ppermute | solution.py:119
  (1 other events, 1.1 us)
Sparse Core Ops, SparseCore 0:
  8.9 26.7 all-gather.3
  37.3 51.0 all-gather.5

commit v4 on v3

v4 whole, which is shorter than its diff:
```python
import math

import jax
import jax.numpy as jnp
from jax import lax
from jax.experimental import pallas as pl
from jax.experimental.pallas import tpu as pltpu
from jax.sharding import PartitionSpec as P

NEG = -1e30
AXES = ("section", "seq", "dp")


def layer_norm(rows, gain):
    mean = jnp.mean(rows, axis=-1, keepdims=True)
    centered = rows - mean
    var = jnp.mean(centered * centered, axis=-1, keepdims=True)
    return centered * lax.rsqrt(var + 1e-06) * gain


def slide_place(lengths_row, index):
    ends = jnp.cumsum(lengths_row, dtype=jnp.int32)
    after = index[:, None] >= ends[None, :]
    slide = jnp.sum(after.astype(jnp.int32), axis=1, dtype=jnp.int32)
    before = jnp.sum(jnp.where(after, lengths_row[None, :], 0), axis=1, dtype=jnp.int32)
    return (slide, index - before)


def attend_kernel(sec_ref, near_ref, *refs, heads, masks):
    far, refs = refs[:3], refs[3:]
    core_ref, w_ref, out_w_ref, emb_ref, q_ref, k_ref, keep_ref, send_ref = refs
    own = near_ref.shape[0]
    keys = jnp.concatenate(
        [near_ref[...], far[0][...], core_ref[0], core_ref[1], far[1][...], far[2][...]]
        + [core_ref[2], core_ref[3]],
        axis=0,
    )
    count, rows = keys.shape[0], q_ref.shape[0]
    width = w_ref.shape[1]
    size = width // heads
    scale = math.log2(math.e) / math.sqrt(size)

    def project(x, which):
        return lax.dot_general(
            x, w_ref[which], (((1,), (1,)), ((), ())), preferred_element_type=jnp.float32
        ).astype(jnp.bfloat16)

    key, query, value = project(keys, 1), project(keys[:rows], 0), project(keys, 2)
    lane_head = lax.broadcasted_iota(jnp.int32, (rows, width), 1) // size
    diag = lax.broadcasted_iota(jnp.int32, (rows, count), 0) == lax.broadcasted_iota(
        jnp.int32, (rows, count), 1
    )
    att = jnp.zeros((rows, width), jnp.float32)
    for h in range(heads):
        scores = lax.dot_general(
            jnp.where(lane_head == h, query, jnp.zeros_like(query)),
            key,
            (((1,), (1,)), ((), ())),
            preferred_element_type=jnp.float32,
        )
        ok = (q_ref[:, h : h + 1] == k_ref[h : h + 1, :]) | diag
        scores = jnp.where(ok, scores, NEG)
        top = jnp.max(scores, axis=1, keepdims=True)
        weight = jnp.exp2((scores - top) * scale)
        total = jnp.sum(weight, axis=1, keepdims=True)
        mixed = jnp.dot(weight.astype(jnp.bfloat16), value, preferred_element_type=jnp.float32)
        att = jnp.where(lane_head == h, mixed / total, att)
    att = att.astype(jnp.bfloat16)
    for m in range(len(masks)):
        part = jnp.dot(att, out_w_ref[m], preferred_element_type=jnp.float32)
        target = send_ref if m % 2 else keep_ref
        for block, mask in enumerate(masks):
            piece = part[block * own : (block + 1) * own]
            if block == 0:
                piece = piece + emb_ref[m]
            at = pl.multiple_of((mask ^ sec_ref[0]) * own, own)
            target[m // 2, pl.ds(at, own), :] = piece.astype(target.dtype)


def build(n_sec, n_seq, n_dp):
    sizes = {"section": n_sec, "seq": n_seq, "dp": n_dp}

    def flip(x, **masks):
        names = tuple(a for a in AXES if masks.get(a))
        pairs = []
        total = math.prod(sizes[a] for a in names)
        for source in range(total):
            rest, coords = source, []
            for a in reversed(names):
                coords.append(rest % sizes[a])
                rest //= sizes[a]
            target = 0
            for a, c in zip(names, reversed(coords)):
                target = target * sizes[a] + (c ^ masks[a])
            pairs.append((source, target))
        return lax.ppermute(x, names if len(names) > 1 else names[0], pairs)

    def rotate(x, k):
        return lax.ppermute(x, "dp", [(i, (i + k) % n_dp) for i in range(n_dp)])

    def after(x, *others):
        return lax.optimization_barrier((x,) + others)[0]

    def gather_section(x):
        across = flip(x, section=2)
        return [x, flip(after(x, across), section=1), across, flip(across, section=1)]

    def gather_rows(same, other, seq_at, dp_at):
        mats, rows, units = same.shape
        part = jnp.zeros((mats, n_dp * rows, units), same.dtype)
        for k in range(n_dp):
            block = rotate(other if k % 2 else same, k) if k else same
            part = lax.dynamic_update_slice(part, block, (0, ((dp_at - k) % n_dp) * rows, 0))
        return lax.all_gather(part, "seq", axis=1, tiled=True)

    def place_rows(blocks):
        seq_at, dp_at = lax.axis_index("seq"), lax.axis_index("dp")
        mats, rows, units = blocks[0, 0].shape
        whole = jnp.zeros((mats, n_seq * n_dp * rows, units), blocks[0, 0].dtype)
        for (y, k), block in blocks.items():
            at = ((seq_at ^ y) * n_dp + (dp_at - k) % n_dp) * rows
            whole = lax.dynamic_update_slice(whole, block, (0, at, 0))
        return whole

    def per_device(
        tile_feats,
        tile_gain,
        w_gate,
        w_up,
        w_down,
        w_proj,
        slide_gain,
        w_qkv,
        w_out,
        lengths,
        seg_len,
        rate,
    ):
        sec = lax.axis_index("section")
        seq_at = lax.axis_index("seq")
        dp_at = lax.axis_index("dp")
        core, side, odd = sec % 2, sec // 2, dp_at % 2
        mine = tile_feats[0]
        tokens, feats = mine.shape
        own_rows = tokens // n_sec
        half = w_gate.shape[1] // 2

        def absolute(blocks):
            stacked = jnp.stack(blocks)
            return [lax.dynamic_index_in_dim(stacked, sec ^ j, 0, False) for j in range(n_sec)]

        def halves(x, which):
            return lax.dynamic_slice_in_dim(x, which * half, half, x.ndim - 1)

        pair = jnp.stack([w_gate, w_up])
        pair_same, pair_other = halves(pair, odd), halves(pair, 1 - odd)
        down = w_down.T[None]
        down_same, down_other = halves(down, odd), halves(down, 1 - odd)
        ordered = n_seq == 2 and n_dp == 4

        beside = flip(mine, dp=1)
        both = jnp.concatenate([mine, beside], axis=0)
        rows = jnp.concatenate(absolute(gather_section(both)), axis=1)
        normed = layer_norm(rows.astype(jnp.float32), tile_gain).astype(jnp.bfloat16)

        if ordered:
            g = {(0, 0): pair_same, (0, 2): rotate(pair_same, 2)}
            g[0, 1] = rotate(after(pair_other, g[0, 2]), 1)
            g[0, 3] = rotate(after(pair_other, g[0, 2]), 3)
            for k in (0, 2, 1, 3):
                g[1, k] = flip(g[0, k], seq=1)
            gate_up = place_rows(g)
            d = {(0, 0): down_same, (0, 2): rotate(after(down_same, g[0, 1]), 2)}
            d[0, 1] = rotate(after(down_other, d[0, 2], normed), 1)
            d[0, 3] = rotate(after(down_other, d[0, 2], normed), 3)
            for k in (0, 2, 1, 3):
                d[1, k] = flip(d[0, k], seq=1)
        else:
            gate_up = gather_rows(pair_same, pair_other, seq_at, dp_at)
            down_all = gather_rows(down_same, down_other, seq_at, dp_at)[0]

        proj = lax.all_gather(w_proj, "section", axis=0, tiled=True)
        gate = jnp.dot(normed, gate_up[0], preferred_element_type=jnp.float32)
        up = jnp.dot(normed, gate_up[1], preferred_element_type=jnp.float32)
        hidden = (jax.nn.silu(gate) * up).astype(jnp.bfloat16)
        hidden = hidden.reshape(2, n_sec // 2, 2, own_rows, half)

        def fold(proj_rows, down_rows):
            return lax.dot_general(
                proj_rows, down_rows, (((0,), (0,)), ((), ())), preferred_element_type=jnp.float32
            )

        if ordered:
            late = [d.pop((1, 1)), d.pop((1, 3))]
            folded = fold(proj, place_rows(d)[0])
            for k, block in zip((1, 3), late):
                at = ((1 - seq_at) * n_dp + (dp_at - k) % n_dp) * block.shape[1]
                folded = folded + fold(
                    lax.dynamic_slice_in_dim(proj, at, block.shape[1], 0), block[0]
                )
        else:
            folded = fold(proj, down_all)
        folded = folded.astype(jnp.bfloat16)

        def project(x):
            return lax.dot_general(
                x, folded, (((x.ndim - 1,), (1,)), ((), ())), preferred_element_type=jnp.float32
            )

        send = project(lax.dynamic_index_in_dim(hidden, 1 - core, 2, False)).astype(jnp.bfloat16)
        got = flip(send, section=1)
        kept = project(lax.dynamic_index_in_dim(hidden, core, 2, False)) + got.astype(jnp.float32)
        here = lax.dynamic_index_in_dim(kept, side, 1, False)
        there = lax.dynamic_index_in_dim(kept, 1 - side, 1, False).astype(jnp.bfloat16)
        from_x = flip(there[0], section=2)
        from_z = flip(here[1].astype(jnp.bfloat16), dp=1)
        from_xz = flip(there[1], section=2, dp=1)
        residual = jnp.dot(
            lax.dynamic_slice_in_dim(rows[:tokens], sec * own_rows, own_rows, 0),
            proj,
            preferred_element_type=jnp.float32,
        )
        emb = (
            residual
            + here[0]
            + from_x.astype(jnp.float32)
            + from_z.astype(jnp.float32)
            + from_xz.astype(jnp.float32)
        )
        slide_normed = layer_norm(emb, slide_gain).astype(jnp.bfloat16)

        span = jnp.arange(own_rows, dtype=jnp.int32)
        if n_seq == 2:
            near = [
                flip(slide_normed, section=2),
                flip(slide_normed, seq=1),
                flip(slide_normed, section=2, seq=1),
            ]
            from_core = flip(jnp.stack([slide_normed] + near), section=1)
            masks = (0, 2, 1, 3)
            k_idx = jnp.concatenate(
                [(seq_at ^ y) * tokens + (sec ^ m) * own_rows + span for y in (0, 1) for m in masks]
            )
            q_idx = k_idx[:tokens]
        else:
            keys = lax.all_gather(slide_normed, ("seq", "section"), axis=0, tiled=True)
            k_idx = jnp.arange(keys.shape[0], dtype=jnp.int32)
            q_idx = seq_at * tokens + jnp.arange(tokens, dtype=jnp.int32)

        count = k_idx.shape[0]
        local_heads = seg_len.shape[0]
        heads = sec * local_heads + jnp.arange(local_heads, dtype=jnp.int32)

        def codes(index):
            slide, pos = slide_place(lengths[0], index)
            block = slide[None, :] * count + pos[None, :] // seg_len[:, None]
            return block, pos[None, :] % rate[:, None] == (heads % rate)[:, None]

        k_block, picked = codes(k_idx)
        k_code = jnp.where(picked, k_block, -1)
        q_code = codes(q_idx)[0].T

        width = w_qkv.shape[2]
        qkv = jnp.swapaxes(w_qkv, 1, 2)
        out_w = jnp.stack(absolute(list(jnp.split(w_out, n_sec, axis=1))))
        emb_cut = jnp.stack(absolute(list(jnp.split(emb, n_sec, axis=1))))
        if n_seq == 2:
            vmem = pl.BlockSpec(memory_space=pltpu.VMEM)
            keep, send = pl.pallas_call(
                lambda *refs: attend_kernel(*refs, heads=local_heads, masks=masks),
                out_shape=[
                    jax.ShapeDtypeStruct((2, tokens, width), jnp.float32),
                    jax.ShapeDtypeStruct((2, tokens, width), jnp.bfloat16),
                ],
                in_specs=[pl.BlockSpec(memory_space=pltpu.SMEM)] + [vmem] * 10,
                out_specs=[vmem] * 2,
                compiler_params=pltpu.CompilerParams(vmem_limit_bytes=40 * 2**20),
                cost_estimate=pl.CostEstimate(
                    flops=2 * count * width * (3 * 768 + 2 * local_heads * tokens),
                    bytes_accessed=8 * 2**20,
                    transcendentals=local_heads * tokens * count,
                ),
            )(sec[None], slide_normed, *near, from_core, qkv, out_w, emb_cut, q_code, k_code)
        else:

            def by_head(x, matrix):
                x = jnp.dot(x, matrix.T, preferred_element_type=jnp.float32)
                x = x.astype(jnp.bfloat16).reshape(x.shape[0], local_heads, width // local_heads)
                return x.transpose(1, 0, 2)

            def one_head(args):
                q, k, v, q_row, k_row = args
                scores = jnp.dot(q, k.T, preferred_element_type=jnp.float32)
                scores = scores / math.sqrt(width // local_heads)
                ok = (q_row[:, None] == k_row[None, :]) | (q_idx[:, None] == k_idx[None, :])
                weight = jax.nn.softmax(jnp.where(ok, scores, NEG), axis=-1)
                return jnp.dot(weight, v, preferred_element_type=jnp.float32)

            queries = lax.dynamic_slice_in_dim(keys, seq_at * tokens, tokens, 0)
            att = lax.map(
                one_head,
                (by_head(queries, qkv[0]), by_head(keys, qkv[1]), by_head(keys, qkv[2]))
                + (q_code.T, k_code),
            )
            att = att.transpose(1, 0, 2).reshape(tokens, width).astype(jnp.bfloat16)
            parts = jnp.einsum("re,mec->mrc", att, out_w, preferred_element_type=jnp.float32)
            old = lax.dynamic_slice_in_dim(parts, sec * own_rows, own_rows, 1)
            parts = lax.dynamic_update_slice_in_dim(parts, old + emb_cut, sec * own_rows, 1)
            keep, send = parts[0::2], parts[1::2].astype(jnp.bfloat16)

        kept = keep + flip(send, section=1).astype(jnp.float32)
        out = kept[0] + flip(kept[1].astype(jnp.bfloat16), section=2).astype(jnp.float32)
        return out.astype(jnp.bfloat16)[None]

    return per_device


def solution(mesh):
    placed = (
        P("dp", "seq", "section"),
        P(),
        P(("seq", "dp"), "section"),
        P(("seq", "dp"), "section"),
        P("section", ("seq", "dp")),
        P("section", None),
        P(),
        P(None, None, "section"),
        P("section", None),
        P("dp", None),
        P("section"),
        P("section"),
    )
    shape = mesh.shape
    return jax.shard_map(
        build(shape["section"], shape["seq"], shape["dp"]),
        mesh=mesh,
        in_specs=placed,
        out_specs=P("dp", "seq", "section"),
        check_vma=False,
    )
```

time: 180 us -> 163 us (0.906)
  waiting for transfers between devices: 85.6 us -> 59.9 us
  local copies, waits for them, and re-layouts: 13 us -> 20.1 us
  Pallas kernels: 11.7 us -> 5.45 us
  starting transfers between devices: 28.7 us -> 33.8 us
  matrix products: 13 us -> 15.8 us
    ppermute x6, waiting for transfers between devices: 20.8 us -> 6.36 us  [rotate(): return lax.ppermute(x, 'dp', [(i, (i + k) % n_dp) for i in range(n_dp)])]
    ppermute x23 -> x22, waiting for transfers between devices: 64.1 us -> 53.5 us  [flip(): return lax.ppermute(x, names if len(names) > 1 else names[0], pairs)]
    dynamic_update_slice x14 -> x13, local copies, waits for them, and re-layouts: 7.62 us -> 14.5 us  [place_rows(): whole = lax.dynamic_update_slice(whole, block, (0, at, 0))]
    pallas_call x1, Pallas kernels: 11.7 us -> 5.45 us  [per_device(): pl.pallas_call(lambda *refs: attend_kernel(*refs, heads=local_heads, mask...]
    ppermute x6, starting transfers between devices: 6.61 us -> 12.7 us  [rotate(): return lax.ppermute(x, 'dp', [(i, (i + k) % n_dp) for i in range(n_dp)])]
    dot_general x2 -> x3, matrix products: 3.67 us -> 6.5 us  [fold(): lax.dot_general(proj_rows, down_rows, (((0,), (0,)), ((), ())), preferred...]
    add x0 -> x4, other arithmetic: none -> 2.8 us  [the longest x1 2.68 us: codes(): block = slide[None, :] * count + pos[None, :] // seg_len[:, None]]
    another operation x3 -> x4, other arithmetic: 2.64 us -> 0.78 us  [absolute(): stacked = jnp.stack(blocks)]
  transfers between devices with their start and end apart: 31 -> 29, of which waited for: 15 -> 15; matrix products, arithmetic and copies ran while one was open for 21% -> 26% of each run, Pallas kernels for 0% -> 0%
where the time goes in v4:
time: 163 us
  waiting for transfers between devices  59.9 us (37%)
  starting transfers between devices  33.8 us (21%)
  local copies, waits for them, and re-layouts  20.1 us (12%)
  matrix products  15.8 us (10%)
  between operations  14.1 us (9%)
  other arithmetic  13.8 us (8%)
  Pallas kernels  5.45 us (3%)
    ppermute x22, waiting for transfers between devices, flip(): return lax.ppermute(x, names if len(names) > 1 else names[0], pairs)  53.5 us
    ppermute x22, starting transfers between devices, flip(): return lax.ppermute(x, names if len(names) > 1 else names[0], pairs)  21.1 us
    dynamic_update_slice x13, local copies, waits for them, and re-layouts, place_rows(): whole = lax.dynamic_update_slice(whole, block, (0, at, 0))  14.5 us
    ppermute x6, starting transfers between devices, rotate(): return lax.ppermute(x, 'dp', [(i, (i + k) % n_dp) for i in range(n_dp)])  12.7 us
    dot_general x3, matrix products, fold(): lax.dot_general(proj_rows, down_rows, (((0,), (0,)), ((), ())), preferred...  6.5 us
    ppermute x6, waiting for transfers between devices, rotate(): return lax.ppermute(x, 'dp', [(i, (i + k) % n_dp) for i in range(n_dp)])  6.36 us
    pallas_call x1, Pallas kernels, per_device(): pl.pallas_call(lambda *refs: attend_kernel(*refs, heads=local_heads, mask...  5.45 us
    dot_general x1, matrix products, per_device(): up = jnp.dot(normed, gate_up[1], preferred_element_type=jnp.float32)  4.51 us
  transfers between devices with their start and end apart: 29, of which 15 were waited for; matrix products, arithmetic and copies ran while one was open for 26% of the time, Pallas kernels for 0%

profile of v4, /device:TPU:0, one launch (start us, length us, event | category | flops | bytes accessed | tf_op | source)
XLA Modules:
  0.0 163.0 jit_solution(14569459532672643922)
XLA Ops:
  6.6 1.9 %broadcast_in_dim.31 = bf16[2,1536,512]{2,1,0:T(8,128)(2,1)} broadcast(bf16[]{:T(256)} %constant.189.clone.1), dimensions={} | broadcast | bytes 3145730 | tf_op jit(solution)/shard_map/broadcast_in_dim | solution.py:119
  8.5 1.1 constant_dynamic-update-slice_fusion.7
  9.6 4.0 %collective-permute-start.4 = (bf16[2,192,512]{2,1,0:T(8,128)(2,1)}, bf16[2,192,512]{2,1,0:T(8,128)(2,1)S(1)}, u32[]{:S(2)}, u32[]{:S(2)}) collective-permute-start(bf16[2,192,512]{2,1,0:T(8,128)(2,1)} %get-tuple-element.28), channel_id=1, source_target_pairs={{0,2},{1,3},{2,0},{3,1},{4,6},{5,7},{6,4},{7,5},{8,10},{9,11},{10,... | collective-permute-start | bytes 1179656 | tf_op jit(solution)/shard_map/ppermute | solution.py:99
  13.6 1.5 collective-permute-start.7
  15.2 1.6 collective-permute-start
  18.1 14.6 %collective-permute-done = bf16[512,384]{1,0:T(8,128)(2,1)S(1)} collective-permute-done((bf16[512,384]{1,0:T(8,128)(2,1)S(1)}, bf16[512,384]{1,0:T(8,128)(2,1)S(1)}, u32[]{:S(2)}, u32[]{:S(2)}) %collective-permute-start) | collective-permute-done | bytes 393248 | tf_op jit(solution)/shard_map/ppermute | solution.py:96
  32.9 1.6 collective-permute-start.1
  34.5 1.4 compare_select_fusion.2
  36.2 1.2 broadcast_compare_fusion
  37.5 3.4 %collective-permute-start.6 = (bf16[2,192,512]{2,1,0:T(8,128)(2,1)}, bf16[2,192,512]{2,1,0:T(8,128)(2,1)}, u32[]{:S(2)}, u32[]{:S(2)}) collective-permute-start(bf16[2,192,512]{2,1,0:T(8,128)(2,1)} %get-tuple-element.12), channel_id=1, source_target_pairs={{0,3},{1,0},{2,1},{3,2},{4,7},{5,4},{6,5},{7,6},{8,11},{9,8},{10,9... | collective-permute-start | bytes 1179656 | tf_op jit(solution)/shard_map/ppermute | solution.py:99
  41.7 1.2 squeeze.87
  43.6 1.2 sign.33
  46.1 4.0 %collective-permute-done.5 = bf16[2,192,512]{2,1,0:T(8,128)(2,1)} collective-permute-done((bf16[2,192,512]{2,1,0:T(8,128)(2,1)}, bf16[2,192,512]{2,1,0:T(8,128)(2,1)}, u32[]{:S(2)}, u32[]{:S(2)}) %collective-permute-start.5) | collective-permute-done | bytes 393248 | tf_op jit(solution)/shard_map/ppermute | solution.py:99
  50.1 1.8 %constant_dynamic-update-slice_fusion.5 = bf16[2,1536,512]{2,1,0:T(8,128)(2,1)} fusion(bf16[2,1536,512]{2,1,0:T(8,128)(2,1)} %constant_dynamic-update-slice_fusion.6, bf16[2,192,512]{2,1,0:T(8,128)(2,1)} %collective-permute-done.5, s32[]{:T(128)S(6)} %select_n.192), kind=kLoop, calls=%fused_computation.121 | loop fusion | bytes 786436 | tf_op jit(solution)/shard_map/dynamic_update_slice | solution.py:122
  51.9 1.7 %collective-permute-done.1 = bf16[1024,384]{1,0:T(8,128)(2,1)S(1)} collective-permute-done((bf16[1024,384]{1,0:T(8,128)(2,1)S(1)}, bf16[1024,384]{1,0:T(8,128)(2,1)S(1)}, u32[]{:S(2)}, u32[]{:S(2)}) %collective-permute-start.1) | collective-permute-done | bytes 786464 | tf_op jit(solution)/shard_map/ppermute | solution.py:96
  54.5 1.8 %constant_dynamic-update-slice_fusion.4 = bf16[2,1536,512]{2,1,0:T(8,128)(2,1)} fusion(bf16[2,1536,512]{2,1,0:T(8,128)(2,1)} %constant_dynamic-update-slice_fusion.5, bf16[2,192,512]{2,1,0:T(8,128)(2,1)} %collective-permute-done.6, s32[]{:T(128)S(6)} %select_n.194), kind=kLoop, calls=%fused_computation.120 | loop fusion | bytes 786436 | tf_op jit(solution)/shard_map/dynamic_update_slice | solution.py:122
  56.2 1.6 collective-permute-start.9
  57.8 1.8 %constant_dynamic-update-slice_fusion.3 = bf16[2,1536,512]{2,1,0:T(8,128)(2,1)} fusion(bf16[2,1536,512]{2,1,0:T(8,128)(2,1)} %constant_dynamic-update-slice_fusion.4, bf16[2,192,512]{2,1,0:T(8,128)(2,1)} %collective-permute-done.7, s32[]{:T(128)S(6)} %select_n.195), kind=kLoop, calls=%fused_computation.119 | loop fusion | bytes 786436 | tf_op jit(solution)/shard_map/dynamic_update_slice | solution.py:122
  60.8 1.5 collective-permute-done.11
  62.3 1.5 collective-permute-start.14
  64.6 3.8 %collective-permute-done.9 = bf16[2,192,512]{2,1,0:T(8,128)(2,1)S(1)} collective-permute-done((bf16[2,192,512]{2,1,0:T(8,128)(2,1)}, bf16[2,192,512]{2,1,0:T(8,128)(2,1)S(1)}, u32[]{:S(2)}, u32[]{:S(2)}) %collective-permute-start.9) | collective-permute-done | bytes 393248 | tf_op jit(solution)/shard_map/ppermute | solution.py:96
  68.4 1.6 collective-permute-start.15
  70.7 6.1 %collective-permute-done.10 = bf16[2,192,512]{2,1,0:T(8,128)(2,1)S(1)} collective-permute-done((bf16[2,192,512]{2,1,0:T(8,128)(2,1)}, bf16[2,192,512]{2,1,0:T(8,128)(2,1)S(1)}, u32[]{:S(2)}, u32[]{:S(2)}) %collective-permute-start.10) | collective-permute-done | bytes 393248 | tf_op jit(solution)/shard_map/ppermute | solution.py:96
  79.2 1.0 fusion.2
  80.2 1.0 fusion.4
  81.2 4.8 %collective-permute-start.12 = (bf16[1,192,512]{2,1,0:T(8,128)(2,1)S(1)}, bf16[1,192,512]{2,1,0:T(8,128)(2,1)}, u32[]{:S(2)}, u32[]{:S(2)}) collective-permute-start(bf16[1,192,512]{2,1,0:T(8,128)(2,1)S(1)} %copy-done.9), channel_id=1, source_target_pairs={{0,1},{1,2},{2,3},{3,0},{4,5},{5,6},{6,7},{7,4},{8,9},{9,10},{10,1... | collective-permute-start | bytes 589832 | tf_op jit(solution)/shard_map/ppermute | solution.py:99
  86.0 3.2 %fusion.6 = f32[1024,512]{1,0:T(8,128)S(1)} fusion(bf16[1024,1536]{1,0:T(8,128)(2,1)S(1)} %fusion.4, bf16[2,1536,512]{2,1,0:T(8,128)(2,1)} %constant_dynamic-update-slice_fusion), kind=kOutput, calls=%fused_computation.13 | convolution fusion | flops 1610612736 | bytes 6815744 | tf_op jit(solution)/shard_map/dot_general | solution.py:183
  89.2 4.5 %multiply_convert_fusion = bf16[1024,512]{1,0:T(8,128)(2,1)} fusion(f32[1024,512]{1,0:T(8,128)S(1)} %fusion.6, bf16[1024,1536]{1,0:T(8,128)(2,1)S(1)} %fusion.4, bf16[2,1536,512]{2,1,0:T(8,128)(2,1)} %constant_dynamic-update-slice_fusion), kind=kOutput, calls=%fused_computation.9 | convolution fusion | flops 1613758464 | bytes 7864320 | tf_op jit(solution)/shard_map/dot_general | solution.py:184
  93.7 1.3 collective-permute-start.16
  95.9 1.6 bitcast_dynamic-update-slice_fusion.3
  97.5 1.6 bitcast_dynamic-update-slice_fusion.2
  100.5 3.7 %fusion.63 = f32[512,768]{1,0:T(8,128)S(1)} fusion(bf16[1536,512]{1,0:T(8,128)(2,1)} %bitcast_dynamic-update-slice_fusion, bf16[1536,768]{1,0:T(8,128)(2,1)} %all-gather.2.cloned.1.call-done), kind=kOutput, calls=%fused_computation.156 | convolution fusion | flops 1207959552 | bytes 5505024 | tf_op jit(solution)/shard_map/dot_general | solution.py:189
  104.2 1.4 fusion.31
  105.7 1.4 fusion.9
  108.7 2.7 %fusion.33.refs_9_ = s32[512,4]{1,0:T(8,128)S(1)} fusion(s32[4]{0:T(128)S(1)} %copy-done.14, s32[512]{0:T(512)S(1)} %copy-done.13, s32[4]{0:T(128)S(1)} %copy-done.15, s32[512]{0:T(512)S(1)} %broadcast_multiply_fusion.2, s32[512]{0:T(512)S(1)} %copy-done.12), kind=kLoop, calls=%fused_computation.62 | loop fusion | flops 16384 | bytes 14368 | tf_op jit(solution)/shard_map/add | solution.py:256
  112.8 2.9 %collective-permute-start.21 = (bf16[128,768]{1,0:T(8,128)(2,1)S(1)}, bf16[128,768]{1,0:T(8,128)(2,1)S(1)}, u32[]{:S(2)}, u32[]{:S(2)}) collective-permute-start(bf16[128,768]{1,0:T(8,128)(2,1)S(1)} %get-tuple-element.51), channel_id=1, source_target_pairs={{0,17},{1,16},{2,19},{3,18},{8,25},{9,24},{10,27},{11,26},{16,1},{... | collective-permute-start | bytes 589832 | tf_op jit(solution)/shard_map/ppermute | solution.py:96
  116.3 7.4 %collective-permute-done.19 = bf16[128,768]{1,0:T(8,128)(2,1)S(1)} collective-permute-done((bf16[128,768]{1,0:T(8,128)(2,1)S(1)}, bf16[128,768]{1,0:T(8,128)(2,1)S(1)}, u32[]{:S(2)}, u32[]{:S(2)}) %collective-permute-start.19) | collective-permute-done | bytes 196640 | tf_op jit(solution)/shard_map/ppermute | solution.py:96
  123.8 1.2 collective-permute-done.20
  125.5 0.8 collective-permute-start.22
  126.4 1.0 collective-permute-start.23
  127.4 1.7 %collective-permute-start.24 = (bf16[128,768]{1,0:T(8,128)(2,1)S(1)}, bf16[128,768]{1,0:T(8,128)(2,1)S(1)}, u32[]{:S(2)}, u32[]{:S(2)}) collective-permute-start(bf16[128,768]{1,0:T(8,128)(2,1)S(1)} %multiply_convert_fusion.1.refs_1_), channel_id=1, source_target_pairs={{0,20},{4,16},{8,28},{12,24},{16,4},{20,0},{24,12},{28,8},{1,21},{... | collective-permute-start | bytes 589832 | tf_op jit(solution)/shard_map/ppermute | solution.py:96
  129.2 4.2 %collective-permute-done.22.refs_2_ = bf16[128,768]{1,0:T(8,128)(2,1)S(1)} collective-permute-done((bf16[128,768]{1,0:T(8,128)(2,1)S(1)}, bf16[128,768]{1,0:T(8,128)(2,1)S(1)}, u32[]{:S(2)}, u32[]{:S(2)}) %collective-permute-start.22) | collective-permute-done | bytes 196640 | tf_op jit(solution)/shard_map/ppermute | solution.py:96
  134.2 2.6 %collective-permute-done.24.refs_4_ = bf16[128,768]{1,0:T(8,128)(2,1)S(1)} collective-permute-done((bf16[128,768]{1,0:T(8,128)(2,1)S(1)}, bf16[128,768]{1,0:T(8,128)(2,1)S(1)}, u32[]{:S(2)}, u32[]{:S(2)}) %collective-permute-start.24) | collective-permute-done | bytes 196640 | tf_op jit(solution)/shard_map/ppermute | solution.py:96
  137.4 1.8 %collective-permute-done.25.refs_5_ = bf16[4,128,768]{2,1,0:T(8,128)(2,1)S(1)} collective-permute-done((bf16[4,128,768]{2,1,0:T(8,128)(2,1)S(1)}, bf16[4,128,768]{2,1,0:T(8,128)(2,1)S(1)}, u32[]{:S(2)}, u32[]{:S(2)}) %collective-permute-start.25) | collective-permute-done | bytes 786464 | tf_op jit(solution)/shard_map/ppermute | solution.py:96
  139.3 5.5 %shard_map.118 = (f32[2,512,192]{2,1,0:T(8,128)S(1)}, bf16[2,512,192]{2,1,0:T(8,128)(2,1)S(1)}) custom-call(s32[1]{0:T(128)} %bitcast.refs_0_, bf16[128,768]{1,0:T(8,128)(2,1)S(1)} %multiply_convert_fusion.1.refs_1_, bf16[128,768]{1,0:T(8,128)(2,1)S(1)} %collective-permute-done.22.refs_2_, bf16[128,768]{1,0:T(8,128)(2,1)S(1)} %collective-permute-done.23.refs_3_, ...), custom_call_target="tpu_custom_call" | custom-call | flops 2516582400 | bytes 8388608 | tf_op jit(solution)/shard_map/pallas_call | solution.py:269
  144.9 1.8 %collective-permute-done.26 = bf16[2,512,192]{2,1,0:T(8,128)(2,1)S(1)} collective-permute-done((bf16[2,512,192]{2,1,0:T(8,128)(2,1)S(1)}, bf16[2,512,192]{2,1,0:T(8,128)(2,1)S(1)}, u32[]{:S(2)}, u32[]{:S(2)}) %collective-permute-start.26) | collective-permute-done | bytes 393248 | tf_op jit(solution)/shard_map/ppermute | solution.py:96
  146.8 1.0 collective-permute-start.27
  147.9 7.4 %collective-permute-done.27 = bf16[512,192]{1,0:T(8,128)(2,1)S(1)} collective-permute-done((bf16[512,192]{1,0:T(8,128)(2,1)S(1)}, bf16[512,192]{1,0:T(8,128)(2,1)S(1)}, u32[]{:S(2)}, u32[]{:S(2)}) %collective-permute-start.27) | collective-permute-done | bytes 196640 | tf_op jit(solution)/shard_map/ppermute | solution.py:96
  (132 shorter events, 19.3 us)
Async XLA Ops:
  6.5 2.0 %copy-start.6 = (bf16[192,1024]{1,0:T(8,128)(2,1)S(1)}, bf16[192,1024]{1,0:T(8,128)(2,1)}, u32[]{:S(2)}) copy-start(bf16[192,1024]{1,0:T(8,128)(2,1)} %param.14) | copy-start | bytes 1179652
  6.5 2.0 %copy-start.5 = (bf16[192,1024]{1,0:T(8,128)(2,1)S(1)}, bf16[192,1024]{1,0:T(8,128)(2,1)}, u32[]{:S(2)}) copy-start(bf16[192,1024]{1,0:T(8,128)(2,1)} %param.15) | copy-start | bytes 1179652
  6.5 8.7 %copy-start.4 = (bf16[1,512,384]{2,1,0:T(8,128)(2,1)S(1)}, bf16[1,512,384]{2,1,0:T(8,128)(2,1)}, u32[]{:S(2)}) copy-start(bf16[1,512,384]{2,1,0:T(8,128)(2,1)} %param.12) | copy-start | bytes 1179652
  6.5 10.3 %copy-start.3 = (bf16[192,768]{1,0:T(8,128)(2,1)S(1)}, bf16[192,768]{1,0:T(8,128)(2,1)}, u32[]{:S(2)}) copy-start(bf16[192,768]{1,0:T(8,128)(2,1)} %param.20) | copy-start | bytes 884740
  6.5 93.9 %all-gather.2.cloned.1.call-start = ((), (), s32[]{:S(2)}) async-start(), calls=%async_computation | async-start | bytes 2949120 | tf_op jit(solution)/shard_map/all_gather | solution.py:182
  6.6 10.5 %copy-start.18 = (s32[1,3]{1,0:T(1,128)S(1)}, s32[1,3]{1,0:T(1,128)}, u32[]{:S(2)}) copy-start(s32[1,3]{1,0:T(1,128)} %param.21) | copy-start | bytes 40
  8.5 32.4 %copy-start.2 = (bf16[1024,192]{0,1:T(8,128)(2,1)S(1)}, bf16[1024,192]{0,1:T(8,128)(2,1)}, u32[]{:S(2)}) copy-start(bf16[1024,192]{0,1:T(8,128)(2,1)} %param.16) | copy-start | bytes 1179652
  9.6 26.2 %collective-permute-start.4 = (bf16[2,192,512]{2,1,0:T(8,128)(2,1)}, bf16[2,192,512]{2,1,0:T(8,128)(2,1)S(1)}, u32[]{:S(2)}, u32[]{:S(2)}) collective-permute-start(bf16[2,192,512]{2,1,0:T(8,128)(2,1)} %get-tuple-element.28), channel_id=1, source_target_pairs={{0,2},{1,3},{2,0},{3,1},{4,6},{5,7},{6,4},{7,5},{8,10},{9,11},{10,... | collective-permute-start | bytes 1179656 | tf_op jit(solution)/shard_map/ppermute | solution.py:99
  13.6 42.6 %collective-permute-start.7 = (bf16[2,192,512]{2,1,0:T(8,128)(2,1)}, bf16[2,192,512]{2,1,0:T(8,128)(2,1)}, u32[]{:S(2)}, u32[]{:S(2)}) collective-permute-start(bf16[2,192,512]{2,1,0:T(8,128)(2,1)} %get-tuple-element.28), channel_id=1, source_target_pairs={{0,4},{4,0},{1,5},{5,1},{2,6},{6,2},{3,7},{7,3},{8,12},{12,8},{9,1... | collective-permute-start | bytes 1179656 | tf_op jit(solution)/shard_map/ppermute | solution.py:96
  15.2 17.5 %collective-permute-start = (bf16[512,384]{1,0:T(8,128)(2,1)S(1)}, bf16[512,384]{1,0:T(8,128)(2,1)S(1)}, u32[]{:S(2)}, u32[]{:S(2)}) collective-permute-start(bf16[512,384]{1,0:T(8,128)(2,1)S(1)} %bitcast.138), channel_id=1, source_target_pairs={{0,1},{1,0},{2,3},{3,2},{4,5},{5,4},{6,7},{7,6},{8,9},{9,8},{10,11... | collective-permute-start | bytes 1179656 | tf_op jit(solution)/shard_map/ppermute | solution.py:96
  32.9 20.7 %collective-permute-start.1 = (bf16[1024,384]{1,0:T(8,128)(2,1)S(1)}, bf16[1024,384]{1,0:T(8,128)(2,1)S(1)}, u32[]{:S(2)}, u32[]{:S(2)}) collective-permute-start(bf16[1024,384]{1,0:T(8,128)(2,1)S(1)} %get-tuple-element.11), channel_id=1, source_target_pairs={{0,16},{8,24},{16,0},{24,8},{1,17},{9,25},{17,1},{25,9},{2,18},{10... | collective-permute-start | bytes 2359304 | tf_op jit(solution)/shard_map/ppermute | solution.py:96
  35.8 14.2 %collective-permute-start.5 = (bf16[2,192,512]{2,1,0:T(8,128)(2,1)}, bf16[2,192,512]{2,1,0:T(8,128)(2,1)}, u32[]{:S(2)}, u32[]{:S(2)}) collective-permute-start(bf16[2,192,512]{2,1,0:T(8,128)(2,1)} %get-tuple-element.12), channel_id=1, source_target_pairs={{0,1},{1,2},{2,3},{3,0},{4,5},{5,6},{6,7},{7,4},{8,9},{9,10},{10,1... | collective-permute-start | bytes 1179656 | tf_op jit(solution)/shard_map/ppermute | solution.py:99
  37.5 17.0 %collective-permute-start.6 = (bf16[2,192,512]{2,1,0:T(8,128)(2,1)}, bf16[2,192,512]{2,1,0:T(8,128)(2,1)}, u32[]{:S(2)}, u32[]{:S(2)}) collective-permute-start(bf16[2,192,512]{2,1,0:T(8,128)(2,1)} %get-tuple-element.12), channel_id=1, source_target_pairs={{0,3},{1,0},{2,1},{3,2},{4,7},{5,4},{6,5},{7,6},{8,11},{9,8},{10,9... | collective-permute-start | bytes 1179656 | tf_op jit(solution)/shard_map/ppermute | solution.py:99
  44.8 17.5 %copy-start.8 = (bf16[1,192,512]{2,1,0:T(8,128)(2,1)S(1)}, bf16[1,192,512]{2,1,0:T(8,128)(2,1)}, u32[]{:S(2)}) copy-start(bf16[1,192,512]{2,1,0:T(8,128)(2,1)} %get-tuple-element.13) | copy-start | bytes 589828
  44.8 14.8 %collective-permute-start.8 = (bf16[2,192,512]{2,1,0:T(8,128)(2,1)S(1)}, bf16[2,192,512]{2,1,0:T(8,128)(2,1)S(1)}, u32[]{:S(2)}, u32[]{:S(2)}) collective-permute-start(bf16[2,192,512]{2,1,0:T(8,128)(2,1)S(1)} %collective-permute-done.4), channel_id=1, source_target_pairs={{0,4},{4,0},{1,5},{5,1},{2,6},{6,2},{3,7},{7,3},{8,12},{12,8},{9,1... | collective-permute-start | bytes 1179656 | tf_op jit(solution)/shard_map/ppermute | solution.py:96
  50.1 12.3 %collective-permute-start.11 = (bf16[1,192,512]{2,1,0:T(8,128)(2,1)}, bf16[1,192,512]{2,1,0:T(8,128)(2,1)S(1)}, u32[]{:S(2)}, u32[]{:S(2)}) collective-permute-start(bf16[1,192,512]{2,1,0:T(8,128)(2,1)} %get-tuple-element.13), channel_id=1, source_target_pairs={{0,2},{1,3},{2,0},{3,1},{4,6},{5,7},{6,4},{7,5},{8,10},{9,11},{10,... | collective-permute-start | bytes 589832 | tf_op jit(solution)/shard_map/ppermute | solution.py:99
  53.6 24.0 %collective-permute-start.2 = (bf16[1024,384]{1,0:T(8,128)(2,1)S(1)}, bf16[1024,384]{1,0:T(8,128)(2,1)S(1)}, u32[]{:S(2)}, u32[]{:S(2)}) collective-permute-start(bf16[1024,384]{1,0:T(8,128)(2,1)S(1)} %get-tuple-element.11), channel_id=1, source_target_pairs={{0,8},{8,0},{16,24},{24,16},{1,9},{9,1},{17,25},{25,17},{2,10},{10... | collective-permute-start | bytes 2359304 | tf_op jit(solution)/shard_map/ppermute | solution.py:96
  54.5 23.1 %collective-permute-start.3 = (bf16[1024,384]{1,0:T(8,128)(2,1)S(1)}, bf16[1024,384]{1,0:T(8,128)(2,1)S(1)}, u32[]{:S(2)}, u32[]{:S(2)}) collective-permute-start(bf16[1024,384]{1,0:T(8,128)(2,1)S(1)} %collective-permute-done.1), channel_id=1, source_target_pairs={{0,8},{8,0},{16,24},{24,16},{1,9},{9,1},{17,25},{25,17},{2,10},{10... | collective-permute-start | bytes 2359304 | tf_op jit(solution)/shard_map/ppermute | solution.py:96
  56.2 12.1 %collective-permute-start.9 = (bf16[2,192,512]{2,1,0:T(8,128)(2,1)}, bf16[2,192,512]{2,1,0:T(8,128)(2,1)S(1)}, u32[]{:S(2)}, u32[]{:S(2)}) collective-permute-start(bf16[2,192,512]{2,1,0:T(8,128)(2,1)} %collective-permute-done.5), channel_id=1, source_target_pairs={{0,4},{4,0},{1,5},{5,1},{2,6},{6,2},{3,7},{7,3},{8,12},{12,8},{9,1... | collective-permute-start | bytes 1179656 | tf_op jit(solution)/shard_map/ppermute | solution.py:96
  59.6 17.2 %collective-permute-start.10 = (bf16[2,192,512]{2,1,0:T(8,128)(2,1)}, bf16[2,192,512]{2,1,0:T(8,128)(2,1)S(1)}, u32[]{:S(2)}, u32[]{:S(2)}) collective-permute-start(bf16[2,192,512]{2,1,0:T(8,128)(2,1)} %collective-permute-done.6), channel_id=1, source_target_pairs={{0,4},{4,0},{1,5},{5,1},{2,6},{6,2},{3,7},{7,3},{8,12},{12,8},{9,1... | collective-permute-start | bytes 1179656 | tf_op jit(solution)/shard_map/ppermute | solution.py:96
  62.3 36.8 %collective-permute-start.14 = (bf16[1,192,512]{2,1,0:T(8,128)(2,1)S(1)}, bf16[1,192,512]{2,1,0:T(8,128)(2,1)S(1)}, u32[]{:S(2)}, u32[]{:S(2)}) collective-permute-start(bf16[1,192,512]{2,1,0:T(8,128)(2,1)S(1)} %copy-done.8), channel_id=1, source_target_pairs={{0,4},{4,0},{1,5},{5,1},{2,6},{6,2},{3,7},{7,3},{8,12},{12,8},{9,1... | collective-permute-start | bytes 589832 | tf_op jit(solution)/shard_map/ppermute | solution.py:96
  68.4 31.4 %collective-permute-start.15 = (bf16[1,192,512]{2,1,0:T(8,128)(2,1)S(1)}, bf16[1,192,512]{2,1,0:T(8,128)(2,1)S(1)}, u32[]{:S(2)}, u32[]{:S(2)}) collective-permute-start(bf16[1,192,512]{2,1,0:T(8,128)(2,1)S(1)} %collective-permute-done.11), channel_id=1, source_target_pairs={{0,4},{4,0},{1,5},{5,1},{2,6},{6,2},{3,7},{7,3},{8,12},{12,8},{9,1... | collective-permute-start | bytes 589832 | tf_op jit(solution)/shard_map/ppermute | solution.py:96
  80.2 1.0 copy-start.9
  81.2 12.5 %collective-permute-start.12 = (bf16[1,192,512]{2,1,0:T(8,128)(2,1)S(1)}, bf16[1,192,512]{2,1,0:T(8,128)(2,1)}, u32[]{:S(2)}, u32[]{:S(2)}) collective-permute-start(bf16[1,192,512]{2,1,0:T(8,128)(2,1)S(1)} %copy-done.9), channel_id=1, source_target_pairs={{0,1},{1,2},{2,3},{3,0},{4,5},{5,6},{6,7},{7,4},{8,9},{9,10},{10,1... | collective-permute-start | bytes 589832 | tf_op jit(solution)/shard_map/ppermute | solution.py:99
  86.0 9.1 %collective-permute-start.13 = (bf16[1,192,512]{2,1,0:T(8,128)(2,1)S(1)}, bf16[1,192,512]{2,1,0:T(8,128)(2,1)}, u32[]{:S(2)}, u32[]{:S(2)}) collective-permute-start(bf16[1,192,512]{2,1,0:T(8,128)(2,1)S(1)} %copy-done.9), channel_id=1, source_target_pairs={{0,3},{1,0},{2,1},{3,2},{4,7},{5,4},{6,5},{7,6},{8,11},{9,8},{10,9... | collective-permute-start | bytes 589832 | tf_op jit(solution)/shard_map/ppermute | solution.py:99
  93.7 10.5 %collective-permute-start.16 = (bf16[1,192,512]{2,1,0:T(8,128)(2,1)}, bf16[1,192,512]{2,1,0:T(8,128)(2,1)}, u32[]{:S(2)}, u32[]{:S(2)}) collective-permute-start(bf16[1,192,512]{2,1,0:T(8,128)(2,1)} %collective-permute-done.12), channel_id=1, source_target_pairs={{0,4},{4,0},{1,5},{5,1},{2,6},{6,2},{3,7},{7,3},{8,12},{12,8},{9,1... | collective-permute-start | bytes 589832 | tf_op jit(solution)/shard_map/ppermute | solution.py:96
  95.1 10.6 %collective-permute-start.17 = (bf16[1,192,512]{2,1,0:T(8,128)(2,1)}, bf16[1,192,512]{2,1,0:T(8,128)(2,1)}, u32[]{:S(2)}, u32[]{:S(2)}) collective-permute-start(bf16[1,192,512]{2,1,0:T(8,128)(2,1)} %collective-permute-done.13), channel_id=1, source_target_pairs={{0,4},{4,0},{1,5},{5,1},{2,6},{6,2},{3,7},{7,3},{8,12},{12,8},{9,1... | collective-permute-start | bytes 589832 | tf_op jit(solution)/shard_map/ppermute | solution.py:96
  100.5 3.8 %copy-start.1 = (bf16[1536,768]{1,0:T(8,128)(2,1)S(1)}, bf16[1536,768]{1,0:T(8,128)(2,1)}, u32[]{:S(2)}) copy-start(bf16[1536,768]{1,0:T(8,128)(2,1)} %all-gather.2.cloned.1.call-done) | copy-start | bytes 7077892
  104.2 2.9 %copy-start.7 = (bf16[1024,512]{1,0:T(8,128)(2,1)S(1)}, bf16[1024,512]{1,0:T(8,128)(2,1)}, u32[]{:S(2)}) copy-start(bf16[1024,512]{1,0:T(8,128)(2,1)} %multiply_convert_fusion) | copy-start | bytes 3145732
  105.7 2.2 %copy-start.14 = (s32[4]{0:T(128)S(1)}, s32[4]{0:T(128)}, u32[]{:S(2)}) copy-start(s32[4]{0:T(128)} %param.22) | copy-start | bytes 52
  105.7 2.2 %copy-start.15 = (s32[4]{0:T(128)S(1)}, s32[4]{0:T(128)}, u32[]{:S(2)}) copy-start(s32[4]{0:T(128)} %sign.33) | copy-start | bytes 52
  105.7 2.2 %copy-start.16 = (s32[4]{0:T(128)S(1)}, s32[4]{0:T(128)}, u32[]{:S(2)}) copy-start(s32[4]{0:T(128)} %get-tuple-element.58) | copy-start | bytes 52
  105.7 2.2 %copy-start.17 = (s32[4]{0:T(128)S(1)}, s32[4]{0:T(128)}, u32[]{:S(2)}) copy-start(s32[4]{0:T(128)} %get-tuple-element.59) | copy-start | bytes 52
  105.7 2.2 %copy-start.19 = (pred[4]{0:T(512)(128)(4,1)S(1)}, pred[4]{0:T(512)(128)(4,1)}, u32[]{:S(2)}) copy-start(pred[4]{0:T(512)(128)(4,1)} %broadcast_compare_fusion) | copy-start | bytes 16
  105.7 3.0 %copy-start.12 = (s32[512]{0:T(512)S(1)}, s32[512]{0:T(512)}, u32[]{:S(2)}) copy-start(s32[512]{0:T(512)} %get-tuple-element.23) | copy-start | bytes 6148
  105.7 3.0 %copy-start.13 = (s32[512]{0:T(512)S(1)}, s32[512]{0:T(512)}, u32[]{:S(2)}) copy-start(s32[512]{0:T(512)} %get-tuple-element.24) | copy-start | bytes 6148
  107.7 3.8 %collective-permute-start.18 = (bf16[2,2,128,768]{3,2,1,0:T(8,128)(2,1)S(1)}, bf16[2,2,128,768]{3,2,1,0:T(8,128)(2,1)S(1)}, u32[]{:S(2)}, u32[]{:S(2)}) collective-permute-start(bf16[2,2,128,768]{3,2,1,0:T(8,128)(2,1)S(1)} %convolution_convert_fusion), channel_id=1, source_target_pairs={{0,8},{8,0},{16,24},{24,16},{1,9},{9,1},{17,25},{25,17},{2,10},{10... | collective-permute-start | bytes 2359304 | tf_op jit(solution)/shard_map/ppermute | solution.py:96
  112.1 13.3 %copy-start.10 = (f32[768]{0:T(1024)S(1)}, f32[768]{0:T(1024)}, u32[]{:S(2)}) copy-start(f32[768]{0:T(1024)} %param.18) | copy-start | bytes 9220
  112.2 11.6 %collective-permute-start.19 = (bf16[128,768]{1,0:T(8,128)(2,1)S(1)}, bf16[128,768]{1,0:T(8,128)(2,1)S(1)}, u32[]{:S(2)}, u32[]{:S(2)}) collective-permute-start(bf16[128,768]{1,0:T(8,128)(2,1)S(1)} %get-tuple-element.50), channel_id=1, source_target_pairs={{0,16},{8,24},{16,0},{24,8},{1,17},{9,25},{17,1},{25,9},{2,18},{10... | collective-permute-start | bytes 589832 | tf_op jit(solution)/shard_map/ppermute | solution.py:96
  112.8 11.0 %collective-permute-start.21 = (bf16[128,768]{1,0:T(8,128)(2,1)S(1)}, bf16[128,768]{1,0:T(8,128)(2,1)S(1)}, u32[]{:S(2)}, u32[]{:S(2)}) collective-permute-start(bf16[128,768]{1,0:T(8,128)(2,1)S(1)} %get-tuple-element.51), channel_id=1, source_target_pairs={{0,17},{1,16},{2,19},{3,18},{8,25},{9,24},{10,27},{11,26},{16,1},{... | collective-permute-start | bytes 589832 | tf_op jit(solution)/shard_map/ppermute | solution.py:96
  115.7 9.3 %collective-permute-start.20 = (bf16[128,768]{1,0:T(8,128)(2,1)S(1)}, bf16[128,768]{1,0:T(8,128)(2,1)S(1)}, u32[]{:S(2)}, u32[]{:S(2)}) collective-permute-start(bf16[128,768]{1,0:T(8,128)(2,1)S(1)} %fusion.37), channel_id=1, source_target_pairs={{0,1},{1,0},{2,3},{3,2},{4,5},{5,4},{6,7},{7,6},{8,9},{9,8},{10,11... | collective-permute-start | bytes 589832 | tf_op jit(solution)/shard_map/ppermute | solution.py:96
  125.5 7.9 %collective-permute-start.22 = (bf16[128,768]{1,0:T(8,128)(2,1)S(1)}, bf16[128,768]{1,0:T(8,128)(2,1)S(1)}, u32[]{:S(2)}, u32[]{:S(2)}) collective-permute-start(bf16[128,768]{1,0:T(8,128)(2,1)S(1)} %multiply_convert_fusion.1.refs_1_), channel_id=1, source_target_pairs={{0,16},{8,24},{16,0},{24,8},{1,17},{9,25},{17,1},{25,9},{2,18},{10... | collective-permute-start | bytes 589832 | tf_op jit(solution)/shard_map/ppermute | solution.py:96
  126.4 7.8 %collective-permute-start.23 = (bf16[128,768]{1,0:T(8,128)(2,1)S(1)}, bf16[128,768]{1,0:T(8,128)(2,1)S(1)}, u32[]{:S(2)}, u32[]{:S(2)}) collective-permute-start(bf16[128,768]{1,0:T(8,128)(2,1)S(1)} %multiply_convert_fusion.1.refs_1_), channel_id=1, source_target_pairs={{0,4},{4,0},{1,5},{5,1},{2,6},{6,2},{3,7},{7,3},{8,12},{12,8},{9,1... | collective-permute-start | bytes 589832 | tf_op jit(solution)/shard_map/ppermute | solution.py:96
  127.4 9.4 %collective-permute-start.24 = (bf16[128,768]{1,0:T(8,128)(2,1)S(1)}, bf16[128,768]{1,0:T(8,128)(2,1)S(1)}, u32[]{:S(2)}, u32[]{:S(2)}) collective-permute-start(bf16[128,768]{1,0:T(8,128)(2,1)S(1)} %multiply_convert_fusion.1.refs_1_), channel_id=1, source_target_pairs={{0,20},{4,16},{8,28},{12,24},{16,4},{20,0},{24,12},{28,8},{1,21},{... | collective-permute-start | bytes 589832 | tf_op jit(solution)/shard_map/ppermute | solution.py:96
  136.9 2.4 %copy-start = (bf16[3,768,192]{1,2,0:T(8,128)(2,1)S(1)}, bf16[3,768,192]{1,2,0:T(8,128)(2,1)}, u32[]{:S(2)}) copy-start(bf16[3,768,192]{1,2,0:T(8,128)(2,1)} %param.19) | copy-start | bytes 2654212
  136.9 2.4 %collective-permute-start.25 = (bf16[4,128,768]{2,1,0:T(8,128)(2,1)S(1)}, bf16[4,128,768]{2,1,0:T(8,128)(2,1)S(1)}, u32[]{:S(2)}, u32[]{:S(2)}) collective-permute-start(bf16[4,128,768]{2,1,0:T(8,128)(2,1)S(1)} %pad_maximum_fusion.3), channel_id=1, source_target_pairs={{0,8},{8,0},{16,24},{24,16},{1,9},{9,1},{17,25},{25,17},{2,10},{10... | collective-permute-start | bytes 2359304 | tf_op jit(solution)/shard_map/ppermute | solution.py:96
  144.7 2.0 %collective-permute-start.26 = (bf16[2,512,192]{2,1,0:T(8,128)(2,1)S(1)}, bf16[2,512,192]{2,1,0:T(8,128)(2,1)S(1)}, u32[]{:S(2)}, u32[]{:S(2)}) collective-permute-start(bf16[2,512,192]{2,1,0:T(8,128)(2,1)S(1)} %get-tuple-element.16), channel_id=1, source_target_pairs={{0,8},{8,0},{16,24},{24,16},{1,9},{9,1},{17,25},{25,17},{2,10},{10... | collective-permute-start | bytes 1179656 | tf_op jit(solution)/shard_map/ppermute | solution.py:96
  146.8 8.4 %collective-permute-start.27 = (bf16[512,192]{1,0:T(8,128)(2,1)S(1)}, bf16[512,192]{1,0:T(8,128)(2,1)S(1)}, u32[]{:S(2)}, u32[]{:S(2)}) collective-permute-start(bf16[512,192]{1,0:T(8,128)(2,1)S(1)} %fusion.35), channel_id=1, source_target_pairs={{0,16},{8,24},{16,0},{24,8},{1,17},{9,25},{17,1},{25,9},{2,18},{10... | collective-permute-start | bytes 589832 | tf_op jit(solution)/shard_map/ppermute | solution.py:96
  (1 other events, 1.0 us)
Sparse Core Ops, SparseCore 0:
  16.9 24.5 all-gather.1

commit v5 on v4

--- a/solution.py
+++ b/solution.py
@@ -29,6 +29,7 @@
 def attend_kernel(sec_ref, near_ref, *refs, heads, masks):
     far, refs = refs[:3], refs[3:]
     core_ref, w_ref, out_w_ref, emb_ref, q_ref, k_ref, keep_ref, send_ref = refs
+    core, side = sec_ref[0] % 2, sec_ref[0] // 2
     own = near_ref.shape[0]
     keys = jnp.concatenate(
         [near_ref[...], far[0][...], core_ref[0], core_ref[1], far[1][...], far[2][...]]
@@ -65,16 +66,19 @@
         total = jnp.sum(weight, axis=1, keepdims=True)
         mixed = jnp.dot(weight.astype(jnp.bfloat16), value, preferred_element_type=jnp.float32)
         att = jnp.where(lane_head == h, mixed / total, att)
-    att = att.astype(jnp.bfloat16)
-    for m in range(len(masks)):
-        part = jnp.dot(att, out_w_ref[m], preferred_element_type=jnp.float32)
-        target = send_ref if m % 2 else keep_ref
-        for block, mask in enumerate(masks):
-            piece = part[block * own : (block + 1) * own]
-            if block == 0:
-                piece = piece + emb_ref[m]
-            at = pl.multiple_of((mask ^ sec_ref[0]) * own, own)
-            target[m // 2, pl.ds(at, own), :] = piece.astype(target.dtype)
+    part = jnp.dot(att.astype(jnp.bfloat16), out_w_ref[...], preferred_element_type=jnp.float32)
+    for block, mask in enumerate(masks):
+        piece = part[block * own : (block + 1) * own]
+        if block == 0:
+            piece = piece + emb_ref[...]
+        at = pl.multiple_of((mask ^ sec_ref[0]) * own, own)
+        for j in range(part.shape[1] // width // 2):
+            low = piece[:, 2 * j * width : (2 * j + 1) * width]
+            high = piece[:, (2 * j + 1) * width : (2 * j + 2) * width]
+            keep_ref[j ^ side, pl.ds(at, own), :] = jnp.where(core == 0, low, high)
+            send_ref[j ^ side, pl.ds(at, own), :] = jnp.where(core == 0, high, low).astype(
+                send_ref.dtype
+            )
 
 
 def build(n_sec, n_seq, n_dp):
@@ -101,6 +105,10 @@
     def after(x, *others):
         return lax.optimization_barrier((x,) + others)[0]
 
+    def absolute(blocks):
+        stacked, sec = jnp.stack(blocks), lax.axis_index("section")
+        return [lax.dynamic_index_in_dim(stacked, sec ^ j, 0, False) for j in range(n_sec)]
+
     def gather_section(x):
         across = flip(x, section=2)
         return [x, flip(after(x, across), section=1), across, flip(across, section=1)]
@@ -111,15 +119,21 @@
         for k in range(n_dp):
             block = rotate(other if k % 2 else same, k) if k else same
             part = lax.dynamic_update_slice(part, block, (0, ((dp_at - k) % n_dp) * rows, 0))
-        return lax.all_gather(part, "seq", axis=1, tiled=True)
+        whole = lax.all_gather(part, "seq", axis=1, tiled=True)
+        return jnp.concatenate(absolute(jnp.split(whole, n_sec, axis=1)), axis=1)
+
+    def row_of(y, k, rows):
+        sec, seq_at, dp_at = (lax.axis_index(a) for a in AXES)
+        block = (seq_at ^ y) * n_dp + (dp_at - k) % n_dp
+        each = n_seq * n_dp // n_sec
+        return ((block // each ^ sec) * each + block % each) * rows
 
     def place_rows(blocks):
-        seq_at, dp_at = lax.axis_index("seq"), lax.axis_index("dp")
-        mats, rows, units = blocks[0, 0].shape
-        whole = jnp.zeros((mats, n_seq * n_dp * rows, units), blocks[0, 0].dtype)
+        first = blocks[0, 2]
+        mats, rows, units = first.shape
+        whole = after(jnp.zeros((mats, n_seq * n_dp * rows, units), first.dtype), first)
         for (y, k), block in blocks.items():
-            at = ((seq_at ^ y) * n_dp + (dp_at - k) % n_dp) * rows
-            whole = lax.dynamic_update_slice(whole, block, (0, at, 0))
+            whole = lax.dynamic_update_slice(whole, block, (0, row_of(y, k, rows), 0))
         return whole
 
     def per_device(
@@ -145,10 +159,6 @@
         own_rows = tokens // n_sec
         half = w_gate.shape[1] // 2
 
-        def absolute(blocks):
-            stacked = jnp.stack(blocks)
-            return [lax.dynamic_index_in_dim(stacked, sec ^ j, 0, False) for j in range(n_sec)]
-
         def halves(x, which):
             return lax.dynamic_slice_in_dim(x, which * half, half, x.ndim - 1)
 
@@ -160,26 +170,31 @@
 
         beside = flip(mine, dp=1)
         both = jnp.concatenate([mine, beside], axis=0)
-        rows = jnp.concatenate(absolute(gather_section(both)), axis=1)
-        normed = layer_norm(rows.astype(jnp.float32), tile_gain).astype(jnp.bfloat16)
+        row_blocks = gather_section(both)
+        rows = jnp.concatenate(row_blocks, axis=1)
+        gain = jnp.concatenate(absolute(jnp.split(tile_gain, n_sec)))
+        normed = layer_norm(rows.astype(jnp.float32), gain).astype(jnp.bfloat16)
+        proj_blocks = gather_section(w_proj)
+        proj = jnp.concatenate(proj_blocks, axis=0)
 
         if ordered:
             g = {(0, 0): pair_same, (0, 2): rotate(pair_same, 2)}
             g[0, 1] = rotate(after(pair_other, g[0, 2]), 1)
             g[0, 3] = rotate(after(pair_other, g[0, 2]), 3)
-            for k in (0, 2, 1, 3):
-                g[1, k] = flip(g[0, k], seq=1)
+            g[1, 0], g[1, 2], g[1, 1] = (flip(g[0, k], seq=1) for k in (0, 2, 1))
+            g[1, 3] = flip(after(g[0, 3], normed), seq=1)
             gate_up = place_rows(g)
             d = {(0, 0): down_same, (0, 2): rotate(after(down_same, g[0, 1]), 2)}
-            d[0, 1] = rotate(after(down_other, d[0, 2], normed), 1)
-            d[0, 3] = rotate(after(down_other, d[0, 2], normed), 3)
-            for k in (0, 2, 1, 3):
+            d[1, 0] = flip(down_same, seq=1)
+            there = [row_blocks[1], row_blocks[3], proj_blocks[1], proj_blocks[3], d[1, 0]]
+            d[0, 1] = rotate(after(down_other, d[0, 2], *there), 1)
+            d[0, 3] = rotate(after(down_other, d[0, 2], *there), 3)
+            for k in (2, 1, 3):
                 d[1, k] = flip(d[0, k], seq=1)
         else:
             gate_up = gather_rows(pair_same, pair_other, seq_at, dp_at)
             down_all = gather_rows(down_same, down_other, seq_at, dp_at)[0]
 
-        proj = lax.all_gather(w_proj, "section", axis=0, tiled=True)
         gate = jnp.dot(normed, gate_up[0], preferred_element_type=jnp.float32)
         up = jnp.dot(normed, gate_up[1], preferred_element_type=jnp.float32)
         hidden = (jax.nn.silu(gate) * up).astype(jnp.bfloat16)
@@ -192,9 +207,9 @@
 
         if ordered:
             late = [d.pop((1, 1)), d.pop((1, 3))]
-            folded = fold(proj, place_rows(d)[0])
+            folded = fold(proj, after(place_rows(d)[0], hidden))
             for k, block in zip((1, 3), late):
-                at = ((1 - seq_at) * n_dp + (dp_at - k) % n_dp) * block.shape[1]
+                at = row_of(1, k, block.shape[1])
                 folded = folded + fold(
                     lax.dynamic_slice_in_dim(proj, at, block.shape[1], 0), block[0]
                 )
@@ -262,8 +277,6 @@
 
         width = w_qkv.shape[2]
         qkv = jnp.swapaxes(w_qkv, 1, 2)
-        out_w = jnp.stack(absolute(list(jnp.split(w_out, n_sec, axis=1))))
-        emb_cut = jnp.stack(absolute(list(jnp.split(emb, n_sec, axis=1))))
         if n_seq == 2:
             vmem = pl.BlockSpec(memory_space=pltpu.VMEM)
             keep, send = pl.pallas_call(
@@ -280,7 +293,7 @@
                     bytes_accessed=8 * 2**20,
                     transcendentals=local_heads * tokens * count,
                 ),
-            )(sec[None], slide_normed, *near, from_core, qkv, out_w, emb_cut, q_code, k_code)
+            )(sec[None], slide_normed, *near, from_core, qkv, w_out, emb, q_code, k_code)
         else:
 
             def by_head(x, matrix):
@@ -303,9 +316,10 @@
                 + (q_code.T, k_code),
             )
             att = att.transpose(1, 0, 2).reshape(tokens, width).astype(jnp.bfloat16)
-            parts = jnp.einsum("re,mec->mrc", att, out_w, preferred_element_type=jnp.float32)
-            old = lax.dynamic_slice_in_dim(parts, sec * own_rows, own_rows, 1)
-            parts = lax.dynamic_update_slice_in_dim(parts, old + emb_cut, sec * own_rows, 1)
+            parts = jnp.dot(att, w_out, preferred_element_type=jnp.float32)
+            old = lax.dynamic_slice_in_dim(parts, sec * own_rows, own_rows, 0)
+            parts = lax.dynamic_update_slice_in_dim(parts, old + emb, sec * own_rows, 0)
+            parts = jnp.stack(absolute(jnp.split(parts, n_sec, axis=1)))
             keep, send = parts[0::2], parts[1::2].astype(jnp.bfloat16)
 
         kept = keep + flip(send, section=1).astype(jnp.float32)

time: 163 us -> 141 us (0.87)
  between operations: 14.1 us -> 0.84 us
  local copies, waits for them, and re-layouts: 20.1 us -> 10.2 us
  matrix products: 15.8 us -> 7.91 us
  waiting for transfers between devices: 59.9 us -> 64.9 us
  starting transfers between devices: 33.8 us -> 38.3 us
    ppermute x6, waiting for transfers between devices: 6.36 us -> 26.5 us  [rotate(): return lax.ppermute(x, 'dp', [(i, (i + k) % n_dp) for i in range(n_dp)])]
    ppermute x22 -> x25, waiting for transfers between devices: 53.5 us -> 38.3 us  [flip(): return lax.ppermute(x, names if len(names) > 1 else names[0], pairs)]
    dynamic_update_slice x13 -> x14, local copies, waits for them, and re-layouts: 14.5 us -> 3.36 us  [place_rows(): whole = lax.dynamic_update_slice(whole, block, (0, row_of(y, k, rows), 0))]
    dot_general x3, matrix products: 6.5 us -> 2.26 us  [fold(): lax.dot_general(proj_rows, down_rows, (((0,), (0,)), ((), ())), preferred...]
    unnamed x40 -> x53, local copies, waits for them, and re-layouts: 0.09 us -> 2.79 us
    ppermute x6, starting transfers between devices: 12.7 us -> 15.2 us  [rotate(): return lax.ppermute(x, 'dp', [(i, (i + k) % n_dp) for i in range(n_dp)])]
    dot_general x1, matrix products: 4.51 us -> 2.03 us  [per_device(): up = jnp.dot(normed, gate_up[1], preferred_element_type=jnp.float32)]
    reduce_sum x2 -> x1, other arithmetic: 0.9 us -> 3.24 us  [layer_norm(): mean = jnp.mean(rows, axis=-1, keepdims=True)]
  transfers between devices with their start and end apart: 29 -> 31, of which waited for: 15 -> 15; matrix products, arithmetic and copies ran while one was open for 26% -> 17% of each run, Pallas kernels for 0% -> 0%
where the time goes in v5:
time: 141 us; the launch traced here: 140 us
  waiting for transfers between devices  64.9 us (46%)
  starting transfers between devices  38.3 us (27%)
  other arithmetic  12.7 us (9%)
  local copies, waits for them, and re-layouts  10.2 us (7%)
  matrix products  7.91 us (6%)
  Pallas kernels  5.63 us (4%)
    ppermute x25, waiting for transfers between devices, flip(): return lax.ppermute(x, names if len(names) > 1 else names[0], pairs)  38.3 us
    ppermute x6, waiting for transfers between devices, rotate(): return lax.ppermute(x, 'dp', [(i, (i + k) % n_dp) for i in range(n_dp)])  26.5 us
    ppermute x25, starting transfers between devices, flip(): return lax.ppermute(x, names if len(names) > 1 else names[0], pairs)  23.1 us
    ppermute x6, starting transfers between devices, rotate(): return lax.ppermute(x, 'dp', [(i, (i + k) % n_dp) for i in range(n_dp)])  15.2 us
    pallas_call x1, Pallas kernels, per_device(): pl.pallas_call(lambda *refs: attend_kernel(*refs, heads=local_heads, mask...  5.63 us
    dynamic_update_slice x14, local copies, waits for them, and re-layouts, place_rows(): whole = lax.dynamic_update_slice(whole, block, (0, row_of(y, k, rows), 0))  3.36 us
    reduce_sum x1, other arithmetic, layer_norm(): mean = jnp.mean(rows, axis=-1, keepdims=True)  3.24 us
  transfers between devices with their start and end apart: 31, of which 15 were waited for; matrix products, arithmetic and copies ran while one was open for 17% of the time, Pallas kernels for 0%

profile of v5, /device:TPU:0, one launch (start us, length us, event | category | flops | bytes accessed | tf_op | source)
XLA Modules:
  0.0 140.4 jit_solution(16418722376640025134)
XLA Ops:
  0.0 2.1 %fusion.21 = (bf16[2,192,512]{2,1,0:T(8,128)(2,1)S(1)}, bf16[2,192,512]{2,1,0:T(8,128)(2,1)}) fusion(s32[]{:T(128)S(6)} %select_n.251, bf16[1,192,1024]{2,1,0:T(8,128)(2,1)} %bitcast.97, bf16[1,192,1024]{2,1,0:T(8,128)(2,1)} %bitcast.98, s32[]{:T(128)S(6)} %select_n.260), kind=kLoop, calls=%fused_computation.39 | loop fusion | flops 1572864 | bytes 1572872 | tf_op jit(solution)/shard_map/stack | solution.py:165
  2.1 4.0 %collective-permute-start.7 = (bf16[2,192,512]{2,1,0:T(8,128)(2,1)S(1)}, bf16[2,192,512]{2,1,0:T(8,128)(2,1)}, u32[]{:S(2)}, u32[]{:S(2)}) collective-permute-start(bf16[2,192,512]{2,1,0:T(8,128)(2,1)S(1)} %get-tuple-element.41), channel_id=1, source_target_pairs={{0,2},{1,3},{2,0},{3,1},{4,6},{5,7},{6,4},{7,5},{8,10},{9,11},{10,... | collective-permute-start | bytes 1179656 | tf_op jit(solution)/shard_map/ppermute | solution.py:103
  6.1 1.5 %collective-permute-start.10 = (bf16[2,192,512]{2,1,0:T(8,128)(2,1)S(1)}, bf16[2,192,512]{2,1,0:T(8,128)(2,1)}, u32[]{:S(2)}, u32[]{:S(2)}) collective-permute-start(bf16[2,192,512]{2,1,0:T(8,128)(2,1)S(1)} %get-tuple-element.41), channel_id=1, source_target_pairs={{0,4},{4,0},{1,5},{5,1},{2,6},{6,2},{3,7},{7,3},{8,12},{12,8},{9,1... | collective-permute-start | bytes 1179656 | tf_op jit(solution)/shard_map/ppermute | solution.py:100
  7.6 1.6 %collective-permute-start = (bf16[512,384]{1,0:T(8,128)(2,1)}, bf16[512,384]{1,0:T(8,128)(2,1)S(1)}, u32[]{:S(2)}, u32[]{:S(2)}) collective-permute-start(bf16[512,384]{1,0:T(8,128)(2,1)} %bitcast.94), channel_id=1, source_target_pairs={{0,1},{1,0},{2,3},{3,2},{4,5},{5,4},{6,7},{7,6},{8,9},{9,8},{10,11... | collective-permute-start | bytes 1179656 | tf_op jit(solution)/shard_map/ppermute | solution.py:100
  9.2 1.5 %collective-permute-start.4 = (bf16[384,768]{1,0:T(8,128)(2,1)}, bf16[384,768]{1,0:T(8,128)(2,1)}, u32[]{:S(2)}, u32[]{:S(2)}) collective-permute-start(bf16[384,768]{1,0:T(8,128)(2,1)} %param.17), channel_id=1, source_target_pairs={{0,16},{8,24},{16,0},{24,8},{1,17},{9,25},{17,1},{25,9},{2,18},{10... | collective-permute-start | bytes 1769480 | tf_op jit(solution)/shard_map/ppermute | solution.py:100
  10.7 0.8 fusion.59
  11.5 1.8 %dynamic-slice_bitcast_fusion.1 = (bf16[1,192,512]{2,1,0:T(8,128)(2,1)}, bf16[1,192,512]{2,1,0:T(8,128)(2,1)}) fusion(bf16[1024,192]{0,1:T(8,128)(2,1)} %param.16, s32[]{:T(128)S(6)} %select_n.260, s32[]{:T(128)S(6)} %select_n.251), kind=kLoop, calls=%fused_computation.66 | loop fusion | bytes 786440 | tf_op jit(solution)/shard_map/dynamic_slice | solution.py:163
  14.3 1.1 constant_dynamic-update-slice_fusion.3
  15.4 8.4 %collective-permute-done.7 = bf16[2,192,512]{2,1,0:T(8,128)(2,1)} collective-permute-done((bf16[2,192,512]{2,1,0:T(8,128)(2,1)S(1)}, bf16[2,192,512]{2,1,0:T(8,128)(2,1)}, u32[]{:S(2)}, u32[]{:S(2)}) %collective-permute-start.7) | collective-permute-done | bytes 393248 | tf_op jit(solution)/shard_map/ppermute | solution.py:103
  25.0 3.3 %collective-permute-start.9 = (bf16[2,192,512]{2,1,0:T(8,128)(2,1)}, bf16[2,192,512]{2,1,0:T(8,128)(2,1)S(1)}, u32[]{:S(2)}, u32[]{:S(2)}) collective-permute-start(bf16[2,192,512]{2,1,0:T(8,128)(2,1)} %get-tuple-element.19), channel_id=1, source_target_pairs={{0,3},{1,0},{2,1},{3,2},{4,7},{5,4},{6,5},{7,6},{8,11},{9,8},{10,9... | collective-permute-start | bytes 1179656 | tf_op jit(solution)/shard_map/ppermute | solution.py:103
  28.4 1.6 %collective-permute-start.1 = (bf16[1024,384]{1,0:T(8,128)(2,1)S(1)}, bf16[1024,384]{1,0:T(8,128)(2,1)S(1)}, u32[]{:S(2)}, u32[]{:S(2)}) collective-permute-start(bf16[1024,384]{1,0:T(8,128)(2,1)S(1)} %pad_maximum_fusion.1), channel_id=1, source_target_pairs={{0,16},{8,24},{16,0},{24,8},{1,17},{9,25},{17,1},{25,9},{2,18},{10... | collective-permute-start | bytes 2359304 | tf_op jit(solution)/shard_map/ppermute | solution.py:100
  30.3 1.6 %collective-permute-start.11 = (bf16[2,192,512]{2,1,0:T(8,128)(2,1)}, bf16[2,192,512]{2,1,0:T(8,128)(2,1)S(1)}, u32[]{:S(2)}, u32[]{:S(2)}) collective-permute-start(bf16[2,192,512]{2,1,0:T(8,128)(2,1)} %collective-permute-done.7), channel_id=1, source_target_pairs={{0,4},{4,0},{1,5},{5,1},{2,6},{6,2},{3,7},{7,3},{8,12},{12,8},{9,1... | collective-permute-start | bytes 1179656 | tf_op jit(solution)/shard_map/ppermute | solution.py:100
  31.9 1.1 constant_dynamic-update-slice_fusion.11
  32.9 5.1 %collective-permute-done.8 = bf16[2,192,512]{2,1,0:T(8,128)(2,1)} collective-permute-done((bf16[2,192,512]{2,1,0:T(8,128)(2,1)}, bf16[2,192,512]{2,1,0:T(8,128)(2,1)}, u32[]{:S(2)}, u32[]{:S(2)}) %collective-permute-start.8) | collective-permute-done | bytes 393248 | tf_op jit(solution)/shard_map/ppermute | solution.py:103
  38.0 1.6 %collective-permute-start.15 = (bf16[1,192,512]{2,1,0:T(8,128)(2,1)S(1)}, bf16[1,192,512]{2,1,0:T(8,128)(2,1)S(1)}, u32[]{:S(2)}, u32[]{:S(2)}) collective-permute-start(bf16[1,192,512]{2,1,0:T(8,128)(2,1)S(1)} %copy-done.6), channel_id=1, source_target_pairs={{0,4},{4,0},{1,5},{5,1},{2,6},{6,2},{3,7},{7,3},{8,12},{12,8},{9,1... | collective-permute-start | bytes 589832 | tf_op jit(solution)/shard_map/ppermute | solution.py:100
  39.6 1.0 constant_dynamic-update-slice_fusion.10
  40.6 3.8 %collective-permute-done.9 = bf16[2,192,512]{2,1,0:T(8,128)(2,1)S(1)} collective-permute-done((bf16[2,192,512]{2,1,0:T(8,128)(2,1)}, bf16[2,192,512]{2,1,0:T(8,128)(2,1)S(1)}, u32[]{:S(2)}, u32[]{:S(2)}) %collective-permute-start.9) | collective-permute-done | bytes 393248 | tf_op jit(solution)/shard_map/ppermute | solution.py:103
  44.5 3.5 %collective-permute-start.14 = (bf16[1,192,512]{2,1,0:T(8,128)(2,1)S(1)}, bf16[1,192,512]{2,1,0:T(8,128)(2,1)S(1)}, u32[]{:S(2)}, u32[]{:S(2)}) collective-permute-start(bf16[1,192,512]{2,1,0:T(8,128)(2,1)S(1)} %copy-done.6), channel_id=1, source_target_pairs={{0,2},{1,3},{2,0},{3,1},{4,6},{5,7},{6,4},{7,5},{8,10},{9,11},{10,... | collective-permute-start | bytes 589832 | tf_op jit(solution)/shard_map/ppermute | solution.py:103
  47.9 1.0 constant_dynamic-update-slice_fusion.8
  49.6 8.1 %collective-permute-done.14 = bf16[1,192,512]{2,1,0:T(8,128)(2,1)S(1)} collective-permute-done((bf16[1,192,512]{2,1,0:T(8,128)(2,1)S(1)}, bf16[1,192,512]{2,1,0:T(8,128)(2,1)S(1)}, u32[]{:S(2)}, u32[]{:S(2)}) %collective-permute-start.14) | collective-permute-done | bytes 196640 | tf_op jit(solution)/shard_map/ppermute | solution.py:103
  58.6 1.8 %collective-permute-done.12 = bf16[2,192,512]{2,1,0:T(8,128)(2,1)S(1)} collective-permute-done((bf16[2,192,512]{2,1,0:T(8,128)(2,1)}, bf16[2,192,512]{2,1,0:T(8,128)(2,1)S(1)}, u32[]{:S(2)}, u32[]{:S(2)}) %collective-permute-start.12) | collective-permute-done | bytes 393248 | tf_op jit(solution)/shard_map/ppermute | solution.py:100
  61.1 1.1 constant_dynamic-update-slice_fusion.1
  62.3 2.5 %collective-permute-start.16 = (bf16[1,192,512]{2,1,0:T(8,128)(2,1)S(1)}, bf16[1,192,512]{2,1,0:T(8,128)(2,1)S(1)}, u32[]{:S(2)}, u32[]{:S(2)}) collective-permute-start(bf16[1,192,512]{2,1,0:T(8,128)(2,1)S(1)} %copy-done.5), channel_id=1, source_target_pairs={{0,1},{1,2},{2,3},{3,0},{4,5},{5,6},{6,7},{7,4},{8,9},{9,10},{10,1... | collective-permute-start | bytes 589832 | tf_op jit(solution)/shard_map/ppermute | solution.py:103
  64.8 1.3 collective-permute-start.17
  66.2 3.2 %convert_reduce_fusion = (f32[1024]{0:T(1024)S(1)}, bf16[1024,1536]{1,0:T(8,128)(2,1)S(1)}) fusion(bf16[1024,384]{1,0:T(8,128)(2,1)S(1)} %collective-permute-done.3, bf16[1024,384]{1,0:T(8,128)(2,1)S(1)} %collective-permute-done.1, bf16[1024,384]{1,0:T(8,128)(2,1)S(1)} %collective-permute-done.2, bf16[512,384]{1,0:T(8,128)(2,1)S(1)} %collective-permute-done, ...), kind=kLoop, calls=%fused_computation.1 | loop fusion | flops 18873344 | bytes 6295552 | tf_op jit(solution)/shard_map/reduce_sum | solution.py:15
  69.4 1.0 fusion.2
  70.4 1.0 fusion.4
  71.4 1.5 %collective-permute-start.13 = (bf16[2,192,512]{2,1,0:T(8,128)(2,1)S(1)}, bf16[2,192,512]{2,1,0:T(8,128)(2,1)S(1)}, u32[]{:S(2)}, u32[]{:S(2)}) collective-permute-start(bf16[2,192,512]{2,1,0:T(8,128)(2,1)S(1)} %collective-permute-done.9), channel_id=1, source_target_pairs={{0,4},{4,0},{1,5},{5,1},{2,6},{6,2},{3,7},{7,3},{8,12},{12,8},{9,1... | collective-permute-start | bytes 1179656 | tf_op jit(solution)/shard_map/ppermute | solution.py:100
  73.6 1.1 collective-permute-done.17
  74.7 1.2 collective-permute-start.20
  76.0 7.6 %collective-permute-done.13 = bf16[2,192,512]{2,1,0:T(8,128)(2,1)S(1)} collective-permute-done((bf16[2,192,512]{2,1,0:T(8,128)(2,1)S(1)}, bf16[2,192,512]{2,1,0:T(8,128)(2,1)S(1)}, u32[]{:S(2)}, u32[]{:S(2)}) %collective-permute-start.13) | collective-permute-done | bytes 393248 | tf_op jit(solution)/shard_map/ppermute | solution.py:100
  83.6 1.8 %fusion.6 = f32[1024,512]{1,0:T(8,128)S(1)} fusion(bf16[1024,1536]{1,0:T(8,128)(2,1)S(1)} %fusion.4, bf16[2,1536,512]{2,1,0:T(8,128)(2,1)S(1)} %constant_dynamic-update-slice_fusion.5), kind=kOutput, calls=%fused_computation.12 | convolution fusion | flops 1610612736 | bytes 6815744 | tf_op jit(solution)/shard_map/dot_general | solution.py:198
  85.4 2.0 %multiply_convert_fusion = bf16[1024,512]{1,0:T(8,128)(2,1)S(1)} fusion(f32[1024,512]{1,0:T(8,128)S(1)} %fusion.6, bf16[1024,1536]{1,0:T(8,128)(2,1)S(1)} %fusion.4, bf16[2,1536,512]{2,1,0:T(8,128)(2,1)S(1)} %constant_dynamic-update-slice_fusion.5), kind=kOutput, calls=%fused_computation.8 | convolution fusion | flops 1613758464 | bytes 7864320 | tf_op jit(solution)/shard_map/dot_general | solution.py:199
  87.4 1.4 %fusion.61 = f32[768,512]{1,0:T(8,128)S(1)} fusion(bf16[1536,768]{1,0:T(8,128)(2,1)S(1)} %constant_dynamic-update-slice_fusion, bf16[1536,512]{1,0:T(8,128)(2,1)S(1)} %bitcast_dynamic-update-slice_fusion), kind=kOutput, calls=%fused_computation.142 | convolution fusion | flops 1207959552 | bytes 5505024 | tf_op jit(solution)/shard_map/dot_general | solution.py:204
  89.3 1.1 collective-permute-done.20
  91.8 2.1 %collective-permute-done.21 = bf16[2,2,128,768]{3,2,1,0:T(8,128)(2,1)S(1)} collective-permute-done((bf16[2,2,128,768]{3,2,1,0:T(8,128)(2,1)S(1)}, bf16[2,2,128,768]{3,2,1,0:T(8,128)(2,1)S(1)}, u32[]{:S(2)}, u32[]{:S(2)}) %collective-permute-start.21) | collective-permute-done | bytes 786464 | tf_op jit(solution)/shard_map/ppermute | solution.py:100
  94.6 1.5 %collective-permute-start.22 = (bf16[128,768]{1,0:T(8,128)(2,1)S(1)}, bf16[128,768]{1,0:T(8,128)(2,1)S(1)}, u32[]{:S(2)}, u32[]{:S(2)}) collective-permute-start(bf16[128,768]{1,0:T(8,128)(2,1)S(1)} %get-tuple-element.43), channel_id=1, source_target_pairs={{0,16},{8,24},{16,0},{24,8},{1,17},{9,25},{17,1},{25,9},{2,18},{10... | collective-permute-start | bytes 589832 | tf_op jit(solution)/shard_map/ppermute | solution.py:100
  96.2 2.1 %collective-permute-start.23 = (bf16[128,768]{1,0:T(8,128)(2,1)S(1)}, bf16[128,768]{1,0:T(8,128)(2,1)S(1)}, u32[]{:S(2)}, u32[]{:S(2)}) collective-permute-start(bf16[128,768]{1,0:T(8,128)(2,1)S(1)} %fusion.33), channel_id=1, source_target_pairs={{0,1},{1,0},{2,3},{3,2},{4,5},{5,4},{6,7},{7,6},{8,9},{9,8},{10,11... | collective-permute-start | bytes 589832 | tf_op jit(solution)/shard_map/ppermute | solution.py:100
  98.5 7.3 %collective-permute-done.22 = bf16[128,768]{1,0:T(8,128)(2,1)S(1)} collective-permute-done((bf16[128,768]{1,0:T(8,128)(2,1)S(1)}, bf16[128,768]{1,0:T(8,128)(2,1)S(1)}, u32[]{:S(2)}, u32[]{:S(2)}) %collective-permute-start.22) | collective-permute-done | bytes 196640 | tf_op jit(solution)/shard_map/ppermute | solution.py:100
  105.8 1.2 collective-permute-done.23
  108.0 1.5 %collective-permute-start.25 = (bf16[128,768]{1,0:T(8,128)(2,1)S(1)}, bf16[128,768]{1,0:T(8,128)(2,1)S(1)}, u32[]{:S(2)}, u32[]{:S(2)}) collective-permute-start(bf16[128,768]{1,0:T(8,128)(2,1)S(1)} %multiply_convert_fusion.1.refs_1_), channel_id=1, source_target_pairs={{0,16},{8,24},{16,0},{24,8},{1,17},{9,25},{17,1},{25,9},{2,18},{10... | collective-permute-start | bytes 589832 | tf_op jit(solution)/shard_map/ppermute | solution.py:100
  110.3 1.3 collective-permute-start.27
  111.7 4.0 %collective-permute-done.25.refs_2_ = bf16[128,768]{1,0:T(8,128)(2,1)S(1)} collective-permute-done((bf16[128,768]{1,0:T(8,128)(2,1)S(1)}, bf16[128,768]{1,0:T(8,128)(2,1)S(1)}, u32[]{:S(2)}, u32[]{:S(2)}) %collective-permute-start.25) | collective-permute-done | bytes 196640 | tf_op jit(solution)/shard_map/ppermute | solution.py:100
  115.8 3.6 %collective-permute-done.26.refs_3_ = bf16[128,768]{1,0:T(8,128)(2,1)S(1)} collective-permute-done((bf16[128,768]{1,0:T(8,128)(2,1)S(1)}, bf16[128,768]{1,0:T(8,128)(2,1)S(1)}, u32[]{:S(2)}, u32[]{:S(2)}) %collective-permute-start.26) | collective-permute-done | bytes 196640 | tf_op jit(solution)/shard_map/ppermute | solution.py:100
  120.3 2.7 %fusion.29.refs_9_ = s32[512,4]{1,0:T(8,128)S(1)} fusion(s32[4]{0:T(128)S(1)} %copy-done.15, s32[512]{0:T(512)S(1)} %get-tuple-element.38, s32[4]{0:T(128)S(1)} %sign.89, s32[512]{0:T(512)S(1)} %broadcast_multiply_fusion.2, s32[512]{0:T(512)S(1)} %get-tuple-element.37), kind=kLoop, calls=%fused_computation.50 | loop fusion | flops 16384 | bytes 14368 | tf_op jit(solution)/shard_map/add | solution.py:271
  123.1 5.6 %shard_map.118 = (f32[2,512,192]{2,1,0:T(8,128)S(1)}, bf16[2,512,192]{2,1,0:T(8,128)(2,1)S(1)}) custom-call(s32[1]{0:T(128)} %bitcast.refs_0_, bf16[128,768]{1,0:T(8,128)(2,1)S(1)} %multiply_convert_fusion.1.refs_1_, bf16[128,768]{1,0:T(8,128)(2,1)S(1)} %collective-permute-done.25.refs_2_, bf16[128,768]{1,0:T(8,128)(2,1)S(1)} %collective-permute-done.26.refs_3_, ...), custom_call_target="tpu_custom_call" | custom-call | flops 2516582400 | bytes 8388608 | tf_op jit(solution)/shard_map/pallas_call | solution.py:282
  129.2 1.5 %collective-permute-done.29 = bf16[2,512,192]{2,1,0:T(8,128)(2,1)S(1)} collective-permute-done((bf16[2,512,192]{2,1,0:T(8,128)(2,1)S(1)}, bf16[2,512,192]{2,1,0:T(8,128)(2,1)S(1)}, u32[]{:S(2)}, u32[]{:S(2)}) %collective-permute-start.29) | collective-permute-done | bytes 393248 | tf_op jit(solution)/shard_map/ppermute | solution.py:100
  131.6 8.0 %collective-permute-done.30 = bf16[512,192]{1,0:T(8,128)(2,1)S(1)} collective-permute-done((bf16[512,192]{1,0:T(8,128)(2,1)S(1)}, bf16[512,192]{1,0:T(8,128)(2,1)S(1)}, u32[]{:S(2)}, u32[]{:S(2)}) %collective-permute-start.30) | collective-permute-done | bytes 196640 | tf_op jit(solution)/shard_map/ppermute | solution.py:100
  (147 shorter events, 12.8 us)
Async XLA Ops:
  0.0 28.3 %copy-start.2 = (bf16[1,512,384]{2,1,0:T(8,128)(2,1)S(1)}, bf16[1,512,384]{2,1,0:T(8,128)(2,1)}, u32[]{:S(2)}) copy-start(bf16[1,512,384]{2,1,0:T(8,128)(2,1)} %param.12) | copy-start | bytes 1179652
  0.0 13.3 %copy-start.16 = (s32[1,3]{1,0:T(1,128)S(1)}, s32[1,3]{1,0:T(1,128)}, u32[]{:S(2)}) copy-start(s32[1,3]{1,0:T(1,128)} %param.21) | copy-start | bytes 40
  2.1 21.8 %collective-permute-start.7 = (bf16[2,192,512]{2,1,0:T(8,128)(2,1)S(1)}, bf16[2,192,512]{2,1,0:T(8,128)(2,1)}, u32[]{:S(2)}, u32[]{:S(2)}) collective-permute-start(bf16[2,192,512]{2,1,0:T(8,128)(2,1)S(1)} %get-tuple-element.41), channel_id=1, source_target_pairs={{0,2},{1,3},{2,0},{3,1},{4,6},{5,7},{6,4},{7,5},{8,10},{9,11},{10,... | collective-permute-start | bytes 1179656 | tf_op jit(solution)/shard_map/ppermute | solution.py:103
  6.1 38.4 %collective-permute-start.10 = (bf16[2,192,512]{2,1,0:T(8,128)(2,1)S(1)}, bf16[2,192,512]{2,1,0:T(8,128)(2,1)}, u32[]{:S(2)}, u32[]{:S(2)}) collective-permute-start(bf16[2,192,512]{2,1,0:T(8,128)(2,1)S(1)} %get-tuple-element.41), channel_id=1, source_target_pairs={{0,4},{4,0},{1,5},{5,1},{2,6},{6,2},{3,7},{7,3},{8,12},{12,8},{9,1... | collective-permute-start | bytes 1179656 | tf_op jit(solution)/shard_map/ppermute | solution.py:100
  7.6 20.7 %collective-permute-start = (bf16[512,384]{1,0:T(8,128)(2,1)}, bf16[512,384]{1,0:T(8,128)(2,1)S(1)}, u32[]{:S(2)}, u32[]{:S(2)}) collective-permute-start(bf16[512,384]{1,0:T(8,128)(2,1)} %bitcast.94), channel_id=1, source_target_pairs={{0,1},{1,0},{2,3},{3,2},{4,5},{5,4},{6,7},{7,6},{8,9},{9,8},{10,11... | collective-permute-start | bytes 1179656 | tf_op jit(solution)/shard_map/ppermute | solution.py:100
  9.2 21.1 %collective-permute-start.4 = (bf16[384,768]{1,0:T(8,128)(2,1)}, bf16[384,768]{1,0:T(8,128)(2,1)}, u32[]{:S(2)}, u32[]{:S(2)}) collective-permute-start(bf16[384,768]{1,0:T(8,128)(2,1)} %param.17), channel_id=1, source_target_pairs={{0,16},{8,24},{16,0},{24,8},{1,17},{9,25},{17,1},{25,9},{2,18},{10... | collective-permute-start | bytes 1769480 | tf_op jit(solution)/shard_map/ppermute | solution.py:100
  13.6 10.8 %copy-start.20 = (s32[128]{0:T(128)}, s32[128]{0:T(128)S(1)}, u32[]{:S(2)}) copy-start(s32[128]{0:T(128)S(1)} %get-tuple-element.56) | copy-start | bytes 1540
  14.3 10.2 %copy-start.11 = (s32[128]{0:T(128)}, s32[128]{0:T(128)S(1)}, u32[]{:S(2)}) copy-start(s32[128]{0:T(128)S(1)} %get-tuple-element.57) | copy-start | bytes 1540
  14.3 10.2 %copy-start.13 = (s32[128]{0:T(128)}, s32[128]{0:T(128)S(1)}, u32[]{:S(2)}) copy-start(s32[128]{0:T(128)S(1)} %get-tuple-element.58) | copy-start | bytes 1540
  14.3 10.1 %copy-start.22 = (s32[128]{0:T(128)}, s32[128]{0:T(128)S(1)}, u32[]{:S(2)}) copy-start(s32[128]{0:T(128)S(1)} %iota_add_fusion.3) | copy-start | bytes 1540
  23.9 14.1 %collective-permute-start.8 = (bf16[2,192,512]{2,1,0:T(8,128)(2,1)}, bf16[2,192,512]{2,1,0:T(8,128)(2,1)}, u32[]{:S(2)}, u32[]{:S(2)}) collective-permute-start(bf16[2,192,512]{2,1,0:T(8,128)(2,1)} %get-tuple-element.19), channel_id=1, source_target_pairs={{0,1},{1,2},{2,3},{3,0},{4,5},{5,6},{6,7},{7,4},{8,9},{9,10},{10,1... | collective-permute-start | bytes 1179656 | tf_op jit(solution)/shard_map/ppermute | solution.py:103
  25.0 19.4 %collective-permute-start.9 = (bf16[2,192,512]{2,1,0:T(8,128)(2,1)}, bf16[2,192,512]{2,1,0:T(8,128)(2,1)S(1)}, u32[]{:S(2)}, u32[]{:S(2)}) collective-permute-start(bf16[2,192,512]{2,1,0:T(8,128)(2,1)} %get-tuple-element.19), channel_id=1, source_target_pairs={{0,3},{1,0},{2,1},{3,2},{4,7},{5,4},{6,5},{7,6},{8,11},{9,8},{10,9... | collective-permute-start | bytes 1179656 | tf_op jit(solution)/shard_map/ppermute | solution.py:103
  28.4 9.6 %copy-start.6 = (bf16[1,192,512]{2,1,0:T(8,128)(2,1)S(1)}, bf16[1,192,512]{2,1,0:T(8,128)(2,1)}, u32[]{:S(2)}) copy-start(bf16[1,192,512]{2,1,0:T(8,128)(2,1)} %get-tuple-element.21) | copy-start | bytes 589828
  28.4 16.0 %copy-start.4 = (bf16[384,768]{1,0:T(8,128)(2,1)S(1)}, bf16[384,768]{1,0:T(8,128)(2,1)}, u32[]{:S(2)}) copy-start(bf16[384,768]{1,0:T(8,128)(2,1)} %param.17) | copy-start | bytes 1769476
  28.4 29.4 %collective-permute-start.1 = (bf16[1024,384]{1,0:T(8,128)(2,1)S(1)}, bf16[1024,384]{1,0:T(8,128)(2,1)S(1)}, u32[]{:S(2)}, u32[]{:S(2)}) collective-permute-start(bf16[1024,384]{1,0:T(8,128)(2,1)S(1)} %pad_maximum_fusion.1), channel_id=1, source_target_pairs={{0,16},{8,24},{16,0},{24,8},{1,17},{9,25},{17,1},{25,9},{2,18},{10... | collective-permute-start | bytes 2359304 | tf_op jit(solution)/shard_map/ppermute | solution.py:100
  30.3 18.7 %collective-permute-start.11 = (bf16[2,192,512]{2,1,0:T(8,128)(2,1)}, bf16[2,192,512]{2,1,0:T(8,128)(2,1)S(1)}, u32[]{:S(2)}, u32[]{:S(2)}) collective-permute-start(bf16[2,192,512]{2,1,0:T(8,128)(2,1)} %collective-permute-done.7), channel_id=1, source_target_pairs={{0,4},{4,0},{1,5},{5,1},{2,6},{6,2},{3,7},{7,3},{8,12},{12,8},{9,1... | collective-permute-start | bytes 1179656 | tf_op jit(solution)/shard_map/ppermute | solution.py:100
  38.0 19.8 %copy-start.3 = (bf16[1024,192]{0,1:T(8,128)(2,1)S(1)}, bf16[1024,192]{0,1:T(8,128)(2,1)}, u32[]{:S(2)}) copy-start(bf16[1024,192]{0,1:T(8,128)(2,1)} %param.16) | copy-start | bytes 1179652
  38.0 20.5 %collective-permute-start.15 = (bf16[1,192,512]{2,1,0:T(8,128)(2,1)S(1)}, bf16[1,192,512]{2,1,0:T(8,128)(2,1)S(1)}, u32[]{:S(2)}, u32[]{:S(2)}) collective-permute-start(bf16[1,192,512]{2,1,0:T(8,128)(2,1)S(1)} %copy-done.6), channel_id=1, source_target_pairs={{0,4},{4,0},{1,5},{5,1},{2,6},{6,2},{3,7},{7,3},{8,12},{12,8},{9,1... | collective-permute-start | bytes 589832 | tf_op jit(solution)/shard_map/ppermute | solution.py:100
  44.4 16.6 %collective-permute-start.5 = (bf16[384,768]{1,0:T(8,128)(2,1)S(1)}, bf16[384,768]{1,0:T(8,128)(2,1)S(1)}, u32[]{:S(2)}, u32[]{:S(2)}) collective-permute-start(bf16[384,768]{1,0:T(8,128)(2,1)S(1)} %copy-done.4), channel_id=1, source_target_pairs={{0,8},{8,0},{16,24},{24,16},{1,9},{9,1},{17,25},{25,17},{2,10},{10... | collective-permute-start | bytes 1769480 | tf_op jit(solution)/shard_map/ppermute | solution.py:100
  44.5 13.2 %collective-permute-start.14 = (bf16[1,192,512]{2,1,0:T(8,128)(2,1)S(1)}, bf16[1,192,512]{2,1,0:T(8,128)(2,1)S(1)}, u32[]{:S(2)}, u32[]{:S(2)}) collective-permute-start(bf16[1,192,512]{2,1,0:T(8,128)(2,1)S(1)} %copy-done.6), channel_id=1, source_target_pairs={{0,2},{1,3},{2,0},{3,1},{4,6},{5,7},{6,4},{7,5},{8,10},{9,11},{10,... | collective-permute-start | bytes 589832 | tf_op jit(solution)/shard_map/ppermute | solution.py:103
  49.0 11.5 %collective-permute-start.12 = (bf16[2,192,512]{2,1,0:T(8,128)(2,1)}, bf16[2,192,512]{2,1,0:T(8,128)(2,1)S(1)}, u32[]{:S(2)}, u32[]{:S(2)}) collective-permute-start(bf16[2,192,512]{2,1,0:T(8,128)(2,1)} %collective-permute-done.8), channel_id=1, source_target_pairs={{0,4},{4,0},{1,5},{5,1},{2,6},{6,2},{3,7},{7,3},{8,12},{12,8},{9,1... | collective-permute-start | bytes 1179656 | tf_op jit(solution)/shard_map/ppermute | solution.py:100
  57.9 4.4 %collective-permute-start.2 = (bf16[1024,384]{1,0:T(8,128)(2,1)S(1)}, bf16[1024,384]{1,0:T(8,128)(2,1)S(1)}, u32[]{:S(2)}, u32[]{:S(2)}) collective-permute-start(bf16[1024,384]{1,0:T(8,128)(2,1)S(1)} %pad_maximum_fusion.1), channel_id=1, source_target_pairs={{0,8},{8,0},{16,24},{24,16},{1,9},{9,1},{17,25},{25,17},{2,10},{10... | collective-permute-start | bytes 2359304 | tf_op jit(solution)/shard_map/ppermute | solution.py:100
  57.9 4.4 %collective-permute-start.3 = (bf16[1024,384]{1,0:T(8,128)(2,1)S(1)}, bf16[1024,384]{1,0:T(8,128)(2,1)S(1)}, u32[]{:S(2)}, u32[]{:S(2)}) collective-permute-start(bf16[1024,384]{1,0:T(8,128)(2,1)S(1)} %collective-permute-done.1), channel_id=1, source_target_pairs={{0,8},{8,0},{16,24},{24,16},{1,9},{9,1},{17,25},{25,17},{2,10},{10... | collective-permute-start | bytes 2359304 | tf_op jit(solution)/shard_map/ppermute | solution.py:100
  58.4 3.9 %copy-start.5 = (bf16[1,192,512]{2,1,0:T(8,128)(2,1)S(1)}, bf16[1,192,512]{2,1,0:T(8,128)(2,1)}, u32[]{:S(2)}) copy-start(bf16[1,192,512]{2,1,0:T(8,128)(2,1)} %get-tuple-element.23) | copy-start | bytes 589828
  58.5 3.8 %collective-permute-start.6 = (bf16[384,768]{1,0:T(8,128)(2,1)}, bf16[384,768]{1,0:T(8,128)(2,1)S(1)}, u32[]{:S(2)}, u32[]{:S(2)}) collective-permute-start(bf16[384,768]{1,0:T(8,128)(2,1)} %collective-permute-done.4), channel_id=1, source_target_pairs={{0,8},{8,0},{16,24},{24,16},{1,9},{9,1},{17,25},{25,17},{2,10},{10... | collective-permute-start | bytes 1769480 | tf_op jit(solution)/shard_map/ppermute | solution.py:100
  60.5 15.5 %collective-permute-start.18 = (bf16[1,192,512]{2,1,0:T(8,128)(2,1)S(1)}, bf16[1,192,512]{2,1,0:T(8,128)(2,1)S(1)}, u32[]{:S(2)}, u32[]{:S(2)}) collective-permute-start(bf16[1,192,512]{2,1,0:T(8,128)(2,1)S(1)} %collective-permute-done.14), channel_id=1, source_target_pairs={{0,4},{4,0},{1,5},{5,1},{2,6},{6,2},{3,7},{7,3},{8,12},{12,8},{9,1... | collective-permute-start | bytes 589832 | tf_op jit(solution)/shard_map/ppermute | solution.py:100
  62.3 10.7 %collective-permute-start.16 = (bf16[1,192,512]{2,1,0:T(8,128)(2,1)S(1)}, bf16[1,192,512]{2,1,0:T(8,128)(2,1)S(1)}, u32[]{:S(2)}, u32[]{:S(2)}) collective-permute-start(bf16[1,192,512]{2,1,0:T(8,128)(2,1)S(1)} %copy-done.5), channel_id=1, source_target_pairs={{0,1},{1,2},{2,3},{3,0},{4,5},{5,6},{6,7},{7,4},{8,9},{9,10},{10,1... | collective-permute-start | bytes 589832 | tf_op jit(solution)/shard_map/ppermute | solution.py:103
  64.8 9.9 %collective-permute-start.17 = (bf16[1,192,512]{2,1,0:T(8,128)(2,1)S(1)}, bf16[1,192,512]{2,1,0:T(8,128)(2,1)S(1)}, u32[]{:S(2)}, u32[]{:S(2)}) collective-permute-start(bf16[1,192,512]{2,1,0:T(8,128)(2,1)S(1)} %copy-done.5), channel_id=1, source_target_pairs={{0,3},{1,0},{2,1},{3,2},{4,7},{5,4},{6,5},{7,6},{8,11},{9,8},{10,9... | collective-permute-start | bytes 589832 | tf_op jit(solution)/shard_map/ppermute | solution.py:103
  71.4 12.1 %collective-permute-start.13 = (bf16[2,192,512]{2,1,0:T(8,128)(2,1)S(1)}, bf16[2,192,512]{2,1,0:T(8,128)(2,1)S(1)}, u32[]{:S(2)}, u32[]{:S(2)}) collective-permute-start(bf16[2,192,512]{2,1,0:T(8,128)(2,1)S(1)} %collective-permute-done.9), channel_id=1, source_target_pairs={{0,4},{4,0},{1,5},{5,1},{2,6},{6,2},{3,7},{7,3},{8,12},{12,8},{9,1... | collective-permute-start | bytes 1179656 | tf_op jit(solution)/shard_map/ppermute | solution.py:100
  73.0 15.8 %collective-permute-start.19 = (bf16[1,192,512]{2,1,0:T(8,128)(2,1)S(1)}, bf16[1,192,512]{2,1,0:T(8,128)(2,1)S(1)}, u32[]{:S(2)}, u32[]{:S(2)}) collective-permute-start(bf16[1,192,512]{2,1,0:T(8,128)(2,1)S(1)} %collective-permute-done.16), channel_id=1, source_target_pairs={{0,4},{4,0},{1,5},{5,1},{2,6},{6,2},{3,7},{7,3},{8,12},{12,8},{9,1... | collective-permute-start | bytes 589832 | tf_op jit(solution)/shard_map/ppermute | solution.py:100
  74.7 15.8 %collective-permute-start.20 = (bf16[1,192,512]{2,1,0:T(8,128)(2,1)S(1)}, bf16[1,192,512]{2,1,0:T(8,128)(2,1)S(1)}, u32[]{:S(2)}, u32[]{:S(2)}) collective-permute-start(bf16[1,192,512]{2,1,0:T(8,128)(2,1)S(1)} %collective-permute-done.17), channel_id=1, source_target_pairs={{0,4},{4,0},{1,5},{5,1},{2,6},{6,2},{3,7},{7,3},{8,12},{12,8},{9,1... | collective-permute-start | bytes 589832 | tf_op jit(solution)/shard_map/ppermute | solution.py:100
  89.3 2.5 %copy-start.12 = (s32[128]{0:T(128)S(1)}, s32[128]{0:T(128)}, u32[]{:S(2)}) copy-start(s32[128]{0:T(128)} %copy-done.11) | copy-start | bytes 1540
  91.5 2.4 %collective-permute-start.21 = (bf16[2,2,128,768]{3,2,1,0:T(8,128)(2,1)S(1)}, bf16[2,2,128,768]{3,2,1,0:T(8,128)(2,1)S(1)}, u32[]{:S(2)}, u32[]{:S(2)}) collective-permute-start(bf16[2,2,128,768]{3,2,1,0:T(8,128)(2,1)S(1)} %convolution_convert_fusion), channel_id=1, source_target_pairs={{0,8},{8,0},{16,24},{24,16},{1,9},{9,1},{17,25},{25,17},{2,10},{10... | collective-permute-start | bytes 2359304 | tf_op jit(solution)/shard_map/ppermute | solution.py:100
  91.8 6.4 %copy-start.24 = (s32[4]{0:T(128)S(1)}, s32[4]{0:T(128)}, u32[]{:S(2)}) copy-start(s32[4]{0:T(128)} %param.23) | copy-start | bytes 52
  94.6 11.2 %collective-permute-start.22 = (bf16[128,768]{1,0:T(8,128)(2,1)S(1)}, bf16[128,768]{1,0:T(8,128)(2,1)S(1)}, u32[]{:S(2)}, u32[]{:S(2)}) collective-permute-start(bf16[128,768]{1,0:T(8,128)(2,1)S(1)} %get-tuple-element.43), channel_id=1, source_target_pairs={{0,16},{8,24},{16,0},{24,8},{1,17},{9,25},{17,1},{25,9},{2,18},{10... | collective-permute-start | bytes 589832 | tf_op jit(solution)/shard_map/ppermute | solution.py:100
  96.1 9.7 %collective-permute-start.24 = (bf16[128,768]{1,0:T(8,128)(2,1)S(1)}, bf16[128,768]{1,0:T(8,128)(2,1)S(1)}, u32[]{:S(2)}, u32[]{:S(2)}) collective-permute-start(bf16[128,768]{1,0:T(8,128)(2,1)S(1)} %get-tuple-element.44), channel_id=1, source_target_pairs={{0,17},{1,16},{2,19},{3,18},{8,25},{9,24},{10,27},{11,26},{16,1},{... | collective-permute-start | bytes 589832 | tf_op jit(solution)/shard_map/ppermute | solution.py:100
  96.2 10.9 %collective-permute-start.23 = (bf16[128,768]{1,0:T(8,128)(2,1)S(1)}, bf16[128,768]{1,0:T(8,128)(2,1)S(1)}, u32[]{:S(2)}, u32[]{:S(2)}) collective-permute-start(bf16[128,768]{1,0:T(8,128)(2,1)S(1)} %fusion.33), channel_id=1, source_target_pairs={{0,1},{1,0},{2,3},{3,2},{4,5},{5,4},{6,7},{7,6},{8,9},{9,8},{10,11... | collective-permute-start | bytes 589832 | tf_op jit(solution)/shard_map/ppermute | solution.py:100
  98.5 9.4 %copy-start.7 = (f32[768]{0:T(1024)S(1)}, f32[768]{0:T(1024)}, u32[]{:S(2)}) copy-start(f32[768]{0:T(1024)} %param.18) | copy-start | bytes 9220
  107.6 11.9 %copy-start.15 = (s32[4]{0:T(128)S(1)}, s32[4]{0:T(128)}, u32[]{:S(2)}) copy-start(s32[4]{0:T(128)} %param.22) | copy-start | bytes 52
  107.7 11.9 %copy-start.9 = (s32[1024]{0:T(1024)S(1)}, s32[1024]{0:T(1024)}, u32[]{:S(2)}) copy-start(s32[1024]{0:T(1024)} %copy-done.8) | copy-start | bytes 12292
  107.7 15.4 %copy-start = (bf16[3,768,192]{1,2,0:T(8,128)(2,1)S(1)}, bf16[3,768,192]{1,2,0:T(8,128)(2,1)}, u32[]{:S(2)}) copy-start(bf16[3,768,192]{1,2,0:T(8,128)(2,1)} %param.19) | copy-start | bytes 2654212
  107.7 15.4 %copy-start.1 = (bf16[192,768]{1,0:T(8,128)(2,1)S(1)}, bf16[192,768]{1,0:T(8,128)(2,1)}, u32[]{:S(2)}) copy-start(bf16[192,768]{1,0:T(8,128)(2,1)} %refs_7_.1) | copy-start | bytes 884740
  108.0 7.7 %collective-permute-start.25 = (bf16[128,768]{1,0:T(8,128)(2,1)S(1)}, bf16[128,768]{1,0:T(8,128)(2,1)S(1)}, u32[]{:S(2)}, u32[]{:S(2)}) collective-permute-start(bf16[128,768]{1,0:T(8,128)(2,1)S(1)} %multiply_convert_fusion.1.refs_1_), channel_id=1, source_target_pairs={{0,16},{8,24},{16,0},{24,8},{1,17},{9,25},{17,1},{25,9},{2,18},{10... | collective-permute-start | bytes 589832 | tf_op jit(solution)/shard_map/ppermute | solution.py:100
  109.6 9.8 %collective-permute-start.26 = (bf16[128,768]{1,0:T(8,128)(2,1)S(1)}, bf16[128,768]{1,0:T(8,128)(2,1)S(1)}, u32[]{:S(2)}, u32[]{:S(2)}) collective-permute-start(bf16[128,768]{1,0:T(8,128)(2,1)S(1)} %multiply_convert_fusion.1.refs_1_), channel_id=1, source_target_pairs={{0,4},{4,0},{1,5},{5,1},{2,6},{6,2},{3,7},{7,3},{8,12},{12,8},{9,1... | collective-permute-start | bytes 589832 | tf_op jit(solution)/shard_map/ppermute | solution.py:100
  110.3 9.1 %collective-permute-start.27 = (bf16[128,768]{1,0:T(8,128)(2,1)S(1)}, bf16[128,768]{1,0:T(8,128)(2,1)S(1)}, u32[]{:S(2)}, u32[]{:S(2)}) collective-permute-start(bf16[128,768]{1,0:T(8,128)(2,1)S(1)} %multiply_convert_fusion.1.refs_1_), channel_id=1, source_target_pairs={{0,20},{4,16},{8,28},{12,24},{16,4},{20,0},{24,12},{28,8},{1,21},{... | collective-permute-start | bytes 589832 | tf_op jit(solution)/shard_map/ppermute | solution.py:100
  119.5 3.6 %collective-permute-start.28 = (bf16[4,128,768]{2,1,0:T(8,128)(2,1)S(1)}, bf16[4,128,768]{2,1,0:T(8,128)(2,1)S(1)}, u32[]{:S(2)}, u32[]{:S(2)}) collective-permute-start(bf16[4,128,768]{2,1,0:T(8,128)(2,1)S(1)} %pad_maximum_fusion.2), channel_id=1, source_target_pairs={{0,8},{8,0},{16,24},{24,16},{1,9},{9,1},{17,25},{25,17},{2,10},{10... | collective-permute-start | bytes 2359304 | tf_op jit(solution)/shard_map/ppermute | solution.py:100
  128.7 2.1 %collective-permute-start.29 = (bf16[2,512,192]{2,1,0:T(8,128)(2,1)S(1)}, bf16[2,512,192]{2,1,0:T(8,128)(2,1)S(1)}, u32[]{:S(2)}, u32[]{:S(2)}) collective-permute-start(bf16[2,512,192]{2,1,0:T(8,128)(2,1)S(1)} %get-tuple-element.26), channel_id=1, source_target_pairs={{0,8},{8,0},{16,24},{24,16},{1,9},{9,1},{17,25},{25,17},{2,10},{10... | collective-permute-start | bytes 1179656 | tf_op jit(solution)/shard_map/ppermute | solution.py:100
  130.9 8.7 %collective-permute-start.30 = (bf16[512,192]{1,0:T(8,128)(2,1)S(1)}, bf16[512,192]{1,0:T(8,128)(2,1)S(1)}, u32[]{:S(2)}, u32[]{:S(2)}) collective-permute-start(bf16[512,192]{1,0:T(8,128)(2,1)S(1)} %fusion.31), channel_id=1, source_target_pairs={{0,16},{8,24},{16,0},{24,8},{1,17},{9,25},{17,1},{25,9},{2,18},{10... | collective-permute-start | bytes 589832 | tf_op jit(solution)/shard_map/ppermute | solution.py:100
  (8 other events, 15.6 us)

commit v6 on v5

--- a/solution.py
+++ b/solution.py
@@ -66,19 +66,20 @@
         total = jnp.sum(weight, axis=1, keepdims=True)
         mixed = jnp.dot(weight.astype(jnp.bfloat16), value, preferred_element_type=jnp.float32)
         att = jnp.where(lane_head == h, mixed / total, att)
-    part = jnp.dot(att.astype(jnp.bfloat16), out_w_ref[...], preferred_element_type=jnp.float32)
+    part = jnp.dot(
+        out_w_ref[...], jnp.transpose(att).astype(jnp.bfloat16), preferred_element_type=jnp.float32
+    )
+    emb = jnp.transpose(emb_ref[...])
     for block, mask in enumerate(masks):
-        piece = part[block * own : (block + 1) * own]
+        piece = part[:, block * own : (block + 1) * own]
         if block == 0:
-            piece = piece + emb_ref[...]
-        at = pl.multiple_of((mask ^ sec_ref[0]) * own, own)
-        for j in range(part.shape[1] // width // 2):
-            low = piece[:, 2 * j * width : (2 * j + 1) * width]
-            high = piece[:, (2 * j + 1) * width : (2 * j + 2) * width]
-            keep_ref[j ^ side, pl.ds(at, own), :] = jnp.where(core == 0, low, high)
-            send_ref[j ^ side, pl.ds(at, own), :] = jnp.where(core == 0, high, low).astype(
-                send_ref.dtype
-            )
+            piece = piece + emb
+        at = pl.ds(pl.multiple_of((mask ^ sec_ref[0]) * own, own), own)
+        for j in range(part.shape[0] // width // 2):
+            low = piece[2 * j * width : (2 * j + 1) * width]
+            high = piece[(2 * j + 1) * width : (2 * j + 2) * width]
+            keep_ref[j ^ side, :, at] = jnp.where(core == 0, low, high)
+            send_ref[j ^ side, :, at] = jnp.where(core == 0, high, low).astype(send_ref.dtype)
 
 
 def build(n_sec, n_seq, n_dp):
@@ -177,16 +178,39 @@
         proj_blocks = gather_section(w_proj)
         proj = jnp.concatenate(proj_blocks, axis=0)
 
+        if n_seq == 2:
+            masks = (0, 2, 1, 3)
+            span = jnp.arange(own_rows, dtype=jnp.int32)
+            k_idx = jnp.concatenate(
+                [(seq_at ^ y) * tokens + (sec ^ m) * own_rows + span for y in (0, 1) for m in masks]
+            )
+            q_idx = k_idx[:tokens]
+        else:
+            k_idx = jnp.arange(n_seq * tokens, dtype=jnp.int32)
+            q_idx = seq_at * tokens + jnp.arange(tokens, dtype=jnp.int32)
+        count = k_idx.shape[0]
+        local_heads = seg_len.shape[0]
+        heads = sec * local_heads + jnp.arange(local_heads, dtype=jnp.int32)
+
+        def codes(index):
+            slide, pos = slide_place(lengths[0], index)
+            block = slide[None, :] * count + pos[None, :] // seg_len[:, None]
+            return block, pos[None, :] % rate[:, None] == (heads % rate)[:, None]
+
+        k_block, picked = codes(k_idx)
+        k_code = jnp.where(picked, k_block, -1)
+        q_code = codes(q_idx)[0].T
+
         if ordered:
             g = {(0, 0): pair_same, (0, 2): rotate(pair_same, 2)}
-            g[0, 1] = rotate(after(pair_other, g[0, 2]), 1)
-            g[0, 3] = rotate(after(pair_other, g[0, 2]), 3)
+            d = {(0, 0): down_same, (1, 0): flip(down_same, seq=1)}
+            g[0, 1] = rotate(after(pair_other, g[0, 2], d[1, 0]), 1)
+            g[0, 3] = rotate(after(pair_other, g[0, 2], d[1, 0]), 3)
             g[1, 0], g[1, 2], g[1, 1] = (flip(g[0, k], seq=1) for k in (0, 2, 1))
             g[1, 3] = flip(after(g[0, 3], normed), seq=1)
             gate_up = place_rows(g)
-            d = {(0, 0): down_same, (0, 2): rotate(after(down_same, g[0, 1]), 2)}
-            d[1, 0] = flip(down_same, seq=1)
-            there = [row_blocks[1], row_blocks[3], proj_blocks[1], proj_blocks[3], d[1, 0]]
+            d[0, 2] = rotate(after(down_same, g[0, 1], proj_blocks[1], proj_blocks[3]), 2)
+            there = [row_blocks[1], row_blocks[3], k_code, q_code]
             d[0, 1] = rotate(after(down_other, d[0, 2], *there), 1)
             d[0, 3] = rotate(after(down_other, d[0, 2], *there), 3)
             for k in (2, 1, 3):
@@ -244,7 +268,6 @@
         )
         slide_normed = layer_norm(emb, slide_gain).astype(jnp.bfloat16)
 
-        span = jnp.arange(own_rows, dtype=jnp.int32)
         if n_seq == 2:
             near = [
                 flip(slide_normed, section=2),
@@ -252,28 +275,8 @@
                 flip(slide_normed, section=2, seq=1),
             ]
             from_core = flip(jnp.stack([slide_normed] + near), section=1)
-            masks = (0, 2, 1, 3)
-            k_idx = jnp.concatenate(
-                [(seq_at ^ y) * tokens + (sec ^ m) * own_rows + span for y in (0, 1) for m in masks]
-            )
-            q_idx = k_idx[:tokens]
         else:
             keys = lax.all_gather(slide_normed, ("seq", "section"), axis=0, tiled=True)
-            k_idx = jnp.arange(keys.shape[0], dtype=jnp.int32)
-            q_idx = seq_at * tokens + jnp.arange(tokens, dtype=jnp.int32)
-
-        count = k_idx.shape[0]
-        local_heads = seg_len.shape[0]
-        heads = sec * local_heads + jnp.arange(local_heads, dtype=jnp.int32)
-
-        def codes(index):
-            slide, pos = slide_place(lengths[0], index)
-            block = slide[None, :] * count + pos[None, :] // seg_len[:, None]
-            return block, pos[None, :] % rate[:, None] == (heads % rate)[:, None]
-
-        k_block, picked = codes(k_idx)
-        k_code = jnp.where(picked, k_block, -1)
-        q_code = codes(q_idx)[0].T
 
         width = w_qkv.shape[2]
         qkv = jnp.swapaxes(w_qkv, 1, 2)
@@ -282,8 +285,8 @@
             keep, send = pl.pallas_call(
                 lambda *refs: attend_kernel(*refs, heads=local_heads, masks=masks),
                 out_shape=[
-                    jax.ShapeDtypeStruct((2, tokens, width), jnp.float32),
-                    jax.ShapeDtypeStruct((2, tokens, width), jnp.bfloat16),
+                    jax.ShapeDtypeStruct((2, width, tokens), jnp.float32),
+                    jax.ShapeDtypeStruct((2, width, tokens), jnp.bfloat16),
                 ],
                 in_specs=[pl.BlockSpec(memory_space=pltpu.SMEM)] + [vmem] * 10,
                 out_specs=[vmem] * 2,
@@ -293,7 +296,7 @@
                     bytes_accessed=8 * 2**20,
                     transcendentals=local_heads * tokens * count,
                 ),
-            )(sec[None], slide_normed, *near, from_core, qkv, w_out, emb, q_code, k_code)
+            )(sec[None], slide_normed, *near, from_core, qkv, w_out.T, emb, q_code, k_code)
         else:
 
             def by_head(x, matrix):
@@ -319,12 +322,12 @@
             parts = jnp.dot(att, w_out, preferred_element_type=jnp.float32)
             old = lax.dynamic_slice_in_dim(parts, sec * own_rows, own_rows, 0)
             parts = lax.dynamic_update_slice_in_dim(parts, old + emb, sec * own_rows, 0)
-            parts = jnp.stack(absolute(jnp.split(parts, n_sec, axis=1)))
+            parts = jnp.stack(absolute(jnp.split(parts.T, n_sec, axis=0)))
             keep, send = parts[0::2], parts[1::2].astype(jnp.bfloat16)
 
         kept = keep + flip(send, section=1).astype(jnp.float32)
         out = kept[0] + flip(kept[1].astype(jnp.bfloat16), section=2).astype(jnp.float32)
-        return out.astype(jnp.bfloat16)[None]
+        return out.astype(jnp.bfloat16).T[None]
 
     return per_device
 

time: 141 us -> 147 us (1.043)
  matrix products: 7.91 us -> 13.6 us
  waiting for transfers between devices: 64.9 us -> 62.2 us
  other arithmetic: 12.7 us -> 15.3 us
  local copies, waits for them, and re-layouts: 10.2 us -> 12.8 us
  starting transfers between devices: 38.3 us -> 36.3 us
    ppermute x6, waiting for transfers between devices: 26.5 us -> 17.4 us  [rotate(): return lax.ppermute(x, 'dp', [(i, (i + k) % n_dp) for i in range(n_dp)])]
    ppermute x25, waiting for transfers between devices: 38.3 us -> 44.8 us  [flip(): return lax.ppermute(x, names if len(names) > 1 else names[0], pairs)]
    dot_general x2, matrix products: 1.22 us -> 4.78 us  [project(): lax.dot_general(x, folded, (((x.ndim - 1,), (1,)), ((), ())), preferred_e...]
    dynamic_update_slice x14, local copies, waits for them, and re-layouts: 3.36 us -> 5.27 us  [place_rows(): whole = lax.dynamic_update_slice(whole, block, (0, row_of(y, k, rows), 0))]
    concatenate x1, other arithmetic: 0.08 us -> 1.98 us  [per_device(): both = jnp.concatenate([mine, beside], axis=0)]
    ppermute x6, starting transfers between devices: 15.2 us -> 13.5 us  [rotate(): return lax.ppermute(x, 'dp', [(i, (i + k) % n_dp) for i in range(n_dp)])]
    unnamed x53 -> x34, local copies, waits for them, and re-layouts: 2.79 us -> 3.5 us
  transfers between devices with their start and end apart: 31 -> 31, of which waited for: 15 -> 16; matrix products, arithmetic and copies ran while one was open for 17% -> 19% of each run, Pallas kernels for 0% -> 0%
where the time goes in v6:
time: 147 us; the launch traced here: 146 us
  waiting for transfers between devices  62.2 us (42%)
  starting transfers between devices  36.3 us (25%)
  other arithmetic  15.3 us (10%)
  matrix products  13.6 us (9%)
  local copies, waits for them, and re-layouts  12.8 us (9%)
  Pallas kernels  5.3 us (4%)
    ppermute x25, waiting for transfers between devices, flip(): return lax.ppermute(x, names if len(names) > 1 else names[0], pairs)  44.8 us
    ppermute x25, starting transfers between devices, flip(): return lax.ppermute(x, names if len(names) > 1 else names[0], pairs)  22.8 us
    ppermute x6, waiting for transfers between devices, rotate(): return lax.ppermute(x, 'dp', [(i, (i + k) % n_dp) for i in range(n_dp)])  17.4 us
    ppermute x6, starting transfers between devices, rotate(): return lax.ppermute(x, 'dp', [(i, (i + k) % n_dp) for i in range(n_dp)])  13.5 us
    pallas_call x1, Pallas kernels, per_device(): pl.pallas_call(lambda *refs: attend_kernel(*refs, heads=local_heads, mask...  5.3 us
    dynamic_update_slice x14, local copies, waits for them, and re-layouts, place_rows(): whole = lax.dynamic_update_slice(whole, block, (0, row_of(y, k, rows), 0))  5.27 us
    dot_general x2, matrix products, project(): lax.dot_general(x, folded, (((x.ndim - 1,), (1,)), ((), ())), preferred_e...  4.78 us
    unnamed x34, local copies, waits for them, and re-layouts  3.5 us
  transfers between devices with their start and end apart: 31, of which 16 were waited for; matrix products, arithmetic and copies ran while one was open for 19% of the time, Pallas kernels for 0%

profile of v6, /device:TPU:0, one launch (start us, length us, event | category | flops | bytes accessed | tf_op | source)
XLA Modules:
  0.0 146.2 jit_solution(2140819220953278532)
XLA Ops:
  0.0 2.1 %fusion.19 = (bf16[2,192,512]{2,1,0:T(8,128)(2,1)S(1)}, bf16[2,192,512]{2,1,0:T(8,128)(2,1)}) fusion(s32[]{:T(128)S(6)} %select_n.251, bf16[1,192,1024]{2,1,0:T(8,128)(2,1)} %bitcast.101, bf16[1,192,1024]{2,1,0:T(8,128)(2,1)} %bitcast.102, s32[]{:T(128)S(6)} %select_n.260), kind=kLoop, calls=%fused_computation.35 | loop fusion | flops 1572864 | bytes 1572872 | tf_op jit(solution)/shard_map/stack | solution.py:166
  2.1 4.0 %collective-permute-start.7 = (bf16[2,192,512]{2,1,0:T(8,128)(2,1)S(1)}, bf16[2,192,512]{2,1,0:T(8,128)(2,1)}, u32[]{:S(2)}, u32[]{:S(2)}) collective-permute-start(bf16[2,192,512]{2,1,0:T(8,128)(2,1)S(1)} %get-tuple-element.41), channel_id=1, source_target_pairs={{0,2},{1,3},{2,0},{3,1},{4,6},{5,7},{6,4},{7,5},{8,10},{9,11},{10,... | collective-permute-start | bytes 1179656 | tf_op jit(solution)/shard_map/ppermute | solution.py:104
  6.2 1.5 %collective-permute-start.11 = (bf16[2,192,512]{2,1,0:T(8,128)(2,1)S(1)}, bf16[2,192,512]{2,1,0:T(8,128)(2,1)}, u32[]{:S(2)}, u32[]{:S(2)}) collective-permute-start(bf16[2,192,512]{2,1,0:T(8,128)(2,1)S(1)} %get-tuple-element.41), channel_id=1, source_target_pairs={{0,4},{4,0},{1,5},{5,1},{2,6},{6,2},{3,7},{7,3},{8,12},{12,8},{9,1... | collective-permute-start | bytes 1179656 | tf_op jit(solution)/shard_map/ppermute | solution.py:101
  7.7 1.8 %dynamic-slice_bitcast_fusion.1 = (bf16[1,192,512]{2,1,0:T(8,128)(2,1)}, bf16[1,192,512]{2,1,0:T(8,128)(2,1)}) fusion(bf16[1024,192]{0,1:T(8,128)(2,1)} %param.16, s32[]{:T(128)S(6)} %select_n.260, s32[]{:T(128)S(6)} %select_n.251), kind=kLoop, calls=%fused_computation.66 | loop fusion | bytes 786440 | tf_op jit(solution)/shard_map/dynamic_slice | solution.py:164
  10.0 1.6 %collective-permute-start = (bf16[512,384]{1,0:T(8,128)(2,1)S(1)}, bf16[512,384]{1,0:T(8,128)(2,1)}, u32[]{:S(2)}, u32[]{:S(2)}) collective-permute-start(bf16[512,384]{1,0:T(8,128)(2,1)S(1)} %bitcast.98), channel_id=1, source_target_pairs={{0,1},{1,0},{2,3},{3,2},{4,5},{5,4},{6,7},{7,6},{8,9},{9,8},{10,11... | collective-permute-start | bytes 1179656 | tf_op jit(solution)/shard_map/ppermute | solution.py:101
  11.6 1.5 %collective-permute-start.4 = (bf16[384,768]{1,0:T(8,128)(2,1)}, bf16[384,768]{1,0:T(8,128)(2,1)}, u32[]{:S(2)}, u32[]{:S(2)}) collective-permute-start(bf16[384,768]{1,0:T(8,128)(2,1)} %param.17), channel_id=1, source_target_pairs={{0,16},{8,24},{16,0},{24,8},{1,17},{9,25},{17,1},{25,9},{2,18},{10... | collective-permute-start | bytes 1769480 | tf_op jit(solution)/shard_map/ppermute | solution.py:101
  13.8 2.7 %fusion.29.refs_9_ = s32[512,4]{1,0:T(8,128)S(1)} fusion(s32[4]{0:T(128)S(1)} %copy-done.12, s32[512]{0:T(512)S(1)} %get-tuple-element.38, s32[4]{0:T(128)S(1)} %sign.88, s32[512]{0:T(512)S(1)} %broadcast_multiply_fusion.2, s32[512]{0:T(512)S(1)} %get-tuple-element.37), kind=kLoop, calls=%fused_computation.50 | loop fusion | flops 16384 | bytes 14368 | tf_op jit(solution)/shard_map/add | solution.py:197
  17.3 1.1 constant_dynamic-update-slice_fusion.3
  18.4 2.7 %collective-permute-done.8 = bf16[1,192,512]{2,1,0:T(8,128)(2,1)} collective-permute-done((bf16[1,192,512]{2,1,0:T(8,128)(2,1)}, bf16[1,192,512]{2,1,0:T(8,128)(2,1)}, u32[]{:S(2)}, u32[]{:S(2)}) %collective-permute-start.8) | collective-permute-done | bytes 196640 | tf_op jit(solution)/shard_map/ppermute | solution.py:101
  21.1 2.9 %collective-permute-done.7 = bf16[2,192,512]{2,1,0:T(8,128)(2,1)} collective-permute-done((bf16[2,192,512]{2,1,0:T(8,128)(2,1)S(1)}, bf16[2,192,512]{2,1,0:T(8,128)(2,1)}, u32[]{:S(2)}, u32[]{:S(2)}) %collective-permute-start.7) | collective-permute-done | bytes 393248 | tf_op jit(solution)/shard_map/ppermute | solution.py:104
  24.5 3.3 %collective-permute-start.10 = (bf16[2,192,512]{2,1,0:T(8,128)(2,1)}, bf16[2,192,512]{2,1,0:T(8,128)(2,1)}, u32[]{:S(2)}, u32[]{:S(2)}) collective-permute-start(bf16[2,192,512]{2,1,0:T(8,128)(2,1)} %get-tuple-element.19), channel_id=1, source_target_pairs={{0,3},{1,0},{2,1},{3,2},{4,7},{5,4},{6,5},{7,6},{8,11},{9,8},{10,9... | collective-permute-start | bytes 1179656 | tf_op jit(solution)/shard_map/ppermute | solution.py:104
  27.9 2.0 %pad_maximum_fusion.1 = bf16[1024,384]{1,0:T(8,128)(2,1)} fusion(bf16[512,384]{1,0:T(8,128)(2,1)} %collective-permute-done, bf16[512,384]{1,0:T(8,128)(2,1)S(1)} %bitcast.99), kind=kLoop, calls=%fused_computation.25 | loop fusion | flops 1572864 | bytes 1572864 | tf_op jit(solution)/shard_map/concatenate | solution.py:173
  29.8 1.5 %collective-permute-start.1 = (bf16[1024,384]{1,0:T(8,128)(2,1)}, bf16[1024,384]{1,0:T(8,128)(2,1)}, u32[]{:S(2)}, u32[]{:S(2)}) collective-permute-start(bf16[1024,384]{1,0:T(8,128)(2,1)} %pad_maximum_fusion.1), channel_id=1, source_target_pairs={{0,16},{8,24},{16,0},{24,8},{1,17},{9,25},{17,1},{25,9},{2,18},{10... | collective-permute-start | bytes 2359304 | tf_op jit(solution)/shard_map/ppermute | solution.py:101
  31.7 1.6 %collective-permute-start.12 = (bf16[2,192,512]{2,1,0:T(8,128)(2,1)}, bf16[2,192,512]{2,1,0:T(8,128)(2,1)S(1)}, u32[]{:S(2)}, u32[]{:S(2)}) collective-permute-start(bf16[2,192,512]{2,1,0:T(8,128)(2,1)} %collective-permute-done.7), channel_id=1, source_target_pairs={{0,4},{4,0},{1,5},{5,1},{2,6},{6,2},{3,7},{7,3},{8,12},{12,8},{9,1... | collective-permute-start | bytes 1179656 | tf_op jit(solution)/shard_map/ppermute | solution.py:101
  33.2 4.9 %collective-permute-done.9 = bf16[2,192,512]{2,1,0:T(8,128)(2,1)} collective-permute-done((bf16[2,192,512]{2,1,0:T(8,128)(2,1)}, bf16[2,192,512]{2,1,0:T(8,128)(2,1)}, u32[]{:S(2)}, u32[]{:S(2)}) %collective-permute-start.9) | collective-permute-done | bytes 393248 | tf_op jit(solution)/shard_map/ppermute | solution.py:104
  38.1 6.2 %collective-permute-done.10 = bf16[2,192,512]{2,1,0:T(8,128)(2,1)} collective-permute-done((bf16[2,192,512]{2,1,0:T(8,128)(2,1)}, bf16[2,192,512]{2,1,0:T(8,128)(2,1)}, u32[]{:S(2)}, u32[]{:S(2)}) %collective-permute-start.10) | collective-permute-done | bytes 393248 | tf_op jit(solution)/shard_map/ppermute | solution.py:104
  47.4 1.6 %collective-permute-start.13 = (bf16[2,192,512]{2,1,0:T(8,128)(2,1)}, bf16[2,192,512]{2,1,0:T(8,128)(2,1)S(1)}, u32[]{:S(2)}, u32[]{:S(2)}) collective-permute-start(bf16[2,192,512]{2,1,0:T(8,128)(2,1)} %collective-permute-done.9), channel_id=1, source_target_pairs={{0,4},{4,0},{1,5},{5,1},{2,6},{6,2},{3,7},{7,3},{8,12},{12,8},{9,1... | collective-permute-start | bytes 1179656 | tf_op jit(solution)/shard_map/ppermute | solution.py:101
  50.4 1.8 %collective-permute-start.15 = (bf16[1,192,512]{2,1,0:T(8,128)(2,1)}, bf16[1,192,512]{2,1,0:T(8,128)(2,1)S(1)}, u32[]{:S(2)}, u32[]{:S(2)}) collective-permute-start(bf16[1,192,512]{2,1,0:T(8,128)(2,1)} %get-tuple-element.21), channel_id=1, source_target_pairs={{0,2},{1,3},{2,0},{3,1},{4,6},{5,7},{6,4},{7,5},{8,10},{9,11},{10,... | collective-permute-start | bytes 589832 | tf_op jit(solution)/shard_map/ppermute | solution.py:104
  52.2 1.2 constant_dynamic-update-slice_fusion.1
  53.4 5.8 %collective-permute-done.13 = bf16[2,192,512]{2,1,0:T(8,128)(2,1)S(1)} collective-permute-done((bf16[2,192,512]{2,1,0:T(8,128)(2,1)}, bf16[2,192,512]{2,1,0:T(8,128)(2,1)S(1)}, u32[]{:S(2)}, u32[]{:S(2)}) %collective-permute-start.13) | collective-permute-done | bytes 393248 | tf_op jit(solution)/shard_map/ppermute | solution.py:101
  59.3 3.5 %collective-permute-done.15 = bf16[1,192,512]{2,1,0:T(8,128)(2,1)S(1)} collective-permute-done((bf16[1,192,512]{2,1,0:T(8,128)(2,1)}, bf16[1,192,512]{2,1,0:T(8,128)(2,1)S(1)}, u32[]{:S(2)}, u32[]{:S(2)}) %collective-permute-start.15) | collective-permute-done | bytes 196640 | tf_op jit(solution)/shard_map/ppermute | solution.py:104
  64.5 3.8 %collective-permute-start.17 = (bf16[1,192,512]{2,1,0:T(8,128)(2,1)S(1)}, bf16[1,192,512]{2,1,0:T(8,128)(2,1)S(1)}, u32[]{:S(2)}, u32[]{:S(2)}) collective-permute-start(bf16[1,192,512]{2,1,0:T(8,128)(2,1)S(1)} %copy-done.9), channel_id=1, source_target_pairs={{0,3},{1,0},{2,1},{3,2},{4,7},{5,4},{6,5},{7,6},{8,11},{9,8},{10,9... | collective-permute-start | bytes 589832 | tf_op jit(solution)/shard_map/ppermute | solution.py:104
  68.3 2.9 %convert_reduce_fusion = (f32[1024]{0:T(1024)S(1)}, bf16[1024,1536]{1,0:T(8,128)(2,1)S(1)}) fusion(bf16[1024,384]{1,0:T(8,128)(2,1)S(1)} %collective-permute-done.3, bf16[1024,384]{1,0:T(8,128)(2,1)} %collective-permute-done.1, bf16[1024,384]{1,0:T(8,128)(2,1)S(1)} %collective-permute-done.2, bf16[512,384]{1,0:T(8,128)(2,1)} %collective-permute-done, ...), kind=kLoop, calls=%fused_computation.1 | loop fusion | flops 18873344 | bytes 6295552 | tf_op jit(solution)/shard_map/reduce_sum | solution.py:15
  73.2 1.6 %collective-permute-start.14 = (bf16[2,192,512]{2,1,0:T(8,128)(2,1)}, bf16[2,192,512]{2,1,0:T(8,128)(2,1)S(1)}, u32[]{:S(2)}, u32[]{:S(2)}) collective-permute-start(bf16[2,192,512]{2,1,0:T(8,128)(2,1)} %collective-permute-done.10), channel_id=1, source_target_pairs={{0,4},{4,0},{1,5},{5,1},{2,6},{6,2},{3,7},{7,3},{8,12},{12,8},{9,1... | collective-permute-start | bytes 1179656 | tf_op jit(solution)/shard_map/ppermute | solution.py:101
  75.7 1.2 collective-permute-start.20
  77.0 8.5 %collective-permute-done.14 = bf16[2,192,512]{2,1,0:T(8,128)(2,1)S(1)} collective-permute-done((bf16[2,192,512]{2,1,0:T(8,128)(2,1)}, bf16[2,192,512]{2,1,0:T(8,128)(2,1)S(1)}, u32[]{:S(2)}, u32[]{:S(2)}) %collective-permute-start.14) | collective-permute-done | bytes 393248 | tf_op jit(solution)/shard_map/ppermute | solution.py:101
  85.6 1.8 %fusion.6 = f32[1024,512]{1,0:T(8,128)S(1)} fusion(bf16[1024,1536]{1,0:T(8,128)(2,1)S(1)} %fusion.4, bf16[2,1536,512]{2,1,0:T(8,128)(2,1)S(1)} %constant_dynamic-update-slice_fusion.5), kind=kOutput, calls=%fused_computation.12 | convolution fusion | flops 1610612736 | bytes 6815744 | tf_op jit(solution)/shard_map/dot_general | solution.py:222
  87.4 2.0 %multiply_convert_fusion = bf16[1024,512]{1,0:T(8,128)(2,1)S(1)} fusion(f32[1024,512]{1,0:T(8,128)S(1)} %fusion.6, bf16[1024,1536]{1,0:T(8,128)(2,1)S(1)} %fusion.4, bf16[2,1536,512]{2,1,0:T(8,128)(2,1)S(1)} %constant_dynamic-update-slice_fusion.5), kind=kOutput, calls=%fused_computation.8 | convolution fusion | flops 1613758464 | bytes 7864320 | tf_op jit(solution)/shard_map/dot_general | solution.py:223
  89.4 1.4 fusion.61
  91.6 1.3 fusion.10
  92.9 2.6 %convolution_convert_fusion = bf16[2,2,128,768]{3,2,1,0:T(8,128)(2,1)} fusion(bf16[768,512,1,1]{1,0,3,2:T(8,128)(2,1)} %fusion.10, bf16[2,2,2,128,512]{4,3,2,1,0:T(8,128)(2,1)S(1)} %bitcast.103, s32[]{:T(128)S(6)} %select_n.291), kind=kOutput, calls=%fused_computation.15 | convolution fusion | flops 403046400 | bytes 2097156 | tf_op jit(solution)/shard_map/dot_general | solution.py:245
  95.5 2.6 %collective-permute-done.21 = bf16[2,2,128,768]{3,2,1,0:T(8,128)(2,1)} collective-permute-done((bf16[2,2,128,768]{3,2,1,0:T(8,128)(2,1)}, bf16[2,2,128,768]{3,2,1,0:T(8,128)(2,1)}, u32[]{:S(2)}, u32[]{:S(2)}) %collective-permute-start.21) | collective-permute-done | bytes 786464 | tf_op jit(solution)/shard_map/ppermute | solution.py:101
  98.2 2.1 %convert_add_fusion = f32[2,2,128,768]{3,2,1,0:T(8,128)S(1)} fusion(bf16[2,2,128,768]{3,2,1,0:T(8,128)(2,1)} %collective-permute-done.21, bf16[768,512,1,1]{1,0,3,2:T(8,128)(2,1)} %fusion.10, bf16[2,2,2,128,512]{4,3,2,1,0:T(8,128)(2,1)} %bitcast.104, s32[]{:T(128)S(6)} %select_n.282), kind=kOutput, calls=%fused_computation.13 | convolution fusion | flops 403439616 | bytes 3670020 | tf_op jit(solution)/shard_map/dot_general | solution.py:245
  101.3 1.6 %collective-permute-start.22 = (bf16[128,768]{1,0:T(8,128)(2,1)}, bf16[128,768]{1,0:T(8,128)(2,1)}, u32[]{:S(2)}, u32[]{:S(2)}) collective-permute-start(bf16[128,768]{1,0:T(8,128)(2,1)} %get-tuple-element.43), channel_id=1, source_target_pairs={{0,16},{8,24},{16,0},{24,8},{1,17},{9,25},{17,1},{25,9},{2,18},{10... | collective-permute-start | bytes 589832 | tf_op jit(solution)/shard_map/ppermute | solution.py:101
  103.6 1.9 %collective-permute-start.23 = (bf16[128,768]{1,0:T(8,128)(2,1)}, bf16[128,768]{1,0:T(8,128)(2,1)}, u32[]{:S(2)}, u32[]{:S(2)}) collective-permute-start(bf16[128,768]{1,0:T(8,128)(2,1)} %fusion.31), channel_id=1, source_target_pairs={{0,1},{1,0},{2,3},{3,2},{4,5},{5,4},{6,7},{7,6},{8,9},{9,8},{10,11... | collective-permute-start | bytes 589832 | tf_op jit(solution)/shard_map/ppermute | solution.py:101
  105.6 7.2 %collective-permute-done.22 = bf16[128,768]{1,0:T(8,128)(2,1)} collective-permute-done((bf16[128,768]{1,0:T(8,128)(2,1)}, bf16[128,768]{1,0:T(8,128)(2,1)}, u32[]{:S(2)}, u32[]{:S(2)}) %collective-permute-start.22) | collective-permute-done | bytes 196640 | tf_op jit(solution)/shard_map/ppermute | solution.py:101
  112.8 1.2 collective-permute-done.23
  114.0 1.9 %fusion.60 = (f32[128]{0:T(128)S(1)}, f32[128,768]{1,0:T(8,128)S(1)}) fusion(bf16[128,768]{1,0:T(8,128)(2,1)} %collective-permute-done.24, bf16[128,768]{1,0:T(8,128)(2,1)} %collective-permute-done.23, bf16[128,768]{1,0:T(8,128)(2,1)} %collective-permute-done.22, f32[2,2,128,768]{3,2,1,0:T(8,128)} %copy-done.4, s32[]{:T(128)S(6)} %select_n.293, ...), kind=kOutput, calls=%fused_computation.141 | convolution fusion | flops 302776192 | bytes 4129288 | tf_op jit(solution)/shard_map/dot_general | solution.py:257
  116.3 1.6 %collective-permute-start.25 = (bf16[128,768]{1,0:T(8,128)(2,1)S(1)}, bf16[128,768]{1,0:T(8,128)(2,1)S(1)}, u32[]{:S(2)}, u32[]{:S(2)}) collective-permute-start(bf16[128,768]{1,0:T(8,128)(2,1)S(1)} %multiply_convert_fusion.1.refs_1_), channel_id=1, source_target_pairs={{0,16},{8,24},{16,0},{24,8},{1,17},{9,25},{17,1},{25,9},{2,18},{10... | collective-permute-start | bytes 589832 | tf_op jit(solution)/shard_map/ppermute | solution.py:101
  117.9 1.5 %collective-permute-start.26 = (bf16[128,768]{1,0:T(8,128)(2,1)S(1)}, bf16[128,768]{1,0:T(8,128)(2,1)S(1)}, u32[]{:S(2)}, u32[]{:S(2)}) collective-permute-start(bf16[128,768]{1,0:T(8,128)(2,1)S(1)} %multiply_convert_fusion.1.refs_1_), channel_id=1, source_target_pairs={{0,4},{4,0},{1,5},{5,1},{2,6},{6,2},{3,7},{7,3},{8,12},{12,8},{9,1... | collective-permute-start | bytes 589832 | tf_op jit(solution)/shard_map/ppermute | solution.py:101
  120.0 4.0 %collective-permute-done.25.refs_2_ = bf16[128,768]{1,0:T(8,128)(2,1)S(1)} collective-permute-done((bf16[128,768]{1,0:T(8,128)(2,1)S(1)}, bf16[128,768]{1,0:T(8,128)(2,1)S(1)}, u32[]{:S(2)}, u32[]{:S(2)}) %collective-permute-start.25) | collective-permute-done | bytes 196640 | tf_op jit(solution)/shard_map/ppermute | solution.py:101
  124.0 3.8 %collective-permute-done.26.refs_3_ = bf16[128,768]{1,0:T(8,128)(2,1)S(1)} collective-permute-done((bf16[128,768]{1,0:T(8,128)(2,1)S(1)}, bf16[128,768]{1,0:T(8,128)(2,1)S(1)}, u32[]{:S(2)}, u32[]{:S(2)}) %collective-permute-start.26) | collective-permute-done | bytes 196640 | tf_op jit(solution)/shard_map/ppermute | solution.py:101
  128.7 1.1 copy.14
  129.9 1.4 collective-permute-done.28.refs_5_
  131.2 5.3 %shard_map.118 = (f32[2,192,512]{2,1,0:T(8,128)S(1)}, bf16[2,192,512]{2,1,0:T(8,128)(2,1)S(1)}) custom-call(s32[1]{0:T(128)} %bitcast.refs_0_, bf16[128,768]{1,0:T(8,128)(2,1)S(1)} %multiply_convert_fusion.1.refs_1_, bf16[128,768]{1,0:T(8,128)(2,1)S(1)} %collective-permute-done.25.refs_2_, bf16[128,768]{1,0:T(8,128)(2,1)S(1)} %collective-permute-done.26.refs_3_, ...), custom_call_target="tpu_custom_call" | custom-call | flops 2516582400 | bytes 8388608 | tf_op jit(solution)/shard_map/pallas_call | solution.py:285
  136.7 1.6 %collective-permute-done.29 = bf16[2,192,512]{2,1,0:T(8,128)(2,1)S(1)} collective-permute-done((bf16[2,192,512]{2,1,0:T(8,128)(2,1)S(1)}, bf16[2,192,512]{2,1,0:T(8,128)(2,1)S(1)}, u32[]{:S(2)}, u32[]{:S(2)}) %collective-permute-start.29) | collective-permute-done | bytes 393248 | tf_op jit(solution)/shard_map/ppermute | solution.py:101
  138.5 1.2 collective-permute-start.30
  139.7 5.8 %collective-permute-done.30 = bf16[192,512]{1,0:T(8,128)(2,1)S(1)} collective-permute-done((bf16[192,512]{1,0:T(8,128)(2,1)S(1)}, bf16[192,512]{1,0:T(8,128)(2,1)S(1)}, u32[]{:S(2)}, u32[]{:S(2)}) %collective-permute-start.30) | collective-permute-done | bytes 196640 | tf_op jit(solution)/shard_map/ppermute | solution.py:101
  (127 shorter events, 17.3 us)
Async XLA Ops:
  0.0 10.0 %copy-start.5 = (bf16[1,512,384]{2,1,0:T(8,128)(2,1)S(1)}, bf16[1,512,384]{2,1,0:T(8,128)(2,1)}, u32[]{:S(2)}) copy-start(bf16[1,512,384]{2,1,0:T(8,128)(2,1)} %param.12) | copy-start | bytes 1179652
  0.0 13.1 %copy-start.13 = (s32[1,3]{1,0:T(1,128)S(1)}, s32[1,3]{1,0:T(1,128)}, u32[]{:S(2)}) copy-start(s32[1,3]{1,0:T(1,128)} %param.21) | copy-start | bytes 40
  0.0 13.4 %copy-start.12 = (s32[4]{0:T(128)S(1)}, s32[4]{0:T(128)}, u32[]{:S(2)}) copy-start(s32[4]{0:T(128)} %param.22) | copy-start | bytes 52
  0.0 13.6 %copy-start.14 = (s32[4]{0:T(128)S(1)}, s32[4]{0:T(128)}, u32[]{:S(2)}) copy-start(s32[4]{0:T(128)} %param.23) | copy-start | bytes 52
  0.0 17.2 %copy-start.11 = (f32[1536]{0:T(1024)S(1)}, f32[1536]{0:T(1024)}, u32[]{:S(2)}) copy-start(f32[1536]{0:T(1024)} %param.13) | copy-start | bytes 18436
  2.1 21.8 %collective-permute-start.7 = (bf16[2,192,512]{2,1,0:T(8,128)(2,1)S(1)}, bf16[2,192,512]{2,1,0:T(8,128)(2,1)}, u32[]{:S(2)}, u32[]{:S(2)}) collective-permute-start(bf16[2,192,512]{2,1,0:T(8,128)(2,1)S(1)} %get-tuple-element.41), channel_id=1, source_target_pairs={{0,2},{1,3},{2,0},{3,1},{4,6},{5,7},{6,4},{7,5},{8,10},{9,11},{10,... | collective-permute-start | bytes 1179656 | tf_op jit(solution)/shard_map/ppermute | solution.py:104
  6.2 41.2 %collective-permute-start.11 = (bf16[2,192,512]{2,1,0:T(8,128)(2,1)S(1)}, bf16[2,192,512]{2,1,0:T(8,128)(2,1)}, u32[]{:S(2)}, u32[]{:S(2)}) collective-permute-start(bf16[2,192,512]{2,1,0:T(8,128)(2,1)S(1)} %get-tuple-element.41), channel_id=1, source_target_pairs={{0,4},{4,0},{1,5},{5,1},{2,6},{6,2},{3,7},{7,3},{8,12},{12,8},{9,1... | collective-permute-start | bytes 1179656 | tf_op jit(solution)/shard_map/ppermute | solution.py:101
  9.5 11.6 %collective-permute-start.8 = (bf16[1,192,512]{2,1,0:T(8,128)(2,1)}, bf16[1,192,512]{2,1,0:T(8,128)(2,1)}, u32[]{:S(2)}, u32[]{:S(2)}) collective-permute-start(bf16[1,192,512]{2,1,0:T(8,128)(2,1)} %get-tuple-element.21), channel_id=1, source_target_pairs={{0,4},{4,0},{1,5},{5,1},{2,6},{6,2},{3,7},{7,3},{8,12},{12,8},{9,1... | collective-permute-start | bytes 589832 | tf_op jit(solution)/shard_map/ppermute | solution.py:101
  10.0 17.8 %collective-permute-start = (bf16[512,384]{1,0:T(8,128)(2,1)S(1)}, bf16[512,384]{1,0:T(8,128)(2,1)}, u32[]{:S(2)}, u32[]{:S(2)}) collective-permute-start(bf16[512,384]{1,0:T(8,128)(2,1)S(1)} %bitcast.98), channel_id=1, source_target_pairs={{0,1},{1,0},{2,3},{3,2},{4,5},{5,4},{6,7},{7,6},{8,9},{9,8},{10,11... | collective-permute-start | bytes 1179656 | tf_op jit(solution)/shard_map/ppermute | solution.py:101
  11.6 20.0 %collective-permute-start.4 = (bf16[384,768]{1,0:T(8,128)(2,1)}, bf16[384,768]{1,0:T(8,128)(2,1)}, u32[]{:S(2)}, u32[]{:S(2)}) collective-permute-start(bf16[384,768]{1,0:T(8,128)(2,1)} %param.17), channel_id=1, source_target_pairs={{0,16},{8,24},{16,0},{24,8},{1,17},{9,25},{17,1},{25,9},{2,18},{10... | collective-permute-start | bytes 1769480 | tf_op jit(solution)/shard_map/ppermute | solution.py:101
  23.9 14.1 %collective-permute-start.9 = (bf16[2,192,512]{2,1,0:T(8,128)(2,1)}, bf16[2,192,512]{2,1,0:T(8,128)(2,1)}, u32[]{:S(2)}, u32[]{:S(2)}) collective-permute-start(bf16[2,192,512]{2,1,0:T(8,128)(2,1)} %get-tuple-element.19), channel_id=1, source_target_pairs={{0,1},{1,2},{2,3},{3,0},{4,5},{5,6},{6,7},{7,4},{8,9},{9,10},{10,1... | collective-permute-start | bytes 1179656 | tf_op jit(solution)/shard_map/ppermute | solution.py:104
  24.5 19.7 %collective-permute-start.10 = (bf16[2,192,512]{2,1,0:T(8,128)(2,1)}, bf16[2,192,512]{2,1,0:T(8,128)(2,1)}, u32[]{:S(2)}, u32[]{:S(2)}) collective-permute-start(bf16[2,192,512]{2,1,0:T(8,128)(2,1)} %get-tuple-element.19), channel_id=1, source_target_pairs={{0,3},{1,0},{2,1},{3,2},{4,7},{5,4},{6,5},{7,6},{8,11},{9,8},{10,9... | collective-permute-start | bytes 1179656 | tf_op jit(solution)/shard_map/ppermute | solution.py:104
  29.8 20.2 %collective-permute-start.1 = (bf16[1024,384]{1,0:T(8,128)(2,1)}, bf16[1024,384]{1,0:T(8,128)(2,1)}, u32[]{:S(2)}, u32[]{:S(2)}) collective-permute-start(bf16[1024,384]{1,0:T(8,128)(2,1)} %pad_maximum_fusion.1), channel_id=1, source_target_pairs={{0,16},{8,24},{16,0},{24,8},{1,17},{9,25},{17,1},{25,9},{2,18},{10... | collective-permute-start | bytes 2359304 | tf_op jit(solution)/shard_map/ppermute | solution.py:101
  31.7 18.4 %collective-permute-start.12 = (bf16[2,192,512]{2,1,0:T(8,128)(2,1)}, bf16[2,192,512]{2,1,0:T(8,128)(2,1)S(1)}, u32[]{:S(2)}, u32[]{:S(2)}) collective-permute-start(bf16[2,192,512]{2,1,0:T(8,128)(2,1)} %collective-permute-done.7), channel_id=1, source_target_pairs={{0,4},{4,0},{1,5},{5,1},{2,6},{6,2},{3,7},{7,3},{8,12},{12,8},{9,1... | collective-permute-start | bytes 1179656 | tf_op jit(solution)/shard_map/ppermute | solution.py:101
  38.1 12.3 %collective-permute-start.5 = (bf16[384,768]{1,0:T(8,128)(2,1)}, bf16[384,768]{1,0:T(8,128)(2,1)S(1)}, u32[]{:S(2)}, u32[]{:S(2)}) collective-permute-start(bf16[384,768]{1,0:T(8,128)(2,1)} %param.17), channel_id=1, source_target_pairs={{0,8},{8,0},{16,24},{24,16},{1,9},{9,1},{17,25},{25,17},{2,10},{10... | collective-permute-start | bytes 1769480 | tf_op jit(solution)/shard_map/ppermute | solution.py:101
  44.2 6.1 %collective-permute-start.6 = (bf16[384,768]{1,0:T(8,128)(2,1)}, bf16[384,768]{1,0:T(8,128)(2,1)S(1)}, u32[]{:S(2)}, u32[]{:S(2)}) collective-permute-start(bf16[384,768]{1,0:T(8,128)(2,1)} %collective-permute-done.4), channel_id=1, source_target_pairs={{0,8},{8,0},{16,24},{24,16},{1,9},{9,1},{17,25},{25,17},{2,10},{10... | collective-permute-start | bytes 1769480 | tf_op jit(solution)/shard_map/ppermute | solution.py:101
  47.4 11.8 %collective-permute-start.13 = (bf16[2,192,512]{2,1,0:T(8,128)(2,1)}, bf16[2,192,512]{2,1,0:T(8,128)(2,1)S(1)}, u32[]{:S(2)}, u32[]{:S(2)}) collective-permute-start(bf16[2,192,512]{2,1,0:T(8,128)(2,1)} %collective-permute-done.9), channel_id=1, source_target_pairs={{0,4},{4,0},{1,5},{5,1},{2,6},{6,2},{3,7},{7,3},{8,12},{12,8},{9,1... | collective-permute-start | bytes 1179656 | tf_op jit(solution)/shard_map/ppermute | solution.py:101
  50.1 14.3 %collective-permute-start.2 = (bf16[1024,384]{1,0:T(8,128)(2,1)}, bf16[1024,384]{1,0:T(8,128)(2,1)S(1)}, u32[]{:S(2)}, u32[]{:S(2)}) collective-permute-start(bf16[1024,384]{1,0:T(8,128)(2,1)} %pad_maximum_fusion.1), channel_id=1, source_target_pairs={{0,8},{8,0},{16,24},{24,16},{1,9},{9,1},{17,25},{25,17},{2,10},{10... | collective-permute-start | bytes 2359304 | tf_op jit(solution)/shard_map/ppermute | solution.py:101
  50.4 12.4 %collective-permute-start.15 = (bf16[1,192,512]{2,1,0:T(8,128)(2,1)}, bf16[1,192,512]{2,1,0:T(8,128)(2,1)S(1)}, u32[]{:S(2)}, u32[]{:S(2)}) collective-permute-start(bf16[1,192,512]{2,1,0:T(8,128)(2,1)} %get-tuple-element.21), channel_id=1, source_target_pairs={{0,2},{1,3},{2,0},{3,1},{4,6},{5,7},{6,4},{7,5},{8,10},{9,11},{10,... | collective-permute-start | bytes 589832 | tf_op jit(solution)/shard_map/ppermute | solution.py:104
  52.2 12.2 %collective-permute-start.3 = (bf16[1024,384]{1,0:T(8,128)(2,1)}, bf16[1024,384]{1,0:T(8,128)(2,1)S(1)}, u32[]{:S(2)}, u32[]{:S(2)}) collective-permute-start(bf16[1024,384]{1,0:T(8,128)(2,1)} %collective-permute-done.1), channel_id=1, source_target_pairs={{0,8},{8,0},{16,24},{24,16},{1,9},{9,1},{17,25},{25,17},{2,10},{10... | collective-permute-start | bytes 2359304 | tf_op jit(solution)/shard_map/ppermute | solution.py:101
  52.2 11.2 %copy-start.7 = (bf16[1024,192]{0,1:T(8,128)(2,1)S(1)}, bf16[1024,192]{0,1:T(8,128)(2,1)}, u32[]{:S(2)}) copy-start(bf16[1024,192]{0,1:T(8,128)(2,1)} %param.16) | copy-start | bytes 1179652
  53.4 11.0 %copy-start.9 = (bf16[1,192,512]{2,1,0:T(8,128)(2,1)S(1)}, bf16[1,192,512]{2,1,0:T(8,128)(2,1)}, u32[]{:S(2)}) copy-start(bf16[1,192,512]{2,1,0:T(8,128)(2,1)} %get-tuple-element.23) | copy-start | bytes 589828
  53.4 14.9 %copy-start.6 = (bf16[1,512,384]{2,1,0:T(8,128)(2,1)S(1)}, bf16[1,512,384]{2,1,0:T(8,128)(2,1)}, u32[]{:S(2)}) copy-start(bf16[1,512,384]{2,1,0:T(8,128)(2,1)} %param.12) | copy-start | bytes 1179652
  59.2 5.2 %copy-start.1 = (bf16[1536,768]{1,0:T(8,128)(2,1)}, bf16[1536,768]{1,0:T(8,128)(2,1)S(1)}, u32[]{:S(2)}) copy-start(bf16[1536,768]{1,0:T(8,128)(2,1)S(1)} %constant_dynamic-update-slice_fusion) | copy-start | bytes 7077892
  62.8 14.2 %collective-permute-start.18 = (bf16[1,192,512]{2,1,0:T(8,128)(2,1)S(1)}, bf16[1,192,512]{2,1,0:T(8,128)(2,1)S(1)}, u32[]{:S(2)}, u32[]{:S(2)}) collective-permute-start(bf16[1,192,512]{2,1,0:T(8,128)(2,1)S(1)} %collective-permute-done.15), channel_id=1, source_target_pairs={{0,4},{4,0},{1,5},{5,1},{2,6},{6,2},{3,7},{7,3},{8,12},{12,8},{9,1... | collective-permute-start | bytes 589832 | tf_op jit(solution)/shard_map/ppermute | solution.py:101
  64.4 10.4 %collective-permute-start.16 = (bf16[1,192,512]{2,1,0:T(8,128)(2,1)S(1)}, bf16[1,192,512]{2,1,0:T(8,128)(2,1)S(1)}, u32[]{:S(2)}, u32[]{:S(2)}) collective-permute-start(bf16[1,192,512]{2,1,0:T(8,128)(2,1)S(1)} %copy-done.9), channel_id=1, source_target_pairs={{0,1},{1,2},{2,3},{3,0},{4,5},{5,6},{6,7},{7,4},{8,9},{9,10},{10,1... | collective-permute-start | bytes 589832 | tf_op jit(solution)/shard_map/ppermute | solution.py:104
  64.5 11.2 %collective-permute-start.17 = (bf16[1,192,512]{2,1,0:T(8,128)(2,1)S(1)}, bf16[1,192,512]{2,1,0:T(8,128)(2,1)S(1)}, u32[]{:S(2)}, u32[]{:S(2)}) collective-permute-start(bf16[1,192,512]{2,1,0:T(8,128)(2,1)S(1)} %copy-done.9), channel_id=1, source_target_pairs={{0,3},{1,0},{2,1},{3,2},{4,7},{5,4},{6,5},{7,6},{8,11},{9,8},{10,9... | collective-permute-start | bytes 589832 | tf_op jit(solution)/shard_map/ppermute | solution.py:104
  73.2 12.3 %collective-permute-start.14 = (bf16[2,192,512]{2,1,0:T(8,128)(2,1)}, bf16[2,192,512]{2,1,0:T(8,128)(2,1)S(1)}, u32[]{:S(2)}, u32[]{:S(2)}) collective-permute-start(bf16[2,192,512]{2,1,0:T(8,128)(2,1)} %collective-permute-done.10), channel_id=1, source_target_pairs={{0,4},{4,0},{1,5},{5,1},{2,6},{6,2},{3,7},{7,3},{8,12},{12,8},{9,1... | collective-permute-start | bytes 1179656 | tf_op jit(solution)/shard_map/ppermute | solution.py:101
  74.8 16.0 %collective-permute-start.19 = (bf16[1,192,512]{2,1,0:T(8,128)(2,1)S(1)}, bf16[1,192,512]{2,1,0:T(8,128)(2,1)S(1)}, u32[]{:S(2)}, u32[]{:S(2)}) collective-permute-start(bf16[1,192,512]{2,1,0:T(8,128)(2,1)S(1)} %collective-permute-done.16), channel_id=1, source_target_pairs={{0,4},{4,0},{1,5},{5,1},{2,6},{6,2},{3,7},{7,3},{8,12},{12,8},{9,1... | collective-permute-start | bytes 589832 | tf_op jit(solution)/shard_map/ppermute | solution.py:101
  75.7 15.8 %collective-permute-start.20 = (bf16[1,192,512]{2,1,0:T(8,128)(2,1)S(1)}, bf16[1,192,512]{2,1,0:T(8,128)(2,1)S(1)}, u32[]{:S(2)}, u32[]{:S(2)}) collective-permute-start(bf16[1,192,512]{2,1,0:T(8,128)(2,1)S(1)} %collective-permute-done.17), channel_id=1, source_target_pairs={{0,4},{4,0},{1,5},{5,1},{2,6},{6,2},{3,7},{7,3},{8,12},{12,8},{9,1... | collective-permute-start | bytes 589832 | tf_op jit(solution)/shard_map/ppermute | solution.py:101
  87.4 2.1 %copy-start.2 = (bf16[1536,768]{1,0:T(8,128)(2,1)S(1)}, bf16[1536,768]{1,0:T(8,128)(2,1)}, u32[]{:S(2)}) copy-start(bf16[1536,768]{1,0:T(8,128)(2,1)} %copy-done.1) | copy-start | bytes 7077892
  89.4 3.5 %copy-start.8 = (bf16[1024,512]{1,0:T(8,128)(2,1)}, bf16[1024,512]{1,0:T(8,128)(2,1)S(1)}, u32[]{:S(2)}) copy-start(bf16[1024,512]{1,0:T(8,128)(2,1)S(1)} %multiply_convert_fusion) | copy-start | bytes 3145732
  95.5 2.6 %collective-permute-start.21 = (bf16[2,2,128,768]{3,2,1,0:T(8,128)(2,1)}, bf16[2,2,128,768]{3,2,1,0:T(8,128)(2,1)}, u32[]{:S(2)}, u32[]{:S(2)}) collective-permute-start(bf16[2,2,128,768]{3,2,1,0:T(8,128)(2,1)} %convolution_convert_fusion), channel_id=1, source_target_pairs={{0,8},{8,0},{16,24},{24,16},{1,9},{9,1},{17,25},{25,17},{2,10},{10... | collective-permute-start | bytes 2359304 | tf_op jit(solution)/shard_map/ppermute | solution.py:101
  100.3 2.6 %copy-start.4 = (f32[2,2,128,768]{3,2,1,0:T(8,128)}, f32[2,2,128,768]{3,2,1,0:T(8,128)S(1)}, u32[]{:S(2)}) copy-start(f32[2,2,128,768]{3,2,1,0:T(8,128)S(1)} %convert_add_fusion) | copy-start | bytes 4718596
  101.3 11.5 %collective-permute-start.22 = (bf16[128,768]{1,0:T(8,128)(2,1)}, bf16[128,768]{1,0:T(8,128)(2,1)}, u32[]{:S(2)}, u32[]{:S(2)}) collective-permute-start(bf16[128,768]{1,0:T(8,128)(2,1)} %get-tuple-element.43), channel_id=1, source_target_pairs={{0,16},{8,24},{16,0},{24,8},{1,17},{9,25},{17,1},{25,9},{2,18},{10... | collective-permute-start | bytes 589832 | tf_op jit(solution)/shard_map/ppermute | solution.py:101
  102.8 9.9 %collective-permute-start.24 = (bf16[128,768]{1,0:T(8,128)(2,1)}, bf16[128,768]{1,0:T(8,128)(2,1)}, u32[]{:S(2)}, u32[]{:S(2)}) collective-permute-start(bf16[128,768]{1,0:T(8,128)(2,1)} %get-tuple-element.44), channel_id=1, source_target_pairs={{0,17},{1,16},{2,19},{3,18},{8,25},{9,24},{10,27},{11,26},{16,1},{... | collective-permute-start | bytes 589832 | tf_op jit(solution)/shard_map/ppermute | solution.py:101
  103.6 10.4 %collective-permute-start.23 = (bf16[128,768]{1,0:T(8,128)(2,1)}, bf16[128,768]{1,0:T(8,128)(2,1)}, u32[]{:S(2)}, u32[]{:S(2)}) collective-permute-start(bf16[128,768]{1,0:T(8,128)(2,1)} %fusion.31), channel_id=1, source_target_pairs={{0,1},{1,0},{2,3},{3,2},{4,5},{5,4},{6,7},{7,6},{8,9},{9,8},{10,11... | collective-permute-start | bytes 589832 | tf_op jit(solution)/shard_map/ppermute | solution.py:101
  105.5 8.5 %copy-start.3 = (bf16[1536,768]{1,0:T(8,128)(2,1)S(1)}, bf16[1536,768]{1,0:T(8,128)(2,1)}, u32[]{:S(2)}) copy-start(bf16[1536,768]{1,0:T(8,128)(2,1)} %copy-done.1) | copy-start | bytes 7077892
  105.6 10.6 %copy-start.10 = (f32[768]{0:T(1024)S(1)}, f32[768]{0:T(1024)}, u32[]{:S(2)}) copy-start(f32[768]{0:T(1024)} %param.18) | copy-start | bytes 9220
  115.9 15.3 %copy-start = (bf16[3,768,192]{1,2,0:T(8,128)(2,1)S(1)}, bf16[3,768,192]{1,2,0:T(8,128)(2,1)}, u32[]{:S(2)}) copy-start(bf16[3,768,192]{1,2,0:T(8,128)(2,1)} %param.19) | copy-start | bytes 2654212
  116.3 7.7 %collective-permute-start.25 = (bf16[128,768]{1,0:T(8,128)(2,1)S(1)}, bf16[128,768]{1,0:T(8,128)(2,1)S(1)}, u32[]{:S(2)}, u32[]{:S(2)}) collective-permute-start(bf16[128,768]{1,0:T(8,128)(2,1)S(1)} %multiply_convert_fusion.1.refs_1_), channel_id=1, source_target_pairs={{0,16},{8,24},{16,0},{24,8},{1,17},{9,25},{17,1},{25,9},{2,18},{10... | collective-permute-start | bytes 589832 | tf_op jit(solution)/shard_map/ppermute | solution.py:101
  117.9 9.8 %collective-permute-start.26 = (bf16[128,768]{1,0:T(8,128)(2,1)S(1)}, bf16[128,768]{1,0:T(8,128)(2,1)S(1)}, u32[]{:S(2)}, u32[]{:S(2)}) collective-permute-start(bf16[128,768]{1,0:T(8,128)(2,1)S(1)} %multiply_convert_fusion.1.refs_1_), channel_id=1, source_target_pairs={{0,4},{4,0},{1,5},{5,1},{2,6},{6,2},{3,7},{7,3},{8,12},{12,8},{9,1... | collective-permute-start | bytes 589832 | tf_op jit(solution)/shard_map/ppermute | solution.py:101
  119.4 8.3 %collective-permute-start.27 = (bf16[128,768]{1,0:T(8,128)(2,1)S(1)}, bf16[128,768]{1,0:T(8,128)(2,1)S(1)}, u32[]{:S(2)}, u32[]{:S(2)}) collective-permute-start(bf16[128,768]{1,0:T(8,128)(2,1)S(1)} %multiply_convert_fusion.1.refs_1_), channel_id=1, source_target_pairs={{0,20},{4,16},{8,28},{12,24},{16,4},{20,0},{24,12},{28,8},{1,21},{... | collective-permute-start | bytes 589832 | tf_op jit(solution)/shard_map/ppermute | solution.py:101
  128.7 2.5 %collective-permute-start.28 = (bf16[4,128,768]{2,1,0:T(8,128)(2,1)}, bf16[4,128,768]{2,1,0:T(8,128)(2,1)S(1)}, u32[]{:S(2)}, u32[]{:S(2)}) collective-permute-start(bf16[4,128,768]{2,1,0:T(8,128)(2,1)} %pad_maximum_fusion.2), channel_id=1, source_target_pairs={{0,8},{8,0},{16,24},{24,16},{1,9},{9,1},{17,25},{25,17},{2,10},{10... | collective-permute-start | bytes 2359304 | tf_op jit(solution)/shard_map/ppermute | solution.py:101
  136.5 1.8 %collective-permute-start.29 = (bf16[2,192,512]{2,1,0:T(8,128)(2,1)S(1)}, bf16[2,192,512]{2,1,0:T(8,128)(2,1)S(1)}, u32[]{:S(2)}, u32[]{:S(2)}) collective-permute-start(bf16[2,192,512]{2,1,0:T(8,128)(2,1)S(1)} %get-tuple-element.26), channel_id=1, source_target_pairs={{0,8},{8,0},{16,24},{24,16},{1,9},{9,1},{17,25},{25,17},{2,10},{10... | collective-permute-start | bytes 1179656 | tf_op jit(solution)/shard_map/ppermute | solution.py:101
  138.5 7.0 %collective-permute-start.30 = (bf16[192,512]{1,0:T(8,128)(2,1)S(1)}, bf16[192,512]{1,0:T(8,128)(2,1)S(1)}, u32[]{:S(2)}, u32[]{:S(2)}) collective-permute-start(bf16[192,512]{1,0:T(8,128)(2,1)S(1)} %fusion.33), channel_id=1, source_target_pairs={{0,16},{8,24},{16,0},{24,8},{1,17},{9,25},{17,1},{25,9},{2,18},{10... | collective-permute-start | bytes 589832 | tf_op jit(solution)/shard_map/ppermute | solution.py:101

commit v7 on v6

--- a/solution.py
+++ b/solution.py
@@ -82,6 +82,78 @@
             send_ref[j ^ side, :, at] = jnp.where(core == 0, high, low).astype(send_ref.dtype)
 
 
+def norm_kernel(gain_ref, *refs):
+    out_ref = refs[-1]
+    parts = (len(refs) - 1) // 2
+    tokens, width = refs[0].shape
+    step = 64
+    for pack in range(2):
+        pieces = refs[pack * parts : (pack + 1) * parts]
+
+        def rows(i, carry, pack=pack, pieces=pieces):
+            at = pl.multiple_of(i * step, step)
+            x = [piece[pl.ds(at, step), :].astype(jnp.float32) for piece in pieces]
+            total = sum(jnp.sum(part, axis=1, keepdims=True) for part in x)
+            x = [part - total / (width * parts) for part in x]
+            square = sum(jnp.sum(part * part, axis=1, keepdims=True) for part in x)
+            factor = lax.rsqrt(square / (width * parts) + 1e-06)
+            to = pl.ds(pl.multiple_of(pack * tokens + i * step, step), step)
+            for m, part in enumerate(x):
+                out_ref[to, m * width : (m + 1) * width] = (part * factor * gain_ref[m]).astype(
+                    out_ref.dtype
+                )
+            return carry
+
+        lax.fori_loop(0, tokens // step, rows, 0, unroll=2)
+
+
+def gate_kernel(at_ref, normed_ref, *refs):
+    blocks, (out_ref, all_ref, sem) = refs[:-3], refs[-3:]
+    rows = blocks[0].shape[1]
+    copies = []
+    for i, block in enumerate(blocks):
+        to = pl.ds(pl.multiple_of(at_ref[i], rows), rows)
+        copies.append(pltpu.make_async_copy(block, all_ref.at[:, to, :], sem.at[i]))
+        copies[-1].start()
+    for copy in copies:
+        copy.wait()
+    step = 256
+    for i in range(normed_ref.shape[0] // step):
+        x = normed_ref[i * step : (i + 1) * step, :]
+        gate = jnp.dot(x, all_ref[0], preferred_element_type=jnp.float32)
+        up = jnp.dot(x, all_ref[1], preferred_element_type=jnp.float32)
+        out_ref[i * step : (i + 1) * step, :] = (gate * jax.nn.sigmoid(gate) * up).astype(
+            out_ref.dtype
+        )
+
+
+def project_kernel(at_ref, core_ref, hidden_ref, proj_ref, *refs):
+    blocks, (send_ref, keep_ref, all_ref, sem) = refs[:-4], refs[-4:]
+    rows = blocks[0].shape[1]
+    copies = []
+    for i, block in enumerate(blocks):
+        to = pl.ds(pl.multiple_of(at_ref[i], rows), rows)
+        copies.append(pltpu.make_async_copy(block.at[0], all_ref.at[to, :], sem.at[i]))
+        copies[-1].start()
+    for copy in copies:
+        copy.wait()
+    folded = jnp.dot(proj_ref[...], all_ref[...], preferred_element_type=jnp.float32)
+    folded = folded.astype(jnp.bfloat16)
+    packs, sides, _, own, units = hidden_ref.shape
+    core = core_ref[0]
+    for target, which in ((send_ref, 1 - core), (keep_ref, core)):
+        x = jnp.concatenate(
+            [hidden_ref[p, x, which] for p in range(packs) for x in range(sides)], axis=0
+        )
+        x = lax.dot_general(
+            x, folded, (((1,), (1,)), ((), ())), preferred_element_type=jnp.float32
+        ).astype(target.dtype)
+        for p in range(packs):
+            for j in range(sides):
+                i = p * sides + j
+                target[p, j] = x[i * own : (i + 1) * own]
+
+
 def build(n_sec, n_seq, n_dp):
     sizes = {"section": n_sec, "seq": n_seq, "dp": n_dp}
 
@@ -128,14 +200,6 @@
         block = (seq_at ^ y) * n_dp + (dp_at - k) % n_dp
         each = n_seq * n_dp // n_sec
         return ((block // each ^ sec) * each + block % each) * rows
-
-    def place_rows(blocks):
-        first = blocks[0, 2]
-        mats, rows, units = first.shape
-        whole = after(jnp.zeros((mats, n_seq * n_dp * rows, units), first.dtype), first)
-        for (y, k), block in blocks.items():
-            whole = lax.dynamic_update_slice(whole, block, (0, row_of(y, k, rows), 0))
-        return whole
 
     def per_device(
         tile_feats,
@@ -169,15 +233,6 @@
         down_same, down_other = halves(down, odd), halves(down, 1 - odd)
         ordered = n_seq == 2 and n_dp == 4
 
-        beside = flip(mine, dp=1)
-        both = jnp.concatenate([mine, beside], axis=0)
-        row_blocks = gather_section(both)
-        rows = jnp.concatenate(row_blocks, axis=1)
-        gain = jnp.concatenate(absolute(jnp.split(tile_gain, n_sec)))
-        normed = layer_norm(rows.astype(jnp.float32), gain).astype(jnp.bfloat16)
-        proj_blocks = gather_section(w_proj)
-        proj = jnp.concatenate(proj_blocks, axis=0)
-
         if n_seq == 2:
             masks = (0, 2, 1, 3)
             span = jnp.arange(own_rows, dtype=jnp.int32)
@@ -201,64 +256,128 @@
         k_code = jnp.where(picked, k_block, -1)
         q_code = codes(q_idx)[0].T
 
+        gain = jnp.stack(absolute(jnp.split(tile_gain, n_sec)))
+        own_at = sec * own_rows
+        vmem = pl.BlockSpec(memory_space=pltpu.VMEM)
+        anywhere = pl.BlockSpec(memory_space=pl.ANY)
+        smem = pl.BlockSpec(memory_space=pltpu.SMEM)
+
+        def residual_of(blocks, proj):
+            rows = [lax.dynamic_slice_in_dim(block, own_at, own_rows, 0) for block in blocks]
+            return jnp.dot(
+                jnp.concatenate(rows, axis=1), proj, preferred_element_type=jnp.float32
+            )
+
         if ordered:
-            g = {(0, 0): pair_same, (0, 2): rotate(pair_same, 2)}
-            d = {(0, 0): down_same, (1, 0): flip(down_same, seq=1)}
-            g[0, 1] = rotate(after(pair_other, g[0, 2], d[1, 0]), 1)
-            g[0, 3] = rotate(after(pair_other, g[0, 2], d[1, 0]), 3)
-            g[1, 0], g[1, 2], g[1, 1] = (flip(g[0, k], seq=1) for k in (0, 2, 1))
-            g[1, 3] = flip(after(g[0, 3], normed), seq=1)
-            gate_up = place_rows(g)
-            d[0, 2] = rotate(after(down_same, g[0, 1], proj_blocks[1], proj_blocks[3]), 2)
-            there = [row_blocks[1], row_blocks[3], k_code, q_code]
-            d[0, 1] = rotate(after(down_other, d[0, 2], *there), 1)
-            d[0, 3] = rotate(after(down_other, d[0, 2], *there), 3)
-            for k in (2, 1, 3):
-                d[1, k] = flip(d[0, k], seq=1)
+            g, d = {(0, 0): pair_same}, {(0, 0): down_same}
+            beside = flip(mine, dp=1)
+            mine_x = flip(mine, section=2)
+            proj_x = flip(w_proj, section=2)
+            g[0, 2] = rotate(pair_same, 2)
+            g[1, 0] = flip(pair_same, seq=1)
+            d[1, 0] = flip(after(down_same, g[1, 0]), seq=1)
+            mine_c = flip(after(mine, mine_x), section=1)
+            mine_xc = flip(mine_x, section=1)
+            beside_x = flip(after(beside, mine_c, mine_xc), section=2)
+            for k in (1, 3):
+                g[0, k] = rotate(after(pair_other, g[0, 2], d[1, 0], proj_x), k)
+            g[1, 2] = flip(g[0, 2], seq=1)
+            proj_c = flip(after(w_proj, proj_x), section=1)
+            proj_xc = flip(proj_x, section=1)
+            beside_c = flip(after(beside, beside_x), section=1)
+            beside_xc = flip(beside_x, section=1)
+            d[0, 2] = rotate(
+                after(down_same, g[0, 1], g[1, 2], proj_c, proj_xc, k_code, q_code), 2
+            )
+            g[1, 1], g[1, 3] = flip(g[0, 1], seq=1), flip(g[0, 3], seq=1)
+            normed = pl.pallas_call(
+                norm_kernel,
+                out_shape=jax.ShapeDtypeStruct((2 * tokens, feats * n_sec), jnp.bfloat16),
+                in_specs=[vmem] * 9,
+                out_specs=vmem,
+                compiler_params=pltpu.CompilerParams(vmem_limit_bytes=16 * 2**20),
+                cost_estimate=pl.CostEstimate(
+                    flops=16 * tokens * feats * n_sec,
+                    bytes_accessed=8 * tokens * feats * n_sec,
+                    transcendentals=2 * tokens,
+                ),
+            )(
+                gain[:, None, :],
+                *(mine, mine_c, mine_x, mine_xc),
+                *(beside, beside_c, beside_x, beside_xc),
+            )
+            proj = jnp.concatenate([w_proj, proj_c, proj_x, proj_xc], axis=0)
+            proj_t = proj.T
+            residual = residual_of((mine, mine_c, mine_x, mine_xc), proj)
+            for k in (1, 3):
+                d[0, k] = rotate(after(down_other, d[0, 2], normed, proj_t, residual), k)
+            d[1, 2], d[1, 1], d[1, 3] = (flip(d[0, k], seq=1) for k in (2, 1, 3))
+
+            order = list(g)
+            places = jnp.stack([row_of(y, k, pair.shape[1]) for y, k in order])
+            normed = after(normed, d[0, 1], d[0, 3])
+            hidden = pl.pallas_call(
+                gate_kernel,
+                out_shape=jax.ShapeDtypeStruct((2 * tokens, half), jnp.bfloat16),
+                in_specs=[smem, vmem] + [anywhere] * len(order),
+                out_specs=vmem,
+                scratch_shapes=[
+                    pltpu.VMEM((2, feats * n_sec, half), jnp.bfloat16),
+                    pltpu.SemaphoreType.DMA((len(order),)),
+                ],
+                compiler_params=pltpu.CompilerParams(vmem_limit_bytes=24 * 2**20),
+                cost_estimate=pl.CostEstimate(
+                    flops=8 * tokens * feats * n_sec * half,
+                    bytes_accessed=8 * 2**20,
+                    transcendentals=2 * tokens * half,
+                ),
+            )(places, normed, *(g[at] for at in order))
+            hidden = hidden.reshape(2, n_sec // 2, 2, own_rows, half)
+            sums = (2, n_sec // 2, own_rows, proj.shape[1])
+            send, kept = pl.pallas_call(
+                project_kernel,
+                out_shape=[
+                    jax.ShapeDtypeStruct(sums, jnp.bfloat16),
+                    jax.ShapeDtypeStruct(sums, jnp.float32),
+                ],
+                in_specs=[smem, smem, vmem, vmem] + [anywhere] * len(order),
+                out_specs=[vmem] * 2,
+                scratch_shapes=[
+                    pltpu.VMEM((feats * n_sec, half), jnp.bfloat16),
+                    pltpu.SemaphoreType.DMA((len(order),)),
+                ],
+                compiler_params=pltpu.CompilerParams(vmem_limit_bytes=24 * 2**20),
+                cost_estimate=pl.CostEstimate(
+                    flops=2 * half * proj.shape[1] * (feats * n_sec + 2 * tokens),
+                    bytes_accessed=8 * 2**20,
+                    transcendentals=0,
+                ),
+            )(places, core[None], hidden, proj_t, *(d[at] for at in order))
         else:
             gate_up = gather_rows(pair_same, pair_other, seq_at, dp_at)
             down_all = gather_rows(down_same, down_other, seq_at, dp_at)[0]
-
-        gate = jnp.dot(normed, gate_up[0], preferred_element_type=jnp.float32)
-        up = jnp.dot(normed, gate_up[1], preferred_element_type=jnp.float32)
-        hidden = (jax.nn.silu(gate) * up).astype(jnp.bfloat16)
-        hidden = hidden.reshape(2, n_sec // 2, 2, own_rows, half)
-
-        def fold(proj_rows, down_rows):
-            return lax.dot_general(
-                proj_rows, down_rows, (((0,), (0,)), ((), ())), preferred_element_type=jnp.float32
-            )
-
-        if ordered:
-            late = [d.pop((1, 1)), d.pop((1, 3))]
-            folded = fold(proj, after(place_rows(d)[0], hidden))
-            for k, block in zip((1, 3), late):
-                at = row_of(1, k, block.shape[1])
-                folded = folded + fold(
-                    lax.dynamic_slice_in_dim(proj, at, block.shape[1], 0), block[0]
-                )
-        else:
-            folded = fold(proj, down_all)
-        folded = folded.astype(jnp.bfloat16)
-
-        def project(x):
-            return lax.dot_general(
-                x, folded, (((x.ndim - 1,), (1,)), ((), ())), preferred_element_type=jnp.float32
-            )
-
-        send = project(lax.dynamic_index_in_dim(hidden, 1 - core, 2, False)).astype(jnp.bfloat16)
-        got = flip(send, section=1)
-        kept = project(lax.dynamic_index_in_dim(hidden, core, 2, False)) + got.astype(jnp.float32)
+            blocks = gather_section(jnp.concatenate([mine, flip(mine, dp=1)], axis=0))
+            proj = jnp.concatenate(gather_section(w_proj), axis=0)
+            residual = residual_of([block[:tokens] for block in blocks], proj)
+            rows = jnp.concatenate(blocks, axis=1).astype(jnp.float32)
+            normed = layer_norm(rows, gain.reshape(-1)).astype(jnp.bfloat16)
+            gate = jnp.dot(normed, gate_up[0], preferred_element_type=jnp.float32)
+            up = jnp.dot(normed, gate_up[1], preferred_element_type=jnp.float32)
+            hidden = (jax.nn.silu(gate) * up).astype(jnp.bfloat16)
+            folded = lax.dot_general(
+                down_all, proj, (((0,), (0,)), ((), ())), preferred_element_type=jnp.float32
+            ).astype(jnp.bfloat16)
+            sums = jnp.dot(hidden, folded, preferred_element_type=jnp.float32)
+            sums = sums.reshape(2, n_sec // 2, 2, own_rows, proj.shape[1])
+            send = lax.dynamic_index_in_dim(sums, 1 - core, 2, False).astype(jnp.bfloat16)
+            kept = lax.dynamic_index_in_dim(sums, core, 2, False)
+
+        kept = kept + flip(send, section=1).astype(jnp.float32)
         here = lax.dynamic_index_in_dim(kept, side, 1, False)
         there = lax.dynamic_index_in_dim(kept, 1 - side, 1, False).astype(jnp.bfloat16)
         from_x = flip(there[0], section=2)
         from_z = flip(here[1].astype(jnp.bfloat16), dp=1)
         from_xz = flip(there[1], section=2, dp=1)
-        residual = jnp.dot(
-            lax.dynamic_slice_in_dim(rows[:tokens], sec * own_rows, own_rows, 0),
-            proj,
-            preferred_element_type=jnp.float32,
-        )
         emb = (
             residual
             + here[0]
@@ -281,14 +400,13 @@
         width = w_qkv.shape[2]
         qkv = jnp.swapaxes(w_qkv, 1, 2)
         if n_seq == 2:
-            vmem = pl.BlockSpec(memory_space=pltpu.VMEM)
             keep, send = pl.pallas_call(
                 lambda *refs: attend_kernel(*refs, heads=local_heads, masks=masks),
                 out_shape=[
                     jax.ShapeDtypeStruct((2, width, tokens), jnp.float32),
                     jax.ShapeDtypeStruct((2, width, tokens), jnp.bfloat16),
                 ],
-                in_specs=[pl.BlockSpec(memory_space=pltpu.SMEM)] + [vmem] * 10,
+                in_specs=[smem] + [vmem] * 10,
                 out_specs=[vmem] * 2,
                 compiler_params=pltpu.CompilerParams(vmem_limit_bytes=40 * 2**20),
                 cost_estimate=pl.CostEstimate(

time: 147 us -> 156 us (1.061)
  Pallas kernels: 5.3 us -> 18.2 us
  matrix products: 13.6 us -> 3.06 us
  local copies, waits for them, and re-layouts: 12.8 us -> 22.3 us
    pallas_call x0 -> x3, Pallas kernels: none -> 12.9 us  [the longest x1 5.73 us: per_device(): pl.pallas_call(gate_kernel, out_shape=jax.ShapeDtypeStruct((2 * tokens, h...]
    dot_general x8 -> x1, matrix products: 13.6 us -> 3.06 us  [residual_of(): jnp.dot(jnp.concatenate(rows, axis=1), proj, preferred_element_type=jnp.f...]
    ppermute x25 -> x28, waiting for transfers between devices: 44.8 us -> 34.3 us  [flip(): return lax.ppermute(x, names if len(names) > 1 else names[0], pairs)]
    ppermute x6, waiting for transfers between devices: 17.4 us -> 26.8 us  [rotate(): return lax.ppermute(x, 'dp', [(i, (i + k) % n_dp) for i in range(n_dp)])]
    unnamed x34 -> x58, local copies, waits for them, and re-layouts: 3.5 us -> 11.3 us
    dynamic_update_slice x14 -> x0, local copies, waits for them, and re-layouts: 5.27 us -> none  [place_rows(): whole = lax.dynamic_update_slice(whole, block, (0, row_of(y, k, rows), 0))]
    another operation x4, local copies, waits for them, and re-layouts: 0.01 us -> 4.95 us  [absolute(): stacked, sec = (jnp.stack(blocks), lax.axis_index('section'))]
    transpose x0 -> x1, other arithmetic: none -> 3.02 us  [per_device(): proj_t = proj.T]
  transfers between devices with their start and end apart: 31 -> 34, of which waited for: 16 -> 15; matrix products, arithmetic and copies ran while one was open for 19% -> 17% of each run, Pallas kernels for 0% -> 6%
where the time goes in v7:
time: 156 us; the launch traced here: 155 us
  waiting for transfers between devices  61 us (39%)
  starting transfers between devices  35.3 us (23%)
  local copies, waits for them, and re-layouts  22.3 us (14%)
  Pallas kernels  18.2 us (12%)
  other arithmetic  14.5 us (9%)
  matrix products  3.06 us (2%)
    ppermute x28, waiting for transfers between devices, flip(): return lax.ppermute(x, names if len(names) > 1 else names[0], pairs)  34.3 us
    ppermute x6, waiting for transfers between devices, rotate(): return lax.ppermute(x, 'dp', [(i, (i + k) % n_dp) for i in range(n_dp)])  26.8 us
    ppermute x28, starting transfers between devices, flip(): return lax.ppermute(x, names if len(names) > 1 else names[0], pairs)  23.8 us
    ppermute x6, starting transfers between devices, rotate(): return lax.ppermute(x, 'dp', [(i, (i + k) % n_dp) for i in range(n_dp)])  11.5 us
    unnamed x58, local copies, waits for them, and re-layouts  11.3 us
    pallas_call x1, Pallas kernels, per_device(): pl.pallas_call(gate_kernel, out_shape=jax.ShapeDtypeStruct((2 * tokens, h...  5.73 us
    pallas_call x1, Pallas kernels, per_device(): pl.pallas_call(lambda *refs: attend_kernel(*refs, heads=local_heads, mask...  5.3 us
    another operation x4, local copies, waits for them, and re-layouts, absolute(): stacked, sec = (jnp.stack(blocks), lax.axis_index('section'))  4.95 us
  transfers between devices with their start and end apart: 34, of which 15 were waited for; matrix products, arithmetic and copies ran while one was open for 17% of the time, Pallas kernels for 6%

profile of v7, /device:TPU:0, one launch (start us, length us, event | category | flops | bytes accessed | tf_op | source)
XLA Modules:
  0.0 154.9 jit_solution(17584657625204921604)
XLA Ops:
  0.0 2.1 %fusion.2 = (bf16[2,192,512]{2,1,0:T(8,128)(2,1)S(1)}, bf16[2,192,512]{2,1,0:T(8,128)(2,1)}) fusion(s32[]{:T(128)S(6)} %select_n.197, bf16[1,192,1024]{2,1,0:T(8,128)(2,1)} %bitcast.77, bf16[1,192,1024]{2,1,0:T(8,128)(2,1)} %bitcast.78, s32[]{:T(128)S(6)} %select_n.196), kind=kLoop, calls=%fused_computation.11 | loop fusion | flops 1572864 | bytes 1572872 | tf_op jit(solution)/shard_map/stack | solution.py:230
  2.1 3.0 %collective-permute-start.11 = (bf16[2,192,512]{2,1,0:T(8,128)(2,1)S(1)}, bf16[2,192,512]{2,1,0:T(8,128)(2,1)S(1)}, u32[]{:S(2)}, u32[]{:S(2)}) collective-permute-start(bf16[2,192,512]{2,1,0:T(8,128)(2,1)S(1)} %get-tuple-element.41.refs_0_), channel_id=1, source_target_pairs={{0,4},{4,0},{1,5},{5,1},{2,6},{6,2},{3,7},{7,3},{8,12},{12,8},{9,1... | collective-permute-start | bytes 1179656 | tf_op jit(solution)/shard_map/ppermute | solution.py:173
  5.1 2.6 %collective-permute-start.10 = (bf16[2,192,512]{2,1,0:T(8,128)(2,1)S(1)}, bf16[2,192,512]{2,1,0:T(8,128)(2,1)S(1)}, u32[]{:S(2)}, u32[]{:S(2)}) collective-permute-start(bf16[2,192,512]{2,1,0:T(8,128)(2,1)S(1)} %get-tuple-element.41.refs_0_), channel_id=1, source_target_pairs={{0,2},{1,3},{2,0},{3,1},{4,6},{5,7},{6,4},{7,5},{8,10},{9,11},{10,... | collective-permute-start | bytes 1179656 | tf_op jit(solution)/shard_map/ppermute | solution.py:176
  7.7 1.5 collective-permute-start
  9.2 1.6 %collective-permute-start.6 = (bf16[512,384]{1,0:T(8,128)(2,1)}, bf16[512,384]{1,0:T(8,128)(2,1)S(1)}, u32[]{:S(2)}, u32[]{:S(2)}) collective-permute-start(bf16[512,384]{1,0:T(8,128)(2,1)} %bitcast.68), channel_id=1, source_target_pairs={{0,1},{1,0},{2,3},{3,2},{4,5},{5,4},{6,7},{7,6},{8,9},{9,8},{10,11... | collective-permute-start | bytes 1179656 | tf_op jit(solution)/shard_map/ppermute | solution.py:173
  10.8 1.4 copy.19
  14.2 3.4 %fusion.17.refs_9_ = s32[512,4]{1,0:T(8,128)} fusion(s32[4]{0:T(128)S(1)} %copy-done.25, s32[512]{0:T(512)S(1)} %get-tuple-element.38, s32[4]{0:T(128)S(1)} %sign.72, s32[512]{0:T(512)S(1)} %broadcast_multiply_fusion.1, s32[512]{0:T(512)S(1)} %get-tuple-element.37), kind=kLoop, calls=%fused_computation.33 | loop fusion | flops 16384 | bytes 14368 | tf_op jit(solution)/shard_map/add | solution.py:252
  20.0 5.1 %collective-permute-done.10.refs_1_ = bf16[2,192,512]{2,1,0:T(8,128)(2,1)S(1)} collective-permute-done((bf16[2,192,512]{2,1,0:T(8,128)(2,1)S(1)}, bf16[2,192,512]{2,1,0:T(8,128)(2,1)S(1)}, u32[]{:S(2)}, u32[]{:S(2)}) %collective-permute-start.10) | collective-permute-done | bytes 393248 | tf_op jit(solution)/shard_map/ppermute | solution.py:176
  25.1 5.8 %collective-permute-done.3 = bf16[384,768]{0,1:T(8,128)(2,1)} collective-permute-done((bf16[384,768]{0,1:T(8,128)(2,1)S(1)}, bf16[384,768]{0,1:T(8,128)(2,1)}, u32[]{:S(2)}, u32[]{:S(2)}) %collective-permute-start.3) | collective-permute-done | bytes 589856 | tf_op jit(solution)/shard_map/ppermute | solution.py:173
  31.5 1.4 fusion.39
  32.9 1.3 stack.82
  34.1 1.2 stack.83
  35.4 1.2 stack.84
  36.6 1.2 stack.85
  37.8 1.3 pad_maximum_fusion.3
  39.1 2.1 %copy.18 = bf16[384,768]{0,1:T(8,128)(2,1)} copy(bf16[384,768]{1,0:T(8,128)(2,1)} %param.17) | data formatting | bytes 1179648 | tf_op jit(solution)/shard_map/optimization_barrier | solution.py:179
  41.8 1.4 constant_dynamic-slice_fusion.3
  43.3 1.6 %collective-permute-start.13 = (bf16[2,192,512]{2,1,0:T(8,128)(2,1)}, bf16[2,192,512]{2,1,0:T(8,128)(2,1)}, u32[]{:S(2)}, u32[]{:S(2)}) collective-permute-start(bf16[2,192,512]{2,1,0:T(8,128)(2,1)} %get-tuple-element.23), channel_id=1, source_target_pairs={{0,1},{1,2},{2,3},{3,0},{4,5},{5,6},{6,7},{7,4},{8,9},{9,10},{10,1... | collective-permute-start | bytes 1179656 | tf_op jit(solution)/shard_map/ppermute | solution.py:176
  44.9 2.2 %collective-permute-start.18 = (bf16[2,192,512]{2,1,0:T(8,128)(2,1)}, bf16[2,192,512]{2,1,0:T(8,128)(2,1)}, u32[]{:S(2)}, u32[]{:S(2)}) collective-permute-start(bf16[2,192,512]{2,1,0:T(8,128)(2,1)} %get-tuple-element.23), channel_id=1, source_target_pairs={{0,3},{1,0},{2,1},{3,2},{4,7},{5,4},{6,5},{7,6},{8,11},{9,8},{10,9... | collective-permute-start | bytes 1179656 | tf_op jit(solution)/shard_map/ppermute | solution.py:176
  47.2 1.5 collective-permute-start.7
  49.5 8.0 %collective-permute-done.13.refs_3_ = bf16[2,192,512]{2,1,0:T(8,128)(2,1)} collective-permute-done((bf16[2,192,512]{2,1,0:T(8,128)(2,1)}, bf16[2,192,512]{2,1,0:T(8,128)(2,1)}, u32[]{:S(2)}, u32[]{:S(2)}) %collective-permute-start.13) | collective-permute-done | bytes 393248 | tf_op jit(solution)/shard_map/ppermute | solution.py:176
  57.5 1.5 collective-permute-start.19
  59.0 5.5 %collective-permute-done.18.refs_4_ = bf16[2,192,512]{2,1,0:T(8,128)(2,1)} collective-permute-done((bf16[2,192,512]{2,1,0:T(8,128)(2,1)}, bf16[2,192,512]{2,1,0:T(8,128)(2,1)}, u32[]{:S(2)}, u32[]{:S(2)}) %collective-permute-start.18) | collective-permute-done | bytes 393248 | tf_op jit(solution)/shard_map/ppermute | solution.py:176
  64.5 1.5 collective-permute-start.20
  67.6 3.0 %fusion.proj_ref = bf16[768,1536]{1,0:T(8,128)(2,1)} fusion(bf16[384,768]{0,1:T(8,128)(2,1)} %collective-permute-done.5, bf16[384,768]{0,1:T(8,128)(2,1)} %collective-permute-done.3, bf16[384,768]{0,1:T(8,128)(2,1)} %collective-permute-done.4, bf16[384,768]{0,1:T(8,128)(2,1)S(1)} %copy.19), kind=kLoop, calls=%fused_computation.9 | loop fusion | flops 9437184 | bytes 4718592 | tf_op jit(solution)/shard_map/transpose | solution.py:310
  70.7 3.1 %fusion.1 = f32[128,768]{1,0:T(8,128)} fusion(bf16[384,768]{0,1:T(8,128)(2,1)} %collective-permute-done.5, bf16[384,768]{0,1:T(8,128)(2,1)} %collective-permute-done.3, bf16[384,768]{0,1:T(8,128)(2,1)} %collective-permute-done.4, bf16[384,768]{0,1:T(8,128)(2,1)S(1)} %copy.19, bf16[128,384]{1,0:T(8,128)(2,1)S(1)} %constant_dynamic-slice_fusion.4, ...), kind=kOutput, calls=%fused_computation.10 | convolution fusion | flops 312999936 | bytes 3145728 | tf_op jit(solution)/shard_map/dot_general | solution.py:267
  77.8 3.0 %shard_map.118.normed_ref = bf16[1024,1536]{1,0:T(8,128)(2,1)S(1)} custom-call(f32[4,1,384]{2,1,0:T(1,128)S(1)} %broadcast_in_dim.38.gain_ref, bf16[512,384]{1,0:T(8,128)(2,1)S(1)} %bitcast.70, bf16[512,384]{1,0:T(8,128)(2,1)S(1)} %copy-done.5, bf16[512,384]{1,0:T(8,128)(2,1)S(1)} %copy-done.3, bf16[512,384]{1,0:T(8,128)(2,1)S(1)} %copy-done.7, ...), custom_call_target="tpu_custom_call" | custom-call | flops 12582912 | bytes 6291456 | tf_op jit(solution)/shard_map/pallas_call | solution.py:293
  80.8 1.6 %collective-permute-start.16 = (bf16[1,192,512]{2,1,0:T(8,128)(2,1)}, bf16[1,192,512]{2,1,0:T(8,128)(2,1)}, u32[]{:S(2)}, u32[]{:S(2)}) collective-permute-start(bf16[1,192,512]{2,1,0:T(8,128)(2,1)} %get-tuple-element.25), channel_id=1, source_target_pairs={{0,1},{1,2},{2,3},{3,0},{4,5},{5,6},{6,7},{7,4},{8,9},{9,10},{10,1... | collective-permute-start | bytes 589832 | tf_op jit(solution)/shard_map/ppermute | solution.py:176
  82.3 2.3 %collective-permute-start.17 = (bf16[1,192,512]{2,1,0:T(8,128)(2,1)}, bf16[1,192,512]{2,1,0:T(8,128)(2,1)}, u32[]{:S(2)}, u32[]{:S(2)}) collective-permute-start(bf16[1,192,512]{2,1,0:T(8,128)(2,1)} %get-tuple-element.25), channel_id=1, source_target_pairs={{0,3},{1,0},{2,1},{3,2},{4,7},{5,4},{6,5},{7,6},{8,11},{9,8},{10,9... | collective-permute-start | bytes 589832 | tf_op jit(solution)/shard_map/ppermute | solution.py:176
  85.3 5.5 %collective-permute-done.16.refs_3_ = bf16[1,192,512]{2,1,0:T(8,128)(2,1)} collective-permute-done((bf16[1,192,512]{2,1,0:T(8,128)(2,1)}, bf16[1,192,512]{2,1,0:T(8,128)(2,1)}, u32[]{:S(2)}, u32[]{:S(2)}) %collective-permute-start.16) | collective-permute-done | bytes 196640 | tf_op jit(solution)/shard_map/ppermute | solution.py:176
  90.7 2.7 %collective-permute-done.17.refs_4_ = bf16[1,192,512]{2,1,0:T(8,128)(2,1)} collective-permute-done((bf16[1,192,512]{2,1,0:T(8,128)(2,1)}, bf16[1,192,512]{2,1,0:T(8,128)(2,1)}, u32[]{:S(2)}, u32[]{:S(2)}) %collective-permute-start.17) | collective-permute-done | bytes 196640 | tf_op jit(solution)/shard_map/ppermute | solution.py:176
  93.9 1.5 collective-permute-start.23
  99.4 5.7 %shard_map.119 = bf16[1024,512]{1,0:T(8,128)(2,1)S(1)} custom-call(s32[8]{0:T(128)S(1)} %stack.81.at_ref, bf16[1024,1536]{1,0:T(8,128)(2,1)S(1)} %shard_map.118.normed_ref, bf16[2,192,512]{2,1,0:T(8,128)(2,1)S(1)} %copy-done.11, bf16[2,192,512]{2,1,0:T(8,128)(2,1)S(1)} %copy-done.17, bf16[2,192,512]{2,1,0:T(8,128)(2,1)S(1)} %copy-done.15, ...), custom_call_target="tpu_custom_call" | custom-call | flops 3221225472 | bytes 8388608 | tf_op jit(solution)/shard_map/pallas_call | solution.py:319
  105.2 4.2 %shard_map.120 = (bf16[2,2,128,768]{3,2,1,0:T(8,128)(2,1)S(1)}, f32[2,2,128,768]{3,2,1,0:T(8,128)S(1)}) custom-call(s32[8]{0:T(128)S(1)} %stack.81.at_ref, s32[1]{0:T(128)} %bitcast.11.core_ref, bf16[2,2,2,128,512]{4,3,2,1,0:T(8,128)(2,1)S(1)} %bitcast.76, bf16[768,1536]{1,0:T(8,128)(2,1)S(1)} %copy-done, bf16[1,192,512]{2,1,0:T(8,128)(2,1)} %get-tuple-element.24.refs_0_, ...), custom_call_target="tpu_custom_call" | custom-call | flops 2013265920 | bytes 8388608 | tf_op jit(solution)/shard_map/pallas_call | solution.py:337
  109.5 2.2 %collective-permute-done.24 = bf16[2,2,128,768]{3,2,1,0:T(8,128)(2,1)S(1)} collective-permute-done((bf16[2,2,128,768]{3,2,1,0:T(8,128)(2,1)S(1)}, bf16[2,2,128,768]{3,2,1,0:T(8,128)(2,1)S(1)}, u32[]{:S(2)}, u32[]{:S(2)}) %collective-permute-start.24) | collective-permute-done | bytes 786464 | tf_op jit(solution)/shard_map/ppermute | solution.py:173
  112.0 1.6 %collective-permute-start.25 = (bf16[128,768]{1,0:T(8,128)(2,1)S(1)}, bf16[128,768]{1,0:T(8,128)(2,1)S(1)}, u32[]{:S(2)}, u32[]{:S(2)}) collective-permute-start(bf16[128,768]{1,0:T(8,128)(2,1)S(1)} %get-tuple-element.43), channel_id=1, source_target_pairs={{0,16},{8,24},{16,0},{24,8},{1,17},{9,25},{17,1},{25,9},{2,18},{10... | collective-permute-start | bytes 589832 | tf_op jit(solution)/shard_map/ppermute | solution.py:173
  114.4 1.2 collective-permute-start.26
  115.7 7.6 %collective-permute-done.25 = bf16[128,768]{1,0:T(8,128)(2,1)S(1)} collective-permute-done((bf16[128,768]{1,0:T(8,128)(2,1)S(1)}, bf16[128,768]{1,0:T(8,128)(2,1)S(1)}, u32[]{:S(2)}, u32[]{:S(2)}) %collective-permute-start.25) | collective-permute-done | bytes 196640 | tf_op jit(solution)/shard_map/ppermute | solution.py:173
  123.2 1.2 collective-permute-done.26
  125.0 1.6 %collective-permute-start.28 = (bf16[128,768]{1,0:T(8,128)(2,1)S(1)}, bf16[128,768]{1,0:T(8,128)(2,1)S(1)}, u32[]{:S(2)}, u32[]{:S(2)}) collective-permute-start(bf16[128,768]{1,0:T(8,128)(2,1)S(1)} %multiply_convert_fusion.refs_1_), channel_id=1, source_target_pairs={{0,16},{8,24},{16,0},{24,8},{1,17},{9,25},{17,1},{25,9},{2,18},{10... | collective-permute-start | bytes 589832 | tf_op jit(solution)/shard_map/ppermute | solution.py:173
  127.1 1.5 collective-permute-start.30
  128.7 4.0 %collective-permute-done.28.refs_2_ = bf16[128,768]{1,0:T(8,128)(2,1)S(1)} collective-permute-done((bf16[128,768]{1,0:T(8,128)(2,1)S(1)}, bf16[128,768]{1,0:T(8,128)(2,1)S(1)}, u32[]{:S(2)}, u32[]{:S(2)}) %collective-permute-start.28) | collective-permute-done | bytes 196640 | tf_op jit(solution)/shard_map/ppermute | solution.py:173
  132.8 3.6 %collective-permute-done.29.refs_3_ = bf16[128,768]{1,0:T(8,128)(2,1)S(1)} collective-permute-done((bf16[128,768]{1,0:T(8,128)(2,1)S(1)}, bf16[128,768]{1,0:T(8,128)(2,1)S(1)}, u32[]{:S(2)}, u32[]{:S(2)}) %collective-permute-start.29) | collective-permute-done | bytes 196640 | tf_op jit(solution)/shard_map/ppermute | solution.py:173
  137.4 1.1 copy.20
  138.5 1.4 collective-permute-done.31.refs_5_
  139.9 5.3 %shard_map.121 = (f32[2,192,512]{2,1,0:T(8,128)S(1)}, bf16[2,192,512]{2,1,0:T(8,128)(2,1)S(1)}) custom-call(s32[1]{0:T(128)} %bitcast.refs_0_, bf16[128,768]{1,0:T(8,128)(2,1)S(1)} %multiply_convert_fusion.refs_1_, bf16[128,768]{1,0:T(8,128)(2,1)S(1)} %collective-permute-done.28.refs_2_, bf16[128,768]{1,0:T(8,128)(2,1)S(1)} %collective-permute-done.29.refs_3_, ...), custom_call_target="tpu_custom_call" | custom-call | flops 2516582400 | bytes 8388608 | tf_op jit(solution)/shard_map/pallas_call | solution.py:403
  145.4 1.6 %collective-permute-done.32 = bf16[2,192,512]{2,1,0:T(8,128)(2,1)S(1)} collective-permute-done((bf16[2,192,512]{2,1,0:T(8,128)(2,1)S(1)}, bf16[2,192,512]{2,1,0:T(8,128)(2,1)S(1)}, u32[]{:S(2)}, u32[]{:S(2)}) %collective-permute-start.32) | collective-permute-done | bytes 393248 | tf_op jit(solution)/shard_map/ppermute | solution.py:173
  147.7 6.4 %collective-permute-done.33 = bf16[192,512]{1,0:T(8,128)(2,1)S(1)} collective-permute-done((bf16[192,512]{1,0:T(8,128)(2,1)S(1)}, bf16[192,512]{1,0:T(8,128)(2,1)S(1)}, u32[]{:S(2)}, u32[]{:S(2)}) %collective-permute-start.33) | collective-permute-done | bytes 196640 | tf_op jit(solution)/shard_map/ppermute | solution.py:173
  (139 shorter events, 21.9 us)
Async XLA Ops:
  0.0 20.0 %copy-start.1 = (bf16[1,512,384]{2,1,0:T(8,128)(2,1)S(1)}, bf16[1,512,384]{2,1,0:T(8,128)(2,1)}, u32[]{:S(2)}) copy-start(bf16[1,512,384]{2,1,0:T(8,128)(2,1)} %param.12) | copy-start | bytes 1179652
  0.0 13.3 %copy-start.27 = (s32[4]{0:T(128)S(1)}, s32[4]{0:T(128)}, u32[]{:S(2)}) copy-start(s32[4]{0:T(128)} %param.23) | copy-start | bytes 52
  0.0 17.6 %copy-start.22 = (bf16[1024,192]{0,1:T(8,128)(2,1)S(1)}, bf16[1024,192]{0,1:T(8,128)(2,1)}, u32[]{:S(2)}) copy-start(bf16[1024,192]{0,1:T(8,128)(2,1)} %param.16) | copy-start | bytes 1179652
  2.1 17.9 %copy-start.10 = (bf16[2,192,512]{2,1,0:T(8,128)(2,1)}, bf16[2,192,512]{2,1,0:T(8,128)(2,1)S(1)}, u32[]{:S(2)}) copy-start(bf16[2,192,512]{2,1,0:T(8,128)(2,1)S(1)} %get-tuple-element.41.refs_0_) | copy-start | bytes 1179652
  2.1 16.2 %collective-permute-start.11 = (bf16[2,192,512]{2,1,0:T(8,128)(2,1)S(1)}, bf16[2,192,512]{2,1,0:T(8,128)(2,1)S(1)}, u32[]{:S(2)}, u32[]{:S(2)}) collective-permute-start(bf16[2,192,512]{2,1,0:T(8,128)(2,1)S(1)} %get-tuple-element.41.refs_0_), channel_id=1, source_target_pairs={{0,4},{4,0},{1,5},{5,1},{2,6},{6,2},{3,7},{7,3},{8,12},{12,8},{9,1... | collective-permute-start | bytes 1179656 | tf_op jit(solution)/shard_map/ppermute | solution.py:173
  5.1 20.0 %collective-permute-start.10 = (bf16[2,192,512]{2,1,0:T(8,128)(2,1)S(1)}, bf16[2,192,512]{2,1,0:T(8,128)(2,1)S(1)}, u32[]{:S(2)}, u32[]{:S(2)}) collective-permute-start(bf16[2,192,512]{2,1,0:T(8,128)(2,1)S(1)} %get-tuple-element.41.refs_0_), channel_id=1, source_target_pairs={{0,2},{1,3},{2,0},{3,1},{4,6},{5,7},{6,4},{7,5},{8,10},{9,11},{10,... | collective-permute-start | bytes 1179656 | tf_op jit(solution)/shard_map/ppermute | solution.py:176
  7.7 12.3 %collective-permute-start = (bf16[512,384]{1,0:T(8,128)(2,1)}, bf16[512,384]{1,0:T(8,128)(2,1)S(1)}, u32[]{:S(2)}, u32[]{:S(2)}) collective-permute-start(bf16[512,384]{1,0:T(8,128)(2,1)} %bitcast.67), channel_id=1, source_target_pairs={{0,16},{8,24},{16,0},{24,8},{1,17},{9,25},{17,1},{25,9},{2,18},{10... | collective-permute-start | bytes 1179656 | tf_op jit(solution)/shard_map/ppermute | solution.py:173
  9.2 32.1 %collective-permute-start.6 = (bf16[512,384]{1,0:T(8,128)(2,1)}, bf16[512,384]{1,0:T(8,128)(2,1)S(1)}, u32[]{:S(2)}, u32[]{:S(2)}) collective-permute-start(bf16[512,384]{1,0:T(8,128)(2,1)} %bitcast.68), channel_id=1, source_target_pairs={{0,1},{1,0},{2,3},{3,2},{4,5},{5,4},{6,7},{7,6},{8,9},{9,8},{10,11... | collective-permute-start | bytes 1179656 | tf_op jit(solution)/shard_map/ppermute | solution.py:173
  12.2 18.8 %collective-permute-start.3 = (bf16[384,768]{0,1:T(8,128)(2,1)S(1)}, bf16[384,768]{0,1:T(8,128)(2,1)}, u32[]{:S(2)}, u32[]{:S(2)}) collective-permute-start(bf16[384,768]{0,1:T(8,128)(2,1)S(1)} %copy.19), channel_id=1, source_target_pairs={{0,16},{8,24},{16,0},{24,8},{1,17},{9,25},{17,1},{25,9},{2,18},{10... | collective-permute-start | bytes 1769480 | tf_op jit(solution)/shard_map/ppermute | solution.py:173
  19.2 22.1 %collective-permute-start.12 = (bf16[1,192,512]{2,1,0:T(8,128)(2,1)}, bf16[1,192,512]{2,1,0:T(8,128)(2,1)S(1)}, u32[]{:S(2)}, u32[]{:S(2)}) collective-permute-start(bf16[1,192,512]{2,1,0:T(8,128)(2,1)} %get-tuple-element.24.refs_0_), channel_id=1, source_target_pairs={{0,4},{4,0},{1,5},{5,1},{2,6},{6,2},{3,7},{7,3},{8,12},{12,8},{9,1... | collective-permute-start | bytes 589832 | tf_op jit(solution)/shard_map/ppermute | solution.py:173
  20.0 50.7 %copy-start.2 = (bf16[512,384]{1,0:T(8,128)(2,1)}, bf16[512,384]{1,0:T(8,128)(2,1)S(1)}, u32[]{:S(2)}) copy-start(bf16[512,384]{1,0:T(8,128)(2,1)S(1)} %collective-permute-done.refs_2_) | copy-start | bytes 1179652
  20.0 23.3 %collective-permute-start.1 = (bf16[512,384]{1,0:T(8,128)(2,1)S(1)}, bf16[512,384]{1,0:T(8,128)(2,1)S(1)}, u32[]{:S(2)}, u32[]{:S(2)}) collective-permute-start(bf16[512,384]{1,0:T(8,128)(2,1)S(1)} %bitcast.69), channel_id=1, source_target_pairs={{0,8},{8,0},{16,24},{24,16},{1,9},{9,1},{17,25},{25,17},{2,10},{10... | collective-permute-start | bytes 1179656 | tf_op jit(solution)/shard_map/ppermute | solution.py:173
  25.1 45.5 %copy-start.16 = (bf16[2,192,512]{2,1,0:T(8,128)(2,1)}, bf16[2,192,512]{2,1,0:T(8,128)(2,1)S(1)}, u32[]{:S(2)}) copy-start(bf16[2,192,512]{2,1,0:T(8,128)(2,1)S(1)} %collective-permute-done.10.refs_1_) | copy-start | bytes 1179652
  25.1 19.8 %collective-permute-start.2 = (bf16[512,384]{1,0:T(8,128)(2,1)S(1)}, bf16[512,384]{1,0:T(8,128)(2,1)S(1)}, u32[]{:S(2)}, u32[]{:S(2)}) collective-permute-start(bf16[512,384]{1,0:T(8,128)(2,1)S(1)} %collective-permute-done.refs_2_), channel_id=1, source_target_pairs={{0,8},{8,0},{16,24},{24,16},{1,9},{9,1},{17,25},{25,17},{2,10},{10... | collective-permute-start | bytes 1179656 | tf_op jit(solution)/shard_map/ppermute | solution.py:173
  31.0 16.2 %collective-permute-start.14 = (bf16[2,192,512]{2,1,0:T(8,128)(2,1)S(1)}, bf16[2,192,512]{2,1,0:T(8,128)(2,1)S(1)}, u32[]{:S(2)}, u32[]{:S(2)}) collective-permute-start(bf16[2,192,512]{2,1,0:T(8,128)(2,1)S(1)} %collective-permute-done.10.refs_1_), channel_id=1, source_target_pairs={{0,4},{4,0},{1,5},{5,1},{2,6},{6,2},{3,7},{7,3},{8,12},{12,8},{9,1... | collective-permute-start | bytes 1179656 | tf_op jit(solution)/shard_map/ppermute | solution.py:173
  41.3 29.4 %copy-start.8 = (bf16[512,384]{1,0:T(8,128)(2,1)}, bf16[512,384]{1,0:T(8,128)(2,1)S(1)}, u32[]{:S(2)}) copy-start(bf16[512,384]{1,0:T(8,128)(2,1)S(1)} %collective-permute-done.6.refs_4_) | copy-start | bytes 1179652
  41.3 24.7 %collective-permute-start.4 = (bf16[384,768]{0,1:T(8,128)(2,1)}, bf16[384,768]{0,1:T(8,128)(2,1)}, u32[]{:S(2)}, u32[]{:S(2)}) collective-permute-start(bf16[384,768]{0,1:T(8,128)(2,1)} %copy.18), channel_id=1, source_target_pairs={{0,8},{8,0},{16,24},{24,16},{1,9},{9,1},{17,25},{25,17},{2,10},{10... | collective-permute-start | bytes 1769480 | tf_op jit(solution)/shard_map/ppermute | solution.py:173
  41.3 29.4 %copy-start.20 = (bf16[1,192,512]{2,1,0:T(8,128)(2,1)}, bf16[1,192,512]{2,1,0:T(8,128)(2,1)S(1)}, u32[]{:S(2)}) copy-start(bf16[1,192,512]{2,1,0:T(8,128)(2,1)S(1)} %collective-permute-done.12.refs_2_) | copy-start | bytes 589828
  41.3 24.7 %collective-permute-start.5 = (bf16[384,768]{0,1:T(8,128)(2,1)}, bf16[384,768]{0,1:T(8,128)(2,1)}, u32[]{:S(2)}, u32[]{:S(2)}) collective-permute-start(bf16[384,768]{0,1:T(8,128)(2,1)} %collective-permute-done.3), channel_id=1, source_target_pairs={{0,8},{8,0},{16,24},{24,16},{1,9},{9,1},{17,25},{25,17},{2,10},{10... | collective-permute-start | bytes 1769480 | tf_op jit(solution)/shard_map/ppermute | solution.py:173
  43.3 27.4 %copy-start.4 = (bf16[512,384]{1,0:T(8,128)(2,1)}, bf16[512,384]{1,0:T(8,128)(2,1)S(1)}, u32[]{:S(2)}) copy-start(bf16[512,384]{1,0:T(8,128)(2,1)S(1)} %collective-permute-done.1.refs_1_) | copy-start | bytes 1179652
  43.3 14.2 %collective-permute-start.13 = (bf16[2,192,512]{2,1,0:T(8,128)(2,1)}, bf16[2,192,512]{2,1,0:T(8,128)(2,1)}, u32[]{:S(2)}, u32[]{:S(2)}) collective-permute-start(bf16[2,192,512]{2,1,0:T(8,128)(2,1)} %get-tuple-element.23), channel_id=1, source_target_pairs={{0,1},{1,2},{2,3},{3,0},{4,5},{5,6},{6,7},{7,4},{8,9},{9,10},{10,1... | collective-permute-start | bytes 1179656 | tf_op jit(solution)/shard_map/ppermute | solution.py:176
  44.9 25.8 %copy-start.6 = (bf16[512,384]{1,0:T(8,128)(2,1)}, bf16[512,384]{1,0:T(8,128)(2,1)S(1)}, u32[]{:S(2)}) copy-start(bf16[512,384]{1,0:T(8,128)(2,1)S(1)} %collective-permute-done.2.refs_3_) | copy-start | bytes 1179652
  44.9 19.6 %collective-permute-start.18 = (bf16[2,192,512]{2,1,0:T(8,128)(2,1)}, bf16[2,192,512]{2,1,0:T(8,128)(2,1)}, u32[]{:S(2)}, u32[]{:S(2)}) collective-permute-start(bf16[2,192,512]{2,1,0:T(8,128)(2,1)} %get-tuple-element.23), channel_id=1, source_target_pairs={{0,3},{1,0},{2,1},{3,2},{4,7},{5,4},{6,5},{7,6},{8,11},{9,8},{10,9... | collective-permute-start | bytes 1179656 | tf_op jit(solution)/shard_map/ppermute | solution.py:176
  47.2 23.5 %copy-start.18 = (bf16[2,192,512]{2,1,0:T(8,128)(2,1)}, bf16[2,192,512]{2,1,0:T(8,128)(2,1)S(1)}, u32[]{:S(2)}) copy-start(bf16[2,192,512]{2,1,0:T(8,128)(2,1)S(1)} %collective-permute-done.14.refs_5_) | copy-start | bytes 1179652
  47.2 20.0 %collective-permute-start.7 = (bf16[512,384]{1,0:T(8,128)(2,1)S(1)}, bf16[512,384]{1,0:T(8,128)(2,1)S(1)}, u32[]{:S(2)}, u32[]{:S(2)}) collective-permute-start(bf16[512,384]{1,0:T(8,128)(2,1)S(1)} %collective-permute-done.6.refs_4_), channel_id=1, source_target_pairs={{0,16},{8,24},{16,0},{24,8},{1,17},{9,25},{17,1},{25,9},{2,18},{10... | collective-permute-start | bytes 1179656 | tf_op jit(solution)/shard_map/ppermute | solution.py:173
  57.5 38.0 %collective-permute-start.19 = (bf16[2,192,512]{2,1,0:T(8,128)(2,1)}, bf16[2,192,512]{2,1,0:T(8,128)(2,1)}, u32[]{:S(2)}, u32[]{:S(2)}) collective-permute-start(bf16[2,192,512]{2,1,0:T(8,128)(2,1)} %collective-permute-done.13.refs_3_), channel_id=1, source_target_pairs={{0,4},{4,0},{1,5},{5,1},{2,6},{6,2},{3,7},{7,3},{8,12},{12,8},{9,1... | collective-permute-start | bytes 1179656 | tf_op jit(solution)/shard_map/ppermute | solution.py:173
  64.5 30.9 %collective-permute-start.20 = (bf16[2,192,512]{2,1,0:T(8,128)(2,1)}, bf16[2,192,512]{2,1,0:T(8,128)(2,1)}, u32[]{:S(2)}, u32[]{:S(2)}) collective-permute-start(bf16[2,192,512]{2,1,0:T(8,128)(2,1)} %collective-permute-done.18.refs_4_), channel_id=1, source_target_pairs={{0,4},{4,0},{1,5},{5,1},{2,6},{6,2},{3,7},{7,3},{8,12},{12,8},{9,1... | collective-permute-start | bytes 1179656 | tf_op jit(solution)/shard_map/ppermute | solution.py:173
  66.0 14.7 %collective-permute-start.15 = (bf16[1,192,512]{2,1,0:T(8,128)(2,1)}, bf16[1,192,512]{2,1,0:T(8,128)(2,1)}, u32[]{:S(2)}, u32[]{:S(2)}) collective-permute-start(bf16[1,192,512]{2,1,0:T(8,128)(2,1)} %get-tuple-element.24.refs_0_), channel_id=1, source_target_pairs={{0,2},{1,3},{2,0},{3,1},{4,6},{5,7},{6,4},{7,5},{8,10},{9,11},{10,... | collective-permute-start | bytes 589832 | tf_op jit(solution)/shard_map/ppermute | solution.py:176
  67.1 6.6 %collective-permute-start.8 = (bf16[512,384]{1,0:T(8,128)(2,1)S(1)}, bf16[512,384]{1,0:T(8,128)(2,1)S(1)}, u32[]{:S(2)}, u32[]{:S(2)}) collective-permute-start(bf16[512,384]{1,0:T(8,128)(2,1)S(1)} %collective-permute-done.6.refs_4_), channel_id=1, source_target_pairs={{0,8},{8,0},{16,24},{24,16},{1,9},{9,1},{17,25},{25,17},{2,10},{10... | collective-permute-start | bytes 1179656 | tf_op jit(solution)/shard_map/ppermute | solution.py:173
  67.1 6.6 %collective-permute-start.9 = (bf16[512,384]{1,0:T(8,128)(2,1)S(1)}, bf16[512,384]{1,0:T(8,128)(2,1)S(1)}, u32[]{:S(2)}, u32[]{:S(2)}) collective-permute-start(bf16[512,384]{1,0:T(8,128)(2,1)S(1)} %collective-permute-done.7.refs_6_), channel_id=1, source_target_pairs={{0,8},{8,0},{16,24},{24,16},{1,9},{9,1},{17,25},{25,17},{2,10},{10... | collective-permute-start | bytes 1179656 | tf_op jit(solution)/shard_map/ppermute | solution.py:173
  80.8 10.0 %collective-permute-start.16 = (bf16[1,192,512]{2,1,0:T(8,128)(2,1)}, bf16[1,192,512]{2,1,0:T(8,128)(2,1)}, u32[]{:S(2)}, u32[]{:S(2)}) collective-permute-start(bf16[1,192,512]{2,1,0:T(8,128)(2,1)} %get-tuple-element.25), channel_id=1, source_target_pairs={{0,1},{1,2},{2,3},{3,0},{4,5},{5,6},{6,7},{7,4},{8,9},{9,10},{10,1... | collective-permute-start | bytes 589832 | tf_op jit(solution)/shard_map/ppermute | solution.py:176
  82.3 11.1 %collective-permute-start.17 = (bf16[1,192,512]{2,1,0:T(8,128)(2,1)}, bf16[1,192,512]{2,1,0:T(8,128)(2,1)}, u32[]{:S(2)}, u32[]{:S(2)}) collective-permute-start(bf16[1,192,512]{2,1,0:T(8,128)(2,1)} %get-tuple-element.25), channel_id=1, source_target_pairs={{0,3},{1,0},{2,1},{3,2},{4,7},{5,4},{6,5},{7,6},{8,11},{9,8},{10,9... | collective-permute-start | bytes 589832 | tf_op jit(solution)/shard_map/ppermute | solution.py:176
  84.7 20.5 %copy-start = (bf16[768,1536]{1,0:T(8,128)(2,1)S(1)}, bf16[768,1536]{1,0:T(8,128)(2,1)}, u32[]{:S(2)}) copy-start(bf16[768,1536]{1,0:T(8,128)(2,1)} %fusion.proj_ref) | copy-start | bytes 7077892
  84.7 20.4 %collective-permute-start.21 = (bf16[1,192,512]{2,1,0:T(8,128)(2,1)}, bf16[1,192,512]{2,1,0:T(8,128)(2,1)S(1)}, u32[]{:S(2)}, u32[]{:S(2)}) collective-permute-start(bf16[1,192,512]{2,1,0:T(8,128)(2,1)} %collective-permute-done.15.refs_1_), channel_id=1, source_target_pairs={{0,4},{4,0},{1,5},{5,1},{2,6},{6,2},{3,7},{7,3},{8,12},{12,8},{9,1... | collective-permute-start | bytes 589832 | tf_op jit(solution)/shard_map/ppermute | solution.py:173
  93.4 11.8 %collective-permute-start.22 = (bf16[1,192,512]{2,1,0:T(8,128)(2,1)}, bf16[1,192,512]{2,1,0:T(8,128)(2,1)S(1)}, u32[]{:S(2)}, u32[]{:S(2)}) collective-permute-start(bf16[1,192,512]{2,1,0:T(8,128)(2,1)} %collective-permute-done.16.refs_3_), channel_id=1, source_target_pairs={{0,4},{4,0},{1,5},{5,1},{2,6},{6,2},{3,7},{7,3},{8,12},{12,8},{9,1... | collective-permute-start | bytes 589832 | tf_op jit(solution)/shard_map/ppermute | solution.py:173
  93.9 11.3 %collective-permute-start.23 = (bf16[1,192,512]{2,1,0:T(8,128)(2,1)}, bf16[1,192,512]{2,1,0:T(8,128)(2,1)S(1)}, u32[]{:S(2)}, u32[]{:S(2)}) collective-permute-start(bf16[1,192,512]{2,1,0:T(8,128)(2,1)} %collective-permute-done.17.refs_4_), channel_id=1, source_target_pairs={{0,4},{4,0},{1,5},{5,1},{2,6},{6,2},{3,7},{7,3},{8,12},{12,8},{9,1... | collective-permute-start | bytes 589832 | tf_op jit(solution)/shard_map/ppermute | solution.py:173
  109.4 2.4 %collective-permute-start.24 = (bf16[2,2,128,768]{3,2,1,0:T(8,128)(2,1)S(1)}, bf16[2,2,128,768]{3,2,1,0:T(8,128)(2,1)S(1)}, u32[]{:S(2)}, u32[]{:S(2)}) collective-permute-start(bf16[2,2,128,768]{3,2,1,0:T(8,128)(2,1)S(1)} %get-tuple-element.28), channel_id=1, source_target_pairs={{0,8},{8,0},{16,24},{24,16},{1,9},{9,1},{17,25},{25,17},{2,10},{10... | collective-permute-start | bytes 2359304 | tf_op jit(solution)/shard_map/ppermute | solution.py:173
  112.0 11.2 %collective-permute-start.25 = (bf16[128,768]{1,0:T(8,128)(2,1)S(1)}, bf16[128,768]{1,0:T(8,128)(2,1)S(1)}, u32[]{:S(2)}, u32[]{:S(2)}) collective-permute-start(bf16[128,768]{1,0:T(8,128)(2,1)S(1)} %get-tuple-element.43), channel_id=1, source_target_pairs={{0,16},{8,24},{16,0},{24,8},{1,17},{9,25},{17,1},{25,9},{2,18},{10... | collective-permute-start | bytes 589832 | tf_op jit(solution)/shard_map/ppermute | solution.py:173
  113.6 9.7 %collective-permute-start.27 = (bf16[128,768]{1,0:T(8,128)(2,1)S(1)}, bf16[128,768]{1,0:T(8,128)(2,1)S(1)}, u32[]{:S(2)}, u32[]{:S(2)}) collective-permute-start(bf16[128,768]{1,0:T(8,128)(2,1)S(1)} %get-tuple-element.44), channel_id=1, source_target_pairs={{0,17},{1,16},{2,19},{3,18},{8,25},{9,24},{10,27},{11,26},{16,1},{... | collective-permute-start | bytes 589832 | tf_op jit(solution)/shard_map/ppermute | solution.py:173
  114.4 10.0 %collective-permute-start.26 = (bf16[128,768]{1,0:T(8,128)(2,1)S(1)}, bf16[128,768]{1,0:T(8,128)(2,1)S(1)}, u32[]{:S(2)}, u32[]{:S(2)}) collective-permute-start(bf16[128,768]{1,0:T(8,128)(2,1)S(1)} %fusion.19), channel_id=1, source_target_pairs={{0,1},{1,0},{2,3},{3,2},{4,5},{5,4},{6,7},{7,6},{8,9},{9,8},{10,11... | collective-permute-start | bytes 589832 | tf_op jit(solution)/shard_map/ppermute | solution.py:173
  124.7 15.2 %copy-start.12 = (s32[512,4]{1,0:T(8,128)S(1)}, s32[512,4]{1,0:T(8,128)}, u32[]{:S(2)}) copy-start(s32[512,4]{1,0:T(8,128)} %fusion.17.refs_9_) | copy-start | bytes 24580
  124.7 15.2 %copy-start.13 = (bf16[3,768,192]{1,2,0:T(8,128)(2,1)S(1)}, bf16[3,768,192]{1,2,0:T(8,128)(2,1)}, u32[]{:S(2)}) copy-start(bf16[3,768,192]{1,2,0:T(8,128)(2,1)} %param.19) | copy-start | bytes 2654212
  125.0 7.7 %collective-permute-start.28 = (bf16[128,768]{1,0:T(8,128)(2,1)S(1)}, bf16[128,768]{1,0:T(8,128)(2,1)S(1)}, u32[]{:S(2)}, u32[]{:S(2)}) collective-permute-start(bf16[128,768]{1,0:T(8,128)(2,1)S(1)} %multiply_convert_fusion.refs_1_), channel_id=1, source_target_pairs={{0,16},{8,24},{16,0},{24,8},{1,17},{9,25},{17,1},{25,9},{2,18},{10... | collective-permute-start | bytes 589832 | tf_op jit(solution)/shard_map/ppermute | solution.py:173
  126.6 9.8 %collective-permute-start.29 = (bf16[128,768]{1,0:T(8,128)(2,1)S(1)}, bf16[128,768]{1,0:T(8,128)(2,1)S(1)}, u32[]{:S(2)}, u32[]{:S(2)}) collective-permute-start(bf16[128,768]{1,0:T(8,128)(2,1)S(1)} %multiply_convert_fusion.refs_1_), channel_id=1, source_target_pairs={{0,4},{4,0},{1,5},{5,1},{2,6},{6,2},{3,7},{7,3},{8,12},{12,8},{9,1... | collective-permute-start | bytes 589832 | tf_op jit(solution)/shard_map/ppermute | solution.py:173
  127.1 9.3 %collective-permute-start.30 = (bf16[128,768]{1,0:T(8,128)(2,1)S(1)}, bf16[128,768]{1,0:T(8,128)(2,1)S(1)}, u32[]{:S(2)}, u32[]{:S(2)}) collective-permute-start(bf16[128,768]{1,0:T(8,128)(2,1)S(1)} %multiply_convert_fusion.refs_1_), channel_id=1, source_target_pairs={{0,20},{4,16},{8,28},{12,24},{16,4},{20,0},{24,12},{28,8},{1,21},{... | collective-permute-start | bytes 589832 | tf_op jit(solution)/shard_map/ppermute | solution.py:173
  137.4 2.5 %collective-permute-start.31 = (bf16[4,128,768]{2,1,0:T(8,128)(2,1)}, bf16[4,128,768]{2,1,0:T(8,128)(2,1)S(1)}, u32[]{:S(2)}, u32[]{:S(2)}) collective-permute-start(bf16[4,128,768]{2,1,0:T(8,128)(2,1)} %pad_maximum_fusion.1), channel_id=1, source_target_pairs={{0,8},{8,0},{16,24},{24,16},{1,9},{9,1},{17,25},{25,17},{2,10},{10... | collective-permute-start | bytes 2359304 | tf_op jit(solution)/shard_map/ppermute | solution.py:173
  145.2 1.8 %collective-permute-start.32 = (bf16[2,192,512]{2,1,0:T(8,128)(2,1)S(1)}, bf16[2,192,512]{2,1,0:T(8,128)(2,1)S(1)}, u32[]{:S(2)}, u32[]{:S(2)}) collective-permute-start(bf16[2,192,512]{2,1,0:T(8,128)(2,1)S(1)} %get-tuple-element.30), channel_id=1, source_target_pairs={{0,8},{8,0},{16,24},{24,16},{1,9},{9,1},{17,25},{25,17},{2,10},{10... | collective-permute-start | bytes 1179656 | tf_op jit(solution)/shard_map/ppermute | solution.py:173
  147.1 7.0 %collective-permute-start.33 = (bf16[192,512]{1,0:T(8,128)(2,1)S(1)}, bf16[192,512]{1,0:T(8,128)(2,1)S(1)}, u32[]{:S(2)}, u32[]{:S(2)}) collective-permute-start(bf16[192,512]{1,0:T(8,128)(2,1)S(1)} %fusion.21), channel_id=1, source_target_pairs={{0,16},{8,24},{16,0},{24,8},{1,17},{9,25},{17,1},{25,9},{2,18},{10... | collective-permute-start | bytes 589832 | tf_op jit(solution)/shard_map/ppermute | solution.py:173
  (14 other events, 65.9 us)

commit v8 on v7

--- a/solution.py
+++ b/solution.py
@@ -26,17 +26,14 @@
     return (slide, index - before)
 
 
-def attend_kernel(sec_ref, near_ref, *refs, heads, masks):
-    far, refs = refs[:3], refs[3:]
-    core_ref, w_ref, out_w_ref, emb_ref, q_ref, k_ref, keep_ref, send_ref = refs
-    core, side = sec_ref[0] % 2, sec_ref[0] // 2
-    own = near_ref.shape[0]
-    keys = jnp.concatenate(
-        [near_ref[...], far[0][...], core_ref[0], core_ref[1], far[1][...], far[2][...]]
-        + [core_ref[2], core_ref[3]],
-        axis=0,
-    )
-    count, rows = keys.shape[0], q_ref.shape[0]
+def attend_kernel(*refs, heads, masks):
+    blocks, (w_ref, out_w_ref, emb_ref, code_ref, keep_ref, send_ref) = refs[:-6], refs[-6:]
+    sec = lax.axis_index("section")
+    core, side = sec % 2, sec // 2
+    own = blocks[0].shape[0]
+    keys = jnp.concatenate([block[...] for block in blocks], axis=0)
+    count, rows = keys.shape[0], own * len(masks)
+    q_code = jnp.transpose(code_ref[:, :rows])
     width = w_ref.shape[1]
     size = width // heads
     scale = math.log2(math.e) / math.sqrt(size)
@@ -59,7 +56,7 @@
             (((1,), (1,)), ((), ())),
             preferred_element_type=jnp.float32,
         )
-        ok = (q_ref[:, h : h + 1] == k_ref[h : h + 1, :]) | diag
+        ok = (q_code[:, h : h + 1] == code_ref[heads + h : heads + h + 1, :]) | diag
         scores = jnp.where(ok, scores, NEG)
         top = jnp.max(scores, axis=1, keepdims=True)
         weight = jnp.exp2((scores - top) * scale)
@@ -74,7 +71,7 @@
         piece = part[:, block * own : (block + 1) * own]
         if block == 0:
             piece = piece + emb
-        at = pl.ds(pl.multiple_of((mask ^ sec_ref[0]) * own, own), own)
+        at = pl.ds(pl.multiple_of((mask ^ sec) * own, own), own)
         for j in range(part.shape[0] // width // 2):
             low = piece[2 * j * width : (2 * j + 1) * width]
             high = piece[(2 * j + 1) * width : (2 * j + 2) * width]
@@ -83,7 +80,7 @@
 
 
 def norm_kernel(gain_ref, *refs):
-    out_ref = refs[-1]
+    out_ref, sec = refs[-1], lax.axis_index("section")
     parts = (len(refs) - 1) // 2
     tokens, width = refs[0].shape
     step = 64
@@ -99,7 +96,7 @@
             factor = lax.rsqrt(square / (width * parts) + 1e-06)
             to = pl.ds(pl.multiple_of(pack * tokens + i * step, step), step)
             for m, part in enumerate(x):
-                out_ref[to, m * width : (m + 1) * width] = (part * factor * gain_ref[m]).astype(
+                out_ref[to, m * width : (m + 1) * width] = (part * factor * gain_ref[m ^ sec]).astype(
                     out_ref.dtype
                 )
             return carry
@@ -107,12 +104,12 @@
         lax.fori_loop(0, tokens // step, rows, 0, unroll=2)
 
 
-def gate_kernel(at_ref, normed_ref, *refs):
+def gate_kernel(normed_ref, *refs, places):
     blocks, (out_ref, all_ref, sem) = refs[:-3], refs[-3:]
     rows = blocks[0].shape[1]
     copies = []
-    for i, block in enumerate(blocks):
-        to = pl.ds(pl.multiple_of(at_ref[i], rows), rows)
+    for i, (block, at) in enumerate(zip(blocks, places(rows))):
+        to = pl.ds(pl.multiple_of(at, rows), rows)
         copies.append(pltpu.make_async_copy(block, all_ref.at[:, to, :], sem.at[i]))
         copies[-1].start()
     for copy in copies:
@@ -127,23 +124,30 @@
         )
 
 
-def project_kernel(at_ref, core_ref, hidden_ref, proj_ref, *refs):
-    blocks, (send_ref, keep_ref, all_ref, sem) = refs[:-4], refs[-4:]
+def project_kernel(hidden_ref, *refs, places, parts):
+    proj, blocks, (send_ref, keep_ref, all_ref, sem) = refs[:parts], refs[parts:-4], refs[-4:]
     rows = blocks[0].shape[1]
     copies = []
-    for i, block in enumerate(blocks):
-        to = pl.ds(pl.multiple_of(at_ref[i], rows), rows)
+    for i, (block, at) in enumerate(zip(blocks, places(rows))):
+        to = pl.ds(pl.multiple_of(at, rows), rows)
         copies.append(pltpu.make_async_copy(block.at[0], all_ref.at[to, :], sem.at[i]))
         copies[-1].start()
     for copy in copies:
         copy.wait()
-    folded = jnp.dot(proj_ref[...], all_ref[...], preferred_element_type=jnp.float32)
-    folded = folded.astype(jnp.bfloat16)
+    depth = proj[0].shape[1]
+    folded = sum(
+        jnp.dot(
+            proj[m][...],
+            all_ref[m * depth : (m + 1) * depth],
+            preferred_element_type=jnp.float32,
+        )
+        for m in range(parts)
+    ).astype(jnp.bfloat16)
     packs, sides, _, own, units = hidden_ref.shape
-    core = core_ref[0]
+    core = lax.axis_index("section") % 2
     for target, which in ((send_ref, 1 - core), (keep_ref, core)):
         x = jnp.concatenate(
-            [hidden_ref[p, x, which] for p in range(packs) for x in range(sides)], axis=0
+            [hidden_ref[p, j, which] for p in range(packs) for j in range(sides)], axis=0
         )
         x = lax.dot_general(
             x, folded, (((1,), (1,)), ((), ())), preferred_element_type=jnp.float32
@@ -254,123 +258,131 @@
 
         k_block, picked = codes(k_idx)
         k_code = jnp.where(picked, k_block, -1)
-        q_code = codes(q_idx)[0].T
-
-        gain = jnp.stack(absolute(jnp.split(tile_gain, n_sec)))
+        code = jnp.concatenate([k_block, k_code], axis=0)
+
         own_at = sec * own_rows
         vmem = pl.BlockSpec(memory_space=pltpu.VMEM)
         anywhere = pl.BlockSpec(memory_space=pl.ANY)
-        smem = pl.BlockSpec(memory_space=pltpu.SMEM)
-
-        def residual_of(blocks, proj):
-            rows = [lax.dynamic_slice_in_dim(block, own_at, own_rows, 0) for block in blocks]
-            return jnp.dot(
-                jnp.concatenate(rows, axis=1), proj, preferred_element_type=jnp.float32
+        whole_vmem = pltpu.CompilerParams(vmem_limit_bytes=58 * 2**20)
+
+        def residual_of(blocks, proj_t):
+            return sum(
+                lax.dot_general(
+                    lax.dynamic_slice_in_dim(block, own_at, own_rows, 0),
+                    matrix,
+                    (((1,), (1,)), ((), ())),
+                    preferred_element_type=jnp.float32,
+                )
+                for block, matrix in zip(blocks, proj_t)
             )
 
         if ordered:
             g, d = {(0, 0): pair_same}, {(0, 0): down_same}
             beside = flip(mine, dp=1)
             mine_x = flip(mine, section=2)
-            proj_x = flip(w_proj, section=2)
             g[0, 2] = rotate(pair_same, 2)
             g[1, 0] = flip(pair_same, seq=1)
             d[1, 0] = flip(after(down_same, g[1, 0]), seq=1)
-            mine_c = flip(after(mine, mine_x), section=1)
-            mine_xc = flip(mine_x, section=1)
-            beside_x = flip(after(beside, mine_c, mine_xc), section=2)
+            mine_c = flip(after(mine, mine_x, g[0, 2]), section=1)
+            mine_xc = flip(after(mine_x, g[0, 2]), section=1)
+            beside_x = flip(beside, section=2)
             for k in (1, 3):
-                g[0, k] = rotate(after(pair_other, g[0, 2], d[1, 0], proj_x), k)
+                g[0, k] = rotate(after(pair_other, g[0, 2], d[1, 0]), k)
             g[1, 2] = flip(g[0, 2], seq=1)
-            proj_c = flip(after(w_proj, proj_x), section=1)
-            proj_xc = flip(proj_x, section=1)
             beside_c = flip(after(beside, beside_x), section=1)
             beside_xc = flip(beside_x, section=1)
-            d[0, 2] = rotate(
-                after(down_same, g[0, 1], g[1, 2], proj_c, proj_xc, k_code, q_code), 2
-            )
+            proj = after(w_proj.T, beside)
+            proj_x = flip(after(proj, beside_x, g[0, 2]), section=2)
+            d[0, 2] = rotate(after(down_same, g[0, 1], g[1, 2], mine_c, mine_xc, code), 2)
+            proj_c = flip(after(proj, proj_x), section=1)
+            proj_xc = flip(proj_x, section=1)
             g[1, 1], g[1, 3] = flip(g[0, 1], seq=1), flip(g[0, 3], seq=1)
             normed = pl.pallas_call(
                 norm_kernel,
                 out_shape=jax.ShapeDtypeStruct((2 * tokens, feats * n_sec), jnp.bfloat16),
                 in_specs=[vmem] * 9,
                 out_specs=vmem,
-                compiler_params=pltpu.CompilerParams(vmem_limit_bytes=16 * 2**20),
+                compiler_params=whole_vmem,
                 cost_estimate=pl.CostEstimate(
                     flops=16 * tokens * feats * n_sec,
                     bytes_accessed=8 * tokens * feats * n_sec,
                     transcendentals=2 * tokens,
                 ),
             )(
-                gain[:, None, :],
+                tile_gain.reshape(n_sec, 1, feats),
                 *(mine, mine_c, mine_x, mine_xc),
                 *(beside, beside_c, beside_x, beside_xc),
             )
-            proj = jnp.concatenate([w_proj, proj_c, proj_x, proj_xc], axis=0)
-            proj_t = proj.T
-            residual = residual_of((mine, mine_c, mine_x, mine_xc), proj)
+            proj = [proj, proj_c, proj_x, proj_xc]
+            out_w = w_out.T
             for k in (1, 3):
-                d[0, k] = rotate(after(down_other, d[0, 2], normed, proj_t, residual), k)
+                d[0, k] = rotate(after(down_other, d[0, 2], normed, proj_c, proj_xc, out_w), k)
             d[1, 2], d[1, 1], d[1, 3] = (flip(d[0, k], seq=1) for k in (2, 1, 3))
 
             order = list(g)
-            places = jnp.stack([row_of(y, k, pair.shape[1]) for y, k in order])
+
+            def places(rows):
+                return [row_of(y, k, rows) for y, k in order]
+
             normed = after(normed, d[0, 1], d[0, 3])
             hidden = pl.pallas_call(
-                gate_kernel,
+                lambda *refs: gate_kernel(*refs, places=places),
                 out_shape=jax.ShapeDtypeStruct((2 * tokens, half), jnp.bfloat16),
-                in_specs=[smem, vmem] + [anywhere] * len(order),
+                in_specs=[vmem] + [anywhere] * len(order),
                 out_specs=vmem,
                 scratch_shapes=[
                     pltpu.VMEM((2, feats * n_sec, half), jnp.bfloat16),
                     pltpu.SemaphoreType.DMA((len(order),)),
                 ],
-                compiler_params=pltpu.CompilerParams(vmem_limit_bytes=24 * 2**20),
+                compiler_params=whole_vmem,
                 cost_estimate=pl.CostEstimate(
                     flops=8 * tokens * feats * n_sec * half,
                     bytes_accessed=8 * 2**20,
                     transcendentals=2 * tokens * half,
                 ),
-            )(places, normed, *(g[at] for at in order))
+            )(normed, *(g[at] for at in order))
             hidden = hidden.reshape(2, n_sec // 2, 2, own_rows, half)
-            sums = (2, n_sec // 2, own_rows, proj.shape[1])
+            sums = (2, n_sec // 2, own_rows, w_proj.shape[1])
             send, kept = pl.pallas_call(
-                project_kernel,
+                lambda *refs: project_kernel(*refs, places=places, parts=n_sec),
                 out_shape=[
                     jax.ShapeDtypeStruct(sums, jnp.bfloat16),
                     jax.ShapeDtypeStruct(sums, jnp.float32),
                 ],
-                in_specs=[smem, smem, vmem, vmem] + [anywhere] * len(order),
+                in_specs=[vmem] * (1 + n_sec) + [anywhere] * len(order),
                 out_specs=[vmem] * 2,
                 scratch_shapes=[
                     pltpu.VMEM((feats * n_sec, half), jnp.bfloat16),
                     pltpu.SemaphoreType.DMA((len(order),)),
                 ],
-                compiler_params=pltpu.CompilerParams(vmem_limit_bytes=24 * 2**20),
+                compiler_params=whole_vmem,
                 cost_estimate=pl.CostEstimate(
-                    flops=2 * half * proj.shape[1] * (feats * n_sec + 2 * tokens),
+                    flops=2 * half * w_proj.shape[1] * (feats * n_sec + 2 * tokens),
                     bytes_accessed=8 * 2**20,
                     transcendentals=0,
                 ),
-            )(places, core[None], hidden, proj_t, *(d[at] for at in order))
+            )(hidden, *proj, *(d[at] for at in order))
+            tiles = [mine, mine_c, mine_x, mine_xc]
         else:
             gate_up = gather_rows(pair_same, pair_other, seq_at, dp_at)
             down_all = gather_rows(down_same, down_other, seq_at, dp_at)[0]
             blocks = gather_section(jnp.concatenate([mine, flip(mine, dp=1)], axis=0))
-            proj = jnp.concatenate(gather_section(w_proj), axis=0)
-            residual = residual_of([block[:tokens] for block in blocks], proj)
+            proj = gather_section(w_proj.T)
+            tiles = [block[:tokens] for block in blocks]
             rows = jnp.concatenate(blocks, axis=1).astype(jnp.float32)
-            normed = layer_norm(rows, gain.reshape(-1)).astype(jnp.bfloat16)
+            gain = jnp.concatenate(absolute(jnp.split(tile_gain, n_sec)))
+            normed = layer_norm(rows, gain).astype(jnp.bfloat16)
             gate = jnp.dot(normed, gate_up[0], preferred_element_type=jnp.float32)
             up = jnp.dot(normed, gate_up[1], preferred_element_type=jnp.float32)
             hidden = (jax.nn.silu(gate) * up).astype(jnp.bfloat16)
-            folded = lax.dot_general(
-                down_all, proj, (((0,), (0,)), ((), ())), preferred_element_type=jnp.float32
+            folded = jnp.dot(
+                jnp.concatenate(proj, axis=1), down_all, preferred_element_type=jnp.float32
             ).astype(jnp.bfloat16)
-            sums = jnp.dot(hidden, folded, preferred_element_type=jnp.float32)
-            sums = sums.reshape(2, n_sec // 2, 2, own_rows, proj.shape[1])
+            sums = jnp.dot(hidden, folded.T, preferred_element_type=jnp.float32)
+            sums = sums.reshape(2, n_sec // 2, 2, own_rows, w_proj.shape[1])
             send = lax.dynamic_index_in_dim(sums, 1 - core, 2, False).astype(jnp.bfloat16)
             kept = lax.dynamic_index_in_dim(sums, core, 2, False)
+            out_w = w_out.T
 
         kept = kept + flip(send, section=1).astype(jnp.float32)
         here = lax.dynamic_index_in_dim(kept, side, 1, False)
@@ -378,8 +390,9 @@
         from_x = flip(there[0], section=2)
         from_z = flip(here[1].astype(jnp.bfloat16), dp=1)
         from_xz = flip(there[1], section=2, dp=1)
+        tiles = [after(tile, kept) for tile in tiles]
         emb = (
-            residual
+            residual_of(tiles, proj)
             + here[0]
             + from_x.astype(jnp.float32)
             + from_z.astype(jnp.float32)
@@ -388,12 +401,14 @@
         slide_normed = layer_norm(emb, slide_gain).astype(jnp.bfloat16)
 
         if n_seq == 2:
-            near = [
+            keys = [
+                slide_normed,
                 flip(slide_normed, section=2),
                 flip(slide_normed, seq=1),
                 flip(slide_normed, section=2, seq=1),
             ]
-            from_core = flip(jnp.stack([slide_normed] + near), section=1)
+            others = [flip(block, section=1) for block in keys]
+            keys = keys[:2] + others[:2] + keys[2:] + others[2:]
         else:
             keys = lax.all_gather(slide_normed, ("seq", "section"), axis=0, tiled=True)
 
@@ -406,7 +421,7 @@
                     jax.ShapeDtypeStruct((2, width, tokens), jnp.float32),
                     jax.ShapeDtypeStruct((2, width, tokens), jnp.bfloat16),
                 ],
-                in_specs=[smem] + [vmem] * 10,
+                in_specs=[vmem] * 12,
                 out_specs=[vmem] * 2,
                 compiler_params=pltpu.CompilerParams(vmem_limit_bytes=40 * 2**20),
                 cost_estimate=pl.CostEstimate(
@@ -414,7 +429,7 @@
                     bytes_accessed=8 * 2**20,
                     transcendentals=local_heads * tokens * count,
                 ),
-            )(sec[None], slide_normed, *near, from_core, qkv, w_out.T, emb, q_code, k_code)
+            )(*keys, qkv, out_w, emb, code)
         else:
 
             def by_head(x, matrix):
@@ -434,7 +449,7 @@
             att = lax.map(
                 one_head,
                 (by_head(queries, qkv[0]), by_head(keys, qkv[1]), by_head(keys, qkv[2]))
-                + (q_code.T, k_code),
+                + (codes(q_idx)[0], k_code),
             )
             att = att.transpose(1, 0, 2).reshape(tokens, width).astype(jnp.bfloat16)
             parts = jnp.dot(att, w_out, preferred_element_type=jnp.float32)

time: 156 us -> 150 us (0.962)
  local copies, waits for them, and re-layouts: 22.3 us -> 3.73 us
  Pallas kernels: 18.2 us -> 27.3 us
  waiting for transfers between devices: 61 us -> 70.1 us
  other arithmetic: 14.5 us -> 6.13 us
  matrix products: 3.06 us -> 5.46 us
    ppermute x28 -> x31, waiting for transfers between devices: 34.3 us -> 55.9 us  [flip(): return lax.ppermute(x, names if len(names) > 1 else names[0], pairs)]
    ppermute x6, waiting for transfers between devices: 26.8 us -> 14.2 us  [rotate(): return lax.ppermute(x, 'dp', [(i, (i + k) % n_dp) for i in range(n_dp)])]
    unnamed x58 -> x56, local copies, waits for them, and re-layouts: 11.3 us -> 2.22 us
    pallas_call x2, Pallas kernels: 9.92 us -> 15.5 us  [the longest x1 8.2 us: per_device(): pl.pallas_call(lambda *refs: gate_kernel(*refs, places=places), out_shape...]
    another operation x5 -> x0, local copies, waits for them, and re-layouts: 5.04 us -> none  [the longest x4 4.95 us: absolute(): stacked, sec = (jnp.stack(blocks), lax.axis_index('section'))]
    pallas_call x1, Pallas kernels: 2.98 us -> 6.48 us  [per_device(): pl.pallas_call(norm_kernel, out_shape=jax.ShapeDtypeStruct((2 * tokens, f...]
    another operation x5 -> x1, other arithmetic: 3.3 us -> 0.18 us  [the longest x1 1.29 us: absolute(): stacked, sec = (jnp.stack(blocks), lax.axis_index('section'))]
    transpose x1 -> x0, other arithmetic: 3.02 us -> none  [per_device(): proj_t = proj.T]
  transfers between devices with their start and end apart: 34 -> 37, of which waited for: 15 -> 18; matrix products, arithmetic and copies ran while one was open for 17% -> 6% of each run, Pallas kernels for 6% -> 10%
where the time goes in v8:
time: 150 us; the launch traced here: 149 us
  waiting for transfers between devices  70.1 us (47%)
  starting transfers between devices  35.9 us (24%)
  Pallas kernels  27.3 us (18%)
  other arithmetic  6.13 us (4%)
  matrix products  5.46 us (4%)
  local copies, waits for them, and re-layouts  3.73 us (2%)
    ppermute x31, waiting for transfers between devices, flip(): return lax.ppermute(x, names if len(names) > 1 else names[0], pairs)  55.9 us
    ppermute x31, starting transfers between devices, flip(): return lax.ppermute(x, names if len(names) > 1 else names[0], pairs)  24.1 us
    ppermute x6, waiting for transfers between devices, rotate(): return lax.ppermute(x, 'dp', [(i, (i + k) % n_dp) for i in range(n_dp)])  14.2 us
    ppermute x6, starting transfers between devices, rotate(): return lax.ppermute(x, 'dp', [(i, (i + k) % n_dp) for i in range(n_dp)])  11.8 us
    pallas_call x1, Pallas kernels, per_device(): pl.pallas_call(lambda *refs: gate_kernel(*refs, places=places), out_shape...  8.2 us
    pallas_call x1, Pallas kernels, per_device(): pl.pallas_call(lambda *refs: project_kernel(*refs, places=places, parts=n...  7.26 us
    pallas_call x1, Pallas kernels, per_device(): pl.pallas_call(norm_kernel, out_shape=jax.ShapeDtypeStruct((2 * tokens, f...  6.48 us
    dot_general x4, matrix products, residual_of(): lax.dot_general(lax.dynamic_slice_in_dim(block, own_at, own_rows, 0), mat...  5.46 us
  transfers between devices with their start and end apart: 37, of which 18 were waited for; matrix products, arithmetic and copies ran while one was open for 6% of the time, Pallas kernels for 10%

profile of v8, /device:TPU:0, one launch (start us, length us, event | category | flops | bytes accessed | tf_op | source)
XLA Modules:
  0.0 149.1 jit_solution(7261609711430396700)
XLA Ops:
  0.0 2.1 %fusion.5 = (bf16[2,192,512]{2,1,0:T(8,128)(2,1)}, bf16[2,192,512]{2,1,0:T(8,128)(2,1)S(1)}) fusion(s32[]{:T(128)S(6)} %select_n.64, bf16[1,192,1024]{2,1,0:T(8,128)(2,1)} %bitcast.57, bf16[1,192,1024]{2,1,0:T(8,128)(2,1)} %bitcast.58, s32[]{:T(128)S(6)} %select_n.63), kind=kLoop, calls=%fused_computation.14 | loop fusion | flops 1572864 | bytes 1572872 | tf_op jit(solution)/shard_map/stack | solution.py:234
  2.1 3.0 %collective-permute-start.8 = (bf16[2,192,512]{2,1,0:T(8,128)(2,1)S(1)}, bf16[2,192,512]{2,1,0:T(8,128)(2,1)S(1)}, u32[]{:S(2)}, u32[]{:S(2)}) collective-permute-start(bf16[2,192,512]{2,1,0:T(8,128)(2,1)S(1)} %get-tuple-element.48.refs_1_), channel_id=1, source_target_pairs={{0,4},{4,0},{1,5},{5,1},{2,6},{6,2},{3,7},{7,3},{8,12},{12,8},{9,1... | collective-permute-start | bytes 1179656 | tf_op jit(solution)/shard_map/ppermute | solution.py:177
  5.1 2.6 %collective-permute-start.1 = (bf16[2,192,512]{2,1,0:T(8,128)(2,1)S(1)}, bf16[2,192,512]{2,1,0:T(8,128)(2,1)}, u32[]{:S(2)}, u32[]{:S(2)}) collective-permute-start(bf16[2,192,512]{2,1,0:T(8,128)(2,1)S(1)} %get-tuple-element.48.refs_1_), channel_id=1, source_target_pairs={{0,2},{1,3},{2,0},{3,1},{4,6},{5,7},{6,4},{7,5},{8,10},{9,11},{10,... | collective-permute-start | bytes 1179656 | tf_op jit(solution)/shard_map/ppermute | solution.py:180
  7.7 1.5 collective-permute-start
  9.2 1.6 %collective-permute-start.4 = (bf16[512,384]{1,0:T(8,128)(2,1)S(1)}, bf16[512,384]{1,0:T(8,128)(2,1)}, u32[]{:S(2)}, u32[]{:S(2)}) collective-permute-start(bf16[512,384]{1,0:T(8,128)(2,1)S(1)} %bitcast.55), channel_id=1, source_target_pairs={{0,1},{1,0},{2,3},{3,2},{4,5},{5,4},{6,7},{7,6},{8,9},{9,8},{10,11... | collective-permute-start | bytes 1179656 | tf_op jit(solution)/shard_map/ppermute | solution.py:177
  11.0 15.7 %collective-permute-done.4.refs_4_ = bf16[512,384]{1,0:T(8,128)(2,1)} collective-permute-done((bf16[512,384]{1,0:T(8,128)(2,1)S(1)}, bf16[512,384]{1,0:T(8,128)(2,1)}, u32[]{:S(2)}, u32[]{:S(2)}) %collective-permute-start.4) | collective-permute-done | bytes 393248 | tf_op jit(solution)/shard_map/ppermute | solution.py:177
  27.6 0.8 dynamic-slice_bitcast_fusion.1
  28.9 7.5 %collective-permute-done.5.refs_6_ = bf16[512,384]{1,0:T(8,128)(2,1)} collective-permute-done((bf16[512,384]{1,0:T(8,128)(2,1)}, bf16[512,384]{1,0:T(8,128)(2,1)}, u32[]{:S(2)}, u32[]{:S(2)}) %collective-permute-start.5) | collective-permute-done | bytes 393248 | tf_op jit(solution)/shard_map/ppermute | solution.py:177
  37.8 1.7 %collective-permute-start.10 = (bf16[2,192,512]{2,1,0:T(8,128)(2,1)}, bf16[2,192,512]{2,1,0:T(8,128)(2,1)}, u32[]{:S(2)}, u32[]{:S(2)}) collective-permute-start(bf16[2,192,512]{2,1,0:T(8,128)(2,1)} %get-tuple-element.28), channel_id=1, source_target_pairs={{0,1},{1,2},{2,3},{3,0},{4,5},{5,6},{6,7},{7,4},{8,9},{9,10},{10,1... | collective-permute-start | bytes 1179656 | tf_op jit(solution)/shard_map/ppermute | solution.py:180
  39.8 7.6 %collective-permute-done.13.refs_3_ = bf16[768,384]{1,0:T(8,128)(2,1)} collective-permute-done((bf16[768,384]{1,0:T(8,128)(2,1)S(1)}, bf16[768,384]{1,0:T(8,128)(2,1)}, u32[]{:S(2)}, u32[]{:S(2)}) %collective-permute-start.13) | collective-permute-done | bytes 589856 | tf_op jit(solution)/shard_map/ppermute | solution.py:177
  47.4 3.0 %collective-permute-start.18 = (bf16[2,192,512]{2,1,0:T(8,128)(2,1)}, bf16[2,192,512]{2,1,0:T(8,128)(2,1)}, u32[]{:S(2)}, u32[]{:S(2)}) collective-permute-start(bf16[2,192,512]{2,1,0:T(8,128)(2,1)} %get-tuple-element.28), channel_id=1, source_target_pairs={{0,3},{1,0},{2,1},{3,2},{4,7},{5,4},{6,5},{7,6},{8,11},{9,8},{10,9... | collective-permute-start | bytes 1179656 | tf_op jit(solution)/shard_map/ppermute | solution.py:180
  51.0 0.9 collective-permute-done.10.refs_4_
  52.0 0.7 fusion.18
  52.7 6.6 %collective-permute-done.18.refs_5_ = bf16[2,192,512]{2,1,0:T(8,128)(2,1)} collective-permute-done((bf16[2,192,512]{2,1,0:T(8,128)(2,1)}, bf16[2,192,512]{2,1,0:T(8,128)(2,1)}, u32[]{:S(2)}, u32[]{:S(2)}) %collective-permute-start.18) | collective-permute-done | bytes 393248 | tf_op jit(solution)/shard_map/ppermute | solution.py:180
  59.4 0.7 collective-permute-start.12
  60.1 1.5 %collective-permute-start.19 = (bf16[2,192,512]{2,1,0:T(8,128)(2,1)}, bf16[2,192,512]{2,1,0:T(8,128)(2,1)}, u32[]{:S(2)}, u32[]{:S(2)}) collective-permute-start(bf16[2,192,512]{2,1,0:T(8,128)(2,1)} %collective-permute-done.10.refs_4_), channel_id=1, source_target_pairs={{0,4},{4,0},{1,5},{5,1},{2,6},{6,2},{3,7},{7,3},{8,12},{12,8},{9,1... | collective-permute-start | bytes 1179656 | tf_op jit(solution)/shard_map/ppermute | solution.py:177
  62.7 1.1 copy.16
  63.9 6.5 %shard_map.118.refs_0_ = bf16[1024,1536]{1,0:T(8,128)(2,1)} custom-call(f32[4,1,384]{2,1,0:T(1,128)} %reshape.157.gain_ref, bf16[512,384]{1,0:T(8,128)(2,1)} %bitcast.52, bf16[512,384]{1,0:T(8,128)(2,1)} %copy-done.6, bf16[512,384]{1,0:T(8,128)(2,1)} %copy-done.5, bf16[512,384]{1,0:T(8,128)(2,1)} %copy-done.4, ...), custom_call_target="tpu_custom_call" | custom-call | flops 12582912 | bytes 6291456 | tf_op jit(solution)/shard_map/pallas_call | solution.py:300
  70.5 2.4 %collective-permute-start.16 = (bf16[1,192,512]{2,1,0:T(8,128)(2,1)S(1)}, bf16[1,192,512]{2,1,0:T(8,128)(2,1)S(1)}, u32[]{:S(2)}, u32[]{:S(2)}) collective-permute-start(bf16[1,192,512]{2,1,0:T(8,128)(2,1)S(1)} %copy-done.14), channel_id=1, source_target_pairs={{0,1},{1,2},{2,3},{3,0},{4,5},{5,6},{6,7},{7,4},{8,9},{9,10},{10,1... | collective-permute-start | bytes 589832 | tf_op jit(solution)/shard_map/ppermute | solution.py:180
  72.9 1.4 collective-permute-start.17
  74.4 2.0 %collective-permute-start.21 = (bf16[1,192,512]{2,1,0:T(8,128)(2,1)}, bf16[1,192,512]{2,1,0:T(8,128)(2,1)S(1)}, u32[]{:S(2)}, u32[]{:S(2)}) collective-permute-start(bf16[1,192,512]{2,1,0:T(8,128)(2,1)} %collective-permute-done.12.refs_6_), channel_id=1, source_target_pairs={{0,4},{4,0},{1,5},{5,1},{2,6},{6,2},{3,7},{7,3},{8,12},{12,8},{9,1... | collective-permute-start | bytes 589832 | tf_op jit(solution)/shard_map/ppermute | solution.py:177
  76.4 3.8 %collective-permute-done.16.refs_8_ = bf16[1,192,512]{2,1,0:T(8,128)(2,1)S(1)} collective-permute-done((bf16[1,192,512]{2,1,0:T(8,128)(2,1)S(1)}, bf16[1,192,512]{2,1,0:T(8,128)(2,1)S(1)}, u32[]{:S(2)}, u32[]{:S(2)}) %collective-permute-start.16) | collective-permute-done | bytes 196640 | tf_op jit(solution)/shard_map/ppermute | solution.py:180
  80.2 2.7 %collective-permute-done.17.refs_9_ = bf16[1,192,512]{2,1,0:T(8,128)(2,1)S(1)} collective-permute-done((bf16[1,192,512]{2,1,0:T(8,128)(2,1)S(1)}, bf16[1,192,512]{2,1,0:T(8,128)(2,1)S(1)}, u32[]{:S(2)}, u32[]{:S(2)}) %collective-permute-start.17) | collective-permute-done | bytes 196640 | tf_op jit(solution)/shard_map/ppermute | solution.py:180
  83.0 1.5 %collective-permute-start.22 = (bf16[1,192,512]{2,1,0:T(8,128)(2,1)S(1)}, bf16[1,192,512]{2,1,0:T(8,128)(2,1)S(1)}, u32[]{:S(2)}, u32[]{:S(2)}) collective-permute-start(bf16[1,192,512]{2,1,0:T(8,128)(2,1)S(1)} %collective-permute-done.16.refs_8_), channel_id=1, source_target_pairs={{0,4},{4,0},{1,5},{5,1},{2,6},{6,2},{3,7},{7,3},{8,12},{12,8},{9,1... | collective-permute-start | bytes 589832 | tf_op jit(solution)/shard_map/ppermute | solution.py:177
  85.0 8.2 %shard_map.119 = bf16[1024,512]{1,0:T(8,128)(2,1)} custom-call(bf16[1024,1536]{1,0:T(8,128)(2,1)} %shard_map.118.refs_0_, bf16[2,192,512]{2,1,0:T(8,128)(2,1)} %copy-done.12, bf16[2,192,512]{2,1,0:T(8,128)(2,1)} %collective-permute-done.1.refs_2_, bf16[2,192,512]{2,1,0:T(8,128)(2,1)} %copy-done.20, bf16[2,192,512]{2,1,0:T(8,128)(2,1)} %collective-permute-done.10.refs_4_, ...), custom_call_target="tpu_custom_call" | custom-call | flops 3221225472 | bytes 8388608 | tf_op jit(solution)/shard_map/pallas_call | solution.py:328
  93.3 0.7 collective-permute-done.23.refs_12_
  94.6 7.3 %shard_map.120 = (bf16[2,2,128,768]{3,2,1,0:T(8,128)(2,1)}, f32[2,2,128,768]{3,2,1,0:T(8,128)}) custom-call(bf16[2,2,2,128,512]{4,3,2,1,0:T(8,128)(2,1)} %bitcast.62, bf16[768,384]{1,0:T(8,128)(2,1)} %bitcast.50, bf16[768,384]{1,0:T(8,128)(2,1)} %collective-permute-done.14.refs_2_, bf16[768,384]{1,0:T(8,128)(2,1)} %collective-permute-done.13.refs_3_, ...), custom_call_target="tpu_custom_call" | custom-call | flops 2013265920 | bytes 8388608 | tf_op jit(solution)/shard_map/pallas_call | solution.py:346
  102.0 2.5 %collective-permute-done.24 = bf16[2,2,128,768]{3,2,1,0:T(8,128)(2,1)S(1)} collective-permute-done((bf16[2,2,128,768]{3,2,1,0:T(8,128)(2,1)}, bf16[2,2,128,768]{3,2,1,0:T(8,128)(2,1)S(1)}, u32[]{:S(2)}, u32[]{:S(2)}) %collective-permute-start.24) | collective-permute-done | bytes 786464 | tf_op jit(solution)/shard_map/ppermute | solution.py:177
  104.5 1.6 %convert_add_fusion = f32[2,2,128,768]{3,2,1,0:T(8,128)S(1)} fusion(f32[2,2,128,768]{3,2,1,0:T(8,128)} %get-tuple-element.35, bf16[2,2,128,768]{3,2,1,0:T(8,128)(2,1)S(1)} %collective-permute-done.24), kind=kLoop, calls=%fused_computation | loop fusion | flops 786432 | bytes 3932160 | tf_op jit(solution)/shard_map/add | solution.py:387
  106.2 2.0 %collective-permute-start.25 = (bf16[128,768]{1,0:T(8,128)(2,1)S(1)}, bf16[128,768]{1,0:T(8,128)(2,1)S(1)}, u32[]{:S(2)}, u32[]{:S(2)}) collective-permute-start(bf16[128,768]{1,0:T(8,128)(2,1)S(1)} %get-tuple-element.49), channel_id=1, source_target_pairs={{0,16},{8,24},{16,0},{24,8},{1,17},{9,25},{17,1},{25,9},{2,18},{10... | collective-permute-start | bytes 589832 | tf_op jit(solution)/shard_map/ppermute | solution.py:177
  108.2 0.7 collective-permute-start.27
  108.9 1.0 collective-permute-start.26
  109.9 1.4 fusion.15
  111.3 1.5 %fusion.13 = f32[128,768]{1,0:T(8,128)S(1)} fusion(bf16[768,384]{1,0:T(8,128)(2,1)} %collective-permute-done.13.refs_3_, bf16[512,384]{1,0:T(8,128)(2,1)} %copy-done.5, s32[]{:T(128)S(6)} %select_n.71), kind=kOutput, calls=%fused_computation.32 | convolution fusion | flops 75497472 | bytes 1081348 | tf_op jit(solution)/shard_map/dot_general | solution.py:270
  112.8 1.2 fusion
  114.1 3.6 %collective-permute-done.25 = bf16[128,768]{1,0:T(8,128)(2,1)S(1)} collective-permute-done((bf16[128,768]{1,0:T(8,128)(2,1)S(1)}, bf16[128,768]{1,0:T(8,128)(2,1)S(1)}, u32[]{:S(2)}, u32[]{:S(2)}) %collective-permute-start.25) | collective-permute-done | bytes 196640 | tf_op jit(solution)/shard_map/ppermute | solution.py:177
  117.7 1.3 collective-permute-done.26
  119.0 1.3 fusion.31
  120.6 1.7 %collective-permute-start.28 = (bf16[128,768]{1,0:T(8,128)(2,1)S(1)}, bf16[128,768]{1,0:T(8,128)(2,1)S(1)}, u32[]{:S(2)}, u32[]{:S(2)}) collective-permute-start(bf16[128,768]{1,0:T(8,128)(2,1)S(1)} %multiply_convert_fusion.refs_0_), channel_id=1, source_target_pairs={{0,16},{8,24},{16,0},{24,8},{1,17},{9,25},{17,1},{25,9},{2,18},{10... | collective-permute-start | bytes 589832 | tf_op jit(solution)/shard_map/ppermute | solution.py:177
  122.4 1.5 collective-permute-start.31
  124.2 4.3 %collective-permute-done.28.refs_1_ = bf16[128,768]{1,0:T(8,128)(2,1)S(1)} collective-permute-done((bf16[128,768]{1,0:T(8,128)(2,1)S(1)}, bf16[128,768]{1,0:T(8,128)(2,1)S(1)}, u32[]{:S(2)}, u32[]{:S(2)}) %collective-permute-start.28) | collective-permute-done | bytes 196640 | tf_op jit(solution)/shard_map/ppermute | solution.py:177
  128.5 3.7 %collective-permute-done.31.refs_4_ = bf16[128,768]{1,0:T(8,128)(2,1)S(1)} collective-permute-done((bf16[128,768]{1,0:T(8,128)(2,1)S(1)}, bf16[128,768]{1,0:T(8,128)(2,1)S(1)}, u32[]{:S(2)}, u32[]{:S(2)}) %collective-permute-start.31) | collective-permute-done | bytes 196640 | tf_op jit(solution)/shard_map/ppermute | solution.py:177
  132.8 0.9 collective-permute-done.33.refs_6_
  134.0 5.4 %shard_map.121 = (f32[2,192,512]{2,1,0:T(8,128)S(1)}, bf16[2,192,512]{2,1,0:T(8,128)(2,1)S(1)}) custom-call(bf16[128,768]{1,0:T(8,128)(2,1)S(1)} %multiply_convert_fusion.refs_0_, bf16[128,768]{1,0:T(8,128)(2,1)S(1)} %collective-permute-done.28.refs_1_, bf16[128,768]{1,0:T(8,128)(2,1)S(1)} %collective-permute-done.29.refs_2_, ...), custom_call_target="tpu_custom_call" | custom-call | flops 2516582400 | bytes 8388608 | tf_op jit(solution)/shard_map/pallas_call | solution.py:418
  139.7 1.5 collective-permute-done.35
  141.3 0.9 collective-permute-start.36
  142.2 6.3 %collective-permute-done.36 = bf16[192,512]{1,0:T(8,128)(2,1)S(1)} collective-permute-done((bf16[192,512]{1,0:T(8,128)(2,1)S(1)}, bf16[192,512]{1,0:T(8,128)(2,1)S(1)}, u32[]{:S(2)}, u32[]{:S(2)}) %collective-permute-start.36) | collective-permute-done | bytes 196640 | tf_op jit(solution)/shard_map/ppermute | solution.py:177
  148.4 0.7 fusion.10
  (121 shorter events, 8.4 us)
Async XLA Ops:
  0.0 27.2 %copy-start.9 = (bf16[384,768]{1,0:T(8,128)(2,1)S(1)}, bf16[384,768]{1,0:T(8,128)(2,1)}, u32[]{:S(2)}) copy-start(bf16[384,768]{1,0:T(8,128)(2,1)} %param.17) | copy-start | bytes 1769476
  0.0 27.5 %copy-start.11 = (bf16[1024,192]{0,1:T(8,128)(2,1)S(1)}, bf16[1024,192]{0,1:T(8,128)(2,1)}, u32[]{:S(2)}) copy-start(bf16[1024,192]{0,1:T(8,128)(2,1)} %param.16) | copy-start | bytes 1179652
  0.0 39.5 %copy-start.19 = (s32[1,3]{1,0:T(1,128)S(1)}, s32[1,3]{1,0:T(1,128)}, u32[]{:S(2)}) copy-start(s32[1,3]{1,0:T(1,128)} %param.21) | copy-start | bytes 40
  0.0 51.9 %copy-start.17 = (s32[4]{0:T(128)S(1)}, s32[4]{0:T(128)}, u32[]{:S(2)}) copy-start(s32[4]{0:T(128)} %param.22) | copy-start | bytes 52
  0.0 62.1 %copy-start.15 = (f32[1536]{0:T(1024)S(1)}, f32[1536]{0:T(1024)}, u32[]{:S(2)}) copy-start(f32[1536]{0:T(1024)} %param.13) | copy-start | bytes 18436
  2.1 34.6 %copy-start.12 = (bf16[2,192,512]{2,1,0:T(8,128)(2,1)}, bf16[2,192,512]{2,1,0:T(8,128)(2,1)S(1)}, u32[]{:S(2)}) copy-start(bf16[2,192,512]{2,1,0:T(8,128)(2,1)S(1)} %get-tuple-element.48.refs_1_) | copy-start | bytes 1179652
  2.1 26.2 %collective-permute-start.8 = (bf16[2,192,512]{2,1,0:T(8,128)(2,1)S(1)}, bf16[2,192,512]{2,1,0:T(8,128)(2,1)S(1)}, u32[]{:S(2)}, u32[]{:S(2)}) collective-permute-start(bf16[2,192,512]{2,1,0:T(8,128)(2,1)S(1)} %get-tuple-element.48.refs_1_), channel_id=1, source_target_pairs={{0,4},{4,0},{1,5},{5,1},{2,6},{6,2},{3,7},{7,3},{8,12},{12,8},{9,1... | collective-permute-start | bytes 1179656 | tf_op jit(solution)/shard_map/ppermute | solution.py:177
  5.1 23.7 %collective-permute-start.1 = (bf16[2,192,512]{2,1,0:T(8,128)(2,1)S(1)}, bf16[2,192,512]{2,1,0:T(8,128)(2,1)}, u32[]{:S(2)}, u32[]{:S(2)}) collective-permute-start(bf16[2,192,512]{2,1,0:T(8,128)(2,1)S(1)} %get-tuple-element.48.refs_1_), channel_id=1, source_target_pairs={{0,2},{1,3},{2,0},{3,1},{4,6},{5,7},{6,4},{7,5},{8,10},{9,11},{10,... | collective-permute-start | bytes 1179656 | tf_op jit(solution)/shard_map/ppermute | solution.py:180
  7.7 29.0 %collective-permute-start = (bf16[512,384]{1,0:T(8,128)(2,1)S(1)}, bf16[512,384]{1,0:T(8,128)(2,1)S(1)}, u32[]{:S(2)}, u32[]{:S(2)}) collective-permute-start(bf16[512,384]{1,0:T(8,128)(2,1)S(1)} %bitcast.54), channel_id=1, source_target_pairs={{0,16},{8,24},{16,0},{24,8},{1,17},{9,25},{17,1},{25,9},{2,18},{10... | collective-permute-start | bytes 1179656 | tf_op jit(solution)/shard_map/ppermute | solution.py:177
  9.2 17.4 %collective-permute-start.4 = (bf16[512,384]{1,0:T(8,128)(2,1)S(1)}, bf16[512,384]{1,0:T(8,128)(2,1)}, u32[]{:S(2)}, u32[]{:S(2)}) collective-permute-start(bf16[512,384]{1,0:T(8,128)(2,1)S(1)} %bitcast.55), channel_id=1, source_target_pairs={{0,1},{1,0},{2,3},{3,2},{4,5},{5,4},{6,7},{7,6},{8,9},{9,8},{10,11... | collective-permute-start | bytes 1179656 | tf_op jit(solution)/shard_map/ppermute | solution.py:177
  26.7 9.7 %collective-permute-start.5 = (bf16[512,384]{1,0:T(8,128)(2,1)}, bf16[512,384]{1,0:T(8,128)(2,1)}, u32[]{:S(2)}, u32[]{:S(2)}) collective-permute-start(bf16[512,384]{1,0:T(8,128)(2,1)} %collective-permute-done.4.refs_4_), channel_id=1, source_target_pairs={{0,16},{8,24},{16,0},{24,8},{1,17},{9,25},{17,1},{25,9},{2,18},{10... | collective-permute-start | bytes 1179656 | tf_op jit(solution)/shard_map/ppermute | solution.py:177
  27.6 42.8 %copy-start.1 = (bf16[384,768]{0,1:T(8,128)(2,1)}, bf16[384,768]{0,1:T(8,128)(2,1)S(1)}, u32[]{:S(2)}) copy-start(bf16[384,768]{0,1:T(8,128)(2,1)S(1)} %copy.15) | copy-start | bytes 1769476
  28.3 64.9 %copy-start.13 = (bf16[1,192,512]{2,1,0:T(8,128)(2,1)}, bf16[1,192,512]{2,1,0:T(8,128)(2,1)S(1)}, u32[]{:S(2)}) copy-start(bf16[1,192,512]{2,1,0:T(8,128)(2,1)S(1)} %get-tuple-element.29.refs_5_) | copy-start | bytes 589828
  28.4 22.6 %copy-start.20 = (bf16[2,192,512]{2,1,0:T(8,128)(2,1)}, bf16[2,192,512]{2,1,0:T(8,128)(2,1)S(1)}, u32[]{:S(2)}) copy-start(bf16[2,192,512]{2,1,0:T(8,128)(2,1)S(1)} %collective-permute-done.8.refs_3_) | copy-start | bytes 1179652
  28.4 9.5 %collective-permute-start.9 = (bf16[1,192,512]{2,1,0:T(8,128)(2,1)S(1)}, bf16[1,192,512]{2,1,0:T(8,128)(2,1)S(1)}, u32[]{:S(2)}, u32[]{:S(2)}) collective-permute-start(bf16[1,192,512]{2,1,0:T(8,128)(2,1)S(1)} %get-tuple-element.29.refs_5_), channel_id=1, source_target_pairs={{0,4},{4,0},{1,5},{5,1},{2,6},{6,2},{3,7},{7,3},{8,12},{12,8},{9,1... | collective-permute-start | bytes 589832 | tf_op jit(solution)/shard_map/ppermute | solution.py:177
  36.4 11.0 %collective-permute-start.13 = (bf16[768,384]{1,0:T(8,128)(2,1)S(1)}, bf16[768,384]{1,0:T(8,128)(2,1)}, u32[]{:S(2)}, u32[]{:S(2)}) collective-permute-start(bf16[768,384]{1,0:T(8,128)(2,1)S(1)} %bitcast.48), channel_id=1, source_target_pairs={{0,16},{8,24},{16,0},{24,8},{1,17},{9,25},{17,1},{25,9},{2,18},{10... | collective-permute-start | bytes 1769480 | tf_op jit(solution)/shard_map/ppermute | solution.py:177
  36.7 27.1 %copy-start.5 = (bf16[512,384]{1,0:T(8,128)(2,1)}, bf16[512,384]{1,0:T(8,128)(2,1)S(1)}, u32[]{:S(2)}) copy-start(bf16[512,384]{1,0:T(8,128)(2,1)S(1)} %collective-permute-done.refs_2_) | copy-start | bytes 1179652
  36.7 13.6 %collective-permute-start.3 = (bf16[512,384]{1,0:T(8,128)(2,1)S(1)}, bf16[512,384]{1,0:T(8,128)(2,1)S(1)}, u32[]{:S(2)}, u32[]{:S(2)}) collective-permute-start(bf16[512,384]{1,0:T(8,128)(2,1)S(1)} %collective-permute-done.refs_2_), channel_id=1, source_target_pairs={{0,8},{8,0},{16,24},{24,16},{1,9},{9,1},{17,25},{25,17},{2,10},{10... | collective-permute-start | bytes 1179656 | tf_op jit(solution)/shard_map/ppermute | solution.py:177
  36.8 13.6 %collective-permute-start.2 = (bf16[512,384]{1,0:T(8,128)(2,1)S(1)}, bf16[512,384]{1,0:T(8,128)(2,1)S(1)}, u32[]{:S(2)}, u32[]{:S(2)}) collective-permute-start(bf16[512,384]{1,0:T(8,128)(2,1)S(1)} %bitcast.56), channel_id=1, source_target_pairs={{0,8},{8,0},{16,24},{24,16},{1,9},{9,1},{17,25},{25,17},{2,10},{10... | collective-permute-start | bytes 1179656 | tf_op jit(solution)/shard_map/ppermute | solution.py:177
  37.3 13.6 %collective-permute-start.11 = (bf16[2,192,512]{2,1,0:T(8,128)(2,1)}, bf16[2,192,512]{2,1,0:T(8,128)(2,1)}, u32[]{:S(2)}, u32[]{:S(2)}) collective-permute-start(bf16[2,192,512]{2,1,0:T(8,128)(2,1)} %collective-permute-done.1.refs_2_), channel_id=1, source_target_pairs={{0,4},{4,0},{1,5},{5,1},{2,6},{6,2},{3,7},{7,3},{8,12},{12,8},{9,1... | collective-permute-start | bytes 1179656 | tf_op jit(solution)/shard_map/ppermute | solution.py:177
  37.8 14.1 %collective-permute-start.10 = (bf16[2,192,512]{2,1,0:T(8,128)(2,1)}, bf16[2,192,512]{2,1,0:T(8,128)(2,1)}, u32[]{:S(2)}, u32[]{:S(2)}) collective-permute-start(bf16[2,192,512]{2,1,0:T(8,128)(2,1)} %get-tuple-element.28), channel_id=1, source_target_pairs={{0,1},{1,2},{2,3},{3,0},{4,5},{5,6},{6,7},{7,4},{8,9},{9,10},{10,1... | collective-permute-start | bytes 1179656 | tf_op jit(solution)/shard_map/ppermute | solution.py:180
  47.4 12.0 %collective-permute-start.18 = (bf16[2,192,512]{2,1,0:T(8,128)(2,1)}, bf16[2,192,512]{2,1,0:T(8,128)(2,1)}, u32[]{:S(2)}, u32[]{:S(2)}) collective-permute-start(bf16[2,192,512]{2,1,0:T(8,128)(2,1)} %get-tuple-element.28), channel_id=1, source_target_pairs={{0,3},{1,0},{2,1},{3,2},{4,7},{5,4},{6,5},{7,6},{8,11},{9,8},{10,9... | collective-permute-start | bytes 1179656 | tf_op jit(solution)/shard_map/ppermute | solution.py:180
  50.4 9.7 %collective-permute-start.6 = (bf16[512,384]{1,0:T(8,128)(2,1)}, bf16[512,384]{1,0:T(8,128)(2,1)S(1)}, u32[]{:S(2)}, u32[]{:S(2)}) collective-permute-start(bf16[512,384]{1,0:T(8,128)(2,1)} %collective-permute-done.4.refs_4_), channel_id=1, source_target_pairs={{0,8},{8,0},{16,24},{24,16},{1,9},{9,1},{17,25},{25,17},{2,10},{10... | collective-permute-start | bytes 1179656 | tf_op jit(solution)/shard_map/ppermute | solution.py:177
  50.4 11.2 %collective-permute-start.7 = (bf16[512,384]{1,0:T(8,128)(2,1)}, bf16[512,384]{1,0:T(8,128)(2,1)}, u32[]{:S(2)}, u32[]{:S(2)}) collective-permute-start(bf16[512,384]{1,0:T(8,128)(2,1)} %collective-permute-done.5.refs_6_), channel_id=1, source_target_pairs={{0,8},{8,0},{16,24},{24,16},{1,9},{9,1},{17,25},{25,17},{2,10},{10... | collective-permute-start | bytes 1179656 | tf_op jit(solution)/shard_map/ppermute | solution.py:177
  50.9 19.6 %collective-permute-start.14 = (bf16[768,384]{1,0:T(8,128)(2,1)S(1)}, bf16[768,384]{1,0:T(8,128)(2,1)}, u32[]{:S(2)}, u32[]{:S(2)}) collective-permute-start(bf16[768,384]{1,0:T(8,128)(2,1)S(1)} %bitcast.49), channel_id=1, source_target_pairs={{0,8},{8,0},{16,24},{24,16},{1,9},{9,1},{17,25},{25,17},{2,10},{10... | collective-permute-start | bytes 1769480 | tf_op jit(solution)/shard_map/ppermute | solution.py:177
  51.9 18.6 %collective-permute-start.15 = (bf16[768,384]{1,0:T(8,128)(2,1)}, bf16[768,384]{1,0:T(8,128)(2,1)S(1)}, u32[]{:S(2)}, u32[]{:S(2)}) collective-permute-start(bf16[768,384]{1,0:T(8,128)(2,1)} %collective-permute-done.13.refs_3_), channel_id=1, source_target_pairs={{0,8},{8,0},{16,24},{24,16},{1,9},{9,1},{17,25},{25,17},{2,10},{10... | collective-permute-start | bytes 1769480 | tf_op jit(solution)/shard_map/ppermute | solution.py:177
  59.4 11.1 %collective-permute-start.12 = (bf16[1,192,512]{2,1,0:T(8,128)(2,1)S(1)}, bf16[1,192,512]{2,1,0:T(8,128)(2,1)}, u32[]{:S(2)}, u32[]{:S(2)}) collective-permute-start(bf16[1,192,512]{2,1,0:T(8,128)(2,1)S(1)} %get-tuple-element.29.refs_5_), channel_id=1, source_target_pairs={{0,2},{1,3},{2,0},{3,1},{4,6},{5,7},{6,4},{7,5},{8,10},{9,11},{10,... | collective-permute-start | bytes 589832 | tf_op jit(solution)/shard_map/ppermute | solution.py:180
  60.1 24.9 %collective-permute-start.19 = (bf16[2,192,512]{2,1,0:T(8,128)(2,1)}, bf16[2,192,512]{2,1,0:T(8,128)(2,1)}, u32[]{:S(2)}, u32[]{:S(2)}) collective-permute-start(bf16[2,192,512]{2,1,0:T(8,128)(2,1)} %collective-permute-done.10.refs_4_), channel_id=1, source_target_pairs={{0,4},{4,0},{1,5},{5,1},{2,6},{6,2},{3,7},{7,3},{8,12},{12,8},{9,1... | collective-permute-start | bytes 1179656 | tf_op jit(solution)/shard_map/ppermute | solution.py:177
  61.6 23.4 %collective-permute-start.20 = (bf16[2,192,512]{2,1,0:T(8,128)(2,1)}, bf16[2,192,512]{2,1,0:T(8,128)(2,1)}, u32[]{:S(2)}, u32[]{:S(2)}) collective-permute-start(bf16[2,192,512]{2,1,0:T(8,128)(2,1)} %collective-permute-done.18.refs_5_), channel_id=1, source_target_pairs={{0,4},{4,0},{1,5},{5,1},{2,6},{6,2},{3,7},{7,3},{8,12},{12,8},{9,1... | collective-permute-start | bytes 1179656 | tf_op jit(solution)/shard_map/ppermute | solution.py:177
  70.5 22.7 %copy-start.7 = (bf16[768,384]{1,0:T(8,128)(2,1)}, bf16[768,384]{1,0:T(8,128)(2,1)S(1)}, u32[]{:S(2)}) copy-start(bf16[768,384]{1,0:T(8,128)(2,1)S(1)} %collective-permute-done.15.refs_4_) | copy-start | bytes 1769476
  70.5 9.7 %collective-permute-start.16 = (bf16[1,192,512]{2,1,0:T(8,128)(2,1)S(1)}, bf16[1,192,512]{2,1,0:T(8,128)(2,1)S(1)}, u32[]{:S(2)}, u32[]{:S(2)}) collective-permute-start(bf16[1,192,512]{2,1,0:T(8,128)(2,1)S(1)} %copy-done.14), channel_id=1, source_target_pairs={{0,1},{1,2},{2,3},{3,0},{4,5},{5,6},{6,7},{7,4},{8,9},{9,10},{10,1... | collective-permute-start | bytes 589832 | tf_op jit(solution)/shard_map/ppermute | solution.py:180
  72.9 10.0 %collective-permute-start.17 = (bf16[1,192,512]{2,1,0:T(8,128)(2,1)S(1)}, bf16[1,192,512]{2,1,0:T(8,128)(2,1)S(1)}, u32[]{:S(2)}, u32[]{:S(2)}) collective-permute-start(bf16[1,192,512]{2,1,0:T(8,128)(2,1)S(1)} %copy-done.14), channel_id=1, source_target_pairs={{0,3},{1,0},{2,1},{3,2},{4,7},{5,4},{6,5},{7,6},{8,11},{9,8},{10,9... | collective-permute-start | bytes 589832 | tf_op jit(solution)/shard_map/ppermute | solution.py:180
  74.4 18.9 %collective-permute-start.21 = (bf16[1,192,512]{2,1,0:T(8,128)(2,1)}, bf16[1,192,512]{2,1,0:T(8,128)(2,1)S(1)}, u32[]{:S(2)}, u32[]{:S(2)}) collective-permute-start(bf16[1,192,512]{2,1,0:T(8,128)(2,1)} %collective-permute-done.12.refs_6_), channel_id=1, source_target_pairs={{0,4},{4,0},{1,5},{5,1},{2,6},{6,2},{3,7},{7,3},{8,12},{12,8},{9,1... | collective-permute-start | bytes 589832 | tf_op jit(solution)/shard_map/ppermute | solution.py:177
  83.0 10.3 %collective-permute-start.22 = (bf16[1,192,512]{2,1,0:T(8,128)(2,1)S(1)}, bf16[1,192,512]{2,1,0:T(8,128)(2,1)S(1)}, u32[]{:S(2)}, u32[]{:S(2)}) collective-permute-start(bf16[1,192,512]{2,1,0:T(8,128)(2,1)S(1)} %collective-permute-done.16.refs_8_), channel_id=1, source_target_pairs={{0,4},{4,0},{1,5},{5,1},{2,6},{6,2},{3,7},{7,3},{8,12},{12,8},{9,1... | collective-permute-start | bytes 589832 | tf_op jit(solution)/shard_map/ppermute | solution.py:177
  84.5 9.5 %collective-permute-start.23 = (bf16[1,192,512]{2,1,0:T(8,128)(2,1)S(1)}, bf16[1,192,512]{2,1,0:T(8,128)(2,1)S(1)}, u32[]{:S(2)}, u32[]{:S(2)}) collective-permute-start(bf16[1,192,512]{2,1,0:T(8,128)(2,1)S(1)} %collective-permute-done.17.refs_9_), channel_id=1, source_target_pairs={{0,4},{4,0},{1,5},{5,1},{2,6},{6,2},{3,7},{7,3},{8,12},{12,8},{9,1... | collective-permute-start | bytes 589832 | tf_op jit(solution)/shard_map/ppermute | solution.py:177
  101.9 2.6 %collective-permute-start.24 = (bf16[2,2,128,768]{3,2,1,0:T(8,128)(2,1)}, bf16[2,2,128,768]{3,2,1,0:T(8,128)(2,1)S(1)}, u32[]{:S(2)}, u32[]{:S(2)}) collective-permute-start(bf16[2,2,128,768]{3,2,1,0:T(8,128)(2,1)} %get-tuple-element.36), channel_id=1, source_target_pairs={{0,8},{8,0},{16,24},{24,16},{1,9},{9,1},{17,25},{25,17},{2,10},{10... | collective-permute-start | bytes 2359304 | tf_op jit(solution)/shard_map/ppermute | solution.py:177
  106.2 11.5 %collective-permute-start.25 = (bf16[128,768]{1,0:T(8,128)(2,1)S(1)}, bf16[128,768]{1,0:T(8,128)(2,1)S(1)}, u32[]{:S(2)}, u32[]{:S(2)}) collective-permute-start(bf16[128,768]{1,0:T(8,128)(2,1)S(1)} %get-tuple-element.49), channel_id=1, source_target_pairs={{0,16},{8,24},{16,0},{24,8},{1,17},{9,25},{17,1},{25,9},{2,18},{10... | collective-permute-start | bytes 589832 | tf_op jit(solution)/shard_map/ppermute | solution.py:177
  108.2 9.4 %collective-permute-start.27 = (bf16[128,768]{1,0:T(8,128)(2,1)S(1)}, bf16[128,768]{1,0:T(8,128)(2,1)S(1)}, u32[]{:S(2)}, u32[]{:S(2)}) collective-permute-start(bf16[128,768]{1,0:T(8,128)(2,1)S(1)} %get-tuple-element.50), channel_id=1, source_target_pairs={{0,17},{1,16},{2,19},{3,18},{8,25},{9,24},{10,27},{11,26},{16,1},{... | collective-permute-start | bytes 589832 | tf_op jit(solution)/shard_map/ppermute | solution.py:177
  108.9 10.0 %collective-permute-start.26 = (bf16[128,768]{1,0:T(8,128)(2,1)S(1)}, bf16[128,768]{1,0:T(8,128)(2,1)S(1)}, u32[]{:S(2)}, u32[]{:S(2)}) collective-permute-start(bf16[128,768]{1,0:T(8,128)(2,1)S(1)} %fusion.9), channel_id=1, source_target_pairs={{0,1},{1,0},{2,3},{3,2},{4,5},{5,4},{6,7},{7,6},{8,9},{9,8},{10,11... | collective-permute-start | bytes 589832 | tf_op jit(solution)/shard_map/ppermute | solution.py:177
  120.6 7.9 %collective-permute-start.28 = (bf16[128,768]{1,0:T(8,128)(2,1)S(1)}, bf16[128,768]{1,0:T(8,128)(2,1)S(1)}, u32[]{:S(2)}, u32[]{:S(2)}) collective-permute-start(bf16[128,768]{1,0:T(8,128)(2,1)S(1)} %multiply_convert_fusion.refs_0_), channel_id=1, source_target_pairs={{0,16},{8,24},{16,0},{24,8},{1,17},{9,25},{17,1},{25,9},{2,18},{10... | collective-permute-start | bytes 589832 | tf_op jit(solution)/shard_map/ppermute | solution.py:177
  122.4 9.9 %collective-permute-start.31 = (bf16[128,768]{1,0:T(8,128)(2,1)S(1)}, bf16[128,768]{1,0:T(8,128)(2,1)S(1)}, u32[]{:S(2)}, u32[]{:S(2)}) collective-permute-start(bf16[128,768]{1,0:T(8,128)(2,1)S(1)} %multiply_convert_fusion.refs_0_), channel_id=1, source_target_pairs={{0,4},{4,0},{1,5},{5,1},{2,6},{6,2},{3,7},{7,3},{8,12},{12,8},{9,1... | collective-permute-start | bytes 589832 | tf_op jit(solution)/shard_map/ppermute | solution.py:177
  123.8 8.4 %collective-permute-start.32 = (bf16[128,768]{1,0:T(8,128)(2,1)S(1)}, bf16[128,768]{1,0:T(8,128)(2,1)S(1)}, u32[]{:S(2)}, u32[]{:S(2)}) collective-permute-start(bf16[128,768]{1,0:T(8,128)(2,1)S(1)} %multiply_convert_fusion.refs_0_), channel_id=1, source_target_pairs={{0,20},{4,16},{8,28},{12,24},{16,4},{20,0},{24,12},{28,8},{1,21},{... | collective-permute-start | bytes 589832 | tf_op jit(solution)/shard_map/ppermute | solution.py:177
  124.2 8.6 %collective-permute-start.29 = (bf16[128,768]{1,0:T(8,128)(2,1)S(1)}, bf16[128,768]{1,0:T(8,128)(2,1)S(1)}, u32[]{:S(2)}, u32[]{:S(2)}) collective-permute-start(bf16[128,768]{1,0:T(8,128)(2,1)S(1)} %multiply_convert_fusion.refs_0_), channel_id=1, source_target_pairs={{0,8},{8,0},{16,24},{24,16},{1,9},{9,1},{17,25},{25,17},{2,10},{10... | collective-permute-start | bytes 589832 | tf_op jit(solution)/shard_map/ppermute | solution.py:177
  128.5 4.2 %collective-permute-start.30 = (bf16[128,768]{1,0:T(8,128)(2,1)S(1)}, bf16[128,768]{1,0:T(8,128)(2,1)S(1)}, u32[]{:S(2)}, u32[]{:S(2)}) collective-permute-start(bf16[128,768]{1,0:T(8,128)(2,1)S(1)} %collective-permute-done.28.refs_1_), channel_id=1, source_target_pairs={{0,8},{8,0},{16,24},{24,16},{1,9},{9,1},{17,25},{25,17},{2,10},{10... | collective-permute-start | bytes 589832 | tf_op jit(solution)/shard_map/ppermute | solution.py:177
  132.2 1.4 collective-permute-start.33
  132.2 1.7 %collective-permute-start.34 = (bf16[128,768]{1,0:T(8,128)(2,1)S(1)}, bf16[128,768]{1,0:T(8,128)(2,1)S(1)}, u32[]{:S(2)}, u32[]{:S(2)}) collective-permute-start(bf16[128,768]{1,0:T(8,128)(2,1)S(1)} %collective-permute-done.32.refs_5_), channel_id=1, source_target_pairs={{0,8},{8,0},{16,24},{24,16},{1,9},{9,1},{17,25},{25,17},{2,10},{10... | collective-permute-start | bytes 589832 | tf_op jit(solution)/shard_map/ppermute | solution.py:177
  139.3 1.8 %collective-permute-start.35 = (bf16[2,192,512]{2,1,0:T(8,128)(2,1)S(1)}, bf16[2,192,512]{2,1,0:T(8,128)(2,1)S(1)}, u32[]{:S(2)}, u32[]{:S(2)}) collective-permute-start(bf16[2,192,512]{2,1,0:T(8,128)(2,1)S(1)} %get-tuple-element.42), channel_id=1, source_target_pairs={{0,8},{8,0},{16,24},{24,16},{1,9},{9,1},{17,25},{25,17},{2,10},{10... | collective-permute-start | bytes 1179656 | tf_op jit(solution)/shard_map/ppermute | solution.py:177
  141.3 7.1 %collective-permute-start.36 = (bf16[192,512]{1,0:T(8,128)(2,1)S(1)}, bf16[192,512]{1,0:T(8,128)(2,1)S(1)}, u32[]{:S(2)}, u32[]{:S(2)}) collective-permute-start(bf16[192,512]{1,0:T(8,128)(2,1)S(1)} %fusion.11), channel_id=1, source_target_pairs={{0,16},{8,24},{16,0},{24,8},{1,17},{9,25},{17,1},{25,9},{2,18},{10... | collective-permute-start | bytes 589832 | tf_op jit(solution)/shard_map/ppermute | solution.py:177
  (16 other events, 121.9 us)

commit v9 on v6

--- a/solution.py
+++ b/solution.py
@@ -26,17 +26,14 @@
     return (slide, index - before)
 
 
-def attend_kernel(sec_ref, near_ref, *refs, heads, masks):
-    far, refs = refs[:3], refs[3:]
-    core_ref, w_ref, out_w_ref, emb_ref, q_ref, k_ref, keep_ref, send_ref = refs
-    core, side = sec_ref[0] % 2, sec_ref[0] // 2
-    own = near_ref.shape[0]
-    keys = jnp.concatenate(
-        [near_ref[...], far[0][...], core_ref[0], core_ref[1], far[1][...], far[2][...]]
-        + [core_ref[2], core_ref[3]],
-        axis=0,
-    )
-    count, rows = keys.shape[0], q_ref.shape[0]
+def attend_kernel(*refs, heads, masks):
+    blocks, (w_ref, out_w_ref, emb_ref, code_ref, keep_ref, send_ref) = refs[:-6], refs[-6:]
+    sec = lax.axis_index("section")
+    core, side = sec % 2, sec // 2
+    own = blocks[0].shape[0]
+    keys = jnp.concatenate([block[...] for block in blocks], axis=0)
+    count, rows = keys.shape[0], own * len(masks)
+    q_code = jnp.transpose(code_ref[:, :rows])
     width = w_ref.shape[1]
     size = width // heads
     scale = math.log2(math.e) / math.sqrt(size)
@@ -59,7 +56,7 @@
             (((1,), (1,)), ((), ())),
             preferred_element_type=jnp.float32,
         )
-        ok = (q_ref[:, h : h + 1] == k_ref[h : h + 1, :]) | diag
+        ok = (q_code[:, h : h + 1] == code_ref[heads + h : heads + h + 1, :]) | diag
         scores = jnp.where(ok, scores, NEG)
         top = jnp.max(scores, axis=1, keepdims=True)
         weight = jnp.exp2((scores - top) * scale)
@@ -74,7 +71,7 @@
         piece = part[:, block * own : (block + 1) * own]
         if block == 0:
             piece = piece + emb
-        at = pl.ds(pl.multiple_of((mask ^ sec_ref[0]) * own, own), own)
+        at = pl.ds(pl.multiple_of((mask ^ sec) * own, own), own)
         for j in range(part.shape[0] // width // 2):
             low = piece[2 * j * width : (2 * j + 1) * width]
             high = piece[(2 * j + 1) * width : (2 * j + 2) * width]
@@ -169,15 +166,6 @@
         down_same, down_other = halves(down, odd), halves(down, 1 - odd)
         ordered = n_seq == 2 and n_dp == 4
 
-        beside = flip(mine, dp=1)
-        both = jnp.concatenate([mine, beside], axis=0)
-        row_blocks = gather_section(both)
-        rows = jnp.concatenate(row_blocks, axis=1)
-        gain = jnp.concatenate(absolute(jnp.split(tile_gain, n_sec)))
-        normed = layer_norm(rows.astype(jnp.float32), gain).astype(jnp.bfloat16)
-        proj_blocks = gather_section(w_proj)
-        proj = jnp.concatenate(proj_blocks, axis=0)
-
         if n_seq == 2:
             masks = (0, 2, 1, 3)
             span = jnp.arange(own_rows, dtype=jnp.int32)
@@ -199,25 +187,47 @@
 
         k_block, picked = codes(k_idx)
         k_code = jnp.where(picked, k_block, -1)
-        q_code = codes(q_idx)[0].T
+        code = jnp.concatenate([k_block, k_code], axis=0)
+
+        own_at = sec * own_rows
+        gain = jnp.concatenate(absolute(jnp.split(tile_gain, n_sec)))
+        out_w = w_out.T
 
         if ordered:
-            g = {(0, 0): pair_same, (0, 2): rotate(pair_same, 2)}
-            d = {(0, 0): down_same, (1, 0): flip(down_same, seq=1)}
-            g[0, 1] = rotate(after(pair_other, g[0, 2], d[1, 0]), 1)
-            g[0, 3] = rotate(after(pair_other, g[0, 2], d[1, 0]), 3)
-            g[1, 0], g[1, 2], g[1, 1] = (flip(g[0, k], seq=1) for k in (0, 2, 1))
-            g[1, 3] = flip(after(g[0, 3], normed), seq=1)
+            g, d = {(0, 0): pair_same}, {(0, 0): down_same}
+            beside = flip(mine, dp=1)
+            mine_x = flip(mine, section=2)
+            g[0, 2] = rotate(pair_same, 2)
+            g[1, 0] = flip(pair_same, seq=1)
+            d[1, 0] = flip(down_same, seq=1)
+            beside_x = flip(beside, section=2)
+            for k in (1, 3):
+                g[0, k] = rotate(after(pair_other, g[0, 2], d[1, 0]), k)
+            g[1, 2] = flip(g[0, 2], seq=1)
+            across = after(jnp.concatenate([mine_x, beside_x], axis=0), g[0, 2])
+            both = after(jnp.concatenate([mine, beside], axis=0), across)
+            both_c, across_c = flip(both, section=1), flip(across, section=1)
+            proj_x = flip(after(w_proj, across), section=2)
+            d[0, 2] = rotate(after(down_same, g[0, 1], g[1, 2], both_c, across_c, code), 2)
+            proj_c = flip(after(w_proj, proj_x, d[0, 2]), section=1)
+            proj_xc = flip(after(proj_x, d[0, 2]), section=1)
+            rows = jnp.concatenate([both, both_c, across, across_c], axis=1)
+            normed = layer_norm(rows.astype(jnp.float32), gain).astype(jnp.bfloat16)
+            g[1, 1], g[1, 3] = flip(g[0, 1], seq=1), flip(after(g[0, 3], normed), seq=1)
             gate_up = place_rows(g)
-            d[0, 2] = rotate(after(down_same, g[0, 1], proj_blocks[1], proj_blocks[3]), 2)
-            there = [row_blocks[1], row_blocks[3], k_code, q_code]
-            d[0, 1] = rotate(after(down_other, d[0, 2], *there), 1)
-            d[0, 3] = rotate(after(down_other, d[0, 2], *there), 3)
+            for k in (1, 3):
+                d[0, k] = rotate(after(down_other, d[0, 2], proj_c, proj_xc, out_w), k)
+            normed = after(normed, d[0, 1], d[0, 3])
+            proj = jnp.concatenate([w_proj, proj_c, proj_x, proj_xc], axis=0)
             for k in (2, 1, 3):
                 d[1, k] = flip(d[0, k], seq=1)
         else:
             gate_up = gather_rows(pair_same, pair_other, seq_at, dp_at)
             down_all = gather_rows(down_same, down_other, seq_at, dp_at)[0]
+            both = jnp.concatenate([mine, flip(mine, dp=1)], axis=0)
+            rows = jnp.concatenate(gather_section(both), axis=1)
+            normed = layer_norm(rows.astype(jnp.float32), gain).astype(jnp.bfloat16)
+            proj = jnp.concatenate(gather_section(w_proj), axis=0)
 
         gate = jnp.dot(normed, gate_up[0], preferred_element_type=jnp.float32)
         up = jnp.dot(normed, gate_up[1], preferred_element_type=jnp.float32)
@@ -268,35 +278,37 @@
         )
         slide_normed = layer_norm(emb, slide_gain).astype(jnp.bfloat16)
 
+        vmem = pl.BlockSpec(memory_space=pltpu.VMEM)
         if n_seq == 2:
-            near = [
+            keys = [
+                slide_normed,
                 flip(slide_normed, section=2),
                 flip(slide_normed, seq=1),
                 flip(slide_normed, section=2, seq=1),
             ]
-            from_core = flip(jnp.stack([slide_normed] + near), section=1)
+            others = [flip(block, section=1) for block in keys]
+            keys = keys[:2] + others[:2] + keys[2:] + others[2:]
         else:
             keys = lax.all_gather(slide_normed, ("seq", "section"), axis=0, tiled=True)
 
         width = w_qkv.shape[2]
         qkv = jnp.swapaxes(w_qkv, 1, 2)
         if n_seq == 2:
-            vmem = pl.BlockSpec(memory_space=pltpu.VMEM)
             keep, send = pl.pallas_call(
                 lambda *refs: attend_kernel(*refs, heads=local_heads, masks=masks),
                 out_shape=[
                     jax.ShapeDtypeStruct((2, width, tokens), jnp.float32),
                     jax.ShapeDtypeStruct((2, width, tokens), jnp.bfloat16),
                 ],
-                in_specs=[pl.BlockSpec(memory_space=pltpu.SMEM)] + [vmem] * 10,
+                in_specs=[vmem] * 12,
                 out_specs=[vmem] * 2,
-                compiler_params=pltpu.CompilerParams(vmem_limit_bytes=40 * 2**20),
+                compiler_params=pltpu.CompilerParams(vmem_limit_bytes=28 * 2**20),
                 cost_estimate=pl.CostEstimate(
                     flops=2 * count * width * (3 * 768 + 2 * local_heads * tokens),
                     bytes_accessed=8 * 2**20,
                     transcendentals=local_heads * tokens * count,
                 ),
-            )(sec[None], slide_normed, *near, from_core, qkv, w_out.T, emb, q_code, k_code)
+            )(*keys, qkv, out_w, emb, code)
         else:
 
             def by_head(x, matrix):
@@ -316,7 +328,7 @@
             att = lax.map(
                 one_head,
                 (by_head(queries, qkv[0]), by_head(keys, qkv[1]), by_head(keys, qkv[2]))
-                + (q_code.T, k_code),
+                + (codes(q_idx)[0], k_code),
             )
             att = att.transpose(1, 0, 2).reshape(tokens, width).astype(jnp.bfloat16)
             parts = jnp.dot(att, w_out, preferred_element_type=jnp.float32)

time: 147 us -> 142 us (0.966)
  other arithmetic: 15.3 us -> 9.34 us
  waiting for transfers between devices: 62.2 us -> 67.7 us
  local copies, waits for them, and re-layouts: 12.8 us -> 10.6 us
  matrix products: 13.6 us -> 11.5 us
    ppermute x25 -> x29, waiting for transfers between devices: 44.8 us -> 53.2 us  [flip(): return lax.ppermute(x, names if len(names) > 1 else names[0], pairs)]
    ppermute x6, waiting for transfers between devices: 17.4 us -> 14.4 us  [rotate(): return lax.ppermute(x, 'dp', [(i, (i + k) % n_dp) for i in range(n_dp)])]
    dynamic_update_slice x14, local copies, waits for them, and re-layouts: 5.27 us -> 2.36 us  [place_rows(): whole = lax.dynamic_update_slice(whole, block, (0, row_of(y, k, rows), 0))]
    reduce_sum x1, other arithmetic: 2.91 us -> 0.48 us  [layer_norm(): mean = jnp.mean(rows, axis=-1, keepdims=True)]
    add x1, other arithmetic: 2.68 us -> 0.74 us  [codes(): block = slide[None, :] * count + pos[None, :] // seg_len[:, None]]
    ppermute x25 -> x29, starting transfers between devices: 22.8 us -> 24.1 us  [flip(): return lax.ppermute(x, names if len(names) > 1 else names[0], pairs)]
    unnamed x34 -> x37, local copies, waits for them, and re-layouts: 3.5 us -> 3.37 us
  transfers between devices with their start and end apart: 31 -> 35, of which waited for: 16 -> 20; matrix products, arithmetic and copies ran while one was open for 19% -> 14% of each run, Pallas kernels for 0% -> 0%
where the time goes in v9:
time: 142 us
  waiting for transfers between devices  67.7 us (48%)
  starting transfers between devices  36.5 us (26%)
  matrix products  11.5 us (8%)
  local copies, waits for them, and re-layouts  10.6 us (7%)
  other arithmetic  9.34 us (7%)
  Pallas kernels  5.34 us (4%)
    ppermute x29, waiting for transfers between devices, flip(): return lax.ppermute(x, names if len(names) > 1 else names[0], pairs)  53.2 us
    ppermute x29, starting transfers between devices, flip(): return lax.ppermute(x, names if len(names) > 1 else names[0], pairs)  24.1 us
    ppermute x6, waiting for transfers between devices, rotate(): return lax.ppermute(x, 'dp', [(i, (i + k) % n_dp) for i in range(n_dp)])  14.4 us
    ppermute x6, starting transfers between devices, rotate(): return lax.ppermute(x, 'dp', [(i, (i + k) % n_dp) for i in range(n_dp)])  12.4 us
    pallas_call x1, Pallas kernels, per_device(): pl.pallas_call(lambda *refs: attend_kernel(*refs, heads=local_heads, mask...  5.34 us
    dot_general x2, matrix products, project(): lax.dot_general(x, folded, (((x.ndim - 1,), (1,)), ((), ())), preferred_e...  3.62 us
    unnamed x37, local copies, waits for them, and re-layouts  3.37 us
  transfers between devices with their start and end apart: 35, of which 20 were waited for; matrix products, arithmetic and copies ran while one was open for 14% of the time, Pallas kernels for 0%

profile of v9, /device:TPU:0, one launch (start us, length us, event | category | flops | bytes accessed | tf_op | source)
XLA Modules:
  0.0 141.7 jit_solution(8420217178526202501)
XLA Ops:
  0.0 2.1 %fusion.18 = (bf16[2,192,512]{2,1,0:T(8,128)(2,1)}, bf16[2,192,512]{2,1,0:T(8,128)(2,1)S(1)}) fusion(s32[]{:T(128)S(6)} %select_n.238, bf16[1,192,1024]{2,1,0:T(8,128)(2,1)} %bitcast.89, bf16[1,192,1024]{2,1,0:T(8,128)(2,1)} %bitcast.90, s32[]{:T(128)S(6)} %select_n.236), kind=kLoop, calls=%fused_computation.33 | loop fusion | flops 1572864 | bytes 1572872 | tf_op jit(solution)/shard_map/stack | solution.py:163
  2.1 4.0 %collective-permute-start.3 = (bf16[2,192,512]{2,1,0:T(8,128)(2,1)S(1)}, bf16[2,192,512]{2,1,0:T(8,128)(2,1)}, u32[]{:S(2)}, u32[]{:S(2)}) collective-permute-start(bf16[2,192,512]{2,1,0:T(8,128)(2,1)S(1)} %get-tuple-element.44), channel_id=1, source_target_pairs={{0,2},{1,3},{2,0},{3,1},{4,6},{5,7},{6,4},{7,5},{8,10},{9,11},{10,... | collective-permute-start | bytes 1179656 | tf_op jit(solution)/shard_map/ppermute | solution.py:101
  6.2 1.5 %collective-permute-start.15 = (bf16[2,192,512]{2,1,0:T(8,128)(2,1)S(1)}, bf16[2,192,512]{2,1,0:T(8,128)(2,1)}, u32[]{:S(2)}, u32[]{:S(2)}) collective-permute-start(bf16[2,192,512]{2,1,0:T(8,128)(2,1)S(1)} %get-tuple-element.44), channel_id=1, source_target_pairs={{0,4},{4,0},{1,5},{5,1},{2,6},{6,2},{3,7},{7,3},{8,12},{12,8},{9,1... | collective-permute-start | bytes 1179656 | tf_op jit(solution)/shard_map/ppermute | solution.py:98
  7.7 1.6 %collective-permute-start = (bf16[512,384]{1,0:T(8,128)(2,1)}, bf16[512,384]{1,0:T(8,128)(2,1)}, u32[]{:S(2)}, u32[]{:S(2)}) collective-permute-start(bf16[512,384]{1,0:T(8,128)(2,1)} %bitcast.91), channel_id=1, source_target_pairs={{0,1},{1,0},{2,3},{3,2},{4,5},{5,4},{6,7},{7,6},{8,9},{9,8},{10,11... | collective-permute-start | bytes 1179656 | tf_op jit(solution)/shard_map/ppermute | solution.py:98
  9.3 1.5 %collective-permute-start.1 = (bf16[512,384]{1,0:T(8,128)(2,1)}, bf16[512,384]{1,0:T(8,128)(2,1)}, u32[]{:S(2)}, u32[]{:S(2)}) collective-permute-start(bf16[512,384]{1,0:T(8,128)(2,1)} %bitcast.92), channel_id=1, source_target_pairs={{0,16},{8,24},{16,0},{24,8},{1,17},{9,25},{17,1},{25,9},{2,18},{10... | collective-permute-start | bytes 1179656 | tf_op jit(solution)/shard_map/ppermute | solution.py:98
  10.8 1.8 %dynamic-slice_bitcast_fusion.1 = (bf16[1,192,512]{2,1,0:T(8,128)(2,1)}, bf16[1,192,512]{2,1,0:T(8,128)(2,1)}) fusion(bf16[1024,192]{0,1:T(8,128)(2,1)} %param.16, s32[]{:T(128)S(6)} %select_n.238, s32[]{:T(128)S(6)} %select_n.236), kind=kLoop, calls=%fused_computation.60 | loop fusion | bytes 786440 | tf_op jit(solution)/shard_map/dynamic_slice | solution.py:161
  14.6 10.9 %collective-permute-done = bf16[512,384]{1,0:T(8,128)(2,1)} collective-permute-done((bf16[512,384]{1,0:T(8,128)(2,1)}, bf16[512,384]{1,0:T(8,128)(2,1)}, u32[]{:S(2)}, u32[]{:S(2)}) %collective-permute-start) | collective-permute-done | bytes 393248 | tf_op jit(solution)/shard_map/ppermute | solution.py:98
  25.6 1.5 %collective-permute-start.2 = (bf16[512,384]{1,0:T(8,128)(2,1)}, bf16[512,384]{1,0:T(8,128)(2,1)}, u32[]{:S(2)}, u32[]{:S(2)}) collective-permute-start(bf16[512,384]{1,0:T(8,128)(2,1)} %collective-permute-done), channel_id=1, source_target_pairs={{0,16},{8,24},{16,0},{24,8},{1,17},{9,25},{17,1},{25,9},{2,18},{10... | collective-permute-start | bytes 1179656 | tf_op jit(solution)/shard_map/ppermute | solution.py:98
  27.4 1.1 constant_dynamic-update-slice_fusion.8
  28.5 3.8 %collective-permute-start.16 = (bf16[2,192,512]{2,1,0:T(8,128)(2,1)}, bf16[2,192,512]{2,1,0:T(8,128)(2,1)S(1)}, u32[]{:S(2)}, u32[]{:S(2)}) collective-permute-start(bf16[2,192,512]{2,1,0:T(8,128)(2,1)} %get-tuple-element.23), channel_id=1, source_target_pairs={{0,3},{1,0},{2,1},{3,2},{4,7},{5,4},{6,5},{7,6},{8,11},{9,8},{10,9... | collective-permute-start | bytes 1179656 | tf_op jit(solution)/shard_map/ppermute | solution.py:101
  32.4 1.2 pad_maximum_fusion
  34.4 1.2 pad_maximum_fusion.1
  35.7 1.0 constant_dynamic-update-slice_fusion.17
  36.7 1.0 constant_dynamic-update-slice_fusion.16
  38.3 3.8 %collective-permute-done.8 = bf16[2,192,512]{2,1,0:T(8,128)(2,1)S(1)} collective-permute-done((bf16[2,192,512]{2,1,0:T(8,128)(2,1)}, bf16[2,192,512]{2,1,0:T(8,128)(2,1)S(1)}, u32[]{:S(2)}, u32[]{:S(2)}) %collective-permute-start.8) | collective-permute-done | bytes 393248 | tf_op jit(solution)/shard_map/ppermute | solution.py:101
  42.2 0.9 collective-permute-start.17
  43.1 3.0 %collective-permute-done.16 = bf16[2,192,512]{2,1,0:T(8,128)(2,1)S(1)} collective-permute-done((bf16[2,192,512]{2,1,0:T(8,128)(2,1)}, bf16[2,192,512]{2,1,0:T(8,128)(2,1)S(1)}, u32[]{:S(2)}, u32[]{:S(2)}) %collective-permute-start.16) | collective-permute-done | bytes 393248 | tf_op jit(solution)/shard_map/ppermute | solution.py:101
  47.0 3.3 %collective-permute-done.17 = bf16[2,192,512]{2,1,0:T(8,128)(2,1)S(1)} collective-permute-done((bf16[2,192,512]{2,1,0:T(8,128)(2,1)S(1)}, bf16[2,192,512]{2,1,0:T(8,128)(2,1)S(1)}, u32[]{:S(2)}, u32[]{:S(2)}) %collective-permute-start.17) | collective-permute-done | bytes 393248 | tf_op jit(solution)/shard_map/ppermute | solution.py:98
  51.4 1.0 fusion.2
  53.0 1.0 fusion.4
  54.0 1.6 %collective-permute-start.18 = (bf16[2,192,512]{2,1,0:T(8,128)(2,1)S(1)}, bf16[2,192,512]{2,1,0:T(8,128)(2,1)S(1)}, u32[]{:S(2)}, u32[]{:S(2)}) collective-permute-start(bf16[2,192,512]{2,1,0:T(8,128)(2,1)S(1)} %collective-permute-done.16), channel_id=1, source_target_pairs={{0,4},{4,0},{1,5},{5,1},{2,6},{6,2},{3,7},{7,3},{8,12},{12,8},{9,1... | collective-permute-start | bytes 1179656 | tf_op jit(solution)/shard_map/ppermute | solution.py:98
  55.6 5.8 %collective-permute-done.6 = bf16[384,768]{1,0:T(8,128)(2,1)S(1)} collective-permute-done((bf16[384,768]{1,0:T(8,128)(2,1)S(1)}, bf16[384,768]{1,0:T(8,128)(2,1)S(1)}, u32[]{:S(2)}, u32[]{:S(2)}) %collective-permute-start.6) | collective-permute-done | bytes 589856 | tf_op jit(solution)/shard_map/ppermute | solution.py:98
  62.4 1.6 %collective-permute-start.19 = (bf16[1,192,512]{2,1,0:T(8,128)(2,1)S(1)}, bf16[1,192,512]{2,1,0:T(8,128)(2,1)S(1)}, u32[]{:S(2)}, u32[]{:S(2)}) collective-permute-start(bf16[1,192,512]{2,1,0:T(8,128)(2,1)S(1)} %collective-permute-done.10), channel_id=1, source_target_pairs={{0,4},{4,0},{1,5},{5,1},{2,6},{6,2},{3,7},{7,3},{8,12},{12,8},{9,1... | collective-permute-start | bytes 589832 | tf_op jit(solution)/shard_map/ppermute | solution.py:98
  64.8 3.5 %collective-permute-start.14 = (bf16[1,192,512]{2,1,0:T(8,128)(2,1)S(1)}, bf16[1,192,512]{2,1,0:T(8,128)(2,1)S(1)}, u32[]{:S(2)}, u32[]{:S(2)}) collective-permute-start(bf16[1,192,512]{2,1,0:T(8,128)(2,1)S(1)} %copy-done.9), channel_id=1, source_target_pairs={{0,3},{1,0},{2,1},{3,2},{4,7},{5,4},{6,5},{7,6},{8,11},{9,8},{10,9... | collective-permute-start | bytes 589832 | tf_op jit(solution)/shard_map/ppermute | solution.py:101
  68.5 5.6 %collective-permute-done.13 = bf16[1,192,512]{2,1,0:T(8,128)(2,1)S(1)} collective-permute-done((bf16[1,192,512]{2,1,0:T(8,128)(2,1)S(1)}, bf16[1,192,512]{2,1,0:T(8,128)(2,1)S(1)}, u32[]{:S(2)}, u32[]{:S(2)}) %collective-permute-start.13) | collective-permute-done | bytes 196640 | tf_op jit(solution)/shard_map/ppermute | solution.py:101
  74.2 1.6 %collective-permute-done.14 = bf16[1,192,512]{2,1,0:T(8,128)(2,1)S(1)} collective-permute-done((bf16[1,192,512]{2,1,0:T(8,128)(2,1)S(1)}, bf16[1,192,512]{2,1,0:T(8,128)(2,1)S(1)}, u32[]{:S(2)}, u32[]{:S(2)}) %collective-permute-start.14) | collective-permute-done | bytes 196640 | tf_op jit(solution)/shard_map/ppermute | solution.py:101
  75.7 1.8 %fusion.6 = f32[1024,512]{1,0:T(8,128)S(1)} fusion(bf16[1024,1536]{1,0:T(8,128)(2,1)S(1)} %fusion.4, bf16[2,1536,512]{2,1,0:T(8,128)(2,1)S(1)} %constant_dynamic-update-slice_fusion.11), kind=kOutput, calls=%fused_computation.11 | convolution fusion | flops 1610612736 | bytes 6815744 | tf_op jit(solution)/shard_map/dot_general | solution.py:232
  77.5 2.0 %multiply_convert_fusion = bf16[1024,512]{1,0:T(8,128)(2,1)S(1)} fusion(f32[1024,512]{1,0:T(8,128)S(1)} %fusion.6, bf16[1024,1536]{1,0:T(8,128)(2,1)S(1)} %fusion.4, bf16[2,1536,512]{2,1,0:T(8,128)(2,1)S(1)} %constant_dynamic-update-slice_fusion.11), kind=kOutput, calls=%fused_computation.7 | convolution fusion | flops 1613758464 | bytes 7864320 | tf_op jit(solution)/shard_map/dot_general | solution.py:233
  79.6 1.6 %collective-permute-start.20 = (bf16[1,192,512]{2,1,0:T(8,128)(2,1)S(1)}, bf16[1,192,512]{2,1,0:T(8,128)(2,1)S(1)}, u32[]{:S(2)}, u32[]{:S(2)}) collective-permute-start(bf16[1,192,512]{2,1,0:T(8,128)(2,1)S(1)} %collective-permute-done.13), channel_id=1, source_target_pairs={{0,4},{4,0},{1,5},{5,1},{2,6},{6,2},{3,7},{7,3},{8,12},{12,8},{9,1... | collective-permute-start | bytes 589832 | tf_op jit(solution)/shard_map/ppermute | solution.py:98
  81.2 1.4 fusion.51
  83.2 3.9 %collective-permute-done.20 = bf16[1,192,512]{2,1,0:T(8,128)(2,1)S(1)} collective-permute-done((bf16[1,192,512]{2,1,0:T(8,128)(2,1)S(1)}, bf16[1,192,512]{2,1,0:T(8,128)(2,1)S(1)}, u32[]{:S(2)}, u32[]{:S(2)}) %collective-permute-start.20) | collective-permute-done | bytes 196640 | tf_op jit(solution)/shard_map/ppermute | solution.py:98
  87.5 2.3 %collective-permute-done.21 = bf16[1,192,512]{2,1,0:T(8,128)(2,1)S(1)} collective-permute-done((bf16[1,192,512]{2,1,0:T(8,128)(2,1)S(1)}, bf16[1,192,512]{2,1,0:T(8,128)(2,1)S(1)}, u32[]{:S(2)}, u32[]{:S(2)}) %collective-permute-start.21) | collective-permute-done | bytes 196640 | tf_op jit(solution)/shard_map/ppermute | solution.py:98
  91.1 1.5 %convolution_convert_fusion = bf16[2,2,128,768]{3,2,1,0:T(8,128)(2,1)} fusion(bf16[768,512,1,1]{1,0,3,2:T(8,128)(2,1)S(1)} %fusion.7, bf16[2,2,2,128,512]{4,3,2,1,0:T(8,128)(2,1)S(1)} %bitcast.94, s32[]{:T(128)S(6)} %select_n.279), kind=kOutput, calls=%fused_computation.14 | convolution fusion | flops 403046400 | bytes 2097156 | tf_op jit(solution)/shard_map/dot_general | solution.py:255
  92.6 2.6 %collective-permute-done.22 = bf16[2,2,128,768]{3,2,1,0:T(8,128)(2,1)} collective-permute-done((bf16[2,2,128,768]{3,2,1,0:T(8,128)(2,1)}, bf16[2,2,128,768]{3,2,1,0:T(8,128)(2,1)}, u32[]{:S(2)}, u32[]{:S(2)}) %collective-permute-start.22) | collective-permute-done | bytes 786464 | tf_op jit(solution)/shard_map/ppermute | solution.py:98
  95.2 2.1 %convert_add_fusion = f32[2,2,128,768]{3,2,1,0:T(8,128)S(1)} fusion(bf16[2,2,128,768]{3,2,1,0:T(8,128)(2,1)} %collective-permute-done.22, bf16[768,512,1,1]{1,0,3,2:T(8,128)(2,1)} %copy-done.3, bf16[2,2,2,128,512]{4,3,2,1,0:T(8,128)(2,1)} %bitcast.95, s32[]{:T(128)S(6)} %select_n.278), kind=kOutput, calls=%fused_computation.12 | convolution fusion | flops 403439616 | bytes 3670020 | tf_op jit(solution)/shard_map/dot_general | solution.py:255
  98.3 1.8 %collective-permute-start.23 = (bf16[128,768]{1,0:T(8,128)(2,1)}, bf16[128,768]{1,0:T(8,128)(2,1)S(1)}, u32[]{:S(2)}, u32[]{:S(2)}) collective-permute-start(bf16[128,768]{1,0:T(8,128)(2,1)} %get-tuple-element.45), channel_id=1, source_target_pairs={{0,16},{8,24},{16,0},{24,8},{1,17},{9,25},{17,1},{25,9},{2,18},{10... | collective-permute-start | bytes 589832 | tf_op jit(solution)/shard_map/ppermute | solution.py:98
  100.1 0.9 collective-permute-start.25
  101.9 1.5 %slice.42 = bf16[512,1536]{1,0:T(8,128)(2,1)S(1)} slice(bf16[1024,1536]{1,0:T(8,128)(2,1)} %copy-done.1), slice={[0:512], [0:1536]} | slice | bytes 3145728 | tf_op jit(solution)/shard_map/slice | solution.py:268
  103.4 6.3 %collective-permute-done.23 = bf16[128,768]{1,0:T(8,128)(2,1)S(1)} collective-permute-done((bf16[128,768]{1,0:T(8,128)(2,1)}, bf16[128,768]{1,0:T(8,128)(2,1)S(1)}, u32[]{:S(2)}, u32[]{:S(2)}) %collective-permute-start.23) | collective-permute-done | bytes 196640 | tf_op jit(solution)/shard_map/ppermute | solution.py:98
  111.1 1.8 %fusion.50 = (f32[128]{0:T(128)S(1)}, f32[128,768]{1,0:T(8,128)S(1)}) fusion(bf16[128,768]{1,0:T(8,128)(2,1)} %copy-done.8, bf16[128,768]{1,0:T(8,128)(2,1)} %collective-permute-done.24, bf16[128,768]{1,0:T(8,128)(2,1)S(1)} %collective-permute-done.23, f32[2,2,128,768]{3,2,1,0:T(8,128)} %copy-done.2, s32[]{:T(128)S(6)} %select_n.281, ...), kind=kOutput, calls=%fused_computation.128 | convolution fusion | flops 302776192 | bytes 4129288 | tf_op jit(solution)/shard_map/dot_general | solution.py:267
  113.3 1.8 %collective-permute-start.26 = (bf16[128,768]{1,0:T(8,128)(2,1)S(1)}, bf16[128,768]{1,0:T(8,128)(2,1)S(1)}, u32[]{:S(2)}, u32[]{:S(2)}) collective-permute-start(bf16[128,768]{1,0:T(8,128)(2,1)S(1)} %multiply_convert_fusion.1.refs_0_), channel_id=1, source_target_pairs={{0,16},{8,24},{16,0},{24,8},{1,17},{9,25},{17,1},{25,9},{2,18},{10... | collective-permute-start | bytes 589832 | tf_op jit(solution)/shard_map/ppermute | solution.py:98
  115.0 1.5 %collective-permute-start.29 = (bf16[128,768]{1,0:T(8,128)(2,1)S(1)}, bf16[128,768]{1,0:T(8,128)(2,1)S(1)}, u32[]{:S(2)}, u32[]{:S(2)}) collective-permute-start(bf16[128,768]{1,0:T(8,128)(2,1)S(1)} %multiply_convert_fusion.1.refs_0_), channel_id=1, source_target_pairs={{0,4},{4,0},{1,5},{5,1},{2,6},{6,2},{3,7},{7,3},{8,12},{12,8},{9,1... | collective-permute-start | bytes 589832 | tf_op jit(solution)/shard_map/ppermute | solution.py:98
  116.8 4.3 %collective-permute-done.26.refs_1_ = bf16[128,768]{1,0:T(8,128)(2,1)S(1)} collective-permute-done((bf16[128,768]{1,0:T(8,128)(2,1)S(1)}, bf16[128,768]{1,0:T(8,128)(2,1)S(1)}, u32[]{:S(2)}, u32[]{:S(2)}) %collective-permute-start.26) | collective-permute-done | bytes 196640 | tf_op jit(solution)/shard_map/ppermute | solution.py:98
  121.1 3.8 %collective-permute-done.29.refs_4_ = bf16[128,768]{1,0:T(8,128)(2,1)S(1)} collective-permute-done((bf16[128,768]{1,0:T(8,128)(2,1)S(1)}, bf16[128,768]{1,0:T(8,128)(2,1)S(1)}, u32[]{:S(2)}, u32[]{:S(2)}) %collective-permute-start.29) | collective-permute-done | bytes 196640 | tf_op jit(solution)/shard_map/ppermute | solution.py:98
  126.6 5.3 %shard_map.118 = (f32[2,192,512]{2,1,0:T(8,128)S(1)}, bf16[2,192,512]{2,1,0:T(8,128)(2,1)S(1)}) custom-call(bf16[128,768]{1,0:T(8,128)(2,1)S(1)} %multiply_convert_fusion.1.refs_0_, bf16[128,768]{1,0:T(8,128)(2,1)S(1)} %collective-permute-done.26.refs_1_, bf16[128,768]{1,0:T(8,128)(2,1)S(1)} %collective-permute-done.27.refs_2_, ...), custom_call_target="tpu_custom_call" | custom-call | flops 2516582400 | bytes 8388608 | tf_op jit(solution)/shard_map/pallas_call | solution.py:297
  132.2 1.5 %collective-permute-done.33 = bf16[2,192,512]{2,1,0:T(8,128)(2,1)S(1)} collective-permute-done((bf16[2,192,512]{2,1,0:T(8,128)(2,1)S(1)}, bf16[2,192,512]{2,1,0:T(8,128)(2,1)S(1)}, u32[]{:S(2)}, u32[]{:S(2)}) %collective-permute-start.33) | collective-permute-done | bytes 393248 | tf_op jit(solution)/shard_map/ppermute | solution.py:98
  133.9 0.9 collective-permute-start.34
  134.8 6.2 %collective-permute-done.34 = bf16[192,512]{1,0:T(8,128)(2,1)S(1)} collective-permute-done((bf16[192,512]{1,0:T(8,128)(2,1)S(1)}, bf16[192,512]{1,0:T(8,128)(2,1)S(1)}, u32[]{:S(2)}, u32[]{:S(2)}) %collective-permute-start.34) | collective-permute-done | bytes 196640 | tf_op jit(solution)/shard_map/ppermute | solution.py:98
  (131 shorter events, 17.0 us)
Async XLA Ops:
  0.0 13.1 %copy-start.14 = (s32[1,3]{1,0:T(1,128)S(1)}, s32[1,3]{1,0:T(1,128)}, u32[]{:S(2)}) copy-start(s32[1,3]{1,0:T(1,128)} %param.21) | copy-start | bytes 40
  0.0 13.2 %copy-start.13 = (s32[4]{0:T(128)S(1)}, s32[4]{0:T(128)}, u32[]{:S(2)}) copy-start(s32[4]{0:T(128)} %param.23) | copy-start | bytes 52
  0.0 13.4 %copy-start.12 = (s32[4]{0:T(128)S(1)}, s32[4]{0:T(128)}, u32[]{:S(2)}) copy-start(s32[4]{0:T(128)} %param.22) | copy-start | bytes 52
  0.0 14.4 %copy-start.10 = (f32[1536]{0:T(1024)S(1)}, f32[1536]{0:T(1024)}, u32[]{:S(2)}) copy-start(f32[1536]{0:T(1024)} %param.13) | copy-start | bytes 18436
  0.0 27.1 %copy-start.6 = (bf16[192,768]{1,0:T(8,128)(2,1)S(1)}, bf16[192,768]{1,0:T(8,128)(2,1)}, u32[]{:S(2)}) copy-start(bf16[192,768]{1,0:T(8,128)(2,1)} %param.20) | copy-start | bytes 884740
  2.1 26.3 %collective-permute-start.3 = (bf16[2,192,512]{2,1,0:T(8,128)(2,1)S(1)}, bf16[2,192,512]{2,1,0:T(8,128)(2,1)}, u32[]{:S(2)}, u32[]{:S(2)}) collective-permute-start(bf16[2,192,512]{2,1,0:T(8,128)(2,1)S(1)} %get-tuple-element.44), channel_id=1, source_target_pairs={{0,2},{1,3},{2,0},{3,1},{4,6},{5,7},{6,4},{7,5},{8,10},{9,11},{10,... | collective-permute-start | bytes 1179656 | tf_op jit(solution)/shard_map/ppermute | solution.py:101
  6.2 30.5 %collective-permute-start.15 = (bf16[2,192,512]{2,1,0:T(8,128)(2,1)S(1)}, bf16[2,192,512]{2,1,0:T(8,128)(2,1)}, u32[]{:S(2)}, u32[]{:S(2)}) collective-permute-start(bf16[2,192,512]{2,1,0:T(8,128)(2,1)S(1)} %get-tuple-element.44), channel_id=1, source_target_pairs={{0,4},{4,0},{1,5},{5,1},{2,6},{6,2},{3,7},{7,3},{8,12},{12,8},{9,1... | collective-permute-start | bytes 1179656 | tf_op jit(solution)/shard_map/ppermute | solution.py:98
  7.7 17.9 %collective-permute-start = (bf16[512,384]{1,0:T(8,128)(2,1)}, bf16[512,384]{1,0:T(8,128)(2,1)}, u32[]{:S(2)}, u32[]{:S(2)}) collective-permute-start(bf16[512,384]{1,0:T(8,128)(2,1)} %bitcast.91), channel_id=1, source_target_pairs={{0,1},{1,0},{2,3},{3,2},{4,5},{5,4},{6,7},{7,6},{8,9},{9,8},{10,11... | collective-permute-start | bytes 1179656 | tf_op jit(solution)/shard_map/ppermute | solution.py:98
  9.3 24.5 %collective-permute-start.1 = (bf16[512,384]{1,0:T(8,128)(2,1)}, bf16[512,384]{1,0:T(8,128)(2,1)}, u32[]{:S(2)}, u32[]{:S(2)}) collective-permute-start(bf16[512,384]{1,0:T(8,128)(2,1)} %bitcast.92), channel_id=1, source_target_pairs={{0,16},{8,24},{16,0},{24,8},{1,17},{9,25},{17,1},{25,9},{2,18},{10... | collective-permute-start | bytes 1179656 | tf_op jit(solution)/shard_map/ppermute | solution.py:98
  12.6 15.9 %collective-permute-start.7 = (bf16[1,192,512]{2,1,0:T(8,128)(2,1)}, bf16[1,192,512]{2,1,0:T(8,128)(2,1)S(1)}, u32[]{:S(2)}, u32[]{:S(2)}) collective-permute-start(bf16[1,192,512]{2,1,0:T(8,128)(2,1)} %get-tuple-element.24), channel_id=1, source_target_pairs={{0,4},{4,0},{1,5},{5,1},{2,6},{6,2},{3,7},{7,3},{8,12},{12,8},{9,1... | collective-permute-start | bytes 589832 | tf_op jit(solution)/shard_map/ppermute | solution.py:98
  25.6 8.8 %collective-permute-start.2 = (bf16[512,384]{1,0:T(8,128)(2,1)}, bf16[512,384]{1,0:T(8,128)(2,1)}, u32[]{:S(2)}, u32[]{:S(2)}) collective-permute-start(bf16[512,384]{1,0:T(8,128)(2,1)} %collective-permute-done), channel_id=1, source_target_pairs={{0,16},{8,24},{16,0},{24,8},{1,17},{9,25},{17,1},{25,9},{2,18},{10... | collective-permute-start | bytes 1179656 | tf_op jit(solution)/shard_map/ppermute | solution.py:98
  28.5 13.7 %collective-permute-start.8 = (bf16[2,192,512]{2,1,0:T(8,128)(2,1)}, bf16[2,192,512]{2,1,0:T(8,128)(2,1)S(1)}, u32[]{:S(2)}, u32[]{:S(2)}) collective-permute-start(bf16[2,192,512]{2,1,0:T(8,128)(2,1)} %get-tuple-element.23), channel_id=1, source_target_pairs={{0,1},{1,2},{2,3},{3,0},{4,5},{5,6},{6,7},{7,4},{8,9},{9,10},{10,1... | collective-permute-start | bytes 1179656 | tf_op jit(solution)/shard_map/ppermute | solution.py:101
  28.5 17.6 %collective-permute-start.16 = (bf16[2,192,512]{2,1,0:T(8,128)(2,1)}, bf16[2,192,512]{2,1,0:T(8,128)(2,1)S(1)}, u32[]{:S(2)}, u32[]{:S(2)}) collective-permute-start(bf16[2,192,512]{2,1,0:T(8,128)(2,1)} %get-tuple-element.23), channel_id=1, source_target_pairs={{0,3},{1,0},{2,1},{3,2},{4,7},{5,4},{6,5},{7,6},{8,11},{9,8},{10,9... | collective-permute-start | bytes 1179656 | tf_op jit(solution)/shard_map/ppermute | solution.py:101
  33.8 12.4 %copy-start.5 = (bf16[384,768]{1,0:T(8,128)(2,1)S(1)}, bf16[384,768]{1,0:T(8,128)(2,1)}, u32[]{:S(2)}) copy-start(bf16[384,768]{1,0:T(8,128)(2,1)} %param.17) | copy-start | bytes 1769476
  33.8 13.0 %collective-permute-start.9 = (bf16[2,192,512]{2,1,0:T(8,128)(2,1)}, bf16[2,192,512]{2,1,0:T(8,128)(2,1)S(1)}, u32[]{:S(2)}, u32[]{:S(2)}) collective-permute-start(bf16[2,192,512]{2,1,0:T(8,128)(2,1)} %collective-permute-done.3), channel_id=1, source_target_pairs={{0,4},{4,0},{1,5},{5,1},{2,6},{6,2},{3,7},{7,3},{8,12},{12,8},{9,1... | collective-permute-start | bytes 1179656 | tf_op jit(solution)/shard_map/ppermute | solution.py:98
  35.6 14.7 %collective-permute-start.4 = (bf16[1024,384]{1,0:T(8,128)(2,1)S(1)}, bf16[1024,384]{1,0:T(8,128)(2,1)S(1)}, u32[]{:S(2)}, u32[]{:S(2)}) collective-permute-start(bf16[1024,384]{1,0:T(8,128)(2,1)S(1)} %pad_maximum_fusion), channel_id=1, source_target_pairs={{0,8},{8,0},{16,24},{24,16},{1,9},{9,1},{17,25},{25,17},{2,10},{10... | collective-permute-start | bytes 2359304 | tf_op jit(solution)/shard_map/ppermute | solution.py:98
  37.8 12.9 %collective-permute-start.5 = (bf16[1024,384]{1,0:T(8,128)(2,1)S(1)}, bf16[1024,384]{1,0:T(8,128)(2,1)S(1)}, u32[]{:S(2)}, u32[]{:S(2)}) collective-permute-start(bf16[1024,384]{1,0:T(8,128)(2,1)S(1)} %pad_maximum_fusion.1), channel_id=1, source_target_pairs={{0,8},{8,0},{16,24},{24,16},{1,9},{9,1},{17,25},{25,17},{2,10},{10... | collective-permute-start | bytes 2359304 | tf_op jit(solution)/shard_map/ppermute | solution.py:98
  42.2 8.1 %collective-permute-start.17 = (bf16[2,192,512]{2,1,0:T(8,128)(2,1)S(1)}, bf16[2,192,512]{2,1,0:T(8,128)(2,1)S(1)}, u32[]{:S(2)}, u32[]{:S(2)}) collective-permute-start(bf16[2,192,512]{2,1,0:T(8,128)(2,1)S(1)} %collective-permute-done.8), channel_id=1, source_target_pairs={{0,4},{4,0},{1,5},{5,1},{2,6},{6,2},{3,7},{7,3},{8,12},{12,8},{9,1... | collective-permute-start | bytes 1179656 | tf_op jit(solution)/shard_map/ppermute | solution.py:98
  46.2 15.2 %collective-permute-start.6 = (bf16[384,768]{1,0:T(8,128)(2,1)S(1)}, bf16[384,768]{1,0:T(8,128)(2,1)S(1)}, u32[]{:S(2)}, u32[]{:S(2)}) collective-permute-start(bf16[384,768]{1,0:T(8,128)(2,1)S(1)} %copy-done.5), channel_id=1, source_target_pairs={{0,16},{8,24},{16,0},{24,8},{1,17},{9,25},{17,1},{25,9},{2,18},{10... | collective-permute-start | bytes 1769480 | tf_op jit(solution)/shard_map/ppermute | solution.py:98
  50.9 2.1 %copy-start.1 = (bf16[1024,1536]{1,0:T(8,128)(2,1)}, bf16[1024,1536]{1,0:T(8,128)(2,1)S(1)}, u32[]{:S(2)}) copy-start(bf16[1024,1536]{1,0:T(8,128)(2,1)S(1)} %constant_dynamic-update-slice_fusion) | copy-start | bytes 9437188
  52.4 10.0 %copy-start.4 = (bf16[1024,192]{0,1:T(8,128)(2,1)S(1)}, bf16[1024,192]{0,1:T(8,128)(2,1)}, u32[]{:S(2)}) copy-start(bf16[1024,192]{0,1:T(8,128)(2,1)} %param.16) | copy-start | bytes 1179652
  52.4 9.4 %collective-permute-start.10 = (bf16[1,192,512]{2,1,0:T(8,128)(2,1)}, bf16[1,192,512]{2,1,0:T(8,128)(2,1)S(1)}, u32[]{:S(2)}, u32[]{:S(2)}) collective-permute-start(bf16[1,192,512]{2,1,0:T(8,128)(2,1)} %get-tuple-element.24), channel_id=1, source_target_pairs={{0,2},{1,3},{2,0},{3,1},{4,6},{5,7},{6,4},{7,5},{8,10},{9,11},{10,... | collective-permute-start | bytes 589832 | tf_op jit(solution)/shard_map/ppermute | solution.py:101
  54.0 10.6 %copy-start.9 = (bf16[1,192,512]{2,1,0:T(8,128)(2,1)S(1)}, bf16[1,192,512]{2,1,0:T(8,128)(2,1)}, u32[]{:S(2)}) copy-start(bf16[1,192,512]{2,1,0:T(8,128)(2,1)} %get-tuple-element.27) | copy-start | bytes 589828
  54.0 10.0 %collective-permute-start.18 = (bf16[2,192,512]{2,1,0:T(8,128)(2,1)S(1)}, bf16[2,192,512]{2,1,0:T(8,128)(2,1)S(1)}, u32[]{:S(2)}, u32[]{:S(2)}) collective-permute-start(bf16[2,192,512]{2,1,0:T(8,128)(2,1)S(1)} %collective-permute-done.16), channel_id=1, source_target_pairs={{0,4},{4,0},{1,5},{5,1},{2,6},{6,2},{3,7},{7,3},{8,12},{12,8},{9,1... | collective-permute-start | bytes 1179656 | tf_op jit(solution)/shard_map/ppermute | solution.py:98
  61.7 2.4 %collective-permute-start.12 = (bf16[384,768]{1,0:T(8,128)(2,1)S(1)}, bf16[384,768]{1,0:T(8,128)(2,1)S(1)}, u32[]{:S(2)}, u32[]{:S(2)}) collective-permute-start(bf16[384,768]{1,0:T(8,128)(2,1)S(1)} %collective-permute-done.6), channel_id=1, source_target_pairs={{0,8},{8,0},{16,24},{24,16},{1,9},{9,1},{17,25},{25,17},{2,10},{10... | collective-permute-start | bytes 1769480 | tf_op jit(solution)/shard_map/ppermute | solution.py:98
  61.7 2.8 %collective-permute-start.11 = (bf16[384,768]{1,0:T(8,128)(2,1)S(1)}, bf16[384,768]{1,0:T(8,128)(2,1)S(1)}, u32[]{:S(2)}, u32[]{:S(2)}) collective-permute-start(bf16[384,768]{1,0:T(8,128)(2,1)S(1)} %copy-done.5), channel_id=1, source_target_pairs={{0,8},{8,0},{16,24},{24,16},{1,9},{9,1},{17,25},{25,17},{2,10},{10... | collective-permute-start | bytes 1769480 | tf_op jit(solution)/shard_map/ppermute | solution.py:98
  62.4 17.2 %collective-permute-start.19 = (bf16[1,192,512]{2,1,0:T(8,128)(2,1)S(1)}, bf16[1,192,512]{2,1,0:T(8,128)(2,1)S(1)}, u32[]{:S(2)}, u32[]{:S(2)}) collective-permute-start(bf16[1,192,512]{2,1,0:T(8,128)(2,1)S(1)} %collective-permute-done.10), channel_id=1, source_target_pairs={{0,4},{4,0},{1,5},{5,1},{2,6},{6,2},{3,7},{7,3},{8,12},{12,8},{9,1... | collective-permute-start | bytes 589832 | tf_op jit(solution)/shard_map/ppermute | solution.py:98
  64.6 9.6 %collective-permute-start.13 = (bf16[1,192,512]{2,1,0:T(8,128)(2,1)S(1)}, bf16[1,192,512]{2,1,0:T(8,128)(2,1)S(1)}, u32[]{:S(2)}, u32[]{:S(2)}) collective-permute-start(bf16[1,192,512]{2,1,0:T(8,128)(2,1)S(1)} %copy-done.9), channel_id=1, source_target_pairs={{0,1},{1,2},{2,3},{3,0},{4,5},{5,6},{6,7},{7,4},{8,9},{9,10},{10,1... | collective-permute-start | bytes 589832 | tf_op jit(solution)/shard_map/ppermute | solution.py:101
  64.8 10.9 %collective-permute-start.14 = (bf16[1,192,512]{2,1,0:T(8,128)(2,1)S(1)}, bf16[1,192,512]{2,1,0:T(8,128)(2,1)S(1)}, u32[]{:S(2)}, u32[]{:S(2)}) collective-permute-start(bf16[1,192,512]{2,1,0:T(8,128)(2,1)S(1)} %copy-done.9), channel_id=1, source_target_pairs={{0,3},{1,0},{2,1},{3,2},{4,7},{5,4},{6,5},{7,6},{8,11},{9,8},{10,9... | collective-permute-start | bytes 589832 | tf_op jit(solution)/shard_map/ppermute | solution.py:101
  79.5 10.6 %copy-start.7 = (bf16[1024,512]{1,0:T(8,128)(2,1)}, bf16[1024,512]{1,0:T(8,128)(2,1)S(1)}, u32[]{:S(2)}) copy-start(bf16[1024,512]{1,0:T(8,128)(2,1)S(1)} %multiply_convert_fusion) | copy-start | bytes 3145732
  79.6 7.4 %collective-permute-start.20 = (bf16[1,192,512]{2,1,0:T(8,128)(2,1)S(1)}, bf16[1,192,512]{2,1,0:T(8,128)(2,1)S(1)}, u32[]{:S(2)}, u32[]{:S(2)}) collective-permute-start(bf16[1,192,512]{2,1,0:T(8,128)(2,1)S(1)} %collective-permute-done.13), channel_id=1, source_target_pairs={{0,4},{4,0},{1,5},{5,1},{2,6},{6,2},{3,7},{7,3},{8,12},{12,8},{9,1... | collective-permute-start | bytes 589832 | tf_op jit(solution)/shard_map/ppermute | solution.py:98
  82.6 7.1 %collective-permute-start.21 = (bf16[1,192,512]{2,1,0:T(8,128)(2,1)S(1)}, bf16[1,192,512]{2,1,0:T(8,128)(2,1)S(1)}, u32[]{:S(2)}, u32[]{:S(2)}) collective-permute-start(bf16[1,192,512]{2,1,0:T(8,128)(2,1)S(1)} %collective-permute-done.14), channel_id=1, source_target_pairs={{0,4},{4,0},{1,5},{5,1},{2,6},{6,2},{3,7},{7,3},{8,12},{12,8},{9,1... | collective-permute-start | bytes 589832 | tf_op jit(solution)/shard_map/ppermute | solution.py:98
  92.5 2.6 %collective-permute-start.22 = (bf16[2,2,128,768]{3,2,1,0:T(8,128)(2,1)}, bf16[2,2,128,768]{3,2,1,0:T(8,128)(2,1)}, u32[]{:S(2)}, u32[]{:S(2)}) collective-permute-start(bf16[2,2,128,768]{3,2,1,0:T(8,128)(2,1)} %convolution_convert_fusion), channel_id=1, source_target_pairs={{0,8},{8,0},{16,24},{24,16},{1,9},{9,1},{17,25},{25,17},{2,10},{10... | collective-permute-start | bytes 2359304 | tf_op jit(solution)/shard_map/ppermute | solution.py:98
  97.3 3.7 %copy-start.2 = (f32[2,2,128,768]{3,2,1,0:T(8,128)}, f32[2,2,128,768]{3,2,1,0:T(8,128)S(1)}, u32[]{:S(2)}) copy-start(f32[2,2,128,768]{3,2,1,0:T(8,128)S(1)} %convert_add_fusion) | copy-start | bytes 4718596
  98.3 11.5 %collective-permute-start.23 = (bf16[128,768]{1,0:T(8,128)(2,1)}, bf16[128,768]{1,0:T(8,128)(2,1)S(1)}, u32[]{:S(2)}, u32[]{:S(2)}) collective-permute-start(bf16[128,768]{1,0:T(8,128)(2,1)} %get-tuple-element.45), channel_id=1, source_target_pairs={{0,16},{8,24},{16,0},{24,8},{1,17},{9,25},{17,1},{25,9},{2,18},{10... | collective-permute-start | bytes 589832 | tf_op jit(solution)/shard_map/ppermute | solution.py:98
  100.1 9.6 %collective-permute-start.25 = (bf16[128,768]{1,0:T(8,128)(2,1)}, bf16[128,768]{1,0:T(8,128)(2,1)S(1)}, u32[]{:S(2)}, u32[]{:S(2)}) collective-permute-start(bf16[128,768]{1,0:T(8,128)(2,1)} %get-tuple-element.46), channel_id=1, source_target_pairs={{0,17},{1,16},{2,19},{3,18},{8,25},{9,24},{10,27},{11,26},{16,1},{... | collective-permute-start | bytes 589832 | tf_op jit(solution)/shard_map/ppermute | solution.py:98
  101.1 10.0 %collective-permute-start.24 = (bf16[128,768]{1,0:T(8,128)(2,1)S(1)}, bf16[128,768]{1,0:T(8,128)(2,1)}, u32[]{:S(2)}, u32[]{:S(2)}) collective-permute-start(bf16[128,768]{1,0:T(8,128)(2,1)S(1)} %fusion.26), channel_id=1, source_target_pairs={{0,1},{1,0},{2,3},{3,2},{4,5},{5,4},{6,7},{7,6},{8,9},{9,8},{10,11... | collective-permute-start | bytes 589832 | tf_op jit(solution)/shard_map/ppermute | solution.py:98
  103.4 9.8 %copy-start.11 = (f32[768]{0:T(1024)S(1)}, f32[768]{0:T(1024)}, u32[]{:S(2)}) copy-start(f32[768]{0:T(1024)} %param.18) | copy-start | bytes 9220
  103.4 23.2 %copy-start = (bf16[3,768,192]{1,2,0:T(8,128)(2,1)S(1)}, bf16[3,768,192]{1,2,0:T(8,128)(2,1)}, u32[]{:S(2)}) copy-start(bf16[3,768,192]{1,2,0:T(8,128)(2,1)} %param.19) | copy-start | bytes 2654212
  113.3 7.8 %collective-permute-start.26 = (bf16[128,768]{1,0:T(8,128)(2,1)S(1)}, bf16[128,768]{1,0:T(8,128)(2,1)S(1)}, u32[]{:S(2)}, u32[]{:S(2)}) collective-permute-start(bf16[128,768]{1,0:T(8,128)(2,1)S(1)} %multiply_convert_fusion.1.refs_0_), channel_id=1, source_target_pairs={{0,16},{8,24},{16,0},{24,8},{1,17},{9,25},{17,1},{25,9},{2,18},{10... | collective-permute-start | bytes 589832 | tf_op jit(solution)/shard_map/ppermute | solution.py:98
  115.0 9.8 %collective-permute-start.29 = (bf16[128,768]{1,0:T(8,128)(2,1)S(1)}, bf16[128,768]{1,0:T(8,128)(2,1)S(1)}, u32[]{:S(2)}, u32[]{:S(2)}) collective-permute-start(bf16[128,768]{1,0:T(8,128)(2,1)S(1)} %multiply_convert_fusion.1.refs_0_), channel_id=1, source_target_pairs={{0,4},{4,0},{1,5},{5,1},{2,6},{6,2},{3,7},{7,3},{8,12},{12,8},{9,1... | collective-permute-start | bytes 589832 | tf_op jit(solution)/shard_map/ppermute | solution.py:98
  116.5 8.4 %collective-permute-start.30 = (bf16[128,768]{1,0:T(8,128)(2,1)S(1)}, bf16[128,768]{1,0:T(8,128)(2,1)S(1)}, u32[]{:S(2)}, u32[]{:S(2)}) collective-permute-start(bf16[128,768]{1,0:T(8,128)(2,1)S(1)} %multiply_convert_fusion.1.refs_0_), channel_id=1, source_target_pairs={{0,20},{4,16},{8,28},{12,24},{16,4},{20,0},{24,12},{28,8},{1,21},{... | collective-permute-start | bytes 589832 | tf_op jit(solution)/shard_map/ppermute | solution.py:98
  116.8 8.5 %collective-permute-start.27 = (bf16[128,768]{1,0:T(8,128)(2,1)S(1)}, bf16[128,768]{1,0:T(8,128)(2,1)S(1)}, u32[]{:S(2)}, u32[]{:S(2)}) collective-permute-start(bf16[128,768]{1,0:T(8,128)(2,1)S(1)} %multiply_convert_fusion.1.refs_0_), channel_id=1, source_target_pairs={{0,8},{8,0},{16,24},{24,16},{1,9},{9,1},{17,25},{25,17},{2,10},{10... | collective-permute-start | bytes 589832 | tf_op jit(solution)/shard_map/ppermute | solution.py:98
  121.1 4.3 %collective-permute-start.28 = (bf16[128,768]{1,0:T(8,128)(2,1)S(1)}, bf16[128,768]{1,0:T(8,128)(2,1)S(1)}, u32[]{:S(2)}, u32[]{:S(2)}) collective-permute-start(bf16[128,768]{1,0:T(8,128)(2,1)S(1)} %collective-permute-done.26.refs_1_), channel_id=1, source_target_pairs={{0,8},{8,0},{16,24},{24,16},{1,9},{9,1},{17,25},{25,17},{2,10},{10... | collective-permute-start | bytes 589832 | tf_op jit(solution)/shard_map/ppermute | solution.py:98
  124.8 1.4 %collective-permute-start.31 = (bf16[128,768]{1,0:T(8,128)(2,1)S(1)}, bf16[128,768]{1,0:T(8,128)(2,1)S(1)}, u32[]{:S(2)}, u32[]{:S(2)}) collective-permute-start(bf16[128,768]{1,0:T(8,128)(2,1)S(1)} %collective-permute-done.29.refs_4_), channel_id=1, source_target_pairs={{0,8},{8,0},{16,24},{24,16},{1,9},{9,1},{17,25},{25,17},{2,10},{10... | collective-permute-start | bytes 589832 | tf_op jit(solution)/shard_map/ppermute | solution.py:98
  124.9 1.7 %collective-permute-start.32 = (bf16[128,768]{1,0:T(8,128)(2,1)S(1)}, bf16[128,768]{1,0:T(8,128)(2,1)S(1)}, u32[]{:S(2)}, u32[]{:S(2)}) collective-permute-start(bf16[128,768]{1,0:T(8,128)(2,1)S(1)} %collective-permute-done.30.refs_5_), channel_id=1, source_target_pairs={{0,8},{8,0},{16,24},{24,16},{1,9},{9,1},{17,25},{25,17},{2,10},{10... | collective-permute-start | bytes 589832 | tf_op jit(solution)/shard_map/ppermute | solution.py:98
  131.9 1.8 %collective-permute-start.33 = (bf16[2,192,512]{2,1,0:T(8,128)(2,1)S(1)}, bf16[2,192,512]{2,1,0:T(8,128)(2,1)S(1)}, u32[]{:S(2)}, u32[]{:S(2)}) collective-permute-start(bf16[2,192,512]{2,1,0:T(8,128)(2,1)S(1)} %get-tuple-element.34), channel_id=1, source_target_pairs={{0,8},{8,0},{16,24},{24,16},{1,9},{9,1},{17,25},{25,17},{2,10},{10... | collective-permute-start | bytes 1179656 | tf_op jit(solution)/shard_map/ppermute | solution.py:98
  133.9 7.1 %collective-permute-start.34 = (bf16[192,512]{1,0:T(8,128)(2,1)S(1)}, bf16[192,512]{1,0:T(8,128)(2,1)S(1)}, u32[]{:S(2)}, u32[]{:S(2)}) collective-permute-start(bf16[192,512]{1,0:T(8,128)(2,1)S(1)} %fusion.28), channel_id=1, source_target_pairs={{0,16},{8,24},{16,0},{24,8},{1,17},{9,25},{17,1},{25,9},{2,18},{10... | collective-permute-start | bytes 589832 | tf_op jit(solution)/shard_map/ppermute | solution.py:98
  (2 other events, 1.6 us)

commit v10 on v9

--- a/solution.py
+++ b/solution.py
@@ -208,16 +208,15 @@
             both = after(jnp.concatenate([mine, beside], axis=0), across)
             both_c, across_c = flip(both, section=1), flip(across, section=1)
             proj_x = flip(after(w_proj, across), section=2)
-            d[0, 2] = rotate(after(down_same, g[0, 1], g[1, 2], both_c, across_c, code), 2)
-            proj_c = flip(after(w_proj, proj_x, d[0, 2]), section=1)
-            proj_xc = flip(after(proj_x, d[0, 2]), section=1)
+            d[0, 2] = rotate(after(down_same, g[0, 1]), 2)
             rows = jnp.concatenate([both, both_c, across, across_c], axis=1)
             normed = layer_norm(rows.astype(jnp.float32), gain).astype(jnp.bfloat16)
-            g[1, 1], g[1, 3] = flip(g[0, 1], seq=1), flip(after(g[0, 3], normed), seq=1)
+            g[1, 1], g[1, 3] = flip(g[0, 1], seq=1), flip(g[0, 3], seq=1)
             gate_up = place_rows(g)
             for k in (1, 3):
-                d[0, k] = rotate(after(down_other, d[0, 2], proj_c, proj_xc, out_w), k)
-            normed = after(normed, d[0, 1], d[0, 3])
+                d[0, k] = rotate(after(down_other, d[0, 2], normed, code, out_w), k)
+            proj_c = flip(after(w_proj, proj_x, d[0, 1]), section=1)
+            proj_xc = flip(after(proj_x, d[0, 1]), section=1)
             proj = jnp.concatenate([w_proj, proj_c, proj_x, proj_xc], axis=0)
             for k in (2, 1, 3):
                 d[1, k] = flip(d[0, k], seq=1)
@@ -229,6 +228,12 @@
             normed = layer_norm(rows.astype(jnp.float32), gain).astype(jnp.bfloat16)
             proj = jnp.concatenate(gather_section(w_proj), axis=0)
 
+        residual = jnp.dot(
+            lax.dynamic_slice_in_dim(rows[:tokens], own_at, own_rows, 0),
+            proj,
+            preferred_element_type=jnp.float32,
+        )
+        normed = after(normed, residual)
         gate = jnp.dot(normed, gate_up[0], preferred_element_type=jnp.float32)
         up = jnp.dot(normed, gate_up[1], preferred_element_type=jnp.float32)
         hidden = (jax.nn.silu(gate) * up).astype(jnp.bfloat16)
@@ -264,11 +269,6 @@
         from_x = flip(there[0], section=2)
         from_z = flip(here[1].astype(jnp.bfloat16), dp=1)
         from_xz = flip(there[1], section=2, dp=1)
-        residual = jnp.dot(
-            lax.dynamic_slice_in_dim(rows[:tokens], sec * own_rows, own_rows, 0),
-            proj,
-            preferred_element_type=jnp.float32,
-        )
         emb = (
             residual
             + here[0]

time: 142 us -> 129 us (0.908)
  waiting for transfers between devices: 67.7 us -> 57.1 us
  matrix products: 11.5 us -> 9 us
  local copies, waits for them, and re-layouts: 10.6 us -> 8.51 us
  starting transfers between devices: 36.5 us -> 38.3 us
    ppermute x29, waiting for transfers between devices: 53.2 us -> 43.8 us  [flip(): return lax.ppermute(x, names if len(names) > 1 else names[0], pairs)]
    ppermute x6, starting transfers between devices: 12.4 us -> 14.3 us  [rotate(): return lax.ppermute(x, 'dp', [(i, (i + k) % n_dp) for i in range(n_dp)])]
    unnamed x37 -> x31, local copies, waits for them, and re-layouts: 3.37 us -> 2.59 us
  transfers between devices with their start and end apart: 35 -> 35, of which waited for: 20 -> 18; matrix products, arithmetic and copies ran while one was open for 14% -> 17% of each run, Pallas kernels for 0% -> 0%
where the time goes in v10:
time: 129 us
  waiting for transfers between devices  57.1 us (44%)
  starting transfers between devices  38.3 us (30%)
  other arithmetic  9.35 us (7%)
  matrix products  9 us (7%)
  local copies, waits for them, and re-layouts  8.51 us (7%)
  Pallas kernels  5.35 us (4%)
    ppermute x29, waiting for transfers between devices, flip(): return lax.ppermute(x, names if len(names) > 1 else names[0], pairs)  43.8 us
    ppermute x29, starting transfers between devices, flip(): return lax.ppermute(x, names if len(names) > 1 else names[0], pairs)  24 us
    ppermute x6, starting transfers between devices, rotate(): return lax.ppermute(x, 'dp', [(i, (i + k) % n_dp) for i in range(n_dp)])  14.3 us
    ppermute x6, waiting for transfers between devices, rotate(): return lax.ppermute(x, 'dp', [(i, (i + k) % n_dp) for i in range(n_dp)])  13.3 us
    pallas_call x1, Pallas kernels, per_device(): pl.pallas_call(lambda *refs: attend_kernel(*refs, heads=local_heads, mask...  5.35 us
    dynamic_update_slice x14, local copies, waits for them, and re-layouts, place_rows(): whole = lax.dynamic_update_slice(whole, block, (0, row_of(y, k, rows), 0))  3.33 us
    unnamed x31, local copies, waits for them, and re-layouts  2.59 us
  transfers between devices with their start and end apart: 35, of which 18 were waited for; matrix products, arithmetic and copies ran while one was open for 17% of the time, Pallas kernels for 0%

profile of v10, /device:TPU:0, one launch (start us, length us, event | category | flops | bytes accessed | tf_op | source)
XLA Modules:
  0.0 128.7 jit_solution(4175927307410265684)
XLA Ops:
  0.0 3.1 %collective-permute-start = (bf16[512,384]{1,0:T(8,128)(2,1)}, bf16[512,384]{1,0:T(8,128)(2,1)}, u32[]{:S(2)}, u32[]{:S(2)}) collective-permute-start(bf16[512,384]{1,0:T(8,128)(2,1)} %bitcast.98), channel_id=1, source_target_pairs={{0,1},{1,0},{2,3},{3,2},{4,5},{5,4},{6,7},{7,6},{8,9},{9,8},{10,11... | collective-permute-start | bytes 1179656 | tf_op jit(solution)/shard_map/ppermute | solution.py:98
  3.1 1.5 %collective-permute-start.1 = (bf16[512,384]{1,0:T(8,128)(2,1)}, bf16[512,384]{1,0:T(8,128)(2,1)}, u32[]{:S(2)}, u32[]{:S(2)}) collective-permute-start(bf16[512,384]{1,0:T(8,128)(2,1)} %bitcast.99), channel_id=1, source_target_pairs={{0,16},{8,24},{16,0},{24,8},{1,17},{9,25},{17,1},{25,9},{2,18},{10... | collective-permute-start | bytes 1179656 | tf_op jit(solution)/shard_map/ppermute | solution.py:98
  4.6 2.0 %fusion.15 = (bf16[2,192,512]{2,1,0:T(8,128)(2,1)}, bf16[2,192,512]{2,1,0:T(8,128)(2,1)S(1)}) fusion(s32[]{:T(128)S(6)} %select_n.238, bf16[1,192,1024]{2,1,0:T(8,128)(2,1)} %bitcast.96, bf16[1,192,1024]{2,1,0:T(8,128)(2,1)} %bitcast.97, s32[]{:T(128)S(6)} %select_n.236), kind=kLoop, calls=%fused_computation.29 | loop fusion | flops 1572864 | bytes 1572872 | tf_op jit(solution)/shard_map/stack | solution.py:163
  6.6 2.6 %collective-permute-start.3 = (bf16[2,192,512]{2,1,0:T(8,128)(2,1)S(1)}, bf16[2,192,512]{2,1,0:T(8,128)(2,1)}, u32[]{:S(2)}, u32[]{:S(2)}) collective-permute-start(bf16[2,192,512]{2,1,0:T(8,128)(2,1)S(1)} %get-tuple-element.44), channel_id=1, source_target_pairs={{0,2},{1,3},{2,0},{3,1},{4,6},{5,7},{6,4},{7,5},{8,10},{9,11},{10,... | collective-permute-start | bytes 1179656 | tf_op jit(solution)/shard_map/ppermute | solution.py:101
  9.2 1.5 %collective-permute-start.13 = (bf16[2,192,512]{2,1,0:T(8,128)(2,1)S(1)}, bf16[2,192,512]{2,1,0:T(8,128)(2,1)}, u32[]{:S(2)}, u32[]{:S(2)}) collective-permute-start(bf16[2,192,512]{2,1,0:T(8,128)(2,1)S(1)} %get-tuple-element.44), channel_id=1, source_target_pairs={{0,4},{4,0},{1,5},{5,1},{2,6},{6,2},{3,7},{7,3},{8,12},{12,8},{9,1... | collective-permute-start | bytes 1179656 | tf_op jit(solution)/shard_map/ppermute | solution.py:98
  10.8 1.8 %dynamic-slice_bitcast_fusion.2 = (bf16[1,192,512]{2,1,0:T(8,128)(2,1)}, bf16[1,192,512]{2,1,0:T(8,128)(2,1)}) fusion(bf16[1024,192]{0,1:T(8,128)(2,1)} %param.16, s32[]{:T(128)S(6)} %select_n.236, s32[]{:T(128)S(6)} %select_n.238), kind=kLoop, calls=%fused_computation.62 | loop fusion | bytes 786440 | tf_op jit(solution)/shard_map/dynamic_slice | solution.py:161
  14.9 1.1 copy.14
  16.1 7.5 %collective-permute-done.7 = bf16[1,192,512]{2,1,0:T(8,128)(2,1)} collective-permute-done((bf16[1,192,512]{2,1,0:T(8,128)(2,1)}, bf16[1,192,512]{2,1,0:T(8,128)(2,1)}, u32[]{:S(2)}, u32[]{:S(2)}) %collective-permute-start.7) | collective-permute-done | bytes 196640 | tf_op jit(solution)/shard_map/ppermute | solution.py:98
  23.6 2.8 %collective-permute-done.3 = bf16[2,192,512]{2,1,0:T(8,128)(2,1)} collective-permute-done((bf16[2,192,512]{2,1,0:T(8,128)(2,1)S(1)}, bf16[2,192,512]{2,1,0:T(8,128)(2,1)}, u32[]{:S(2)}, u32[]{:S(2)}) %collective-permute-start.3) | collective-permute-done | bytes 393248 | tf_op jit(solution)/shard_map/ppermute | solution.py:101
  26.7 3.5 %collective-permute-start.14 = (bf16[2,192,512]{2,1,0:T(8,128)(2,1)}, bf16[2,192,512]{2,1,0:T(8,128)(2,1)S(1)}, u32[]{:S(2)}, u32[]{:S(2)}) collective-permute-start(bf16[2,192,512]{2,1,0:T(8,128)(2,1)} %get-tuple-element.22), channel_id=1, source_target_pairs={{0,3},{1,0},{2,1},{3,2},{4,7},{5,4},{6,5},{7,6},{8,11},{9,8},{10,9... | collective-permute-start | bytes 1179656 | tf_op jit(solution)/shard_map/ppermute | solution.py:101
  30.8 1.2 pad_maximum_fusion
  32.2 1.1 constant_dynamic-update-slice_fusion.17
  33.3 1.6 %collective-permute-start.15 = (bf16[2,192,512]{2,1,0:T(8,128)(2,1)}, bf16[2,192,512]{2,1,0:T(8,128)(2,1)S(1)}, u32[]{:S(2)}, u32[]{:S(2)}) collective-permute-start(bf16[2,192,512]{2,1,0:T(8,128)(2,1)} %collective-permute-done.3), channel_id=1, source_target_pairs={{0,4},{4,0},{1,5},{5,1},{2,6},{6,2},{3,7},{7,3},{8,12},{12,8},{9,1... | collective-permute-start | bytes 1179656 | tf_op jit(solution)/shard_map/ppermute | solution.py:98
  34.9 1.0 constant_dynamic-update-slice_fusion.16
  36.0 3.4 %collective-permute-done.2 = bf16[512,384]{1,0:T(8,128)(2,1)S(1)} collective-permute-done((bf16[512,384]{1,0:T(8,128)(2,1)}, bf16[512,384]{1,0:T(8,128)(2,1)S(1)}, u32[]{:S(2)}, u32[]{:S(2)}) %collective-permute-start.2) | collective-permute-done | bytes 393248 | tf_op jit(solution)/shard_map/ppermute | solution.py:98
  39.3 1.1 pad_maximum_fusion.1
  41.1 4.0 %collective-permute-start.9 = (bf16[1,192,512]{2,1,0:T(8,128)(2,1)}, bf16[1,192,512]{2,1,0:T(8,128)(2,1)S(1)}, u32[]{:S(2)}, u32[]{:S(2)}) collective-permute-start(bf16[1,192,512]{2,1,0:T(8,128)(2,1)} %get-tuple-element.23), channel_id=1, source_target_pairs={{0,2},{1,3},{2,0},{3,1},{4,6},{5,7},{6,4},{7,5},{8,10},{9,11},{10,... | collective-permute-start | bytes 589832 | tf_op jit(solution)/shard_map/ppermute | solution.py:101
  45.3 1.6 %collective-permute-start.16 = (bf16[2,192,512]{2,1,0:T(8,128)(2,1)S(1)}, bf16[2,192,512]{2,1,0:T(8,128)(2,1)S(1)}, u32[]{:S(2)}, u32[]{:S(2)}) collective-permute-start(bf16[2,192,512]{2,1,0:T(8,128)(2,1)S(1)} %collective-permute-done.8), channel_id=1, source_target_pairs={{0,4},{4,0},{1,5},{5,1},{2,6},{6,2},{3,7},{7,3},{8,12},{12,8},{9,1... | collective-permute-start | bytes 1179656 | tf_op jit(solution)/shard_map/ppermute | solution.py:98
  47.0 6.9 %collective-permute-done.9 = bf16[1,192,512]{2,1,0:T(8,128)(2,1)S(1)} collective-permute-done((bf16[1,192,512]{2,1,0:T(8,128)(2,1)}, bf16[1,192,512]{2,1,0:T(8,128)(2,1)S(1)}, u32[]{:S(2)}, u32[]{:S(2)}) %collective-permute-start.9) | collective-permute-done | bytes 196640 | tf_op jit(solution)/shard_map/ppermute | solution.py:101
  53.9 1.5 %collective-permute-start.17 = (bf16[2,192,512]{2,1,0:T(8,128)(2,1)S(1)}, bf16[2,192,512]{2,1,0:T(8,128)(2,1)S(1)}, u32[]{:S(2)}, u32[]{:S(2)}) collective-permute-start(bf16[2,192,512]{2,1,0:T(8,128)(2,1)S(1)} %collective-permute-done.14), channel_id=1, source_target_pairs={{0,4},{4,0},{1,5},{5,1},{2,6},{6,2},{3,7},{7,3},{8,12},{12,8},{9,1... | collective-permute-start | bytes 1179656 | tf_op jit(solution)/shard_map/ppermute | solution.py:98
  55.6 0.9 bitcast_dynamic-update-slice_fusion.4
  58.2 1.0 fusion.2
  59.2 1.0 fusion.4
  60.3 3.8 %collective-permute-start.18 = (bf16[1,192,512]{2,1,0:T(8,128)(2,1)S(1)}, bf16[1,192,512]{2,1,0:T(8,128)(2,1)S(1)}, u32[]{:S(2)}, u32[]{:S(2)}) collective-permute-start(bf16[1,192,512]{2,1,0:T(8,128)(2,1)S(1)} %copy-done.6), channel_id=1, source_target_pairs={{0,3},{1,0},{2,1},{3,2},{4,7},{5,4},{6,5},{7,6},{8,11},{9,8},{10,9... | collective-permute-start | bytes 589832 | tf_op jit(solution)/shard_map/ppermute | solution.py:101
  64.1 1.9 %collective-permute-done.17 = bf16[2,192,512]{2,1,0:T(8,128)(2,1)S(1)} collective-permute-done((bf16[2,192,512]{2,1,0:T(8,128)(2,1)S(1)}, bf16[2,192,512]{2,1,0:T(8,128)(2,1)S(1)}, u32[]{:S(2)}, u32[]{:S(2)}) %collective-permute-start.17) | collective-permute-done | bytes 393248 | tf_op jit(solution)/shard_map/ppermute | solution.py:98
  66.2 3.5 %collective-permute-done.10 = bf16[1,192,512]{2,1,0:T(8,128)(2,1)S(1)} collective-permute-done((bf16[1,192,512]{2,1,0:T(8,128)(2,1)S(1)}, bf16[1,192,512]{2,1,0:T(8,128)(2,1)S(1)}, u32[]{:S(2)}, u32[]{:S(2)}) %collective-permute-start.10) | collective-permute-done | bytes 196640 | tf_op jit(solution)/shard_map/ppermute | solution.py:101
  70.2 1.5 %collective-permute-start.20 = (bf16[1,192,512]{2,1,0:T(8,128)(2,1)S(1)}, bf16[1,192,512]{2,1,0:T(8,128)(2,1)S(1)}, u32[]{:S(2)}, u32[]{:S(2)}) collective-permute-start(bf16[1,192,512]{2,1,0:T(8,128)(2,1)S(1)} %collective-permute-done.10), channel_id=1, source_target_pairs={{0,4},{4,0},{1,5},{5,1},{2,6},{6,2},{3,7},{7,3},{8,12},{12,8},{9,1... | collective-permute-start | bytes 589832 | tf_op jit(solution)/shard_map/ppermute | solution.py:98
  73.0 1.8 %fusion.6 = f32[1024,512]{1,0:T(8,128)S(1)} fusion(bf16[1024,1536]{1,0:T(8,128)(2,1)S(1)} %fusion.4, bf16[2,1536,512]{2,1,0:T(8,128)(2,1)S(1)} %constant_dynamic-update-slice_fusion.11), kind=kOutput, calls=%fused_computation.11 | convolution fusion | flops 1610612736 | bytes 6815744 | tf_op jit(solution)/shard_map/dot_general | solution.py:237
  74.8 2.0 %multiply_convert_fusion = bf16[1024,512]{1,0:T(8,128)(2,1)S(1)} fusion(f32[1024,512]{1,0:T(8,128)S(1)} %fusion.6, bf16[1024,1536]{1,0:T(8,128)(2,1)S(1)} %fusion.4, bf16[2,1536,512]{2,1,0:T(8,128)(2,1)S(1)} %constant_dynamic-update-slice_fusion.11), kind=kOutput, calls=%fused_computation.7 | convolution fusion | flops 1613758464 | bytes 7864320 | tf_op jit(solution)/shard_map/dot_general | solution.py:238
  76.8 1.4 %fusion.54 = f32[768,512]{1,0:T(8,128)S(1)} fusion(bf16[1536,768]{1,0:T(8,128)(2,1)S(1)} %constant_dynamic-update-slice_fusion.5, bf16[1536,512]{1,0:T(8,128)(2,1)S(1)} %bitcast_dynamic-update-slice_fusion), kind=kOutput, calls=%fused_computation.130 | convolution fusion | flops 1207959552 | bytes 5505024 | tf_op jit(solution)/shard_map/dot_general | solution.py:243
  78.7 2.5 %collective-permute-done.21 = bf16[1,192,512]{2,1,0:T(8,128)(2,1)S(1)} collective-permute-done((bf16[1,192,512]{2,1,0:T(8,128)(2,1)S(1)}, bf16[1,192,512]{2,1,0:T(8,128)(2,1)S(1)}, u32[]{:S(2)}, u32[]{:S(2)}) %collective-permute-start.21) | collective-permute-done | bytes 196640 | tf_op jit(solution)/shard_map/ppermute | solution.py:98
  81.7 0.9 copy-done.1
  83.3 2.2 %collective-permute-done.22 = bf16[2,2,128,768]{3,2,1,0:T(8,128)(2,1)S(1)} collective-permute-done((bf16[2,2,128,768]{3,2,1,0:T(8,128)(2,1)S(1)}, bf16[2,2,128,768]{3,2,1,0:T(8,128)(2,1)S(1)}, u32[]{:S(2)}, u32[]{:S(2)}) %collective-permute-start.22) | collective-permute-done | bytes 786464 | tf_op jit(solution)/shard_map/ppermute | solution.py:98
  85.5 1.9 %convert_add_fusion = f32[2,2,128,768]{3,2,1,0:T(8,128)S(1)} fusion(bf16[2,2,128,768]{3,2,1,0:T(8,128)(2,1)S(1)} %collective-permute-done.22, bf16[768,512,1,1]{1,0,3,2:T(8,128)(2,1)} %copy-done.1, bf16[2,2,2,128,512]{4,3,2,1,0:T(8,128)(2,1)} %bitcast.102, s32[]{:T(128)S(6)} %select_n.278), kind=kOutput, calls=%fused_computation.12 | convolution fusion | flops 403439616 | bytes 3670020 | tf_op jit(solution)/shard_map/dot_general | solution.py:260
  87.7 2.2 %collective-permute-start.24 = (bf16[128,768]{1,0:T(8,128)(2,1)S(1)}, bf16[128,768]{1,0:T(8,128)(2,1)S(1)}, u32[]{:S(2)}, u32[]{:S(2)}) collective-permute-start(bf16[128,768]{1,0:T(8,128)(2,1)S(1)} %fusion.28), channel_id=1, source_target_pairs={{0,1},{1,0},{2,3},{3,2},{4,5},{5,4},{6,7},{7,6},{8,9},{9,8},{10,11... | collective-permute-start | bytes 589832 | tf_op jit(solution)/shard_map/ppermute | solution.py:98
  89.9 1.3 collective-permute-start.23
  91.2 5.1 %collective-permute-done.25 = bf16[128,768]{1,0:T(8,128)(2,1)S(1)} collective-permute-done((bf16[128,768]{1,0:T(8,128)(2,1)S(1)}, bf16[128,768]{1,0:T(8,128)(2,1)S(1)}, u32[]{:S(2)}, u32[]{:S(2)}) %collective-permute-start.25) | collective-permute-done | bytes 196640 | tf_op jit(solution)/shard_map/ppermute | solution.py:98
  96.3 2.7 %collective-permute-done.24 = bf16[128,768]{1,0:T(8,128)(2,1)S(1)} collective-permute-done((bf16[128,768]{1,0:T(8,128)(2,1)S(1)}, bf16[128,768]{1,0:T(8,128)(2,1)S(1)}, u32[]{:S(2)}, u32[]{:S(2)}) %collective-permute-start.24) | collective-permute-done | bytes 196640 | tf_op jit(solution)/shard_map/ppermute | solution.py:98
  101.0 1.5 %collective-permute-start.29 = (bf16[128,768]{1,0:T(8,128)(2,1)S(1)}, bf16[128,768]{1,0:T(8,128)(2,1)S(1)}, u32[]{:S(2)}, u32[]{:S(2)}) collective-permute-start(bf16[128,768]{1,0:T(8,128)(2,1)S(1)} %multiply_convert_fusion.1.refs_0_), channel_id=1, source_target_pairs={{0,4},{4,0},{1,5},{5,1},{2,6},{6,2},{3,7},{7,3},{8,12},{12,8},{9,1... | collective-permute-start | bytes 589832 | tf_op jit(solution)/shard_map/ppermute | solution.py:98
  102.5 1.2 collective-permute-start.30
  103.7 4.3 %collective-permute-done.26.refs_1_ = bf16[128,768]{1,0:T(8,128)(2,1)S(1)} collective-permute-done((bf16[128,768]{1,0:T(8,128)(2,1)S(1)}, bf16[128,768]{1,0:T(8,128)(2,1)S(1)}, u32[]{:S(2)}, u32[]{:S(2)}) %collective-permute-start.26) | collective-permute-done | bytes 196640 | tf_op jit(solution)/shard_map/ppermute | solution.py:98
  108.0 2.8 %collective-permute-done.29.refs_4_ = bf16[128,768]{1,0:T(8,128)(2,1)S(1)} collective-permute-done((bf16[128,768]{1,0:T(8,128)(2,1)S(1)}, bf16[128,768]{1,0:T(8,128)(2,1)S(1)}, u32[]{:S(2)}, u32[]{:S(2)}) %collective-permute-start.29) | collective-permute-done | bytes 196640 | tf_op jit(solution)/shard_map/ppermute | solution.py:98
  110.9 1.4 %collective-permute-done.30.refs_5_ = bf16[128,768]{1,0:T(8,128)(2,1)S(1)} collective-permute-done((bf16[128,768]{1,0:T(8,128)(2,1)S(1)}, bf16[128,768]{1,0:T(8,128)(2,1)S(1)}, u32[]{:S(2)}, u32[]{:S(2)}) %collective-permute-start.30) | collective-permute-done | bytes 196640 | tf_op jit(solution)/shard_map/ppermute | solution.py:98
  112.3 1.4 %collective-permute-done.32.refs_7_ = bf16[128,768]{1,0:T(8,128)(2,1)S(1)} collective-permute-done((bf16[128,768]{1,0:T(8,128)(2,1)S(1)}, bf16[128,768]{1,0:T(8,128)(2,1)S(1)}, u32[]{:S(2)}, u32[]{:S(2)}) %collective-permute-start.32) | collective-permute-done | bytes 196640 | tf_op jit(solution)/shard_map/ppermute | solution.py:98
  113.7 5.3 %shard_map.118 = (f32[2,192,512]{2,1,0:T(8,128)S(1)}, bf16[2,192,512]{2,1,0:T(8,128)(2,1)S(1)}) custom-call(bf16[128,768]{1,0:T(8,128)(2,1)S(1)} %multiply_convert_fusion.1.refs_0_, bf16[128,768]{1,0:T(8,128)(2,1)S(1)} %collective-permute-done.26.refs_1_, bf16[128,768]{1,0:T(8,128)(2,1)S(1)} %collective-permute-done.27.refs_2_, ...), custom_call_target="tpu_custom_call" | custom-call | flops 2516582400 | bytes 8388608 | tf_op jit(solution)/shard_map/pallas_call | solution.py:297
  119.3 1.6 %collective-permute-done.33 = bf16[2,192,512]{2,1,0:T(8,128)(2,1)S(1)} collective-permute-done((bf16[2,192,512]{2,1,0:T(8,128)(2,1)S(1)}, bf16[2,192,512]{2,1,0:T(8,128)(2,1)S(1)}, u32[]{:S(2)}, u32[]{:S(2)}) %collective-permute-start.33) | collective-permute-done | bytes 393248 | tf_op jit(solution)/shard_map/ppermute | solution.py:98
  121.0 0.8 collective-permute-start.34
  121.8 6.2 %collective-permute-done.34 = bf16[192,512]{1,0:T(8,128)(2,1)S(1)} collective-permute-done((bf16[192,512]{1,0:T(8,128)(2,1)S(1)}, bf16[192,512]{1,0:T(8,128)(2,1)S(1)}, u32[]{:S(2)}, u32[]{:S(2)}) %collective-permute-start.34) | collective-permute-done | bytes 196640 | tf_op jit(solution)/shard_map/ppermute | solution.py:98
  (126 shorter events, 12.5 us)
Async XLA Ops:
  0.0 13.0 %copy-start.7 = (f32[1536]{0:T(1024)S(1)}, f32[1536]{0:T(1024)}, u32[]{:S(2)}) copy-start(f32[1536]{0:T(1024)} %param.13) | copy-start | bytes 18436
  0.0 13.1 %copy-start.11 = (s32[1,3]{1,0:T(1,128)S(1)}, s32[1,3]{1,0:T(1,128)}, u32[]{:S(2)}) copy-start(s32[1,3]{1,0:T(1,128)} %param.21) | copy-start | bytes 40
  0.0 13.3 %copy-start.9 = (s32[4]{0:T(128)S(1)}, s32[4]{0:T(128)}, u32[]{:S(2)}) copy-start(s32[4]{0:T(128)} %param.22) | copy-start | bytes 52
  0.0 13.3 %copy-start.10 = (s32[4]{0:T(128)S(1)}, s32[4]{0:T(128)}, u32[]{:S(2)}) copy-start(s32[4]{0:T(128)} %param.23) | copy-start | bytes 52
  0.0 14.5 %copy-start.3 = (bf16[384,768]{1,0:T(8,128)(2,1)S(1)}, bf16[384,768]{1,0:T(8,128)(2,1)}, u32[]{:S(2)}) copy-start(bf16[384,768]{1,0:T(8,128)(2,1)} %param.17) | copy-start | bytes 1769476
  0.0 30.2 %collective-permute-start = (bf16[512,384]{1,0:T(8,128)(2,1)}, bf16[512,384]{1,0:T(8,128)(2,1)}, u32[]{:S(2)}, u32[]{:S(2)}) collective-permute-start(bf16[512,384]{1,0:T(8,128)(2,1)} %bitcast.98), channel_id=1, source_target_pairs={{0,1},{1,0},{2,3},{3,2},{4,5},{5,4},{6,7},{7,6},{8,9},{9,8},{10,11... | collective-permute-start | bytes 1179656 | tf_op jit(solution)/shard_map/ppermute | solution.py:98
  3.1 32.8 %collective-permute-start.1 = (bf16[512,384]{1,0:T(8,128)(2,1)}, bf16[512,384]{1,0:T(8,128)(2,1)}, u32[]{:S(2)}, u32[]{:S(2)}) collective-permute-start(bf16[512,384]{1,0:T(8,128)(2,1)} %bitcast.99), channel_id=1, source_target_pairs={{0,16},{8,24},{16,0},{24,8},{1,17},{9,25},{17,1},{25,9},{2,18},{10... | collective-permute-start | bytes 1179656 | tf_op jit(solution)/shard_map/ppermute | solution.py:98
  6.6 19.8 %collective-permute-start.3 = (bf16[2,192,512]{2,1,0:T(8,128)(2,1)S(1)}, bf16[2,192,512]{2,1,0:T(8,128)(2,1)}, u32[]{:S(2)}, u32[]{:S(2)}) collective-permute-start(bf16[2,192,512]{2,1,0:T(8,128)(2,1)S(1)} %get-tuple-element.44), channel_id=1, source_target_pairs={{0,2},{1,3},{2,0},{3,1},{4,6},{5,7},{6,4},{7,5},{8,10},{9,11},{10,... | collective-permute-start | bytes 1179656 | tf_op jit(solution)/shard_map/ppermute | solution.py:101
  9.2 24.1 %collective-permute-start.13 = (bf16[2,192,512]{2,1,0:T(8,128)(2,1)S(1)}, bf16[2,192,512]{2,1,0:T(8,128)(2,1)}, u32[]{:S(2)}, u32[]{:S(2)}) collective-permute-start(bf16[2,192,512]{2,1,0:T(8,128)(2,1)S(1)} %get-tuple-element.44), channel_id=1, source_target_pairs={{0,4},{4,0},{1,5},{5,1},{2,6},{6,2},{3,7},{7,3},{8,12},{12,8},{9,1... | collective-permute-start | bytes 1179656 | tf_op jit(solution)/shard_map/ppermute | solution.py:98
  12.5 11.0 %collective-permute-start.7 = (bf16[1,192,512]{2,1,0:T(8,128)(2,1)}, bf16[1,192,512]{2,1,0:T(8,128)(2,1)}, u32[]{:S(2)}, u32[]{:S(2)}) collective-permute-start(bf16[1,192,512]{2,1,0:T(8,128)(2,1)} %get-tuple-element.23), channel_id=1, source_target_pairs={{0,4},{4,0},{1,5},{5,1},{2,6},{6,2},{3,7},{7,3},{8,12},{12,8},{9,1... | collective-permute-start | bytes 589832 | tf_op jit(solution)/shard_map/ppermute | solution.py:98
  26.4 14.7 %collective-permute-start.8 = (bf16[2,192,512]{2,1,0:T(8,128)(2,1)}, bf16[2,192,512]{2,1,0:T(8,128)(2,1)S(1)}, u32[]{:S(2)}, u32[]{:S(2)}) collective-permute-start(bf16[2,192,512]{2,1,0:T(8,128)(2,1)} %get-tuple-element.22), channel_id=1, source_target_pairs={{0,1},{1,2},{2,3},{3,0},{4,5},{5,6},{6,7},{7,4},{8,9},{9,10},{10,1... | collective-permute-start | bytes 1179656 | tf_op jit(solution)/shard_map/ppermute | solution.py:101
  26.7 18.4 %collective-permute-start.14 = (bf16[2,192,512]{2,1,0:T(8,128)(2,1)}, bf16[2,192,512]{2,1,0:T(8,128)(2,1)S(1)}, u32[]{:S(2)}, u32[]{:S(2)}) collective-permute-start(bf16[2,192,512]{2,1,0:T(8,128)(2,1)} %get-tuple-element.22), channel_id=1, source_target_pairs={{0,3},{1,0},{2,1},{3,2},{4,7},{5,4},{6,5},{7,6},{8,11},{9,8},{10,9... | collective-permute-start | bytes 1179656 | tf_op jit(solution)/shard_map/ppermute | solution.py:101
  30.2 9.1 %collective-permute-start.2 = (bf16[512,384]{1,0:T(8,128)(2,1)}, bf16[512,384]{1,0:T(8,128)(2,1)S(1)}, u32[]{:S(2)}, u32[]{:S(2)}) collective-permute-start(bf16[512,384]{1,0:T(8,128)(2,1)} %collective-permute-done), channel_id=1, source_target_pairs={{0,16},{8,24},{16,0},{24,8},{1,17},{9,25},{17,1},{25,9},{2,18},{10... | collective-permute-start | bytes 1179656 | tf_op jit(solution)/shard_map/ppermute | solution.py:98
  32.2 8.3 %copy-start.4 = (bf16[384,768]{1,0:T(8,128)(2,1)S(1)}, bf16[384,768]{1,0:T(8,128)(2,1)}, u32[]{:S(2)}) copy-start(bf16[384,768]{1,0:T(8,128)(2,1)} %param.17) | copy-start | bytes 1769476
  33.3 11.9 %collective-permute-start.15 = (bf16[2,192,512]{2,1,0:T(8,128)(2,1)}, bf16[2,192,512]{2,1,0:T(8,128)(2,1)S(1)}, u32[]{:S(2)}, u32[]{:S(2)}) collective-permute-start(bf16[2,192,512]{2,1,0:T(8,128)(2,1)} %collective-permute-done.3), channel_id=1, source_target_pairs={{0,4},{4,0},{1,5},{5,1},{2,6},{6,2},{3,7},{7,3},{8,12},{12,8},{9,1... | collective-permute-start | bytes 1179656 | tf_op jit(solution)/shard_map/ppermute | solution.py:98
  40.4 17.1 %collective-permute-start.5 = (bf16[1024,384]{1,0:T(8,128)(2,1)S(1)}, bf16[1024,384]{1,0:T(8,128)(2,1)S(1)}, u32[]{:S(2)}, u32[]{:S(2)}) collective-permute-start(bf16[1024,384]{1,0:T(8,128)(2,1)S(1)} %pad_maximum_fusion.1), channel_id=1, source_target_pairs={{0,8},{8,0},{16,24},{24,16},{1,9},{9,1},{17,25},{25,17},{2,10},{10... | collective-permute-start | bytes 2359304 | tf_op jit(solution)/shard_map/ppermute | solution.py:98
  40.5 25.7 %collective-permute-start.6 = (bf16[384,768]{1,0:T(8,128)(2,1)S(1)}, bf16[384,768]{1,0:T(8,128)(2,1)S(1)}, u32[]{:S(2)}, u32[]{:S(2)}) collective-permute-start(bf16[384,768]{1,0:T(8,128)(2,1)S(1)} %copy-done.4), channel_id=1, source_target_pairs={{0,16},{8,24},{16,0},{24,8},{1,17},{9,25},{17,1},{25,9},{2,18},{10... | collective-permute-start | bytes 1769480 | tf_op jit(solution)/shard_map/ppermute | solution.py:98
  41.1 12.9 %collective-permute-start.9 = (bf16[1,192,512]{2,1,0:T(8,128)(2,1)}, bf16[1,192,512]{2,1,0:T(8,128)(2,1)S(1)}, u32[]{:S(2)}, u32[]{:S(2)}) collective-permute-start(bf16[1,192,512]{2,1,0:T(8,128)(2,1)} %get-tuple-element.23), channel_id=1, source_target_pairs={{0,2},{1,3},{2,0},{3,1},{4,6},{5,7},{6,4},{7,5},{8,10},{9,11},{10,... | collective-permute-start | bytes 589832 | tf_op jit(solution)/shard_map/ppermute | solution.py:101
  45.1 10.5 %copy-start.2 = (bf16[1024,192]{0,1:T(8,128)(2,1)S(1)}, bf16[1024,192]{0,1:T(8,128)(2,1)}, u32[]{:S(2)}) copy-start(bf16[1024,192]{0,1:T(8,128)(2,1)} %param.16) | copy-start | bytes 1179652
  45.1 11.5 %collective-permute-start.4 = (bf16[1024,384]{1,0:T(8,128)(2,1)S(1)}, bf16[1024,384]{1,0:T(8,128)(2,1)S(1)}, u32[]{:S(2)}, u32[]{:S(2)}) collective-permute-start(bf16[1024,384]{1,0:T(8,128)(2,1)S(1)} %pad_maximum_fusion), channel_id=1, source_target_pairs={{0,8},{8,0},{16,24},{24,16},{1,9},{9,1},{17,25},{25,17},{2,10},{10... | collective-permute-start | bytes 2359304 | tf_op jit(solution)/shard_map/ppermute | solution.py:98
  45.3 15.0 %collective-permute-start.16 = (bf16[2,192,512]{2,1,0:T(8,128)(2,1)S(1)}, bf16[2,192,512]{2,1,0:T(8,128)(2,1)S(1)}, u32[]{:S(2)}, u32[]{:S(2)}) collective-permute-start(bf16[2,192,512]{2,1,0:T(8,128)(2,1)S(1)} %collective-permute-done.8), channel_id=1, source_target_pairs={{0,4},{4,0},{1,5},{5,1},{2,6},{6,2},{3,7},{7,3},{8,12},{12,8},{9,1... | collective-permute-start | bytes 1179656 | tf_op jit(solution)/shard_map/ppermute | solution.py:98
  53.9 12.1 %collective-permute-start.17 = (bf16[2,192,512]{2,1,0:T(8,128)(2,1)S(1)}, bf16[2,192,512]{2,1,0:T(8,128)(2,1)S(1)}, u32[]{:S(2)}, u32[]{:S(2)}) collective-permute-start(bf16[2,192,512]{2,1,0:T(8,128)(2,1)S(1)} %collective-permute-done.14), channel_id=1, source_target_pairs={{0,4},{4,0},{1,5},{5,1},{2,6},{6,2},{3,7},{7,3},{8,12},{12,8},{9,1... | collective-permute-start | bytes 1179656 | tf_op jit(solution)/shard_map/ppermute | solution.py:98
  56.6 15.6 %collective-permute-start.19 = (bf16[1,192,512]{2,1,0:T(8,128)(2,1)S(1)}, bf16[1,192,512]{2,1,0:T(8,128)(2,1)S(1)}, u32[]{:S(2)}, u32[]{:S(2)}) collective-permute-start(bf16[1,192,512]{2,1,0:T(8,128)(2,1)S(1)} %collective-permute-done.9), channel_id=1, source_target_pairs={{0,4},{4,0},{1,5},{5,1},{2,6},{6,2},{3,7},{7,3},{8,12},{12,8},{9,1... | collective-permute-start | bytes 589832 | tf_op jit(solution)/shard_map/ppermute | solution.py:98
  59.2 1.0 copy-start.6
  60.2 9.5 %collective-permute-start.10 = (bf16[1,192,512]{2,1,0:T(8,128)(2,1)S(1)}, bf16[1,192,512]{2,1,0:T(8,128)(2,1)S(1)}, u32[]{:S(2)}, u32[]{:S(2)}) collective-permute-start(bf16[1,192,512]{2,1,0:T(8,128)(2,1)S(1)} %copy-done.6), channel_id=1, source_target_pairs={{0,1},{1,2},{2,3},{3,0},{4,5},{5,6},{6,7},{7,4},{8,9},{9,10},{10,1... | collective-permute-start | bytes 589832 | tf_op jit(solution)/shard_map/ppermute | solution.py:101
  60.3 11.4 %collective-permute-start.18 = (bf16[1,192,512]{2,1,0:T(8,128)(2,1)S(1)}, bf16[1,192,512]{2,1,0:T(8,128)(2,1)S(1)}, u32[]{:S(2)}, u32[]{:S(2)}) collective-permute-start(bf16[1,192,512]{2,1,0:T(8,128)(2,1)S(1)} %copy-done.6), channel_id=1, source_target_pairs={{0,3},{1,0},{2,1},{3,2},{4,7},{5,4},{6,5},{7,6},{8,11},{9,8},{10,9... | collective-permute-start | bytes 589832 | tf_op jit(solution)/shard_map/ppermute | solution.py:101
  69.7 2.6 %collective-permute-start.11 = (bf16[384,768]{1,0:T(8,128)(2,1)S(1)}, bf16[384,768]{1,0:T(8,128)(2,1)S(1)}, u32[]{:S(2)}, u32[]{:S(2)}) collective-permute-start(bf16[384,768]{1,0:T(8,128)(2,1)S(1)} %copy-done.4), channel_id=1, source_target_pairs={{0,8},{8,0},{16,24},{24,16},{1,9},{9,1},{17,25},{25,17},{2,10},{10... | collective-permute-start | bytes 1769480 | tf_op jit(solution)/shard_map/ppermute | solution.py:98
  69.7 2.8 %collective-permute-start.12 = (bf16[384,768]{1,0:T(8,128)(2,1)S(1)}, bf16[384,768]{1,0:T(8,128)(2,1)S(1)}, u32[]{:S(2)}, u32[]{:S(2)}) collective-permute-start(bf16[384,768]{1,0:T(8,128)(2,1)S(1)} %collective-permute-done.6), channel_id=1, source_target_pairs={{0,8},{8,0},{16,24},{24,16},{1,9},{9,1},{17,25},{25,17},{2,10},{10... | collective-permute-start | bytes 1769480 | tf_op jit(solution)/shard_map/ppermute | solution.py:98
  70.2 8.1 %collective-permute-start.20 = (bf16[1,192,512]{2,1,0:T(8,128)(2,1)S(1)}, bf16[1,192,512]{2,1,0:T(8,128)(2,1)S(1)}, u32[]{:S(2)}, u32[]{:S(2)}) collective-permute-start(bf16[1,192,512]{2,1,0:T(8,128)(2,1)S(1)} %collective-permute-done.10), channel_id=1, source_target_pairs={{0,4},{4,0},{1,5},{5,1},{2,6},{6,2},{3,7},{7,3},{8,12},{12,8},{9,1... | collective-permute-start | bytes 589832 | tf_op jit(solution)/shard_map/ppermute | solution.py:98
  71.7 9.5 %collective-permute-start.21 = (bf16[1,192,512]{2,1,0:T(8,128)(2,1)S(1)}, bf16[1,192,512]{2,1,0:T(8,128)(2,1)S(1)}, u32[]{:S(2)}, u32[]{:S(2)}) collective-permute-start(bf16[1,192,512]{2,1,0:T(8,128)(2,1)S(1)} %collective-permute-done.18), channel_id=1, source_target_pairs={{0,4},{4,0},{1,5},{5,1},{2,6},{6,2},{3,7},{7,3},{8,12},{12,8},{9,1... | collective-permute-start | bytes 589832 | tf_op jit(solution)/shard_map/ppermute | solution.py:98
  76.8 4.8 %copy-start.5 = (bf16[1024,512]{1,0:T(8,128)(2,1)}, bf16[1024,512]{1,0:T(8,128)(2,1)S(1)}, u32[]{:S(2)}) copy-start(bf16[1024,512]{1,0:T(8,128)(2,1)S(1)} %multiply_convert_fusion) | copy-start | bytes 3145732
  81.6 0.9 copy-start.1
  83.1 2.4 %collective-permute-start.22 = (bf16[2,2,128,768]{3,2,1,0:T(8,128)(2,1)S(1)}, bf16[2,2,128,768]{3,2,1,0:T(8,128)(2,1)S(1)}, u32[]{:S(2)}, u32[]{:S(2)}) collective-permute-start(bf16[2,2,128,768]{3,2,1,0:T(8,128)(2,1)S(1)} %convolution_convert_fusion), channel_id=1, source_target_pairs={{0,8},{8,0},{16,24},{24,16},{1,9},{9,1},{17,25},{25,17},{2,10},{10... | collective-permute-start | bytes 2359304 | tf_op jit(solution)/shard_map/ppermute | solution.py:98
  87.4 12.6 %copy-start.8 = (f32[768]{0:T(1024)S(1)}, f32[768]{0:T(1024)}, u32[]{:S(2)}) copy-start(f32[768]{0:T(1024)} %param.18) | copy-start | bytes 9220
  87.4 26.3 %copy-start = (bf16[3,768,192]{1,2,0:T(8,128)(2,1)S(1)}, bf16[3,768,192]{1,2,0:T(8,128)(2,1)}, u32[]{:S(2)}) copy-start(bf16[3,768,192]{1,2,0:T(8,128)(2,1)} %param.19) | copy-start | bytes 2654212
  87.5 8.8 %collective-permute-start.25 = (bf16[128,768]{1,0:T(8,128)(2,1)S(1)}, bf16[128,768]{1,0:T(8,128)(2,1)S(1)}, u32[]{:S(2)}, u32[]{:S(2)}) collective-permute-start(bf16[128,768]{1,0:T(8,128)(2,1)S(1)} %get-tuple-element.46), channel_id=1, source_target_pairs={{0,17},{1,16},{2,19},{3,18},{8,25},{9,24},{10,27},{11,26},{16,1},{... | collective-permute-start | bytes 589832 | tf_op jit(solution)/shard_map/ppermute | solution.py:98
  87.7 11.3 %collective-permute-start.24 = (bf16[128,768]{1,0:T(8,128)(2,1)S(1)}, bf16[128,768]{1,0:T(8,128)(2,1)S(1)}, u32[]{:S(2)}, u32[]{:S(2)}) collective-permute-start(bf16[128,768]{1,0:T(8,128)(2,1)S(1)} %fusion.28), channel_id=1, source_target_pairs={{0,1},{1,0},{2,3},{3,2},{4,5},{5,4},{6,7},{7,6},{8,9},{9,8},{10,11... | collective-permute-start | bytes 589832 | tf_op jit(solution)/shard_map/ppermute | solution.py:98
  89.9 9.8 %collective-permute-start.23 = (bf16[128,768]{1,0:T(8,128)(2,1)S(1)}, bf16[128,768]{1,0:T(8,128)(2,1)S(1)}, u32[]{:S(2)}, u32[]{:S(2)}) collective-permute-start(bf16[128,768]{1,0:T(8,128)(2,1)S(1)} %get-tuple-element.45), channel_id=1, source_target_pairs={{0,16},{8,24},{16,0},{24,8},{1,17},{9,25},{17,1},{25,9},{2,18},{10... | collective-permute-start | bytes 589832 | tf_op jit(solution)/shard_map/ppermute | solution.py:98
  100.2 7.8 %collective-permute-start.26 = (bf16[128,768]{1,0:T(8,128)(2,1)S(1)}, bf16[128,768]{1,0:T(8,128)(2,1)S(1)}, u32[]{:S(2)}, u32[]{:S(2)}) collective-permute-start(bf16[128,768]{1,0:T(8,128)(2,1)S(1)} %multiply_convert_fusion.1.refs_0_), channel_id=1, source_target_pairs={{0,16},{8,24},{16,0},{24,8},{1,17},{9,25},{17,1},{25,9},{2,18},{10... | collective-permute-start | bytes 589832 | tf_op jit(solution)/shard_map/ppermute | solution.py:98
  101.0 9.8 %collective-permute-start.29 = (bf16[128,768]{1,0:T(8,128)(2,1)S(1)}, bf16[128,768]{1,0:T(8,128)(2,1)S(1)}, u32[]{:S(2)}, u32[]{:S(2)}) collective-permute-start(bf16[128,768]{1,0:T(8,128)(2,1)S(1)} %multiply_convert_fusion.1.refs_0_), channel_id=1, source_target_pairs={{0,4},{4,0},{1,5},{5,1},{2,6},{6,2},{3,7},{7,3},{8,12},{12,8},{9,1... | collective-permute-start | bytes 589832 | tf_op jit(solution)/shard_map/ppermute | solution.py:98
  102.5 9.7 %collective-permute-start.30 = (bf16[128,768]{1,0:T(8,128)(2,1)S(1)}, bf16[128,768]{1,0:T(8,128)(2,1)S(1)}, u32[]{:S(2)}, u32[]{:S(2)}) collective-permute-start(bf16[128,768]{1,0:T(8,128)(2,1)S(1)} %multiply_convert_fusion.1.refs_0_), channel_id=1, source_target_pairs={{0,20},{4,16},{8,28},{12,24},{16,4},{20,0},{24,12},{28,8},{1,21},{... | collective-permute-start | bytes 589832 | tf_op jit(solution)/shard_map/ppermute | solution.py:98
  103.7 8.5 %collective-permute-start.27 = (bf16[128,768]{1,0:T(8,128)(2,1)S(1)}, bf16[128,768]{1,0:T(8,128)(2,1)S(1)}, u32[]{:S(2)}, u32[]{:S(2)}) collective-permute-start(bf16[128,768]{1,0:T(8,128)(2,1)S(1)} %multiply_convert_fusion.1.refs_0_), channel_id=1, source_target_pairs={{0,8},{8,0},{16,24},{24,16},{1,9},{9,1},{17,25},{25,17},{2,10},{10... | collective-permute-start | bytes 589832 | tf_op jit(solution)/shard_map/ppermute | solution.py:98
  108.0 4.3 %collective-permute-start.28 = (bf16[128,768]{1,0:T(8,128)(2,1)S(1)}, bf16[128,768]{1,0:T(8,128)(2,1)S(1)}, u32[]{:S(2)}, u32[]{:S(2)}) collective-permute-start(bf16[128,768]{1,0:T(8,128)(2,1)S(1)} %collective-permute-done.26.refs_1_), channel_id=1, source_target_pairs={{0,8},{8,0},{16,24},{24,16},{1,9},{9,1},{17,25},{25,17},{2,10},{10... | collective-permute-start | bytes 589832 | tf_op jit(solution)/shard_map/ppermute | solution.py:98
  110.8 1.4 %collective-permute-start.31 = (bf16[128,768]{1,0:T(8,128)(2,1)S(1)}, bf16[128,768]{1,0:T(8,128)(2,1)S(1)}, u32[]{:S(2)}, u32[]{:S(2)}) collective-permute-start(bf16[128,768]{1,0:T(8,128)(2,1)S(1)} %collective-permute-done.29.refs_4_), channel_id=1, source_target_pairs={{0,8},{8,0},{16,24},{24,16},{1,9},{9,1},{17,25},{25,17},{2,10},{10... | collective-permute-start | bytes 589832 | tf_op jit(solution)/shard_map/ppermute | solution.py:98
  112.3 1.4 %collective-permute-start.32 = (bf16[128,768]{1,0:T(8,128)(2,1)S(1)}, bf16[128,768]{1,0:T(8,128)(2,1)S(1)}, u32[]{:S(2)}, u32[]{:S(2)}) collective-permute-start(bf16[128,768]{1,0:T(8,128)(2,1)S(1)} %collective-permute-done.30.refs_5_), channel_id=1, source_target_pairs={{0,8},{8,0},{16,24},{24,16},{1,9},{9,1},{17,25},{25,17},{2,10},{10... | collective-permute-start | bytes 589832 | tf_op jit(solution)/shard_map/ppermute | solution.py:98
  119.1 1.8 %collective-permute-start.33 = (bf16[2,192,512]{2,1,0:T(8,128)(2,1)S(1)}, bf16[2,192,512]{2,1,0:T(8,128)(2,1)S(1)}, u32[]{:S(2)}, u32[]{:S(2)}) collective-permute-start(bf16[2,192,512]{2,1,0:T(8,128)(2,1)S(1)} %get-tuple-element.32), channel_id=1, source_target_pairs={{0,8},{8,0},{16,24},{24,16},{1,9},{9,1},{17,25},{25,17},{2,10},{10... | collective-permute-start | bytes 1179656 | tf_op jit(solution)/shard_map/ppermute | solution.py:98
  121.0 7.0 %collective-permute-start.34 = (bf16[192,512]{1,0:T(8,128)(2,1)S(1)}, bf16[192,512]{1,0:T(8,128)(2,1)S(1)}, u32[]{:S(2)}, u32[]{:S(2)}) collective-permute-start(bf16[192,512]{1,0:T(8,128)(2,1)S(1)} %fusion.30), channel_id=1, source_target_pairs={{0,16},{8,24},{16,0},{24,8},{1,17},{9,25},{17,1},{25,9},{2,18},{10... | collective-permute-start | bytes 589832 | tf_op jit(solution)/shard_map/ppermute | solution.py:98

commit v11 on v10

--- a/solution.py
+++ b/solution.py
@@ -200,26 +200,26 @@
             g[0, 2] = rotate(pair_same, 2)
             g[1, 0] = flip(pair_same, seq=1)
             d[1, 0] = flip(down_same, seq=1)
-            beside_x = flip(beside, section=2)
-            for k in (1, 3):
-                g[0, k] = rotate(after(pair_other, g[0, 2], d[1, 0]), k)
+            proj_x = flip(after(w_proj, mine_x), section=2)
+            g[0, 1] = rotate(after(pair_other, g[0, 2], g[1, 0], d[1, 0], mine_x), 1)
+            beside_x = flip(after(beside, g[0, 2]), section=2)
             g[1, 2] = flip(g[0, 2], seq=1)
-            across = after(jnp.concatenate([mine_x, beside_x], axis=0), g[0, 2])
+            g[0, 3] = rotate(after(pair_other, g[0, 1], g[1, 2]), 3)
+            across = jnp.concatenate([after(mine_x, g[0, 1]), beside_x], axis=0)
             both = after(jnp.concatenate([mine, beside], axis=0), across)
             both_c, across_c = flip(both, section=1), flip(across, section=1)
-            proj_x = flip(after(w_proj, across), section=2)
-            d[0, 2] = rotate(after(down_same, g[0, 1]), 2)
             rows = jnp.concatenate([both, both_c, across, across_c], axis=1)
             normed = layer_norm(rows.astype(jnp.float32), gain).astype(jnp.bfloat16)
-            g[1, 1], g[1, 3] = flip(g[0, 1], seq=1), flip(g[0, 3], seq=1)
+            g[1, 1] = flip(g[0, 1], seq=1)
+            g[1, 3] = flip(g[0, 3], seq=1)
             gate_up = place_rows(g)
             for k in (1, 3):
-                d[0, k] = rotate(after(down_other, d[0, 2], normed, code, out_w), k)
-            proj_c = flip(after(w_proj, proj_x, d[0, 1]), section=1)
-            proj_xc = flip(after(proj_x, d[0, 1]), section=1)
+                d[0, k] = rotate(after(down_other, g[0, 3], g[1, 1], both_c, across_c, code, out_w), k)
+            d[0, 2] = rotate(after(down_same, d[0, 1], d[0, 3], g[1, 3], normed), 2)
+            proj_c = flip(after(w_proj, proj_x, both_c), section=1)
+            proj_xc = flip(after(proj_x, across_c), section=1)
             proj = jnp.concatenate([w_proj, proj_c, proj_x, proj_xc], axis=0)
-            for k in (2, 1, 3):
-                d[1, k] = flip(d[0, k], seq=1)
+            d[1, 1], d[1, 3] = flip(d[0, 1], seq=1), flip(d[0, 3], seq=1)
         else:
             gate_up = gather_rows(pair_same, pair_other, seq_at, dp_at)
             down_all = gather_rows(down_same, down_other, seq_at, dp_at)[0]
@@ -245,13 +245,12 @@
             )
 
         if ordered:
-            late = [d.pop((1, 1)), d.pop((1, 3))]
+            late = flip(after(d[0, 2], d[1, 1], d[1, 3], hidden), seq=1)[0]
             folded = fold(proj, after(place_rows(d)[0], hidden))
-            for k, block in zip((1, 3), late):
-                at = row_of(1, k, block.shape[1])
-                folded = folded + fold(
-                    lax.dynamic_slice_in_dim(proj, at, block.shape[1], 0), block[0]
-                )
+            at = row_of(1, 2, late.shape[0])
+            folded = folded + fold(
+                lax.dynamic_slice_in_dim(proj, at, late.shape[0], 0), late
+            )
         else:
             folded = fold(proj, down_all)
         folded = folded.astype(jnp.bfloat16)
@@ -263,7 +262,8 @@
 
         send = project(lax.dynamic_index_in_dim(hidden, 1 - core, 2, False)).astype(jnp.bfloat16)
         got = flip(send, section=1)
-        kept = project(lax.dynamic_index_in_dim(hidden, core, 2, False)) + got.astype(jnp.float32)
+        kept = after(project(lax.dynamic_index_in_dim(hidden, core, 2, False)), send)
+        kept = kept + got.astype(jnp.float32)
         here = lax.dynamic_index_in_dim(kept, side, 1, False)
         there = lax.dynamic_index_in_dim(kept, 1 - side, 1, False).astype(jnp.bfloat16)
         from_x = flip(there[0], section=2)

time: 129 us -> 136 us (1.054)
  waiting for transfers between devices: 57.1 us -> 64.1 us
  starting transfers between devices: 38.3 us -> 35.7 us
  other arithmetic: 9.35 us -> 11.2 us
    ppermute x6, waiting for transfers between devices: 13.3 us -> 22.7 us  [rotate(): return lax.ppermute(x, 'dp', [(i, (i + k) % n_dp) for i in range(n_dp)])]
    ppermute x6, starting transfers between devices: 14.3 us -> 10.5 us  [rotate(): return lax.ppermute(x, 'dp', [(i, (i + k) % n_dp) for i in range(n_dp)])]
    ppermute x29, waiting for transfers between devices: 43.8 us -> 41.4 us  [flip(): return lax.ppermute(x, names if len(names) > 1 else names[0], pairs)]
    reduce_sum x2, other arithmetic: 0.66 us -> 2.52 us  [layer_norm(): mean = jnp.mean(rows, axis=-1, keepdims=True)]
    concatenate x1, local copies, waits for them, and re-layouts: 0.16 us -> 1.79 us  [per_device(): across = jnp.concatenate([after(mine_x, g[0, 1]), beside_x], axis=0)]
    dynamic_update_slice x14 -> x15, local copies, waits for them, and re-layouts: 3.33 us -> 2.41 us  [place_rows(): whole = lax.dynamic_update_slice(whole, block, (0, row_of(y, k, rows), 0))]
where the time goes in v11:
time: 136 us; the launch traced here: 135 us
  waiting for transfers between devices  64.1 us (47%)
  starting transfers between devices  35.7 us (26%)
  other arithmetic  11.2 us (8%)
  matrix products  9.47 us (7%)
  local copies, waits for them, and re-layouts  8.65 us (6%)
  Pallas kernels  5.36 us (4%)
    ppermute x29, waiting for transfers between devices, flip(): return lax.ppermute(x, names if len(names) > 1 else names[0], pairs)  41.4 us
    ppermute x29, starting transfers between devices, flip(): return lax.ppermute(x, names if len(names) > 1 else names[0], pairs)  25.2 us
    ppermute x6, waiting for transfers between devices, rotate(): return lax.ppermute(x, 'dp', [(i, (i + k) % n_dp) for i in range(n_dp)])  22.7 us
    ppermute x6, starting transfers between devices, rotate(): return lax.ppermute(x, 'dp', [(i, (i + k) % n_dp) for i in range(n_dp)])  10.5 us
    pallas_call x1, Pallas kernels, per_device(): pl.pallas_call(lambda *refs: attend_kernel(*refs, heads=local_heads, mask...  5.36 us
    dot_general x2, matrix products, project(): lax.dot_general(x, folded, (((x.ndim - 1,), (1,)), ((), ())), preferred_e...  3.4 us
  transfers between devices with their start and end apart: 35, of which 18 were waited for; matrix products, arithmetic and copies ran while one was open for 17% of the time, Pallas kernels for 0%

profile of v11, /device:TPU:0, one launch (start us, length us, event | category | flops | bytes accessed | tf_op | source)
XLA Modules:
  0.0 135.2 jit_solution(11727259180017062220)
XLA Ops:
  0.0 3.0 %collective-permute-start.1 = (bf16[512,384]{1,0:T(8,128)(2,1)}, bf16[512,384]{1,0:T(8,128)(2,1)S(1)}, u32[]{:S(2)}, u32[]{:S(2)}) collective-permute-start(bf16[512,384]{1,0:T(8,128)(2,1)} %bitcast.95), channel_id=1, source_target_pairs={{0,16},{8,24},{16,0},{24,8},{1,17},{9,25},{17,1},{25,9},{2,18},{10... | collective-permute-start | bytes 1179656 | tf_op jit(solution)/shard_map/ppermute | solution.py:98
  3.0 1.6 %collective-permute-start = (bf16[512,384]{1,0:T(8,128)(2,1)}, bf16[512,384]{1,0:T(8,128)(2,1)}, u32[]{:S(2)}, u32[]{:S(2)}) collective-permute-start(bf16[512,384]{1,0:T(8,128)(2,1)} %bitcast.96), channel_id=1, source_target_pairs={{0,1},{1,0},{2,3},{3,2},{4,5},{5,4},{6,7},{7,6},{8,9},{9,8},{10,11... | collective-permute-start | bytes 1179656 | tf_op jit(solution)/shard_map/ppermute | solution.py:98
  4.6 2.0 %fusion.13 = (bf16[2,192,512]{2,1,0:T(8,128)(2,1)S(1)}, bf16[2,192,512]{2,1,0:T(8,128)(2,1)}) fusion(s32[]{:T(128)S(6)} %select_n.237, bf16[1,192,1024]{2,1,0:T(8,128)(2,1)} %bitcast.93, bf16[1,192,1024]{2,1,0:T(8,128)(2,1)} %bitcast.94, s32[]{:T(128)S(6)} %select_n.236), kind=kLoop, calls=%fused_computation.29 | loop fusion | flops 1572864 | bytes 1572872 | tf_op jit(solution)/shard_map/stack | solution.py:163
  6.6 2.6 %collective-permute-start.2 = (bf16[2,192,512]{2,1,0:T(8,128)(2,1)S(1)}, bf16[2,192,512]{2,1,0:T(8,128)(2,1)S(1)}, u32[]{:S(2)}, u32[]{:S(2)}) collective-permute-start(bf16[2,192,512]{2,1,0:T(8,128)(2,1)S(1)} %get-tuple-element.53), channel_id=1, source_target_pairs={{0,2},{1,3},{2,0},{3,1},{4,6},{5,7},{6,4},{7,5},{8,10},{9,11},{10,... | collective-permute-start | bytes 1179656 | tf_op jit(solution)/shard_map/ppermute | solution.py:101
  9.2 1.5 %collective-permute-start.3 = (bf16[2,192,512]{2,1,0:T(8,128)(2,1)S(1)}, bf16[2,192,512]{2,1,0:T(8,128)(2,1)S(1)}, u32[]{:S(2)}, u32[]{:S(2)}) collective-permute-start(bf16[2,192,512]{2,1,0:T(8,128)(2,1)S(1)} %get-tuple-element.53), channel_id=1, source_target_pairs={{0,4},{4,0},{1,5},{5,1},{2,6},{6,2},{3,7},{7,3},{8,12},{12,8},{9,1... | collective-permute-start | bytes 1179656 | tf_op jit(solution)/shard_map/ppermute | solution.py:98
  10.8 1.7 %dynamic-slice_bitcast_fusion.1 = (bf16[1,192,512]{2,1,0:T(8,128)(2,1)}, bf16[1,192,512]{2,1,0:T(8,128)(2,1)S(1)}) fusion(bf16[1024,192]{0,1:T(8,128)(2,1)} %param.16, s32[]{:T(128)S(6)} %select_n.236, s32[]{:T(128)S(6)} %select_n.237), kind=kLoop, calls=%fused_computation.60 | loop fusion | bytes 786440 | tf_op jit(solution)/shard_map/dynamic_slice | solution.py:161
  14.3 9.1 %collective-permute-done.4 = bf16[1,192,512]{2,1,0:T(8,128)(2,1)S(1)} collective-permute-done((bf16[1,192,512]{2,1,0:T(8,128)(2,1)S(1)}, bf16[1,192,512]{2,1,0:T(8,128)(2,1)S(1)}, u32[]{:S(2)}, u32[]{:S(2)}) %collective-permute-start.4) | collective-permute-done | bytes 196640 | tf_op jit(solution)/shard_map/ppermute | solution.py:98
  23.5 2.8 %collective-permute-done.2 = bf16[2,192,512]{2,1,0:T(8,128)(2,1)S(1)} collective-permute-done((bf16[2,192,512]{2,1,0:T(8,128)(2,1)S(1)}, bf16[2,192,512]{2,1,0:T(8,128)(2,1)S(1)}, u32[]{:S(2)}, u32[]{:S(2)}) %collective-permute-start.2) | collective-permute-done | bytes 393248 | tf_op jit(solution)/shard_map/ppermute | solution.py:101
  27.8 1.6 %collective-permute-start.12 = (bf16[2,192,512]{2,1,0:T(8,128)(2,1)}, bf16[2,192,512]{2,1,0:T(8,128)(2,1)}, u32[]{:S(2)}, u32[]{:S(2)}) collective-permute-start(bf16[2,192,512]{2,1,0:T(8,128)(2,1)} %copy-done.9), channel_id=1, source_target_pairs={{0,4},{4,0},{1,5},{5,1},{2,6},{6,2},{3,7},{7,3},{8,12},{12,8},{9,1... | collective-permute-start | bytes 1179656 | tf_op jit(solution)/shard_map/ppermute | solution.py:98
  29.4 2.1 %pad_maximum_fusion.1 = bf16[1024,384]{1,0:T(8,128)(2,1)} fusion(bf16[512,384]{1,0:T(8,128)(2,1)} %collective-permute-done, bf16[512,384]{1,0:T(8,128)(2,1)} %bitcast.97), kind=kLoop, calls=%fused_computation.21 | loop fusion | flops 1572864 | bytes 1572864 | tf_op jit(solution)/shard_map/concatenate | solution.py:209
  31.4 6.5 %collective-permute-done.5 = bf16[2,192,512]{2,1,0:T(8,128)(2,1)} collective-permute-done((bf16[2,192,512]{2,1,0:T(8,128)(2,1)}, bf16[2,192,512]{2,1,0:T(8,128)(2,1)}, u32[]{:S(2)}, u32[]{:S(2)}) %collective-permute-start.5) | collective-permute-done | bytes 393248 | tf_op jit(solution)/shard_map/ppermute | solution.py:101
  38.7 1.8 %constant_dynamic-update-slice_fusion = bf16[1024,384]{1,0:T(8,128)(2,1)} fusion(bf16[1024,384]{1,0:T(8,128)(2,1)} %constant_dynamic-update-slice_fusion.1, bf16[512,384]{1,0:T(8,128)(2,1)} %collective-permute-done.6), kind=kLoop, calls=%fused_computation.74 | loop fusion | bytes 786432 | tf_op jit(solution)/shard_map/concatenate | solution.py:208
  42.2 1.1 collective-permute-start.13
  43.3 1.6 %collective-permute-start.14 = (bf16[2,192,512]{2,1,0:T(8,128)(2,1)}, bf16[2,192,512]{2,1,0:T(8,128)(2,1)S(1)}, u32[]{:S(2)}, u32[]{:S(2)}) collective-permute-start(bf16[2,192,512]{2,1,0:T(8,128)(2,1)} %collective-permute-done.5), channel_id=1, source_target_pairs={{0,4},{4,0},{1,5},{5,1},{2,6},{6,2},{3,7},{7,3},{8,12},{12,8},{9,1... | collective-permute-start | bytes 1179656 | tf_op jit(solution)/shard_map/ppermute | solution.py:98
  45.0 1.1 constant_dynamic-update-slice_fusion.11
  46.0 1.0 constant_dynamic-update-slice_fusion.10
  47.0 6.4 %collective-permute-done.13 = bf16[2,192,512]{2,1,0:T(8,128)(2,1)S(1)} collective-permute-done((bf16[2,192,512]{2,1,0:T(8,128)(2,1)}, bf16[2,192,512]{2,1,0:T(8,128)(2,1)S(1)}, u32[]{:S(2)}, u32[]{:S(2)}) %collective-permute-start.13) | collective-permute-done | bytes 393248 | tf_op jit(solution)/shard_map/ppermute | solution.py:101
  53.5 1.5 %collective-permute-start.15 = (bf16[2,192,512]{2,1,0:T(8,128)(2,1)S(1)}, bf16[2,192,512]{2,1,0:T(8,128)(2,1)S(1)}, u32[]{:S(2)}, u32[]{:S(2)}) collective-permute-start(bf16[2,192,512]{2,1,0:T(8,128)(2,1)S(1)} %collective-permute-done.13), channel_id=1, source_target_pairs={{0,4},{4,0},{1,5},{5,1},{2,6},{6,2},{3,7},{7,3},{8,12},{12,8},{9,1... | collective-permute-start | bytes 1179656 | tf_op jit(solution)/shard_map/ppermute | solution.py:98
  55.8 3.2 %collective-permute-start.17 = (bf16[1,192,512]{2,1,0:T(8,128)(2,1)S(1)}, bf16[1,192,512]{2,1,0:T(8,128)(2,1)S(1)}, u32[]{:S(2)}, u32[]{:S(2)}) collective-permute-start(bf16[1,192,512]{2,1,0:T(8,128)(2,1)S(1)} %copy-done.17), channel_id=1, source_target_pairs={{0,3},{1,0},{2,1},{3,2},{4,7},{5,4},{6,5},{7,6},{8,11},{9,8},{10,9... | collective-permute-start | bytes 589832 | tf_op jit(solution)/shard_map/ppermute | solution.py:101
  59.0 2.3 %convert_reduce_fusion = (f32[1024]{0:T(1024)S(1)}, bf16[1024,1536]{1,0:T(8,128)(2,1)S(1)}) fusion(bf16[1024,384]{1,0:T(8,128)(2,1)} %collective-permute-done.8, bf16[1024,384]{1,0:T(8,128)(2,1)} %constant_dynamic-update-slice_fusion, bf16[1024,384]{1,0:T(8,128)(2,1)} %collective-permute-done.7, bf16[1024,384]{1,0:T(8,128)(2,1)} %pad_maximum_fusion.1), kind=kLoop, calls=%fused_computation.1 | loop fusion | flops 15727616 | bytes 6295552 | tf_op jit(solution)/shard_map/reduce_sum | solution.py:15
  61.3 1.0 fusion.2
  62.3 1.0 fusion.4
  63.7 1.1 collective-permute-done.16
  65.1 2.3 %collective-permute-start.18 = (bf16[1,192,512]{2,1,0:T(8,128)(2,1)S(1)}, bf16[1,192,512]{2,1,0:T(8,128)(2,1)S(1)}, u32[]{:S(2)}, u32[]{:S(2)}) collective-permute-start(bf16[1,192,512]{2,1,0:T(8,128)(2,1)S(1)} %copy-done.16), channel_id=1, source_target_pairs={{0,2},{1,3},{2,0},{3,1},{4,6},{5,7},{6,4},{7,5},{8,10},{9,11},{10,... | collective-permute-start | bytes 589832 | tf_op jit(solution)/shard_map/ppermute | solution.py:101
  68.3 0.9 collective-permute-start.19
  69.1 1.2 collective-permute-start.20
  70.4 5.5 %collective-permute-done.18 = bf16[1,192,512]{2,1,0:T(8,128)(2,1)S(1)} collective-permute-done((bf16[1,192,512]{2,1,0:T(8,128)(2,1)S(1)}, bf16[1,192,512]{2,1,0:T(8,128)(2,1)S(1)}, u32[]{:S(2)}, u32[]{:S(2)}) %collective-permute-start.18) | collective-permute-done | bytes 196640 | tf_op jit(solution)/shard_map/ppermute | solution.py:101
  76.8 1.8 %fusion.6 = f32[1024,512]{1,0:T(8,128)S(1)} fusion(bf16[1024,1536]{1,0:T(8,128)(2,1)S(1)} %fusion.4, bf16[2,1536,512]{2,1,0:T(8,128)(2,1)S(1)} %constant_dynamic-update-slice_fusion.7), kind=kOutput, calls=%fused_computation.12 | convolution fusion | flops 1610612736 | bytes 6815744 | tf_op jit(solution)/shard_map/dot_general | solution.py:237
  78.6 2.0 %multiply_convert_fusion = bf16[1024,512]{1,0:T(8,128)(2,1)S(1)} fusion(f32[1024,512]{1,0:T(8,128)S(1)} %fusion.6, bf16[1024,1536]{1,0:T(8,128)(2,1)S(1)} %fusion.4, bf16[2,1536,512]{2,1,0:T(8,128)(2,1)S(1)} %constant_dynamic-update-slice_fusion.7), kind=kOutput, calls=%fused_computation.8 | convolution fusion | flops 1613758464 | bytes 7864320 | tf_op jit(solution)/shard_map/dot_general | solution.py:238
  80.6 1.0 collective-permute-start.21
  81.7 4.7 %collective-permute-done.21 = bf16[1,192,512]{2,1,0:T(8,128)(2,1)S(1)} collective-permute-done((bf16[1,192,512]{2,1,0:T(8,128)(2,1)S(1)}, bf16[1,192,512]{2,1,0:T(8,128)(2,1)S(1)}, u32[]{:S(2)}, u32[]{:S(2)}) %collective-permute-start.21) | collective-permute-done | bytes 196640 | tf_op jit(solution)/shard_map/ppermute | solution.py:98
  86.8 1.4 %fusion.7 = bf16[768,512,1,1]{1,0,3,2:T(8,128)(2,1)S(1)} fusion(f32[768,512]{1,0:T(8,128)S(1)} %fusion.23, bf16[1536,768]{1,0:T(8,128)(2,1)S(1)} %constant_dynamic-update-slice_fusion.2, bf16[1536,512]{1,0:T(8,128)(2,1)S(1)} %bitcast_dynamic-update-slice_fusion), kind=kOutput, calls=%fused_computation.16 | convolution fusion | flops 1208745984 | bytes 6291456 | tf_op jit(solution)/shard_map/dot_general | solution.py:243
  88.2 0.9 copy-done.2
  89.1 1.5 %convolution_convert_fusion = bf16[2,2,128,768]{3,2,1,0:T(8,128)(2,1)} fusion(bf16[768,512,1,1]{1,0,3,2:T(8,128)(2,1)S(1)} %fusion.7, bf16[2,2,2,128,512]{4,3,2,1,0:T(8,128)(2,1)S(1)} %bitcast.98, s32[]{:T(128)S(6)} %select_n.279), kind=kOutput, calls=%fused_computation.15 | convolution fusion | flops 403046400 | bytes 2097156 | tf_op jit(solution)/shard_map/dot_general | solution.py:259
  90.6 1.9 %fusion.9 = f32[2,2,128,768]{3,2,1,0:T(8,128)S(1)} fusion(bf16[768,512,1,1]{1,0,3,2:T(8,128)(2,1)} %copy-done.2, bf16[2,2,2,128,512]{4,3,2,1,0:T(8,128)(2,1)} %bitcast.99, s32[]{:T(128)S(6)} %select_n.272), kind=kOutput, calls=%fused_computation.25 | convolution fusion | flops 402653184 | bytes 2883588 | tf_op jit(solution)/shard_map/dot_general | solution.py:259
  93.4 2.0 %collective-permute-start.25 = (bf16[128,768]{1,0:T(8,128)(2,1)S(1)}, bf16[128,768]{1,0:T(8,128)(2,1)S(1)}, u32[]{:S(2)}, u32[]{:S(2)}) collective-permute-start(bf16[128,768]{1,0:T(8,128)(2,1)S(1)} %get-tuple-element.56), channel_id=1, source_target_pairs={{0,17},{1,16},{2,19},{3,18},{8,25},{9,24},{10,27},{11,26},{16,1},{... | collective-permute-start | bytes 589832 | tf_op jit(solution)/shard_map/ppermute | solution.py:98
  95.4 1.1 collective-permute-start.24
  97.0 5.1 %collective-permute-done.25 = bf16[128,768]{1,0:T(8,128)(2,1)S(1)} collective-permute-done((bf16[128,768]{1,0:T(8,128)(2,1)S(1)}, bf16[128,768]{1,0:T(8,128)(2,1)S(1)}, u32[]{:S(2)}, u32[]{:S(2)}) %collective-permute-start.25) | collective-permute-done | bytes 196640 | tf_op jit(solution)/shard_map/ppermute | solution.py:98
  102.1 3.4 %collective-permute-done.24 = bf16[128,768]{1,0:T(8,128)(2,1)S(1)} collective-permute-done((bf16[128,768]{1,0:T(8,128)(2,1)S(1)}, bf16[128,768]{1,0:T(8,128)(2,1)S(1)}, u32[]{:S(2)}, u32[]{:S(2)}) %collective-permute-start.24) | collective-permute-done | bytes 196640 | tf_op jit(solution)/shard_map/ppermute | solution.py:98
  106.1 1.5 %collective-permute-start.26 = (bf16[128,768]{1,0:T(8,128)(2,1)S(1)}, bf16[128,768]{1,0:T(8,128)(2,1)S(1)}, u32[]{:S(2)}, u32[]{:S(2)}) collective-permute-start(bf16[128,768]{1,0:T(8,128)(2,1)S(1)} %multiply_convert_fusion.1.refs_0_), channel_id=1, source_target_pairs={{0,16},{8,24},{16,0},{24,8},{1,17},{9,25},{17,1},{25,9},{2,18},{10... | collective-permute-start | bytes 589832 | tf_op jit(solution)/shard_map/ppermute | solution.py:98
  107.6 1.0 collective-permute-start.29
  108.6 1.1 collective-permute-start.30
  109.7 4.3 %collective-permute-done.26.refs_1_ = bf16[128,768]{1,0:T(8,128)(2,1)S(1)} collective-permute-done((bf16[128,768]{1,0:T(8,128)(2,1)S(1)}, bf16[128,768]{1,0:T(8,128)(2,1)S(1)}, u32[]{:S(2)}, u32[]{:S(2)}) %collective-permute-start.26) | collective-permute-done | bytes 196640 | tf_op jit(solution)/shard_map/ppermute | solution.py:98
  114.0 4.4 %collective-permute-done.29.refs_4_ = bf16[128,768]{1,0:T(8,128)(2,1)S(1)} collective-permute-done((bf16[128,768]{1,0:T(8,128)(2,1)S(1)}, bf16[128,768]{1,0:T(8,128)(2,1)S(1)}, u32[]{:S(2)}, u32[]{:S(2)}) %collective-permute-start.29) | collective-permute-done | bytes 196640 | tf_op jit(solution)/shard_map/ppermute | solution.py:98
  118.9 0.9 collective-permute-done.31.refs_6_
  120.1 5.4 %shard_map.118 = (f32[2,192,512]{2,1,0:T(8,128)S(1)}, bf16[2,192,512]{2,1,0:T(8,128)(2,1)S(1)}) custom-call(bf16[128,768]{1,0:T(8,128)(2,1)S(1)} %multiply_convert_fusion.1.refs_0_, bf16[128,768]{1,0:T(8,128)(2,1)S(1)} %collective-permute-done.26.refs_1_, bf16[128,768]{1,0:T(8,128)(2,1)S(1)} %collective-permute-done.27.refs_2_, ...), custom_call_target="tpu_custom_call" | custom-call | flops 2516582400 | bytes 8388608 | tf_op jit(solution)/shard_map/pallas_call | solution.py:297
  125.8 1.5 %collective-permute-done.33 = bf16[2,192,512]{2,1,0:T(8,128)(2,1)S(1)} collective-permute-done((bf16[2,192,512]{2,1,0:T(8,128)(2,1)S(1)}, bf16[2,192,512]{2,1,0:T(8,128)(2,1)S(1)}, u32[]{:S(2)}, u32[]{:S(2)}) %collective-permute-start.33) | collective-permute-done | bytes 393248 | tf_op jit(solution)/shard_map/ppermute | solution.py:98
  127.9 6.6 %collective-permute-done.34 = bf16[192,512]{1,0:T(8,128)(2,1)S(1)} collective-permute-done((bf16[192,512]{1,0:T(8,128)(2,1)S(1)}, bf16[192,512]{1,0:T(8,128)(2,1)S(1)}, u32[]{:S(2)}, u32[]{:S(2)}) %collective-permute-start.34) | collective-permute-done | bytes 196640 | tf_op jit(solution)/shard_map/ppermute | solution.py:98
  (146 shorter events, 13.3 us)
Async XLA Ops:
  0.0 13.0 %copy-start.22 = (s32[1,3]{1,0:T(1,128)S(1)}, s32[1,3]{1,0:T(1,128)}, u32[]{:S(2)}) copy-start(s32[1,3]{1,0:T(1,128)} %param.21) | copy-start | bytes 40
  0.0 13.2 %copy-start.20 = (s32[4]{0:T(128)S(1)}, s32[4]{0:T(128)}, u32[]{:S(2)}) copy-start(s32[4]{0:T(128)} %param.22) | copy-start | bytes 52
  0.0 13.2 %copy-start.21 = (s32[4]{0:T(128)S(1)}, s32[4]{0:T(128)}, u32[]{:S(2)}) copy-start(s32[4]{0:T(128)} %param.23) | copy-start | bytes 52
  0.0 14.3 %copy-start.18 = (f32[1536]{0:T(1024)S(1)}, f32[1536]{0:T(1024)}, u32[]{:S(2)}) copy-start(f32[1536]{0:T(1024)} %param.13) | copy-start | bytes 18436
  0.0 27.7 %copy-start.3 = (bf16[384,768]{1,0:T(8,128)(2,1)S(1)}, bf16[384,768]{1,0:T(8,128)(2,1)}, u32[]{:S(2)}) copy-start(bf16[384,768]{1,0:T(8,128)(2,1)} %param.17) | copy-start | bytes 1769476
  0.0 23.4 %collective-permute-start.1 = (bf16[512,384]{1,0:T(8,128)(2,1)}, bf16[512,384]{1,0:T(8,128)(2,1)S(1)}, u32[]{:S(2)}, u32[]{:S(2)}) collective-permute-start(bf16[512,384]{1,0:T(8,128)(2,1)} %bitcast.95), channel_id=1, source_target_pairs={{0,16},{8,24},{16,0},{24,8},{1,17},{9,25},{17,1},{25,9},{2,18},{10... | collective-permute-start | bytes 1179656 | tf_op jit(solution)/shard_map/ppermute | solution.py:98
  3.0 23.9 %collective-permute-start = (bf16[512,384]{1,0:T(8,128)(2,1)}, bf16[512,384]{1,0:T(8,128)(2,1)}, u32[]{:S(2)}, u32[]{:S(2)}) collective-permute-start(bf16[512,384]{1,0:T(8,128)(2,1)} %bitcast.96), channel_id=1, source_target_pairs={{0,1},{1,0},{2,3},{3,2},{4,5},{5,4},{6,7},{7,6},{8,9},{9,8},{10,11... | collective-permute-start | bytes 1179656 | tf_op jit(solution)/shard_map/ppermute | solution.py:98
  6.6 19.7 %collective-permute-start.2 = (bf16[2,192,512]{2,1,0:T(8,128)(2,1)S(1)}, bf16[2,192,512]{2,1,0:T(8,128)(2,1)S(1)}, u32[]{:S(2)}, u32[]{:S(2)}) collective-permute-start(bf16[2,192,512]{2,1,0:T(8,128)(2,1)S(1)} %get-tuple-element.53), channel_id=1, source_target_pairs={{0,2},{1,3},{2,0},{3,1},{4,6},{5,7},{6,4},{7,5},{8,10},{9,11},{10,... | collective-permute-start | bytes 1179656 | tf_op jit(solution)/shard_map/ppermute | solution.py:101
  9.2 17.1 %collective-permute-start.3 = (bf16[2,192,512]{2,1,0:T(8,128)(2,1)S(1)}, bf16[2,192,512]{2,1,0:T(8,128)(2,1)S(1)}, u32[]{:S(2)}, u32[]{:S(2)}) collective-permute-start(bf16[2,192,512]{2,1,0:T(8,128)(2,1)S(1)} %get-tuple-element.53), channel_id=1, source_target_pairs={{0,4},{4,0},{1,5},{5,1},{2,6},{6,2},{3,7},{7,3},{8,12},{12,8},{9,1... | collective-permute-start | bytes 1179656 | tf_op jit(solution)/shard_map/ppermute | solution.py:98
  12.5 15.1 %copy-start.15 = (bf16[1,192,512]{2,1,0:T(8,128)(2,1)}, bf16[1,192,512]{2,1,0:T(8,128)(2,1)S(1)}, u32[]{:S(2)}) copy-start(bf16[1,192,512]{2,1,0:T(8,128)(2,1)S(1)} %get-tuple-element.34) | copy-start | bytes 589828
  12.5 11.0 %collective-permute-start.4 = (bf16[1,192,512]{2,1,0:T(8,128)(2,1)S(1)}, bf16[1,192,512]{2,1,0:T(8,128)(2,1)S(1)}, u32[]{:S(2)}, u32[]{:S(2)}) collective-permute-start(bf16[1,192,512]{2,1,0:T(8,128)(2,1)S(1)} %get-tuple-element.34), channel_id=1, source_target_pairs={{0,4},{4,0},{1,5},{5,1},{2,6},{6,2},{3,7},{7,3},{8,12},{12,8},{9,1... | collective-permute-start | bytes 589832 | tf_op jit(solution)/shard_map/ppermute | solution.py:98
  26.3 11.6 %collective-permute-start.5 = (bf16[2,192,512]{2,1,0:T(8,128)(2,1)}, bf16[2,192,512]{2,1,0:T(8,128)(2,1)}, u32[]{:S(2)}, u32[]{:S(2)}) collective-permute-start(bf16[2,192,512]{2,1,0:T(8,128)(2,1)} %get-tuple-element.32), channel_id=1, source_target_pairs={{0,1},{1,2},{2,3},{3,0},{4,5},{5,6},{6,7},{7,4},{8,9},{9,10},{10,1... | collective-permute-start | bytes 1179656 | tf_op jit(solution)/shard_map/ppermute | solution.py:101
  27.0 11.8 %collective-permute-start.6 = (bf16[512,384]{1,0:T(8,128)(2,1)}, bf16[512,384]{1,0:T(8,128)(2,1)}, u32[]{:S(2)}, u32[]{:S(2)}) collective-permute-start(bf16[512,384]{1,0:T(8,128)(2,1)} %collective-permute-done), channel_id=1, source_target_pairs={{0,16},{8,24},{16,0},{24,8},{1,17},{9,25},{17,1},{25,9},{2,18},{10... | collective-permute-start | bytes 1179656 | tf_op jit(solution)/shard_map/ppermute | solution.py:98
  27.7 10.2 %copy-start.6 = (bf16[512,384]{1,0:T(8,128)(2,1)S(1)}, bf16[512,384]{1,0:T(8,128)(2,1)}, u32[]{:S(2)}) copy-start(bf16[512,384]{1,0:T(8,128)(2,1)} %copy-done.5) | copy-start | bytes 1179652
  27.8 13.3 %copy-start.11 = (bf16[192,768]{1,0:T(8,128)(2,1)S(1)}, bf16[192,768]{1,0:T(8,128)(2,1)}, u32[]{:S(2)}) copy-start(bf16[192,768]{1,0:T(8,128)(2,1)} %param.20) | copy-start | bytes 884740
  27.8 14.4 %collective-permute-start.12 = (bf16[2,192,512]{2,1,0:T(8,128)(2,1)}, bf16[2,192,512]{2,1,0:T(8,128)(2,1)}, u32[]{:S(2)}, u32[]{:S(2)}) collective-permute-start(bf16[2,192,512]{2,1,0:T(8,128)(2,1)} %copy-done.9), channel_id=1, source_target_pairs={{0,4},{4,0},{1,5},{5,1},{2,6},{6,2},{3,7},{7,3},{8,12},{12,8},{9,1... | collective-permute-start | bytes 1179656 | tf_op jit(solution)/shard_map/ppermute | solution.py:98
  40.5 14.6 %collective-permute-start.8 = (bf16[1024,384]{1,0:T(8,128)(2,1)}, bf16[1024,384]{1,0:T(8,128)(2,1)}, u32[]{:S(2)}, u32[]{:S(2)}) collective-permute-start(bf16[1024,384]{1,0:T(8,128)(2,1)} %constant_dynamic-update-slice_fusion), channel_id=1, source_target_pairs={{0,8},{8,0},{16,24},{24,16},{1,9},{9,1},{17,25},{25,17},{2,10},{10... | collective-permute-start | bytes 2359304 | tf_op jit(solution)/shard_map/ppermute | solution.py:98
  40.5 14.6 %collective-permute-start.7 = (bf16[1024,384]{1,0:T(8,128)(2,1)}, bf16[1024,384]{1,0:T(8,128)(2,1)}, u32[]{:S(2)}, u32[]{:S(2)}) collective-permute-start(bf16[1024,384]{1,0:T(8,128)(2,1)} %pad_maximum_fusion.1), channel_id=1, source_target_pairs={{0,8},{8,0},{16,24},{24,16},{1,9},{9,1},{17,25},{25,17},{2,10},{10... | collective-permute-start | bytes 2359304 | tf_op jit(solution)/shard_map/ppermute | solution.py:98
  41.3 26.4 %collective-permute-start.9 = (bf16[384,768]{1,0:T(8,128)(2,1)}, bf16[384,768]{1,0:T(8,128)(2,1)S(1)}, u32[]{:S(2)}, u32[]{:S(2)}) collective-permute-start(bf16[384,768]{1,0:T(8,128)(2,1)} %param.17), channel_id=1, source_target_pairs={{0,16},{8,24},{16,0},{24,8},{1,17},{9,25},{17,1},{25,9},{2,18},{10... | collective-permute-start | bytes 1769480 | tf_op jit(solution)/shard_map/ppermute | solution.py:98
  42.1 13.0 %copy-start.17 = (bf16[1,192,512]{2,1,0:T(8,128)(2,1)S(1)}, bf16[1,192,512]{2,1,0:T(8,128)(2,1)}, u32[]{:S(2)}) copy-start(bf16[1,192,512]{2,1,0:T(8,128)(2,1)} %get-tuple-element.33) | copy-start | bytes 589828
  42.2 11.3 %collective-permute-start.13 = (bf16[2,192,512]{2,1,0:T(8,128)(2,1)}, bf16[2,192,512]{2,1,0:T(8,128)(2,1)S(1)}, u32[]{:S(2)}, u32[]{:S(2)}) collective-permute-start(bf16[2,192,512]{2,1,0:T(8,128)(2,1)} %get-tuple-element.32), channel_id=1, source_target_pairs={{0,3},{1,0},{2,1},{3,2},{4,7},{5,4},{6,5},{7,6},{8,11},{9,8},{10,9... | collective-permute-start | bytes 1179656 | tf_op jit(solution)/shard_map/ppermute | solution.py:101
  43.3 11.7 %collective-permute-start.14 = (bf16[2,192,512]{2,1,0:T(8,128)(2,1)}, bf16[2,192,512]{2,1,0:T(8,128)(2,1)S(1)}, u32[]{:S(2)}, u32[]{:S(2)}) collective-permute-start(bf16[2,192,512]{2,1,0:T(8,128)(2,1)} %collective-permute-done.5), channel_id=1, source_target_pairs={{0,4},{4,0},{1,5},{5,1},{2,6},{6,2},{3,7},{7,3},{8,12},{12,8},{9,1... | collective-permute-start | bytes 1179656 | tf_op jit(solution)/shard_map/ppermute | solution.py:98
  53.5 10.2 %collective-permute-start.15 = (bf16[2,192,512]{2,1,0:T(8,128)(2,1)S(1)}, bf16[2,192,512]{2,1,0:T(8,128)(2,1)S(1)}, u32[]{:S(2)}, u32[]{:S(2)}) collective-permute-start(bf16[2,192,512]{2,1,0:T(8,128)(2,1)S(1)} %collective-permute-done.13), channel_id=1, source_target_pairs={{0,4},{4,0},{1,5},{5,1},{2,6},{6,2},{3,7},{7,3},{8,12},{12,8},{9,1... | collective-permute-start | bytes 1179656 | tf_op jit(solution)/shard_map/ppermute | solution.py:98
  55.1 9.7 %collective-permute-start.16 = (bf16[1,192,512]{2,1,0:T(8,128)(2,1)S(1)}, bf16[1,192,512]{2,1,0:T(8,128)(2,1)S(1)}, u32[]{:S(2)}, u32[]{:S(2)}) collective-permute-start(bf16[1,192,512]{2,1,0:T(8,128)(2,1)S(1)} %copy-done.17), channel_id=1, source_target_pairs={{0,1},{1,2},{2,3},{3,0},{4,5},{5,6},{6,7},{7,4},{8,9},{9,10},{10,1... | collective-permute-start | bytes 589832 | tf_op jit(solution)/shard_map/ppermute | solution.py:101
  55.8 9.4 %collective-permute-start.17 = (bf16[1,192,512]{2,1,0:T(8,128)(2,1)S(1)}, bf16[1,192,512]{2,1,0:T(8,128)(2,1)S(1)}, u32[]{:S(2)}, u32[]{:S(2)}) collective-permute-start(bf16[1,192,512]{2,1,0:T(8,128)(2,1)S(1)} %copy-done.17), channel_id=1, source_target_pairs={{0,3},{1,0},{2,1},{3,2},{4,7},{5,4},{6,5},{7,6},{8,11},{9,8},{10,9... | collective-permute-start | bytes 589832 | tf_op jit(solution)/shard_map/ppermute | solution.py:101
  65.1 10.7 %collective-permute-start.18 = (bf16[1,192,512]{2,1,0:T(8,128)(2,1)S(1)}, bf16[1,192,512]{2,1,0:T(8,128)(2,1)S(1)}, u32[]{:S(2)}, u32[]{:S(2)}) collective-permute-start(bf16[1,192,512]{2,1,0:T(8,128)(2,1)S(1)} %copy-done.16), channel_id=1, source_target_pairs={{0,2},{1,3},{2,0},{3,1},{4,6},{5,7},{6,4},{7,5},{8,10},{9,11},{10,... | collective-permute-start | bytes 589832 | tf_op jit(solution)/shard_map/ppermute | solution.py:101
  67.5 8.4 %copy-start.1 = (bf16[1024,192]{0,1:T(8,128)(2,1)S(1)}, bf16[1024,192]{0,1:T(8,128)(2,1)}, u32[]{:S(2)}) copy-start(bf16[1024,192]{0,1:T(8,128)(2,1)} %param.16) | copy-start | bytes 1179652
  67.5 8.5 %copy-start.14 = (bf16[1,192,512]{2,1,0:T(8,128)(2,1)S(1)}, bf16[1,192,512]{2,1,0:T(8,128)(2,1)}, u32[]{:S(2)}) copy-start(bf16[1,192,512]{2,1,0:T(8,128)(2,1)} %copy-done.13) | copy-start | bytes 589828
  67.7 8.5 %collective-permute-start.10 = (bf16[384,768]{1,0:T(8,128)(2,1)S(1)}, bf16[384,768]{1,0:T(8,128)(2,1)S(1)}, u32[]{:S(2)}, u32[]{:S(2)}) collective-permute-start(bf16[384,768]{1,0:T(8,128)(2,1)S(1)} %copy-done.4), channel_id=1, source_target_pairs={{0,8},{8,0},{16,24},{24,16},{1,9},{9,1},{17,25},{25,17},{2,10},{10... | collective-permute-start | bytes 1769480 | tf_op jit(solution)/shard_map/ppermute | solution.py:98
  67.8 8.5 %collective-permute-start.11 = (bf16[384,768]{1,0:T(8,128)(2,1)S(1)}, bf16[384,768]{1,0:T(8,128)(2,1)S(1)}, u32[]{:S(2)}, u32[]{:S(2)}) collective-permute-start(bf16[384,768]{1,0:T(8,128)(2,1)S(1)} %collective-permute-done.9), channel_id=1, source_target_pairs={{0,8},{8,0},{16,24},{24,16},{1,9},{9,1},{17,25},{25,17},{2,10},{10... | collective-permute-start | bytes 1769480 | tf_op jit(solution)/shard_map/ppermute | solution.py:98
  68.3 7.8 %collective-permute-start.19 = (bf16[1,192,512]{2,1,0:T(8,128)(2,1)S(1)}, bf16[1,192,512]{2,1,0:T(8,128)(2,1)S(1)}, u32[]{:S(2)}, u32[]{:S(2)}) collective-permute-start(bf16[1,192,512]{2,1,0:T(8,128)(2,1)S(1)} %collective-permute-done.16), channel_id=1, source_target_pairs={{0,4},{4,0},{1,5},{5,1},{2,6},{6,2},{3,7},{7,3},{8,12},{12,8},{9,1... | collective-permute-start | bytes 589832 | tf_op jit(solution)/shard_map/ppermute | solution.py:98
  69.1 11.5 %collective-permute-start.20 = (bf16[1,192,512]{2,1,0:T(8,128)(2,1)S(1)}, bf16[1,192,512]{2,1,0:T(8,128)(2,1)S(1)}, u32[]{:S(2)}, u32[]{:S(2)}) collective-permute-start(bf16[1,192,512]{2,1,0:T(8,128)(2,1)S(1)} %collective-permute-done.17), channel_id=1, source_target_pairs={{0,4},{4,0},{1,5},{5,1},{2,6},{6,2},{3,7},{7,3},{8,12},{12,8},{9,1... | collective-permute-start | bytes 589832 | tf_op jit(solution)/shard_map/ppermute | solution.py:98
  80.6 5.7 %collective-permute-start.21 = (bf16[1,192,512]{2,1,0:T(8,128)(2,1)S(1)}, bf16[1,192,512]{2,1,0:T(8,128)(2,1)S(1)}, u32[]{:S(2)}, u32[]{:S(2)}) collective-permute-start(bf16[1,192,512]{2,1,0:T(8,128)(2,1)S(1)} %collective-permute-done.18), channel_id=1, source_target_pairs={{0,4},{4,0},{1,5},{5,1},{2,6},{6,2},{3,7},{7,3},{8,12},{12,8},{9,1... | collective-permute-start | bytes 589832 | tf_op jit(solution)/shard_map/ppermute | solution.py:98
  90.6 2.5 %collective-permute-start.22 = (bf16[2,2,128,768]{3,2,1,0:T(8,128)(2,1)}, bf16[2,2,128,768]{3,2,1,0:T(8,128)(2,1)S(1)}, u32[]{:S(2)}, u32[]{:S(2)}) collective-permute-start(bf16[2,2,128,768]{3,2,1,0:T(8,128)(2,1)} %convolution_convert_fusion), channel_id=1, source_target_pairs={{0,8},{8,0},{16,24},{24,16},{1,9},{9,1},{17,25},{25,17},{2,10},{10... | collective-permute-start | bytes 2359304 | tf_op jit(solution)/shard_map/ppermute | solution.py:98
  93.2 12.7 %copy-start.19 = (f32[768]{0:T(1024)S(1)}, f32[768]{0:T(1024)}, u32[]{:S(2)}) copy-start(f32[768]{0:T(1024)} %param.18) | copy-start | bytes 9220
  93.3 26.8 %copy-start = (bf16[3,768,192]{1,2,0:T(8,128)(2,1)S(1)}, bf16[3,768,192]{1,2,0:T(8,128)(2,1)}, u32[]{:S(2)}) copy-start(bf16[3,768,192]{1,2,0:T(8,128)(2,1)} %param.19) | copy-start | bytes 2654212
  93.4 8.7 %collective-permute-start.25 = (bf16[128,768]{1,0:T(8,128)(2,1)S(1)}, bf16[128,768]{1,0:T(8,128)(2,1)S(1)}, u32[]{:S(2)}, u32[]{:S(2)}) collective-permute-start(bf16[128,768]{1,0:T(8,128)(2,1)S(1)} %get-tuple-element.56), channel_id=1, source_target_pairs={{0,17},{1,16},{2,19},{3,18},{8,25},{9,24},{10,27},{11,26},{16,1},{... | collective-permute-start | bytes 589832 | tf_op jit(solution)/shard_map/ppermute | solution.py:98
  95.4 10.2 %collective-permute-start.24 = (bf16[128,768]{1,0:T(8,128)(2,1)S(1)}, bf16[128,768]{1,0:T(8,128)(2,1)S(1)}, u32[]{:S(2)}, u32[]{:S(2)}) collective-permute-start(bf16[128,768]{1,0:T(8,128)(2,1)S(1)} %fusion.25), channel_id=1, source_target_pairs={{0,1},{1,0},{2,3},{3,2},{4,5},{5,4},{6,7},{7,6},{8,9},{9,8},{10,11... | collective-permute-start | bytes 589832 | tf_op jit(solution)/shard_map/ppermute | solution.py:98
  96.5 9.1 %collective-permute-start.23 = (bf16[128,768]{1,0:T(8,128)(2,1)S(1)}, bf16[128,768]{1,0:T(8,128)(2,1)S(1)}, u32[]{:S(2)}, u32[]{:S(2)}) collective-permute-start(bf16[128,768]{1,0:T(8,128)(2,1)S(1)} %get-tuple-element.55), channel_id=1, source_target_pairs={{0,16},{8,24},{16,0},{24,8},{1,17},{9,25},{17,1},{25,9},{2,18},{10... | collective-permute-start | bytes 589832 | tf_op jit(solution)/shard_map/ppermute | solution.py:98
  106.1 7.8 %collective-permute-start.26 = (bf16[128,768]{1,0:T(8,128)(2,1)S(1)}, bf16[128,768]{1,0:T(8,128)(2,1)S(1)}, u32[]{:S(2)}, u32[]{:S(2)}) collective-permute-start(bf16[128,768]{1,0:T(8,128)(2,1)S(1)} %multiply_convert_fusion.1.refs_0_), channel_id=1, source_target_pairs={{0,16},{8,24},{16,0},{24,8},{1,17},{9,25},{17,1},{25,9},{2,18},{10... | collective-permute-start | bytes 589832 | tf_op jit(solution)/shard_map/ppermute | solution.py:98
  107.6 10.8 %collective-permute-start.29 = (bf16[128,768]{1,0:T(8,128)(2,1)S(1)}, bf16[128,768]{1,0:T(8,128)(2,1)S(1)}, u32[]{:S(2)}, u32[]{:S(2)}) collective-permute-start(bf16[128,768]{1,0:T(8,128)(2,1)S(1)} %multiply_convert_fusion.1.refs_0_), channel_id=1, source_target_pairs={{0,4},{4,0},{1,5},{5,1},{2,6},{6,2},{3,7},{7,3},{8,12},{12,8},{9,1... | collective-permute-start | bytes 589832 | tf_op jit(solution)/shard_map/ppermute | solution.py:98
  108.6 9.8 %collective-permute-start.30 = (bf16[128,768]{1,0:T(8,128)(2,1)S(1)}, bf16[128,768]{1,0:T(8,128)(2,1)S(1)}, u32[]{:S(2)}, u32[]{:S(2)}) collective-permute-start(bf16[128,768]{1,0:T(8,128)(2,1)S(1)} %multiply_convert_fusion.1.refs_0_), channel_id=1, source_target_pairs={{0,20},{4,16},{8,28},{12,24},{16,4},{20,0},{24,12},{28,8},{1,21},{... | collective-permute-start | bytes 589832 | tf_op jit(solution)/shard_map/ppermute | solution.py:98
  109.7 9.2 %collective-permute-start.27 = (bf16[128,768]{1,0:T(8,128)(2,1)S(1)}, bf16[128,768]{1,0:T(8,128)(2,1)S(1)}, u32[]{:S(2)}, u32[]{:S(2)}) collective-permute-start(bf16[128,768]{1,0:T(8,128)(2,1)S(1)} %multiply_convert_fusion.1.refs_0_), channel_id=1, source_target_pairs={{0,8},{8,0},{16,24},{24,16},{1,9},{9,1},{17,25},{25,17},{2,10},{10... | collective-permute-start | bytes 589832 | tf_op jit(solution)/shard_map/ppermute | solution.py:98
  114.0 4.9 %collective-permute-start.28 = (bf16[128,768]{1,0:T(8,128)(2,1)S(1)}, bf16[128,768]{1,0:T(8,128)(2,1)S(1)}, u32[]{:S(2)}, u32[]{:S(2)}) collective-permute-start(bf16[128,768]{1,0:T(8,128)(2,1)S(1)} %collective-permute-done.26.refs_1_), channel_id=1, source_target_pairs={{0,8},{8,0},{16,24},{24,16},{1,9},{9,1},{17,25},{25,17},{2,10},{10... | collective-permute-start | bytes 589832 | tf_op jit(solution)/shard_map/ppermute | solution.py:98
  118.4 1.4 %collective-permute-start.31 = (bf16[128,768]{1,0:T(8,128)(2,1)S(1)}, bf16[128,768]{1,0:T(8,128)(2,1)S(1)}, u32[]{:S(2)}, u32[]{:S(2)}) collective-permute-start(bf16[128,768]{1,0:T(8,128)(2,1)S(1)} %collective-permute-done.29.refs_4_), channel_id=1, source_target_pairs={{0,8},{8,0},{16,24},{24,16},{1,9},{9,1},{17,25},{25,17},{2,10},{10... | collective-permute-start | bytes 589832 | tf_op jit(solution)/shard_map/ppermute | solution.py:98
  118.4 1.7 %collective-permute-start.32 = (bf16[128,768]{1,0:T(8,128)(2,1)S(1)}, bf16[128,768]{1,0:T(8,128)(2,1)S(1)}, u32[]{:S(2)}, u32[]{:S(2)}) collective-permute-start(bf16[128,768]{1,0:T(8,128)(2,1)S(1)} %collective-permute-done.30.refs_5_), channel_id=1, source_target_pairs={{0,8},{8,0},{16,24},{24,16},{1,9},{9,1},{17,25},{25,17},{2,10},{10... | collective-permute-start | bytes 589832 | tf_op jit(solution)/shard_map/ppermute | solution.py:98
  125.4 1.8 %collective-permute-start.33 = (bf16[2,192,512]{2,1,0:T(8,128)(2,1)S(1)}, bf16[2,192,512]{2,1,0:T(8,128)(2,1)S(1)}, u32[]{:S(2)}, u32[]{:S(2)}) collective-permute-start(bf16[2,192,512]{2,1,0:T(8,128)(2,1)S(1)} %get-tuple-element.40), channel_id=1, source_target_pairs={{0,8},{8,0},{16,24},{24,16},{1,9},{9,1},{17,25},{25,17},{2,10},{10... | collective-permute-start | bytes 1179656 | tf_op jit(solution)/shard_map/ppermute | solution.py:98
  127.4 7.1 %collective-permute-start.34 = (bf16[192,512]{1,0:T(8,128)(2,1)S(1)}, bf16[192,512]{1,0:T(8,128)(2,1)S(1)}, u32[]{:S(2)}, u32[]{:S(2)}) collective-permute-start(bf16[192,512]{1,0:T(8,128)(2,1)S(1)} %fusion.27), channel_id=1, source_target_pairs={{0,16},{8,24},{16,0},{24,8},{1,17},{9,25},{17,1},{25,9},{2,18},{10... | collective-permute-start | bytes 589832 | tf_op jit(solution)/shard_map/ppermute | solution.py:98
  (10 other events, 32.3 us)

commit v12 on v10

--- a/solution.py
+++ b/solution.py
@@ -199,27 +199,28 @@
             mine_x = flip(mine, section=2)
             g[0, 2] = rotate(pair_same, 2)
             g[1, 0] = flip(pair_same, seq=1)
-            d[1, 0] = flip(down_same, seq=1)
-            beside_x = flip(beside, section=2)
+            d[1, 0] = flip(after(down_same, mine_x), seq=1)
+            proj_x = flip(after(w_proj, mine_x), section=2)
+            beside_x = flip(after(beside, proj_x, g[0, 2]), section=2)
             for k in (1, 3):
-                g[0, k] = rotate(after(pair_other, g[0, 2], d[1, 0]), k)
+                g[0, k] = rotate(after(pair_other, g[0, 2], g[1, 0], d[1, 0]), k)
             g[1, 2] = flip(g[0, 2], seq=1)
             across = after(jnp.concatenate([mine_x, beside_x], axis=0), g[0, 2])
             both = after(jnp.concatenate([mine, beside], axis=0), across)
             both_c, across_c = flip(both, section=1), flip(across, section=1)
-            proj_x = flip(after(w_proj, across), section=2)
             d[0, 2] = rotate(after(down_same, g[0, 1]), 2)
             rows = jnp.concatenate([both, both_c, across, across_c], axis=1)
             normed = layer_norm(rows.astype(jnp.float32), gain).astype(jnp.bfloat16)
-            g[1, 1], g[1, 3] = flip(g[0, 1], seq=1), flip(g[0, 3], seq=1)
+            g[1, 1] = flip(g[0, 1], seq=1)
+            g[1, 3] = flip(after(g[0, 3], both_c, across_c), seq=1)
             gate_up = place_rows(g)
             for k in (1, 3):
-                d[0, k] = rotate(after(down_other, d[0, 2], normed, code, out_w), k)
+                d[0, k] = rotate(after(down_other, d[0, 2], both_c, across_c, code, out_w), k)
             proj_c = flip(after(w_proj, proj_x, d[0, 1]), section=1)
             proj_xc = flip(after(proj_x, d[0, 1]), section=1)
             proj = jnp.concatenate([w_proj, proj_c, proj_x, proj_xc], axis=0)
-            for k in (2, 1, 3):
-                d[1, k] = flip(d[0, k], seq=1)
+            d[1, 2] = flip(d[0, 2], seq=1)
+            d[1, 1], d[1, 3] = flip(after(d[0, 1], normed), seq=1), flip(d[0, 3], seq=1)
         else:
             gate_up = gather_rows(pair_same, pair_other, seq_at, dp_at)
             down_all = gather_rows(down_same, down_other, seq_at, dp_at)[0]
@@ -238,6 +239,9 @@
         up = jnp.dot(normed, gate_up[1], preferred_element_type=jnp.float32)
         hidden = (jax.nn.silu(gate) * up).astype(jnp.bfloat16)
         hidden = hidden.reshape(2, n_sec // 2, 2, own_rows, half)
+        hidden = jnp.stack(
+            [lax.dynamic_index_in_dim(hidden, c, 2, False) for c in (1 - core, core)]
+        )
 
         def fold(proj_rows, down_rows):
             return lax.dot_general(
@@ -261,9 +265,9 @@
                 x, folded, (((x.ndim - 1,), (1,)), ((), ())), preferred_element_type=jnp.float32
             )
 
-        send = project(lax.dynamic_index_in_dim(hidden, 1 - core, 2, False)).astype(jnp.bfloat16)
-        got = flip(send, section=1)
-        kept = project(lax.dynamic_index_in_dim(hidden, core, 2, False)) + got.astype(jnp.float32)
+        sums = project(hidden)
+        got = flip(sums[0].astype(jnp.bfloat16), section=1)
+        kept = sums[1] + got.astype(jnp.float32)
         here = lax.dynamic_index_in_dim(kept, side, 1, False)
         there = lax.dynamic_index_in_dim(kept, 1 - side, 1, False).astype(jnp.bfloat16)
         from_x = flip(there[0], section=2)

time: 129 us -> 135 us (1.047)
  other arithmetic: 9.35 us -> 12.8 us
  starting transfers between devices: 38.3 us -> 41.2 us
  matrix products: 9 us -> 11.7 us
  local copies, waits for them, and re-layouts: 8.51 us -> 6.92 us
  waiting for transfers between devices: 57.1 us -> 55.7 us
    ppermute x29, waiting for transfers between devices: 43.8 us -> 35.6 us  [flip(): return lax.ppermute(x, names if len(names) > 1 else names[0], pairs)]
    ppermute x6, waiting for transfers between devices: 13.3 us -> 20.1 us  [rotate(): return lax.ppermute(x, 'dp', [(i, (i + k) % n_dp) for i in range(n_dp)])]
    ppermute x6, starting transfers between devices: 14.3 us -> 17.7 us  [rotate(): return lax.ppermute(x, 'dp', [(i, (i + k) % n_dp) for i in range(n_dp)])]
    dot_general x2 -> x1, matrix products: 2.5 us -> 4.48 us  [project(): lax.dot_general(x, folded, (((x.ndim - 1,), (1,)), ((), ())), preferred_e...]
    dynamic_update_slice x14, local copies, waits for them, and re-layouts: 3.33 us -> 1.36 us  [place_rows(): whole = lax.dynamic_update_slice(whole, block, (0, row_of(y, k, rows), 0))]
    dynamic_slice x1, local copies, waits for them, and re-layouts: 1.78 us -> 0.04 us  [halves(): return lax.dynamic_slice_in_dim(x, which * half, half, x.ndim - 1)]
    add x0 -> x1, other arithmetic: none -> 1.55 us  [per_device(): kept = sums[1] + got.astype(jnp.float32)]
    convert_element_type x0 -> x1, local copies, waits for them, and re-layouts: none -> 1.49 us  [per_device(): got = flip(sums[0].astype(jnp.bfloat16), section=1)]
  transfers between devices with their start and end apart: 35 -> 35, of which waited for: 18 -> 19; matrix products, arithmetic and copies ran while one was open for 17% -> 15% of each run, Pallas kernels for 0% -> 0%
where the time goes in v12:
time: 135 us
  waiting for transfers between devices  55.7 us (41%)
  starting transfers between devices  41.2 us (31%)
  other arithmetic  12.8 us (9%)
  matrix products  11.7 us (9%)
  local copies, waits for them, and re-layouts  6.92 us (5%)
  Pallas kernels  5.35 us (4%)
    ppermute x29, waiting for transfers between devices, flip(): return lax.ppermute(x, names if len(names) > 1 else names[0], pairs)  35.6 us
    ppermute x29, starting transfers between devices, flip(): return lax.ppermute(x, names if len(names) > 1 else names[0], pairs)  23.5 us
    ppermute x6, waiting for transfers between devices, rotate(): return lax.ppermute(x, 'dp', [(i, (i + k) % n_dp) for i in range(n_dp)])  20.1 us
    ppermute x6, starting transfers between devices, rotate(): return lax.ppermute(x, 'dp', [(i, (i + k) % n_dp) for i in range(n_dp)])  17.7 us
    pallas_call x1, Pallas kernels, per_device(): pl.pallas_call(lambda *refs: attend_kernel(*refs, heads=local_heads, mask...  5.35 us
    dot_general x1, matrix products, project(): lax.dot_general(x, folded, (((x.ndim - 1,), (1,)), ((), ())), preferred_e...  4.48 us
    dot_general x2, matrix products, fold(): lax.dot_general(proj_rows, down_rows, (((0,), (0,)), ((), ())), preferred...  3 us
  transfers between devices with their start and end apart: 35, of which 19 were waited for; matrix products, arithmetic and copies ran while one was open for 15% of the time, Pallas kernels for 0%

profile of v12, /device:TPU:0, one launch (start us, length us, event | category | flops | bytes accessed | tf_op | source)
XLA Modules:
  0.0 134.8 jit_solution(8661019724453549106)
XLA Ops:
  0.0 2.1 %fusion.12 = (bf16[2,192,512]{2,1,0:T(8,128)(2,1)S(1)}, bf16[2,192,512]{2,1,0:T(8,128)(2,1)}) fusion(s32[]{:T(128)S(6)} %select_n.236, bf16[1,192,1024]{2,1,0:T(8,128)(2,1)} %bitcast.100, bf16[1,192,1024]{2,1,0:T(8,128)(2,1)} %bitcast.101, s32[]{:T(128)S(6)} %select_n.238), kind=kLoop, calls=%fused_computation.31 | loop fusion | flops 1572864 | bytes 1572872 | tf_op jit(solution)/shard_map/stack | solution.py:163
  2.1 4.0 %collective-permute-start.3 = (bf16[2,192,512]{2,1,0:T(8,128)(2,1)S(1)}, bf16[2,192,512]{2,1,0:T(8,128)(2,1)S(1)}, u32[]{:S(2)}, u32[]{:S(2)}) collective-permute-start(bf16[2,192,512]{2,1,0:T(8,128)(2,1)S(1)} %get-tuple-element.53), channel_id=1, source_target_pairs={{0,2},{1,3},{2,0},{3,1},{4,6},{5,7},{6,4},{7,5},{8,10},{9,11},{10,... | collective-permute-start | bytes 1179656 | tf_op jit(solution)/shard_map/ppermute | solution.py:101
  6.2 1.5 %collective-permute-start.7 = (bf16[2,192,512]{2,1,0:T(8,128)(2,1)S(1)}, bf16[2,192,512]{2,1,0:T(8,128)(2,1)}, u32[]{:S(2)}, u32[]{:S(2)}) collective-permute-start(bf16[2,192,512]{2,1,0:T(8,128)(2,1)S(1)} %get-tuple-element.53), channel_id=1, source_target_pairs={{0,4},{4,0},{1,5},{5,1},{2,6},{6,2},{3,7},{7,3},{8,12},{12,8},{9,1... | collective-permute-start | bytes 1179656 | tf_op jit(solution)/shard_map/ppermute | solution.py:98
  7.7 1.5 %collective-permute-start.1 = (bf16[512,384]{1,0:T(8,128)(2,1)}, bf16[512,384]{1,0:T(8,128)(2,1)S(1)}, u32[]{:S(2)}, u32[]{:S(2)}) collective-permute-start(bf16[512,384]{1,0:T(8,128)(2,1)} %bitcast.102), channel_id=1, source_target_pairs={{0,16},{8,24},{16,0},{24,8},{1,17},{9,25},{17,1},{25,9},{2,18},{10... | collective-permute-start | bytes 1179656 | tf_op jit(solution)/shard_map/ppermute | solution.py:98
  9.2 1.6 %collective-permute-start = (bf16[512,384]{1,0:T(8,128)(2,1)}, bf16[512,384]{1,0:T(8,128)(2,1)S(1)}, u32[]{:S(2)}, u32[]{:S(2)}) collective-permute-start(bf16[512,384]{1,0:T(8,128)(2,1)} %bitcast.103), channel_id=1, source_target_pairs={{0,1},{1,0},{2,3},{3,2},{4,5},{5,4},{6,7},{7,6},{8,9},{9,8},{10,11... | collective-permute-start | bytes 1179656 | tf_op jit(solution)/shard_map/ppermute | solution.py:98
  10.8 0.8 reduce-window.8
  14.6 1.4 %fusion.31 = (s32[4,1024]{1,0:T(4,128)S(1)}, s32[4,1024]{1,0:T(4,128)S(1)}) fusion(s32[4]{0:T(128)} %param.22, s32[1024]{0:T(1024)S(1)} %get-tuple-element.50, s32[1024]{0:T(1024)S(1)} %get-tuple-element.49, s32[1024]{0:T(1024)S(1)} %get-tuple-element.67, s32[4]{0:T(128)S(1)} %sign.69, s32[4]{0:T(128)S(1)} %get-tuple-element.66, ...), kind=kLoop, calls=%fused_computation.81 | loop fusion | flops 69632 | bytes 45124 | tf_op jit(solution)/shard_map/add | solution.py:185
  16.0 0.8 fusion.50
  17.2 1.1 copy.14
  19.1 1.1 collective-permute-start.2
  20.2 3.6 %collective-permute-done.3 = bf16[2,192,512]{2,1,0:T(8,128)(2,1)S(1)} collective-permute-done((bf16[2,192,512]{2,1,0:T(8,128)(2,1)S(1)}, bf16[2,192,512]{2,1,0:T(8,128)(2,1)S(1)}, u32[]{:S(2)}, u32[]{:S(2)}) %collective-permute-start.3) | collective-permute-done | bytes 393248 | tf_op jit(solution)/shard_map/ppermute | solution.py:101
  23.8 1.6 %collective-permute-start.15 = (bf16[2,192,512]{2,1,0:T(8,128)(2,1)S(1)}, bf16[2,192,512]{2,1,0:T(8,128)(2,1)S(1)}, u32[]{:S(2)}, u32[]{:S(2)}) collective-permute-start(bf16[2,192,512]{2,1,0:T(8,128)(2,1)S(1)} %collective-permute-done.3), channel_id=1, source_target_pairs={{0,4},{4,0},{1,5},{5,1},{2,6},{6,2},{3,7},{7,3},{8,12},{12,8},{9,1... | collective-permute-start | bytes 1179656 | tf_op jit(solution)/shard_map/ppermute | solution.py:98
  26.8 2.6 %collective-permute-start.14 = (bf16[2,192,512]{2,1,0:T(8,128)(2,1)S(1)}, bf16[2,192,512]{2,1,0:T(8,128)(2,1)S(1)}, u32[]{:S(2)}, u32[]{:S(2)}) collective-permute-start(bf16[2,192,512]{2,1,0:T(8,128)(2,1)S(1)} %copy-done.5), channel_id=1, source_target_pairs={{0,3},{1,0},{2,1},{3,2},{4,7},{5,4},{6,5},{7,6},{8,11},{9,8},{10,9... | collective-permute-start | bytes 1179656 | tf_op jit(solution)/shard_map/ppermute | solution.py:101
  29.7 3.1 %collective-permute-done.2 = bf16[384,768]{1,0:T(8,128)(2,1)S(1)} collective-permute-done((bf16[384,768]{1,0:T(8,128)(2,1)S(1)}, bf16[384,768]{1,0:T(8,128)(2,1)S(1)}, u32[]{:S(2)}, u32[]{:S(2)}) %collective-permute-start.2) | collective-permute-done | bytes 589856 | tf_op jit(solution)/shard_map/ppermute | solution.py:98
  32.8 0.9 collective-permute-start.4
  33.7 1.0 constant_dynamic-update-slice_fusion.16
  34.7 4.8 %collective-permute-done.9 = bf16[2,192,512]{2,1,0:T(8,128)(2,1)S(1)} collective-permute-done((bf16[2,192,512]{2,1,0:T(8,128)(2,1)}, bf16[2,192,512]{2,1,0:T(8,128)(2,1)S(1)}, u32[]{:S(2)}, u32[]{:S(2)}) %collective-permute-start.9) | collective-permute-done | bytes 393248 | tf_op jit(solution)/shard_map/ppermute | solution.py:101
  39.5 6.6 %collective-permute-start.10 = (bf16[1,192,512]{2,1,0:T(8,128)(2,1)S(1)}, bf16[1,192,512]{2,1,0:T(8,128)(2,1)S(1)}, u32[]{:S(2)}, u32[]{:S(2)}) collective-permute-start(bf16[1,192,512]{2,1,0:T(8,128)(2,1)S(1)} %get-tuple-element.29), channel_id=1, source_target_pairs={{0,2},{1,3},{2,0},{3,1},{4,6},{5,7},{6,4},{7,5},{8,10},{9,11},{10,... | collective-permute-start | bytes 589832 | tf_op jit(solution)/shard_map/ppermute | solution.py:101
  46.7 8.2 %collective-permute-done.10 = bf16[1,192,512]{2,1,0:T(8,128)(2,1)S(1)} collective-permute-done((bf16[1,192,512]{2,1,0:T(8,128)(2,1)S(1)}, bf16[1,192,512]{2,1,0:T(8,128)(2,1)S(1)}, u32[]{:S(2)}, u32[]{:S(2)}) %collective-permute-start.10) | collective-permute-done | bytes 196640 | tf_op jit(solution)/shard_map/ppermute | solution.py:101
  56.5 1.4 %collective-permute-done.5 = bf16[1024,384]{1,0:T(8,128)(2,1)S(1)} collective-permute-done((bf16[1024,384]{1,0:T(8,128)(2,1)S(1)}, bf16[1024,384]{1,0:T(8,128)(2,1)S(1)}, u32[]{:S(2)}, u32[]{:S(2)}) %collective-permute-start.5) | collective-permute-done | bytes 786464 | tf_op jit(solution)/shard_map/ppermute | solution.py:98
  59.8 3.8 %collective-permute-start.18 = (bf16[1,192,512]{2,1,0:T(8,128)(2,1)S(1)}, bf16[1,192,512]{2,1,0:T(8,128)(2,1)S(1)}, u32[]{:S(2)}, u32[]{:S(2)}) collective-permute-start(bf16[1,192,512]{2,1,0:T(8,128)(2,1)S(1)} %get-tuple-element.30), channel_id=1, source_target_pairs={{0,3},{1,0},{2,1},{3,2},{4,7},{5,4},{6,5},{7,6},{8,11},{9,8},{10,9... | collective-permute-start | bytes 589832 | tf_op jit(solution)/shard_map/ppermute | solution.py:101
  63.6 1.5 %collective-permute-start.17 = (bf16[2,192,512]{2,1,0:T(8,128)(2,1)S(1)}, bf16[2,192,512]{2,1,0:T(8,128)(2,1)S(1)}, u32[]{:S(2)}, u32[]{:S(2)}) collective-permute-start(bf16[2,192,512]{2,1,0:T(8,128)(2,1)S(1)} %collective-permute-done.14), channel_id=1, source_target_pairs={{0,4},{4,0},{1,5},{5,1},{2,6},{6,2},{3,7},{7,3},{8,12},{12,8},{9,1... | collective-permute-start | bytes 1179656 | tf_op jit(solution)/shard_map/ppermute | solution.py:98
  65.1 1.0 fusion.2
  66.1 1.0 fusion.4
  67.1 2.2 %collective-permute-done.11 = bf16[1,192,512]{2,1,0:T(8,128)(2,1)S(1)} collective-permute-done((bf16[1,192,512]{2,1,0:T(8,128)(2,1)S(1)}, bf16[1,192,512]{2,1,0:T(8,128)(2,1)S(1)}, u32[]{:S(2)}, u32[]{:S(2)}) %collective-permute-start.11) | collective-permute-done | bytes 196640 | tf_op jit(solution)/shard_map/ppermute | solution.py:101
  69.9 1.3 collective-permute-done.18
  71.2 1.5 %collective-permute-start.20 = (bf16[1,192,512]{2,1,0:T(8,128)(2,1)S(1)}, bf16[1,192,512]{2,1,0:T(8,128)(2,1)S(1)}, u32[]{:S(2)}, u32[]{:S(2)}) collective-permute-start(bf16[1,192,512]{2,1,0:T(8,128)(2,1)S(1)} %collective-permute-done.11), channel_id=1, source_target_pairs={{0,4},{4,0},{1,5},{5,1},{2,6},{6,2},{3,7},{7,3},{8,12},{12,8},{9,1... | collective-permute-start | bytes 589832 | tf_op jit(solution)/shard_map/ppermute | solution.py:98
  73.3 1.9 %collective-permute-done.17 = bf16[2,192,512]{2,1,0:T(8,128)(2,1)S(1)} collective-permute-done((bf16[2,192,512]{2,1,0:T(8,128)(2,1)S(1)}, bf16[2,192,512]{2,1,0:T(8,128)(2,1)S(1)}, u32[]{:S(2)}, u32[]{:S(2)}) %collective-permute-start.17) | collective-permute-done | bytes 393248 | tf_op jit(solution)/shard_map/ppermute | solution.py:98
  76.0 1.8 %fusion.7 = f32[1024,512]{1,0:T(8,128)S(1)} fusion(bf16[1024,1536]{1,0:T(8,128)(2,1)S(1)} %fusion.4, bf16[2,1536,512]{2,1,0:T(8,128)(2,1)S(1)} %constant_dynamic-update-slice_fusion.11), kind=kOutput, calls=%fused_computation.14 | convolution fusion | flops 1610612736 | bytes 6815744 | tf_op jit(solution)/shard_map/dot_general | solution.py:238
  77.7 2.0 %multiply_convert_fusion = bf16[1024,512]{1,0:T(8,128)(2,1)S(1)} fusion(f32[1024,512]{1,0:T(8,128)S(1)} %fusion.7, bf16[1024,1536]{1,0:T(8,128)(2,1)S(1)} %fusion.4, bf16[2,1536,512]{2,1,0:T(8,128)(2,1)S(1)} %constant_dynamic-update-slice_fusion.11), kind=kOutput, calls=%fused_computation.7 | convolution fusion | flops 1613758464 | bytes 7864320 | tf_op jit(solution)/shard_map/dot_general | solution.py:239
  79.8 2.6 %fusion.51 = f32[768,512]{1,0:T(8,128)} fusion(bf16[1536,768]{1,0:T(8,128)(2,1)S(1)} %constant_dynamic-update-slice_fusion.5, bf16[1536,512]{1,0:T(8,128)(2,1)S(1)} %bitcast_dynamic-update-slice_fusion), kind=kOutput, calls=%fused_computation.129 | convolution fusion | flops 1207959552 | bytes 5505024 | tf_op jit(solution)/shard_map/dot_general | solution.py:247
  83.5 4.5 %fusion.9 = f32[2,2,2,128,768]{4,3,2,1,0:T(8,128)} fusion(f32[768,512]{1,0:T(8,128)} %fusion.51, f32[768,512]{1,0:T(8,128)S(1)} %fusion.23, bf16[1536,768]{1,0:T(8,128)(2,1)} %copy-done.1, s32[]{:T(128)S(6)} %select_n.276, bf16[1,192,512]{2,1,0:T(8,128)(2,1)} %copy-done.6, bf16[1,2,2,128,512]{4,3,2,1,0:T(8,128)(2,1)S(1)} %get-tuple-element.52, ...), kind=kOutput, calls=%fused_computation.18 | convolution fusion | flops 958005248 | bytes 7831556 | tf_op jit(solution)/shard_map/dot_general | solution.py:264
  88.0 1.5 %fusion.10 = bf16[2,2,128,768]{3,2,1,0:T(8,128)(2,1)S(1)} fusion(f32[2,2,2,128,768]{4,3,2,1,0:T(8,128)} %fusion.9), kind=kLoop, calls=%fused_computation.23 | loop fusion | bytes 1572864 | tf_op jit(solution)/shard_map/convert_element_type | solution.py:269
  89.6 2.2 %collective-permute-done.22 = bf16[2,2,128,768]{3,2,1,0:T(8,128)(2,1)S(1)} collective-permute-done((bf16[2,2,128,768]{3,2,1,0:T(8,128)(2,1)S(1)}, bf16[2,2,128,768]{3,2,1,0:T(8,128)(2,1)S(1)}, u32[]{:S(2)}, u32[]{:S(2)}) %collective-permute-start.22) | collective-permute-done | bytes 786464 | tf_op jit(solution)/shard_map/ppermute | solution.py:98
  91.9 1.6 %fusion.5 = f32[2,2,128,768]{3,2,1,0:T(8,128)S(1)} fusion(f32[2,2,2,128,768]{4,3,2,1,0:T(8,128)} %fusion.9, bf16[2,2,128,768]{3,2,1,0:T(8,128)(2,1)S(1)} %collective-permute-done.22), kind=kLoop, calls=%fused_computation.10 | loop fusion | flops 786432 | bytes 3932160 | tf_op jit(solution)/shard_map/add | solution.py:270
  93.5 1.6 %collective-permute-start.23 = (bf16[128,768]{1,0:T(8,128)(2,1)S(1)}, bf16[128,768]{1,0:T(8,128)(2,1)S(1)}, u32[]{:S(2)}, u32[]{:S(2)}) collective-permute-start(bf16[128,768]{1,0:T(8,128)(2,1)S(1)} %get-tuple-element.55), channel_id=1, source_target_pairs={{0,16},{8,24},{16,0},{24,8},{1,17},{9,25},{17,1},{25,9},{2,18},{10... | collective-permute-start | bytes 589832 | tf_op jit(solution)/shard_map/ppermute | solution.py:98
  95.1 2.1 %collective-permute-start.24 = (bf16[128,768]{1,0:T(8,128)(2,1)S(1)}, bf16[128,768]{1,0:T(8,128)(2,1)S(1)}, u32[]{:S(2)}, u32[]{:S(2)}) collective-permute-start(bf16[128,768]{1,0:T(8,128)(2,1)S(1)} %fusion.25), channel_id=1, source_target_pairs={{0,1},{1,0},{2,3},{3,2},{4,5},{5,4},{6,7},{7,6},{8,9},{9,8},{10,11... | collective-permute-start | bytes 589832 | tf_op jit(solution)/shard_map/ppermute | solution.py:98
  97.2 7.6 %collective-permute-done.23 = bf16[128,768]{1,0:T(8,128)(2,1)S(1)} collective-permute-done((bf16[128,768]{1,0:T(8,128)(2,1)S(1)}, bf16[128,768]{1,0:T(8,128)(2,1)S(1)}, u32[]{:S(2)}, u32[]{:S(2)}) %collective-permute-start.23) | collective-permute-done | bytes 196640 | tf_op jit(solution)/shard_map/ppermute | solution.py:98
  104.8 1.2 collective-permute-done.24
  106.5 1.6 %collective-permute-start.26 = (bf16[128,768]{1,0:T(8,128)(2,1)S(1)}, bf16[128,768]{1,0:T(8,128)(2,1)S(1)}, u32[]{:S(2)}, u32[]{:S(2)}) collective-permute-start(bf16[128,768]{1,0:T(8,128)(2,1)S(1)} %multiply_convert_fusion.1.refs_0_), channel_id=1, source_target_pairs={{0,16},{8,24},{16,0},{24,8},{1,17},{9,25},{17,1},{25,9},{2,18},{10... | collective-permute-start | bytes 589832 | tf_op jit(solution)/shard_map/ppermute | solution.py:98
  108.1 1.5 %collective-permute-start.29 = (bf16[128,768]{1,0:T(8,128)(2,1)S(1)}, bf16[128,768]{1,0:T(8,128)(2,1)S(1)}, u32[]{:S(2)}, u32[]{:S(2)}) collective-permute-start(bf16[128,768]{1,0:T(8,128)(2,1)S(1)} %multiply_convert_fusion.1.refs_0_), channel_id=1, source_target_pairs={{0,4},{4,0},{1,5},{5,1},{2,6},{6,2},{3,7},{7,3},{8,12},{12,8},{9,1... | collective-permute-start | bytes 589832 | tf_op jit(solution)/shard_map/ppermute | solution.py:98
  110.1 4.2 %collective-permute-done.26.refs_1_ = bf16[128,768]{1,0:T(8,128)(2,1)S(1)} collective-permute-done((bf16[128,768]{1,0:T(8,128)(2,1)S(1)}, bf16[128,768]{1,0:T(8,128)(2,1)S(1)}, u32[]{:S(2)}, u32[]{:S(2)}) %collective-permute-start.26) | collective-permute-done | bytes 196640 | tf_op jit(solution)/shard_map/ppermute | solution.py:98
  114.3 3.7 %collective-permute-done.29.refs_4_ = bf16[128,768]{1,0:T(8,128)(2,1)S(1)} collective-permute-done((bf16[128,768]{1,0:T(8,128)(2,1)S(1)}, bf16[128,768]{1,0:T(8,128)(2,1)S(1)}, u32[]{:S(2)}, u32[]{:S(2)}) %collective-permute-start.29) | collective-permute-done | bytes 196640 | tf_op jit(solution)/shard_map/ppermute | solution.py:98
  118.4 0.9 collective-permute-done.31.refs_6_
  119.6 5.3 %shard_map.118 = (f32[2,192,512]{2,1,0:T(8,128)S(1)}, bf16[2,192,512]{2,1,0:T(8,128)(2,1)S(1)}) custom-call(bf16[128,768]{1,0:T(8,128)(2,1)S(1)} %multiply_convert_fusion.1.refs_0_, bf16[128,768]{1,0:T(8,128)(2,1)S(1)} %collective-permute-done.26.refs_1_, bf16[128,768]{1,0:T(8,128)(2,1)S(1)} %collective-permute-done.27.refs_2_, ...), custom_call_target="tpu_custom_call" | custom-call | flops 2516582400 | bytes 8388608 | tf_op jit(solution)/shard_map/pallas_call | solution.py:301
  125.3 1.5 %collective-permute-done.33 = bf16[2,192,512]{2,1,0:T(8,128)(2,1)S(1)} collective-permute-done((bf16[2,192,512]{2,1,0:T(8,128)(2,1)S(1)}, bf16[2,192,512]{2,1,0:T(8,128)(2,1)S(1)}, u32[]{:S(2)}, u32[]{:S(2)}) %collective-permute-start.33) | collective-permute-done | bytes 393248 | tf_op jit(solution)/shard_map/ppermute | solution.py:98
  126.9 0.9 collective-permute-start.34
  127.9 6.2 %collective-permute-done.34 = bf16[192,512]{1,0:T(8,128)(2,1)S(1)} collective-permute-done((bf16[192,512]{1,0:T(8,128)(2,1)S(1)}, bf16[192,512]{1,0:T(8,128)(2,1)S(1)}, u32[]{:S(2)}, u32[]{:S(2)}) %collective-permute-start.34) | collective-permute-done | bytes 196640 | tf_op jit(solution)/shard_map/ppermute | solution.py:98
  (119 shorter events, 15.5 us)
Async XLA Ops:
  0.0 18.5 %copy-start.2 = (bf16[1024,192]{0,1:T(8,128)(2,1)S(1)}, bf16[1024,192]{0,1:T(8,128)(2,1)}, u32[]{:S(2)}) copy-start(bf16[1024,192]{0,1:T(8,128)(2,1)} %param.16) | copy-start | bytes 1179652
  0.0 19.1 %copy-start.3 = (bf16[384,768]{1,0:T(8,128)(2,1)S(1)}, bf16[384,768]{1,0:T(8,128)(2,1)}, u32[]{:S(2)}) copy-start(bf16[384,768]{1,0:T(8,128)(2,1)} %param.17) | copy-start | bytes 1769476
  0.0 26.7 %copy-start.4 = (bf16[1,512,384]{2,1,0:T(8,128)(2,1)S(1)}, bf16[1,512,384]{2,1,0:T(8,128)(2,1)}, u32[]{:S(2)}) copy-start(bf16[1,512,384]{2,1,0:T(8,128)(2,1)} %param.12) | copy-start | bytes 1179652
  2.1 21.7 %collective-permute-start.3 = (bf16[2,192,512]{2,1,0:T(8,128)(2,1)S(1)}, bf16[2,192,512]{2,1,0:T(8,128)(2,1)S(1)}, u32[]{:S(2)}, u32[]{:S(2)}) collective-permute-start(bf16[2,192,512]{2,1,0:T(8,128)(2,1)S(1)} %get-tuple-element.53), channel_id=1, source_target_pairs={{0,2},{1,3},{2,0},{3,1},{4,6},{5,7},{6,4},{7,5},{8,10},{9,11},{10,... | collective-permute-start | bytes 1179656 | tf_op jit(solution)/shard_map/ppermute | solution.py:101
  6.2 19.2 %collective-permute-start.7 = (bf16[2,192,512]{2,1,0:T(8,128)(2,1)S(1)}, bf16[2,192,512]{2,1,0:T(8,128)(2,1)}, u32[]{:S(2)}, u32[]{:S(2)}) collective-permute-start(bf16[2,192,512]{2,1,0:T(8,128)(2,1)S(1)} %get-tuple-element.53), channel_id=1, source_target_pairs={{0,4},{4,0},{1,5},{5,1},{2,6},{6,2},{3,7},{7,3},{8,12},{12,8},{9,1... | collective-permute-start | bytes 1179656 | tf_op jit(solution)/shard_map/ppermute | solution.py:98
  7.7 10.8 %collective-permute-start.1 = (bf16[512,384]{1,0:T(8,128)(2,1)}, bf16[512,384]{1,0:T(8,128)(2,1)S(1)}, u32[]{:S(2)}, u32[]{:S(2)}) collective-permute-start(bf16[512,384]{1,0:T(8,128)(2,1)} %bitcast.102), channel_id=1, source_target_pairs={{0,16},{8,24},{16,0},{24,8},{1,17},{9,25},{17,1},{25,9},{2,18},{10... | collective-permute-start | bytes 1179656 | tf_op jit(solution)/shard_map/ppermute | solution.py:98
  9.2 17.5 %collective-permute-start = (bf16[512,384]{1,0:T(8,128)(2,1)}, bf16[512,384]{1,0:T(8,128)(2,1)S(1)}, u32[]{:S(2)}, u32[]{:S(2)}) collective-permute-start(bf16[512,384]{1,0:T(8,128)(2,1)} %bitcast.103), channel_id=1, source_target_pairs={{0,1},{1,0},{2,3},{3,2},{4,5},{5,4},{6,7},{7,6},{8,9},{9,8},{10,11... | collective-permute-start | bytes 1179656 | tf_op jit(solution)/shard_map/ppermute | solution.py:98
  18.4 8.3 %copy-start.5 = (bf16[2,192,512]{2,1,0:T(8,128)(2,1)S(1)}, bf16[2,192,512]{2,1,0:T(8,128)(2,1)}, u32[]{:S(2)}) copy-start(bf16[2,192,512]{2,1,0:T(8,128)(2,1)} %get-tuple-element.28) | copy-start | bytes 1179652
  18.5 6.9 %collective-permute-start.8 = (bf16[1,192,512]{2,1,0:T(8,128)(2,1)S(1)}, bf16[1,192,512]{2,1,0:T(8,128)(2,1)S(1)}, u32[]{:S(2)}, u32[]{:S(2)}) collective-permute-start(bf16[1,192,512]{2,1,0:T(8,128)(2,1)S(1)} %get-tuple-element.29), channel_id=1, source_target_pairs={{0,4},{4,0},{1,5},{5,1},{2,6},{6,2},{3,7},{7,3},{8,12},{12,8},{9,1... | collective-permute-start | bytes 589832 | tf_op jit(solution)/shard_map/ppermute | solution.py:98
  19.1 13.7 %collective-permute-start.2 = (bf16[384,768]{1,0:T(8,128)(2,1)S(1)}, bf16[384,768]{1,0:T(8,128)(2,1)S(1)}, u32[]{:S(2)}, u32[]{:S(2)}) collective-permute-start(bf16[384,768]{1,0:T(8,128)(2,1)S(1)} %copy-done.3), channel_id=1, source_target_pairs={{0,16},{8,24},{16,0},{24,8},{1,17},{9,25},{17,1},{25,9},{2,18},{10... | collective-permute-start | bytes 1769480 | tf_op jit(solution)/shard_map/ppermute | solution.py:98
  23.8 22.8 %collective-permute-start.15 = (bf16[2,192,512]{2,1,0:T(8,128)(2,1)S(1)}, bf16[2,192,512]{2,1,0:T(8,128)(2,1)S(1)}, u32[]{:S(2)}, u32[]{:S(2)}) collective-permute-start(bf16[2,192,512]{2,1,0:T(8,128)(2,1)S(1)} %collective-permute-done.3), channel_id=1, source_target_pairs={{0,4},{4,0},{1,5},{5,1},{2,6},{6,2},{3,7},{7,3},{8,12},{12,8},{9,1... | collective-permute-start | bytes 1179656 | tf_op jit(solution)/shard_map/ppermute | solution.py:98
  25.4 14.1 %collective-permute-start.9 = (bf16[2,192,512]{2,1,0:T(8,128)(2,1)}, bf16[2,192,512]{2,1,0:T(8,128)(2,1)S(1)}, u32[]{:S(2)}, u32[]{:S(2)}) collective-permute-start(bf16[2,192,512]{2,1,0:T(8,128)(2,1)} %get-tuple-element.28), channel_id=1, source_target_pairs={{0,1},{1,2},{2,3},{3,0},{4,5},{5,6},{6,7},{7,4},{8,9},{9,10},{10,1... | collective-permute-start | bytes 1179656 | tf_op jit(solution)/shard_map/ppermute | solution.py:101
  26.8 19.8 %collective-permute-start.14 = (bf16[2,192,512]{2,1,0:T(8,128)(2,1)S(1)}, bf16[2,192,512]{2,1,0:T(8,128)(2,1)S(1)}, u32[]{:S(2)}, u32[]{:S(2)}) collective-permute-start(bf16[2,192,512]{2,1,0:T(8,128)(2,1)S(1)} %copy-done.5), channel_id=1, source_target_pairs={{0,3},{1,0},{2,1},{3,2},{4,7},{5,4},{6,5},{7,6},{8,11},{9,8},{10,9... | collective-permute-start | bytes 1179656 | tf_op jit(solution)/shard_map/ppermute | solution.py:101
  32.8 22.6 %collective-permute-start.4 = (bf16[512,384]{1,0:T(8,128)(2,1)S(1)}, bf16[512,384]{1,0:T(8,128)(2,1)S(1)}, u32[]{:S(2)}, u32[]{:S(2)}) collective-permute-start(bf16[512,384]{1,0:T(8,128)(2,1)S(1)} %collective-permute-done), channel_id=1, source_target_pairs={{0,16},{8,24},{16,0},{24,8},{1,17},{9,25},{17,1},{25,9},{2,18},{10... | collective-permute-start | bytes 1179656 | tf_op jit(solution)/shard_map/ppermute | solution.py:98
  39.5 15.4 %collective-permute-start.10 = (bf16[1,192,512]{2,1,0:T(8,128)(2,1)S(1)}, bf16[1,192,512]{2,1,0:T(8,128)(2,1)S(1)}, u32[]{:S(2)}, u32[]{:S(2)}) collective-permute-start(bf16[1,192,512]{2,1,0:T(8,128)(2,1)S(1)} %get-tuple-element.29), channel_id=1, source_target_pairs={{0,2},{1,3},{2,0},{3,1},{4,6},{5,7},{6,4},{7,5},{8,10},{9,11},{10,... | collective-permute-start | bytes 589832 | tf_op jit(solution)/shard_map/ppermute | solution.py:101
  46.1 10.3 %collective-permute-start.16 = (bf16[2,192,512]{2,1,0:T(8,128)(2,1)S(1)}, bf16[2,192,512]{2,1,0:T(8,128)(2,1)S(1)}, u32[]{:S(2)}, u32[]{:S(2)}) collective-permute-start(bf16[2,192,512]{2,1,0:T(8,128)(2,1)S(1)} %collective-permute-done.9), channel_id=1, source_target_pairs={{0,4},{4,0},{1,5},{5,1},{2,6},{6,2},{3,7},{7,3},{8,12},{12,8},{9,1... | collective-permute-start | bytes 1179656 | tf_op jit(solution)/shard_map/ppermute | solution.py:98
  54.9 17.8 %collective-permute-start.19 = (bf16[1,192,512]{2,1,0:T(8,128)(2,1)S(1)}, bf16[1,192,512]{2,1,0:T(8,128)(2,1)S(1)}, u32[]{:S(2)}, u32[]{:S(2)}) collective-permute-start(bf16[1,192,512]{2,1,0:T(8,128)(2,1)S(1)} %collective-permute-done.10), channel_id=1, source_target_pairs={{0,4},{4,0},{1,5},{5,1},{2,6},{6,2},{3,7},{7,3},{8,12},{12,8},{9,1... | collective-permute-start | bytes 589832 | tf_op jit(solution)/shard_map/ppermute | solution.py:98
  55.5 2.4 %collective-permute-start.5 = (bf16[1024,384]{1,0:T(8,128)(2,1)S(1)}, bf16[1024,384]{1,0:T(8,128)(2,1)S(1)}, u32[]{:S(2)}, u32[]{:S(2)}) collective-permute-start(bf16[1024,384]{1,0:T(8,128)(2,1)S(1)} %pad_maximum_fusion.1), channel_id=1, source_target_pairs={{0,8},{8,0},{16,24},{24,16},{1,9},{9,1},{17,25},{25,17},{2,10},{10... | collective-permute-start | bytes 2359304 | tf_op jit(solution)/shard_map/ppermute | solution.py:98
  55.7 3.3 %collective-permute-start.6 = (bf16[1024,384]{1,0:T(8,128)(2,1)S(1)}, bf16[1024,384]{1,0:T(8,128)(2,1)S(1)}, u32[]{:S(2)}, u32[]{:S(2)}) collective-permute-start(bf16[1024,384]{1,0:T(8,128)(2,1)S(1)} %pad_maximum_fusion.2), channel_id=1, source_target_pairs={{0,8},{8,0},{16,24},{24,16},{1,9},{9,1},{17,25},{25,17},{2,10},{10... | collective-permute-start | bytes 2359304 | tf_op jit(solution)/shard_map/ppermute | solution.py:98
  59.7 9.6 %collective-permute-start.11 = (bf16[1,192,512]{2,1,0:T(8,128)(2,1)S(1)}, bf16[1,192,512]{2,1,0:T(8,128)(2,1)S(1)}, u32[]{:S(2)}, u32[]{:S(2)}) collective-permute-start(bf16[1,192,512]{2,1,0:T(8,128)(2,1)S(1)} %get-tuple-element.30), channel_id=1, source_target_pairs={{0,1},{1,2},{2,3},{3,0},{4,5},{5,6},{6,7},{7,4},{8,9},{9,10},{10,1... | collective-permute-start | bytes 589832 | tf_op jit(solution)/shard_map/ppermute | solution.py:101
  59.8 11.4 %collective-permute-start.18 = (bf16[1,192,512]{2,1,0:T(8,128)(2,1)S(1)}, bf16[1,192,512]{2,1,0:T(8,128)(2,1)S(1)}, u32[]{:S(2)}, u32[]{:S(2)}) collective-permute-start(bf16[1,192,512]{2,1,0:T(8,128)(2,1)S(1)} %get-tuple-element.30), channel_id=1, source_target_pairs={{0,3},{1,0},{2,1},{3,2},{4,7},{5,4},{6,5},{7,6},{8,11},{9,8},{10,9... | collective-permute-start | bytes 589832 | tf_op jit(solution)/shard_map/ppermute | solution.py:101
  63.6 11.6 %collective-permute-start.17 = (bf16[2,192,512]{2,1,0:T(8,128)(2,1)S(1)}, bf16[2,192,512]{2,1,0:T(8,128)(2,1)S(1)}, u32[]{:S(2)}, u32[]{:S(2)}) collective-permute-start(bf16[2,192,512]{2,1,0:T(8,128)(2,1)S(1)} %collective-permute-done.14), channel_id=1, source_target_pairs={{0,4},{4,0},{1,5},{5,1},{2,6},{6,2},{3,7},{7,3},{8,12},{12,8},{9,1... | collective-permute-start | bytes 1179656 | tf_op jit(solution)/shard_map/ppermute | solution.py:98
  69.4 5.9 %collective-permute-start.12 = (bf16[384,768]{1,0:T(8,128)(2,1)S(1)}, bf16[384,768]{1,0:T(8,128)(2,1)S(1)}, u32[]{:S(2)}, u32[]{:S(2)}) collective-permute-start(bf16[384,768]{1,0:T(8,128)(2,1)S(1)} %copy-done.3), channel_id=1, source_target_pairs={{0,8},{8,0},{16,24},{24,16},{1,9},{9,1},{17,25},{25,17},{2,10},{10... | collective-permute-start | bytes 1769480 | tf_op jit(solution)/shard_map/ppermute | solution.py:98
  69.4 6.0 %collective-permute-start.13 = (bf16[384,768]{1,0:T(8,128)(2,1)S(1)}, bf16[384,768]{1,0:T(8,128)(2,1)S(1)}, u32[]{:S(2)}, u32[]{:S(2)}) collective-permute-start(bf16[384,768]{1,0:T(8,128)(2,1)S(1)} %collective-permute-done.2), channel_id=1, source_target_pairs={{0,8},{8,0},{16,24},{24,16},{1,9},{9,1},{17,25},{25,17},{2,10},{10... | collective-permute-start | bytes 1769480 | tf_op jit(solution)/shard_map/ppermute | solution.py:98
  71.2 11.2 %collective-permute-start.20 = (bf16[1,192,512]{2,1,0:T(8,128)(2,1)S(1)}, bf16[1,192,512]{2,1,0:T(8,128)(2,1)S(1)}, u32[]{:S(2)}, u32[]{:S(2)}) collective-permute-start(bf16[1,192,512]{2,1,0:T(8,128)(2,1)S(1)} %collective-permute-done.11), channel_id=1, source_target_pairs={{0,4},{4,0},{1,5},{5,1},{2,6},{6,2},{3,7},{7,3},{8,12},{12,8},{9,1... | collective-permute-start | bytes 589832 | tf_op jit(solution)/shard_map/ppermute | solution.py:98
  72.8 10.1 %collective-permute-start.21 = (bf16[1,192,512]{2,1,0:T(8,128)(2,1)S(1)}, bf16[1,192,512]{2,1,0:T(8,128)(2,1)S(1)}, u32[]{:S(2)}, u32[]{:S(2)}) collective-permute-start(bf16[1,192,512]{2,1,0:T(8,128)(2,1)S(1)} %collective-permute-done.18), channel_id=1, source_target_pairs={{0,4},{4,0},{1,5},{5,1},{2,6},{6,2},{3,7},{7,3},{8,12},{12,8},{9,1... | collective-permute-start | bytes 589832 | tf_op jit(solution)/shard_map/ppermute | solution.py:98
  75.5 6.9 %copy-start.1 = (bf16[1536,768]{1,0:T(8,128)(2,1)}, bf16[1536,768]{1,0:T(8,128)(2,1)S(1)}, u32[]{:S(2)}) copy-start(bf16[1536,768]{1,0:T(8,128)(2,1)S(1)} %constant_dynamic-update-slice_fusion.5) | copy-start | bytes 7077892
  82.9 0.7 copy-start.6
  89.5 2.4 %collective-permute-start.22 = (bf16[2,2,128,768]{3,2,1,0:T(8,128)(2,1)S(1)}, bf16[2,2,128,768]{3,2,1,0:T(8,128)(2,1)S(1)}, u32[]{:S(2)}, u32[]{:S(2)}) collective-permute-start(bf16[2,2,128,768]{3,2,1,0:T(8,128)(2,1)S(1)} %fusion.10), channel_id=1, source_target_pairs={{0,8},{8,0},{16,24},{24,16},{1,9},{9,1},{17,25},{25,17},{2,10},{10... | collective-permute-start | bytes 2359304 | tf_op jit(solution)/shard_map/ppermute | solution.py:98
  93.4 13.0 %copy-start.7 = (f32[768]{0:T(1024)S(1)}, f32[768]{0:T(1024)}, u32[]{:S(2)}) copy-start(f32[768]{0:T(1024)} %param.18) | copy-start | bytes 9220
  93.4 26.2 %copy-start = (bf16[3,768,192]{1,2,0:T(8,128)(2,1)S(1)}, bf16[3,768,192]{1,2,0:T(8,128)(2,1)}, u32[]{:S(2)}) copy-start(bf16[3,768,192]{1,2,0:T(8,128)(2,1)} %param.19) | copy-start | bytes 2654212
  93.5 11.2 %collective-permute-start.23 = (bf16[128,768]{1,0:T(8,128)(2,1)S(1)}, bf16[128,768]{1,0:T(8,128)(2,1)S(1)}, u32[]{:S(2)}, u32[]{:S(2)}) collective-permute-start(bf16[128,768]{1,0:T(8,128)(2,1)S(1)} %get-tuple-element.55), channel_id=1, source_target_pairs={{0,16},{8,24},{16,0},{24,8},{1,17},{9,25},{17,1},{25,9},{2,18},{10... | collective-permute-start | bytes 589832 | tf_op jit(solution)/shard_map/ppermute | solution.py:98
  95.1 9.7 %collective-permute-start.25 = (bf16[128,768]{1,0:T(8,128)(2,1)S(1)}, bf16[128,768]{1,0:T(8,128)(2,1)S(1)}, u32[]{:S(2)}, u32[]{:S(2)}) collective-permute-start(bf16[128,768]{1,0:T(8,128)(2,1)S(1)} %get-tuple-element.56), channel_id=1, source_target_pairs={{0,17},{1,16},{2,19},{3,18},{8,25},{9,24},{10,27},{11,26},{16,1},{... | collective-permute-start | bytes 589832 | tf_op jit(solution)/shard_map/ppermute | solution.py:98
  95.1 10.9 %collective-permute-start.24 = (bf16[128,768]{1,0:T(8,128)(2,1)S(1)}, bf16[128,768]{1,0:T(8,128)(2,1)S(1)}, u32[]{:S(2)}, u32[]{:S(2)}) collective-permute-start(bf16[128,768]{1,0:T(8,128)(2,1)S(1)} %fusion.25), channel_id=1, source_target_pairs={{0,1},{1,0},{2,3},{3,2},{4,5},{5,4},{6,7},{7,6},{8,9},{9,8},{10,11... | collective-permute-start | bytes 589832 | tf_op jit(solution)/shard_map/ppermute | solution.py:98
  106.5 7.7 %collective-permute-start.26 = (bf16[128,768]{1,0:T(8,128)(2,1)S(1)}, bf16[128,768]{1,0:T(8,128)(2,1)S(1)}, u32[]{:S(2)}, u32[]{:S(2)}) collective-permute-start(bf16[128,768]{1,0:T(8,128)(2,1)S(1)} %multiply_convert_fusion.1.refs_0_), channel_id=1, source_target_pairs={{0,16},{8,24},{16,0},{24,8},{1,17},{9,25},{17,1},{25,9},{2,18},{10... | collective-permute-start | bytes 589832 | tf_op jit(solution)/shard_map/ppermute | solution.py:98
  108.1 9.8 %collective-permute-start.29 = (bf16[128,768]{1,0:T(8,128)(2,1)S(1)}, bf16[128,768]{1,0:T(8,128)(2,1)S(1)}, u32[]{:S(2)}, u32[]{:S(2)}) collective-permute-start(bf16[128,768]{1,0:T(8,128)(2,1)S(1)} %multiply_convert_fusion.1.refs_0_), channel_id=1, source_target_pairs={{0,4},{4,0},{1,5},{5,1},{2,6},{6,2},{3,7},{7,3},{8,12},{12,8},{9,1... | collective-permute-start | bytes 589832 | tf_op jit(solution)/shard_map/ppermute | solution.py:98
  109.6 8.4 %collective-permute-start.30 = (bf16[128,768]{1,0:T(8,128)(2,1)S(1)}, bf16[128,768]{1,0:T(8,128)(2,1)S(1)}, u32[]{:S(2)}, u32[]{:S(2)}) collective-permute-start(bf16[128,768]{1,0:T(8,128)(2,1)S(1)} %multiply_convert_fusion.1.refs_0_), channel_id=1, source_target_pairs={{0,20},{4,16},{8,28},{12,24},{16,4},{20,0},{24,12},{28,8},{1,21},{... | collective-permute-start | bytes 589832 | tf_op jit(solution)/shard_map/ppermute | solution.py:98
  110.1 8.3 %collective-permute-start.27 = (bf16[128,768]{1,0:T(8,128)(2,1)S(1)}, bf16[128,768]{1,0:T(8,128)(2,1)S(1)}, u32[]{:S(2)}, u32[]{:S(2)}) collective-permute-start(bf16[128,768]{1,0:T(8,128)(2,1)S(1)} %multiply_convert_fusion.1.refs_0_), channel_id=1, source_target_pairs={{0,8},{8,0},{16,24},{24,16},{1,9},{9,1},{17,25},{25,17},{2,10},{10... | collective-permute-start | bytes 589832 | tf_op jit(solution)/shard_map/ppermute | solution.py:98
  114.3 4.2 %collective-permute-start.28 = (bf16[128,768]{1,0:T(8,128)(2,1)S(1)}, bf16[128,768]{1,0:T(8,128)(2,1)S(1)}, u32[]{:S(2)}, u32[]{:S(2)}) collective-permute-start(bf16[128,768]{1,0:T(8,128)(2,1)S(1)} %collective-permute-done.26.refs_1_), channel_id=1, source_target_pairs={{0,8},{8,0},{16,24},{24,16},{1,9},{9,1},{17,25},{25,17},{2,10},{10... | collective-permute-start | bytes 589832 | tf_op jit(solution)/shard_map/ppermute | solution.py:98
  117.9 1.4 %collective-permute-start.31 = (bf16[128,768]{1,0:T(8,128)(2,1)S(1)}, bf16[128,768]{1,0:T(8,128)(2,1)S(1)}, u32[]{:S(2)}, u32[]{:S(2)}) collective-permute-start(bf16[128,768]{1,0:T(8,128)(2,1)S(1)} %collective-permute-done.29.refs_4_), channel_id=1, source_target_pairs={{0,8},{8,0},{16,24},{24,16},{1,9},{9,1},{17,25},{25,17},{2,10},{10... | collective-permute-start | bytes 589832 | tf_op jit(solution)/shard_map/ppermute | solution.py:98
  117.9 1.7 %collective-permute-start.32 = (bf16[128,768]{1,0:T(8,128)(2,1)S(1)}, bf16[128,768]{1,0:T(8,128)(2,1)S(1)}, u32[]{:S(2)}, u32[]{:S(2)}) collective-permute-start(bf16[128,768]{1,0:T(8,128)(2,1)S(1)} %collective-permute-done.30.refs_5_), channel_id=1, source_target_pairs={{0,8},{8,0},{16,24},{24,16},{1,9},{9,1},{17,25},{25,17},{2,10},{10... | collective-permute-start | bytes 589832 | tf_op jit(solution)/shard_map/ppermute | solution.py:98
  125.0 1.8 %collective-permute-start.33 = (bf16[2,192,512]{2,1,0:T(8,128)(2,1)S(1)}, bf16[2,192,512]{2,1,0:T(8,128)(2,1)S(1)}, u32[]{:S(2)}, u32[]{:S(2)}) collective-permute-start(bf16[2,192,512]{2,1,0:T(8,128)(2,1)S(1)} %get-tuple-element.40), channel_id=1, source_target_pairs={{0,8},{8,0},{16,24},{24,16},{1,9},{9,1},{17,25},{25,17},{2,10},{10... | collective-permute-start | bytes 1179656 | tf_op jit(solution)/shard_map/ppermute | solution.py:98
  126.9 7.1 %collective-permute-start.34 = (bf16[192,512]{1,0:T(8,128)(2,1)S(1)}, bf16[192,512]{1,0:T(8,128)(2,1)S(1)}, u32[]{:S(2)}, u32[]{:S(2)}) collective-permute-start(bf16[192,512]{1,0:T(8,128)(2,1)S(1)} %fusion.27), channel_id=1, source_target_pairs={{0,16},{8,24},{16,0},{24,8},{1,17},{9,25},{17,1},{25,9},{2,18},{10... | collective-permute-start | bytes 589832 | tf_op jit(solution)/shard_map/ppermute | solution.py:98

commit v13 on v12

--- a/solution.py
+++ b/solution.py
@@ -201,14 +201,14 @@
             g[1, 0] = flip(pair_same, seq=1)
             d[1, 0] = flip(after(down_same, mine_x), seq=1)
             proj_x = flip(after(w_proj, mine_x), section=2)
-            beside_x = flip(after(beside, proj_x, g[0, 2]), section=2)
+            beside_x = flip(after(beside, g[0, 2]), section=2)
             for k in (1, 3):
                 g[0, k] = rotate(after(pair_other, g[0, 2], g[1, 0], d[1, 0]), k)
             g[1, 2] = flip(g[0, 2], seq=1)
             across = after(jnp.concatenate([mine_x, beside_x], axis=0), g[0, 2])
             both = after(jnp.concatenate([mine, beside], axis=0), across)
             both_c, across_c = flip(both, section=1), flip(across, section=1)
-            d[0, 2] = rotate(after(down_same, g[0, 1]), 2)
+            d[0, 2] = rotate(after(down_same, g[0, 1], across), 2)
             rows = jnp.concatenate([both, both_c, across, across_c], axis=1)
             normed = layer_norm(rows.astype(jnp.float32), gain).astype(jnp.bfloat16)
             g[1, 1] = flip(g[0, 1], seq=1)
@@ -239,9 +239,6 @@
         up = jnp.dot(normed, gate_up[1], preferred_element_type=jnp.float32)
         hidden = (jax.nn.silu(gate) * up).astype(jnp.bfloat16)
         hidden = hidden.reshape(2, n_sec // 2, 2, own_rows, half)
-        hidden = jnp.stack(
-            [lax.dynamic_index_in_dim(hidden, c, 2, False) for c in (1 - core, core)]
-        )
 
         def fold(proj_rows, down_rows):
             return lax.dot_general(
@@ -265,9 +262,10 @@
                 x, folded, (((x.ndim - 1,), (1,)), ((), ())), preferred_element_type=jnp.float32
             )
 
-        sums = project(hidden)
-        got = flip(sums[0].astype(jnp.bfloat16), section=1)
-        kept = sums[1] + got.astype(jnp.float32)
+        send = project(lax.dynamic_index_in_dim(hidden, 1 - core, 2, False)).astype(jnp.bfloat16)
+        got = flip(send, section=1)
+        kept = after(project(lax.dynamic_index_in_dim(hidden, core, 2, False)), send)
+        kept = kept + got.astype(jnp.float32)
         here = lax.dynamic_index_in_dim(kept, side, 1, False)
         there = lax.dynamic_index_in_dim(kept, 1 - side, 1, False).astype(jnp.bfloat16)
         from_x = flip(there[0], section=2)
@@ -306,7 +304,7 @@
                 ],
                 in_specs=[vmem] * 12,
                 out_specs=[vmem] * 2,
-                compiler_params=pltpu.CompilerParams(vmem_limit_bytes=28 * 2**20),
+                compiler_params=pltpu.CompilerParams(vmem_limit_bytes=16 * 2**20),
                 cost_estimate=pl.CostEstimate(
                     flops=2 * count * width * (3 * 768 + 2 * local_heads * tokens),
                     bytes_accessed=8 * 2**20,

time: 135 us -> 129 us (0.956)
  waiting for transfers between devices: 55.7 us -> 63.9 us
  starting transfers between devices: 41.2 us -> 33.6 us
  matrix products: 11.7 us -> 8.77 us
  local copies, waits for them, and re-layouts: 6.92 us -> 4.43 us
    ppermute x29, waiting for transfers between devices: 35.6 us -> 43.7 us  [flip(): return lax.ppermute(x, names if len(names) > 1 else names[0], pairs)]
    ppermute x6, starting transfers between devices: 17.7 us -> 13.7 us  [rotate(): return lax.ppermute(x, 'dp', [(i, (i + k) % n_dp) for i in range(n_dp)])]
    ppermute x29, starting transfers between devices: 23.5 us -> 20 us  [flip(): return lax.ppermute(x, names if len(names) > 1 else names[0], pairs)]
    dot_general x1 -> x2, matrix products: 4.48 us -> 2.25 us  [project(): lax.dot_general(x, folded, (((x.ndim - 1,), (1,)), ((), ())), preferred_e...]
    convert_element_type x1 -> x0, local copies, waits for them, and re-layouts: 1.49 us -> none  [per_device(): got = flip(sums[0].astype(jnp.bfloat16), section=1)]
    add x1, other arithmetic: 1.55 us -> 0.19 us  [per_device(): kept = kept + got.astype(jnp.float32)]
    dot_general x2 -> x3, matrix products: 3 us -> 2.25 us  [fold(): lax.dot_general(proj_rows, down_rows, (((0,), (0,)), ((), ())), preferred...]
  transfers between devices with their start and end apart: 35 -> 35, of which waited for: 19 -> 21; matrix products, arithmetic and copies ran while one was open for 15% -> 16% of each run, Pallas kernels for 0% -> 0%
where the time goes in v13:
time: 129 us
  waiting for transfers between devices  63.9 us (50%)
  starting transfers between devices  33.6 us (26%)
  other arithmetic  11.7 us (9%)
  matrix products  8.77 us (7%)
  Pallas kernels  5.59 us (4%)
  local copies, waits for them, and re-layouts  4.43 us (3%)
    ppermute x29, waiting for transfers between devices, flip(): return lax.ppermute(x, names if len(names) > 1 else names[0], pairs)  43.7 us
    ppermute x6, waiting for transfers between devices, rotate(): return lax.ppermute(x, 'dp', [(i, (i + k) % n_dp) for i in range(n_dp)])  20.3 us
    ppermute x29, starting transfers between devices, flip(): return lax.ppermute(x, names if len(names) > 1 else names[0], pairs)  20 us
    ppermute x6, starting transfers between devices, rotate(): return lax.ppermute(x, 'dp', [(i, (i + k) % n_dp) for i in range(n_dp)])  13.7 us
    pallas_call x1, Pallas kernels, per_device(): pl.pallas_call(lambda *refs: attend_kernel(*refs, heads=local_heads, mask...  5.59 us
  transfers between devices with their start and end apart: 35, of which 21 were waited for; matrix products, arithmetic and copies ran while one was open for 16% of the time, Pallas kernels for 0%

profile of v13, /device:TPU:0, one launch (start us, length us, event | category | flops | bytes accessed | tf_op | source)
XLA Modules:
  0.0 128.8 jit_solution(11115376299819493001)
XLA Ops:
  0.0 1.3 %fusion.14 = (bf16[2,192,512]{2,1,0:T(8,128)(2,1)S(1)}, bf16[2,192,512]{2,1,0:T(8,128)(2,1)S(1)}) fusion(s32[]{:T(128)S(6)} %select_n.236, bf16[1,192,1024]{2,1,0:T(8,128)(2,1)} %bitcast.94, bf16[1,192,1024]{2,1,0:T(8,128)(2,1)} %bitcast.95, s32[]{:T(128)S(6)} %select_n.238), kind=kLoop, calls=%fused_computation.30 | loop fusion | flops 1572864 | bytes 1572872 | tf_op jit(solution)/shard_map/stack | solution.py:163
  1.4 4.1 %collective-permute-start.2 = (bf16[2,192,512]{2,1,0:T(8,128)(2,1)S(1)}, bf16[2,192,512]{2,1,0:T(8,128)(2,1)S(1)}, u32[]{:S(2)}, u32[]{:S(2)}) collective-permute-start(bf16[2,192,512]{2,1,0:T(8,128)(2,1)S(1)} %get-tuple-element.53), channel_id=1, source_target_pairs={{0,2},{1,3},{2,0},{3,1},{4,6},{5,7},{6,4},{7,5},{8,10},{9,11},{10,... | collective-permute-start | bytes 1179656 | tf_op jit(solution)/shard_map/ppermute | solution.py:101
  5.5 1.5 %collective-permute-start.7 = (bf16[2,192,512]{2,1,0:T(8,128)(2,1)S(1)}, bf16[2,192,512]{2,1,0:T(8,128)(2,1)S(1)}, u32[]{:S(2)}, u32[]{:S(2)}) collective-permute-start(bf16[2,192,512]{2,1,0:T(8,128)(2,1)S(1)} %get-tuple-element.53), channel_id=1, source_target_pairs={{0,4},{4,0},{1,5},{5,1},{2,6},{6,2},{3,7},{7,3},{8,12},{12,8},{9,1... | collective-permute-start | bytes 1179656 | tf_op jit(solution)/shard_map/ppermute | solution.py:98
  7.0 1.5 %collective-permute-start.1 = (bf16[512,384]{1,0:T(8,128)(2,1)}, bf16[512,384]{1,0:T(8,128)(2,1)S(1)}, u32[]{:S(2)}, u32[]{:S(2)}) collective-permute-start(bf16[512,384]{1,0:T(8,128)(2,1)} %bitcast.96), channel_id=1, source_target_pairs={{0,16},{8,24},{16,0},{24,8},{1,17},{9,25},{17,1},{25,9},{2,18},{10... | collective-permute-start | bytes 1179656 | tf_op jit(solution)/shard_map/ppermute | solution.py:98
  8.5 1.6 %collective-permute-start = (bf16[512,384]{1,0:T(8,128)(2,1)}, bf16[512,384]{1,0:T(8,128)(2,1)}, u32[]{:S(2)}, u32[]{:S(2)}) collective-permute-start(bf16[512,384]{1,0:T(8,128)(2,1)} %bitcast.97), channel_id=1, source_target_pairs={{0,1},{1,0},{2,3},{3,2},{4,5},{5,4},{6,7},{7,6},{8,9},{9,8},{10,11... | collective-permute-start | bytes 1179656 | tf_op jit(solution)/shard_map/ppermute | solution.py:98
  10.0 0.8 reduce-window.8
  13.0 0.8 fusion.51
  14.8 1.4 %fusion.31 = (s32[4,1024]{1,0:T(4,128)S(1)}, s32[4,1024]{1,0:T(4,128)S(1)}) fusion(s32[4]{0:T(128)} %param.22, s32[1024]{0:T(1024)S(1)} %get-tuple-element.52, s32[1024]{0:T(1024)S(1)} %get-tuple-element.51, s32[1024]{0:T(1024)S(1)} %get-tuple-element.67, s32[4]{0:T(128)S(1)} %sign.69, s32[4]{0:T(128)S(1)} %get-tuple-element.66, ...), kind=kLoop, calls=%fused_computation.80 | loop fusion | flops 69632 | bytes 45124 | tf_op jit(solution)/shard_map/add | solution.py:185
  17.1 1.1 copy.14
  19.5 3.6 %collective-permute-done.2 = bf16[2,192,512]{2,1,0:T(8,128)(2,1)S(1)} collective-permute-done((bf16[2,192,512]{2,1,0:T(8,128)(2,1)S(1)}, bf16[2,192,512]{2,1,0:T(8,128)(2,1)S(1)}, u32[]{:S(2)}, u32[]{:S(2)}) %collective-permute-start.2) | collective-permute-done | bytes 393248 | tf_op jit(solution)/shard_map/ppermute | solution.py:101
  23.1 3.0 %collective-permute-done = bf16[512,384]{1,0:T(8,128)(2,1)} collective-permute-done((bf16[512,384]{1,0:T(8,128)(2,1)}, bf16[512,384]{1,0:T(8,128)(2,1)}, u32[]{:S(2)}, u32[]{:S(2)}) %collective-permute-start) | collective-permute-done | bytes 393248 | tf_op jit(solution)/shard_map/ppermute | solution.py:98
  27.5 1.1 pad_maximum_fusion
  28.6 0.8 collective-permute-start.9
  29.4 3.1 %collective-permute-start.14 = (bf16[2,192,512]{2,1,0:T(8,128)(2,1)S(1)}, bf16[2,192,512]{2,1,0:T(8,128)(2,1)S(1)}, u32[]{:S(2)}, u32[]{:S(2)}) collective-permute-start(bf16[2,192,512]{2,1,0:T(8,128)(2,1)S(1)} %get-tuple-element.29), channel_id=1, source_target_pairs={{0,3},{1,0},{2,1},{3,2},{4,7},{5,4},{6,5},{7,6},{8,11},{9,8},{10,9... | collective-permute-start | bytes 1179656 | tf_op jit(solution)/shard_map/ppermute | solution.py:101
  32.6 8.2 %collective-permute-done.3 = bf16[512,384]{1,0:T(8,128)(2,1)S(1)} collective-permute-done((bf16[512,384]{1,0:T(8,128)(2,1)}, bf16[512,384]{1,0:T(8,128)(2,1)S(1)}, u32[]{:S(2)}, u32[]{:S(2)}) %collective-permute-start.3) | collective-permute-done | bytes 393248 | tf_op jit(solution)/shard_map/ppermute | solution.py:98
  41.0 1.4 %collective-permute-done.9 = bf16[2,192,512]{2,1,0:T(8,128)(2,1)S(1)} collective-permute-done((bf16[2,192,512]{2,1,0:T(8,128)(2,1)S(1)}, bf16[2,192,512]{2,1,0:T(8,128)(2,1)S(1)}, u32[]{:S(2)}, u32[]{:S(2)}) %collective-permute-start.9) | collective-permute-done | bytes 393248 | tf_op jit(solution)/shard_map/ppermute | solution.py:101
  42.5 4.5 %collective-permute-done.14 = bf16[2,192,512]{2,1,0:T(8,128)(2,1)S(1)} collective-permute-done((bf16[2,192,512]{2,1,0:T(8,128)(2,1)S(1)}, bf16[2,192,512]{2,1,0:T(8,128)(2,1)S(1)}, u32[]{:S(2)}, u32[]{:S(2)}) %collective-permute-start.14) | collective-permute-done | bytes 393248 | tf_op jit(solution)/shard_map/ppermute | solution.py:101
  47.0 1.8 %collective-permute-start.10 = (bf16[1,192,512]{2,1,0:T(8,128)(2,1)S(1)}, bf16[1,192,512]{2,1,0:T(8,128)(2,1)S(1)}, u32[]{:S(2)}, u32[]{:S(2)}) collective-permute-start(bf16[1,192,512]{2,1,0:T(8,128)(2,1)S(1)} %copy-done.6), channel_id=1, source_target_pairs={{0,2},{1,3},{2,0},{3,1},{4,6},{5,7},{6,4},{7,5},{8,10},{9,11},{10,... | collective-permute-start | bytes 589832 | tf_op jit(solution)/shard_map/ppermute | solution.py:101
  49.5 8.4 %collective-permute-done.10 = bf16[1,192,512]{2,1,0:T(8,128)(2,1)S(1)} collective-permute-done((bf16[1,192,512]{2,1,0:T(8,128)(2,1)S(1)}, bf16[1,192,512]{2,1,0:T(8,128)(2,1)S(1)}, u32[]{:S(2)}, u32[]{:S(2)}) %collective-permute-start.10) | collective-permute-done | bytes 196640 | tf_op jit(solution)/shard_map/ppermute | solution.py:101
  58.7 2.3 %collective-permute-done.16 = bf16[2,192,512]{2,1,0:T(8,128)(2,1)S(1)} collective-permute-done((bf16[2,192,512]{2,1,0:T(8,128)(2,1)S(1)}, bf16[2,192,512]{2,1,0:T(8,128)(2,1)S(1)}, u32[]{:S(2)}, u32[]{:S(2)}) %collective-permute-start.16) | collective-permute-done | bytes 393248 | tf_op jit(solution)/shard_map/ppermute | solution.py:98
  61.0 1.7 %collective-permute-start.11 = (bf16[1,192,512]{2,1,0:T(8,128)(2,1)S(1)}, bf16[1,192,512]{2,1,0:T(8,128)(2,1)S(1)}, u32[]{:S(2)}, u32[]{:S(2)}) collective-permute-start(bf16[1,192,512]{2,1,0:T(8,128)(2,1)S(1)} %copy-done.5), channel_id=1, source_target_pairs={{0,1},{1,2},{2,3},{3,0},{4,5},{5,6},{6,7},{7,4},{8,9},{9,10},{10,1... | collective-permute-start | bytes 589832 | tf_op jit(solution)/shard_map/ppermute | solution.py:101
  62.7 2.2 %collective-permute-start.18 = (bf16[1,192,512]{2,1,0:T(8,128)(2,1)S(1)}, bf16[1,192,512]{2,1,0:T(8,128)(2,1)S(1)}, u32[]{:S(2)}, u32[]{:S(2)}) collective-permute-start(bf16[1,192,512]{2,1,0:T(8,128)(2,1)S(1)} %copy-done.5), channel_id=1, source_target_pairs={{0,3},{1,0},{2,1},{3,2},{4,7},{5,4},{6,5},{7,6},{8,11},{9,8},{10,9... | collective-permute-start | bytes 589832 | tf_op jit(solution)/shard_map/ppermute | solution.py:101
  66.0 1.0 fusion.2
  67.6 1.0 fusion.4
  68.6 0.8 collective-permute-done.11
  70.0 1.4 %collective-permute-done.18 = bf16[1,192,512]{2,1,0:T(8,128)(2,1)S(1)} collective-permute-done((bf16[1,192,512]{2,1,0:T(8,128)(2,1)S(1)}, bf16[1,192,512]{2,1,0:T(8,128)(2,1)S(1)}, u32[]{:S(2)}, u32[]{:S(2)}) %collective-permute-start.18) | collective-permute-done | bytes 196640 | tf_op jit(solution)/shard_map/ppermute | solution.py:101
  71.4 1.4 %collective-permute-start.20 = (bf16[1,192,512]{2,1,0:T(8,128)(2,1)S(1)}, bf16[1,192,512]{2,1,0:T(8,128)(2,1)S(1)}, u32[]{:S(2)}, u32[]{:S(2)}) collective-permute-start(bf16[1,192,512]{2,1,0:T(8,128)(2,1)S(1)} %collective-permute-done.11), channel_id=1, source_target_pairs={{0,4},{4,0},{1,5},{5,1},{2,6},{6,2},{3,7},{7,3},{8,12},{12,8},{9,1... | collective-permute-start | bytes 589832 | tf_op jit(solution)/shard_map/ppermute | solution.py:98
  73.6 3.5 %collective-permute-done.17 = bf16[2,192,512]{2,1,0:T(8,128)(2,1)S(1)} collective-permute-done((bf16[2,192,512]{2,1,0:T(8,128)(2,1)S(1)}, bf16[2,192,512]{2,1,0:T(8,128)(2,1)S(1)}, u32[]{:S(2)}, u32[]{:S(2)}) %collective-permute-start.17) | collective-permute-done | bytes 393248 | tf_op jit(solution)/shard_map/ppermute | solution.py:98
  77.7 1.8 %fusion.6 = f32[1024,512]{1,0:T(8,128)S(1)} fusion(bf16[1024,1536]{1,0:T(8,128)(2,1)S(1)} %fusion.4, bf16[2,1536,512]{2,1,0:T(8,128)(2,1)S(1)} %constant_dynamic-update-slice_fusion.11), kind=kOutput, calls=%fused_computation.11 | convolution fusion | flops 1610612736 | bytes 6815744 | tf_op jit(solution)/shard_map/dot_general | solution.py:238
  79.5 2.0 %multiply_convert_fusion = bf16[1024,512]{1,0:T(8,128)(2,1)S(1)} fusion(f32[1024,512]{1,0:T(8,128)S(1)} %fusion.6, bf16[1024,1536]{1,0:T(8,128)(2,1)S(1)} %fusion.4, bf16[2,1536,512]{2,1,0:T(8,128)(2,1)S(1)} %constant_dynamic-update-slice_fusion.11), kind=kOutput, calls=%fused_computation.7 | convolution fusion | flops 1613758464 | bytes 7864320 | tf_op jit(solution)/shard_map/dot_general | solution.py:239
  81.5 1.4 %fusion.52 = f32[768,512]{1,0:T(8,128)S(1)} fusion(bf16[1536,768]{1,0:T(8,128)(2,1)S(1)} %constant_dynamic-update-slice_fusion.5, bf16[1536,512]{1,0:T(8,128)(2,1)S(1)} %bitcast_dynamic-update-slice_fusion), kind=kOutput, calls=%fused_computation.130 | convolution fusion | flops 1207959552 | bytes 5505024 | tf_op jit(solution)/shard_map/dot_general | solution.py:244
  84.9 1.6 %fusion.9 = f32[2,2,128,768]{3,2,1,0:T(8,128)S(1)} fusion(bf16[768,512,1,1]{1,0,3,2:T(8,128)(2,1)S(1)} %fusion.7, bf16[2,2,2,128,512]{4,3,2,1,0:T(8,128)(2,1)} %bitcast.100, s32[]{:T(128)S(6)} %select_n.278), kind=kOutput, calls=%fused_computation.25 | convolution fusion | flops 402653184 | bytes 2883588 | tf_op jit(solution)/shard_map/dot_general | solution.py:261
  87.4 1.0 collective-permute-start.25
  88.4 1.2 collective-permute-start.24
  89.6 1.4 %collective-permute-start.23 = (bf16[128,768]{1,0:T(8,128)(2,1)S(1)}, bf16[128,768]{1,0:T(8,128)(2,1)S(1)}, u32[]{:S(2)}, u32[]{:S(2)}) collective-permute-start(bf16[128,768]{1,0:T(8,128)(2,1)S(1)} %get-tuple-element.55), channel_id=1, source_target_pairs={{0,16},{8,24},{16,0},{24,8},{1,17},{9,25},{17,1},{25,9},{2,18},{10... | collective-permute-start | bytes 589832 | tf_op jit(solution)/shard_map/ppermute | solution.py:98
  91.1 5.1 %collective-permute-done.25 = bf16[128,768]{1,0:T(8,128)(2,1)S(1)} collective-permute-done((bf16[128,768]{1,0:T(8,128)(2,1)S(1)}, bf16[128,768]{1,0:T(8,128)(2,1)S(1)}, u32[]{:S(2)}, u32[]{:S(2)}) %collective-permute-start.25) | collective-permute-done | bytes 196640 | tf_op jit(solution)/shard_map/ppermute | solution.py:98
  96.2 2.5 %collective-permute-done.24 = bf16[128,768]{1,0:T(8,128)(2,1)S(1)} collective-permute-done((bf16[128,768]{1,0:T(8,128)(2,1)S(1)}, bf16[128,768]{1,0:T(8,128)(2,1)S(1)}, u32[]{:S(2)}, u32[]{:S(2)}) %collective-permute-start.24) | collective-permute-done | bytes 196640 | tf_op jit(solution)/shard_map/ppermute | solution.py:98
  98.7 0.8 collective-permute-done.23
  100.8 1.5 %collective-permute-start.29 = (bf16[128,768]{1,0:T(8,128)(2,1)S(1)}, bf16[128,768]{1,0:T(8,128)(2,1)S(1)}, u32[]{:S(2)}, u32[]{:S(2)}) collective-permute-start(bf16[128,768]{1,0:T(8,128)(2,1)S(1)} %multiply_convert_fusion.1.refs_0_), channel_id=1, source_target_pairs={{0,4},{4,0},{1,5},{5,1},{2,6},{6,2},{3,7},{7,3},{8,12},{12,8},{9,1... | collective-permute-start | bytes 589832 | tf_op jit(solution)/shard_map/ppermute | solution.py:98
  102.3 1.4 %collective-permute-start.30 = (bf16[128,768]{1,0:T(8,128)(2,1)S(1)}, bf16[128,768]{1,0:T(8,128)(2,1)S(1)}, u32[]{:S(2)}, u32[]{:S(2)}) collective-permute-start(bf16[128,768]{1,0:T(8,128)(2,1)S(1)} %multiply_convert_fusion.1.refs_0_), channel_id=1, source_target_pairs={{0,20},{4,16},{8,28},{12,24},{16,4},{20,0},{24,12},{28,8},{1,21},{... | collective-permute-start | bytes 589832 | tf_op jit(solution)/shard_map/ppermute | solution.py:98
  103.7 4.3 %collective-permute-done.26.refs_1_ = bf16[128,768]{1,0:T(8,128)(2,1)S(1)} collective-permute-done((bf16[128,768]{1,0:T(8,128)(2,1)S(1)}, bf16[128,768]{1,0:T(8,128)(2,1)S(1)}, u32[]{:S(2)}, u32[]{:S(2)}) %collective-permute-start.26) | collective-permute-done | bytes 196640 | tf_op jit(solution)/shard_map/ppermute | solution.py:98
  107.9 2.6 %collective-permute-done.29.refs_4_ = bf16[128,768]{1,0:T(8,128)(2,1)S(1)} collective-permute-done((bf16[128,768]{1,0:T(8,128)(2,1)S(1)}, bf16[128,768]{1,0:T(8,128)(2,1)S(1)}, u32[]{:S(2)}, u32[]{:S(2)}) %collective-permute-start.29) | collective-permute-done | bytes 196640 | tf_op jit(solution)/shard_map/ppermute | solution.py:98
  110.5 1.6 %collective-permute-done.30.refs_5_ = bf16[128,768]{1,0:T(8,128)(2,1)S(1)} collective-permute-done((bf16[128,768]{1,0:T(8,128)(2,1)S(1)}, bf16[128,768]{1,0:T(8,128)(2,1)S(1)}, u32[]{:S(2)}, u32[]{:S(2)}) %collective-permute-start.30) | collective-permute-done | bytes 196640 | tf_op jit(solution)/shard_map/ppermute | solution.py:98
  112.1 1.4 %collective-permute-done.32.refs_7_ = bf16[128,768]{1,0:T(8,128)(2,1)S(1)} collective-permute-done((bf16[128,768]{1,0:T(8,128)(2,1)S(1)}, bf16[128,768]{1,0:T(8,128)(2,1)S(1)}, u32[]{:S(2)}, u32[]{:S(2)}) %collective-permute-start.32) | collective-permute-done | bytes 196640 | tf_op jit(solution)/shard_map/ppermute | solution.py:98
  113.6 5.6 %shard_map.118 = (f32[2,192,512]{2,1,0:T(8,128)S(1)}, bf16[2,192,512]{2,1,0:T(8,128)(2,1)S(1)}) custom-call(bf16[128,768]{1,0:T(8,128)(2,1)S(1)} %multiply_convert_fusion.1.refs_0_, bf16[128,768]{1,0:T(8,128)(2,1)S(1)} %collective-permute-done.26.refs_1_, bf16[128,768]{1,0:T(8,128)(2,1)S(1)} %collective-permute-done.27.refs_2_, ...), custom_call_target="tpu_custom_call" | custom-call | flops 2516582400 | bytes 8388608 | tf_op jit(solution)/shard_map/pallas_call | solution.py:299
  119.4 1.6 %collective-permute-done.33 = bf16[2,192,512]{2,1,0:T(8,128)(2,1)S(1)} collective-permute-done((bf16[2,192,512]{2,1,0:T(8,128)(2,1)S(1)}, bf16[2,192,512]{2,1,0:T(8,128)(2,1)S(1)}, u32[]{:S(2)}, u32[]{:S(2)}) %collective-permute-start.33) | collective-permute-done | bytes 393248 | tf_op jit(solution)/shard_map/ppermute | solution.py:98
  121.1 1.2 collective-permute-start.34
  122.3 5.8 %collective-permute-done.34 = bf16[192,512]{1,0:T(8,128)(2,1)S(1)} collective-permute-done((bf16[192,512]{1,0:T(8,128)(2,1)S(1)}, bf16[192,512]{1,0:T(8,128)(2,1)S(1)}, u32[]{:S(2)}, u32[]{:S(2)}) %collective-permute-start.34) | collective-permute-done | bytes 196640 | tf_op jit(solution)/shard_map/ppermute | solution.py:98
  (119 shorter events, 16.8 us)
Async XLA Ops:
  0.0 16.3 %copy-start.1 = (bf16[1024,192]{0,1:T(8,128)(2,1)S(1)}, bf16[1024,192]{0,1:T(8,128)(2,1)}, u32[]{:S(2)}) copy-start(bf16[1024,192]{0,1:T(8,128)(2,1)} %param.16) | copy-start | bytes 1179652
  0.0 18.3 %copy-start.2 = (bf16[384,768]{1,0:T(8,128)(2,1)S(1)}, bf16[384,768]{1,0:T(8,128)(2,1)}, u32[]{:S(2)}) copy-start(bf16[384,768]{1,0:T(8,128)(2,1)} %param.17) | copy-start | bytes 1769476
  1.4 21.7 %collective-permute-start.2 = (bf16[2,192,512]{2,1,0:T(8,128)(2,1)S(1)}, bf16[2,192,512]{2,1,0:T(8,128)(2,1)S(1)}, u32[]{:S(2)}, u32[]{:S(2)}) collective-permute-start(bf16[2,192,512]{2,1,0:T(8,128)(2,1)S(1)} %get-tuple-element.53), channel_id=1, source_target_pairs={{0,2},{1,3},{2,0},{3,1},{4,6},{5,7},{6,4},{7,5},{8,10},{9,11},{10,... | collective-permute-start | bytes 1179656 | tf_op jit(solution)/shard_map/ppermute | solution.py:101
  5.5 23.1 %collective-permute-start.7 = (bf16[2,192,512]{2,1,0:T(8,128)(2,1)S(1)}, bf16[2,192,512]{2,1,0:T(8,128)(2,1)S(1)}, u32[]{:S(2)}, u32[]{:S(2)}) collective-permute-start(bf16[2,192,512]{2,1,0:T(8,128)(2,1)S(1)} %get-tuple-element.53), channel_id=1, source_target_pairs={{0,4},{4,0},{1,5},{5,1},{2,6},{6,2},{3,7},{7,3},{8,12},{12,8},{9,1... | collective-permute-start | bytes 1179656 | tf_op jit(solution)/shard_map/ppermute | solution.py:98
  7.0 11.4 %collective-permute-start.1 = (bf16[512,384]{1,0:T(8,128)(2,1)}, bf16[512,384]{1,0:T(8,128)(2,1)S(1)}, u32[]{:S(2)}, u32[]{:S(2)}) collective-permute-start(bf16[512,384]{1,0:T(8,128)(2,1)} %bitcast.96), channel_id=1, source_target_pairs={{0,16},{8,24},{16,0},{24,8},{1,17},{9,25},{17,1},{25,9},{2,18},{10... | collective-permute-start | bytes 1179656 | tf_op jit(solution)/shard_map/ppermute | solution.py:98
  8.5 17.6 %collective-permute-start = (bf16[512,384]{1,0:T(8,128)(2,1)}, bf16[512,384]{1,0:T(8,128)(2,1)}, u32[]{:S(2)}, u32[]{:S(2)}) collective-permute-start(bf16[512,384]{1,0:T(8,128)(2,1)} %bitcast.97), channel_id=1, source_target_pairs={{0,1},{1,0},{2,3},{3,2},{4,5},{5,4},{6,7},{7,6},{8,9},{9,8},{10,11... | collective-permute-start | bytes 1179656 | tf_op jit(solution)/shard_map/ppermute | solution.py:98
  18.3 9.2 %copy-start.3 = (bf16[1,512,384]{2,1,0:T(8,128)(2,1)S(1)}, bf16[1,512,384]{2,1,0:T(8,128)(2,1)}, u32[]{:S(2)}) copy-start(bf16[1,512,384]{2,1,0:T(8,128)(2,1)} %param.12) | copy-start | bytes 1179652
  18.3 50.3 %collective-permute-start.6 = (bf16[384,768]{1,0:T(8,128)(2,1)S(1)}, bf16[384,768]{1,0:T(8,128)(2,1)S(1)}, u32[]{:S(2)}, u32[]{:S(2)}) collective-permute-start(bf16[384,768]{1,0:T(8,128)(2,1)S(1)} %copy-done.2), channel_id=1, source_target_pairs={{0,16},{8,24},{16,0},{24,8},{1,17},{9,25},{17,1},{25,9},{2,18},{10... | collective-permute-start | bytes 1769480 | tf_op jit(solution)/shard_map/ppermute | solution.py:98
  19.0 9.6 %collective-permute-start.8 = (bf16[1,192,512]{2,1,0:T(8,128)(2,1)}, bf16[1,192,512]{2,1,0:T(8,128)(2,1)S(1)}, u32[]{:S(2)}, u32[]{:S(2)}) collective-permute-start(bf16[1,192,512]{2,1,0:T(8,128)(2,1)} %get-tuple-element.30), channel_id=1, source_target_pairs={{0,4},{4,0},{1,5},{5,1},{2,6},{6,2},{3,7},{7,3},{8,12},{12,8},{9,1... | collective-permute-start | bytes 589832 | tf_op jit(solution)/shard_map/ppermute | solution.py:98
  26.1 14.7 %collective-permute-start.3 = (bf16[512,384]{1,0:T(8,128)(2,1)}, bf16[512,384]{1,0:T(8,128)(2,1)S(1)}, u32[]{:S(2)}, u32[]{:S(2)}) collective-permute-start(bf16[512,384]{1,0:T(8,128)(2,1)} %collective-permute-done), channel_id=1, source_target_pairs={{0,16},{8,24},{16,0},{24,8},{1,17},{9,25},{17,1},{25,9},{2,18},{10... | collective-permute-start | bytes 1179656 | tf_op jit(solution)/shard_map/ppermute | solution.py:98
  26.9 21.9 %collective-permute-start.15 = (bf16[2,192,512]{2,1,0:T(8,128)(2,1)S(1)}, bf16[2,192,512]{2,1,0:T(8,128)(2,1)S(1)}, u32[]{:S(2)}, u32[]{:S(2)}) collective-permute-start(bf16[2,192,512]{2,1,0:T(8,128)(2,1)S(1)} %collective-permute-done.2), channel_id=1, source_target_pairs={{0,4},{4,0},{1,5},{5,1},{2,6},{6,2},{3,7},{7,3},{8,12},{12,8},{9,1... | collective-permute-start | bytes 1179656 | tf_op jit(solution)/shard_map/ppermute | solution.py:98
  28.6 13.9 %collective-permute-start.9 = (bf16[2,192,512]{2,1,0:T(8,128)(2,1)S(1)}, bf16[2,192,512]{2,1,0:T(8,128)(2,1)S(1)}, u32[]{:S(2)}, u32[]{:S(2)}) collective-permute-start(bf16[2,192,512]{2,1,0:T(8,128)(2,1)S(1)} %get-tuple-element.29), channel_id=1, source_target_pairs={{0,1},{1,2},{2,3},{3,0},{4,5},{5,6},{6,7},{7,4},{8,9},{9,10},{10,1... | collective-permute-start | bytes 1179656 | tf_op jit(solution)/shard_map/ppermute | solution.py:101
  29.4 17.6 %copy-start.6 = (bf16[1,192,512]{2,1,0:T(8,128)(2,1)S(1)}, bf16[1,192,512]{2,1,0:T(8,128)(2,1)}, u32[]{:S(2)}) copy-start(bf16[1,192,512]{2,1,0:T(8,128)(2,1)} %get-tuple-element.30) | copy-start | bytes 589828
  29.4 17.6 %collective-permute-start.14 = (bf16[2,192,512]{2,1,0:T(8,128)(2,1)S(1)}, bf16[2,192,512]{2,1,0:T(8,128)(2,1)S(1)}, u32[]{:S(2)}, u32[]{:S(2)}) collective-permute-start(bf16[2,192,512]{2,1,0:T(8,128)(2,1)S(1)} %get-tuple-element.29), channel_id=1, source_target_pairs={{0,3},{1,0},{2,1},{3,2},{4,7},{5,4},{6,5},{7,6},{8,11},{9,8},{10,9... | collective-permute-start | bytes 1179656 | tf_op jit(solution)/shard_map/ppermute | solution.py:101
  40.9 20.1 %collective-permute-start.4 = (bf16[1024,384]{1,0:T(8,128)(2,1)S(1)}, bf16[1024,384]{1,0:T(8,128)(2,1)S(1)}, u32[]{:S(2)}, u32[]{:S(2)}) collective-permute-start(bf16[1024,384]{1,0:T(8,128)(2,1)S(1)} %pad_maximum_fusion), channel_id=1, source_target_pairs={{0,8},{8,0},{16,24},{24,16},{1,9},{9,1},{17,25},{25,17},{2,10},{10... | collective-permute-start | bytes 2359304 | tf_op jit(solution)/shard_map/ppermute | solution.py:98
  42.5 18.5 %collective-permute-start.5 = (bf16[1024,384]{1,0:T(8,128)(2,1)S(1)}, bf16[1024,384]{1,0:T(8,128)(2,1)S(1)}, u32[]{:S(2)}, u32[]{:S(2)}) collective-permute-start(bf16[1024,384]{1,0:T(8,128)(2,1)S(1)} %pad_maximum_fusion.1), channel_id=1, source_target_pairs={{0,8},{8,0},{16,24},{24,16},{1,9},{9,1},{17,25},{25,17},{2,10},{10... | collective-permute-start | bytes 2359304 | tf_op jit(solution)/shard_map/ppermute | solution.py:98
  47.0 10.9 %collective-permute-start.10 = (bf16[1,192,512]{2,1,0:T(8,128)(2,1)S(1)}, bf16[1,192,512]{2,1,0:T(8,128)(2,1)S(1)}, u32[]{:S(2)}, u32[]{:S(2)}) collective-permute-start(bf16[1,192,512]{2,1,0:T(8,128)(2,1)S(1)} %copy-done.6), channel_id=1, source_target_pairs={{0,2},{1,3},{2,0},{3,1},{4,6},{5,7},{6,4},{7,5},{8,10},{9,11},{10,... | collective-permute-start | bytes 589832 | tf_op jit(solution)/shard_map/ppermute | solution.py:101
  48.8 12.2 %copy-start.5 = (bf16[1,192,512]{2,1,0:T(8,128)(2,1)S(1)}, bf16[1,192,512]{2,1,0:T(8,128)(2,1)}, u32[]{:S(2)}) copy-start(bf16[1,192,512]{2,1,0:T(8,128)(2,1)} %get-tuple-element.31) | copy-start | bytes 589828
  48.9 12.1 %collective-permute-start.16 = (bf16[2,192,512]{2,1,0:T(8,128)(2,1)S(1)}, bf16[2,192,512]{2,1,0:T(8,128)(2,1)S(1)}, u32[]{:S(2)}, u32[]{:S(2)}) collective-permute-start(bf16[2,192,512]{2,1,0:T(8,128)(2,1)S(1)} %collective-permute-done.9), channel_id=1, source_target_pairs={{0,4},{4,0},{1,5},{5,1},{2,6},{6,2},{3,7},{7,3},{8,12},{12,8},{9,1... | collective-permute-start | bytes 1179656 | tf_op jit(solution)/shard_map/ppermute | solution.py:98
  57.9 14.9 %collective-permute-start.19 = (bf16[1,192,512]{2,1,0:T(8,128)(2,1)S(1)}, bf16[1,192,512]{2,1,0:T(8,128)(2,1)S(1)}, u32[]{:S(2)}, u32[]{:S(2)}) collective-permute-start(bf16[1,192,512]{2,1,0:T(8,128)(2,1)S(1)} %collective-permute-done.10), channel_id=1, source_target_pairs={{0,4},{4,0},{1,5},{5,1},{2,6},{6,2},{3,7},{7,3},{8,12},{12,8},{9,1... | collective-permute-start | bytes 589832 | tf_op jit(solution)/shard_map/ppermute | solution.py:98
  61.0 8.4 %collective-permute-start.11 = (bf16[1,192,512]{2,1,0:T(8,128)(2,1)S(1)}, bf16[1,192,512]{2,1,0:T(8,128)(2,1)S(1)}, u32[]{:S(2)}, u32[]{:S(2)}) collective-permute-start(bf16[1,192,512]{2,1,0:T(8,128)(2,1)S(1)} %copy-done.5), channel_id=1, source_target_pairs={{0,1},{1,2},{2,3},{3,0},{4,5},{5,6},{6,7},{7,4},{8,9},{9,10},{10,1... | collective-permute-start | bytes 589832 | tf_op jit(solution)/shard_map/ppermute | solution.py:101
  62.7 8.7 %collective-permute-start.18 = (bf16[1,192,512]{2,1,0:T(8,128)(2,1)S(1)}, bf16[1,192,512]{2,1,0:T(8,128)(2,1)S(1)}, u32[]{:S(2)}, u32[]{:S(2)}) collective-permute-start(bf16[1,192,512]{2,1,0:T(8,128)(2,1)S(1)} %copy-done.5), channel_id=1, source_target_pairs={{0,3},{1,0},{2,1},{3,2},{4,7},{5,4},{6,5},{7,6},{8,11},{9,8},{10,9... | collective-permute-start | bytes 589832 | tf_op jit(solution)/shard_map/ppermute | solution.py:101
  67.0 10.0 %collective-permute-start.17 = (bf16[2,192,512]{2,1,0:T(8,128)(2,1)S(1)}, bf16[2,192,512]{2,1,0:T(8,128)(2,1)S(1)}, u32[]{:S(2)}, u32[]{:S(2)}) collective-permute-start(bf16[2,192,512]{2,1,0:T(8,128)(2,1)S(1)} %collective-permute-done.14), channel_id=1, source_target_pairs={{0,4},{4,0},{1,5},{5,1},{2,6},{6,2},{3,7},{7,3},{8,12},{12,8},{9,1... | collective-permute-start | bytes 1179656 | tf_op jit(solution)/shard_map/ppermute | solution.py:98
  69.5 7.6 %collective-permute-start.12 = (bf16[384,768]{1,0:T(8,128)(2,1)S(1)}, bf16[384,768]{1,0:T(8,128)(2,1)S(1)}, u32[]{:S(2)}, u32[]{:S(2)}) collective-permute-start(bf16[384,768]{1,0:T(8,128)(2,1)S(1)} %copy-done.2), channel_id=1, source_target_pairs={{0,8},{8,0},{16,24},{24,16},{1,9},{9,1},{17,25},{25,17},{2,10},{10... | collective-permute-start | bytes 1769480 | tf_op jit(solution)/shard_map/ppermute | solution.py:98
  69.5 7.7 %collective-permute-start.13 = (bf16[384,768]{1,0:T(8,128)(2,1)S(1)}, bf16[384,768]{1,0:T(8,128)(2,1)S(1)}, u32[]{:S(2)}, u32[]{:S(2)}) collective-permute-start(bf16[384,768]{1,0:T(8,128)(2,1)S(1)} %collective-permute-done.6), channel_id=1, source_target_pairs={{0,8},{8,0},{16,24},{24,16},{1,9},{9,1},{17,25},{25,17},{2,10},{10... | collective-permute-start | bytes 1769480 | tf_op jit(solution)/shard_map/ppermute | solution.py:98
  71.4 11.5 %collective-permute-start.20 = (bf16[1,192,512]{2,1,0:T(8,128)(2,1)S(1)}, bf16[1,192,512]{2,1,0:T(8,128)(2,1)S(1)}, u32[]{:S(2)}, u32[]{:S(2)}) collective-permute-start(bf16[1,192,512]{2,1,0:T(8,128)(2,1)S(1)} %collective-permute-done.11), channel_id=1, source_target_pairs={{0,4},{4,0},{1,5},{5,1},{2,6},{6,2},{3,7},{7,3},{8,12},{12,8},{9,1... | collective-permute-start | bytes 589832 | tf_op jit(solution)/shard_map/ppermute | solution.py:98
  72.8 10.9 %collective-permute-start.21 = (bf16[1,192,512]{2,1,0:T(8,128)(2,1)S(1)}, bf16[1,192,512]{2,1,0:T(8,128)(2,1)S(1)}, u32[]{:S(2)}, u32[]{:S(2)}) collective-permute-start(bf16[1,192,512]{2,1,0:T(8,128)(2,1)S(1)} %collective-permute-done.18), channel_id=1, source_target_pairs={{0,4},{4,0},{1,5},{5,1},{2,6},{6,2},{3,7},{7,3},{8,12},{12,8},{9,1... | collective-permute-start | bytes 589832 | tf_op jit(solution)/shard_map/ppermute | solution.py:98
  81.5 2.6 %copy-start.4 = (bf16[1024,512]{1,0:T(8,128)(2,1)}, bf16[1024,512]{1,0:T(8,128)(2,1)S(1)}, u32[]{:S(2)}) copy-start(bf16[1024,512]{1,0:T(8,128)(2,1)S(1)} %multiply_convert_fusion) | copy-start | bytes 3145732
  84.8 2.4 %collective-permute-start.22 = (bf16[2,2,128,768]{3,2,1,0:T(8,128)(2,1)S(1)}, bf16[2,2,128,768]{3,2,1,0:T(8,128)(2,1)S(1)}, u32[]{:S(2)}, u32[]{:S(2)}) collective-permute-start(bf16[2,2,128,768]{3,2,1,0:T(8,128)(2,1)S(1)} %convolution_convert_fusion), channel_id=1, source_target_pairs={{0,8},{8,0},{16,24},{24,16},{1,9},{9,1},{17,25},{25,17},{2,10},{10... | collective-permute-start | bytes 2359304 | tf_op jit(solution)/shard_map/ppermute | solution.py:98
  87.3 12.7 %copy-start.7 = (f32[768]{0:T(1024)S(1)}, f32[768]{0:T(1024)}, u32[]{:S(2)}) copy-start(f32[768]{0:T(1024)} %param.18) | copy-start | bytes 9220
  87.3 26.2 %copy-start = (bf16[3,768,192]{1,2,0:T(8,128)(2,1)S(1)}, bf16[3,768,192]{1,2,0:T(8,128)(2,1)}, u32[]{:S(2)}) copy-start(bf16[3,768,192]{1,2,0:T(8,128)(2,1)} %param.19) | copy-start | bytes 2654212
  87.4 8.8 %collective-permute-start.25 = (bf16[128,768]{1,0:T(8,128)(2,1)S(1)}, bf16[128,768]{1,0:T(8,128)(2,1)S(1)}, u32[]{:S(2)}, u32[]{:S(2)}) collective-permute-start(bf16[128,768]{1,0:T(8,128)(2,1)S(1)} %get-tuple-element.56), channel_id=1, source_target_pairs={{0,17},{1,16},{2,19},{3,18},{8,25},{9,24},{10,27},{11,26},{16,1},{... | collective-permute-start | bytes 589832 | tf_op jit(solution)/shard_map/ppermute | solution.py:98
  88.4 10.3 %collective-permute-start.24 = (bf16[128,768]{1,0:T(8,128)(2,1)S(1)}, bf16[128,768]{1,0:T(8,128)(2,1)S(1)}, u32[]{:S(2)}, u32[]{:S(2)}) collective-permute-start(bf16[128,768]{1,0:T(8,128)(2,1)S(1)} %fusion.26), channel_id=1, source_target_pairs={{0,1},{1,0},{2,3},{3,2},{4,5},{5,4},{6,7},{7,6},{8,9},{9,8},{10,11... | collective-permute-start | bytes 589832 | tf_op jit(solution)/shard_map/ppermute | solution.py:98
  89.6 9.9 %collective-permute-start.23 = (bf16[128,768]{1,0:T(8,128)(2,1)S(1)}, bf16[128,768]{1,0:T(8,128)(2,1)S(1)}, u32[]{:S(2)}, u32[]{:S(2)}) collective-permute-start(bf16[128,768]{1,0:T(8,128)(2,1)S(1)} %get-tuple-element.55), channel_id=1, source_target_pairs={{0,16},{8,24},{16,0},{24,8},{1,17},{9,25},{17,1},{25,9},{2,18},{10... | collective-permute-start | bytes 589832 | tf_op jit(solution)/shard_map/ppermute | solution.py:98
  100.1 7.8 %collective-permute-start.26 = (bf16[128,768]{1,0:T(8,128)(2,1)S(1)}, bf16[128,768]{1,0:T(8,128)(2,1)S(1)}, u32[]{:S(2)}, u32[]{:S(2)}) collective-permute-start(bf16[128,768]{1,0:T(8,128)(2,1)S(1)} %multiply_convert_fusion.1.refs_0_), channel_id=1, source_target_pairs={{0,16},{8,24},{16,0},{24,8},{1,17},{9,25},{17,1},{25,9},{2,18},{10... | collective-permute-start | bytes 589832 | tf_op jit(solution)/shard_map/ppermute | solution.py:98
  100.8 9.8 %collective-permute-start.29 = (bf16[128,768]{1,0:T(8,128)(2,1)S(1)}, bf16[128,768]{1,0:T(8,128)(2,1)S(1)}, u32[]{:S(2)}, u32[]{:S(2)}) collective-permute-start(bf16[128,768]{1,0:T(8,128)(2,1)S(1)} %multiply_convert_fusion.1.refs_0_), channel_id=1, source_target_pairs={{0,4},{4,0},{1,5},{5,1},{2,6},{6,2},{3,7},{7,3},{8,12},{12,8},{9,1... | collective-permute-start | bytes 589832 | tf_op jit(solution)/shard_map/ppermute | solution.py:98
  102.3 9.9 %collective-permute-start.30 = (bf16[128,768]{1,0:T(8,128)(2,1)S(1)}, bf16[128,768]{1,0:T(8,128)(2,1)S(1)}, u32[]{:S(2)}, u32[]{:S(2)}) collective-permute-start(bf16[128,768]{1,0:T(8,128)(2,1)S(1)} %multiply_convert_fusion.1.refs_0_), channel_id=1, source_target_pairs={{0,20},{4,16},{8,28},{12,24},{16,4},{20,0},{24,12},{28,8},{1,21},{... | collective-permute-start | bytes 589832 | tf_op jit(solution)/shard_map/ppermute | solution.py:98
  103.7 8.5 %collective-permute-start.27 = (bf16[128,768]{1,0:T(8,128)(2,1)S(1)}, bf16[128,768]{1,0:T(8,128)(2,1)S(1)}, u32[]{:S(2)}, u32[]{:S(2)}) collective-permute-start(bf16[128,768]{1,0:T(8,128)(2,1)S(1)} %multiply_convert_fusion.1.refs_0_), channel_id=1, source_target_pairs={{0,8},{8,0},{16,24},{24,16},{1,9},{9,1},{17,25},{25,17},{2,10},{10... | collective-permute-start | bytes 589832 | tf_op jit(solution)/shard_map/ppermute | solution.py:98
  107.9 4.2 %collective-permute-start.28 = (bf16[128,768]{1,0:T(8,128)(2,1)S(1)}, bf16[128,768]{1,0:T(8,128)(2,1)S(1)}, u32[]{:S(2)}, u32[]{:S(2)}) collective-permute-start(bf16[128,768]{1,0:T(8,128)(2,1)S(1)} %collective-permute-done.26.refs_1_), channel_id=1, source_target_pairs={{0,8},{8,0},{16,24},{24,16},{1,9},{9,1},{17,25},{25,17},{2,10},{10... | collective-permute-start | bytes 589832 | tf_op jit(solution)/shard_map/ppermute | solution.py:98
  110.5 1.6 %collective-permute-start.31 = (bf16[128,768]{1,0:T(8,128)(2,1)S(1)}, bf16[128,768]{1,0:T(8,128)(2,1)S(1)}, u32[]{:S(2)}, u32[]{:S(2)}) collective-permute-start(bf16[128,768]{1,0:T(8,128)(2,1)S(1)} %collective-permute-done.29.refs_4_), channel_id=1, source_target_pairs={{0,8},{8,0},{16,24},{24,16},{1,9},{9,1},{17,25},{25,17},{2,10},{10... | collective-permute-start | bytes 589832 | tf_op jit(solution)/shard_map/ppermute | solution.py:98
  112.1 1.4 %collective-permute-start.32 = (bf16[128,768]{1,0:T(8,128)(2,1)S(1)}, bf16[128,768]{1,0:T(8,128)(2,1)S(1)}, u32[]{:S(2)}, u32[]{:S(2)}) collective-permute-start(bf16[128,768]{1,0:T(8,128)(2,1)S(1)} %collective-permute-done.30.refs_5_), channel_id=1, source_target_pairs={{0,8},{8,0},{16,24},{24,16},{1,9},{9,1},{17,25},{25,17},{2,10},{10... | collective-permute-start | bytes 589832 | tf_op jit(solution)/shard_map/ppermute | solution.py:98
  119.2 1.8 %collective-permute-start.33 = (bf16[2,192,512]{2,1,0:T(8,128)(2,1)S(1)}, bf16[2,192,512]{2,1,0:T(8,128)(2,1)S(1)}, u32[]{:S(2)}, u32[]{:S(2)}) collective-permute-start(bf16[2,192,512]{2,1,0:T(8,128)(2,1)S(1)} %get-tuple-element.42), channel_id=1, source_target_pairs={{0,8},{8,0},{16,24},{24,16},{1,9},{9,1},{17,25},{25,17},{2,10},{10... | collective-permute-start | bytes 1179656 | tf_op jit(solution)/shard_map/ppermute | solution.py:98
  121.1 7.0 %collective-permute-start.34 = (bf16[192,512]{1,0:T(8,128)(2,1)S(1)}, bf16[192,512]{1,0:T(8,128)(2,1)S(1)}, u32[]{:S(2)}, u32[]{:S(2)}) collective-permute-start(bf16[192,512]{1,0:T(8,128)(2,1)S(1)} %fusion.28), channel_id=1, source_target_pairs={{0,16},{8,24},{16,0},{24,8},{1,17},{9,25},{17,1},{25,9},{2,18},{10... | collective-permute-start | bytes 589832 | tf_op jit(solution)/shard_map/ppermute | solution.py:98

commit v14 on v13

--- a/solution.py
+++ b/solution.py
@@ -206,21 +206,23 @@
                 g[0, k] = rotate(after(pair_other, g[0, 2], g[1, 0], d[1, 0]), k)
             g[1, 2] = flip(g[0, 2], seq=1)
             across = after(jnp.concatenate([mine_x, beside_x], axis=0), g[0, 2])
-            both = after(jnp.concatenate([mine, beside], axis=0), across)
-            both_c, across_c = flip(both, section=1), flip(across, section=1)
-            d[0, 2] = rotate(after(down_same, g[0, 1], across), 2)
+            both = after(jnp.concatenate([mine, beside], axis=0), across, g[1, 2], proj_x)
+            both_c = flip(both, section=1)
+            across_c = flip(after(across, g[1, 2], proj_x), section=1)
+            far = rotate(after(down_same, g[0, 1], across), 2)
             rows = jnp.concatenate([both, both_c, across, across_c], axis=1)
             normed = layer_norm(rows.astype(jnp.float32), gain).astype(jnp.bfloat16)
-            g[1, 1] = flip(g[0, 1], seq=1)
-            g[1, 3] = flip(after(g[0, 3], both_c, across_c), seq=1)
+            g[1, 1] = after(flip(g[0, 1], seq=1), normed)
+            g[1, 3] = flip(after(g[0, 3], normed), seq=1)
             gate_up = place_rows(g)
+            d[0, 2] = after(far, normed)
             for k in (1, 3):
-                d[0, k] = rotate(after(down_other, d[0, 2], both_c, across_c, code, out_w), k)
+                d[0, k] = rotate(after(down_other, d[0, 2], code, out_w), k)
             proj_c = flip(after(w_proj, proj_x, d[0, 1]), section=1)
             proj_xc = flip(after(proj_x, d[0, 1]), section=1)
             proj = jnp.concatenate([w_proj, proj_c, proj_x, proj_xc], axis=0)
             d[1, 2] = flip(d[0, 2], seq=1)
-            d[1, 1], d[1, 3] = flip(after(d[0, 1], normed), seq=1), flip(d[0, 3], seq=1)
+            d[1, 1], d[1, 3] = flip(d[0, 1], seq=1), flip(d[0, 3], seq=1)
         else:
             gate_up = gather_rows(pair_same, pair_other, seq_at, dp_at)
             down_all = gather_rows(down_same, down_other, seq_at, dp_at)[0]

time: 129 us -> 144 us (1.12)
  starting transfers between devices: 33.6 us -> 39.9 us
  local copies, waits for them, and re-layouts: 4.43 us -> 10.5 us
    ppermute x29, starting transfers between devices: 20 us -> 28.2 us  [flip(): return lax.ppermute(x, names if len(names) > 1 else names[0], pairs)]
    dynamic_update_slice x14, local copies, waits for them, and re-layouts: 0.35 us -> 3.35 us  [place_rows(): whole = lax.dynamic_update_slice(whole, block, (0, row_of(y, k, rows), 0))]
    ppermute x29, waiting for transfers between devices: 43.7 us -> 46.4 us  [flip(): return lax.ppermute(x, names if len(names) > 1 else names[0], pairs)]
    ppermute x6, waiting for transfers between devices: 20.3 us -> 17.7 us  [rotate(): return lax.ppermute(x, 'dp', [(i, (i + k) % n_dp) for i in range(n_dp)])]
    unnamed x23 -> x27, local copies, waits for them, and re-layouts: 1.69 us -> 3.77 us
    ppermute x6, starting transfers between devices: 13.7 us -> 11.7 us  [rotate(): return lax.ppermute(x, 'dp', [(i, (i + k) % n_dp) for i in range(n_dp)])]
  transfers between devices with their start and end apart: 35 -> 35, of which waited for: 21 -> 19; matrix products, arithmetic and copies ran while one was open for 16% -> 18% of each run, Pallas kernels for 0% -> 0%
where the time goes in v14:
time: 144 us; the launch traced here: 143 us
  waiting for transfers between devices  64.1 us (45%)
  starting transfers between devices  39.9 us (28%)
  other arithmetic  12.3 us (9%)
  local copies, waits for them, and re-layouts  10.5 us (7%)
  matrix products  9.92 us (7%)
  Pallas kernels  5.35 us (4%)
    ppermute x29, waiting for transfers between devices, flip(): return lax.ppermute(x, names if len(names) > 1 else names[0], pairs)  46.4 us
    ppermute x29, starting transfers between devices, flip(): return lax.ppermute(x, names if len(names) > 1 else names[0], pairs)  28.2 us
    ppermute x6, waiting for transfers between devices, rotate(): return lax.ppermute(x, 'dp', [(i, (i + k) % n_dp) for i in range(n_dp)])  17.7 us
    ppermute x6, starting transfers between devices, rotate(): return lax.ppermute(x, 'dp', [(i, (i + k) % n_dp) for i in range(n_dp)])  11.7 us
    pallas_call x1, Pallas kernels, per_device(): pl.pallas_call(lambda *refs: attend_kernel(*refs, heads=local_heads, mask...  5.35 us
    unnamed x27, local copies, waits for them, and re-layouts  3.77 us
    dot_general x2, matrix products, project(): lax.dot_general(x, folded, (((x.ndim - 1,), (1,)), ((), ())), preferred_e...  3.38 us
    dynamic_update_slice x14, local copies, waits for them, and re-layouts, place_rows(): whole = lax.dynamic_update_slice(whole, block, (0, row_of(y, k, rows), 0))  3.35 us
  transfers between devices with their start and end apart: 35, of which 19 were waited for; matrix products, arithmetic and copies ran while one was open for 18% of the time, Pallas kernels for 0%

profile of v14, /device:TPU:0, one launch (start us, length us, event | category | flops | bytes accessed | tf_op | source)
XLA Modules:
  0.0 143.2 jit_solution(18035618425556622717)
XLA Ops:
  0.0 2.1 %fusion.14 = (bf16[2,192,512]{2,1,0:T(8,128)(2,1)S(1)}, bf16[2,192,512]{2,1,0:T(8,128)(2,1)}) fusion(s32[]{:T(128)S(6)} %select_n.236, bf16[1,192,1024]{2,1,0:T(8,128)(2,1)} %bitcast.94, bf16[1,192,1024]{2,1,0:T(8,128)(2,1)} %bitcast.95, s32[]{:T(128)S(6)} %select_n.238), kind=kLoop, calls=%fused_computation.30 | loop fusion | flops 1572864 | bytes 1572872 | tf_op jit(solution)/shard_map/stack | solution.py:163
  2.1 4.0 %collective-permute-start.2 = (bf16[2,192,512]{2,1,0:T(8,128)(2,1)S(1)}, bf16[2,192,512]{2,1,0:T(8,128)(2,1)}, u32[]{:S(2)}, u32[]{:S(2)}) collective-permute-start(bf16[2,192,512]{2,1,0:T(8,128)(2,1)S(1)} %get-tuple-element.57), channel_id=1, source_target_pairs={{0,2},{1,3},{2,0},{3,1},{4,6},{5,7},{6,4},{7,5},{8,10},{9,11},{10,... | collective-permute-start | bytes 1179656 | tf_op jit(solution)/shard_map/ppermute | solution.py:101
  6.1 1.5 %collective-permute-start.8 = (bf16[2,192,512]{2,1,0:T(8,128)(2,1)S(1)}, bf16[2,192,512]{2,1,0:T(8,128)(2,1)}, u32[]{:S(2)}, u32[]{:S(2)}) collective-permute-start(bf16[2,192,512]{2,1,0:T(8,128)(2,1)S(1)} %get-tuple-element.57), channel_id=1, source_target_pairs={{0,4},{4,0},{1,5},{5,1},{2,6},{6,2},{3,7},{7,3},{8,12},{12,8},{9,1... | collective-permute-start | bytes 1179656 | tf_op jit(solution)/shard_map/ppermute | solution.py:98
  7.6 1.5 %collective-permute-start.1 = (bf16[512,384]{1,0:T(8,128)(2,1)}, bf16[512,384]{1,0:T(8,128)(2,1)S(1)}, u32[]{:S(2)}, u32[]{:S(2)}) collective-permute-start(bf16[512,384]{1,0:T(8,128)(2,1)} %bitcast.96), channel_id=1, source_target_pairs={{0,16},{8,24},{16,0},{24,8},{1,17},{9,25},{17,1},{25,9},{2,18},{10... | collective-permute-start | bytes 1179656 | tf_op jit(solution)/shard_map/ppermute | solution.py:98
  9.1 1.6 %collective-permute-start = (bf16[512,384]{1,0:T(8,128)(2,1)}, bf16[512,384]{1,0:T(8,128)(2,1)}, u32[]{:S(2)}, u32[]{:S(2)}) collective-permute-start(bf16[512,384]{1,0:T(8,128)(2,1)} %bitcast.97), channel_id=1, source_target_pairs={{0,1},{1,0},{2,3},{3,2},{4,5},{5,4},{6,7},{7,6},{8,9},{9,8},{10,11... | collective-permute-start | bytes 1179656 | tf_op jit(solution)/shard_map/ppermute | solution.py:98
  14.7 1.8 %dynamic-slice_bitcast_fusion.2 = (bf16[1,192,512]{2,1,0:T(8,128)(2,1)}, bf16[1,192,512]{2,1,0:T(8,128)(2,1)}) fusion(bf16[1024,192]{0,1:T(8,128)(2,1)} %param.16, s32[]{:T(128)S(6)} %select_n.236, s32[]{:T(128)S(6)} %select_n.238), kind=kLoop, calls=%fused_computation.62 | loop fusion | bytes 786440 | tf_op jit(solution)/shard_map/dynamic_slice | solution.py:161
  16.5 1.1 constant_dynamic-update-slice_fusion.8
  18.3 5.5 %collective-permute-done.2 = bf16[2,192,512]{2,1,0:T(8,128)(2,1)} collective-permute-done((bf16[2,192,512]{2,1,0:T(8,128)(2,1)S(1)}, bf16[2,192,512]{2,1,0:T(8,128)(2,1)}, u32[]{:S(2)}, u32[]{:S(2)}) %collective-permute-start.2) | collective-permute-done | bytes 393248 | tf_op jit(solution)/shard_map/ppermute | solution.py:101
  23.9 2.9 %collective-permute-done = bf16[512,384]{1,0:T(8,128)(2,1)} collective-permute-done((bf16[512,384]{1,0:T(8,128)(2,1)}, bf16[512,384]{1,0:T(8,128)(2,1)}, u32[]{:S(2)}, u32[]{:S(2)}) %collective-permute-start) | collective-permute-done | bytes 393248 | tf_op jit(solution)/shard_map/ppermute | solution.py:98
  27.3 1.4 %collective-permute-start.5 = (bf16[384,768]{1,0:T(8,128)(2,1)}, bf16[384,768]{1,0:T(8,128)(2,1)}, u32[]{:S(2)}, u32[]{:S(2)}) collective-permute-start(bf16[384,768]{1,0:T(8,128)(2,1)} %param.17), channel_id=1, source_target_pairs={{0,16},{8,24},{16,0},{24,8},{1,17},{9,25},{17,1},{25,9},{2,18},{10... | collective-permute-start | bytes 1769480 | tf_op jit(solution)/shard_map/ppermute | solution.py:98
  30.1 1.5 %collective-permute-start.9 = (bf16[1,192,512]{2,1,0:T(8,128)(2,1)}, bf16[1,192,512]{2,1,0:T(8,128)(2,1)S(1)}, u32[]{:S(2)}, u32[]{:S(2)}) collective-permute-start(bf16[1,192,512]{2,1,0:T(8,128)(2,1)} %get-tuple-element.33), channel_id=1, source_target_pairs={{0,4},{4,0},{1,5},{5,1},{2,6},{6,2},{3,7},{7,3},{8,12},{12,8},{9,1... | collective-permute-start | bytes 589832 | tf_op jit(solution)/shard_map/ppermute | solution.py:98
  31.6 1.2 pad_maximum_fusion
  32.9 9.0 %collective-permute-done.9 = bf16[1,192,512]{2,1,0:T(8,128)(2,1)S(1)} collective-permute-done((bf16[1,192,512]{2,1,0:T(8,128)(2,1)}, bf16[1,192,512]{2,1,0:T(8,128)(2,1)S(1)}, u32[]{:S(2)}, u32[]{:S(2)}) %collective-permute-start.9) | collective-permute-done | bytes 196640 | tf_op jit(solution)/shard_map/ppermute | solution.py:98
  41.8 3.8 %collective-permute-start.15 = (bf16[2,192,512]{2,1,0:T(8,128)(2,1)}, bf16[2,192,512]{2,1,0:T(8,128)(2,1)S(1)}, u32[]{:S(2)}, u32[]{:S(2)}) collective-permute-start(bf16[2,192,512]{2,1,0:T(8,128)(2,1)} %get-tuple-element.32), channel_id=1, source_target_pairs={{0,3},{1,0},{2,1},{3,2},{4,7},{5,4},{6,5},{7,6},{8,11},{9,8},{10,9... | collective-permute-start | bytes 1179656 | tf_op jit(solution)/shard_map/ppermute | solution.py:101
  45.6 1.2 pad_maximum_fusion.1
  46.9 1.9 %collective-permute-done.5 = bf16[384,768]{1,0:T(8,128)(2,1)} collective-permute-done((bf16[384,768]{1,0:T(8,128)(2,1)}, bf16[384,768]{1,0:T(8,128)(2,1)}, u32[]{:S(2)}, u32[]{:S(2)}) %collective-permute-start.5) | collective-permute-done | bytes 589856 | tf_op jit(solution)/shard_map/ppermute | solution.py:98
  49.0 1.0 constant_dynamic-update-slice_fusion.17
  50.6 1.0 constant_dynamic-update-slice_fusion.16
  51.6 4.3 %collective-permute-done.10 = bf16[2,192,512]{2,1,0:T(8,128)(2,1)S(1)} collective-permute-done((bf16[2,192,512]{2,1,0:T(8,128)(2,1)}, bf16[2,192,512]{2,1,0:T(8,128)(2,1)S(1)}, u32[]{:S(2)}, u32[]{:S(2)}) %collective-permute-start.10) | collective-permute-done | bytes 393248 | tf_op jit(solution)/shard_map/ppermute | solution.py:101
  55.9 3.5 %collective-permute-start.16 = (bf16[2,192,512]{2,1,0:T(8,128)(2,1)S(1)}, bf16[2,192,512]{2,1,0:T(8,128)(2,1)S(1)}, u32[]{:S(2)}, u32[]{:S(2)}) collective-permute-start(bf16[2,192,512]{2,1,0:T(8,128)(2,1)S(1)} %collective-permute-done.10), channel_id=1, source_target_pairs={{0,4},{4,0},{1,5},{5,1},{2,6},{6,2},{3,7},{7,3},{8,12},{12,8},{9,1... | collective-permute-start | bytes 1179656 | tf_op jit(solution)/shard_map/ppermute | solution.py:98
  59.5 1.0 constant_dynamic-update-slice_fusion.13
  61.6 1.0 fusion.2
  62.6 1.0 fusion.4
  63.7 4.2 %collective-permute-done.11 = bf16[1,192,512]{2,1,0:T(8,128)(2,1)S(1)} collective-permute-done((bf16[1,192,512]{2,1,0:T(8,128)(2,1)S(1)}, bf16[1,192,512]{2,1,0:T(8,128)(2,1)S(1)}, u32[]{:S(2)}, u32[]{:S(2)}) %collective-permute-start.11) | collective-permute-done | bytes 196640 | tf_op jit(solution)/shard_map/ppermute | solution.py:101
  67.9 2.1 %collective-permute-start.12 = (bf16[1,192,512]{2,1,0:T(8,128)(2,1)S(1)}, bf16[1,192,512]{2,1,0:T(8,128)(2,1)S(1)}, u32[]{:S(2)}, u32[]{:S(2)}) collective-permute-start(bf16[1,192,512]{2,1,0:T(8,128)(2,1)S(1)} %copy-done.6), channel_id=1, source_target_pairs={{0,1},{1,2},{2,3},{3,0},{4,5},{5,6},{6,7},{7,4},{8,9},{9,10},{10,1... | collective-permute-start | bytes 589832 | tf_op jit(solution)/shard_map/ppermute | solution.py:101
  70.0 1.8 %collective-permute-start.18 = (bf16[1,192,512]{2,1,0:T(8,128)(2,1)S(1)}, bf16[1,192,512]{2,1,0:T(8,128)(2,1)S(1)}, u32[]{:S(2)}, u32[]{:S(2)}) collective-permute-start(bf16[1,192,512]{2,1,0:T(8,128)(2,1)S(1)} %copy-done.6), channel_id=1, source_target_pairs={{0,3},{1,0},{2,1},{3,2},{4,7},{5,4},{6,5},{7,6},{8,11},{9,8},{10,9... | collective-permute-start | bytes 589832 | tf_op jit(solution)/shard_map/ppermute | solution.py:101
  71.8 2.2 %collective-permute-start.19 = (bf16[1,192,512]{2,1,0:T(8,128)(2,1)S(1)}, bf16[1,192,512]{2,1,0:T(8,128)(2,1)S(1)}, u32[]{:S(2)}, u32[]{:S(2)}) collective-permute-start(bf16[1,192,512]{2,1,0:T(8,128)(2,1)S(1)} %collective-permute-done.11), channel_id=1, source_target_pairs={{0,4},{4,0},{1,5},{5,1},{2,6},{6,2},{3,7},{7,3},{8,12},{12,8},{9,1... | collective-permute-start | bytes 589832 | tf_op jit(solution)/shard_map/ppermute | solution.py:98
  74.2 3.4 %collective-permute-done.12 = bf16[1,192,512]{2,1,0:T(8,128)(2,1)S(1)} collective-permute-done((bf16[1,192,512]{2,1,0:T(8,128)(2,1)S(1)}, bf16[1,192,512]{2,1,0:T(8,128)(2,1)S(1)}, u32[]{:S(2)}, u32[]{:S(2)}) %collective-permute-start.12) | collective-permute-done | bytes 196640 | tf_op jit(solution)/shard_map/ppermute | solution.py:101
  78.5 2.7 %collective-permute-start.20 = (bf16[1,192,512]{2,1,0:T(8,128)(2,1)S(1)}, bf16[1,192,512]{2,1,0:T(8,128)(2,1)S(1)}, u32[]{:S(2)}, u32[]{:S(2)}) collective-permute-start(bf16[1,192,512]{2,1,0:T(8,128)(2,1)S(1)} %collective-permute-done.12), channel_id=1, source_target_pairs={{0,4},{4,0},{1,5},{5,1},{2,6},{6,2},{3,7},{7,3},{8,12},{12,8},{9,1... | collective-permute-start | bytes 589832 | tf_op jit(solution)/shard_map/ppermute | solution.py:98
  81.8 6.3 %collective-permute-done.17 = bf16[2,192,512]{2,1,0:T(8,128)(2,1)S(1)} collective-permute-done((bf16[2,192,512]{2,1,0:T(8,128)(2,1)S(1)}, bf16[2,192,512]{2,1,0:T(8,128)(2,1)S(1)}, u32[]{:S(2)}, u32[]{:S(2)}) %collective-permute-start.17) | collective-permute-done | bytes 393248 | tf_op jit(solution)/shard_map/ppermute | solution.py:98
  88.2 1.1 constant_dynamic-update-slice_fusion.6
  89.9 1.8 %fusion.6 = f32[1024,512]{1,0:T(8,128)S(1)} fusion(bf16[1024,1536]{1,0:T(8,128)(2,1)S(1)} %fusion.4, bf16[2,1536,512]{2,1,0:T(8,128)(2,1)S(1)} %constant_dynamic-update-slice_fusion.11), kind=kOutput, calls=%fused_computation.11 | convolution fusion | flops 1610612736 | bytes 6815744 | tf_op jit(solution)/shard_map/dot_general | solution.py:240
  91.7 2.0 %multiply_convert_fusion = bf16[1024,512]{1,0:T(8,128)(2,1)S(1)} fusion(f32[1024,512]{1,0:T(8,128)S(1)} %fusion.6, bf16[1024,1536]{1,0:T(8,128)(2,1)S(1)} %fusion.4, bf16[2,1536,512]{2,1,0:T(8,128)(2,1)S(1)} %constant_dynamic-update-slice_fusion.11), kind=kOutput, calls=%fused_computation.7 | convolution fusion | flops 1613758464 | bytes 7864320 | tf_op jit(solution)/shard_map/dot_general | solution.py:241
  93.7 1.4 fusion.52
  96.9 1.5 %convolution_convert_fusion = bf16[2,2,128,768]{3,2,1,0:T(8,128)(2,1)} fusion(bf16[768,512,1,1]{1,0,3,2:T(8,128)(2,1)S(1)} %fusion.7, bf16[2,2,2,128,512]{4,3,2,1,0:T(8,128)(2,1)S(1)} %bitcast.99, s32[]{:T(128)S(6)} %select_n.279), kind=kOutput, calls=%fused_computation.14 | convolution fusion | flops 403046400 | bytes 2097156 | tf_op jit(solution)/shard_map/dot_general | solution.py:263
  98.4 1.9 %fusion.9 = f32[2,2,128,768]{3,2,1,0:T(8,128)S(1)} fusion(bf16[768,512,1,1]{1,0,3,2:T(8,128)(2,1)} %copy-done.1, bf16[2,2,2,128,512]{4,3,2,1,0:T(8,128)(2,1)} %bitcast.100, s32[]{:T(128)S(6)} %select_n.278), kind=kOutput, calls=%fused_computation.25 | convolution fusion | flops 402653184 | bytes 2883588 | tf_op jit(solution)/shard_map/dot_general | solution.py:263
  101.2 2.4 %collective-permute-start.23 = (bf16[128,768]{1,0:T(8,128)(2,1)S(1)}, bf16[128,768]{1,0:T(8,128)(2,1)S(1)}, u32[]{:S(2)}, u32[]{:S(2)}) collective-permute-start(bf16[128,768]{1,0:T(8,128)(2,1)S(1)} %get-tuple-element.59), channel_id=1, source_target_pairs={{0,16},{8,24},{16,0},{24,8},{1,17},{9,25},{17,1},{25,9},{2,18},{10... | collective-permute-start | bytes 589832 | tf_op jit(solution)/shard_map/ppermute | solution.py:98
  103.6 1.6 %collective-permute-start.24 = (bf16[128,768]{1,0:T(8,128)(2,1)S(1)}, bf16[128,768]{1,0:T(8,128)(2,1)S(1)}, u32[]{:S(2)}, u32[]{:S(2)}) collective-permute-start(bf16[128,768]{1,0:T(8,128)(2,1)S(1)} %fusion.26), channel_id=1, source_target_pairs={{0,1},{1,0},{2,3},{3,2},{4,5},{5,4},{6,7},{7,6},{8,9},{9,8},{10,11... | collective-permute-start | bytes 589832 | tf_op jit(solution)/shard_map/ppermute | solution.py:98
  105.2 7.8 %collective-permute-done.23 = bf16[128,768]{1,0:T(8,128)(2,1)S(1)} collective-permute-done((bf16[128,768]{1,0:T(8,128)(2,1)S(1)}, bf16[128,768]{1,0:T(8,128)(2,1)S(1)}, u32[]{:S(2)}, u32[]{:S(2)}) %collective-permute-start.23) | collective-permute-done | bytes 196640 | tf_op jit(solution)/shard_map/ppermute | solution.py:98
  113.0 1.3 collective-permute-done.24
  114.8 1.7 %collective-permute-start.26 = (bf16[128,768]{1,0:T(8,128)(2,1)S(1)}, bf16[128,768]{1,0:T(8,128)(2,1)S(1)}, u32[]{:S(2)}, u32[]{:S(2)}) collective-permute-start(bf16[128,768]{1,0:T(8,128)(2,1)S(1)} %multiply_convert_fusion.1.refs_0_), channel_id=1, source_target_pairs={{0,16},{8,24},{16,0},{24,8},{1,17},{9,25},{17,1},{25,9},{2,18},{10... | collective-permute-start | bytes 589832 | tf_op jit(solution)/shard_map/ppermute | solution.py:98
  116.6 2.1 %collective-permute-start.29 = (bf16[128,768]{1,0:T(8,128)(2,1)S(1)}, bf16[128,768]{1,0:T(8,128)(2,1)S(1)}, u32[]{:S(2)}, u32[]{:S(2)}) collective-permute-start(bf16[128,768]{1,0:T(8,128)(2,1)S(1)} %multiply_convert_fusion.1.refs_0_), channel_id=1, source_target_pairs={{0,4},{4,0},{1,5},{5,1},{2,6},{6,2},{3,7},{7,3},{8,12},{12,8},{9,1... | collective-permute-start | bytes 589832 | tf_op jit(solution)/shard_map/ppermute | solution.py:98
  118.6 4.0 %collective-permute-done.26.refs_1_ = bf16[128,768]{1,0:T(8,128)(2,1)S(1)} collective-permute-done((bf16[128,768]{1,0:T(8,128)(2,1)S(1)}, bf16[128,768]{1,0:T(8,128)(2,1)S(1)}, u32[]{:S(2)}, u32[]{:S(2)}) %collective-permute-start.26) | collective-permute-done | bytes 196640 | tf_op jit(solution)/shard_map/ppermute | solution.py:98
  122.6 3.3 %collective-permute-done.29.refs_4_ = bf16[128,768]{1,0:T(8,128)(2,1)S(1)} collective-permute-done((bf16[128,768]{1,0:T(8,128)(2,1)S(1)}, bf16[128,768]{1,0:T(8,128)(2,1)S(1)}, u32[]{:S(2)}, u32[]{:S(2)}) %collective-permute-start.29) | collective-permute-done | bytes 196640 | tf_op jit(solution)/shard_map/ppermute | solution.py:98
  128.2 5.4 %shard_map.118 = (f32[2,192,512]{2,1,0:T(8,128)S(1)}, bf16[2,192,512]{2,1,0:T(8,128)(2,1)S(1)}) custom-call(bf16[128,768]{1,0:T(8,128)(2,1)S(1)} %multiply_convert_fusion.1.refs_0_, bf16[128,768]{1,0:T(8,128)(2,1)S(1)} %collective-permute-done.26.refs_1_, bf16[128,768]{1,0:T(8,128)(2,1)S(1)} %collective-permute-done.27.refs_2_, ...), custom_call_target="tpu_custom_call" | custom-call | flops 2516582400 | bytes 8388608 | tf_op jit(solution)/shard_map/pallas_call | solution.py:301
  133.7 1.6 %collective-permute-done.33 = bf16[2,192,512]{2,1,0:T(8,128)(2,1)S(1)} collective-permute-done((bf16[2,192,512]{2,1,0:T(8,128)(2,1)S(1)}, bf16[2,192,512]{2,1,0:T(8,128)(2,1)S(1)}, u32[]{:S(2)}, u32[]{:S(2)}) %collective-permute-start.33) | collective-permute-done | bytes 393248 | tf_op jit(solution)/shard_map/ppermute | solution.py:98
  135.5 1.5 %collective-permute-start.34 = (bf16[192,512]{1,0:T(8,128)(2,1)S(1)}, bf16[192,512]{1,0:T(8,128)(2,1)S(1)}, u32[]{:S(2)}, u32[]{:S(2)}) collective-permute-start(bf16[192,512]{1,0:T(8,128)(2,1)S(1)} %fusion.28), channel_id=1, source_target_pairs={{0,16},{8,24},{16,0},{24,8},{1,17},{9,25},{17,1},{25,9},{2,18},{10... | collective-permute-start | bytes 589832 | tf_op jit(solution)/shard_map/ppermute | solution.py:98
  136.9 5.5 %collective-permute-done.34 = bf16[192,512]{1,0:T(8,128)(2,1)S(1)} collective-permute-done((bf16[192,512]{1,0:T(8,128)(2,1)S(1)}, bf16[192,512]{1,0:T(8,128)(2,1)S(1)}, u32[]{:S(2)}, u32[]{:S(2)}) %collective-permute-start.34) | collective-permute-done | bytes 196640 | tf_op jit(solution)/shard_map/ppermute | solution.py:98
  (123 shorter events, 17.0 us)
Async XLA Ops:
  0.0 16.5 %copy-start.9 = (s32[4]{0:T(128)S(1)}, s32[4]{0:T(128)}, u32[]{:S(2)}) copy-start(s32[4]{0:T(128)} %param.22) | copy-start | bytes 52
  0.0 29.8 %copy-start.4 = (bf16[192,768]{1,0:T(8,128)(2,1)S(1)}, bf16[192,768]{1,0:T(8,128)(2,1)}, u32[]{:S(2)}) copy-start(bf16[192,768]{1,0:T(8,128)(2,1)} %param.20) | copy-start | bytes 884740
  2.1 21.8 %collective-permute-start.2 = (bf16[2,192,512]{2,1,0:T(8,128)(2,1)S(1)}, bf16[2,192,512]{2,1,0:T(8,128)(2,1)}, u32[]{:S(2)}, u32[]{:S(2)}) collective-permute-start(bf16[2,192,512]{2,1,0:T(8,128)(2,1)S(1)} %get-tuple-element.57), channel_id=1, source_target_pairs={{0,2},{1,3},{2,0},{3,1},{4,6},{5,7},{6,4},{7,5},{8,10},{9,11},{10,... | collective-permute-start | bytes 1179656 | tf_op jit(solution)/shard_map/ppermute | solution.py:101
  6.1 26.7 %collective-permute-start.8 = (bf16[2,192,512]{2,1,0:T(8,128)(2,1)S(1)}, bf16[2,192,512]{2,1,0:T(8,128)(2,1)}, u32[]{:S(2)}, u32[]{:S(2)}) collective-permute-start(bf16[2,192,512]{2,1,0:T(8,128)(2,1)S(1)} %get-tuple-element.57), channel_id=1, source_target_pairs={{0,4},{4,0},{1,5},{5,1},{2,6},{6,2},{3,7},{7,3},{8,12},{12,8},{9,1... | collective-permute-start | bytes 1179656 | tf_op jit(solution)/shard_map/ppermute | solution.py:98
  7.6 19.7 %collective-permute-start.1 = (bf16[512,384]{1,0:T(8,128)(2,1)}, bf16[512,384]{1,0:T(8,128)(2,1)S(1)}, u32[]{:S(2)}, u32[]{:S(2)}) collective-permute-start(bf16[512,384]{1,0:T(8,128)(2,1)} %bitcast.96), channel_id=1, source_target_pairs={{0,16},{8,24},{16,0},{24,8},{1,17},{9,25},{17,1},{25,9},{2,18},{10... | collective-permute-start | bytes 1179656 | tf_op jit(solution)/shard_map/ppermute | solution.py:98
  9.1 17.6 %collective-permute-start = (bf16[512,384]{1,0:T(8,128)(2,1)}, bf16[512,384]{1,0:T(8,128)(2,1)}, u32[]{:S(2)}, u32[]{:S(2)}) collective-permute-start(bf16[512,384]{1,0:T(8,128)(2,1)} %bitcast.97), channel_id=1, source_target_pairs={{0,1},{1,0},{2,3},{3,2},{4,5},{5,4},{6,7},{7,6},{8,9},{9,8},{10,11... | collective-permute-start | bytes 1179656 | tf_op jit(solution)/shard_map/ppermute | solution.py:98
  26.7 18.9 %collective-permute-start.3 = (bf16[512,384]{1,0:T(8,128)(2,1)}, bf16[512,384]{1,0:T(8,128)(2,1)}, u32[]{:S(2)}, u32[]{:S(2)}) collective-permute-start(bf16[512,384]{1,0:T(8,128)(2,1)} %collective-permute-done), channel_id=1, source_target_pairs={{0,16},{8,24},{16,0},{24,8},{1,17},{9,25},{17,1},{25,9},{2,18},{10... | collective-permute-start | bytes 1179656 | tf_op jit(solution)/shard_map/ppermute | solution.py:98
  27.3 2.5 %copy-start.3 = (bf16[512,384]{1,0:T(8,128)(2,1)}, bf16[512,384]{1,0:T(8,128)(2,1)S(1)}, u32[]{:S(2)}) copy-start(bf16[512,384]{1,0:T(8,128)(2,1)S(1)} %collective-permute-done.1) | copy-start | bytes 1179652
  27.3 21.4 %collective-permute-start.5 = (bf16[384,768]{1,0:T(8,128)(2,1)}, bf16[384,768]{1,0:T(8,128)(2,1)}, u32[]{:S(2)}, u32[]{:S(2)}) collective-permute-start(bf16[384,768]{1,0:T(8,128)(2,1)} %param.17), channel_id=1, source_target_pairs={{0,16},{8,24},{16,0},{24,8},{1,17},{9,25},{17,1},{25,9},{2,18},{10... | collective-permute-start | bytes 1769480 | tf_op jit(solution)/shard_map/ppermute | solution.py:98
  28.8 18.1 %collective-permute-start.4 = (bf16[2,192,512]{2,1,0:T(8,128)(2,1)}, bf16[2,192,512]{2,1,0:T(8,128)(2,1)}, u32[]{:S(2)}, u32[]{:S(2)}) collective-permute-start(bf16[2,192,512]{2,1,0:T(8,128)(2,1)} %collective-permute-done.2), channel_id=1, source_target_pairs={{0,4},{4,0},{1,5},{5,1},{2,6},{6,2},{3,7},{7,3},{8,12},{12,8},{9,1... | collective-permute-start | bytes 1179656 | tf_op jit(solution)/shard_map/ppermute | solution.py:98
  30.1 11.7 %collective-permute-start.9 = (bf16[1,192,512]{2,1,0:T(8,128)(2,1)}, bf16[1,192,512]{2,1,0:T(8,128)(2,1)S(1)}, u32[]{:S(2)}, u32[]{:S(2)}) collective-permute-start(bf16[1,192,512]{2,1,0:T(8,128)(2,1)} %get-tuple-element.33), channel_id=1, source_target_pairs={{0,4},{4,0},{1,5},{5,1},{2,6},{6,2},{3,7},{7,3},{8,12},{12,8},{9,1... | collective-permute-start | bytes 589832 | tf_op jit(solution)/shard_map/ppermute | solution.py:98
  41.8 14.1 %collective-permute-start.10 = (bf16[2,192,512]{2,1,0:T(8,128)(2,1)}, bf16[2,192,512]{2,1,0:T(8,128)(2,1)S(1)}, u32[]{:S(2)}, u32[]{:S(2)}) collective-permute-start(bf16[2,192,512]{2,1,0:T(8,128)(2,1)} %get-tuple-element.32), channel_id=1, source_target_pairs={{0,1},{1,2},{2,3},{3,0},{4,5},{5,6},{6,7},{7,4},{8,9},{9,10},{10,1... | collective-permute-start | bytes 1179656 | tf_op jit(solution)/shard_map/ppermute | solution.py:101
  41.8 17.6 %collective-permute-start.15 = (bf16[2,192,512]{2,1,0:T(8,128)(2,1)}, bf16[2,192,512]{2,1,0:T(8,128)(2,1)S(1)}, u32[]{:S(2)}, u32[]{:S(2)}) collective-permute-start(bf16[2,192,512]{2,1,0:T(8,128)(2,1)} %get-tuple-element.32), channel_id=1, source_target_pairs={{0,3},{1,0},{2,1},{3,2},{4,7},{5,4},{6,5},{7,6},{8,11},{9,8},{10,9... | collective-permute-start | bytes 1179656 | tf_op jit(solution)/shard_map/ppermute | solution.py:101
  46.8 9.1 %copy-start.7 = (bf16[1,192,512]{2,1,0:T(8,128)(2,1)S(1)}, bf16[1,192,512]{2,1,0:T(8,128)(2,1)}, u32[]{:S(2)}) copy-start(bf16[1,192,512]{2,1,0:T(8,128)(2,1)} %get-tuple-element.33) | copy-start | bytes 589828
  48.7 11.9 %collective-permute-start.6 = (bf16[1024,384]{1,0:T(8,128)(2,1)S(1)}, bf16[1024,384]{1,0:T(8,128)(2,1)S(1)}, u32[]{:S(2)}, u32[]{:S(2)}) collective-permute-start(bf16[1024,384]{1,0:T(8,128)(2,1)S(1)} %pad_maximum_fusion), channel_id=1, source_target_pairs={{0,8},{8,0},{16,24},{24,16},{1,9},{9,1},{17,25},{25,17},{2,10},{10... | collective-permute-start | bytes 2359304 | tf_op jit(solution)/shard_map/ppermute | solution.py:98
  50.0 10.9 %collective-permute-start.7 = (bf16[1024,384]{1,0:T(8,128)(2,1)S(1)}, bf16[1024,384]{1,0:T(8,128)(2,1)S(1)}, u32[]{:S(2)}, u32[]{:S(2)}) collective-permute-start(bf16[1024,384]{1,0:T(8,128)(2,1)S(1)} %pad_maximum_fusion.1), channel_id=1, source_target_pairs={{0,8},{8,0},{16,24},{24,16},{1,9},{9,1},{17,25},{25,17},{2,10},{10... | collective-permute-start | bytes 2359304 | tf_op jit(solution)/shard_map/ppermute | solution.py:98
  55.9 12.0 %collective-permute-start.11 = (bf16[1,192,512]{2,1,0:T(8,128)(2,1)S(1)}, bf16[1,192,512]{2,1,0:T(8,128)(2,1)S(1)}, u32[]{:S(2)}, u32[]{:S(2)}) collective-permute-start(bf16[1,192,512]{2,1,0:T(8,128)(2,1)S(1)} %copy-done.7), channel_id=1, source_target_pairs={{0,2},{1,3},{2,0},{3,1},{4,6},{5,7},{6,4},{7,5},{8,10},{9,11},{10,... | collective-permute-start | bytes 589832 | tf_op jit(solution)/shard_map/ppermute | solution.py:101
  55.9 18.0 %collective-permute-start.16 = (bf16[2,192,512]{2,1,0:T(8,128)(2,1)S(1)}, bf16[2,192,512]{2,1,0:T(8,128)(2,1)S(1)}, u32[]{:S(2)}, u32[]{:S(2)}) collective-permute-start(bf16[2,192,512]{2,1,0:T(8,128)(2,1)S(1)} %collective-permute-done.10), channel_id=1, source_target_pairs={{0,4},{4,0},{1,5},{5,1},{2,6},{6,2},{3,7},{7,3},{8,12},{12,8},{9,1... | collective-permute-start | bytes 1179656 | tf_op jit(solution)/shard_map/ppermute | solution.py:98
  63.6 4.3 %copy-start.6 = (bf16[1,192,512]{2,1,0:T(8,128)(2,1)S(1)}, bf16[1,192,512]{2,1,0:T(8,128)(2,1)}, u32[]{:S(2)}) copy-start(bf16[1,192,512]{2,1,0:T(8,128)(2,1)} %get-tuple-element.35) | copy-start | bytes 589828
  63.6 10.5 %copy-start.2 = (bf16[1024,192]{0,1:T(8,128)(2,1)S(1)}, bf16[1024,192]{0,1:T(8,128)(2,1)}, u32[]{:S(2)}) copy-start(bf16[1024,192]{0,1:T(8,128)(2,1)} %param.16) | copy-start | bytes 1179652
  67.9 9.6 %collective-permute-start.12 = (bf16[1,192,512]{2,1,0:T(8,128)(2,1)S(1)}, bf16[1,192,512]{2,1,0:T(8,128)(2,1)S(1)}, u32[]{:S(2)}, u32[]{:S(2)}) collective-permute-start(bf16[1,192,512]{2,1,0:T(8,128)(2,1)S(1)} %copy-done.6), channel_id=1, source_target_pairs={{0,1},{1,2},{2,3},{3,0},{4,5},{5,6},{6,7},{7,4},{8,9},{9,10},{10,1... | collective-permute-start | bytes 589832 | tf_op jit(solution)/shard_map/ppermute | solution.py:101
  70.0 8.5 %collective-permute-start.18 = (bf16[1,192,512]{2,1,0:T(8,128)(2,1)S(1)}, bf16[1,192,512]{2,1,0:T(8,128)(2,1)S(1)}, u32[]{:S(2)}, u32[]{:S(2)}) collective-permute-start(bf16[1,192,512]{2,1,0:T(8,128)(2,1)S(1)} %copy-done.6), channel_id=1, source_target_pairs={{0,3},{1,0},{2,1},{3,2},{4,7},{5,4},{6,5},{7,6},{8,11},{9,8},{10,9... | collective-permute-start | bytes 589832 | tf_op jit(solution)/shard_map/ppermute | solution.py:101
  71.8 9.4 %collective-permute-start.19 = (bf16[1,192,512]{2,1,0:T(8,128)(2,1)S(1)}, bf16[1,192,512]{2,1,0:T(8,128)(2,1)S(1)}, u32[]{:S(2)}, u32[]{:S(2)}) collective-permute-start(bf16[1,192,512]{2,1,0:T(8,128)(2,1)S(1)} %collective-permute-done.11), channel_id=1, source_target_pairs={{0,4},{4,0},{1,5},{5,1},{2,6},{6,2},{3,7},{7,3},{8,12},{12,8},{9,1... | collective-permute-start | bytes 589832 | tf_op jit(solution)/shard_map/ppermute | solution.py:98
  73.9 14.2 %collective-permute-start.17 = (bf16[2,192,512]{2,1,0:T(8,128)(2,1)S(1)}, bf16[2,192,512]{2,1,0:T(8,128)(2,1)S(1)}, u32[]{:S(2)}, u32[]{:S(2)}) collective-permute-start(bf16[2,192,512]{2,1,0:T(8,128)(2,1)S(1)} %collective-permute-done.15), channel_id=1, source_target_pairs={{0,4},{4,0},{1,5},{5,1},{2,6},{6,2},{3,7},{7,3},{8,12},{12,8},{9,1... | collective-permute-start | bytes 1179656 | tf_op jit(solution)/shard_map/ppermute | solution.py:98
  77.6 10.6 %collective-permute-start.13 = (bf16[384,768]{1,0:T(8,128)(2,1)}, bf16[384,768]{1,0:T(8,128)(2,1)S(1)}, u32[]{:S(2)}, u32[]{:S(2)}) collective-permute-start(bf16[384,768]{1,0:T(8,128)(2,1)} %param.17), channel_id=1, source_target_pairs={{0,8},{8,0},{16,24},{24,16},{1,9},{9,1},{17,25},{25,17},{2,10},{10... | collective-permute-start | bytes 1769480 | tf_op jit(solution)/shard_map/ppermute | solution.py:98
  77.6 11.8 %collective-permute-start.14 = (bf16[384,768]{1,0:T(8,128)(2,1)}, bf16[384,768]{1,0:T(8,128)(2,1)S(1)}, u32[]{:S(2)}, u32[]{:S(2)}) collective-permute-start(bf16[384,768]{1,0:T(8,128)(2,1)} %collective-permute-done.5), channel_id=1, source_target_pairs={{0,8},{8,0},{16,24},{24,16},{1,9},{9,1},{17,25},{25,17},{2,10},{10... | collective-permute-start | bytes 1769480 | tf_op jit(solution)/shard_map/ppermute | solution.py:98
  78.5 16.7 %collective-permute-start.20 = (bf16[1,192,512]{2,1,0:T(8,128)(2,1)S(1)}, bf16[1,192,512]{2,1,0:T(8,128)(2,1)S(1)}, u32[]{:S(2)}, u32[]{:S(2)}) collective-permute-start(bf16[1,192,512]{2,1,0:T(8,128)(2,1)S(1)} %collective-permute-done.12), channel_id=1, source_target_pairs={{0,4},{4,0},{1,5},{5,1},{2,6},{6,2},{3,7},{7,3},{8,12},{12,8},{9,1... | collective-permute-start | bytes 589832 | tf_op jit(solution)/shard_map/ppermute | solution.py:98
  81.2 14.4 %collective-permute-start.21 = (bf16[1,192,512]{2,1,0:T(8,128)(2,1)S(1)}, bf16[1,192,512]{2,1,0:T(8,128)(2,1)S(1)}, u32[]{:S(2)}, u32[]{:S(2)}) collective-permute-start(bf16[1,192,512]{2,1,0:T(8,128)(2,1)S(1)} %collective-permute-done.18), channel_id=1, source_target_pairs={{0,4},{4,0},{1,5},{5,1},{2,6},{6,2},{3,7},{7,3},{8,12},{12,8},{9,1... | collective-permute-start | bytes 589832 | tf_op jit(solution)/shard_map/ppermute | solution.py:98
  93.7 2.3 %copy-start.5 = (bf16[1024,512]{1,0:T(8,128)(2,1)}, bf16[1024,512]{1,0:T(8,128)(2,1)S(1)}, u32[]{:S(2)}) copy-start(bf16[1024,512]{1,0:T(8,128)(2,1)S(1)} %multiply_convert_fusion) | copy-start | bytes 3145732
  96.0 0.9 copy-start.1
  98.4 2.5 %collective-permute-start.22 = (bf16[2,2,128,768]{3,2,1,0:T(8,128)(2,1)}, bf16[2,2,128,768]{3,2,1,0:T(8,128)(2,1)S(1)}, u32[]{:S(2)}, u32[]{:S(2)}) collective-permute-start(bf16[2,2,128,768]{3,2,1,0:T(8,128)(2,1)} %convolution_convert_fusion), channel_id=1, source_target_pairs={{0,8},{8,0},{16,24},{24,16},{1,9},{9,1},{17,25},{25,17},{2,10},{10... | collective-permute-start | bytes 2359304 | tf_op jit(solution)/shard_map/ppermute | solution.py:98
  101.1 13.6 %copy-start.8 = (f32[768]{0:T(1024)S(1)}, f32[768]{0:T(1024)}, u32[]{:S(2)}) copy-start(f32[768]{0:T(1024)} %param.18) | copy-start | bytes 9220
  101.1 27.1 %copy-start = (bf16[3,768,192]{1,2,0:T(8,128)(2,1)S(1)}, bf16[3,768,192]{1,2,0:T(8,128)(2,1)}, u32[]{:S(2)}) copy-start(bf16[3,768,192]{1,2,0:T(8,128)(2,1)} %param.19) | copy-start | bytes 2654212
  101.2 11.8 %collective-permute-start.23 = (bf16[128,768]{1,0:T(8,128)(2,1)S(1)}, bf16[128,768]{1,0:T(8,128)(2,1)S(1)}, u32[]{:S(2)}, u32[]{:S(2)}) collective-permute-start(bf16[128,768]{1,0:T(8,128)(2,1)S(1)} %get-tuple-element.59), channel_id=1, source_target_pairs={{0,16},{8,24},{16,0},{24,8},{1,17},{9,25},{17,1},{25,9},{2,18},{10... | collective-permute-start | bytes 589832 | tf_op jit(solution)/shard_map/ppermute | solution.py:98
  103.5 9.4 %collective-permute-start.25 = (bf16[128,768]{1,0:T(8,128)(2,1)S(1)}, bf16[128,768]{1,0:T(8,128)(2,1)S(1)}, u32[]{:S(2)}, u32[]{:S(2)}) collective-permute-start(bf16[128,768]{1,0:T(8,128)(2,1)S(1)} %get-tuple-element.60), channel_id=1, source_target_pairs={{0,17},{1,16},{2,19},{3,18},{8,25},{9,24},{10,27},{11,26},{16,1},{... | collective-permute-start | bytes 589832 | tf_op jit(solution)/shard_map/ppermute | solution.py:98
  103.6 10.7 %collective-permute-start.24 = (bf16[128,768]{1,0:T(8,128)(2,1)S(1)}, bf16[128,768]{1,0:T(8,128)(2,1)S(1)}, u32[]{:S(2)}, u32[]{:S(2)}) collective-permute-start(bf16[128,768]{1,0:T(8,128)(2,1)S(1)} %fusion.26), channel_id=1, source_target_pairs={{0,1},{1,0},{2,3},{3,2},{4,5},{5,4},{6,7},{7,6},{8,9},{9,8},{10,11... | collective-permute-start | bytes 589832 | tf_op jit(solution)/shard_map/ppermute | solution.py:98
  114.8 7.8 %collective-permute-start.26 = (bf16[128,768]{1,0:T(8,128)(2,1)S(1)}, bf16[128,768]{1,0:T(8,128)(2,1)S(1)}, u32[]{:S(2)}, u32[]{:S(2)}) collective-permute-start(bf16[128,768]{1,0:T(8,128)(2,1)S(1)} %multiply_convert_fusion.1.refs_0_), channel_id=1, source_target_pairs={{0,16},{8,24},{16,0},{24,8},{1,17},{9,25},{17,1},{25,9},{2,18},{10... | collective-permute-start | bytes 589832 | tf_op jit(solution)/shard_map/ppermute | solution.py:98
  116.6 9.4 %collective-permute-start.29 = (bf16[128,768]{1,0:T(8,128)(2,1)S(1)}, bf16[128,768]{1,0:T(8,128)(2,1)S(1)}, u32[]{:S(2)}, u32[]{:S(2)}) collective-permute-start(bf16[128,768]{1,0:T(8,128)(2,1)S(1)} %multiply_convert_fusion.1.refs_0_), channel_id=1, source_target_pairs={{0,4},{4,0},{1,5},{5,1},{2,6},{6,2},{3,7},{7,3},{8,12},{12,8},{9,1... | collective-permute-start | bytes 589832 | tf_op jit(solution)/shard_map/ppermute | solution.py:98
  118.6 8.1 %collective-permute-start.30 = (bf16[128,768]{1,0:T(8,128)(2,1)S(1)}, bf16[128,768]{1,0:T(8,128)(2,1)S(1)}, u32[]{:S(2)}, u32[]{:S(2)}) collective-permute-start(bf16[128,768]{1,0:T(8,128)(2,1)S(1)} %multiply_convert_fusion.1.refs_0_), channel_id=1, source_target_pairs={{0,20},{4,16},{8,28},{12,24},{16,4},{20,0},{24,12},{28,8},{1,21},{... | collective-permute-start | bytes 589832 | tf_op jit(solution)/shard_map/ppermute | solution.py:98
  118.6 8.1 %collective-permute-start.27 = (bf16[128,768]{1,0:T(8,128)(2,1)S(1)}, bf16[128,768]{1,0:T(8,128)(2,1)S(1)}, u32[]{:S(2)}, u32[]{:S(2)}) collective-permute-start(bf16[128,768]{1,0:T(8,128)(2,1)S(1)} %multiply_convert_fusion.1.refs_0_), channel_id=1, source_target_pairs={{0,8},{8,0},{16,24},{24,16},{1,9},{9,1},{17,25},{25,17},{2,10},{10... | collective-permute-start | bytes 589832 | tf_op jit(solution)/shard_map/ppermute | solution.py:98
  122.6 4.1 %collective-permute-start.28 = (bf16[128,768]{1,0:T(8,128)(2,1)S(1)}, bf16[128,768]{1,0:T(8,128)(2,1)S(1)}, u32[]{:S(2)}, u32[]{:S(2)}) collective-permute-start(bf16[128,768]{1,0:T(8,128)(2,1)S(1)} %collective-permute-done.26.refs_1_), channel_id=1, source_target_pairs={{0,8},{8,0},{16,24},{24,16},{1,9},{9,1},{17,25},{25,17},{2,10},{10... | collective-permute-start | bytes 589832 | tf_op jit(solution)/shard_map/ppermute | solution.py:98
  125.9 1.4 %collective-permute-start.31 = (bf16[128,768]{1,0:T(8,128)(2,1)S(1)}, bf16[128,768]{1,0:T(8,128)(2,1)S(1)}, u32[]{:S(2)}, u32[]{:S(2)}) collective-permute-start(bf16[128,768]{1,0:T(8,128)(2,1)S(1)} %collective-permute-done.29.refs_4_), channel_id=1, source_target_pairs={{0,8},{8,0},{16,24},{24,16},{1,9},{9,1},{17,25},{25,17},{2,10},{10... | collective-permute-start | bytes 589832 | tf_op jit(solution)/shard_map/ppermute | solution.py:98
  126.7 1.4 %collective-permute-start.32 = (bf16[128,768]{1,0:T(8,128)(2,1)S(1)}, bf16[128,768]{1,0:T(8,128)(2,1)S(1)}, u32[]{:S(2)}, u32[]{:S(2)}) collective-permute-start(bf16[128,768]{1,0:T(8,128)(2,1)S(1)} %collective-permute-done.30.refs_5_), channel_id=1, source_target_pairs={{0,8},{8,0},{16,24},{24,16},{1,9},{9,1},{17,25},{25,17},{2,10},{10... | collective-permute-start | bytes 589832 | tf_op jit(solution)/shard_map/ppermute | solution.py:98
  133.5 1.8 %collective-permute-start.33 = (bf16[2,192,512]{2,1,0:T(8,128)(2,1)S(1)}, bf16[2,192,512]{2,1,0:T(8,128)(2,1)S(1)}, u32[]{:S(2)}, u32[]{:S(2)}) collective-permute-start(bf16[2,192,512]{2,1,0:T(8,128)(2,1)S(1)} %get-tuple-element.46), channel_id=1, source_target_pairs={{0,8},{8,0},{16,24},{24,16},{1,9},{9,1},{17,25},{25,17},{2,10},{10... | collective-permute-start | bytes 1179656 | tf_op jit(solution)/shard_map/ppermute | solution.py:98
  135.5 7.0 %collective-permute-start.34 = (bf16[192,512]{1,0:T(8,128)(2,1)S(1)}, bf16[192,512]{1,0:T(8,128)(2,1)S(1)}, u32[]{:S(2)}, u32[]{:S(2)}) collective-permute-start(bf16[192,512]{1,0:T(8,128)(2,1)S(1)} %fusion.28), channel_id=1, source_target_pairs={{0,16},{8,24},{16,0},{24,8},{1,17},{9,25},{17,1},{25,9},{2,18},{10... | collective-permute-start | bytes 589832 | tf_op jit(solution)/shard_map/ppermute | solution.py:98

commit v15 on v10

--- a/solution.py
+++ b/solution.py
@@ -202,19 +202,20 @@
             d[1, 0] = flip(down_same, seq=1)
             beside_x = flip(beside, section=2)
             for k in (1, 3):
-                g[0, k] = rotate(after(pair_other, g[0, 2], d[1, 0]), k)
+                g[0, k] = rotate(after(pair_other, g[0, 2], d[1, 0], g[1, 0], mine_x), k)
             g[1, 2] = flip(g[0, 2], seq=1)
-            across = after(jnp.concatenate([mine_x, beside_x], axis=0), g[0, 2])
+            across = after(jnp.concatenate([mine_x, beside_x], axis=0), g[0, 2], g[1, 2])
             both = after(jnp.concatenate([mine, beside], axis=0), across)
             both_c, across_c = flip(both, section=1), flip(across, section=1)
             proj_x = flip(after(w_proj, across), section=2)
-            d[0, 2] = rotate(after(down_same, g[0, 1]), 2)
+            far = rotate(after(down_same, g[0, 1]), 2)
             rows = jnp.concatenate([both, both_c, across, across_c], axis=1)
             normed = layer_norm(rows.astype(jnp.float32), gain).astype(jnp.bfloat16)
             g[1, 1], g[1, 3] = flip(g[0, 1], seq=1), flip(g[0, 3], seq=1)
             gate_up = place_rows(g)
+            d[0, 2] = after(far, normed)
             for k in (1, 3):
-                d[0, k] = rotate(after(down_other, d[0, 2], normed, code, out_w), k)
+                d[0, k] = rotate(after(down_other, d[0, 2], code, out_w), k)
             proj_c = flip(after(w_proj, proj_x, d[0, 1]), section=1)
             proj_xc = flip(after(proj_x, d[0, 1]), section=1)
             proj = jnp.concatenate([w_proj, proj_c, proj_x, proj_xc], axis=0)
@@ -263,7 +264,8 @@
 
         send = project(lax.dynamic_index_in_dim(hidden, 1 - core, 2, False)).astype(jnp.bfloat16)
         got = flip(send, section=1)
-        kept = project(lax.dynamic_index_in_dim(hidden, core, 2, False)) + got.astype(jnp.float32)
+        kept = after(project(lax.dynamic_index_in_dim(hidden, core, 2, False)), send)
+        kept = kept + got.astype(jnp.float32)
         here = lax.dynamic_index_in_dim(kept, side, 1, False)
         there = lax.dynamic_index_in_dim(kept, 1 - side, 1, False).astype(jnp.bfloat16)
         from_x = flip(there[0], section=2)
@@ -302,7 +304,7 @@
                 ],
                 in_specs=[vmem] * 12,
                 out_specs=[vmem] * 2,
-                compiler_params=pltpu.CompilerParams(vmem_limit_bytes=28 * 2**20),
+                compiler_params=pltpu.CompilerParams(vmem_limit_bytes=16 * 2**20),
                 cost_estimate=pl.CostEstimate(
                     flops=2 * count * width * (3 * 768 + 2 * local_heads * tokens),
                     bytes_accessed=8 * 2**20,

time: 129 us -> 133 us (1.031)
  starting transfers between devices: 38.3 us -> 40.8 us
    ppermute x29, waiting for transfers between devices: 43.8 us -> 50.2 us  [flip(): return lax.ppermute(x, names if len(names) > 1 else names[0], pairs)]
    ppermute x6, waiting for transfers between devices: 13.3 us -> 7.45 us  [rotate(): return lax.ppermute(x, 'dp', [(i, (i + k) % n_dp) for i in range(n_dp)])]
    ppermute x29, starting transfers between devices: 24 us -> 28 us  [flip(): return lax.ppermute(x, names if len(names) > 1 else names[0], pairs)]
    ppermute x6, starting transfers between devices: 14.3 us -> 12.8 us  [rotate(): return lax.ppermute(x, 'dp', [(i, (i + k) % n_dp) for i in range(n_dp)])]
  transfers between devices with their start and end apart: 35 -> 35, of which waited for: 18 -> 19; matrix products, arithmetic and copies ran while one was open for 17% -> 18% of each run, Pallas kernels for 0% -> 0%
where the time goes in v15:
time: 133 us; the launch traced here: 132 us
  waiting for transfers between devices  57.7 us (43%)
  starting transfers between devices  40.8 us (31%)
  matrix products  9.92 us (7%)
  other arithmetic  9.52 us (7%)
  local copies, waits for them, and re-layouts  8.53 us (6%)
  Pallas kernels  5.34 us (4%)
    ppermute x29, waiting for transfers between devices, flip(): return lax.ppermute(x, names if len(names) > 1 else names[0], pairs)  50.2 us
    ppermute x29, starting transfers between devices, flip(): return lax.ppermute(x, names if len(names) > 1 else names[0], pairs)  28 us
    ppermute x6, starting transfers between devices, rotate(): return lax.ppermute(x, 'dp', [(i, (i + k) % n_dp) for i in range(n_dp)])  12.8 us
    ppermute x6, waiting for transfers between devices, rotate(): return lax.ppermute(x, 'dp', [(i, (i + k) % n_dp) for i in range(n_dp)])  7.45 us
    pallas_call x1, Pallas kernels, per_device(): pl.pallas_call(lambda *refs: attend_kernel(*refs, heads=local_heads, mask...  5.34 us
    dot_general x2, matrix products, project(): lax.dot_general(x, folded, (((x.ndim - 1,), (1,)), ((), ())), preferred_e...  3.39 us
    dynamic_update_slice x14, local copies, waits for them, and re-layouts, place_rows(): whole = lax.dynamic_update_slice(whole, block, (0, row_of(y, k, rows), 0))  3.35 us
  transfers between devices with their start and end apart: 35, of which 19 were waited for; matrix products, arithmetic and copies ran while one was open for 18% of the time, Pallas kernels for 0%

profile of v15, /device:TPU:0, one launch (start us, length us, event | category | flops | bytes accessed | tf_op | source)
XLA Modules:
  0.0 132.5 jit_solution(7736016473824674951)
XLA Ops:
  0.0 3.1 %collective-permute-start = (bf16[512,384]{1,0:T(8,128)(2,1)}, bf16[512,384]{1,0:T(8,128)(2,1)}, u32[]{:S(2)}, u32[]{:S(2)}) collective-permute-start(bf16[512,384]{1,0:T(8,128)(2,1)} %bitcast.96), channel_id=1, source_target_pairs={{0,1},{1,0},{2,3},{3,2},{4,5},{5,4},{6,7},{7,6},{8,9},{9,8},{10,11... | collective-permute-start | bytes 1179656 | tf_op jit(solution)/shard_map/ppermute | solution.py:98
  3.1 1.5 %collective-permute-start.1 = (bf16[512,384]{1,0:T(8,128)(2,1)}, bf16[512,384]{1,0:T(8,128)(2,1)}, u32[]{:S(2)}, u32[]{:S(2)}) collective-permute-start(bf16[512,384]{1,0:T(8,128)(2,1)} %bitcast.97), channel_id=1, source_target_pairs={{0,16},{8,24},{16,0},{24,8},{1,17},{9,25},{17,1},{25,9},{2,18},{10... | collective-permute-start | bytes 1179656 | tf_op jit(solution)/shard_map/ppermute | solution.py:98
  4.6 2.0 %fusion.13 = (bf16[2,192,512]{2,1,0:T(8,128)(2,1)}, bf16[2,192,512]{2,1,0:T(8,128)(2,1)S(1)}) fusion(s32[]{:T(128)S(6)} %select_n.238, bf16[1,192,1024]{2,1,0:T(8,128)(2,1)} %bitcast.94, bf16[1,192,1024]{2,1,0:T(8,128)(2,1)} %bitcast.95, s32[]{:T(128)S(6)} %select_n.236), kind=kLoop, calls=%fused_computation.29 | loop fusion | flops 1572864 | bytes 1572872 | tf_op jit(solution)/shard_map/stack | solution.py:163
  6.6 2.6 %collective-permute-start.3 = (bf16[2,192,512]{2,1,0:T(8,128)(2,1)S(1)}, bf16[2,192,512]{2,1,0:T(8,128)(2,1)}, u32[]{:S(2)}, u32[]{:S(2)}) collective-permute-start(bf16[2,192,512]{2,1,0:T(8,128)(2,1)S(1)} %get-tuple-element.48), channel_id=1, source_target_pairs={{0,2},{1,3},{2,0},{3,1},{4,6},{5,7},{6,4},{7,5},{8,10},{9,11},{10,... | collective-permute-start | bytes 1179656 | tf_op jit(solution)/shard_map/ppermute | solution.py:101
  9.2 1.5 %collective-permute-start.9 = (bf16[2,192,512]{2,1,0:T(8,128)(2,1)S(1)}, bf16[2,192,512]{2,1,0:T(8,128)(2,1)}, u32[]{:S(2)}, u32[]{:S(2)}) collective-permute-start(bf16[2,192,512]{2,1,0:T(8,128)(2,1)S(1)} %get-tuple-element.48), channel_id=1, source_target_pairs={{0,4},{4,0},{1,5},{5,1},{2,6},{6,2},{3,7},{7,3},{8,12},{12,8},{9,1... | collective-permute-start | bytes 1179656 | tf_op jit(solution)/shard_map/ppermute | solution.py:98
  10.7 1.8 %dynamic-slice_bitcast_fusion.2 = (bf16[1,192,512]{2,1,0:T(8,128)(2,1)}, bf16[1,192,512]{2,1,0:T(8,128)(2,1)}) fusion(bf16[1024,192]{0,1:T(8,128)(2,1)} %param.16, s32[]{:T(128)S(6)} %select_n.236, s32[]{:T(128)S(6)} %select_n.238), kind=kLoop, calls=%fused_computation.62 | loop fusion | bytes 786440 | tf_op jit(solution)/shard_map/dynamic_slice | solution.py:161
  14.6 3.3 %collective-permute-done = bf16[512,384]{1,0:T(8,128)(2,1)} collective-permute-done((bf16[512,384]{1,0:T(8,128)(2,1)}, bf16[512,384]{1,0:T(8,128)(2,1)}, u32[]{:S(2)}, u32[]{:S(2)}) %collective-permute-start) | collective-permute-done | bytes 393248 | tf_op jit(solution)/shard_map/ppermute | solution.py:98
  17.8 2.6 %collective-permute-start.2 = (bf16[512,384]{1,0:T(8,128)(2,1)}, bf16[512,384]{1,0:T(8,128)(2,1)}, u32[]{:S(2)}, u32[]{:S(2)}) collective-permute-start(bf16[512,384]{1,0:T(8,128)(2,1)} %collective-permute-done), channel_id=1, source_target_pairs={{0,16},{8,24},{16,0},{24,8},{1,17},{9,25},{17,1},{25,9},{2,18},{10... | collective-permute-start | bytes 1179656 | tf_op jit(solution)/shard_map/ppermute | solution.py:98
  20.5 1.1 copy.14
  21.7 1.9 %collective-permute-done.8 = bf16[1,192,512]{2,1,0:T(8,128)(2,1)} collective-permute-done((bf16[1,192,512]{2,1,0:T(8,128)(2,1)}, bf16[1,192,512]{2,1,0:T(8,128)(2,1)}, u32[]{:S(2)}, u32[]{:S(2)}) %collective-permute-start.8) | collective-permute-done | bytes 196640 | tf_op jit(solution)/shard_map/ppermute | solution.py:98
  23.6 2.8 %collective-permute-done.3 = bf16[2,192,512]{2,1,0:T(8,128)(2,1)} collective-permute-done((bf16[2,192,512]{2,1,0:T(8,128)(2,1)S(1)}, bf16[2,192,512]{2,1,0:T(8,128)(2,1)}, u32[]{:S(2)}, u32[]{:S(2)}) %collective-permute-start.3) | collective-permute-done | bytes 393248 | tf_op jit(solution)/shard_map/ppermute | solution.py:101
  26.7 3.5 %collective-permute-start.15 = (bf16[2,192,512]{2,1,0:T(8,128)(2,1)}, bf16[2,192,512]{2,1,0:T(8,128)(2,1)S(1)}, u32[]{:S(2)}, u32[]{:S(2)}) collective-permute-start(bf16[2,192,512]{2,1,0:T(8,128)(2,1)} %get-tuple-element.24), channel_id=1, source_target_pairs={{0,3},{1,0},{2,1},{3,2},{4,7},{5,4},{6,5},{7,6},{8,11},{9,8},{10,9... | collective-permute-start | bytes 1179656 | tf_op jit(solution)/shard_map/ppermute | solution.py:101
  30.2 1.5 %collective-permute-start.4 = (bf16[2,192,512]{2,1,0:T(8,128)(2,1)}, bf16[2,192,512]{2,1,0:T(8,128)(2,1)S(1)}, u32[]{:S(2)}, u32[]{:S(2)}) collective-permute-start(bf16[2,192,512]{2,1,0:T(8,128)(2,1)} %collective-permute-done.3), channel_id=1, source_target_pairs={{0,4},{4,0},{1,5},{5,1},{2,6},{6,2},{3,7},{7,3},{8,12},{12,8},{9,1... | collective-permute-start | bytes 1179656 | tf_op jit(solution)/shard_map/ppermute | solution.py:98
  32.0 1.1 constant_dynamic-update-slice_fusion.17
  33.1 1.1 pad_maximum_fusion
  34.2 1.2 pad_maximum_fusion.1
  35.4 3.9 %collective-permute-done.4 = bf16[2,192,512]{2,1,0:T(8,128)(2,1)S(1)} collective-permute-done((bf16[2,192,512]{2,1,0:T(8,128)(2,1)}, bf16[2,192,512]{2,1,0:T(8,128)(2,1)S(1)}, u32[]{:S(2)}, u32[]{:S(2)}) %collective-permute-start.4) | collective-permute-done | bytes 393248 | tf_op jit(solution)/shard_map/ppermute | solution.py:98
  39.3 1.0 constant_dynamic-update-slice_fusion.16
  41.4 1.5 %collective-permute-start.16 = (bf16[2,192,512]{2,1,0:T(8,128)(2,1)S(1)}, bf16[2,192,512]{2,1,0:T(8,128)(2,1)S(1)}, u32[]{:S(2)}, u32[]{:S(2)}) collective-permute-start(bf16[2,192,512]{2,1,0:T(8,128)(2,1)S(1)} %collective-permute-done.10), channel_id=1, source_target_pairs={{0,4},{4,0},{1,5},{5,1},{2,6},{6,2},{3,7},{7,3},{8,12},{12,8},{9,1... | collective-permute-start | bytes 1179656 | tf_op jit(solution)/shard_map/ppermute | solution.py:98
  43.0 1.6 %collective-permute-done.15 = bf16[2,192,512]{2,1,0:T(8,128)(2,1)S(1)} collective-permute-done((bf16[2,192,512]{2,1,0:T(8,128)(2,1)}, bf16[2,192,512]{2,1,0:T(8,128)(2,1)S(1)}, u32[]{:S(2)}, u32[]{:S(2)}) %collective-permute-start.15) | collective-permute-done | bytes 393248 | tf_op jit(solution)/shard_map/ppermute | solution.py:101
  44.5 1.5 %collective-permute-start.17 = (bf16[2,192,512]{2,1,0:T(8,128)(2,1)S(1)}, bf16[2,192,512]{2,1,0:T(8,128)(2,1)S(1)}, u32[]{:S(2)}, u32[]{:S(2)}) collective-permute-start(bf16[2,192,512]{2,1,0:T(8,128)(2,1)S(1)} %collective-permute-done.15), channel_id=1, source_target_pairs={{0,4},{4,0},{1,5},{5,1},{2,6},{6,2},{3,7},{7,3},{8,12},{12,8},{9,1... | collective-permute-start | bytes 1179656 | tf_op jit(solution)/shard_map/ppermute | solution.py:98
  46.2 7.2 %collective-permute-done.16 = bf16[2,192,512]{2,1,0:T(8,128)(2,1)S(1)} collective-permute-done((bf16[2,192,512]{2,1,0:T(8,128)(2,1)S(1)}, bf16[2,192,512]{2,1,0:T(8,128)(2,1)S(1)}, u32[]{:S(2)}, u32[]{:S(2)}) %collective-permute-start.16) | collective-permute-done | bytes 393248 | tf_op jit(solution)/shard_map/ppermute | solution.py:98
  53.5 2.5 %collective-permute-start.11 = (bf16[1,192,512]{2,1,0:T(8,128)(2,1)}, bf16[1,192,512]{2,1,0:T(8,128)(2,1)S(1)}, u32[]{:S(2)}, u32[]{:S(2)}) collective-permute-start(bf16[1,192,512]{2,1,0:T(8,128)(2,1)} %get-tuple-element.25), channel_id=1, source_target_pairs={{0,2},{1,3},{2,0},{3,1},{4,6},{5,7},{6,4},{7,5},{8,10},{9,11},{10,... | collective-permute-start | bytes 589832 | tf_op jit(solution)/shard_map/ppermute | solution.py:101
  56.0 4.7 %collective-permute-done.17 = bf16[2,192,512]{2,1,0:T(8,128)(2,1)S(1)} collective-permute-done((bf16[2,192,512]{2,1,0:T(8,128)(2,1)S(1)}, bf16[2,192,512]{2,1,0:T(8,128)(2,1)S(1)}, u32[]{:S(2)}, u32[]{:S(2)}) %collective-permute-start.17) | collective-permute-done | bytes 393248 | tf_op jit(solution)/shard_map/ppermute | solution.py:98
  61.8 1.0 fusion.2
  62.7 1.0 fusion.4
  64.2 3.4 %collective-permute-start.18 = (bf16[1,192,512]{2,1,0:T(8,128)(2,1)S(1)}, bf16[1,192,512]{2,1,0:T(8,128)(2,1)S(1)}, u32[]{:S(2)}, u32[]{:S(2)}) collective-permute-start(bf16[1,192,512]{2,1,0:T(8,128)(2,1)S(1)} %copy-done.7), channel_id=1, source_target_pairs={{0,3},{1,0},{2,1},{3,2},{4,7},{5,4},{6,5},{7,6},{8,11},{9,8},{10,9... | collective-permute-start | bytes 589832 | tf_op jit(solution)/shard_map/ppermute | solution.py:101
  67.7 1.5 %collective-permute-start.19 = (bf16[1,192,512]{2,1,0:T(8,128)(2,1)S(1)}, bf16[1,192,512]{2,1,0:T(8,128)(2,1)S(1)}, u32[]{:S(2)}, u32[]{:S(2)}) collective-permute-start(bf16[1,192,512]{2,1,0:T(8,128)(2,1)S(1)} %collective-permute-done.11), channel_id=1, source_target_pairs={{0,4},{4,0},{1,5},{5,1},{2,6},{6,2},{3,7},{7,3},{8,12},{12,8},{9,1... | collective-permute-start | bytes 589832 | tf_op jit(solution)/shard_map/ppermute | solution.py:98
  69.4 0.9 bitcast_dynamic-update-slice_fusion.4
  70.4 3.0 %collective-permute-done.12 = bf16[1,192,512]{2,1,0:T(8,128)(2,1)S(1)} collective-permute-done((bf16[1,192,512]{2,1,0:T(8,128)(2,1)S(1)}, bf16[1,192,512]{2,1,0:T(8,128)(2,1)S(1)}, u32[]{:S(2)}, u32[]{:S(2)}) %collective-permute-start.12) | collective-permute-done | bytes 196640 | tf_op jit(solution)/shard_map/ppermute | solution.py:101
  74.0 1.5 %collective-permute-start.20 = (bf16[1,192,512]{2,1,0:T(8,128)(2,1)S(1)}, bf16[1,192,512]{2,1,0:T(8,128)(2,1)S(1)}, u32[]{:S(2)}, u32[]{:S(2)}) collective-permute-start(bf16[1,192,512]{2,1,0:T(8,128)(2,1)S(1)} %collective-permute-done.12), channel_id=1, source_target_pairs={{0,4},{4,0},{1,5},{5,1},{2,6},{6,2},{3,7},{7,3},{8,12},{12,8},{9,1... | collective-permute-start | bytes 589832 | tf_op jit(solution)/shard_map/ppermute | solution.py:98
  76.9 1.8 %fusion.6 = f32[1024,512]{1,0:T(8,128)S(1)} fusion(bf16[1024,1536]{1,0:T(8,128)(2,1)S(1)} %fusion.4, bf16[2,1536,512]{2,1,0:T(8,128)(2,1)S(1)} %constant_dynamic-update-slice_fusion.11), kind=kOutput, calls=%fused_computation.11 | convolution fusion | flops 1610612736 | bytes 6815744 | tf_op jit(solution)/shard_map/dot_general | solution.py:238
  78.6 2.0 %multiply_convert_fusion = bf16[1024,512]{1,0:T(8,128)(2,1)S(1)} fusion(f32[1024,512]{1,0:T(8,128)S(1)} %fusion.6, bf16[1024,1536]{1,0:T(8,128)(2,1)S(1)} %fusion.4, bf16[2,1536,512]{2,1,0:T(8,128)(2,1)S(1)} %constant_dynamic-update-slice_fusion.11), kind=kOutput, calls=%fused_computation.7 | convolution fusion | flops 1613758464 | bytes 7864320 | tf_op jit(solution)/shard_map/dot_general | solution.py:239
  80.7 1.4 %fusion.52 = f32[768,512]{1,0:T(8,128)S(1)} fusion(bf16[1536,768]{1,0:T(8,128)(2,1)S(1)} %constant_dynamic-update-slice_fusion.5, bf16[1536,512]{1,0:T(8,128)(2,1)S(1)} %bitcast_dynamic-update-slice_fusion), kind=kOutput, calls=%fused_computation.130 | convolution fusion | flops 1207959552 | bytes 5505024 | tf_op jit(solution)/shard_map/dot_general | solution.py:244
  82.5 2.5 %collective-permute-done.21 = bf16[1,192,512]{2,1,0:T(8,128)(2,1)S(1)} collective-permute-done((bf16[1,192,512]{2,1,0:T(8,128)(2,1)S(1)}, bf16[1,192,512]{2,1,0:T(8,128)(2,1)S(1)}, u32[]{:S(2)}, u32[]{:S(2)}) %collective-permute-start.21) | collective-permute-done | bytes 196640 | tf_op jit(solution)/shard_map/ppermute | solution.py:98
  86.4 1.5 %convolution_convert_fusion = bf16[2,2,128,768]{3,2,1,0:T(8,128)(2,1)} fusion(bf16[768,512,1,1]{1,0,3,2:T(8,128)(2,1)S(1)} %fusion.7, bf16[2,2,2,128,512]{4,3,2,1,0:T(8,128)(2,1)S(1)} %bitcast.99, s32[]{:T(128)S(6)} %select_n.279), kind=kOutput, calls=%fused_computation.14 | convolution fusion | flops 403046400 | bytes 2097156 | tf_op jit(solution)/shard_map/dot_general | solution.py:261
  87.9 1.9 %fusion.9 = f32[2,2,128,768]{3,2,1,0:T(8,128)S(1)} fusion(bf16[768,512,1,1]{1,0,3,2:T(8,128)(2,1)} %copy-done.1, bf16[2,2,2,128,512]{4,3,2,1,0:T(8,128)(2,1)} %bitcast.100, s32[]{:T(128)S(6)} %select_n.278), kind=kOutput, calls=%fused_computation.25 | convolution fusion | flops 402653184 | bytes 2883588 | tf_op jit(solution)/shard_map/dot_general | solution.py:261
  90.7 3.0 %collective-permute-start.24 = (bf16[128,768]{1,0:T(8,128)(2,1)S(1)}, bf16[128,768]{1,0:T(8,128)(2,1)S(1)}, u32[]{:S(2)}, u32[]{:S(2)}) collective-permute-start(bf16[128,768]{1,0:T(8,128)(2,1)S(1)} %fusion.26), channel_id=1, source_target_pairs={{0,1},{1,0},{2,3},{3,2},{4,5},{5,4},{6,7},{7,6},{8,9},{9,8},{10,11... | collective-permute-start | bytes 589832 | tf_op jit(solution)/shard_map/ppermute | solution.py:98
  94.3 5.1 %collective-permute-done.25 = bf16[128,768]{1,0:T(8,128)(2,1)S(1)} collective-permute-done((bf16[128,768]{1,0:T(8,128)(2,1)S(1)}, bf16[128,768]{1,0:T(8,128)(2,1)S(1)}, u32[]{:S(2)}, u32[]{:S(2)}) %collective-permute-start.25) | collective-permute-done | bytes 196640 | tf_op jit(solution)/shard_map/ppermute | solution.py:98
  99.4 3.5 %collective-permute-done.24 = bf16[128,768]{1,0:T(8,128)(2,1)S(1)} collective-permute-done((bf16[128,768]{1,0:T(8,128)(2,1)S(1)}, bf16[128,768]{1,0:T(8,128)(2,1)S(1)}, u32[]{:S(2)}, u32[]{:S(2)}) %collective-permute-start.24) | collective-permute-done | bytes 196640 | tf_op jit(solution)/shard_map/ppermute | solution.py:98
  103.4 1.5 %collective-permute-start.26 = (bf16[128,768]{1,0:T(8,128)(2,1)S(1)}, bf16[128,768]{1,0:T(8,128)(2,1)S(1)}, u32[]{:S(2)}, u32[]{:S(2)}) collective-permute-start(bf16[128,768]{1,0:T(8,128)(2,1)S(1)} %multiply_convert_fusion.1.refs_0_), channel_id=1, source_target_pairs={{0,16},{8,24},{16,0},{24,8},{1,17},{9,25},{17,1},{25,9},{2,18},{10... | collective-permute-start | bytes 589832 | tf_op jit(solution)/shard_map/ppermute | solution.py:98
  104.9 1.5 %collective-permute-start.29 = (bf16[128,768]{1,0:T(8,128)(2,1)S(1)}, bf16[128,768]{1,0:T(8,128)(2,1)S(1)}, u32[]{:S(2)}, u32[]{:S(2)}) collective-permute-start(bf16[128,768]{1,0:T(8,128)(2,1)S(1)} %multiply_convert_fusion.1.refs_0_), channel_id=1, source_target_pairs={{0,4},{4,0},{1,5},{5,1},{2,6},{6,2},{3,7},{7,3},{8,12},{12,8},{9,1... | collective-permute-start | bytes 589832 | tf_op jit(solution)/shard_map/ppermute | solution.py:98
  106.9 4.3 %collective-permute-done.26.refs_1_ = bf16[128,768]{1,0:T(8,128)(2,1)S(1)} collective-permute-done((bf16[128,768]{1,0:T(8,128)(2,1)S(1)}, bf16[128,768]{1,0:T(8,128)(2,1)S(1)}, u32[]{:S(2)}, u32[]{:S(2)}) %collective-permute-start.26) | collective-permute-done | bytes 196640 | tf_op jit(solution)/shard_map/ppermute | solution.py:98
  111.2 4.4 %collective-permute-done.29.refs_4_ = bf16[128,768]{1,0:T(8,128)(2,1)S(1)} collective-permute-done((bf16[128,768]{1,0:T(8,128)(2,1)S(1)}, bf16[128,768]{1,0:T(8,128)(2,1)S(1)}, u32[]{:S(2)}, u32[]{:S(2)}) %collective-permute-start.29) | collective-permute-done | bytes 196640 | tf_op jit(solution)/shard_map/ppermute | solution.py:98
  117.3 5.3 %shard_map.118 = (f32[2,192,512]{2,1,0:T(8,128)S(1)}, bf16[2,192,512]{2,1,0:T(8,128)(2,1)S(1)}) custom-call(bf16[128,768]{1,0:T(8,128)(2,1)S(1)} %multiply_convert_fusion.1.refs_0_, bf16[128,768]{1,0:T(8,128)(2,1)S(1)} %collective-permute-done.26.refs_1_, bf16[128,768]{1,0:T(8,128)(2,1)S(1)} %collective-permute-done.27.refs_2_, ...), custom_call_target="tpu_custom_call" | custom-call | flops 2516582400 | bytes 8388608 | tf_op jit(solution)/shard_map/pallas_call | solution.py:299
  123.0 1.5 %collective-permute-done.33 = bf16[2,192,512]{2,1,0:T(8,128)(2,1)S(1)} collective-permute-done((bf16[2,192,512]{2,1,0:T(8,128)(2,1)S(1)}, bf16[2,192,512]{2,1,0:T(8,128)(2,1)S(1)}, u32[]{:S(2)}, u32[]{:S(2)}) %collective-permute-start.33) | collective-permute-done | bytes 393248 | tf_op jit(solution)/shard_map/ppermute | solution.py:98
  124.6 1.0 collective-permute-start.34
  125.6 6.1 %collective-permute-done.34 = bf16[192,512]{1,0:T(8,128)(2,1)S(1)} collective-permute-done((bf16[192,512]{1,0:T(8,128)(2,1)S(1)}, bf16[192,512]{1,0:T(8,128)(2,1)S(1)}, u32[]{:S(2)}, u32[]{:S(2)}) %collective-permute-start.34) | collective-permute-done | bytes 196640 | tf_op jit(solution)/shard_map/ppermute | solution.py:98
  (129 shorter events, 14.5 us)
Async XLA Ops:
  0.0 13.0 %copy-start.12 = (s32[1,3]{1,0:T(1,128)S(1)}, s32[1,3]{1,0:T(1,128)}, u32[]{:S(2)}) copy-start(s32[1,3]{1,0:T(1,128)} %param.21) | copy-start | bytes 40
  0.0 13.2 %copy-start.10 = (s32[4]{0:T(128)S(1)}, s32[4]{0:T(128)}, u32[]{:S(2)}) copy-start(s32[4]{0:T(128)} %param.22) | copy-start | bytes 52
  0.0 13.2 %copy-start.11 = (s32[4]{0:T(128)S(1)}, s32[4]{0:T(128)}, u32[]{:S(2)}) copy-start(s32[4]{0:T(128)} %param.23) | copy-start | bytes 52
  0.0 14.3 %copy-start.8 = (f32[1536]{0:T(1024)S(1)}, f32[1536]{0:T(1024)}, u32[]{:S(2)}) copy-start(f32[1536]{0:T(1024)} %param.13) | copy-start | bytes 18436
  0.0 14.5 %copy-start.3 = (bf16[384,768]{1,0:T(8,128)(2,1)S(1)}, bf16[384,768]{1,0:T(8,128)(2,1)}, u32[]{:S(2)}) copy-start(bf16[384,768]{1,0:T(8,128)(2,1)} %param.17) | copy-start | bytes 1769476
  0.0 17.8 %collective-permute-start = (bf16[512,384]{1,0:T(8,128)(2,1)}, bf16[512,384]{1,0:T(8,128)(2,1)}, u32[]{:S(2)}, u32[]{:S(2)}) collective-permute-start(bf16[512,384]{1,0:T(8,128)(2,1)} %bitcast.96), channel_id=1, source_target_pairs={{0,1},{1,0},{2,3},{3,2},{4,5},{5,4},{6,7},{7,6},{8,9},{9,8},{10,11... | collective-permute-start | bytes 1179656 | tf_op jit(solution)/shard_map/ppermute | solution.py:98
  3.1 20.4 %collective-permute-start.1 = (bf16[512,384]{1,0:T(8,128)(2,1)}, bf16[512,384]{1,0:T(8,128)(2,1)}, u32[]{:S(2)}, u32[]{:S(2)}) collective-permute-start(bf16[512,384]{1,0:T(8,128)(2,1)} %bitcast.97), channel_id=1, source_target_pairs={{0,16},{8,24},{16,0},{24,8},{1,17},{9,25},{17,1},{25,9},{2,18},{10... | collective-permute-start | bytes 1179656 | tf_op jit(solution)/shard_map/ppermute | solution.py:98
  6.6 19.8 %collective-permute-start.3 = (bf16[2,192,512]{2,1,0:T(8,128)(2,1)S(1)}, bf16[2,192,512]{2,1,0:T(8,128)(2,1)}, u32[]{:S(2)}, u32[]{:S(2)}) collective-permute-start(bf16[2,192,512]{2,1,0:T(8,128)(2,1)S(1)} %get-tuple-element.48), channel_id=1, source_target_pairs={{0,2},{1,3},{2,0},{3,1},{4,6},{5,7},{6,4},{7,5},{8,10},{9,11},{10,... | collective-permute-start | bytes 1179656 | tf_op jit(solution)/shard_map/ppermute | solution.py:101
  9.2 17.2 %collective-permute-start.9 = (bf16[2,192,512]{2,1,0:T(8,128)(2,1)S(1)}, bf16[2,192,512]{2,1,0:T(8,128)(2,1)}, u32[]{:S(2)}, u32[]{:S(2)}) collective-permute-start(bf16[2,192,512]{2,1,0:T(8,128)(2,1)S(1)} %get-tuple-element.48), channel_id=1, source_target_pairs={{0,4},{4,0},{1,5},{5,1},{2,6},{6,2},{3,7},{7,3},{8,12},{12,8},{9,1... | collective-permute-start | bytes 1179656 | tf_op jit(solution)/shard_map/ppermute | solution.py:98
  12.5 11.0 %collective-permute-start.8 = (bf16[1,192,512]{2,1,0:T(8,128)(2,1)}, bf16[1,192,512]{2,1,0:T(8,128)(2,1)}, u32[]{:S(2)}, u32[]{:S(2)}) collective-permute-start(bf16[1,192,512]{2,1,0:T(8,128)(2,1)} %get-tuple-element.25), channel_id=1, source_target_pairs={{0,4},{4,0},{1,5},{5,1},{2,6},{6,2},{3,7},{7,3},{8,12},{12,8},{9,1... | collective-permute-start | bytes 589832 | tf_op jit(solution)/shard_map/ppermute | solution.py:98
  17.8 16.4 %collective-permute-start.2 = (bf16[512,384]{1,0:T(8,128)(2,1)}, bf16[512,384]{1,0:T(8,128)(2,1)}, u32[]{:S(2)}, u32[]{:S(2)}) collective-permute-start(bf16[512,384]{1,0:T(8,128)(2,1)} %collective-permute-done), channel_id=1, source_target_pairs={{0,16},{8,24},{16,0},{24,8},{1,17},{9,25},{17,1},{25,9},{2,18},{10... | collective-permute-start | bytes 1179656 | tf_op jit(solution)/shard_map/ppermute | solution.py:98
  26.4 6.7 %copy-start.5 = (bf16[1,512,384]{2,1,0:T(8,128)(2,1)S(1)}, bf16[1,512,384]{2,1,0:T(8,128)(2,1)}, u32[]{:S(2)}) copy-start(bf16[1,512,384]{2,1,0:T(8,128)(2,1)} %param.12) | copy-start | bytes 1179652
  26.4 15.0 %collective-permute-start.10 = (bf16[2,192,512]{2,1,0:T(8,128)(2,1)}, bf16[2,192,512]{2,1,0:T(8,128)(2,1)S(1)}, u32[]{:S(2)}, u32[]{:S(2)}) collective-permute-start(bf16[2,192,512]{2,1,0:T(8,128)(2,1)} %get-tuple-element.24), channel_id=1, source_target_pairs={{0,1},{1,2},{2,3},{3,0},{4,5},{5,6},{6,7},{7,4},{8,9},{9,10},{10,1... | collective-permute-start | bytes 1179656 | tf_op jit(solution)/shard_map/ppermute | solution.py:101
  26.7 17.8 %collective-permute-start.15 = (bf16[2,192,512]{2,1,0:T(8,128)(2,1)}, bf16[2,192,512]{2,1,0:T(8,128)(2,1)S(1)}, u32[]{:S(2)}, u32[]{:S(2)}) collective-permute-start(bf16[2,192,512]{2,1,0:T(8,128)(2,1)} %get-tuple-element.24), channel_id=1, source_target_pairs={{0,3},{1,0},{2,1},{3,2},{4,7},{5,4},{6,5},{7,6},{8,11},{9,8},{10,9... | collective-permute-start | bytes 1179656 | tf_op jit(solution)/shard_map/ppermute | solution.py:101
  30.2 9.1 %collective-permute-start.4 = (bf16[2,192,512]{2,1,0:T(8,128)(2,1)}, bf16[2,192,512]{2,1,0:T(8,128)(2,1)S(1)}, u32[]{:S(2)}, u32[]{:S(2)}) collective-permute-start(bf16[2,192,512]{2,1,0:T(8,128)(2,1)} %collective-permute-done.3), channel_id=1, source_target_pairs={{0,4},{4,0},{1,5},{5,1},{2,6},{6,2},{3,7},{7,3},{8,12},{12,8},{9,1... | collective-permute-start | bytes 1179656 | tf_op jit(solution)/shard_map/ppermute | solution.py:98
  32.0 8.9 %copy-start.4 = (bf16[384,768]{1,0:T(8,128)(2,1)S(1)}, bf16[384,768]{1,0:T(8,128)(2,1)}, u32[]{:S(2)}) copy-start(bf16[384,768]{1,0:T(8,128)(2,1)} %param.17) | copy-start | bytes 1769476
  39.3 21.4 %collective-permute-start.5 = (bf16[1024,384]{1,0:T(8,128)(2,1)S(1)}, bf16[1024,384]{1,0:T(8,128)(2,1)S(1)}, u32[]{:S(2)}, u32[]{:S(2)}) collective-permute-start(bf16[1024,384]{1,0:T(8,128)(2,1)S(1)} %pad_maximum_fusion), channel_id=1, source_target_pairs={{0,8},{8,0},{16,24},{24,16},{1,9},{9,1},{17,25},{25,17},{2,10},{10... | collective-permute-start | bytes 2359304 | tf_op jit(solution)/shard_map/ppermute | solution.py:98
  40.3 20.8 %collective-permute-start.6 = (bf16[1024,384]{1,0:T(8,128)(2,1)S(1)}, bf16[1024,384]{1,0:T(8,128)(2,1)S(1)}, u32[]{:S(2)}, u32[]{:S(2)}) collective-permute-start(bf16[1024,384]{1,0:T(8,128)(2,1)S(1)} %pad_maximum_fusion.1), channel_id=1, source_target_pairs={{0,8},{8,0},{16,24},{24,16},{1,9},{9,1},{17,25},{25,17},{2,10},{10... | collective-permute-start | bytes 2359304 | tf_op jit(solution)/shard_map/ppermute | solution.py:98
  40.9 29.5 %collective-permute-start.7 = (bf16[384,768]{1,0:T(8,128)(2,1)S(1)}, bf16[384,768]{1,0:T(8,128)(2,1)S(1)}, u32[]{:S(2)}, u32[]{:S(2)}) collective-permute-start(bf16[384,768]{1,0:T(8,128)(2,1)S(1)} %copy-done.4), channel_id=1, source_target_pairs={{0,16},{8,24},{16,0},{24,8},{1,17},{9,25},{17,1},{25,9},{2,18},{10... | collective-permute-start | bytes 1769480 | tf_op jit(solution)/shard_map/ppermute | solution.py:98
  41.4 12.0 %collective-permute-start.16 = (bf16[2,192,512]{2,1,0:T(8,128)(2,1)S(1)}, bf16[2,192,512]{2,1,0:T(8,128)(2,1)S(1)}, u32[]{:S(2)}, u32[]{:S(2)}) collective-permute-start(bf16[2,192,512]{2,1,0:T(8,128)(2,1)S(1)} %collective-permute-done.10), channel_id=1, source_target_pairs={{0,4},{4,0},{1,5},{5,1},{2,6},{6,2},{3,7},{7,3},{8,12},{12,8},{9,1... | collective-permute-start | bytes 1179656 | tf_op jit(solution)/shard_map/ppermute | solution.py:98
  44.5 16.2 %collective-permute-start.17 = (bf16[2,192,512]{2,1,0:T(8,128)(2,1)S(1)}, bf16[2,192,512]{2,1,0:T(8,128)(2,1)S(1)}, u32[]{:S(2)}, u32[]{:S(2)}) collective-permute-start(bf16[2,192,512]{2,1,0:T(8,128)(2,1)S(1)} %collective-permute-done.15), channel_id=1, source_target_pairs={{0,4},{4,0},{1,5},{5,1},{2,6},{6,2},{3,7},{7,3},{8,12},{12,8},{9,1... | collective-permute-start | bytes 1179656 | tf_op jit(solution)/shard_map/ppermute | solution.py:98
  53.5 10.3 %collective-permute-start.11 = (bf16[1,192,512]{2,1,0:T(8,128)(2,1)}, bf16[1,192,512]{2,1,0:T(8,128)(2,1)S(1)}, u32[]{:S(2)}, u32[]{:S(2)}) collective-permute-start(bf16[1,192,512]{2,1,0:T(8,128)(2,1)} %get-tuple-element.25), channel_id=1, source_target_pairs={{0,2},{1,3},{2,0},{3,1},{4,6},{5,7},{6,4},{7,5},{8,10},{9,11},{10,... | collective-permute-start | bytes 589832 | tf_op jit(solution)/shard_map/ppermute | solution.py:101
  62.7 1.0 copy-start.7
  63.8 5.6 %copy-start.2 = (bf16[1024,192]{0,1:T(8,128)(2,1)S(1)}, bf16[1024,192]{0,1:T(8,128)(2,1)}, u32[]{:S(2)}) copy-start(bf16[1024,192]{0,1:T(8,128)(2,1)} %param.16) | copy-start | bytes 1179652
  63.8 9.7 %collective-permute-start.12 = (bf16[1,192,512]{2,1,0:T(8,128)(2,1)S(1)}, bf16[1,192,512]{2,1,0:T(8,128)(2,1)S(1)}, u32[]{:S(2)}, u32[]{:S(2)}) collective-permute-start(bf16[1,192,512]{2,1,0:T(8,128)(2,1)S(1)} %copy-done.7), channel_id=1, source_target_pairs={{0,1},{1,2},{2,3},{3,0},{4,5},{5,6},{6,7},{7,4},{8,9},{9,10},{10,1... | collective-permute-start | bytes 589832 | tf_op jit(solution)/shard_map/ppermute | solution.py:101
  64.2 11.3 %collective-permute-start.18 = (bf16[1,192,512]{2,1,0:T(8,128)(2,1)S(1)}, bf16[1,192,512]{2,1,0:T(8,128)(2,1)S(1)}, u32[]{:S(2)}, u32[]{:S(2)}) collective-permute-start(bf16[1,192,512]{2,1,0:T(8,128)(2,1)S(1)} %copy-done.7), channel_id=1, source_target_pairs={{0,3},{1,0},{2,1},{3,2},{4,7},{5,4},{6,5},{7,6},{8,11},{9,8},{10,9... | collective-permute-start | bytes 589832 | tf_op jit(solution)/shard_map/ppermute | solution.py:101
  67.7 8.4 %collective-permute-start.19 = (bf16[1,192,512]{2,1,0:T(8,128)(2,1)S(1)}, bf16[1,192,512]{2,1,0:T(8,128)(2,1)S(1)}, u32[]{:S(2)}, u32[]{:S(2)}) collective-permute-start(bf16[1,192,512]{2,1,0:T(8,128)(2,1)S(1)} %collective-permute-done.11), channel_id=1, source_target_pairs={{0,4},{4,0},{1,5},{5,1},{2,6},{6,2},{3,7},{7,3},{8,12},{12,8},{9,1... | collective-permute-start | bytes 589832 | tf_op jit(solution)/shard_map/ppermute | solution.py:98
  73.5 2.6 %collective-permute-start.13 = (bf16[384,768]{1,0:T(8,128)(2,1)S(1)}, bf16[384,768]{1,0:T(8,128)(2,1)S(1)}, u32[]{:S(2)}, u32[]{:S(2)}) collective-permute-start(bf16[384,768]{1,0:T(8,128)(2,1)S(1)} %copy-done.4), channel_id=1, source_target_pairs={{0,8},{8,0},{16,24},{24,16},{1,9},{9,1},{17,25},{25,17},{2,10},{10... | collective-permute-start | bytes 1769480 | tf_op jit(solution)/shard_map/ppermute | solution.py:98
  73.5 2.8 %collective-permute-start.14 = (bf16[384,768]{1,0:T(8,128)(2,1)S(1)}, bf16[384,768]{1,0:T(8,128)(2,1)S(1)}, u32[]{:S(2)}, u32[]{:S(2)}) collective-permute-start(bf16[384,768]{1,0:T(8,128)(2,1)S(1)} %collective-permute-done.7), channel_id=1, source_target_pairs={{0,8},{8,0},{16,24},{24,16},{1,9},{9,1},{17,25},{25,17},{2,10},{10... | collective-permute-start | bytes 1769480 | tf_op jit(solution)/shard_map/ppermute | solution.py:98
  74.0 8.1 %collective-permute-start.20 = (bf16[1,192,512]{2,1,0:T(8,128)(2,1)S(1)}, bf16[1,192,512]{2,1,0:T(8,128)(2,1)S(1)}, u32[]{:S(2)}, u32[]{:S(2)}) collective-permute-start(bf16[1,192,512]{2,1,0:T(8,128)(2,1)S(1)} %collective-permute-done.12), channel_id=1, source_target_pairs={{0,4},{4,0},{1,5},{5,1},{2,6},{6,2},{3,7},{7,3},{8,12},{12,8},{9,1... | collective-permute-start | bytes 589832 | tf_op jit(solution)/shard_map/ppermute | solution.py:98
  75.5 9.5 %collective-permute-start.21 = (bf16[1,192,512]{2,1,0:T(8,128)(2,1)S(1)}, bf16[1,192,512]{2,1,0:T(8,128)(2,1)S(1)}, u32[]{:S(2)}, u32[]{:S(2)}) collective-permute-start(bf16[1,192,512]{2,1,0:T(8,128)(2,1)S(1)} %collective-permute-done.18), channel_id=1, source_target_pairs={{0,4},{4,0},{1,5},{5,1},{2,6},{6,2},{3,7},{7,3},{8,12},{12,8},{9,1... | collective-permute-start | bytes 589832 | tf_op jit(solution)/shard_map/ppermute | solution.py:98
  80.7 4.8 %copy-start.6 = (bf16[1024,512]{1,0:T(8,128)(2,1)}, bf16[1024,512]{1,0:T(8,128)(2,1)S(1)}, u32[]{:S(2)}) copy-start(bf16[1024,512]{1,0:T(8,128)(2,1)S(1)} %multiply_convert_fusion) | copy-start | bytes 3145732
  85.5 0.9 copy-start.1
  87.9 2.5 %collective-permute-start.22 = (bf16[2,2,128,768]{3,2,1,0:T(8,128)(2,1)}, bf16[2,2,128,768]{3,2,1,0:T(8,128)(2,1)S(1)}, u32[]{:S(2)}, u32[]{:S(2)}) collective-permute-start(bf16[2,2,128,768]{3,2,1,0:T(8,128)(2,1)} %convolution_convert_fusion), channel_id=1, source_target_pairs={{0,8},{8,0},{16,24},{24,16},{1,9},{9,1},{17,25},{25,17},{2,10},{10... | collective-permute-start | bytes 2359304 | tf_op jit(solution)/shard_map/ppermute | solution.py:98
  90.5 12.7 %copy-start.9 = (f32[768]{0:T(1024)S(1)}, f32[768]{0:T(1024)}, u32[]{:S(2)}) copy-start(f32[768]{0:T(1024)} %param.18) | copy-start | bytes 9220
  90.5 26.8 %copy-start = (bf16[3,768,192]{1,2,0:T(8,128)(2,1)S(1)}, bf16[3,768,192]{1,2,0:T(8,128)(2,1)}, u32[]{:S(2)}) copy-start(bf16[3,768,192]{1,2,0:T(8,128)(2,1)} %param.19) | copy-start | bytes 2654212
  90.6 8.7 %collective-permute-start.25 = (bf16[128,768]{1,0:T(8,128)(2,1)S(1)}, bf16[128,768]{1,0:T(8,128)(2,1)S(1)}, u32[]{:S(2)}, u32[]{:S(2)}) collective-permute-start(bf16[128,768]{1,0:T(8,128)(2,1)S(1)} %get-tuple-element.50), channel_id=1, source_target_pairs={{0,17},{1,16},{2,19},{3,18},{8,25},{9,24},{10,27},{11,26},{16,1},{... | collective-permute-start | bytes 589832 | tf_op jit(solution)/shard_map/ppermute | solution.py:98
  90.7 12.1 %collective-permute-start.24 = (bf16[128,768]{1,0:T(8,128)(2,1)S(1)}, bf16[128,768]{1,0:T(8,128)(2,1)S(1)}, u32[]{:S(2)}, u32[]{:S(2)}) collective-permute-start(bf16[128,768]{1,0:T(8,128)(2,1)S(1)} %fusion.26), channel_id=1, source_target_pairs={{0,1},{1,0},{2,3},{3,2},{4,5},{5,4},{6,7},{7,6},{8,9},{9,8},{10,11... | collective-permute-start | bytes 589832 | tf_op jit(solution)/shard_map/ppermute | solution.py:98
  93.7 9.1 %collective-permute-start.23 = (bf16[128,768]{1,0:T(8,128)(2,1)S(1)}, bf16[128,768]{1,0:T(8,128)(2,1)S(1)}, u32[]{:S(2)}, u32[]{:S(2)}) collective-permute-start(bf16[128,768]{1,0:T(8,128)(2,1)S(1)} %get-tuple-element.49), channel_id=1, source_target_pairs={{0,16},{8,24},{16,0},{24,8},{1,17},{9,25},{17,1},{25,9},{2,18},{10... | collective-permute-start | bytes 589832 | tf_op jit(solution)/shard_map/ppermute | solution.py:98
  103.4 7.8 %collective-permute-start.26 = (bf16[128,768]{1,0:T(8,128)(2,1)S(1)}, bf16[128,768]{1,0:T(8,128)(2,1)S(1)}, u32[]{:S(2)}, u32[]{:S(2)}) collective-permute-start(bf16[128,768]{1,0:T(8,128)(2,1)S(1)} %multiply_convert_fusion.1.refs_0_), channel_id=1, source_target_pairs={{0,16},{8,24},{16,0},{24,8},{1,17},{9,25},{17,1},{25,9},{2,18},{10... | collective-permute-start | bytes 589832 | tf_op jit(solution)/shard_map/ppermute | solution.py:98
  104.9 10.8 %collective-permute-start.29 = (bf16[128,768]{1,0:T(8,128)(2,1)S(1)}, bf16[128,768]{1,0:T(8,128)(2,1)S(1)}, u32[]{:S(2)}, u32[]{:S(2)}) collective-permute-start(bf16[128,768]{1,0:T(8,128)(2,1)S(1)} %multiply_convert_fusion.1.refs_0_), channel_id=1, source_target_pairs={{0,4},{4,0},{1,5},{5,1},{2,6},{6,2},{3,7},{7,3},{8,12},{12,8},{9,1... | collective-permute-start | bytes 589832 | tf_op jit(solution)/shard_map/ppermute | solution.py:98
  106.4 9.3 %collective-permute-start.30 = (bf16[128,768]{1,0:T(8,128)(2,1)S(1)}, bf16[128,768]{1,0:T(8,128)(2,1)S(1)}, u32[]{:S(2)}, u32[]{:S(2)}) collective-permute-start(bf16[128,768]{1,0:T(8,128)(2,1)S(1)} %multiply_convert_fusion.1.refs_0_), channel_id=1, source_target_pairs={{0,20},{4,16},{8,28},{12,24},{16,4},{20,0},{24,12},{28,8},{1,21},{... | collective-permute-start | bytes 589832 | tf_op jit(solution)/shard_map/ppermute | solution.py:98
  106.9 9.2 %collective-permute-start.27 = (bf16[128,768]{1,0:T(8,128)(2,1)S(1)}, bf16[128,768]{1,0:T(8,128)(2,1)S(1)}, u32[]{:S(2)}, u32[]{:S(2)}) collective-permute-start(bf16[128,768]{1,0:T(8,128)(2,1)S(1)} %multiply_convert_fusion.1.refs_0_), channel_id=1, source_target_pairs={{0,8},{8,0},{16,24},{24,16},{1,9},{9,1},{17,25},{25,17},{2,10},{10... | collective-permute-start | bytes 589832 | tf_op jit(solution)/shard_map/ppermute | solution.py:98
  111.2 4.9 %collective-permute-start.28 = (bf16[128,768]{1,0:T(8,128)(2,1)S(1)}, bf16[128,768]{1,0:T(8,128)(2,1)S(1)}, u32[]{:S(2)}, u32[]{:S(2)}) collective-permute-start(bf16[128,768]{1,0:T(8,128)(2,1)S(1)} %collective-permute-done.26.refs_1_), channel_id=1, source_target_pairs={{0,8},{8,0},{16,24},{24,16},{1,9},{9,1},{17,25},{25,17},{2,10},{10... | collective-permute-start | bytes 589832 | tf_op jit(solution)/shard_map/ppermute | solution.py:98
  115.6 1.4 %collective-permute-start.31 = (bf16[128,768]{1,0:T(8,128)(2,1)S(1)}, bf16[128,768]{1,0:T(8,128)(2,1)S(1)}, u32[]{:S(2)}, u32[]{:S(2)}) collective-permute-start(bf16[128,768]{1,0:T(8,128)(2,1)S(1)} %collective-permute-done.29.refs_4_), channel_id=1, source_target_pairs={{0,8},{8,0},{16,24},{24,16},{1,9},{9,1},{17,25},{25,17},{2,10},{10... | collective-permute-start | bytes 589832 | tf_op jit(solution)/shard_map/ppermute | solution.py:98
  115.6 1.7 %collective-permute-start.32 = (bf16[128,768]{1,0:T(8,128)(2,1)S(1)}, bf16[128,768]{1,0:T(8,128)(2,1)S(1)}, u32[]{:S(2)}, u32[]{:S(2)}) collective-permute-start(bf16[128,768]{1,0:T(8,128)(2,1)S(1)} %collective-permute-done.30.refs_5_), channel_id=1, source_target_pairs={{0,8},{8,0},{16,24},{24,16},{1,9},{9,1},{17,25},{25,17},{2,10},{10... | collective-permute-start | bytes 589832 | tf_op jit(solution)/shard_map/ppermute | solution.py:98
  122.7 1.8 %collective-permute-start.33 = (bf16[2,192,512]{2,1,0:T(8,128)(2,1)S(1)}, bf16[2,192,512]{2,1,0:T(8,128)(2,1)S(1)}, u32[]{:S(2)}, u32[]{:S(2)}) collective-permute-start(bf16[2,192,512]{2,1,0:T(8,128)(2,1)S(1)} %get-tuple-element.36), channel_id=1, source_target_pairs={{0,8},{8,0},{16,24},{24,16},{1,9},{9,1},{17,25},{25,17},{2,10},{10... | collective-permute-start | bytes 1179656 | tf_op jit(solution)/shard_map/ppermute | solution.py:98
  124.6 7.1 %collective-permute-start.34 = (bf16[192,512]{1,0:T(8,128)(2,1)S(1)}, bf16[192,512]{1,0:T(8,128)(2,1)S(1)}, u32[]{:S(2)}, u32[]{:S(2)}) collective-permute-start(bf16[192,512]{1,0:T(8,128)(2,1)S(1)} %fusion.28), channel_id=1, source_target_pairs={{0,16},{8,24},{16,0},{24,8},{1,17},{9,25},{17,1},{25,9},{2,18},{10... | collective-permute-start | bytes 589832 | tf_op jit(solution)/shard_map/ppermute | solution.py:98

commit v16 on v15

--- a/solution.py
+++ b/solution.py
@@ -207,11 +207,11 @@
             across = after(jnp.concatenate([mine_x, beside_x], axis=0), g[0, 2], g[1, 2])
             both = after(jnp.concatenate([mine, beside], axis=0), across)
             both_c, across_c = flip(both, section=1), flip(across, section=1)
-            proj_x = flip(after(w_proj, across), section=2)
+            proj_x = flip(after(w_proj, both_c, across_c), section=2)
             far = rotate(after(down_same, g[0, 1]), 2)
             rows = jnp.concatenate([both, both_c, across, across_c], axis=1)
             normed = layer_norm(rows.astype(jnp.float32), gain).astype(jnp.bfloat16)
-            g[1, 1], g[1, 3] = flip(g[0, 1], seq=1), flip(g[0, 3], seq=1)
+            g[1, 1], g[1, 3] = (after(flip(g[0, k], seq=1), normed) for k in (1, 3))
             gate_up = place_rows(g)
             d[0, 2] = after(far, normed)
             for k in (1, 3):

time: 133 us -> 128 us (0.962)
  starting transfers between devices: 40.8 us -> 36.5 us
  waiting for transfers between devices: 57.7 us -> 60.7 us
  other arithmetic: 9.52 us -> 7.74 us
    ppermute x6, waiting for transfers between devices: 7.45 us -> 19.4 us  [rotate(): return lax.ppermute(x, 'dp', [(i, (i + k) % n_dp) for i in range(n_dp)])]
    ppermute x29, waiting for transfers between devices: 50.2 us -> 41.3 us  [flip(): return lax.ppermute(x, names if len(names) > 1 else names[0], pairs)]
    ppermute x29, starting transfers between devices: 28 us -> 24.2 us  [flip(): return lax.ppermute(x, names if len(names) > 1 else names[0], pairs)]
  transfers between devices with their start and end apart: 35 -> 35, of which waited for: 19 -> 22; matrix products, arithmetic and copies ran while one was open for 18% -> 17% of each run, Pallas kernels for 0% -> 0%
where the time goes in v16:
time: 128 us
  waiting for transfers between devices  60.7 us (47%)
  starting transfers between devices  36.5 us (29%)
  matrix products  8.78 us (7%)
  other arithmetic  7.74 us (6%)
  local copies, waits for them, and re-layouts  7.59 us (6%)
  Pallas kernels  5.34 us (4%)
    ppermute x29, waiting for transfers between devices, flip(): return lax.ppermute(x, names if len(names) > 1 else names[0], pairs)  41.3 us
    ppermute x29, starting transfers between devices, flip(): return lax.ppermute(x, names if len(names) > 1 else names[0], pairs)  24.2 us
    ppermute x6, waiting for transfers between devices, rotate(): return lax.ppermute(x, 'dp', [(i, (i + k) % n_dp) for i in range(n_dp)])  19.4 us
    ppermute x6, starting transfers between devices, rotate(): return lax.ppermute(x, 'dp', [(i, (i + k) % n_dp) for i in range(n_dp)])  12.3 us
    pallas_call x1, Pallas kernels, per_device(): pl.pallas_call(lambda *refs: attend_kernel(*refs, heads=local_heads, mask...  5.34 us
    dynamic_update_slice x14, local copies, waits for them, and re-layouts, place_rows(): whole = lax.dynamic_update_slice(whole, block, (0, row_of(y, k, rows), 0))  3.29 us
  transfers between devices with their start and end apart: 35, of which 22 were waited for; matrix products, arithmetic and copies ran while one was open for 17% of the time, Pallas kernels for 0%

profile of v16, /device:TPU:0, one launch (start us, length us, event | category | flops | bytes accessed | tf_op | source)
XLA Modules:
  0.0 127.7 jit_solution(4144050597628750922)
XLA Ops:
  0.0 3.1 %collective-permute-start = (bf16[512,384]{1,0:T(8,128)(2,1)}, bf16[512,384]{1,0:T(8,128)(2,1)S(1)}, u32[]{:S(2)}, u32[]{:S(2)}) collective-permute-start(bf16[512,384]{1,0:T(8,128)(2,1)} %bitcast.94), channel_id=1, source_target_pairs={{0,1},{1,0},{2,3},{3,2},{4,5},{5,4},{6,7},{7,6},{8,9},{9,8},{10,11... | collective-permute-start | bytes 1179656 | tf_op jit(solution)/shard_map/ppermute | solution.py:98
  3.1 1.5 %collective-permute-start.1 = (bf16[512,384]{1,0:T(8,128)(2,1)}, bf16[512,384]{1,0:T(8,128)(2,1)S(1)}, u32[]{:S(2)}, u32[]{:S(2)}) collective-permute-start(bf16[512,384]{1,0:T(8,128)(2,1)} %bitcast.95), channel_id=1, source_target_pairs={{0,16},{8,24},{16,0},{24,8},{1,17},{9,25},{17,1},{25,9},{2,18},{10... | collective-permute-start | bytes 1179656 | tf_op jit(solution)/shard_map/ppermute | solution.py:98
  4.6 1.3 %fusion.12 = (bf16[2,192,512]{2,1,0:T(8,128)(2,1)S(1)}, bf16[2,192,512]{2,1,0:T(8,128)(2,1)S(1)}) fusion(s32[]{:T(128)S(6)} %select_n.238, bf16[1,192,1024]{2,1,0:T(8,128)(2,1)} %bitcast.92, bf16[1,192,1024]{2,1,0:T(8,128)(2,1)} %bitcast.93, s32[]{:T(128)S(6)} %select_n.236), kind=kLoop, calls=%fused_computation.28 | loop fusion | flops 1572864 | bytes 1572872 | tf_op jit(solution)/shard_map/stack | solution.py:163
  5.9 2.7 %collective-permute-start.3 = (bf16[2,192,512]{2,1,0:T(8,128)(2,1)S(1)}, bf16[2,192,512]{2,1,0:T(8,128)(2,1)}, u32[]{:S(2)}, u32[]{:S(2)}) collective-permute-start(bf16[2,192,512]{2,1,0:T(8,128)(2,1)S(1)} %get-tuple-element.52), channel_id=1, source_target_pairs={{0,2},{1,3},{2,0},{3,1},{4,6},{5,7},{6,4},{7,5},{8,10},{9,11},{10,... | collective-permute-start | bytes 1179656 | tf_op jit(solution)/shard_map/ppermute | solution.py:101
  8.6 1.5 %collective-permute-start.9 = (bf16[2,192,512]{2,1,0:T(8,128)(2,1)S(1)}, bf16[2,192,512]{2,1,0:T(8,128)(2,1)S(1)}, u32[]{:S(2)}, u32[]{:S(2)}) collective-permute-start(bf16[2,192,512]{2,1,0:T(8,128)(2,1)S(1)} %get-tuple-element.52), channel_id=1, source_target_pairs={{0,4},{4,0},{1,5},{5,1},{2,6},{6,2},{3,7},{7,3},{8,12},{12,8},{9,1... | collective-permute-start | bytes 1179656 | tf_op jit(solution)/shard_map/ppermute | solution.py:98
  10.1 1.8 %dynamic-slice_bitcast_fusion.2 = (bf16[1,192,512]{2,1,0:T(8,128)(2,1)}, bf16[1,192,512]{2,1,0:T(8,128)(2,1)}) fusion(bf16[1024,192]{0,1:T(8,128)(2,1)} %param.16, s32[]{:T(128)S(6)} %select_n.236, s32[]{:T(128)S(6)} %select_n.238), kind=kLoop, calls=%fused_computation.61 | loop fusion | bytes 786440 | tf_op jit(solution)/shard_map/dynamic_slice | solution.py:161
  13.8 4.6 %collective-permute-done = bf16[512,384]{1,0:T(8,128)(2,1)S(1)} collective-permute-done((bf16[512,384]{1,0:T(8,128)(2,1)}, bf16[512,384]{1,0:T(8,128)(2,1)S(1)}, u32[]{:S(2)}, u32[]{:S(2)}) %collective-permute-start) | collective-permute-done | bytes 393248 | tf_op jit(solution)/shard_map/ppermute | solution.py:98
  18.4 2.6 %collective-permute-start.2 = (bf16[512,384]{1,0:T(8,128)(2,1)S(1)}, bf16[512,384]{1,0:T(8,128)(2,1)}, u32[]{:S(2)}, u32[]{:S(2)}) collective-permute-start(bf16[512,384]{1,0:T(8,128)(2,1)S(1)} %collective-permute-done), channel_id=1, source_target_pairs={{0,16},{8,24},{16,0},{24,8},{1,17},{9,25},{17,1},{25,9},{2,18},{10... | collective-permute-start | bytes 1179656 | tf_op jit(solution)/shard_map/ppermute | solution.py:98
  21.4 4.4 %collective-permute-done.3 = bf16[2,192,512]{2,1,0:T(8,128)(2,1)} collective-permute-done((bf16[2,192,512]{2,1,0:T(8,128)(2,1)S(1)}, bf16[2,192,512]{2,1,0:T(8,128)(2,1)}, u32[]{:S(2)}, u32[]{:S(2)}) %collective-permute-start.3) | collective-permute-done | bytes 393248 | tf_op jit(solution)/shard_map/ppermute | solution.py:101
  25.8 1.5 %collective-permute-start.4 = (bf16[2,192,512]{2,1,0:T(8,128)(2,1)}, bf16[2,192,512]{2,1,0:T(8,128)(2,1)}, u32[]{:S(2)}, u32[]{:S(2)}) collective-permute-start(bf16[2,192,512]{2,1,0:T(8,128)(2,1)} %collective-permute-done.3), channel_id=1, source_target_pairs={{0,4},{4,0},{1,5},{5,1},{2,6},{6,2},{3,7},{7,3},{8,12},{12,8},{9,1... | collective-permute-start | bytes 1179656 | tf_op jit(solution)/shard_map/ppermute | solution.py:98
  27.3 1.1 copy.14
  28.6 3.8 %collective-permute-start.15 = (bf16[2,192,512]{2,1,0:T(8,128)(2,1)S(1)}, bf16[2,192,512]{2,1,0:T(8,128)(2,1)S(1)}, u32[]{:S(2)}, u32[]{:S(2)}) collective-permute-start(bf16[2,192,512]{2,1,0:T(8,128)(2,1)S(1)} %get-tuple-element.26), channel_id=1, source_target_pairs={{0,3},{1,0},{2,1},{3,2},{4,7},{5,4},{6,5},{7,6},{8,11},{9,8},{10,9... | collective-permute-start | bytes 1179656 | tf_op jit(solution)/shard_map/ppermute | solution.py:101
  32.5 1.1 pad_maximum_fusion.1
  33.6 1.9 %collective-permute-done.4 = bf16[2,192,512]{2,1,0:T(8,128)(2,1)} collective-permute-done((bf16[2,192,512]{2,1,0:T(8,128)(2,1)}, bf16[2,192,512]{2,1,0:T(8,128)(2,1)}, u32[]{:S(2)}, u32[]{:S(2)}) %collective-permute-start.4) | collective-permute-done | bytes 393248 | tf_op jit(solution)/shard_map/ppermute | solution.py:98
  35.8 1.0 constant_dynamic-update-slice_fusion.17
  37.4 5.1 %collective-permute-done.10 = bf16[2,192,512]{2,1,0:T(8,128)(2,1)S(1)} collective-permute-done((bf16[2,192,512]{2,1,0:T(8,128)(2,1)S(1)}, bf16[2,192,512]{2,1,0:T(8,128)(2,1)S(1)}, u32[]{:S(2)}, u32[]{:S(2)}) %collective-permute-start.10) | collective-permute-done | bytes 393248 | tf_op jit(solution)/shard_map/ppermute | solution.py:101
  42.5 1.9 %collective-permute-start.11 = (bf16[1,192,512]{2,1,0:T(8,128)(2,1)}, bf16[1,192,512]{2,1,0:T(8,128)(2,1)S(1)}, u32[]{:S(2)}, u32[]{:S(2)}) collective-permute-start(bf16[1,192,512]{2,1,0:T(8,128)(2,1)} %get-tuple-element.27), channel_id=1, source_target_pairs={{0,2},{1,3},{2,0},{3,1},{4,6},{5,7},{6,4},{7,5},{8,10},{9,11},{10,... | collective-permute-start | bytes 589832 | tf_op jit(solution)/shard_map/ppermute | solution.py:101
  44.9 1.3 %collective-permute-done.15 = bf16[2,192,512]{2,1,0:T(8,128)(2,1)S(1)} collective-permute-done((bf16[2,192,512]{2,1,0:T(8,128)(2,1)S(1)}, bf16[2,192,512]{2,1,0:T(8,128)(2,1)S(1)}, u32[]{:S(2)}, u32[]{:S(2)}) %collective-permute-start.15) | collective-permute-done | bytes 393248 | tf_op jit(solution)/shard_map/ppermute | solution.py:101
  46.8 1.0 constant_dynamic-update-slice_fusion.13
  49.0 1.0 fusion.2
  50.0 1.0 fusion.4
  51.0 4.7 %collective-permute-done.11 = bf16[1,192,512]{2,1,0:T(8,128)(2,1)S(1)} collective-permute-done((bf16[1,192,512]{2,1,0:T(8,128)(2,1)}, bf16[1,192,512]{2,1,0:T(8,128)(2,1)S(1)}, u32[]{:S(2)}, u32[]{:S(2)}) %collective-permute-start.11) | collective-permute-done | bytes 196640 | tf_op jit(solution)/shard_map/ppermute | solution.py:101
  55.6 2.1 %collective-permute-start.12 = (bf16[1,192,512]{2,1,0:T(8,128)(2,1)S(1)}, bf16[1,192,512]{2,1,0:T(8,128)(2,1)S(1)}, u32[]{:S(2)}, u32[]{:S(2)}) collective-permute-start(bf16[1,192,512]{2,1,0:T(8,128)(2,1)S(1)} %copy-done.5), channel_id=1, source_target_pairs={{0,1},{1,2},{2,3},{3,0},{4,5},{5,6},{6,7},{7,4},{8,9},{9,10},{10,1... | collective-permute-start | bytes 589832 | tf_op jit(solution)/shard_map/ppermute | solution.py:101
  57.7 1.7 %collective-permute-start.18 = (bf16[1,192,512]{2,1,0:T(8,128)(2,1)S(1)}, bf16[1,192,512]{2,1,0:T(8,128)(2,1)S(1)}, u32[]{:S(2)}, u32[]{:S(2)}) collective-permute-start(bf16[1,192,512]{2,1,0:T(8,128)(2,1)S(1)} %copy-done.5), channel_id=1, source_target_pairs={{0,3},{1,0},{2,1},{3,2},{4,7},{5,4},{6,5},{7,6},{8,11},{9,8},{10,9... | collective-permute-start | bytes 589832 | tf_op jit(solution)/shard_map/ppermute | solution.py:101
  60.6 0.9 bitcast_dynamic-update-slice_fusion.4
  61.6 3.7 %collective-permute-done.12 = bf16[1,192,512]{2,1,0:T(8,128)(2,1)S(1)} collective-permute-done((bf16[1,192,512]{2,1,0:T(8,128)(2,1)S(1)}, bf16[1,192,512]{2,1,0:T(8,128)(2,1)S(1)}, u32[]{:S(2)}, u32[]{:S(2)}) %collective-permute-start.12) | collective-permute-done | bytes 196640 | tf_op jit(solution)/shard_map/ppermute | solution.py:101
  66.1 1.2 collective-permute-start.21
  67.3 6.4 %collective-permute-done.7 = bf16[384,768]{1,0:T(8,128)(2,1)S(1)} collective-permute-done((bf16[384,768]{1,0:T(8,128)(2,1)S(1)}, bf16[384,768]{1,0:T(8,128)(2,1)S(1)}, u32[]{:S(2)}, u32[]{:S(2)}) %collective-permute-start.7) | collective-permute-done | bytes 589856 | tf_op jit(solution)/shard_map/ppermute | solution.py:98
  74.4 1.3 %collective-permute-done.13 = bf16[384,768]{1,0:T(8,128)(2,1)S(1)} collective-permute-done((bf16[384,768]{1,0:T(8,128)(2,1)S(1)}, bf16[384,768]{1,0:T(8,128)(2,1)S(1)}, u32[]{:S(2)}, u32[]{:S(2)}) %collective-permute-start.13) | collective-permute-done | bytes 589856 | tf_op jit(solution)/shard_map/ppermute | solution.py:98
  77.1 1.8 %fusion.5 = f32[1024,512]{1,0:T(8,128)S(1)} fusion(bf16[1024,1536]{1,0:T(8,128)(2,1)S(1)} %fusion.4, bf16[2,1536,512]{2,1,0:T(8,128)(2,1)S(1)} %constant_dynamic-update-slice_fusion.11), kind=kOutput, calls=%fused_computation.10 | convolution fusion | flops 1610612736 | bytes 6815744 | tf_op jit(solution)/shard_map/dot_general | solution.py:238
  78.9 2.0 %multiply_convert_fusion = bf16[1024,512]{1,0:T(8,128)(2,1)S(1)} fusion(f32[1024,512]{1,0:T(8,128)S(1)} %fusion.5, bf16[1024,1536]{1,0:T(8,128)(2,1)S(1)} %fusion.4, bf16[2,1536,512]{2,1,0:T(8,128)(2,1)S(1)} %constant_dynamic-update-slice_fusion.11), kind=kOutput, calls=%fused_computation.7 | convolution fusion | flops 1613758464 | bytes 7864320 | tf_op jit(solution)/shard_map/dot_general | solution.py:239
  80.9 1.4 %fusion.51 = f32[768,512]{1,0:T(8,128)S(1)} fusion(bf16[1536,768]{1,0:T(8,128)(2,1)S(1)} %constant_dynamic-update-slice_fusion.5, bf16[1536,512]{1,0:T(8,128)(2,1)S(1)} %bitcast_dynamic-update-slice_fusion), kind=kOutput, calls=%fused_computation.129 | convolution fusion | flops 1207959552 | bytes 5505024 | tf_op jit(solution)/shard_map/dot_general | solution.py:244
  84.0 1.6 %fusion.8 = f32[2,2,128,768]{3,2,1,0:T(8,128)S(1)} fusion(bf16[768,512,1,1]{1,0,3,2:T(8,128)(2,1)S(1)} %fusion.6, bf16[2,2,2,128,512]{4,3,2,1,0:T(8,128)(2,1)} %bitcast.98, s32[]{:T(128)S(6)} %select_n.278), kind=kOutput, calls=%fused_computation.24 | convolution fusion | flops 402653184 | bytes 2883588 | tf_op jit(solution)/shard_map/dot_general | solution.py:261
  86.6 2.6 %collective-permute-start.24 = (bf16[128,768]{1,0:T(8,128)(2,1)S(1)}, bf16[128,768]{1,0:T(8,128)(2,1)S(1)}, u32[]{:S(2)}, u32[]{:S(2)}) collective-permute-start(bf16[128,768]{1,0:T(8,128)(2,1)S(1)} %fusion.25), channel_id=1, source_target_pairs={{0,1},{1,0},{2,3},{3,2},{4,5},{5,4},{6,7},{7,6},{8,9},{9,8},{10,11... | collective-permute-start | bytes 589832 | tf_op jit(solution)/shard_map/ppermute | solution.py:98
  89.2 0.9 collective-permute-start.23
  90.1 5.1 %collective-permute-done.25 = bf16[128,768]{1,0:T(8,128)(2,1)S(1)} collective-permute-done((bf16[128,768]{1,0:T(8,128)(2,1)S(1)}, bf16[128,768]{1,0:T(8,128)(2,1)S(1)}, u32[]{:S(2)}, u32[]{:S(2)}) %collective-permute-start.25) | collective-permute-done | bytes 196640 | tf_op jit(solution)/shard_map/ppermute | solution.py:98
  95.2 3.0 %collective-permute-done.24 = bf16[128,768]{1,0:T(8,128)(2,1)S(1)} collective-permute-done((bf16[128,768]{1,0:T(8,128)(2,1)S(1)}, bf16[128,768]{1,0:T(8,128)(2,1)S(1)}, u32[]{:S(2)}, u32[]{:S(2)}) %collective-permute-start.24) | collective-permute-done | bytes 196640 | tf_op jit(solution)/shard_map/ppermute | solution.py:98
  99.2 1.2 collective-permute-start.26
  100.3 1.5 %collective-permute-start.29 = (bf16[128,768]{1,0:T(8,128)(2,1)S(1)}, bf16[128,768]{1,0:T(8,128)(2,1)S(1)}, u32[]{:S(2)}, u32[]{:S(2)}) collective-permute-start(bf16[128,768]{1,0:T(8,128)(2,1)S(1)} %multiply_convert_fusion.1.refs_0_), channel_id=1, source_target_pairs={{0,4},{4,0},{1,5},{5,1},{2,6},{6,2},{3,7},{7,3},{8,12},{12,8},{9,1... | collective-permute-start | bytes 589832 | tf_op jit(solution)/shard_map/ppermute | solution.py:98
  101.8 0.9 collective-permute-start.30
  102.7 4.3 %collective-permute-done.26.refs_1_ = bf16[128,768]{1,0:T(8,128)(2,1)S(1)} collective-permute-done((bf16[128,768]{1,0:T(8,128)(2,1)S(1)}, bf16[128,768]{1,0:T(8,128)(2,1)S(1)}, u32[]{:S(2)}, u32[]{:S(2)}) %collective-permute-start.26) | collective-permute-done | bytes 196640 | tf_op jit(solution)/shard_map/ppermute | solution.py:98
  107.0 3.1 %collective-permute-done.29.refs_4_ = bf16[128,768]{1,0:T(8,128)(2,1)S(1)} collective-permute-done((bf16[128,768]{1,0:T(8,128)(2,1)S(1)}, bf16[128,768]{1,0:T(8,128)(2,1)S(1)}, u32[]{:S(2)}, u32[]{:S(2)}) %collective-permute-start.29) | collective-permute-done | bytes 196640 | tf_op jit(solution)/shard_map/ppermute | solution.py:98
  110.1 1.1 collective-permute-done.30.refs_5_
  111.6 1.1 collective-permute-done.32.refs_7_
  112.7 5.3 %shard_map.118 = (f32[2,192,512]{2,1,0:T(8,128)S(1)}, bf16[2,192,512]{2,1,0:T(8,128)(2,1)S(1)}) custom-call(bf16[128,768]{1,0:T(8,128)(2,1)S(1)} %multiply_convert_fusion.1.refs_0_, bf16[128,768]{1,0:T(8,128)(2,1)S(1)} %collective-permute-done.26.refs_1_, bf16[128,768]{1,0:T(8,128)(2,1)S(1)} %collective-permute-done.27.refs_2_, ...), custom_call_target="tpu_custom_call" | custom-call | flops 2516582400 | bytes 8388608 | tf_op jit(solution)/shard_map/pallas_call | solution.py:299
  118.2 1.6 %collective-permute-done.33 = bf16[2,192,512]{2,1,0:T(8,128)(2,1)S(1)} collective-permute-done((bf16[2,192,512]{2,1,0:T(8,128)(2,1)S(1)}, bf16[2,192,512]{2,1,0:T(8,128)(2,1)S(1)}, u32[]{:S(2)}, u32[]{:S(2)}) %collective-permute-start.33) | collective-permute-done | bytes 393248 | tf_op jit(solution)/shard_map/ppermute | solution.py:98
  119.9 1.2 collective-permute-start.34
  121.1 5.8 %collective-permute-done.34 = bf16[192,512]{1,0:T(8,128)(2,1)S(1)} collective-permute-done((bf16[192,512]{1,0:T(8,128)(2,1)S(1)}, bf16[192,512]{1,0:T(8,128)(2,1)S(1)}, u32[]{:S(2)}, u32[]{:S(2)}) %collective-permute-start.34) | collective-permute-done | bytes 196640 | tf_op jit(solution)/shard_map/ppermute | solution.py:98
  (125 shorter events, 13.7 us)
Async XLA Ops:
  0.0 12.4 %copy-start.10 = (s32[1,3]{1,0:T(1,128)S(1)}, s32[1,3]{1,0:T(1,128)}, u32[]{:S(2)}) copy-start(s32[1,3]{1,0:T(1,128)} %param.21) | copy-start | bytes 40
  0.0 12.6 %copy-start.8 = (s32[4]{0:T(128)S(1)}, s32[4]{0:T(128)}, u32[]{:S(2)}) copy-start(s32[4]{0:T(128)} %param.22) | copy-start | bytes 52
  0.0 12.6 %copy-start.9 = (s32[4]{0:T(128)S(1)}, s32[4]{0:T(128)}, u32[]{:S(2)}) copy-start(s32[4]{0:T(128)} %param.23) | copy-start | bytes 52
  0.0 13.7 %copy-start.6 = (f32[1536]{0:T(1024)S(1)}, f32[1536]{0:T(1024)}, u32[]{:S(2)}) copy-start(f32[1536]{0:T(1024)} %param.13) | copy-start | bytes 18436
  0.0 28.5 %copy-start.2 = (bf16[384,768]{1,0:T(8,128)(2,1)S(1)}, bf16[384,768]{1,0:T(8,128)(2,1)}, u32[]{:S(2)}) copy-start(bf16[384,768]{1,0:T(8,128)(2,1)} %param.17) | copy-start | bytes 1769476
  0.0 18.4 %collective-permute-start = (bf16[512,384]{1,0:T(8,128)(2,1)}, bf16[512,384]{1,0:T(8,128)(2,1)S(1)}, u32[]{:S(2)}, u32[]{:S(2)}) collective-permute-start(bf16[512,384]{1,0:T(8,128)(2,1)} %bitcast.94), channel_id=1, source_target_pairs={{0,1},{1,0},{2,3},{3,2},{4,5},{5,4},{6,7},{7,6},{8,9},{9,8},{10,11... | collective-permute-start | bytes 1179656 | tf_op jit(solution)/shard_map/ppermute | solution.py:98
  3.1 25.4 %collective-permute-start.1 = (bf16[512,384]{1,0:T(8,128)(2,1)}, bf16[512,384]{1,0:T(8,128)(2,1)S(1)}, u32[]{:S(2)}, u32[]{:S(2)}) collective-permute-start(bf16[512,384]{1,0:T(8,128)(2,1)} %bitcast.95), channel_id=1, source_target_pairs={{0,16},{8,24},{16,0},{24,8},{1,17},{9,25},{17,1},{25,9},{2,18},{10... | collective-permute-start | bytes 1179656 | tf_op jit(solution)/shard_map/ppermute | solution.py:98
  4.6 27.8 %copy-start.3 = (bf16[1,512,384]{2,1,0:T(8,128)(2,1)S(1)}, bf16[1,512,384]{2,1,0:T(8,128)(2,1)}, u32[]{:S(2)}) copy-start(bf16[1,512,384]{2,1,0:T(8,128)(2,1)} %param.12) | copy-start | bytes 1179652
  5.9 19.8 %collective-permute-start.3 = (bf16[2,192,512]{2,1,0:T(8,128)(2,1)S(1)}, bf16[2,192,512]{2,1,0:T(8,128)(2,1)}, u32[]{:S(2)}, u32[]{:S(2)}) collective-permute-start(bf16[2,192,512]{2,1,0:T(8,128)(2,1)S(1)} %get-tuple-element.52), channel_id=1, source_target_pairs={{0,2},{1,3},{2,0},{3,1},{4,6},{5,7},{6,4},{7,5},{8,10},{9,11},{10,... | collective-permute-start | bytes 1179656 | tf_op jit(solution)/shard_map/ppermute | solution.py:101
  8.6 20.0 %collective-permute-start.9 = (bf16[2,192,512]{2,1,0:T(8,128)(2,1)S(1)}, bf16[2,192,512]{2,1,0:T(8,128)(2,1)S(1)}, u32[]{:S(2)}, u32[]{:S(2)}) collective-permute-start(bf16[2,192,512]{2,1,0:T(8,128)(2,1)S(1)} %get-tuple-element.52), channel_id=1, source_target_pairs={{0,4},{4,0},{1,5},{5,1},{2,6},{6,2},{3,7},{7,3},{8,12},{12,8},{9,1... | collective-permute-start | bytes 1179656 | tf_op jit(solution)/shard_map/ppermute | solution.py:98
  11.9 16.6 %collective-permute-start.8 = (bf16[1,192,512]{2,1,0:T(8,128)(2,1)}, bf16[1,192,512]{2,1,0:T(8,128)(2,1)}, u32[]{:S(2)}, u32[]{:S(2)}) collective-permute-start(bf16[1,192,512]{2,1,0:T(8,128)(2,1)} %get-tuple-element.27), channel_id=1, source_target_pairs={{0,4},{4,0},{1,5},{5,1},{2,6},{6,2},{3,7},{7,3},{8,12},{12,8},{9,1... | collective-permute-start | bytes 589832 | tf_op jit(solution)/shard_map/ppermute | solution.py:98
  18.4 14.2 %collective-permute-start.2 = (bf16[512,384]{1,0:T(8,128)(2,1)S(1)}, bf16[512,384]{1,0:T(8,128)(2,1)}, u32[]{:S(2)}, u32[]{:S(2)}) collective-permute-start(bf16[512,384]{1,0:T(8,128)(2,1)S(1)} %collective-permute-done), channel_id=1, source_target_pairs={{0,16},{8,24},{16,0},{24,8},{1,17},{9,25},{17,1},{25,9},{2,18},{10... | collective-permute-start | bytes 1179656 | tf_op jit(solution)/shard_map/ppermute | solution.py:98
  25.8 9.7 %collective-permute-start.4 = (bf16[2,192,512]{2,1,0:T(8,128)(2,1)}, bf16[2,192,512]{2,1,0:T(8,128)(2,1)}, u32[]{:S(2)}, u32[]{:S(2)}) collective-permute-start(bf16[2,192,512]{2,1,0:T(8,128)(2,1)} %collective-permute-done.3), channel_id=1, source_target_pairs={{0,4},{4,0},{1,5},{5,1},{2,6},{6,2},{3,7},{7,3},{8,12},{12,8},{9,1... | collective-permute-start | bytes 1179656 | tf_op jit(solution)/shard_map/ppermute | solution.py:98
  28.6 13.9 %collective-permute-start.10 = (bf16[2,192,512]{2,1,0:T(8,128)(2,1)S(1)}, bf16[2,192,512]{2,1,0:T(8,128)(2,1)S(1)}, u32[]{:S(2)}, u32[]{:S(2)}) collective-permute-start(bf16[2,192,512]{2,1,0:T(8,128)(2,1)S(1)} %get-tuple-element.26), channel_id=1, source_target_pairs={{0,1},{1,2},{2,3},{3,0},{4,5},{5,6},{6,7},{7,4},{8,9},{9,10},{10,1... | collective-permute-start | bytes 1179656 | tf_op jit(solution)/shard_map/ppermute | solution.py:101
  28.6 17.6 %collective-permute-start.15 = (bf16[2,192,512]{2,1,0:T(8,128)(2,1)S(1)}, bf16[2,192,512]{2,1,0:T(8,128)(2,1)S(1)}, u32[]{:S(2)}, u32[]{:S(2)}) collective-permute-start(bf16[2,192,512]{2,1,0:T(8,128)(2,1)S(1)} %get-tuple-element.26), channel_id=1, source_target_pairs={{0,3},{1,0},{2,1},{3,2},{4,7},{5,4},{6,5},{7,6},{8,11},{9,8},{10,9... | collective-permute-start | bytes 1179656 | tf_op jit(solution)/shard_map/ppermute | solution.py:101
  35.5 12.5 %collective-permute-start.5 = (bf16[1024,384]{1,0:T(8,128)(2,1)S(1)}, bf16[1024,384]{1,0:T(8,128)(2,1)S(1)}, u32[]{:S(2)}, u32[]{:S(2)}) collective-permute-start(bf16[1024,384]{1,0:T(8,128)(2,1)S(1)} %pad_maximum_fusion), channel_id=1, source_target_pairs={{0,8},{8,0},{16,24},{24,16},{1,9},{9,1},{17,25},{25,17},{2,10},{10... | collective-permute-start | bytes 2359304 | tf_op jit(solution)/shard_map/ppermute | solution.py:98
  36.8 11.5 %collective-permute-start.6 = (bf16[1024,384]{1,0:T(8,128)(2,1)S(1)}, bf16[1024,384]{1,0:T(8,128)(2,1)S(1)}, u32[]{:S(2)}, u32[]{:S(2)}) collective-permute-start(bf16[1024,384]{1,0:T(8,128)(2,1)S(1)} %pad_maximum_fusion.1), channel_id=1, source_target_pairs={{0,8},{8,0},{16,24},{24,16},{1,9},{9,1},{17,25},{25,17},{2,10},{10... | collective-permute-start | bytes 2359304 | tf_op jit(solution)/shard_map/ppermute | solution.py:98
  42.5 13.2 %collective-permute-start.11 = (bf16[1,192,512]{2,1,0:T(8,128)(2,1)}, bf16[1,192,512]{2,1,0:T(8,128)(2,1)S(1)}, u32[]{:S(2)}, u32[]{:S(2)}) collective-permute-start(bf16[1,192,512]{2,1,0:T(8,128)(2,1)} %get-tuple-element.27), channel_id=1, source_target_pairs={{0,2},{1,3},{2,0},{3,1},{4,6},{5,7},{6,4},{7,5},{8,10},{9,11},{10,... | collective-permute-start | bytes 589832 | tf_op jit(solution)/shard_map/ppermute | solution.py:101
  44.4 15.7 %collective-permute-start.16 = (bf16[2,192,512]{2,1,0:T(8,128)(2,1)S(1)}, bf16[2,192,512]{2,1,0:T(8,128)(2,1)S(1)}, u32[]{:S(2)}, u32[]{:S(2)}) collective-permute-start(bf16[2,192,512]{2,1,0:T(8,128)(2,1)S(1)} %collective-permute-done.10), channel_id=1, source_target_pairs={{0,4},{4,0},{1,5},{5,1},{2,6},{6,2},{3,7},{7,3},{8,12},{12,8},{9,1... | collective-permute-start | bytes 1179656 | tf_op jit(solution)/shard_map/ppermute | solution.py:98
  46.2 14.3 %collective-permute-start.17 = (bf16[2,192,512]{2,1,0:T(8,128)(2,1)S(1)}, bf16[2,192,512]{2,1,0:T(8,128)(2,1)S(1)}, u32[]{:S(2)}, u32[]{:S(2)}) collective-permute-start(bf16[2,192,512]{2,1,0:T(8,128)(2,1)S(1)} %collective-permute-done.15), channel_id=1, source_target_pairs={{0,4},{4,0},{1,5},{5,1},{2,6},{6,2},{3,7},{7,3},{8,12},{12,8},{9,1... | collective-permute-start | bytes 1179656 | tf_op jit(solution)/shard_map/ppermute | solution.py:98
  49.9 5.7 %copy-start.5 = (bf16[1,192,512]{2,1,0:T(8,128)(2,1)S(1)}, bf16[1,192,512]{2,1,0:T(8,128)(2,1)}, u32[]{:S(2)}) copy-start(bf16[1,192,512]{2,1,0:T(8,128)(2,1)} %get-tuple-element.29) | copy-start | bytes 589828
  55.6 4.9 %copy-start.1 = (bf16[1024,192]{0,1:T(8,128)(2,1)S(1)}, bf16[1024,192]{0,1:T(8,128)(2,1)}, u32[]{:S(2)}) copy-start(bf16[1024,192]{0,1:T(8,128)(2,1)} %param.16) | copy-start | bytes 1179652
  55.6 9.6 %collective-permute-start.12 = (bf16[1,192,512]{2,1,0:T(8,128)(2,1)S(1)}, bf16[1,192,512]{2,1,0:T(8,128)(2,1)S(1)}, u32[]{:S(2)}, u32[]{:S(2)}) collective-permute-start(bf16[1,192,512]{2,1,0:T(8,128)(2,1)S(1)} %copy-done.5), channel_id=1, source_target_pairs={{0,1},{1,2},{2,3},{3,0},{4,5},{5,6},{6,7},{7,4},{8,9},{9,10},{10,1... | collective-permute-start | bytes 589832 | tf_op jit(solution)/shard_map/ppermute | solution.py:101
  57.7 8.3 %collective-permute-start.18 = (bf16[1,192,512]{2,1,0:T(8,128)(2,1)S(1)}, bf16[1,192,512]{2,1,0:T(8,128)(2,1)S(1)}, u32[]{:S(2)}, u32[]{:S(2)}) collective-permute-start(bf16[1,192,512]{2,1,0:T(8,128)(2,1)S(1)} %copy-done.5), channel_id=1, source_target_pairs={{0,3},{1,0},{2,1},{3,2},{4,7},{5,4},{6,5},{7,6},{8,11},{9,8},{10,9... | collective-permute-start | bytes 589832 | tf_op jit(solution)/shard_map/ppermute | solution.py:101
  59.5 14.9 %collective-permute-start.19 = (bf16[1,192,512]{2,1,0:T(8,128)(2,1)S(1)}, bf16[1,192,512]{2,1,0:T(8,128)(2,1)S(1)}, u32[]{:S(2)}, u32[]{:S(2)}) collective-permute-start(bf16[1,192,512]{2,1,0:T(8,128)(2,1)S(1)} %collective-permute-done.11), channel_id=1, source_target_pairs={{0,4},{4,0},{1,5},{5,1},{2,6},{6,2},{3,7},{7,3},{8,12},{12,8},{9,1... | collective-permute-start | bytes 589832 | tf_op jit(solution)/shard_map/ppermute | solution.py:98
  60.1 13.6 %collective-permute-start.7 = (bf16[384,768]{1,0:T(8,128)(2,1)S(1)}, bf16[384,768]{1,0:T(8,128)(2,1)S(1)}, u32[]{:S(2)}, u32[]{:S(2)}) collective-permute-start(bf16[384,768]{1,0:T(8,128)(2,1)S(1)} %copy-done.2), channel_id=1, source_target_pairs={{0,16},{8,24},{16,0},{24,8},{1,17},{9,25},{17,1},{25,9},{2,18},{10... | collective-permute-start | bytes 1769480 | tf_op jit(solution)/shard_map/ppermute | solution.py:98
  65.3 17.0 %collective-permute-start.20 = (bf16[1,192,512]{2,1,0:T(8,128)(2,1)S(1)}, bf16[1,192,512]{2,1,0:T(8,128)(2,1)S(1)}, u32[]{:S(2)}, u32[]{:S(2)}) collective-permute-start(bf16[1,192,512]{2,1,0:T(8,128)(2,1)S(1)} %collective-permute-done.12), channel_id=1, source_target_pairs={{0,4},{4,0},{1,5},{5,1},{2,6},{6,2},{3,7},{7,3},{8,12},{12,8},{9,1... | collective-permute-start | bytes 589832 | tf_op jit(solution)/shard_map/ppermute | solution.py:98
  66.1 16.7 %collective-permute-start.21 = (bf16[1,192,512]{2,1,0:T(8,128)(2,1)S(1)}, bf16[1,192,512]{2,1,0:T(8,128)(2,1)S(1)}, u32[]{:S(2)}, u32[]{:S(2)}) collective-permute-start(bf16[1,192,512]{2,1,0:T(8,128)(2,1)S(1)} %collective-permute-done.18), channel_id=1, source_target_pairs={{0,4},{4,0},{1,5},{5,1},{2,6},{6,2},{3,7},{7,3},{8,12},{12,8},{9,1... | collective-permute-start | bytes 589832 | tf_op jit(solution)/shard_map/ppermute | solution.py:98
  73.7 2.0 %collective-permute-start.13 = (bf16[384,768]{1,0:T(8,128)(2,1)S(1)}, bf16[384,768]{1,0:T(8,128)(2,1)S(1)}, u32[]{:S(2)}, u32[]{:S(2)}) collective-permute-start(bf16[384,768]{1,0:T(8,128)(2,1)S(1)} %copy-done.2), channel_id=1, source_target_pairs={{0,8},{8,0},{16,24},{24,16},{1,9},{9,1},{17,25},{25,17},{2,10},{10... | collective-permute-start | bytes 1769480 | tf_op jit(solution)/shard_map/ppermute | solution.py:98
  73.7 2.8 %collective-permute-start.14 = (bf16[384,768]{1,0:T(8,128)(2,1)S(1)}, bf16[384,768]{1,0:T(8,128)(2,1)S(1)}, u32[]{:S(2)}, u32[]{:S(2)}) collective-permute-start(bf16[384,768]{1,0:T(8,128)(2,1)S(1)} %collective-permute-done.7), channel_id=1, source_target_pairs={{0,8},{8,0},{16,24},{24,16},{1,9},{9,1},{17,25},{25,17},{2,10},{10... | collective-permute-start | bytes 1769480 | tf_op jit(solution)/shard_map/ppermute | solution.py:98
  80.9 2.3 %copy-start.4 = (bf16[1024,512]{1,0:T(8,128)(2,1)}, bf16[1024,512]{1,0:T(8,128)(2,1)S(1)}, u32[]{:S(2)}) copy-start(bf16[1024,512]{1,0:T(8,128)(2,1)S(1)} %multiply_convert_fusion) | copy-start | bytes 3145732
  83.8 2.4 %collective-permute-start.22 = (bf16[2,2,128,768]{3,2,1,0:T(8,128)(2,1)S(1)}, bf16[2,2,128,768]{3,2,1,0:T(8,128)(2,1)S(1)}, u32[]{:S(2)}, u32[]{:S(2)}) collective-permute-start(bf16[2,2,128,768]{3,2,1,0:T(8,128)(2,1)S(1)} %convolution_convert_fusion), channel_id=1, source_target_pairs={{0,8},{8,0},{16,24},{24,16},{1,9},{9,1},{17,25},{25,17},{2,10},{10... | collective-permute-start | bytes 2359304 | tf_op jit(solution)/shard_map/ppermute | solution.py:98
  86.4 12.7 %copy-start.7 = (f32[768]{0:T(1024)S(1)}, f32[768]{0:T(1024)}, u32[]{:S(2)}) copy-start(f32[768]{0:T(1024)} %param.18) | copy-start | bytes 9220
  86.4 26.3 %copy-start = (bf16[3,768,192]{1,2,0:T(8,128)(2,1)S(1)}, bf16[3,768,192]{1,2,0:T(8,128)(2,1)}, u32[]{:S(2)}) copy-start(bf16[3,768,192]{1,2,0:T(8,128)(2,1)} %param.19) | copy-start | bytes 2654212
  86.5 8.8 %collective-permute-start.25 = (bf16[128,768]{1,0:T(8,128)(2,1)S(1)}, bf16[128,768]{1,0:T(8,128)(2,1)S(1)}, u32[]{:S(2)}, u32[]{:S(2)}) collective-permute-start(bf16[128,768]{1,0:T(8,128)(2,1)S(1)} %get-tuple-element.54), channel_id=1, source_target_pairs={{0,17},{1,16},{2,19},{3,18},{8,25},{9,24},{10,27},{11,26},{16,1},{... | collective-permute-start | bytes 589832 | tf_op jit(solution)/shard_map/ppermute | solution.py:98
  86.6 11.7 %collective-permute-start.24 = (bf16[128,768]{1,0:T(8,128)(2,1)S(1)}, bf16[128,768]{1,0:T(8,128)(2,1)S(1)}, u32[]{:S(2)}, u32[]{:S(2)}) collective-permute-start(bf16[128,768]{1,0:T(8,128)(2,1)S(1)} %fusion.25), channel_id=1, source_target_pairs={{0,1},{1,0},{2,3},{3,2},{4,5},{5,4},{6,7},{7,6},{8,9},{9,8},{10,11... | collective-permute-start | bytes 589832 | tf_op jit(solution)/shard_map/ppermute | solution.py:98
  89.2 9.4 %collective-permute-start.23 = (bf16[128,768]{1,0:T(8,128)(2,1)S(1)}, bf16[128,768]{1,0:T(8,128)(2,1)S(1)}, u32[]{:S(2)}, u32[]{:S(2)}) collective-permute-start(bf16[128,768]{1,0:T(8,128)(2,1)S(1)} %get-tuple-element.53), channel_id=1, source_target_pairs={{0,16},{8,24},{16,0},{24,8},{1,17},{9,25},{17,1},{25,9},{2,18},{10... | collective-permute-start | bytes 589832 | tf_op jit(solution)/shard_map/ppermute | solution.py:98
  99.2 7.8 %collective-permute-start.26 = (bf16[128,768]{1,0:T(8,128)(2,1)S(1)}, bf16[128,768]{1,0:T(8,128)(2,1)S(1)}, u32[]{:S(2)}, u32[]{:S(2)}) collective-permute-start(bf16[128,768]{1,0:T(8,128)(2,1)S(1)} %multiply_convert_fusion.1.refs_0_), channel_id=1, source_target_pairs={{0,16},{8,24},{16,0},{24,8},{1,17},{9,25},{17,1},{25,9},{2,18},{10... | collective-permute-start | bytes 589832 | tf_op jit(solution)/shard_map/ppermute | solution.py:98
  100.3 9.8 %collective-permute-start.29 = (bf16[128,768]{1,0:T(8,128)(2,1)S(1)}, bf16[128,768]{1,0:T(8,128)(2,1)S(1)}, u32[]{:S(2)}, u32[]{:S(2)}) collective-permute-start(bf16[128,768]{1,0:T(8,128)(2,1)S(1)} %multiply_convert_fusion.1.refs_0_), channel_id=1, source_target_pairs={{0,4},{4,0},{1,5},{5,1},{2,6},{6,2},{3,7},{7,3},{8,12},{12,8},{9,1... | collective-permute-start | bytes 589832 | tf_op jit(solution)/shard_map/ppermute | solution.py:98
  101.8 9.4 %collective-permute-start.30 = (bf16[128,768]{1,0:T(8,128)(2,1)S(1)}, bf16[128,768]{1,0:T(8,128)(2,1)S(1)}, u32[]{:S(2)}, u32[]{:S(2)}) collective-permute-start(bf16[128,768]{1,0:T(8,128)(2,1)S(1)} %multiply_convert_fusion.1.refs_0_), channel_id=1, source_target_pairs={{0,20},{4,16},{8,28},{12,24},{16,4},{20,0},{24,12},{28,8},{1,21},{... | collective-permute-start | bytes 589832 | tf_op jit(solution)/shard_map/ppermute | solution.py:98
  102.7 8.5 %collective-permute-start.27 = (bf16[128,768]{1,0:T(8,128)(2,1)S(1)}, bf16[128,768]{1,0:T(8,128)(2,1)S(1)}, u32[]{:S(2)}, u32[]{:S(2)}) collective-permute-start(bf16[128,768]{1,0:T(8,128)(2,1)S(1)} %multiply_convert_fusion.1.refs_0_), channel_id=1, source_target_pairs={{0,8},{8,0},{16,24},{24,16},{1,9},{9,1},{17,25},{25,17},{2,10},{10... | collective-permute-start | bytes 589832 | tf_op jit(solution)/shard_map/ppermute | solution.py:98
  107.0 4.2 %collective-permute-start.28 = (bf16[128,768]{1,0:T(8,128)(2,1)S(1)}, bf16[128,768]{1,0:T(8,128)(2,1)S(1)}, u32[]{:S(2)}, u32[]{:S(2)}) collective-permute-start(bf16[128,768]{1,0:T(8,128)(2,1)S(1)} %collective-permute-done.26.refs_1_), channel_id=1, source_target_pairs={{0,8},{8,0},{16,24},{24,16},{1,9},{9,1},{17,25},{25,17},{2,10},{10... | collective-permute-start | bytes 589832 | tf_op jit(solution)/shard_map/ppermute | solution.py:98
  110.1 1.4 %collective-permute-start.31 = (bf16[128,768]{1,0:T(8,128)(2,1)S(1)}, bf16[128,768]{1,0:T(8,128)(2,1)S(1)}, u32[]{:S(2)}, u32[]{:S(2)}) collective-permute-start(bf16[128,768]{1,0:T(8,128)(2,1)S(1)} %collective-permute-done.29.refs_4_), channel_id=1, source_target_pairs={{0,8},{8,0},{16,24},{24,16},{1,9},{9,1},{17,25},{25,17},{2,10},{10... | collective-permute-start | bytes 589832 | tf_op jit(solution)/shard_map/ppermute | solution.py:98
  111.2 1.4 %collective-permute-start.32 = (bf16[128,768]{1,0:T(8,128)(2,1)S(1)}, bf16[128,768]{1,0:T(8,128)(2,1)S(1)}, u32[]{:S(2)}, u32[]{:S(2)}) collective-permute-start(bf16[128,768]{1,0:T(8,128)(2,1)S(1)} %collective-permute-done.30.refs_5_), channel_id=1, source_target_pairs={{0,8},{8,0},{16,24},{24,16},{1,9},{9,1},{17,25},{25,17},{2,10},{10... | collective-permute-start | bytes 589832 | tf_op jit(solution)/shard_map/ppermute | solution.py:98
  118.0 1.8 %collective-permute-start.33 = (bf16[2,192,512]{2,1,0:T(8,128)(2,1)S(1)}, bf16[2,192,512]{2,1,0:T(8,128)(2,1)S(1)}, u32[]{:S(2)}, u32[]{:S(2)}) collective-permute-start(bf16[2,192,512]{2,1,0:T(8,128)(2,1)S(1)} %get-tuple-element.40), channel_id=1, source_target_pairs={{0,8},{8,0},{16,24},{24,16},{1,9},{9,1},{17,25},{25,17},{2,10},{10... | collective-permute-start | bytes 1179656 | tf_op jit(solution)/shard_map/ppermute | solution.py:98
  119.9 7.0 %collective-permute-start.34 = (bf16[192,512]{1,0:T(8,128)(2,1)S(1)}, bf16[192,512]{1,0:T(8,128)(2,1)S(1)}, u32[]{:S(2)}, u32[]{:S(2)}) collective-permute-start(bf16[192,512]{1,0:T(8,128)(2,1)S(1)} %fusion.27), channel_id=1, source_target_pairs={{0,16},{8,24},{16,0},{24,8},{1,17},{9,25},{17,1},{25,9},{2,18},{10... | collective-permute-start | bytes 589832 | tf_op jit(solution)/shard_map/ppermute | solution.py:98

commit v17 on v16

--- a/solution.py
+++ b/solution.py
@@ -201,13 +201,13 @@
             g[1, 0] = flip(pair_same, seq=1)
             d[1, 0] = flip(down_same, seq=1)
             beside_x = flip(beside, section=2)
+            proj_x = flip(after(w_proj, mine_x), section=2)
             for k in (1, 3):
                 g[0, k] = rotate(after(pair_other, g[0, 2], d[1, 0], g[1, 0], mine_x), k)
             g[1, 2] = flip(g[0, 2], seq=1)
             across = after(jnp.concatenate([mine_x, beside_x], axis=0), g[0, 2], g[1, 2])
             both = after(jnp.concatenate([mine, beside], axis=0), across)
             both_c, across_c = flip(both, section=1), flip(across, section=1)
-            proj_x = flip(after(w_proj, both_c, across_c), section=2)
             far = rotate(after(down_same, g[0, 1]), 2)
             rows = jnp.concatenate([both, both_c, across, across_c], axis=1)
             normed = layer_norm(rows.astype(jnp.float32), gain).astype(jnp.bfloat16)
@@ -234,7 +234,6 @@
             proj,
             preferred_element_type=jnp.float32,
         )
-        normed = after(normed, residual)
         gate = jnp.dot(normed, gate_up[0], preferred_element_type=jnp.float32)
         up = jnp.dot(normed, gate_up[1], preferred_element_type=jnp.float32)
         hidden = (jax.nn.silu(gate) * up).astype(jnp.bfloat16)
@@ -247,6 +246,7 @@
 
         if ordered:
             late = [d.pop((1, 1)), d.pop((1, 3))]
+            proj = after(proj, residual)
             folded = fold(proj, after(place_rows(d)[0], hidden))
             for k, block in zip((1, 3), late):
                 at = row_of(1, k, block.shape[1])

time: 128 us -> 132 us (1.031)
  waiting for transfers between devices: 60.7 us -> 63.9 us
    ppermute x29, waiting for transfers between devices: 41.3 us -> 55 us  [flip(): return lax.ppermute(x, names if len(names) > 1 else names[0], pairs)]
    ppermute x6, waiting for transfers between devices: 19.4 us -> 8.88 us  [rotate(): return lax.ppermute(x, 'dp', [(i, (i + k) % n_dp) for i in range(n_dp)])]
  transfers between devices with their start and end apart: 35 -> 35, of which waited for: 22 -> 18; matrix products, arithmetic and copies ran while one was open for 17% -> 15% of each run, Pallas kernels for 0% -> 0%
where the time goes in v17:
time: 132 us
  waiting for transfers between devices  63.9 us (48%)
  starting transfers between devices  36.5 us (28%)
  other arithmetic  8.77 us (7%)
  matrix products  8.74 us (7%)
  local copies, waits for them, and re-layouts  7.62 us (6%)
  Pallas kernels  5.35 us (4%)
    ppermute x29, waiting for transfers between devices, flip(): return lax.ppermute(x, names if len(names) > 1 else names[0], pairs)  55 us
    ppermute x29, starting transfers between devices, flip(): return lax.ppermute(x, names if len(names) > 1 else names[0], pairs)  24.6 us
    ppermute x6, starting transfers between devices, rotate(): return lax.ppermute(x, 'dp', [(i, (i + k) % n_dp) for i in range(n_dp)])  11.8 us
    ppermute x6, waiting for transfers between devices, rotate(): return lax.ppermute(x, 'dp', [(i, (i + k) % n_dp) for i in range(n_dp)])  8.88 us
    pallas_call x1, Pallas kernels, per_device(): pl.pallas_call(lambda *refs: attend_kernel(*refs, heads=local_heads, mask...  5.35 us
    unnamed x29, local copies, waits for them, and re-layouts  2.75 us
  transfers between devices with their start and end apart: 35, of which 18 were waited for; matrix products, arithmetic and copies ran while one was open for 15% of the time, Pallas kernels for 0%

profile of v17, /device:TPU:0, one launch (start us, length us, event | category | flops | bytes accessed | tf_op | source)
XLA Modules:
  0.0 132.0 jit_solution(15457089659735344360)
XLA Ops:
  0.0 1.4 %fusion.13 = (bf16[2,192,512]{2,1,0:T(8,128)(2,1)S(1)}, bf16[2,192,512]{2,1,0:T(8,128)(2,1)S(1)}) fusion(s32[]{:T(128)S(6)} %select_n.236, bf16[1,192,1024]{2,1,0:T(8,128)(2,1)} %bitcast.92, bf16[1,192,1024]{2,1,0:T(8,128)(2,1)} %bitcast.93, s32[]{:T(128)S(6)} %select_n.238), kind=kLoop, calls=%fused_computation.29 | loop fusion | flops 1572864 | bytes 1572872 | tf_op jit(solution)/shard_map/stack | solution.py:163
  1.4 4.1 %collective-permute-start.3 = (bf16[2,192,512]{2,1,0:T(8,128)(2,1)S(1)}, bf16[2,192,512]{2,1,0:T(8,128)(2,1)S(1)}, u32[]{:S(2)}, u32[]{:S(2)}) collective-permute-start(bf16[2,192,512]{2,1,0:T(8,128)(2,1)S(1)} %get-tuple-element.51), channel_id=1, source_target_pairs={{0,2},{1,3},{2,0},{3,1},{4,6},{5,7},{6,4},{7,5},{8,10},{9,11},{10,... | collective-permute-start | bytes 1179656 | tf_op jit(solution)/shard_map/ppermute | solution.py:101
  5.5 1.5 %collective-permute-start.9 = (bf16[2,192,512]{2,1,0:T(8,128)(2,1)S(1)}, bf16[2,192,512]{2,1,0:T(8,128)(2,1)S(1)}, u32[]{:S(2)}, u32[]{:S(2)}) collective-permute-start(bf16[2,192,512]{2,1,0:T(8,128)(2,1)S(1)} %get-tuple-element.51), channel_id=1, source_target_pairs={{0,4},{4,0},{1,5},{5,1},{2,6},{6,2},{3,7},{7,3},{8,12},{12,8},{9,1... | collective-permute-start | bytes 1179656 | tf_op jit(solution)/shard_map/ppermute | solution.py:98
  7.0 1.5 %collective-permute-start.1 = (bf16[512,384]{1,0:T(8,128)(2,1)}, bf16[512,384]{1,0:T(8,128)(2,1)S(1)}, u32[]{:S(2)}, u32[]{:S(2)}) collective-permute-start(bf16[512,384]{1,0:T(8,128)(2,1)} %bitcast.94), channel_id=1, source_target_pairs={{0,16},{8,24},{16,0},{24,8},{1,17},{9,25},{17,1},{25,9},{2,18},{10... | collective-permute-start | bytes 1179656 | tf_op jit(solution)/shard_map/ppermute | solution.py:98
  8.5 1.6 %collective-permute-start = (bf16[512,384]{1,0:T(8,128)(2,1)}, bf16[512,384]{1,0:T(8,128)(2,1)}, u32[]{:S(2)}, u32[]{:S(2)}) collective-permute-start(bf16[512,384]{1,0:T(8,128)(2,1)} %bitcast.95), channel_id=1, source_target_pairs={{0,1},{1,0},{2,3},{3,2},{4,5},{5,4},{6,7},{7,6},{8,9},{9,8},{10,11... | collective-permute-start | bytes 1179656 | tf_op jit(solution)/shard_map/ppermute | solution.py:98
  10.1 1.8 %dynamic-slice_bitcast_fusion.2 = (bf16[1,192,512]{2,1,0:T(8,128)(2,1)}, bf16[1,192,512]{2,1,0:T(8,128)(2,1)}) fusion(bf16[1024,192]{0,1:T(8,128)(2,1)} %param.16, s32[]{:T(128)S(6)} %select_n.236, s32[]{:T(128)S(6)} %select_n.238), kind=kLoop, calls=%fused_computation.61 | loop fusion | bytes 786440 | tf_op jit(solution)/shard_map/dynamic_slice | solution.py:161
  13.0 0.7 fusion.30
  13.8 12.3 %collective-permute-done = bf16[512,384]{1,0:T(8,128)(2,1)} collective-permute-done((bf16[512,384]{1,0:T(8,128)(2,1)}, bf16[512,384]{1,0:T(8,128)(2,1)}, u32[]{:S(2)}, u32[]{:S(2)}) %collective-permute-start) | collective-permute-done | bytes 393248 | tf_op jit(solution)/shard_map/ppermute | solution.py:98
  27.7 1.1 copy.14
  29.0 0.8 collective-permute-start.10
  29.8 3.1 %collective-permute-start.15 = (bf16[2,192,512]{2,1,0:T(8,128)(2,1)S(1)}, bf16[2,192,512]{2,1,0:T(8,128)(2,1)S(1)}, u32[]{:S(2)}, u32[]{:S(2)}) collective-permute-start(bf16[2,192,512]{2,1,0:T(8,128)(2,1)S(1)} %get-tuple-element.26), channel_id=1, source_target_pairs={{0,3},{1,0},{2,1},{3,2},{4,7},{5,4},{6,5},{7,6},{8,11},{9,8},{10,9... | collective-permute-start | bytes 1179656 | tf_op jit(solution)/shard_map/ppermute | solution.py:101
  32.9 1.5 %collective-permute-start.7 = (bf16[384,768]{1,0:T(8,128)(2,1)S(1)}, bf16[384,768]{1,0:T(8,128)(2,1)S(1)}, u32[]{:S(2)}, u32[]{:S(2)}) collective-permute-start(bf16[384,768]{1,0:T(8,128)(2,1)S(1)} %copy-done.2), channel_id=1, source_target_pairs={{0,16},{8,24},{16,0},{24,8},{1,17},{9,25},{17,1},{25,9},{2,18},{10... | collective-permute-start | bytes 1769480 | tf_op jit(solution)/shard_map/ppermute | solution.py:98
  34.4 1.1 pad_maximum_fusion
  35.5 3.0 %collective-permute-done.2 = bf16[512,384]{1,0:T(8,128)(2,1)} collective-permute-done((bf16[512,384]{1,0:T(8,128)(2,1)}, bf16[512,384]{1,0:T(8,128)(2,1)}, u32[]{:S(2)}, u32[]{:S(2)}) %collective-permute-start.2) | collective-permute-done | bytes 393248 | tf_op jit(solution)/shard_map/ppermute | solution.py:98
  38.5 1.1 pad_maximum_fusion.1
  40.6 2.4 %collective-permute-done.10 = bf16[2,192,512]{2,1,0:T(8,128)(2,1)S(1)} collective-permute-done((bf16[2,192,512]{2,1,0:T(8,128)(2,1)S(1)}, bf16[2,192,512]{2,1,0:T(8,128)(2,1)S(1)}, u32[]{:S(2)}, u32[]{:S(2)}) %collective-permute-start.10) | collective-permute-done | bytes 393248 | tf_op jit(solution)/shard_map/ppermute | solution.py:101
  43.0 4.4 %collective-permute-done.15 = bf16[2,192,512]{2,1,0:T(8,128)(2,1)S(1)} collective-permute-done((bf16[2,192,512]{2,1,0:T(8,128)(2,1)S(1)}, bf16[2,192,512]{2,1,0:T(8,128)(2,1)S(1)}, u32[]{:S(2)}, u32[]{:S(2)}) %collective-permute-start.15) | collective-permute-done | bytes 393248 | tf_op jit(solution)/shard_map/ppermute | solution.py:101
  48.0 1.0 constant_dynamic-update-slice_fusion.13
  49.2 1.5 %collective-permute-start.17 = (bf16[2,192,512]{2,1,0:T(8,128)(2,1)S(1)}, bf16[2,192,512]{2,1,0:T(8,128)(2,1)S(1)}, u32[]{:S(2)}, u32[]{:S(2)}) collective-permute-start(bf16[2,192,512]{2,1,0:T(8,128)(2,1)S(1)} %collective-permute-done.15), channel_id=1, source_target_pairs={{0,4},{4,0},{1,5},{5,1},{2,6},{6,2},{3,7},{7,3},{8,12},{12,8},{9,1... | collective-permute-start | bytes 1179656 | tf_op jit(solution)/shard_map/ppermute | solution.py:98
  51.6 1.0 fusion.2
  52.6 1.0 fusion.4
  53.6 2.1 %collective-permute-done.11 = bf16[1,192,512]{2,1,0:T(8,128)(2,1)S(1)} collective-permute-done((bf16[1,192,512]{2,1,0:T(8,128)(2,1)}, bf16[1,192,512]{2,1,0:T(8,128)(2,1)S(1)}, u32[]{:S(2)}, u32[]{:S(2)}) %collective-permute-start.11) | collective-permute-done | bytes 196640 | tf_op jit(solution)/shard_map/ppermute | solution.py:101
  55.7 2.6 %collective-permute-start.12 = (bf16[1,192,512]{2,1,0:T(8,128)(2,1)S(1)}, bf16[1,192,512]{2,1,0:T(8,128)(2,1)S(1)}, u32[]{:S(2)}, u32[]{:S(2)}) collective-permute-start(bf16[1,192,512]{2,1,0:T(8,128)(2,1)S(1)} %copy-done.5), channel_id=1, source_target_pairs={{0,1},{1,2},{2,3},{3,0},{4,5},{5,6},{6,7},{7,4},{8,9},{9,10},{10,1... | collective-permute-start | bytes 589832 | tf_op jit(solution)/shard_map/ppermute | solution.py:101
  58.3 1.3 collective-permute-start.18
  59.6 0.8 collective-permute-start.19
  60.3 7.5 %collective-permute-done.17 = bf16[2,192,512]{2,1,0:T(8,128)(2,1)S(1)} collective-permute-done((bf16[2,192,512]{2,1,0:T(8,128)(2,1)S(1)}, bf16[2,192,512]{2,1,0:T(8,128)(2,1)S(1)}, u32[]{:S(2)}, u32[]{:S(2)}) %collective-permute-start.17) | collective-permute-done | bytes 393248 | tf_op jit(solution)/shard_map/ppermute | solution.py:98
  67.9 1.8 %fusion.5 = f32[1024,512]{1,0:T(8,128)S(1)} fusion(bf16[1024,1536]{1,0:T(8,128)(2,1)S(1)} %fusion.4, bf16[2,1536,512]{2,1,0:T(8,128)(2,1)S(1)} %constant_dynamic-update-slice_fusion.11), kind=kOutput, calls=%fused_computation.10 | convolution fusion | flops 1610612736 | bytes 6815744 | tf_op jit(solution)/shard_map/dot_general | solution.py:237
  69.6 2.0 %multiply_convert_fusion = bf16[1024,512]{1,0:T(8,128)(2,1)S(1)} fusion(f32[1024,512]{1,0:T(8,128)S(1)} %fusion.5, bf16[1024,1536]{1,0:T(8,128)(2,1)S(1)} %fusion.4, bf16[2,1536,512]{2,1,0:T(8,128)(2,1)S(1)} %constant_dynamic-update-slice_fusion.11), kind=kOutput, calls=%fused_computation.7 | convolution fusion | flops 1613758464 | bytes 7864320 | tf_op jit(solution)/shard_map/dot_general | solution.py:238
  71.9 1.0 copy-done.1
  73.0 0.9 bitcast_dynamic-update-slice_fusion.4
  74.6 0.7 collective-permute-start.20
  75.4 1.3 %collective-permute-start.21 = (bf16[1,192,512]{2,1,0:T(8,128)(2,1)S(1)}, bf16[1,192,512]{2,1,0:T(8,128)(2,1)S(1)}, u32[]{:S(2)}, u32[]{:S(2)}) collective-permute-start(bf16[1,192,512]{2,1,0:T(8,128)(2,1)S(1)} %collective-permute-done.18), channel_id=1, source_target_pairs={{0,4},{4,0},{1,5},{5,1},{2,6},{6,2},{3,7},{7,3},{8,12},{12,8},{9,1... | collective-permute-start | bytes 589832 | tf_op jit(solution)/shard_map/ppermute | solution.py:98
  77.4 1.4 %fusion.51 = f32[768,512]{1,0:T(8,128)S(1)} fusion(bf16[1536,768]{1,0:T(8,128)(2,1)S(1)} %constant_dynamic-update-slice_fusion.5, bf16[1536,512]{1,0:T(8,128)(2,1)S(1)} %bitcast_dynamic-update-slice_fusion), kind=kOutput, calls=%fused_computation.129 | convolution fusion | flops 1207959552 | bytes 5505024 | tf_op jit(solution)/shard_map/dot_general | solution.py:243
  78.8 3.6 %collective-permute-done.20 = bf16[1,192,512]{2,1,0:T(8,128)(2,1)S(1)} collective-permute-done((bf16[1,192,512]{2,1,0:T(8,128)(2,1)S(1)}, bf16[1,192,512]{2,1,0:T(8,128)(2,1)S(1)}, u32[]{:S(2)}, u32[]{:S(2)}) %collective-permute-start.20) | collective-permute-done | bytes 196640 | tf_op jit(solution)/shard_map/ppermute | solution.py:98
  82.9 2.9 %collective-permute-done.21 = bf16[1,192,512]{2,1,0:T(8,128)(2,1)S(1)} collective-permute-done((bf16[1,192,512]{2,1,0:T(8,128)(2,1)S(1)}, bf16[1,192,512]{2,1,0:T(8,128)(2,1)S(1)}, u32[]{:S(2)}, u32[]{:S(2)}) %collective-permute-start.21) | collective-permute-done | bytes 196640 | tf_op jit(solution)/shard_map/ppermute | solution.py:98
  87.0 1.6 %fusion.8 = f32[2,2,128,768]{3,2,1,0:T(8,128)S(1)} fusion(bf16[768,512,1,1]{1,0,3,2:T(8,128)(2,1)S(1)} %fusion.6, bf16[2,2,2,128,512]{4,3,2,1,0:T(8,128)(2,1)} %bitcast.98, s32[]{:T(128)S(6)} %select_n.278), kind=kOutput, calls=%fused_computation.24 | convolution fusion | flops 402653184 | bytes 2883588 | tf_op jit(solution)/shard_map/dot_general | solution.py:261
  90.0 4.7 %collective-permute-start.25 = (bf16[128,768]{1,0:T(8,128)(2,1)S(1)}, bf16[128,768]{1,0:T(8,128)(2,1)S(1)}, u32[]{:S(2)}, u32[]{:S(2)}) collective-permute-start(bf16[128,768]{1,0:T(8,128)(2,1)S(1)} %get-tuple-element.54), channel_id=1, source_target_pairs={{0,17},{1,16},{2,19},{3,18},{8,25},{9,24},{10,27},{11,26},{16,1},{... | collective-permute-start | bytes 589832 | tf_op jit(solution)/shard_map/ppermute | solution.py:98
  94.8 5.9 %collective-permute-done.23 = bf16[128,768]{1,0:T(8,128)(2,1)S(1)} collective-permute-done((bf16[128,768]{1,0:T(8,128)(2,1)S(1)}, bf16[128,768]{1,0:T(8,128)(2,1)S(1)}, u32[]{:S(2)}, u32[]{:S(2)}) %collective-permute-start.23) | collective-permute-done | bytes 196640 | tf_op jit(solution)/shard_map/ppermute | solution.py:98
  100.7 2.7 %collective-permute-done.24 = bf16[128,768]{1,0:T(8,128)(2,1)S(1)} collective-permute-done((bf16[128,768]{1,0:T(8,128)(2,1)S(1)}, bf16[128,768]{1,0:T(8,128)(2,1)S(1)}, u32[]{:S(2)}, u32[]{:S(2)}) %collective-permute-start.24) | collective-permute-done | bytes 196640 | tf_op jit(solution)/shard_map/ppermute | solution.py:98
  104.0 1.1 collective-permute-start.26
  105.4 2.1 %collective-permute-start.30 = (bf16[128,768]{1,0:T(8,128)(2,1)S(1)}, bf16[128,768]{1,0:T(8,128)(2,1)S(1)}, u32[]{:S(2)}, u32[]{:S(2)}) collective-permute-start(bf16[128,768]{1,0:T(8,128)(2,1)S(1)} %multiply_convert_fusion.1.refs_0_), channel_id=1, source_target_pairs={{0,20},{4,16},{8,28},{12,24},{16,4},{20,0},{24,12},{28,8},{1,21},{... | collective-permute-start | bytes 589832 | tf_op jit(solution)/shard_map/ppermute | solution.py:98
  107.5 4.3 %collective-permute-done.26.refs_1_ = bf16[128,768]{1,0:T(8,128)(2,1)S(1)} collective-permute-done((bf16[128,768]{1,0:T(8,128)(2,1)S(1)}, bf16[128,768]{1,0:T(8,128)(2,1)S(1)}, u32[]{:S(2)}, u32[]{:S(2)}) %collective-permute-start.26) | collective-permute-done | bytes 196640 | tf_op jit(solution)/shard_map/ppermute | solution.py:98
  111.9 3.3 %collective-permute-done.29.refs_4_ = bf16[128,768]{1,0:T(8,128)(2,1)S(1)} collective-permute-done((bf16[128,768]{1,0:T(8,128)(2,1)S(1)}, bf16[128,768]{1,0:T(8,128)(2,1)S(1)}, u32[]{:S(2)}, u32[]{:S(2)}) %collective-permute-start.29) | collective-permute-done | bytes 196640 | tf_op jit(solution)/shard_map/ppermute | solution.py:98
  115.7 0.9 collective-permute-done.31.refs_6_
  116.9 5.4 %shard_map.118 = (f32[2,192,512]{2,1,0:T(8,128)S(1)}, bf16[2,192,512]{2,1,0:T(8,128)(2,1)S(1)}) custom-call(bf16[128,768]{1,0:T(8,128)(2,1)S(1)} %multiply_convert_fusion.1.refs_0_, bf16[128,768]{1,0:T(8,128)(2,1)S(1)} %collective-permute-done.26.refs_1_, bf16[128,768]{1,0:T(8,128)(2,1)S(1)} %collective-permute-done.27.refs_2_, ...), custom_call_target="tpu_custom_call" | custom-call | flops 2516582400 | bytes 8388608 | tf_op jit(solution)/shard_map/pallas_call | solution.py:299
  122.5 1.5 %collective-permute-done.33 = bf16[2,192,512]{2,1,0:T(8,128)(2,1)S(1)} collective-permute-done((bf16[2,192,512]{2,1,0:T(8,128)(2,1)S(1)}, bf16[2,192,512]{2,1,0:T(8,128)(2,1)S(1)}, u32[]{:S(2)}, u32[]{:S(2)}) %collective-permute-start.33) | collective-permute-done | bytes 393248 | tf_op jit(solution)/shard_map/ppermute | solution.py:98
  124.2 1.0 collective-permute-start.34
  125.2 6.1 %collective-permute-done.34 = bf16[192,512]{1,0:T(8,128)(2,1)S(1)} collective-permute-done((bf16[192,512]{1,0:T(8,128)(2,1)S(1)}, bf16[192,512]{1,0:T(8,128)(2,1)S(1)}, u32[]{:S(2)}, u32[]{:S(2)}) %collective-permute-start.34) | collective-permute-done | bytes 196640 | tf_op jit(solution)/shard_map/ppermute | solution.py:98
  (125 shorter events, 12.3 us)
Async XLA Ops:
  0.0 12.4 %copy-start.10 = (s32[1,3]{1,0:T(1,128)S(1)}, s32[1,3]{1,0:T(1,128)}, u32[]{:S(2)}) copy-start(s32[1,3]{1,0:T(1,128)} %param.21) | copy-start | bytes 40
  0.0 12.6 %copy-start.9 = (s32[4]{0:T(128)S(1)}, s32[4]{0:T(128)}, u32[]{:S(2)}) copy-start(s32[4]{0:T(128)} %param.23) | copy-start | bytes 52
  0.0 12.7 %copy-start.8 = (s32[4]{0:T(128)S(1)}, s32[4]{0:T(128)}, u32[]{:S(2)}) copy-start(s32[4]{0:T(128)} %param.22) | copy-start | bytes 52
  0.0 13.7 %copy-start.6 = (f32[1536]{0:T(1024)S(1)}, f32[1536]{0:T(1024)}, u32[]{:S(2)}) copy-start(f32[1536]{0:T(1024)} %param.13) | copy-start | bytes 18436
  0.0 28.9 %copy-start.2 = (bf16[384,768]{1,0:T(8,128)(2,1)S(1)}, bf16[384,768]{1,0:T(8,128)(2,1)}, u32[]{:S(2)}) copy-start(bf16[384,768]{1,0:T(8,128)(2,1)} %param.17) | copy-start | bytes 1769476
  0.0 34.3 %copy-start.3 = (bf16[1,512,384]{2,1,0:T(8,128)(2,1)S(1)}, bf16[1,512,384]{2,1,0:T(8,128)(2,1)}, u32[]{:S(2)}) copy-start(bf16[1,512,384]{2,1,0:T(8,128)(2,1)} %param.12) | copy-start | bytes 1179652
  1.4 25.7 %collective-permute-start.3 = (bf16[2,192,512]{2,1,0:T(8,128)(2,1)S(1)}, bf16[2,192,512]{2,1,0:T(8,128)(2,1)S(1)}, u32[]{:S(2)}, u32[]{:S(2)}) collective-permute-start(bf16[2,192,512]{2,1,0:T(8,128)(2,1)S(1)} %get-tuple-element.51), channel_id=1, source_target_pairs={{0,2},{1,3},{2,0},{3,1},{4,6},{5,7},{6,4},{7,5},{8,10},{9,11},{10,... | collective-permute-start | bytes 1179656 | tf_op jit(solution)/shard_map/ppermute | solution.py:101
  5.5 23.5 %collective-permute-start.9 = (bf16[2,192,512]{2,1,0:T(8,128)(2,1)S(1)}, bf16[2,192,512]{2,1,0:T(8,128)(2,1)S(1)}, u32[]{:S(2)}, u32[]{:S(2)}) collective-permute-start(bf16[2,192,512]{2,1,0:T(8,128)(2,1)S(1)} %get-tuple-element.51), channel_id=1, source_target_pairs={{0,4},{4,0},{1,5},{5,1},{2,6},{6,2},{3,7},{7,3},{8,12},{12,8},{9,1... | collective-permute-start | bytes 1179656 | tf_op jit(solution)/shard_map/ppermute | solution.py:98
  7.0 22.0 %collective-permute-start.1 = (bf16[512,384]{1,0:T(8,128)(2,1)}, bf16[512,384]{1,0:T(8,128)(2,1)S(1)}, u32[]{:S(2)}, u32[]{:S(2)}) collective-permute-start(bf16[512,384]{1,0:T(8,128)(2,1)} %bitcast.94), channel_id=1, source_target_pairs={{0,16},{8,24},{16,0},{24,8},{1,17},{9,25},{17,1},{25,9},{2,18},{10... | collective-permute-start | bytes 1179656 | tf_op jit(solution)/shard_map/ppermute | solution.py:98
  8.5 17.6 %collective-permute-start = (bf16[512,384]{1,0:T(8,128)(2,1)}, bf16[512,384]{1,0:T(8,128)(2,1)}, u32[]{:S(2)}, u32[]{:S(2)}) collective-permute-start(bf16[512,384]{1,0:T(8,128)(2,1)} %bitcast.95), channel_id=1, source_target_pairs={{0,1},{1,0},{2,3},{3,2},{4,5},{5,4},{6,7},{7,6},{8,9},{9,8},{10,11... | collective-permute-start | bytes 1179656 | tf_op jit(solution)/shard_map/ppermute | solution.py:98
  11.9 17.1 %collective-permute-start.8 = (bf16[1,192,512]{2,1,0:T(8,128)(2,1)}, bf16[1,192,512]{2,1,0:T(8,128)(2,1)}, u32[]{:S(2)}, u32[]{:S(2)}) collective-permute-start(bf16[1,192,512]{2,1,0:T(8,128)(2,1)} %get-tuple-element.27), channel_id=1, source_target_pairs={{0,4},{4,0},{1,5},{5,1},{2,6},{6,2},{3,7},{7,3},{8,12},{12,8},{9,1... | collective-permute-start | bytes 589832 | tf_op jit(solution)/shard_map/ppermute | solution.py:98
  26.1 12.4 %collective-permute-start.2 = (bf16[512,384]{1,0:T(8,128)(2,1)}, bf16[512,384]{1,0:T(8,128)(2,1)}, u32[]{:S(2)}, u32[]{:S(2)}) collective-permute-start(bf16[512,384]{1,0:T(8,128)(2,1)} %collective-permute-done), channel_id=1, source_target_pairs={{0,16},{8,24},{16,0},{24,8},{1,17},{9,25},{17,1},{25,9},{2,18},{10... | collective-permute-start | bytes 1179656 | tf_op jit(solution)/shard_map/ppermute | solution.py:98
  27.2 12.4 %collective-permute-start.4 = (bf16[2,192,512]{2,1,0:T(8,128)(2,1)S(1)}, bf16[2,192,512]{2,1,0:T(8,128)(2,1)}, u32[]{:S(2)}, u32[]{:S(2)}) collective-permute-start(bf16[2,192,512]{2,1,0:T(8,128)(2,1)S(1)} %collective-permute-done.3), channel_id=1, source_target_pairs={{0,4},{4,0},{1,5},{5,1},{2,6},{6,2},{3,7},{7,3},{8,12},{12,8},{9,1... | collective-permute-start | bytes 1179656 | tf_op jit(solution)/shard_map/ppermute | solution.py:98
  29.0 13.9 %collective-permute-start.10 = (bf16[2,192,512]{2,1,0:T(8,128)(2,1)S(1)}, bf16[2,192,512]{2,1,0:T(8,128)(2,1)S(1)}, u32[]{:S(2)}, u32[]{:S(2)}) collective-permute-start(bf16[2,192,512]{2,1,0:T(8,128)(2,1)S(1)} %get-tuple-element.26), channel_id=1, source_target_pairs={{0,1},{1,2},{2,3},{3,0},{4,5},{5,6},{6,7},{7,4},{8,9},{9,10},{10,1... | collective-permute-start | bytes 1179656 | tf_op jit(solution)/shard_map/ppermute | solution.py:101
  29.8 17.6 %collective-permute-start.15 = (bf16[2,192,512]{2,1,0:T(8,128)(2,1)S(1)}, bf16[2,192,512]{2,1,0:T(8,128)(2,1)S(1)}, u32[]{:S(2)}, u32[]{:S(2)}) collective-permute-start(bf16[2,192,512]{2,1,0:T(8,128)(2,1)S(1)} %get-tuple-element.26), channel_id=1, source_target_pairs={{0,3},{1,0},{2,1},{3,2},{4,7},{5,4},{6,5},{7,6},{8,11},{9,8},{10,9... | collective-permute-start | bytes 1179656 | tf_op jit(solution)/shard_map/ppermute | solution.py:101
  32.9 41.1 %collective-permute-start.7 = (bf16[384,768]{1,0:T(8,128)(2,1)S(1)}, bf16[384,768]{1,0:T(8,128)(2,1)S(1)}, u32[]{:S(2)}, u32[]{:S(2)}) collective-permute-start(bf16[384,768]{1,0:T(8,128)(2,1)S(1)} %copy-done.2), channel_id=1, source_target_pairs={{0,16},{8,24},{16,0},{24,8},{1,17},{9,25},{17,1},{25,9},{2,18},{10... | collective-permute-start | bytes 1769480 | tf_op jit(solution)/shard_map/ppermute | solution.py:98
  39.6 9.6 %collective-permute-start.5 = (bf16[1024,384]{1,0:T(8,128)(2,1)S(1)}, bf16[1024,384]{1,0:T(8,128)(2,1)S(1)}, u32[]{:S(2)}, u32[]{:S(2)}) collective-permute-start(bf16[1024,384]{1,0:T(8,128)(2,1)S(1)} %pad_maximum_fusion), channel_id=1, source_target_pairs={{0,8},{8,0},{16,24},{24,16},{1,9},{9,1},{17,25},{25,17},{2,10},{10... | collective-permute-start | bytes 2359304 | tf_op jit(solution)/shard_map/ppermute | solution.py:98
  40.0 11.0 %collective-permute-start.6 = (bf16[1024,384]{1,0:T(8,128)(2,1)S(1)}, bf16[1024,384]{1,0:T(8,128)(2,1)S(1)}, u32[]{:S(2)}, u32[]{:S(2)}) collective-permute-start(bf16[1024,384]{1,0:T(8,128)(2,1)S(1)} %pad_maximum_fusion.1), channel_id=1, source_target_pairs={{0,8},{8,0},{16,24},{24,16},{1,9},{9,1},{17,25},{25,17},{2,10},{10... | collective-permute-start | bytes 2359304 | tf_op jit(solution)/shard_map/ppermute | solution.py:98
  42.9 12.8 %collective-permute-start.11 = (bf16[1,192,512]{2,1,0:T(8,128)(2,1)}, bf16[1,192,512]{2,1,0:T(8,128)(2,1)S(1)}, u32[]{:S(2)}, u32[]{:S(2)}) collective-permute-start(bf16[1,192,512]{2,1,0:T(8,128)(2,1)} %get-tuple-element.27), channel_id=1, source_target_pairs={{0,2},{1,3},{2,0},{3,1},{4,6},{5,7},{6,4},{7,5},{8,10},{9,11},{10,... | collective-permute-start | bytes 589832 | tf_op jit(solution)/shard_map/ppermute | solution.py:101
  47.4 12.2 %collective-permute-start.16 = (bf16[2,192,512]{2,1,0:T(8,128)(2,1)S(1)}, bf16[2,192,512]{2,1,0:T(8,128)(2,1)S(1)}, u32[]{:S(2)}, u32[]{:S(2)}) collective-permute-start(bf16[2,192,512]{2,1,0:T(8,128)(2,1)S(1)} %collective-permute-done.10), channel_id=1, source_target_pairs={{0,4},{4,0},{1,5},{5,1},{2,6},{6,2},{3,7},{7,3},{8,12},{12,8},{9,1... | collective-permute-start | bytes 1179656 | tf_op jit(solution)/shard_map/ppermute | solution.py:98
  49.2 18.6 %collective-permute-start.17 = (bf16[2,192,512]{2,1,0:T(8,128)(2,1)S(1)}, bf16[2,192,512]{2,1,0:T(8,128)(2,1)S(1)}, u32[]{:S(2)}, u32[]{:S(2)}) collective-permute-start(bf16[2,192,512]{2,1,0:T(8,128)(2,1)S(1)} %collective-permute-done.15), channel_id=1, source_target_pairs={{0,4},{4,0},{1,5},{5,1},{2,6},{6,2},{3,7},{7,3},{8,12},{12,8},{9,1... | collective-permute-start | bytes 1179656 | tf_op jit(solution)/shard_map/ppermute | solution.py:98
  52.6 3.1 %copy-start.5 = (bf16[1,192,512]{2,1,0:T(8,128)(2,1)S(1)}, bf16[1,192,512]{2,1,0:T(8,128)(2,1)}, u32[]{:S(2)}) copy-start(bf16[1,192,512]{2,1,0:T(8,128)(2,1)} %get-tuple-element.29) | copy-start | bytes 589828
  55.7 18.2 %collective-permute-start.12 = (bf16[1,192,512]{2,1,0:T(8,128)(2,1)S(1)}, bf16[1,192,512]{2,1,0:T(8,128)(2,1)S(1)}, u32[]{:S(2)}, u32[]{:S(2)}) collective-permute-start(bf16[1,192,512]{2,1,0:T(8,128)(2,1)S(1)} %copy-done.5), channel_id=1, source_target_pairs={{0,1},{1,2},{2,3},{3,0},{4,5},{5,6},{6,7},{7,4},{8,9},{9,10},{10,1... | collective-permute-start | bytes 589832 | tf_op jit(solution)/shard_map/ppermute | solution.py:101
  58.3 16.3 %collective-permute-start.18 = (bf16[1,192,512]{2,1,0:T(8,128)(2,1)S(1)}, bf16[1,192,512]{2,1,0:T(8,128)(2,1)S(1)}, u32[]{:S(2)}, u32[]{:S(2)}) collective-permute-start(bf16[1,192,512]{2,1,0:T(8,128)(2,1)S(1)} %copy-done.5), channel_id=1, source_target_pairs={{0,3},{1,0},{2,1},{3,2},{4,7},{5,4},{6,5},{7,6},{8,11},{9,8},{10,9... | collective-permute-start | bytes 589832 | tf_op jit(solution)/shard_map/ppermute | solution.py:101
  59.6 15.0 %collective-permute-start.19 = (bf16[1,192,512]{2,1,0:T(8,128)(2,1)S(1)}, bf16[1,192,512]{2,1,0:T(8,128)(2,1)S(1)}, u32[]{:S(2)}, u32[]{:S(2)}) collective-permute-start(bf16[1,192,512]{2,1,0:T(8,128)(2,1)S(1)} %collective-permute-done.11), channel_id=1, source_target_pairs={{0,4},{4,0},{1,5},{5,1},{2,6},{6,2},{3,7},{7,3},{8,12},{12,8},{9,1... | collective-permute-start | bytes 589832 | tf_op jit(solution)/shard_map/ppermute | solution.py:98
  71.7 14.6 %copy-start.4 = (bf16[1024,512]{1,0:T(8,128)(2,1)}, bf16[1024,512]{1,0:T(8,128)(2,1)S(1)}, u32[]{:S(2)}) copy-start(bf16[1024,512]{1,0:T(8,128)(2,1)S(1)} %multiply_convert_fusion) | copy-start | bytes 3145732
  71.7 1.3 copy-start.1
  74.0 2.8 %collective-permute-start.13 = (bf16[384,768]{1,0:T(8,128)(2,1)S(1)}, bf16[384,768]{1,0:T(8,128)(2,1)S(1)}, u32[]{:S(2)}, u32[]{:S(2)}) collective-permute-start(bf16[384,768]{1,0:T(8,128)(2,1)S(1)} %copy-done.2), channel_id=1, source_target_pairs={{0,8},{8,0},{16,24},{24,16},{1,9},{9,1},{17,25},{25,17},{2,10},{10... | collective-permute-start | bytes 1769480 | tf_op jit(solution)/shard_map/ppermute | solution.py:98
  74.0 2.8 %collective-permute-start.14 = (bf16[384,768]{1,0:T(8,128)(2,1)S(1)}, bf16[384,768]{1,0:T(8,128)(2,1)S(1)}, u32[]{:S(2)}, u32[]{:S(2)}) collective-permute-start(bf16[384,768]{1,0:T(8,128)(2,1)S(1)} %collective-permute-done.7), channel_id=1, source_target_pairs={{0,8},{8,0},{16,24},{24,16},{1,9},{9,1},{17,25},{25,17},{2,10},{10... | collective-permute-start | bytes 1769480 | tf_op jit(solution)/shard_map/ppermute | solution.py:98
  74.6 7.8 %collective-permute-start.20 = (bf16[1,192,512]{2,1,0:T(8,128)(2,1)S(1)}, bf16[1,192,512]{2,1,0:T(8,128)(2,1)S(1)}, u32[]{:S(2)}, u32[]{:S(2)}) collective-permute-start(bf16[1,192,512]{2,1,0:T(8,128)(2,1)S(1)} %collective-permute-done.12), channel_id=1, source_target_pairs={{0,4},{4,0},{1,5},{5,1},{2,6},{6,2},{3,7},{7,3},{8,12},{12,8},{9,1... | collective-permute-start | bytes 589832 | tf_op jit(solution)/shard_map/ppermute | solution.py:98
  75.4 10.4 %collective-permute-start.21 = (bf16[1,192,512]{2,1,0:T(8,128)(2,1)S(1)}, bf16[1,192,512]{2,1,0:T(8,128)(2,1)S(1)}, u32[]{:S(2)}, u32[]{:S(2)}) collective-permute-start(bf16[1,192,512]{2,1,0:T(8,128)(2,1)S(1)} %collective-permute-done.18), channel_id=1, source_target_pairs={{0,4},{4,0},{1,5},{5,1},{2,6},{6,2},{3,7},{7,3},{8,12},{12,8},{9,1... | collective-permute-start | bytes 589832 | tf_op jit(solution)/shard_map/ppermute | solution.py:98
  86.8 2.4 %collective-permute-start.22 = (bf16[2,2,128,768]{3,2,1,0:T(8,128)(2,1)S(1)}, bf16[2,2,128,768]{3,2,1,0:T(8,128)(2,1)S(1)}, u32[]{:S(2)}, u32[]{:S(2)}) collective-permute-start(bf16[2,2,128,768]{3,2,1,0:T(8,128)(2,1)S(1)} %convolution_convert_fusion), channel_id=1, source_target_pairs={{0,8},{8,0},{16,24},{24,16},{1,9},{9,1},{17,25},{25,17},{2,10},{10... | collective-permute-start | bytes 2359304 | tf_op jit(solution)/shard_map/ppermute | solution.py:98
  89.4 14.4 %copy-start.7 = (f32[768]{0:T(1024)S(1)}, f32[768]{0:T(1024)}, u32[]{:S(2)}) copy-start(f32[768]{0:T(1024)} %param.18) | copy-start | bytes 9220
  89.4 27.5 %copy-start = (bf16[3,768,192]{1,2,0:T(8,128)(2,1)S(1)}, bf16[3,768,192]{1,2,0:T(8,128)(2,1)}, u32[]{:S(2)}) copy-start(bf16[3,768,192]{1,2,0:T(8,128)(2,1)} %param.19) | copy-start | bytes 2654212
  89.5 11.2 %collective-permute-start.23 = (bf16[128,768]{1,0:T(8,128)(2,1)S(1)}, bf16[128,768]{1,0:T(8,128)(2,1)S(1)}, u32[]{:S(2)}, u32[]{:S(2)}) collective-permute-start(bf16[128,768]{1,0:T(8,128)(2,1)S(1)} %get-tuple-element.53), channel_id=1, source_target_pairs={{0,16},{8,24},{16,0},{24,8},{1,17},{9,25},{17,1},{25,9},{2,18},{10... | collective-permute-start | bytes 589832 | tf_op jit(solution)/shard_map/ppermute | solution.py:98
  90.0 10.7 %collective-permute-start.25 = (bf16[128,768]{1,0:T(8,128)(2,1)S(1)}, bf16[128,768]{1,0:T(8,128)(2,1)S(1)}, u32[]{:S(2)}, u32[]{:S(2)}) collective-permute-start(bf16[128,768]{1,0:T(8,128)(2,1)S(1)} %get-tuple-element.54), channel_id=1, source_target_pairs={{0,17},{1,16},{2,19},{3,18},{8,25},{9,24},{10,27},{11,26},{16,1},{... | collective-permute-start | bytes 589832 | tf_op jit(solution)/shard_map/ppermute | solution.py:98
  94.8 8.6 %collective-permute-start.24 = (bf16[128,768]{1,0:T(8,128)(2,1)S(1)}, bf16[128,768]{1,0:T(8,128)(2,1)S(1)}, u32[]{:S(2)}, u32[]{:S(2)}) collective-permute-start(bf16[128,768]{1,0:T(8,128)(2,1)S(1)} %fusion.25), channel_id=1, source_target_pairs={{0,1},{1,0},{2,3},{3,2},{4,5},{5,4},{6,7},{7,6},{8,9},{9,8},{10,11... | collective-permute-start | bytes 589832 | tf_op jit(solution)/shard_map/ppermute | solution.py:98
  104.0 7.9 %collective-permute-start.26 = (bf16[128,768]{1,0:T(8,128)(2,1)S(1)}, bf16[128,768]{1,0:T(8,128)(2,1)S(1)}, u32[]{:S(2)}, u32[]{:S(2)}) collective-permute-start(bf16[128,768]{1,0:T(8,128)(2,1)S(1)} %multiply_convert_fusion.1.refs_0_), channel_id=1, source_target_pairs={{0,16},{8,24},{16,0},{24,8},{1,17},{9,25},{17,1},{25,9},{2,18},{10... | collective-permute-start | bytes 589832 | tf_op jit(solution)/shard_map/ppermute | solution.py:98
  105.1 10.0 %collective-permute-start.29 = (bf16[128,768]{1,0:T(8,128)(2,1)S(1)}, bf16[128,768]{1,0:T(8,128)(2,1)S(1)}, u32[]{:S(2)}, u32[]{:S(2)}) collective-permute-start(bf16[128,768]{1,0:T(8,128)(2,1)S(1)} %multiply_convert_fusion.1.refs_0_), channel_id=1, source_target_pairs={{0,4},{4,0},{1,5},{5,1},{2,6},{6,2},{3,7},{7,3},{8,12},{12,8},{9,1... | collective-permute-start | bytes 589832 | tf_op jit(solution)/shard_map/ppermute | solution.py:98
  105.4 9.8 %collective-permute-start.30 = (bf16[128,768]{1,0:T(8,128)(2,1)S(1)}, bf16[128,768]{1,0:T(8,128)(2,1)S(1)}, u32[]{:S(2)}, u32[]{:S(2)}) collective-permute-start(bf16[128,768]{1,0:T(8,128)(2,1)S(1)} %multiply_convert_fusion.1.refs_0_), channel_id=1, source_target_pairs={{0,20},{4,16},{8,28},{12,24},{16,4},{20,0},{24,12},{28,8},{1,21},{... | collective-permute-start | bytes 589832 | tf_op jit(solution)/shard_map/ppermute | solution.py:98
  107.5 8.2 %collective-permute-start.27 = (bf16[128,768]{1,0:T(8,128)(2,1)S(1)}, bf16[128,768]{1,0:T(8,128)(2,1)S(1)}, u32[]{:S(2)}, u32[]{:S(2)}) collective-permute-start(bf16[128,768]{1,0:T(8,128)(2,1)S(1)} %multiply_convert_fusion.1.refs_0_), channel_id=1, source_target_pairs={{0,8},{8,0},{16,24},{24,16},{1,9},{9,1},{17,25},{25,17},{2,10},{10... | collective-permute-start | bytes 589832 | tf_op jit(solution)/shard_map/ppermute | solution.py:98
  111.9 3.8 %collective-permute-start.28 = (bf16[128,768]{1,0:T(8,128)(2,1)S(1)}, bf16[128,768]{1,0:T(8,128)(2,1)S(1)}, u32[]{:S(2)}, u32[]{:S(2)}) collective-permute-start(bf16[128,768]{1,0:T(8,128)(2,1)S(1)} %collective-permute-done.26.refs_1_), channel_id=1, source_target_pairs={{0,8},{8,0},{16,24},{24,16},{1,9},{9,1},{17,25},{25,17},{2,10},{10... | collective-permute-start | bytes 589832 | tf_op jit(solution)/shard_map/ppermute | solution.py:98
  115.2 1.4 %collective-permute-start.31 = (bf16[128,768]{1,0:T(8,128)(2,1)S(1)}, bf16[128,768]{1,0:T(8,128)(2,1)S(1)}, u32[]{:S(2)}, u32[]{:S(2)}) collective-permute-start(bf16[128,768]{1,0:T(8,128)(2,1)S(1)} %collective-permute-done.29.refs_4_), channel_id=1, source_target_pairs={{0,8},{8,0},{16,24},{24,16},{1,9},{9,1},{17,25},{25,17},{2,10},{10... | collective-permute-start | bytes 589832 | tf_op jit(solution)/shard_map/ppermute | solution.py:98
  115.2 1.7 %collective-permute-start.32 = (bf16[128,768]{1,0:T(8,128)(2,1)S(1)}, bf16[128,768]{1,0:T(8,128)(2,1)S(1)}, u32[]{:S(2)}, u32[]{:S(2)}) collective-permute-start(bf16[128,768]{1,0:T(8,128)(2,1)S(1)} %collective-permute-done.30.refs_5_), channel_id=1, source_target_pairs={{0,8},{8,0},{16,24},{24,16},{1,9},{9,1},{17,25},{25,17},{2,10},{10... | collective-permute-start | bytes 589832 | tf_op jit(solution)/shard_map/ppermute | solution.py:98
  122.2 1.8 %collective-permute-start.33 = (bf16[2,192,512]{2,1,0:T(8,128)(2,1)S(1)}, bf16[2,192,512]{2,1,0:T(8,128)(2,1)S(1)}, u32[]{:S(2)}, u32[]{:S(2)}) collective-permute-start(bf16[2,192,512]{2,1,0:T(8,128)(2,1)S(1)} %get-tuple-element.40), channel_id=1, source_target_pairs={{0,8},{8,0},{16,24},{24,16},{1,9},{9,1},{17,25},{25,17},{2,10},{10... | collective-permute-start | bytes 1179656 | tf_op jit(solution)/shard_map/ppermute | solution.py:98
  124.2 7.1 %collective-permute-start.34 = (bf16[192,512]{1,0:T(8,128)(2,1)S(1)}, bf16[192,512]{1,0:T(8,128)(2,1)S(1)}, u32[]{:S(2)}, u32[]{:S(2)}) collective-permute-start(bf16[192,512]{1,0:T(8,128)(2,1)S(1)} %fusion.27), channel_id=1, source_target_pairs={{0,16},{8,24},{16,0},{24,8},{1,17},{9,25},{17,1},{25,9},{2,18},{10... | collective-permute-start | bytes 589832 | tf_op jit(solution)/shard_map/ppermute | solution.py:98

commit v18 on v17

--- a/solution.py
+++ b/solution.py
@@ -234,6 +234,7 @@
             proj,
             preferred_element_type=jnp.float32,
         )
+        normed = after(normed, residual)
         gate = jnp.dot(normed, gate_up[0], preferred_element_type=jnp.float32)
         up = jnp.dot(normed, gate_up[1], preferred_element_type=jnp.float32)
         hidden = (jax.nn.silu(gate) * up).astype(jnp.bfloat16)
@@ -246,7 +247,6 @@
 
         if ordered:
             late = [d.pop((1, 1)), d.pop((1, 3))]
-            proj = after(proj, residual)
             folded = fold(proj, after(place_rows(d)[0], hidden))
             for k, block in zip((1, 3), late):
                 at = row_of(1, k, block.shape[1])

time: 132 us -> 127 us (0.962)
  waiting for transfers between devices: 63.9 us -> 59 us
    ppermute x29, waiting for transfers between devices: 55 us -> 50.3 us  [flip(): return lax.ppermute(x, names if len(names) > 1 else names[0], pairs)]
  transfers between devices with their start and end apart: 35 -> 35, of which waited for: 18 -> 17; matrix products, arithmetic and copies ran while one was open for 15% -> 16% of each run, Pallas kernels for 0% -> 0%
where the time goes in v18:
time: 127 us
  waiting for transfers between devices  59 us (46%)
  starting transfers between devices  37.2 us (29%)
  other arithmetic  8.78 us (7%)
  matrix products  8.75 us (7%)
  local copies, waits for them, and re-layouts  6.6 us (5%)
  Pallas kernels  5.34 us (4%)
    ppermute x29, waiting for transfers between devices, flip(): return lax.ppermute(x, names if len(names) > 1 else names[0], pairs)  50.3 us
    ppermute x29, starting transfers between devices, flip(): return lax.ppermute(x, names if len(names) > 1 else names[0], pairs)  25.4 us
    ppermute x6, starting transfers between devices, rotate(): return lax.ppermute(x, 'dp', [(i, (i + k) % n_dp) for i in range(n_dp)])  11.8 us
    ppermute x6, waiting for transfers between devices, rotate(): return lax.ppermute(x, 'dp', [(i, (i + k) % n_dp) for i in range(n_dp)])  8.75 us
    pallas_call x1, Pallas kernels, per_device(): pl.pallas_call(lambda *refs: attend_kernel(*refs, heads=local_heads, mask...  5.34 us
  transfers between devices with their start and end apart: 35, of which 17 were waited for; matrix products, arithmetic and copies ran while one was open for 16% of the time, Pallas kernels for 0%

profile of v18, /device:TPU:0, one launch (start us, length us, event | category | flops | bytes accessed | tf_op | source)
XLA Modules:
  0.0 126.9 jit_solution(3493393077734619427)
XLA Ops:
  0.0 1.4 %fusion.13 = (bf16[2,192,512]{2,1,0:T(8,128)(2,1)S(1)}, bf16[2,192,512]{2,1,0:T(8,128)(2,1)S(1)}) fusion(s32[]{:T(128)S(6)} %select_n.236, bf16[1,192,1024]{2,1,0:T(8,128)(2,1)} %bitcast.92, bf16[1,192,1024]{2,1,0:T(8,128)(2,1)} %bitcast.93, s32[]{:T(128)S(6)} %select_n.238), kind=kLoop, calls=%fused_computation.29 | loop fusion | flops 1572864 | bytes 1572872 | tf_op jit(solution)/shard_map/stack | solution.py:163
  1.4 4.1 %collective-permute-start.3 = (bf16[2,192,512]{2,1,0:T(8,128)(2,1)S(1)}, bf16[2,192,512]{2,1,0:T(8,128)(2,1)S(1)}, u32[]{:S(2)}, u32[]{:S(2)}) collective-permute-start(bf16[2,192,512]{2,1,0:T(8,128)(2,1)S(1)} %get-tuple-element.51), channel_id=1, source_target_pairs={{0,2},{1,3},{2,0},{3,1},{4,6},{5,7},{6,4},{7,5},{8,10},{9,11},{10,... | collective-permute-start | bytes 1179656 | tf_op jit(solution)/shard_map/ppermute | solution.py:101
  5.5 1.5 %collective-permute-start.9 = (bf16[2,192,512]{2,1,0:T(8,128)(2,1)S(1)}, bf16[2,192,512]{2,1,0:T(8,128)(2,1)S(1)}, u32[]{:S(2)}, u32[]{:S(2)}) collective-permute-start(bf16[2,192,512]{2,1,0:T(8,128)(2,1)S(1)} %get-tuple-element.51), channel_id=1, source_target_pairs={{0,4},{4,0},{1,5},{5,1},{2,6},{6,2},{3,7},{7,3},{8,12},{12,8},{9,1... | collective-permute-start | bytes 1179656 | tf_op jit(solution)/shard_map/ppermute | solution.py:98
  7.0 1.5 %collective-permute-start.1 = (bf16[512,384]{1,0:T(8,128)(2,1)}, bf16[512,384]{1,0:T(8,128)(2,1)S(1)}, u32[]{:S(2)}, u32[]{:S(2)}) collective-permute-start(bf16[512,384]{1,0:T(8,128)(2,1)} %bitcast.94), channel_id=1, source_target_pairs={{0,16},{8,24},{16,0},{24,8},{1,17},{9,25},{17,1},{25,9},{2,18},{10... | collective-permute-start | bytes 1179656 | tf_op jit(solution)/shard_map/ppermute | solution.py:98
  8.5 1.6 %collective-permute-start = (bf16[512,384]{1,0:T(8,128)(2,1)}, bf16[512,384]{1,0:T(8,128)(2,1)}, u32[]{:S(2)}, u32[]{:S(2)}) collective-permute-start(bf16[512,384]{1,0:T(8,128)(2,1)} %bitcast.95), channel_id=1, source_target_pairs={{0,1},{1,0},{2,3},{3,2},{4,5},{5,4},{6,7},{7,6},{8,9},{9,8},{10,11... | collective-permute-start | bytes 1179656 | tf_op jit(solution)/shard_map/ppermute | solution.py:98
  10.1 1.8 %dynamic-slice_bitcast_fusion.2 = (bf16[1,192,512]{2,1,0:T(8,128)(2,1)}, bf16[1,192,512]{2,1,0:T(8,128)(2,1)}) fusion(bf16[1024,192]{0,1:T(8,128)(2,1)} %param.16, s32[]{:T(128)S(6)} %select_n.236, s32[]{:T(128)S(6)} %select_n.238), kind=kLoop, calls=%fused_computation.61 | loop fusion | bytes 786440 | tf_op jit(solution)/shard_map/dynamic_slice | solution.py:161
  13.0 0.7 fusion.30
  13.8 12.3 %collective-permute-done = bf16[512,384]{1,0:T(8,128)(2,1)} collective-permute-done((bf16[512,384]{1,0:T(8,128)(2,1)}, bf16[512,384]{1,0:T(8,128)(2,1)}, u32[]{:S(2)}, u32[]{:S(2)}) %collective-permute-start) | collective-permute-done | bytes 393248 | tf_op jit(solution)/shard_map/ppermute | solution.py:98
  27.7 1.1 copy.14
  29.0 0.8 collective-permute-start.10
  29.8 3.1 %collective-permute-start.15 = (bf16[2,192,512]{2,1,0:T(8,128)(2,1)S(1)}, bf16[2,192,512]{2,1,0:T(8,128)(2,1)S(1)}, u32[]{:S(2)}, u32[]{:S(2)}) collective-permute-start(bf16[2,192,512]{2,1,0:T(8,128)(2,1)S(1)} %get-tuple-element.26), channel_id=1, source_target_pairs={{0,3},{1,0},{2,1},{3,2},{4,7},{5,4},{6,5},{7,6},{8,11},{9,8},{10,9... | collective-permute-start | bytes 1179656 | tf_op jit(solution)/shard_map/ppermute | solution.py:101
  32.9 1.5 %collective-permute-start.7 = (bf16[384,768]{1,0:T(8,128)(2,1)S(1)}, bf16[384,768]{1,0:T(8,128)(2,1)S(1)}, u32[]{:S(2)}, u32[]{:S(2)}) collective-permute-start(bf16[384,768]{1,0:T(8,128)(2,1)S(1)} %copy-done.2), channel_id=1, source_target_pairs={{0,16},{8,24},{16,0},{24,8},{1,17},{9,25},{17,1},{25,9},{2,18},{10... | collective-permute-start | bytes 1769480 | tf_op jit(solution)/shard_map/ppermute | solution.py:98
  34.4 1.1 pad_maximum_fusion
  35.5 3.0 %collective-permute-done.2 = bf16[512,384]{1,0:T(8,128)(2,1)} collective-permute-done((bf16[512,384]{1,0:T(8,128)(2,1)}, bf16[512,384]{1,0:T(8,128)(2,1)}, u32[]{:S(2)}, u32[]{:S(2)}) %collective-permute-start.2) | collective-permute-done | bytes 393248 | tf_op jit(solution)/shard_map/ppermute | solution.py:98
  38.5 1.1 pad_maximum_fusion.1
  40.6 2.4 %collective-permute-done.10 = bf16[2,192,512]{2,1,0:T(8,128)(2,1)S(1)} collective-permute-done((bf16[2,192,512]{2,1,0:T(8,128)(2,1)S(1)}, bf16[2,192,512]{2,1,0:T(8,128)(2,1)S(1)}, u32[]{:S(2)}, u32[]{:S(2)}) %collective-permute-start.10) | collective-permute-done | bytes 393248 | tf_op jit(solution)/shard_map/ppermute | solution.py:101
  43.0 4.4 %collective-permute-done.15 = bf16[2,192,512]{2,1,0:T(8,128)(2,1)S(1)} collective-permute-done((bf16[2,192,512]{2,1,0:T(8,128)(2,1)S(1)}, bf16[2,192,512]{2,1,0:T(8,128)(2,1)S(1)}, u32[]{:S(2)}, u32[]{:S(2)}) %collective-permute-start.15) | collective-permute-done | bytes 393248 | tf_op jit(solution)/shard_map/ppermute | solution.py:101
  47.4 0.6 collective-permute-start.16
  48.0 1.0 constant_dynamic-update-slice_fusion.13
  49.2 1.5 %collective-permute-start.17 = (bf16[2,192,512]{2,1,0:T(8,128)(2,1)S(1)}, bf16[2,192,512]{2,1,0:T(8,128)(2,1)S(1)}, u32[]{:S(2)}, u32[]{:S(2)}) collective-permute-start(bf16[2,192,512]{2,1,0:T(8,128)(2,1)S(1)} %collective-permute-done.15), channel_id=1, source_target_pairs={{0,4},{4,0},{1,5},{5,1},{2,6},{6,2},{3,7},{7,3},{8,12},{12,8},{9,1... | collective-permute-start | bytes 1179656 | tf_op jit(solution)/shard_map/ppermute | solution.py:98
  51.6 1.0 fusion.2
  52.6 1.0 fusion.4
  53.8 2.0 %collective-permute-done.11 = bf16[1,192,512]{2,1,0:T(8,128)(2,1)S(1)} collective-permute-done((bf16[1,192,512]{2,1,0:T(8,128)(2,1)}, bf16[1,192,512]{2,1,0:T(8,128)(2,1)S(1)}, u32[]{:S(2)}, u32[]{:S(2)}) %collective-permute-start.11) | collective-permute-done | bytes 196640 | tf_op jit(solution)/shard_map/ppermute | solution.py:101
  55.7 3.4 %collective-permute-start.12 = (bf16[1,192,512]{2,1,0:T(8,128)(2,1)S(1)}, bf16[1,192,512]{2,1,0:T(8,128)(2,1)S(1)}, u32[]{:S(2)}, u32[]{:S(2)}) collective-permute-start(bf16[1,192,512]{2,1,0:T(8,128)(2,1)S(1)} %copy-done.5), channel_id=1, source_target_pairs={{0,1},{1,2},{2,3},{3,0},{4,5},{5,6},{6,7},{7,4},{8,9},{9,10},{10,1... | collective-permute-start | bytes 589832 | tf_op jit(solution)/shard_map/ppermute | solution.py:101
  59.6 1.6 %collective-permute-start.19 = (bf16[1,192,512]{2,1,0:T(8,128)(2,1)S(1)}, bf16[1,192,512]{2,1,0:T(8,128)(2,1)S(1)}, u32[]{:S(2)}, u32[]{:S(2)}) collective-permute-start(bf16[1,192,512]{2,1,0:T(8,128)(2,1)S(1)} %collective-permute-done.11), channel_id=1, source_target_pairs={{0,4},{4,0},{1,5},{5,1},{2,6},{6,2},{3,7},{7,3},{8,12},{12,8},{9,1... | collective-permute-start | bytes 589832 | tf_op jit(solution)/shard_map/ppermute | solution.py:98
  61.2 6.6 %collective-permute-done.17 = bf16[2,192,512]{2,1,0:T(8,128)(2,1)S(1)} collective-permute-done((bf16[2,192,512]{2,1,0:T(8,128)(2,1)S(1)}, bf16[2,192,512]{2,1,0:T(8,128)(2,1)S(1)}, u32[]{:S(2)}, u32[]{:S(2)}) %collective-permute-start.17) | collective-permute-done | bytes 393248 | tf_op jit(solution)/shard_map/ppermute | solution.py:98
  68.0 0.9 bitcast_dynamic-update-slice_fusion.4
  69.6 0.7 collective-permute-start.20
  70.3 1.4 %collective-permute-start.21 = (bf16[1,192,512]{2,1,0:T(8,128)(2,1)S(1)}, bf16[1,192,512]{2,1,0:T(8,128)(2,1)S(1)}, u32[]{:S(2)}, u32[]{:S(2)}) collective-permute-start(bf16[1,192,512]{2,1,0:T(8,128)(2,1)S(1)} %collective-permute-done.18), channel_id=1, source_target_pairs={{0,4},{4,0},{1,5},{5,1},{2,6},{6,2},{3,7},{7,3},{8,12},{12,8},{9,1... | collective-permute-start | bytes 589832 | tf_op jit(solution)/shard_map/ppermute | solution.py:98
  72.5 1.8 %fusion.5 = f32[1024,512]{1,0:T(8,128)S(1)} fusion(bf16[1024,1536]{1,0:T(8,128)(2,1)S(1)} %fusion.4, bf16[2,1536,512]{2,1,0:T(8,128)(2,1)S(1)} %constant_dynamic-update-slice_fusion.11), kind=kOutput, calls=%fused_computation.10 | convolution fusion | flops 1610612736 | bytes 6815744 | tf_op jit(solution)/shard_map/dot_general | solution.py:238
  74.2 2.0 %multiply_convert_fusion = bf16[1024,512]{1,0:T(8,128)(2,1)S(1)} fusion(f32[1024,512]{1,0:T(8,128)S(1)} %fusion.5, bf16[1024,1536]{1,0:T(8,128)(2,1)S(1)} %fusion.4, bf16[2,1536,512]{2,1,0:T(8,128)(2,1)S(1)} %constant_dynamic-update-slice_fusion.11), kind=kOutput, calls=%fused_computation.7 | convolution fusion | flops 1613758464 | bytes 7864320 | tf_op jit(solution)/shard_map/dot_general | solution.py:239
  76.3 1.4 %fusion.51 = f32[768,512]{1,0:T(8,128)S(1)} fusion(bf16[1536,768]{1,0:T(8,128)(2,1)S(1)} %constant_dynamic-update-slice_fusion.5, bf16[1536,512]{1,0:T(8,128)(2,1)S(1)} %bitcast_dynamic-update-slice_fusion), kind=kOutput, calls=%fused_computation.129 | convolution fusion | flops 1207959552 | bytes 5505024 | tf_op jit(solution)/shard_map/dot_general | solution.py:244
  78.1 2.6 %collective-permute-done.21 = bf16[1,192,512]{2,1,0:T(8,128)(2,1)S(1)} collective-permute-done((bf16[1,192,512]{2,1,0:T(8,128)(2,1)S(1)}, bf16[1,192,512]{2,1,0:T(8,128)(2,1)S(1)}, u32[]{:S(2)}, u32[]{:S(2)}) %collective-permute-start.21) | collective-permute-done | bytes 196640 | tf_op jit(solution)/shard_map/ppermute | solution.py:98
  81.1 0.6 convolution_convert_fusion
  81.8 1.7 %fusion.8 = f32[2,2,128,768]{3,2,1,0:T(8,128)S(1)} fusion(bf16[768,512,1,1]{1,0,3,2:T(8,128)(2,1)S(1)} %fusion.6, bf16[2,2,2,128,512]{4,3,2,1,0:T(8,128)(2,1)} %bitcast.98, s32[]{:T(128)S(6)} %select_n.278), kind=kOutput, calls=%fused_computation.24 | convolution fusion | flops 402653184 | bytes 2883588 | tf_op jit(solution)/shard_map/dot_general | solution.py:261
  84.9 4.7 %collective-permute-start.25 = (bf16[128,768]{1,0:T(8,128)(2,1)S(1)}, bf16[128,768]{1,0:T(8,128)(2,1)S(1)}, u32[]{:S(2)}, u32[]{:S(2)}) collective-permute-start(bf16[128,768]{1,0:T(8,128)(2,1)S(1)} %get-tuple-element.54), channel_id=1, source_target_pairs={{0,17},{1,16},{2,19},{3,18},{8,25},{9,24},{10,27},{11,26},{16,1},{... | collective-permute-start | bytes 589832 | tf_op jit(solution)/shard_map/ppermute | solution.py:98
  89.7 5.9 %collective-permute-done.23 = bf16[128,768]{1,0:T(8,128)(2,1)S(1)} collective-permute-done((bf16[128,768]{1,0:T(8,128)(2,1)S(1)}, bf16[128,768]{1,0:T(8,128)(2,1)S(1)}, u32[]{:S(2)}, u32[]{:S(2)}) %collective-permute-start.23) | collective-permute-done | bytes 196640 | tf_op jit(solution)/shard_map/ppermute | solution.py:98
  95.6 2.7 %collective-permute-done.24 = bf16[128,768]{1,0:T(8,128)(2,1)S(1)} collective-permute-done((bf16[128,768]{1,0:T(8,128)(2,1)S(1)}, bf16[128,768]{1,0:T(8,128)(2,1)S(1)}, u32[]{:S(2)}, u32[]{:S(2)}) %collective-permute-start.24) | collective-permute-done | bytes 196640 | tf_op jit(solution)/shard_map/ppermute | solution.py:98
  98.8 1.1 collective-permute-start.26
  100.3 2.1 %collective-permute-start.30 = (bf16[128,768]{1,0:T(8,128)(2,1)S(1)}, bf16[128,768]{1,0:T(8,128)(2,1)S(1)}, u32[]{:S(2)}, u32[]{:S(2)}) collective-permute-start(bf16[128,768]{1,0:T(8,128)(2,1)S(1)} %multiply_convert_fusion.1.refs_0_), channel_id=1, source_target_pairs={{0,20},{4,16},{8,28},{12,24},{16,4},{20,0},{24,12},{28,8},{1,21},{... | collective-permute-start | bytes 589832 | tf_op jit(solution)/shard_map/ppermute | solution.py:98
  102.4 4.3 %collective-permute-done.26.refs_1_ = bf16[128,768]{1,0:T(8,128)(2,1)S(1)} collective-permute-done((bf16[128,768]{1,0:T(8,128)(2,1)S(1)}, bf16[128,768]{1,0:T(8,128)(2,1)S(1)}, u32[]{:S(2)}, u32[]{:S(2)}) %collective-permute-start.26) | collective-permute-done | bytes 196640 | tf_op jit(solution)/shard_map/ppermute | solution.py:98
  106.7 3.3 %collective-permute-done.29.refs_4_ = bf16[128,768]{1,0:T(8,128)(2,1)S(1)} collective-permute-done((bf16[128,768]{1,0:T(8,128)(2,1)S(1)}, bf16[128,768]{1,0:T(8,128)(2,1)S(1)}, u32[]{:S(2)}, u32[]{:S(2)}) %collective-permute-start.29) | collective-permute-done | bytes 196640 | tf_op jit(solution)/shard_map/ppermute | solution.py:98
  110.6 0.9 collective-permute-done.31.refs_6_
  111.8 5.3 %shard_map.118 = (f32[2,192,512]{2,1,0:T(8,128)S(1)}, bf16[2,192,512]{2,1,0:T(8,128)(2,1)S(1)}) custom-call(bf16[128,768]{1,0:T(8,128)(2,1)S(1)} %multiply_convert_fusion.1.refs_0_, bf16[128,768]{1,0:T(8,128)(2,1)S(1)} %collective-permute-done.26.refs_1_, bf16[128,768]{1,0:T(8,128)(2,1)S(1)} %collective-permute-done.27.refs_2_, ...), custom_call_target="tpu_custom_call" | custom-call | flops 2516582400 | bytes 8388608 | tf_op jit(solution)/shard_map/pallas_call | solution.py:299
  117.4 1.5 %collective-permute-done.33 = bf16[2,192,512]{2,1,0:T(8,128)(2,1)S(1)} collective-permute-done((bf16[2,192,512]{2,1,0:T(8,128)(2,1)S(1)}, bf16[2,192,512]{2,1,0:T(8,128)(2,1)S(1)}, u32[]{:S(2)}, u32[]{:S(2)}) %collective-permute-start.33) | collective-permute-done | bytes 393248 | tf_op jit(solution)/shard_map/ppermute | solution.py:98
  119.1 1.0 collective-permute-start.34
  120.1 6.1 %collective-permute-done.34 = bf16[192,512]{1,0:T(8,128)(2,1)S(1)} collective-permute-done((bf16[192,512]{1,0:T(8,128)(2,1)S(1)}, bf16[192,512]{1,0:T(8,128)(2,1)S(1)}, u32[]{:S(2)}, u32[]{:S(2)}) %collective-permute-start.34) | collective-permute-done | bytes 196640 | tf_op jit(solution)/shard_map/ppermute | solution.py:98
  126.2 0.7 fusion.26
  (125 shorter events, 10.8 us)
Async XLA Ops:
  0.0 12.4 %copy-start.10 = (s32[1,3]{1,0:T(1,128)S(1)}, s32[1,3]{1,0:T(1,128)}, u32[]{:S(2)}) copy-start(s32[1,3]{1,0:T(1,128)} %param.21) | copy-start | bytes 40
  0.0 12.6 %copy-start.9 = (s32[4]{0:T(128)S(1)}, s32[4]{0:T(128)}, u32[]{:S(2)}) copy-start(s32[4]{0:T(128)} %param.23) | copy-start | bytes 52
  0.0 12.7 %copy-start.8 = (s32[4]{0:T(128)S(1)}, s32[4]{0:T(128)}, u32[]{:S(2)}) copy-start(s32[4]{0:T(128)} %param.22) | copy-start | bytes 52
  0.0 13.7 %copy-start.6 = (f32[1536]{0:T(1024)S(1)}, f32[1536]{0:T(1024)}, u32[]{:S(2)}) copy-start(f32[1536]{0:T(1024)} %param.13) | copy-start | bytes 18436
  0.0 28.9 %copy-start.2 = (bf16[384,768]{1,0:T(8,128)(2,1)S(1)}, bf16[384,768]{1,0:T(8,128)(2,1)}, u32[]{:S(2)}) copy-start(bf16[384,768]{1,0:T(8,128)(2,1)} %param.17) | copy-start | bytes 1769476
  0.0 34.3 %copy-start.3 = (bf16[1,512,384]{2,1,0:T(8,128)(2,1)S(1)}, bf16[1,512,384]{2,1,0:T(8,128)(2,1)}, u32[]{:S(2)}) copy-start(bf16[1,512,384]{2,1,0:T(8,128)(2,1)} %param.12) | copy-start | bytes 1179652
  1.4 25.7 %collective-permute-start.3 = (bf16[2,192,512]{2,1,0:T(8,128)(2,1)S(1)}, bf16[2,192,512]{2,1,0:T(8,128)(2,1)S(1)}, u32[]{:S(2)}, u32[]{:S(2)}) collective-permute-start(bf16[2,192,512]{2,1,0:T(8,128)(2,1)S(1)} %get-tuple-element.51), channel_id=1, source_target_pairs={{0,2},{1,3},{2,0},{3,1},{4,6},{5,7},{6,4},{7,5},{8,10},{9,11},{10,... | collective-permute-start | bytes 1179656 | tf_op jit(solution)/shard_map/ppermute | solution.py:101
  5.5 23.5 %collective-permute-start.9 = (bf16[2,192,512]{2,1,0:T(8,128)(2,1)S(1)}, bf16[2,192,512]{2,1,0:T(8,128)(2,1)S(1)}, u32[]{:S(2)}, u32[]{:S(2)}) collective-permute-start(bf16[2,192,512]{2,1,0:T(8,128)(2,1)S(1)} %get-tuple-element.51), channel_id=1, source_target_pairs={{0,4},{4,0},{1,5},{5,1},{2,6},{6,2},{3,7},{7,3},{8,12},{12,8},{9,1... | collective-permute-start | bytes 1179656 | tf_op jit(solution)/shard_map/ppermute | solution.py:98
  7.0 22.0 %collective-permute-start.1 = (bf16[512,384]{1,0:T(8,128)(2,1)}, bf16[512,384]{1,0:T(8,128)(2,1)S(1)}, u32[]{:S(2)}, u32[]{:S(2)}) collective-permute-start(bf16[512,384]{1,0:T(8,128)(2,1)} %bitcast.94), channel_id=1, source_target_pairs={{0,16},{8,24},{16,0},{24,8},{1,17},{9,25},{17,1},{25,9},{2,18},{10... | collective-permute-start | bytes 1179656 | tf_op jit(solution)/shard_map/ppermute | solution.py:98
  8.5 17.6 %collective-permute-start = (bf16[512,384]{1,0:T(8,128)(2,1)}, bf16[512,384]{1,0:T(8,128)(2,1)}, u32[]{:S(2)}, u32[]{:S(2)}) collective-permute-start(bf16[512,384]{1,0:T(8,128)(2,1)} %bitcast.95), channel_id=1, source_target_pairs={{0,1},{1,0},{2,3},{3,2},{4,5},{5,4},{6,7},{7,6},{8,9},{9,8},{10,11... | collective-permute-start | bytes 1179656 | tf_op jit(solution)/shard_map/ppermute | solution.py:98
  11.9 17.1 %collective-permute-start.8 = (bf16[1,192,512]{2,1,0:T(8,128)(2,1)}, bf16[1,192,512]{2,1,0:T(8,128)(2,1)}, u32[]{:S(2)}, u32[]{:S(2)}) collective-permute-start(bf16[1,192,512]{2,1,0:T(8,128)(2,1)} %get-tuple-element.27), channel_id=1, source_target_pairs={{0,4},{4,0},{1,5},{5,1},{2,6},{6,2},{3,7},{7,3},{8,12},{12,8},{9,1... | collective-permute-start | bytes 589832 | tf_op jit(solution)/shard_map/ppermute | solution.py:98
  26.1 12.4 %collective-permute-start.2 = (bf16[512,384]{1,0:T(8,128)(2,1)}, bf16[512,384]{1,0:T(8,128)(2,1)}, u32[]{:S(2)}, u32[]{:S(2)}) collective-permute-start(bf16[512,384]{1,0:T(8,128)(2,1)} %collective-permute-done), channel_id=1, source_target_pairs={{0,16},{8,24},{16,0},{24,8},{1,17},{9,25},{17,1},{25,9},{2,18},{10... | collective-permute-start | bytes 1179656 | tf_op jit(solution)/shard_map/ppermute | solution.py:98
  27.2 12.4 %collective-permute-start.4 = (bf16[2,192,512]{2,1,0:T(8,128)(2,1)S(1)}, bf16[2,192,512]{2,1,0:T(8,128)(2,1)}, u32[]{:S(2)}, u32[]{:S(2)}) collective-permute-start(bf16[2,192,512]{2,1,0:T(8,128)(2,1)S(1)} %collective-permute-done.3), channel_id=1, source_target_pairs={{0,4},{4,0},{1,5},{5,1},{2,6},{6,2},{3,7},{7,3},{8,12},{12,8},{9,1... | collective-permute-start | bytes 1179656 | tf_op jit(solution)/shard_map/ppermute | solution.py:98
  29.0 13.9 %collective-permute-start.10 = (bf16[2,192,512]{2,1,0:T(8,128)(2,1)S(1)}, bf16[2,192,512]{2,1,0:T(8,128)(2,1)S(1)}, u32[]{:S(2)}, u32[]{:S(2)}) collective-permute-start(bf16[2,192,512]{2,1,0:T(8,128)(2,1)S(1)} %get-tuple-element.26), channel_id=1, source_target_pairs={{0,1},{1,2},{2,3},{3,0},{4,5},{5,6},{6,7},{7,4},{8,9},{9,10},{10,1... | collective-permute-start | bytes 1179656 | tf_op jit(solution)/shard_map/ppermute | solution.py:101
  29.8 17.6 %collective-permute-start.15 = (bf16[2,192,512]{2,1,0:T(8,128)(2,1)S(1)}, bf16[2,192,512]{2,1,0:T(8,128)(2,1)S(1)}, u32[]{:S(2)}, u32[]{:S(2)}) collective-permute-start(bf16[2,192,512]{2,1,0:T(8,128)(2,1)S(1)} %get-tuple-element.26), channel_id=1, source_target_pairs={{0,3},{1,0},{2,1},{3,2},{4,7},{5,4},{6,5},{7,6},{8,11},{9,8},{10,9... | collective-permute-start | bytes 1179656 | tf_op jit(solution)/shard_map/ppermute | solution.py:101
  32.9 36.1 %collective-permute-start.7 = (bf16[384,768]{1,0:T(8,128)(2,1)S(1)}, bf16[384,768]{1,0:T(8,128)(2,1)S(1)}, u32[]{:S(2)}, u32[]{:S(2)}) collective-permute-start(bf16[384,768]{1,0:T(8,128)(2,1)S(1)} %copy-done.2), channel_id=1, source_target_pairs={{0,16},{8,24},{16,0},{24,8},{1,17},{9,25},{17,1},{25,9},{2,18},{10... | collective-permute-start | bytes 1769480 | tf_op jit(solution)/shard_map/ppermute | solution.py:98
  39.6 9.6 %collective-permute-start.5 = (bf16[1024,384]{1,0:T(8,128)(2,1)S(1)}, bf16[1024,384]{1,0:T(8,128)(2,1)S(1)}, u32[]{:S(2)}, u32[]{:S(2)}) collective-permute-start(bf16[1024,384]{1,0:T(8,128)(2,1)S(1)} %pad_maximum_fusion), channel_id=1, source_target_pairs={{0,8},{8,0},{16,24},{24,16},{1,9},{9,1},{17,25},{25,17},{2,10},{10... | collective-permute-start | bytes 2359304 | tf_op jit(solution)/shard_map/ppermute | solution.py:98
  40.0 11.0 %collective-permute-start.6 = (bf16[1024,384]{1,0:T(8,128)(2,1)S(1)}, bf16[1024,384]{1,0:T(8,128)(2,1)S(1)}, u32[]{:S(2)}, u32[]{:S(2)}) collective-permute-start(bf16[1024,384]{1,0:T(8,128)(2,1)S(1)} %pad_maximum_fusion.1), channel_id=1, source_target_pairs={{0,8},{8,0},{16,24},{24,16},{1,9},{9,1},{17,25},{25,17},{2,10},{10... | collective-permute-start | bytes 2359304 | tf_op jit(solution)/shard_map/ppermute | solution.py:98
  42.9 12.8 %collective-permute-start.11 = (bf16[1,192,512]{2,1,0:T(8,128)(2,1)}, bf16[1,192,512]{2,1,0:T(8,128)(2,1)S(1)}, u32[]{:S(2)}, u32[]{:S(2)}) collective-permute-start(bf16[1,192,512]{2,1,0:T(8,128)(2,1)} %get-tuple-element.27), channel_id=1, source_target_pairs={{0,2},{1,3},{2,0},{3,1},{4,6},{5,7},{6,4},{7,5},{8,10},{9,11},{10,... | collective-permute-start | bytes 589832 | tf_op jit(solution)/shard_map/ppermute | solution.py:101
  47.4 12.2 %collective-permute-start.16 = (bf16[2,192,512]{2,1,0:T(8,128)(2,1)S(1)}, bf16[2,192,512]{2,1,0:T(8,128)(2,1)S(1)}, u32[]{:S(2)}, u32[]{:S(2)}) collective-permute-start(bf16[2,192,512]{2,1,0:T(8,128)(2,1)S(1)} %collective-permute-done.10), channel_id=1, source_target_pairs={{0,4},{4,0},{1,5},{5,1},{2,6},{6,2},{3,7},{7,3},{8,12},{12,8},{9,1... | collective-permute-start | bytes 1179656 | tf_op jit(solution)/shard_map/ppermute | solution.py:98
  49.2 18.6 %collective-permute-start.17 = (bf16[2,192,512]{2,1,0:T(8,128)(2,1)S(1)}, bf16[2,192,512]{2,1,0:T(8,128)(2,1)S(1)}, u32[]{:S(2)}, u32[]{:S(2)}) collective-permute-start(bf16[2,192,512]{2,1,0:T(8,128)(2,1)S(1)} %collective-permute-done.15), channel_id=1, source_target_pairs={{0,4},{4,0},{1,5},{5,1},{2,6},{6,2},{3,7},{7,3},{8,12},{12,8},{9,1... | collective-permute-start | bytes 1179656 | tf_op jit(solution)/shard_map/ppermute | solution.py:98
  53.6 2.1 %copy-start.5 = (bf16[1,192,512]{2,1,0:T(8,128)(2,1)S(1)}, bf16[1,192,512]{2,1,0:T(8,128)(2,1)}, u32[]{:S(2)}) copy-start(bf16[1,192,512]{2,1,0:T(8,128)(2,1)} %get-tuple-element.29) | copy-start | bytes 589828
  53.6 14.2 %copy-start.1 = (bf16[1024,192]{0,1:T(8,128)(2,1)S(1)}, bf16[1024,192]{0,1:T(8,128)(2,1)}, u32[]{:S(2)}) copy-start(bf16[1024,192]{0,1:T(8,128)(2,1)} %param.16) | copy-start | bytes 1179652
  55.7 13.3 %collective-permute-start.12 = (bf16[1,192,512]{2,1,0:T(8,128)(2,1)S(1)}, bf16[1,192,512]{2,1,0:T(8,128)(2,1)S(1)}, u32[]{:S(2)}, u32[]{:S(2)}) collective-permute-start(bf16[1,192,512]{2,1,0:T(8,128)(2,1)S(1)} %copy-done.5), channel_id=1, source_target_pairs={{0,1},{1,2},{2,3},{3,0},{4,5},{5,6},{6,7},{7,4},{8,9},{9,10},{10,1... | collective-permute-start | bytes 589832 | tf_op jit(solution)/shard_map/ppermute | solution.py:101
  59.2 11.1 %collective-permute-start.18 = (bf16[1,192,512]{2,1,0:T(8,128)(2,1)S(1)}, bf16[1,192,512]{2,1,0:T(8,128)(2,1)S(1)}, u32[]{:S(2)}, u32[]{:S(2)}) collective-permute-start(bf16[1,192,512]{2,1,0:T(8,128)(2,1)S(1)} %copy-done.5), channel_id=1, source_target_pairs={{0,3},{1,0},{2,1},{3,2},{4,7},{5,4},{6,5},{7,6},{8,11},{9,8},{10,9... | collective-permute-start | bytes 589832 | tf_op jit(solution)/shard_map/ppermute | solution.py:101
  59.6 12.1 %collective-permute-start.19 = (bf16[1,192,512]{2,1,0:T(8,128)(2,1)S(1)}, bf16[1,192,512]{2,1,0:T(8,128)(2,1)S(1)}, u32[]{:S(2)}, u32[]{:S(2)}) collective-permute-start(bf16[1,192,512]{2,1,0:T(8,128)(2,1)S(1)} %collective-permute-done.11), channel_id=1, source_target_pairs={{0,4},{4,0},{1,5},{5,1},{2,6},{6,2},{3,7},{7,3},{8,12},{12,8},{9,1... | collective-permute-start | bytes 589832 | tf_op jit(solution)/shard_map/ppermute | solution.py:98
  69.0 2.7 %collective-permute-start.13 = (bf16[384,768]{1,0:T(8,128)(2,1)S(1)}, bf16[384,768]{1,0:T(8,128)(2,1)S(1)}, u32[]{:S(2)}, u32[]{:S(2)}) collective-permute-start(bf16[384,768]{1,0:T(8,128)(2,1)S(1)} %copy-done.2), channel_id=1, source_target_pairs={{0,8},{8,0},{16,24},{24,16},{1,9},{9,1},{17,25},{25,17},{2,10},{10... | collective-permute-start | bytes 1769480 | tf_op jit(solution)/shard_map/ppermute | solution.py:98
  69.1 2.8 %collective-permute-start.14 = (bf16[384,768]{1,0:T(8,128)(2,1)S(1)}, bf16[384,768]{1,0:T(8,128)(2,1)S(1)}, u32[]{:S(2)}, u32[]{:S(2)}) collective-permute-start(bf16[384,768]{1,0:T(8,128)(2,1)S(1)} %collective-permute-done.7), channel_id=1, source_target_pairs={{0,8},{8,0},{16,24},{24,16},{1,9},{9,1},{17,25},{25,17},{2,10},{10... | collective-permute-start | bytes 1769480 | tf_op jit(solution)/shard_map/ppermute | solution.py:98
  69.6 8.1 %collective-permute-start.20 = (bf16[1,192,512]{2,1,0:T(8,128)(2,1)S(1)}, bf16[1,192,512]{2,1,0:T(8,128)(2,1)S(1)}, u32[]{:S(2)}, u32[]{:S(2)}) collective-permute-start(bf16[1,192,512]{2,1,0:T(8,128)(2,1)S(1)} %collective-permute-done.12), channel_id=1, source_target_pairs={{0,4},{4,0},{1,5},{5,1},{2,6},{6,2},{3,7},{7,3},{8,12},{12,8},{9,1... | collective-permute-start | bytes 589832 | tf_op jit(solution)/shard_map/ppermute | solution.py:98
  70.3 10.4 %collective-permute-start.21 = (bf16[1,192,512]{2,1,0:T(8,128)(2,1)S(1)}, bf16[1,192,512]{2,1,0:T(8,128)(2,1)S(1)}, u32[]{:S(2)}, u32[]{:S(2)}) collective-permute-start(bf16[1,192,512]{2,1,0:T(8,128)(2,1)S(1)} %collective-permute-done.18), channel_id=1, source_target_pairs={{0,4},{4,0},{1,5},{5,1},{2,6},{6,2},{3,7},{7,3},{8,12},{12,8},{9,1... | collective-permute-start | bytes 589832 | tf_op jit(solution)/shard_map/ppermute | solution.py:98
  76.2 4.9 %copy-start.4 = (bf16[1024,512]{1,0:T(8,128)(2,1)}, bf16[1024,512]{1,0:T(8,128)(2,1)S(1)}, u32[]{:S(2)}) copy-start(bf16[1024,512]{1,0:T(8,128)(2,1)S(1)} %multiply_convert_fusion) | copy-start | bytes 3145732
  81.7 2.4 %collective-permute-start.22 = (bf16[2,2,128,768]{3,2,1,0:T(8,128)(2,1)S(1)}, bf16[2,2,128,768]{3,2,1,0:T(8,128)(2,1)S(1)}, u32[]{:S(2)}, u32[]{:S(2)}) collective-permute-start(bf16[2,2,128,768]{3,2,1,0:T(8,128)(2,1)S(1)} %convolution_convert_fusion), channel_id=1, source_target_pairs={{0,8},{8,0},{16,24},{24,16},{1,9},{9,1},{17,25},{25,17},{2,10},{10... | collective-permute-start | bytes 2359304 | tf_op jit(solution)/shard_map/ppermute | solution.py:98
  84.3 14.4 %copy-start.7 = (f32[768]{0:T(1024)S(1)}, f32[768]{0:T(1024)}, u32[]{:S(2)}) copy-start(f32[768]{0:T(1024)} %param.18) | copy-start | bytes 9220
  84.3 27.5 %copy-start = (bf16[3,768,192]{1,2,0:T(8,128)(2,1)S(1)}, bf16[3,768,192]{1,2,0:T(8,128)(2,1)}, u32[]{:S(2)}) copy-start(bf16[3,768,192]{1,2,0:T(8,128)(2,1)} %param.19) | copy-start | bytes 2654212
  84.4 11.2 %collective-permute-start.23 = (bf16[128,768]{1,0:T(8,128)(2,1)S(1)}, bf16[128,768]{1,0:T(8,128)(2,1)S(1)}, u32[]{:S(2)}, u32[]{:S(2)}) collective-permute-start(bf16[128,768]{1,0:T(8,128)(2,1)S(1)} %get-tuple-element.53), channel_id=1, source_target_pairs={{0,16},{8,24},{16,0},{24,8},{1,17},{9,25},{17,1},{25,9},{2,18},{10... | collective-permute-start | bytes 589832 | tf_op jit(solution)/shard_map/ppermute | solution.py:98
  84.9 10.7 %collective-permute-start.25 = (bf16[128,768]{1,0:T(8,128)(2,1)S(1)}, bf16[128,768]{1,0:T(8,128)(2,1)S(1)}, u32[]{:S(2)}, u32[]{:S(2)}) collective-permute-start(bf16[128,768]{1,0:T(8,128)(2,1)S(1)} %get-tuple-element.54), channel_id=1, source_target_pairs={{0,17},{1,16},{2,19},{3,18},{8,25},{9,24},{10,27},{11,26},{16,1},{... | collective-permute-start | bytes 589832 | tf_op jit(solution)/shard_map/ppermute | solution.py:98
  89.6 8.6 %collective-permute-start.24 = (bf16[128,768]{1,0:T(8,128)(2,1)S(1)}, bf16[128,768]{1,0:T(8,128)(2,1)S(1)}, u32[]{:S(2)}, u32[]{:S(2)}) collective-permute-start(bf16[128,768]{1,0:T(8,128)(2,1)S(1)} %fusion.25), channel_id=1, source_target_pairs={{0,1},{1,0},{2,3},{3,2},{4,5},{5,4},{6,7},{7,6},{8,9},{9,8},{10,11... | collective-permute-start | bytes 589832 | tf_op jit(solution)/shard_map/ppermute | solution.py:98
  98.8 7.9 %collective-permute-start.26 = (bf16[128,768]{1,0:T(8,128)(2,1)S(1)}, bf16[128,768]{1,0:T(8,128)(2,1)S(1)}, u32[]{:S(2)}, u32[]{:S(2)}) collective-permute-start(bf16[128,768]{1,0:T(8,128)(2,1)S(1)} %multiply_convert_fusion.1.refs_0_), channel_id=1, source_target_pairs={{0,16},{8,24},{16,0},{24,8},{1,17},{9,25},{17,1},{25,9},{2,18},{10... | collective-permute-start | bytes 589832 | tf_op jit(solution)/shard_map/ppermute | solution.py:98
  100.0 10.0 %collective-permute-start.29 = (bf16[128,768]{1,0:T(8,128)(2,1)S(1)}, bf16[128,768]{1,0:T(8,128)(2,1)S(1)}, u32[]{:S(2)}, u32[]{:S(2)}) collective-permute-start(bf16[128,768]{1,0:T(8,128)(2,1)S(1)} %multiply_convert_fusion.1.refs_0_), channel_id=1, source_target_pairs={{0,4},{4,0},{1,5},{5,1},{2,6},{6,2},{3,7},{7,3},{8,12},{12,8},{9,1... | collective-permute-start | bytes 589832 | tf_op jit(solution)/shard_map/ppermute | solution.py:98
  100.3 9.8 %collective-permute-start.30 = (bf16[128,768]{1,0:T(8,128)(2,1)S(1)}, bf16[128,768]{1,0:T(8,128)(2,1)S(1)}, u32[]{:S(2)}, u32[]{:S(2)}) collective-permute-start(bf16[128,768]{1,0:T(8,128)(2,1)S(1)} %multiply_convert_fusion.1.refs_0_), channel_id=1, source_target_pairs={{0,20},{4,16},{8,28},{12,24},{16,4},{20,0},{24,12},{28,8},{1,21},{... | collective-permute-start | bytes 589832 | tf_op jit(solution)/shard_map/ppermute | solution.py:98
  102.4 8.2 %collective-permute-start.27 = (bf16[128,768]{1,0:T(8,128)(2,1)S(1)}, bf16[128,768]{1,0:T(8,128)(2,1)S(1)}, u32[]{:S(2)}, u32[]{:S(2)}) collective-permute-start(bf16[128,768]{1,0:T(8,128)(2,1)S(1)} %multiply_convert_fusion.1.refs_0_), channel_id=1, source_target_pairs={{0,8},{8,0},{16,24},{24,16},{1,9},{9,1},{17,25},{25,17},{2,10},{10... | collective-permute-start | bytes 589832 | tf_op jit(solution)/shard_map/ppermute | solution.py:98
  106.7 3.8 %collective-permute-start.28 = (bf16[128,768]{1,0:T(8,128)(2,1)S(1)}, bf16[128,768]{1,0:T(8,128)(2,1)S(1)}, u32[]{:S(2)}, u32[]{:S(2)}) collective-permute-start(bf16[128,768]{1,0:T(8,128)(2,1)S(1)} %collective-permute-done.26.refs_1_), channel_id=1, source_target_pairs={{0,8},{8,0},{16,24},{24,16},{1,9},{9,1},{17,25},{25,17},{2,10},{10... | collective-permute-start | bytes 589832 | tf_op jit(solution)/shard_map/ppermute | solution.py:98
  110.0 1.4 %collective-permute-start.31 = (bf16[128,768]{1,0:T(8,128)(2,1)S(1)}, bf16[128,768]{1,0:T(8,128)(2,1)S(1)}, u32[]{:S(2)}, u32[]{:S(2)}) collective-permute-start(bf16[128,768]{1,0:T(8,128)(2,1)S(1)} %collective-permute-done.29.refs_4_), channel_id=1, source_target_pairs={{0,8},{8,0},{16,24},{24,16},{1,9},{9,1},{17,25},{25,17},{2,10},{10... | collective-permute-start | bytes 589832 | tf_op jit(solution)/shard_map/ppermute | solution.py:98
  110.0 1.7 %collective-permute-start.32 = (bf16[128,768]{1,0:T(8,128)(2,1)S(1)}, bf16[128,768]{1,0:T(8,128)(2,1)S(1)}, u32[]{:S(2)}, u32[]{:S(2)}) collective-permute-start(bf16[128,768]{1,0:T(8,128)(2,1)S(1)} %collective-permute-done.30.refs_5_), channel_id=1, source_target_pairs={{0,8},{8,0},{16,24},{24,16},{1,9},{9,1},{17,25},{25,17},{2,10},{10... | collective-permute-start | bytes 589832 | tf_op jit(solution)/shard_map/ppermute | solution.py:98
  117.1 1.8 %collective-permute-start.33 = (bf16[2,192,512]{2,1,0:T(8,128)(2,1)S(1)}, bf16[2,192,512]{2,1,0:T(8,128)(2,1)S(1)}, u32[]{:S(2)}, u32[]{:S(2)}) collective-permute-start(bf16[2,192,512]{2,1,0:T(8,128)(2,1)S(1)} %get-tuple-element.40), channel_id=1, source_target_pairs={{0,8},{8,0},{16,24},{24,16},{1,9},{9,1},{17,25},{25,17},{2,10},{10... | collective-permute-start | bytes 1179656 | tf_op jit(solution)/shard_map/ppermute | solution.py:98
  119.1 7.1 %collective-permute-start.34 = (bf16[192,512]{1,0:T(8,128)(2,1)S(1)}, bf16[192,512]{1,0:T(8,128)(2,1)S(1)}, u32[]{:S(2)}, u32[]{:S(2)}) collective-permute-start(bf16[192,512]{1,0:T(8,128)(2,1)S(1)} %fusion.27), channel_id=1, source_target_pairs={{0,16},{8,24},{16,0},{24,8},{1,17},{9,25},{17,1},{25,9},{2,18},{10... | collective-permute-start | bytes 589832 | tf_op jit(solution)/shard_map/ppermute | solution.py:98

commit v19 on v18

--- a/solution.py
+++ b/solution.py
@@ -211,11 +211,12 @@
             far = rotate(after(down_same, g[0, 1]), 2)
             rows = jnp.concatenate([both, both_c, across, across_c], axis=1)
             normed = layer_norm(rows.astype(jnp.float32), gain).astype(jnp.bfloat16)
-            g[1, 1], g[1, 3] = (after(flip(g[0, k], seq=1), normed) for k in (1, 3))
-            gate_up = place_rows(g)
+            g[1, 1] = after(flip(after(g[0, 1], both_c), seq=1), normed)
             d[0, 2] = after(far, normed)
             for k in (1, 3):
                 d[0, k] = rotate(after(down_other, d[0, 2], code, out_w), k)
+            g[1, 3] = after(flip(g[0, 3], seq=1), d[0, 1], d[0, 3])
+            gate_up = place_rows(g)
             proj_c = flip(after(w_proj, proj_x, d[0, 1]), section=1)
             proj_xc = flip(after(proj_x, d[0, 1]), section=1)
             proj = jnp.concatenate([w_proj, proj_c, proj_x, proj_xc], axis=0)

time: 127 us -> 128 us (level)
  waiting for transfers between devices: 59 us -> 62.3 us
  starting transfers between devices: 37.2 us -> 34.2 us
    ppermute x6, waiting for transfers between devices: 8.75 us -> 14.3 us  [rotate(): return lax.ppermute(x, 'dp', [(i, (i + k) % n_dp) for i in range(n_dp)])]
    ppermute x29, starting transfers between devices: 25.4 us -> 22.4 us  [flip(): return lax.ppermute(x, names if len(names) > 1 else names[0], pairs)]
    ppermute x29, waiting for transfers between devices: 50.3 us -> 48 us  [flip(): return lax.ppermute(x, names if len(names) > 1 else names[0], pairs)]
  transfers between devices with their start and end apart: 35 -> 35, of which waited for: 17 -> 19; matrix products, arithmetic and copies ran while one was open for 16% -> 16% of each run, Pallas kernels for 0% -> 0%
where the time goes in v19:
time: 128 us; the launch traced here: 127 us
  waiting for transfers between devices  62.3 us (49%)
  starting transfers between devices  34.2 us (27%)
  matrix products  8.8 us (7%)
  other arithmetic  8.77 us (7%)
  local copies, waits for them, and re-layouts  6.59 us (5%)
  Pallas kernels  5.35 us (4%)
    ppermute x29, waiting for transfers between devices, flip(): return lax.ppermute(x, names if len(names) > 1 else names[0], pairs)  48 us
    ppermute x29, starting transfers between devices, flip(): return lax.ppermute(x, names if len(names) > 1 else names[0], pairs)  22.4 us
    ppermute x6, waiting for transfers between devices, rotate(): return lax.ppermute(x, 'dp', [(i, (i + k) % n_dp) for i in range(n_dp)])  14.3 us
    ppermute x6, starting transfers between devices, rotate(): return lax.ppermute(x, 'dp', [(i, (i + k) % n_dp) for i in range(n_dp)])  11.8 us
    pallas_call x1, Pallas kernels, per_device(): pl.pallas_call(lambda *refs: attend_kernel(*refs, heads=local_heads, mask...  5.35 us
  transfers between devices with their start and end apart: 35, of which 19 were waited for; matrix products, arithmetic and copies ran while one was open for 16% of the time, Pallas kernels for 0%

profile of v19, /device:TPU:0, one launch (start us, length us, event | category | flops | bytes accessed | tf_op | source)
XLA Modules:
  0.0 127.2 jit_solution(3022036665178769279)
XLA Ops:
  0.0 1.4 %fusion.13 = (bf16[2,192,512]{2,1,0:T(8,128)(2,1)S(1)}, bf16[2,192,512]{2,1,0:T(8,128)(2,1)S(1)}) fusion(s32[]{:T(128)S(6)} %select_n.236, bf16[1,192,1024]{2,1,0:T(8,128)(2,1)} %bitcast.92, bf16[1,192,1024]{2,1,0:T(8,128)(2,1)} %bitcast.93, s32[]{:T(128)S(6)} %select_n.238), kind=kLoop, calls=%fused_computation.29 | loop fusion | flops 1572864 | bytes 1572872 | tf_op jit(solution)/shard_map/stack | solution.py:163
  1.4 4.1 %collective-permute-start.3 = (bf16[2,192,512]{2,1,0:T(8,128)(2,1)S(1)}, bf16[2,192,512]{2,1,0:T(8,128)(2,1)S(1)}, u32[]{:S(2)}, u32[]{:S(2)}) collective-permute-start(bf16[2,192,512]{2,1,0:T(8,128)(2,1)S(1)} %get-tuple-element.53), channel_id=1, source_target_pairs={{0,2},{1,3},{2,0},{3,1},{4,6},{5,7},{6,4},{7,5},{8,10},{9,11},{10,... | collective-permute-start | bytes 1179656 | tf_op jit(solution)/shard_map/ppermute | solution.py:101
  5.5 1.5 %collective-permute-start.9 = (bf16[2,192,512]{2,1,0:T(8,128)(2,1)S(1)}, bf16[2,192,512]{2,1,0:T(8,128)(2,1)S(1)}, u32[]{:S(2)}, u32[]{:S(2)}) collective-permute-start(bf16[2,192,512]{2,1,0:T(8,128)(2,1)S(1)} %get-tuple-element.53), channel_id=1, source_target_pairs={{0,4},{4,0},{1,5},{5,1},{2,6},{6,2},{3,7},{7,3},{8,12},{12,8},{9,1... | collective-permute-start | bytes 1179656 | tf_op jit(solution)/shard_map/ppermute | solution.py:98
  7.0 1.5 %collective-permute-start.1 = (bf16[512,384]{1,0:T(8,128)(2,1)}, bf16[512,384]{1,0:T(8,128)(2,1)S(1)}, u32[]{:S(2)}, u32[]{:S(2)}) collective-permute-start(bf16[512,384]{1,0:T(8,128)(2,1)} %bitcast.94), channel_id=1, source_target_pairs={{0,16},{8,24},{16,0},{24,8},{1,17},{9,25},{17,1},{25,9},{2,18},{10... | collective-permute-start | bytes 1179656 | tf_op jit(solution)/shard_map/ppermute | solution.py:98
  8.5 1.6 %collective-permute-start = (bf16[512,384]{1,0:T(8,128)(2,1)}, bf16[512,384]{1,0:T(8,128)(2,1)}, u32[]{:S(2)}, u32[]{:S(2)}) collective-permute-start(bf16[512,384]{1,0:T(8,128)(2,1)} %bitcast.95), channel_id=1, source_target_pairs={{0,1},{1,0},{2,3},{3,2},{4,5},{5,4},{6,7},{7,6},{8,9},{9,8},{10,11... | collective-permute-start | bytes 1179656 | tf_op jit(solution)/shard_map/ppermute | solution.py:98
  10.1 1.8 %dynamic-slice_bitcast_fusion.2 = (bf16[1,192,512]{2,1,0:T(8,128)(2,1)}, bf16[1,192,512]{2,1,0:T(8,128)(2,1)}) fusion(bf16[1024,192]{0,1:T(8,128)(2,1)} %param.16, s32[]{:T(128)S(6)} %select_n.236, s32[]{:T(128)S(6)} %select_n.238), kind=kLoop, calls=%fused_computation.61 | loop fusion | bytes 786440 | tf_op jit(solution)/shard_map/dynamic_slice | solution.py:161
  13.0 0.7 fusion.30
  13.8 12.3 %collective-permute-done = bf16[512,384]{1,0:T(8,128)(2,1)} collective-permute-done((bf16[512,384]{1,0:T(8,128)(2,1)}, bf16[512,384]{1,0:T(8,128)(2,1)}, u32[]{:S(2)}, u32[]{:S(2)}) %collective-permute-start) | collective-permute-done | bytes 393248 | tf_op jit(solution)/shard_map/ppermute | solution.py:98
  27.7 1.1 copy.14
  29.0 0.8 collective-permute-start.10
  29.8 3.1 %collective-permute-start.15 = (bf16[2,192,512]{2,1,0:T(8,128)(2,1)S(1)}, bf16[2,192,512]{2,1,0:T(8,128)(2,1)S(1)}, u32[]{:S(2)}, u32[]{:S(2)}) collective-permute-start(bf16[2,192,512]{2,1,0:T(8,128)(2,1)S(1)} %get-tuple-element.27), channel_id=1, source_target_pairs={{0,3},{1,0},{2,1},{3,2},{4,7},{5,4},{6,5},{7,6},{8,11},{9,8},{10,9... | collective-permute-start | bytes 1179656 | tf_op jit(solution)/shard_map/ppermute | solution.py:101
  32.9 1.5 %collective-permute-start.7 = (bf16[384,768]{1,0:T(8,128)(2,1)S(1)}, bf16[384,768]{1,0:T(8,128)(2,1)S(1)}, u32[]{:S(2)}, u32[]{:S(2)}) collective-permute-start(bf16[384,768]{1,0:T(8,128)(2,1)S(1)} %copy-done.2), channel_id=1, source_target_pairs={{0,16},{8,24},{16,0},{24,8},{1,17},{9,25},{17,1},{25,9},{2,18},{10... | collective-permute-start | bytes 1769480 | tf_op jit(solution)/shard_map/ppermute | solution.py:98
  34.4 1.1 pad_maximum_fusion
  35.5 3.0 %collective-permute-done.2 = bf16[512,384]{1,0:T(8,128)(2,1)} collective-permute-done((bf16[512,384]{1,0:T(8,128)(2,1)}, bf16[512,384]{1,0:T(8,128)(2,1)}, u32[]{:S(2)}, u32[]{:S(2)}) %collective-permute-start.2) | collective-permute-done | bytes 393248 | tf_op jit(solution)/shard_map/ppermute | solution.py:98
  38.5 1.1 pad_maximum_fusion.1
  40.6 2.4 %collective-permute-done.10 = bf16[2,192,512]{2,1,0:T(8,128)(2,1)S(1)} collective-permute-done((bf16[2,192,512]{2,1,0:T(8,128)(2,1)S(1)}, bf16[2,192,512]{2,1,0:T(8,128)(2,1)S(1)}, u32[]{:S(2)}, u32[]{:S(2)}) %collective-permute-start.10) | collective-permute-done | bytes 393248 | tf_op jit(solution)/shard_map/ppermute | solution.py:101
  42.9 4.4 %collective-permute-done.15 = bf16[2,192,512]{2,1,0:T(8,128)(2,1)S(1)} collective-permute-done((bf16[2,192,512]{2,1,0:T(8,128)(2,1)S(1)}, bf16[2,192,512]{2,1,0:T(8,128)(2,1)S(1)}, u32[]{:S(2)}, u32[]{:S(2)}) %collective-permute-start.15) | collective-permute-done | bytes 393248 | tf_op jit(solution)/shard_map/ppermute | solution.py:101
  47.4 0.6 collective-permute-start.17
  48.1 1.0 constant_dynamic-update-slice_fusion.13
  50.2 1.0 fusion.2
  51.2 1.0 fusion.4
  52.2 3.5 %collective-permute-done.11 = bf16[1,192,512]{2,1,0:T(8,128)(2,1)S(1)} collective-permute-done((bf16[1,192,512]{2,1,0:T(8,128)(2,1)}, bf16[1,192,512]{2,1,0:T(8,128)(2,1)S(1)}, u32[]{:S(2)}, u32[]{:S(2)}) %collective-permute-start.11) | collective-permute-done | bytes 196640 | tf_op jit(solution)/shard_map/ppermute | solution.py:101
  55.7 2.5 %collective-permute-start.12 = (bf16[1,192,512]{2,1,0:T(8,128)(2,1)S(1)}, bf16[1,192,512]{2,1,0:T(8,128)(2,1)S(1)}, u32[]{:S(2)}, u32[]{:S(2)}) collective-permute-start(bf16[1,192,512]{2,1,0:T(8,128)(2,1)S(1)} %copy-done.5), channel_id=1, source_target_pairs={{0,1},{1,2},{2,3},{3,0},{4,5},{5,6},{6,7},{7,4},{8,9},{9,10},{10,1... | collective-permute-start | bytes 589832 | tf_op jit(solution)/shard_map/ppermute | solution.py:101
  58.3 1.3 %collective-permute-start.18 = (bf16[1,192,512]{2,1,0:T(8,128)(2,1)S(1)}, bf16[1,192,512]{2,1,0:T(8,128)(2,1)S(1)}, u32[]{:S(2)}, u32[]{:S(2)}) collective-permute-start(bf16[1,192,512]{2,1,0:T(8,128)(2,1)S(1)} %copy-done.5), channel_id=1, source_target_pairs={{0,3},{1,0},{2,1},{3,2},{4,7},{5,4},{6,5},{7,6},{8,11},{9,8},{10,9... | collective-permute-start | bytes 589832 | tf_op jit(solution)/shard_map/ppermute | solution.py:101
  60.4 0.9 bitcast_dynamic-update-slice_fusion.4
  61.4 1.6 %collective-permute-start.16 = (bf16[2,192,512]{2,1,0:T(8,128)(2,1)S(1)}, bf16[2,192,512]{2,1,0:T(8,128)(2,1)S(1)}, u32[]{:S(2)}, u32[]{:S(2)}) collective-permute-start(bf16[2,192,512]{2,1,0:T(8,128)(2,1)S(1)} %collective-permute-done.10), channel_id=1, source_target_pairs={{0,4},{4,0},{1,5},{5,1},{2,6},{6,2},{3,7},{7,3},{8,12},{12,8},{9,1... | collective-permute-start | bytes 1179656 | tf_op jit(solution)/shard_map/ppermute | solution.py:98
  63.0 2.3 %collective-permute-done.12 = bf16[1,192,512]{2,1,0:T(8,128)(2,1)S(1)} collective-permute-done((bf16[1,192,512]{2,1,0:T(8,128)(2,1)S(1)}, bf16[1,192,512]{2,1,0:T(8,128)(2,1)S(1)}, u32[]{:S(2)}, u32[]{:S(2)}) %collective-permute-start.12) | collective-permute-done | bytes 196640 | tf_op jit(solution)/shard_map/ppermute | solution.py:101
  65.3 1.6 %collective-permute-done.18 = bf16[1,192,512]{2,1,0:T(8,128)(2,1)S(1)} collective-permute-done((bf16[1,192,512]{2,1,0:T(8,128)(2,1)S(1)}, bf16[1,192,512]{2,1,0:T(8,128)(2,1)S(1)}, u32[]{:S(2)}, u32[]{:S(2)}) %collective-permute-start.18) | collective-permute-done | bytes 196640 | tf_op jit(solution)/shard_map/ppermute | solution.py:101
  67.8 1.9 %collective-permute-start.21 = (bf16[1,192,512]{2,1,0:T(8,128)(2,1)S(1)}, bf16[1,192,512]{2,1,0:T(8,128)(2,1)S(1)}, u32[]{:S(2)}, u32[]{:S(2)}) collective-permute-start(bf16[1,192,512]{2,1,0:T(8,128)(2,1)S(1)} %collective-permute-done.18), channel_id=1, source_target_pairs={{0,4},{4,0},{1,5},{5,1},{2,6},{6,2},{3,7},{7,3},{8,12},{12,8},{9,1... | collective-permute-start | bytes 589832 | tf_op jit(solution)/shard_map/ppermute | solution.py:98
  69.7 6.3 %collective-permute-done.16 = bf16[2,192,512]{2,1,0:T(8,128)(2,1)S(1)} collective-permute-done((bf16[2,192,512]{2,1,0:T(8,128)(2,1)S(1)}, bf16[2,192,512]{2,1,0:T(8,128)(2,1)S(1)}, u32[]{:S(2)}, u32[]{:S(2)}) %collective-permute-start.16) | collective-permute-done | bytes 393248 | tf_op jit(solution)/shard_map/ppermute | solution.py:98
  76.7 1.8 %fusion.5 = f32[1024,512]{1,0:T(8,128)S(1)} fusion(bf16[1024,1536]{1,0:T(8,128)(2,1)S(1)} %fusion.4, bf16[2,1536,512]{2,1,0:T(8,128)(2,1)S(1)} %constant_dynamic-update-slice_fusion.11), kind=kOutput, calls=%fused_computation.10 | convolution fusion | flops 1610612736 | bytes 6815744 | tf_op jit(solution)/shard_map/dot_general | solution.py:239
  78.5 2.0 %multiply_convert_fusion = bf16[1024,512]{1,0:T(8,128)(2,1)S(1)} fusion(f32[1024,512]{1,0:T(8,128)S(1)} %fusion.5, bf16[1024,1536]{1,0:T(8,128)(2,1)S(1)} %fusion.4, bf16[2,1536,512]{2,1,0:T(8,128)(2,1)S(1)} %constant_dynamic-update-slice_fusion.11), kind=kOutput, calls=%fused_computation.7 | convolution fusion | flops 1613758464 | bytes 7864320 | tf_op jit(solution)/shard_map/dot_general | solution.py:240
  80.6 1.4 %fusion.51 = f32[768,512]{1,0:T(8,128)S(1)} fusion(bf16[1536,768]{1,0:T(8,128)(2,1)S(1)} %constant_dynamic-update-slice_fusion.5, bf16[1536,512]{1,0:T(8,128)(2,1)S(1)} %bitcast_dynamic-update-slice_fusion), kind=kOutput, calls=%fused_computation.129 | convolution fusion | flops 1207959552 | bytes 5505024 | tf_op jit(solution)/shard_map/dot_general | solution.py:245
  84.0 1.6 %fusion.8 = f32[2,2,128,768]{3,2,1,0:T(8,128)S(1)} fusion(bf16[768,512,1,1]{1,0,3,2:T(8,128)(2,1)S(1)} %fusion.6, bf16[2,2,2,128,512]{4,3,2,1,0:T(8,128)(2,1)} %bitcast.98, s32[]{:T(128)S(6)} %select_n.278), kind=kOutput, calls=%fused_computation.24 | convolution fusion | flops 402653184 | bytes 2883588 | tf_op jit(solution)/shard_map/dot_general | solution.py:262
  86.5 1.0 collective-permute-start.23
  87.6 2.6 %collective-permute-start.24 = (bf16[128,768]{1,0:T(8,128)(2,1)S(1)}, bf16[128,768]{1,0:T(8,128)(2,1)S(1)}, u32[]{:S(2)}, u32[]{:S(2)}) collective-permute-start(bf16[128,768]{1,0:T(8,128)(2,1)S(1)} %fusion.25), channel_id=1, source_target_pairs={{0,1},{1,0},{2,3},{3,2},{4,5},{5,4},{6,7},{7,6},{8,9},{9,8},{10,11... | collective-permute-start | bytes 589832 | tf_op jit(solution)/shard_map/ppermute | solution.py:98
  90.2 7.6 %collective-permute-done.23 = bf16[128,768]{1,0:T(8,128)(2,1)S(1)} collective-permute-done((bf16[128,768]{1,0:T(8,128)(2,1)S(1)}, bf16[128,768]{1,0:T(8,128)(2,1)S(1)}, u32[]{:S(2)}, u32[]{:S(2)}) %collective-permute-start.23) | collective-permute-done | bytes 196640 | tf_op jit(solution)/shard_map/ppermute | solution.py:98
  97.7 1.2 collective-permute-done.24
  99.5 1.0 collective-permute-start.26
  101.0 2.1 %collective-permute-start.30 = (bf16[128,768]{1,0:T(8,128)(2,1)S(1)}, bf16[128,768]{1,0:T(8,128)(2,1)S(1)}, u32[]{:S(2)}, u32[]{:S(2)}) collective-permute-start(bf16[128,768]{1,0:T(8,128)(2,1)S(1)} %multiply_convert_fusion.1.refs_0_), channel_id=1, source_target_pairs={{0,20},{4,16},{8,28},{12,24},{16,4},{20,0},{24,12},{28,8},{1,21},{... | collective-permute-start | bytes 589832 | tf_op jit(solution)/shard_map/ppermute | solution.py:98
  103.1 4.3 %collective-permute-done.26.refs_1_ = bf16[128,768]{1,0:T(8,128)(2,1)S(1)} collective-permute-done((bf16[128,768]{1,0:T(8,128)(2,1)S(1)}, bf16[128,768]{1,0:T(8,128)(2,1)S(1)}, u32[]{:S(2)}, u32[]{:S(2)}) %collective-permute-start.26) | collective-permute-done | bytes 196640 | tf_op jit(solution)/shard_map/ppermute | solution.py:98
  107.4 2.9 %collective-permute-done.29.refs_4_ = bf16[128,768]{1,0:T(8,128)(2,1)S(1)} collective-permute-done((bf16[128,768]{1,0:T(8,128)(2,1)S(1)}, bf16[128,768]{1,0:T(8,128)(2,1)S(1)}, u32[]{:S(2)}, u32[]{:S(2)}) %collective-permute-start.29) | collective-permute-done | bytes 196640 | tf_op jit(solution)/shard_map/ppermute | solution.py:98
  110.8 0.9 collective-permute-done.31.refs_6_
  112.1 5.3 %shard_map.118 = (f32[2,192,512]{2,1,0:T(8,128)S(1)}, bf16[2,192,512]{2,1,0:T(8,128)(2,1)S(1)}) custom-call(bf16[128,768]{1,0:T(8,128)(2,1)S(1)} %multiply_convert_fusion.1.refs_0_, bf16[128,768]{1,0:T(8,128)(2,1)S(1)} %collective-permute-done.26.refs_1_, bf16[128,768]{1,0:T(8,128)(2,1)S(1)} %collective-permute-done.27.refs_2_, ...), custom_call_target="tpu_custom_call" | custom-call | flops 2516582400 | bytes 8388608 | tf_op jit(solution)/shard_map/pallas_call | solution.py:300
  117.7 1.5 %collective-permute-done.33 = bf16[2,192,512]{2,1,0:T(8,128)(2,1)S(1)} collective-permute-done((bf16[2,192,512]{2,1,0:T(8,128)(2,1)S(1)}, bf16[2,192,512]{2,1,0:T(8,128)(2,1)S(1)}, u32[]{:S(2)}, u32[]{:S(2)}) %collective-permute-start.33) | collective-permute-done | bytes 393248 | tf_op jit(solution)/shard_map/ppermute | solution.py:98
  119.3 1.1 collective-permute-start.34
  120.5 6.0 %collective-permute-done.34 = bf16[192,512]{1,0:T(8,128)(2,1)S(1)} collective-permute-done((bf16[192,512]{1,0:T(8,128)(2,1)S(1)}, bf16[192,512]{1,0:T(8,128)(2,1)S(1)}, u32[]{:S(2)}, u32[]{:S(2)}) %collective-permute-start.34) | collective-permute-done | bytes 196640 | tf_op jit(solution)/shard_map/ppermute | solution.py:98
  126.5 0.7 fusion.26
  (125 shorter events, 11.8 us)
Async XLA Ops:
  0.0 12.4 %copy-start.10 = (s32[1,3]{1,0:T(1,128)S(1)}, s32[1,3]{1,0:T(1,128)}, u32[]{:S(2)}) copy-start(s32[1,3]{1,0:T(1,128)} %param.21) | copy-start | bytes 40
  0.0 12.6 %copy-start.9 = (s32[4]{0:T(128)S(1)}, s32[4]{0:T(128)}, u32[]{:S(2)}) copy-start(s32[4]{0:T(128)} %param.23) | copy-start | bytes 52
  0.0 12.7 %copy-start.8 = (s32[4]{0:T(128)S(1)}, s32[4]{0:T(128)}, u32[]{:S(2)}) copy-start(s32[4]{0:T(128)} %param.22) | copy-start | bytes 52
  0.0 13.7 %copy-start.6 = (f32[1536]{0:T(1024)S(1)}, f32[1536]{0:T(1024)}, u32[]{:S(2)}) copy-start(f32[1536]{0:T(1024)} %param.13) | copy-start | bytes 18436
  0.0 28.9 %copy-start.2 = (bf16[384,768]{1,0:T(8,128)(2,1)S(1)}, bf16[384,768]{1,0:T(8,128)(2,1)}, u32[]{:S(2)}) copy-start(bf16[384,768]{1,0:T(8,128)(2,1)} %param.17) | copy-start | bytes 1769476
  0.0 34.3 %copy-start.3 = (bf16[1,512,384]{2,1,0:T(8,128)(2,1)S(1)}, bf16[1,512,384]{2,1,0:T(8,128)(2,1)}, u32[]{:S(2)}) copy-start(bf16[1,512,384]{2,1,0:T(8,128)(2,1)} %param.12) | copy-start | bytes 1179652
  1.4 25.7 %collective-permute-start.3 = (bf16[2,192,512]{2,1,0:T(8,128)(2,1)S(1)}, bf16[2,192,512]{2,1,0:T(8,128)(2,1)S(1)}, u32[]{:S(2)}, u32[]{:S(2)}) collective-permute-start(bf16[2,192,512]{2,1,0:T(8,128)(2,1)S(1)} %get-tuple-element.53), channel_id=1, source_target_pairs={{0,2},{1,3},{2,0},{3,1},{4,6},{5,7},{6,4},{7,5},{8,10},{9,11},{10,... | collective-permute-start | bytes 1179656 | tf_op jit(solution)/shard_map/ppermute | solution.py:101
  5.5 23.5 %collective-permute-start.9 = (bf16[2,192,512]{2,1,0:T(8,128)(2,1)S(1)}, bf16[2,192,512]{2,1,0:T(8,128)(2,1)S(1)}, u32[]{:S(2)}, u32[]{:S(2)}) collective-permute-start(bf16[2,192,512]{2,1,0:T(8,128)(2,1)S(1)} %get-tuple-element.53), channel_id=1, source_target_pairs={{0,4},{4,0},{1,5},{5,1},{2,6},{6,2},{3,7},{7,3},{8,12},{12,8},{9,1... | collective-permute-start | bytes 1179656 | tf_op jit(solution)/shard_map/ppermute | solution.py:98
  7.0 22.0 %collective-permute-start.1 = (bf16[512,384]{1,0:T(8,128)(2,1)}, bf16[512,384]{1,0:T(8,128)(2,1)S(1)}, u32[]{:S(2)}, u32[]{:S(2)}) collective-permute-start(bf16[512,384]{1,0:T(8,128)(2,1)} %bitcast.94), channel_id=1, source_target_pairs={{0,16},{8,24},{16,0},{24,8},{1,17},{9,25},{17,1},{25,9},{2,18},{10... | collective-permute-start | bytes 1179656 | tf_op jit(solution)/shard_map/ppermute | solution.py:98
  8.5 17.6 %collective-permute-start = (bf16[512,384]{1,0:T(8,128)(2,1)}, bf16[512,384]{1,0:T(8,128)(2,1)}, u32[]{:S(2)}, u32[]{:S(2)}) collective-permute-start(bf16[512,384]{1,0:T(8,128)(2,1)} %bitcast.95), channel_id=1, source_target_pairs={{0,1},{1,0},{2,3},{3,2},{4,5},{5,4},{6,7},{7,6},{8,9},{9,8},{10,11... | collective-permute-start | bytes 1179656 | tf_op jit(solution)/shard_map/ppermute | solution.py:98
  11.9 17.1 %collective-permute-start.8 = (bf16[1,192,512]{2,1,0:T(8,128)(2,1)}, bf16[1,192,512]{2,1,0:T(8,128)(2,1)}, u32[]{:S(2)}, u32[]{:S(2)}) collective-permute-start(bf16[1,192,512]{2,1,0:T(8,128)(2,1)} %get-tuple-element.28), channel_id=1, source_target_pairs={{0,4},{4,0},{1,5},{5,1},{2,6},{6,2},{3,7},{7,3},{8,12},{12,8},{9,1... | collective-permute-start | bytes 589832 | tf_op jit(solution)/shard_map/ppermute | solution.py:98
  26.1 12.4 %collective-permute-start.2 = (bf16[512,384]{1,0:T(8,128)(2,1)}, bf16[512,384]{1,0:T(8,128)(2,1)}, u32[]{:S(2)}, u32[]{:S(2)}) collective-permute-start(bf16[512,384]{1,0:T(8,128)(2,1)} %collective-permute-done), channel_id=1, source_target_pairs={{0,16},{8,24},{16,0},{24,8},{1,17},{9,25},{17,1},{25,9},{2,18},{10... | collective-permute-start | bytes 1179656 | tf_op jit(solution)/shard_map/ppermute | solution.py:98
  27.2 12.4 %collective-permute-start.4 = (bf16[2,192,512]{2,1,0:T(8,128)(2,1)S(1)}, bf16[2,192,512]{2,1,0:T(8,128)(2,1)}, u32[]{:S(2)}, u32[]{:S(2)}) collective-permute-start(bf16[2,192,512]{2,1,0:T(8,128)(2,1)S(1)} %collective-permute-done.3), channel_id=1, source_target_pairs={{0,4},{4,0},{1,5},{5,1},{2,6},{6,2},{3,7},{7,3},{8,12},{12,8},{9,1... | collective-permute-start | bytes 1179656 | tf_op jit(solution)/shard_map/ppermute | solution.py:98
  29.0 13.9 %collective-permute-start.10 = (bf16[2,192,512]{2,1,0:T(8,128)(2,1)S(1)}, bf16[2,192,512]{2,1,0:T(8,128)(2,1)S(1)}, u32[]{:S(2)}, u32[]{:S(2)}) collective-permute-start(bf16[2,192,512]{2,1,0:T(8,128)(2,1)S(1)} %get-tuple-element.27), channel_id=1, source_target_pairs={{0,1},{1,2},{2,3},{3,0},{4,5},{5,6},{6,7},{7,4},{8,9},{9,10},{10,1... | collective-permute-start | bytes 1179656 | tf_op jit(solution)/shard_map/ppermute | solution.py:101
  29.8 17.6 %collective-permute-start.15 = (bf16[2,192,512]{2,1,0:T(8,128)(2,1)S(1)}, bf16[2,192,512]{2,1,0:T(8,128)(2,1)S(1)}, u32[]{:S(2)}, u32[]{:S(2)}) collective-permute-start(bf16[2,192,512]{2,1,0:T(8,128)(2,1)S(1)} %get-tuple-element.27), channel_id=1, source_target_pairs={{0,3},{1,0},{2,1},{3,2},{4,7},{5,4},{6,5},{7,6},{8,11},{9,8},{10,9... | collective-permute-start | bytes 1179656 | tf_op jit(solution)/shard_map/ppermute | solution.py:101
  32.9 28.5 %collective-permute-start.7 = (bf16[384,768]{1,0:T(8,128)(2,1)S(1)}, bf16[384,768]{1,0:T(8,128)(2,1)S(1)}, u32[]{:S(2)}, u32[]{:S(2)}) collective-permute-start(bf16[384,768]{1,0:T(8,128)(2,1)S(1)} %copy-done.2), channel_id=1, source_target_pairs={{0,16},{8,24},{16,0},{24,8},{1,17},{9,25},{17,1},{25,9},{2,18},{10... | collective-permute-start | bytes 1769480 | tf_op jit(solution)/shard_map/ppermute | solution.py:98
  39.6 9.6 %collective-permute-start.5 = (bf16[1024,384]{1,0:T(8,128)(2,1)S(1)}, bf16[1024,384]{1,0:T(8,128)(2,1)S(1)}, u32[]{:S(2)}, u32[]{:S(2)}) collective-permute-start(bf16[1024,384]{1,0:T(8,128)(2,1)S(1)} %pad_maximum_fusion), channel_id=1, source_target_pairs={{0,8},{8,0},{16,24},{24,16},{1,9},{9,1},{17,25},{25,17},{2,10},{10... | collective-permute-start | bytes 2359304 | tf_op jit(solution)/shard_map/ppermute | solution.py:98
  40.0 9.6 %collective-permute-start.6 = (bf16[1024,384]{1,0:T(8,128)(2,1)S(1)}, bf16[1024,384]{1,0:T(8,128)(2,1)S(1)}, u32[]{:S(2)}, u32[]{:S(2)}) collective-permute-start(bf16[1024,384]{1,0:T(8,128)(2,1)S(1)} %pad_maximum_fusion.1), channel_id=1, source_target_pairs={{0,8},{8,0},{16,24},{24,16},{1,9},{9,1},{17,25},{25,17},{2,10},{10... | collective-permute-start | bytes 2359304 | tf_op jit(solution)/shard_map/ppermute | solution.py:98
  42.9 12.8 %collective-permute-start.11 = (bf16[1,192,512]{2,1,0:T(8,128)(2,1)}, bf16[1,192,512]{2,1,0:T(8,128)(2,1)S(1)}, u32[]{:S(2)}, u32[]{:S(2)}) collective-permute-start(bf16[1,192,512]{2,1,0:T(8,128)(2,1)} %get-tuple-element.28), channel_id=1, source_target_pairs={{0,2},{1,3},{2,0},{3,1},{4,6},{5,7},{6,4},{7,5},{8,10},{9,11},{10,... | collective-permute-start | bytes 589832 | tf_op jit(solution)/shard_map/ppermute | solution.py:101
  47.4 20.4 %collective-permute-start.17 = (bf16[2,192,512]{2,1,0:T(8,128)(2,1)S(1)}, bf16[2,192,512]{2,1,0:T(8,128)(2,1)S(1)}, u32[]{:S(2)}, u32[]{:S(2)}) collective-permute-start(bf16[2,192,512]{2,1,0:T(8,128)(2,1)S(1)} %collective-permute-done.15), channel_id=1, source_target_pairs={{0,4},{4,0},{1,5},{5,1},{2,6},{6,2},{3,7},{7,3},{8,12},{12,8},{9,1... | collective-permute-start | bytes 1179656 | tf_op jit(solution)/shard_map/ppermute | solution.py:98
  51.2 4.6 %copy-start.5 = (bf16[1,192,512]{2,1,0:T(8,128)(2,1)S(1)}, bf16[1,192,512]{2,1,0:T(8,128)(2,1)}, u32[]{:S(2)}) copy-start(bf16[1,192,512]{2,1,0:T(8,128)(2,1)} %get-tuple-element.30) | copy-start | bytes 589828
  55.7 4.6 %copy-start.1 = (bf16[1024,192]{0,1:T(8,128)(2,1)S(1)}, bf16[1024,192]{0,1:T(8,128)(2,1)}, u32[]{:S(2)}) copy-start(bf16[1024,192]{0,1:T(8,128)(2,1)} %param.16) | copy-start | bytes 1179652
  55.7 9.6 %collective-permute-start.12 = (bf16[1,192,512]{2,1,0:T(8,128)(2,1)S(1)}, bf16[1,192,512]{2,1,0:T(8,128)(2,1)S(1)}, u32[]{:S(2)}, u32[]{:S(2)}) collective-permute-start(bf16[1,192,512]{2,1,0:T(8,128)(2,1)S(1)} %copy-done.5), channel_id=1, source_target_pairs={{0,1},{1,2},{2,3},{3,0},{4,5},{5,6},{6,7},{7,4},{8,9},{9,10},{10,1... | collective-permute-start | bytes 589832 | tf_op jit(solution)/shard_map/ppermute | solution.py:101
  58.3 8.7 %collective-permute-start.18 = (bf16[1,192,512]{2,1,0:T(8,128)(2,1)S(1)}, bf16[1,192,512]{2,1,0:T(8,128)(2,1)S(1)}, u32[]{:S(2)}, u32[]{:S(2)}) collective-permute-start(bf16[1,192,512]{2,1,0:T(8,128)(2,1)S(1)} %copy-done.5), channel_id=1, source_target_pairs={{0,3},{1,0},{2,1},{3,2},{4,7},{5,4},{6,5},{7,6},{8,11},{9,8},{10,9... | collective-permute-start | bytes 589832 | tf_op jit(solution)/shard_map/ppermute | solution.py:101
  59.7 7.9 %collective-permute-start.19 = (bf16[1,192,512]{2,1,0:T(8,128)(2,1)S(1)}, bf16[1,192,512]{2,1,0:T(8,128)(2,1)S(1)}, u32[]{:S(2)}, u32[]{:S(2)}) collective-permute-start(bf16[1,192,512]{2,1,0:T(8,128)(2,1)S(1)} %collective-permute-done.11), channel_id=1, source_target_pairs={{0,4},{4,0},{1,5},{5,1},{2,6},{6,2},{3,7},{7,3},{8,12},{12,8},{9,1... | collective-permute-start | bytes 589832 | tf_op jit(solution)/shard_map/ppermute | solution.py:98
  61.4 14.6 %collective-permute-start.16 = (bf16[2,192,512]{2,1,0:T(8,128)(2,1)S(1)}, bf16[2,192,512]{2,1,0:T(8,128)(2,1)S(1)}, u32[]{:S(2)}, u32[]{:S(2)}) collective-permute-start(bf16[2,192,512]{2,1,0:T(8,128)(2,1)S(1)} %collective-permute-done.10), channel_id=1, source_target_pairs={{0,4},{4,0},{1,5},{5,1},{2,6},{6,2},{3,7},{7,3},{8,12},{12,8},{9,1... | collective-permute-start | bytes 1179656 | tf_op jit(solution)/shard_map/ppermute | solution.py:98
  65.3 10.8 %collective-permute-start.13 = (bf16[384,768]{1,0:T(8,128)(2,1)S(1)}, bf16[384,768]{1,0:T(8,128)(2,1)S(1)}, u32[]{:S(2)}, u32[]{:S(2)}) collective-permute-start(bf16[384,768]{1,0:T(8,128)(2,1)S(1)} %copy-done.2), channel_id=1, source_target_pairs={{0,8},{8,0},{16,24},{24,16},{1,9},{9,1},{17,25},{25,17},{2,10},{10... | collective-permute-start | bytes 1769480 | tf_op jit(solution)/shard_map/ppermute | solution.py:98
  67.0 9.2 %collective-permute-start.14 = (bf16[384,768]{1,0:T(8,128)(2,1)S(1)}, bf16[384,768]{1,0:T(8,128)(2,1)S(1)}, u32[]{:S(2)}, u32[]{:S(2)}) collective-permute-start(bf16[384,768]{1,0:T(8,128)(2,1)S(1)} %collective-permute-done.7), channel_id=1, source_target_pairs={{0,8},{8,0},{16,24},{24,16},{1,9},{9,1},{17,25},{25,17},{2,10},{10... | collective-permute-start | bytes 1769480 | tf_op jit(solution)/shard_map/ppermute | solution.py:98
  67.6 14.4 %collective-permute-start.20 = (bf16[1,192,512]{2,1,0:T(8,128)(2,1)S(1)}, bf16[1,192,512]{2,1,0:T(8,128)(2,1)S(1)}, u32[]{:S(2)}, u32[]{:S(2)}) collective-permute-start(bf16[1,192,512]{2,1,0:T(8,128)(2,1)S(1)} %collective-permute-done.12), channel_id=1, source_target_pairs={{0,4},{4,0},{1,5},{5,1},{2,6},{6,2},{3,7},{7,3},{8,12},{12,8},{9,1... | collective-permute-start | bytes 589832 | tf_op jit(solution)/shard_map/ppermute | solution.py:98
  67.8 15.0 %collective-permute-start.21 = (bf16[1,192,512]{2,1,0:T(8,128)(2,1)S(1)}, bf16[1,192,512]{2,1,0:T(8,128)(2,1)S(1)}, u32[]{:S(2)}, u32[]{:S(2)}) collective-permute-start(bf16[1,192,512]{2,1,0:T(8,128)(2,1)S(1)} %collective-permute-done.18), channel_id=1, source_target_pairs={{0,4},{4,0},{1,5},{5,1},{2,6},{6,2},{3,7},{7,3},{8,12},{12,8},{9,1... | collective-permute-start | bytes 589832 | tf_op jit(solution)/shard_map/ppermute | solution.py:98
  80.5 2.7 %copy-start.4 = (bf16[1024,512]{1,0:T(8,128)(2,1)}, bf16[1024,512]{1,0:T(8,128)(2,1)S(1)}, u32[]{:S(2)}) copy-start(bf16[1024,512]{1,0:T(8,128)(2,1)S(1)} %multiply_convert_fusion) | copy-start | bytes 3145732
  83.9 2.4 %collective-permute-start.22 = (bf16[2,2,128,768]{3,2,1,0:T(8,128)(2,1)S(1)}, bf16[2,2,128,768]{3,2,1,0:T(8,128)(2,1)S(1)}, u32[]{:S(2)}, u32[]{:S(2)}) collective-permute-start(bf16[2,2,128,768]{3,2,1,0:T(8,128)(2,1)S(1)} %convolution_convert_fusion), channel_id=1, source_target_pairs={{0,8},{8,0},{16,24},{24,16},{1,9},{9,1},{17,25},{25,17},{2,10},{10... | collective-permute-start | bytes 2359304 | tf_op jit(solution)/shard_map/ppermute | solution.py:98
  86.4 13.0 %copy-start.7 = (f32[768]{0:T(1024)S(1)}, f32[768]{0:T(1024)}, u32[]{:S(2)}) copy-start(f32[768]{0:T(1024)} %param.18) | copy-start | bytes 9220
  86.4 25.6 %copy-start = (bf16[3,768,192]{1,2,0:T(8,128)(2,1)S(1)}, bf16[3,768,192]{1,2,0:T(8,128)(2,1)}, u32[]{:S(2)}) copy-start(bf16[3,768,192]{1,2,0:T(8,128)(2,1)} %param.19) | copy-start | bytes 2654212
  86.5 11.2 %collective-permute-start.23 = (bf16[128,768]{1,0:T(8,128)(2,1)S(1)}, bf16[128,768]{1,0:T(8,128)(2,1)S(1)}, u32[]{:S(2)}, u32[]{:S(2)}) collective-permute-start(bf16[128,768]{1,0:T(8,128)(2,1)S(1)} %get-tuple-element.55), channel_id=1, source_target_pairs={{0,16},{8,24},{16,0},{24,8},{1,17},{9,25},{17,1},{25,9},{2,18},{10... | collective-permute-start | bytes 589832 | tf_op jit(solution)/shard_map/ppermute | solution.py:98
  87.5 10.2 %collective-permute-start.25 = (bf16[128,768]{1,0:T(8,128)(2,1)S(1)}, bf16[128,768]{1,0:T(8,128)(2,1)S(1)}, u32[]{:S(2)}, u32[]{:S(2)}) collective-permute-start(bf16[128,768]{1,0:T(8,128)(2,1)S(1)} %get-tuple-element.56), channel_id=1, source_target_pairs={{0,17},{1,16},{2,19},{3,18},{8,25},{9,24},{10,27},{11,26},{16,1},{... | collective-permute-start | bytes 589832 | tf_op jit(solution)/shard_map/ppermute | solution.py:98
  87.6 11.4 %collective-permute-start.24 = (bf16[128,768]{1,0:T(8,128)(2,1)S(1)}, bf16[128,768]{1,0:T(8,128)(2,1)S(1)}, u32[]{:S(2)}, u32[]{:S(2)}) collective-permute-start(bf16[128,768]{1,0:T(8,128)(2,1)S(1)} %fusion.25), channel_id=1, source_target_pairs={{0,1},{1,0},{2,3},{3,2},{4,5},{5,4},{6,7},{7,6},{8,9},{9,8},{10,11... | collective-permute-start | bytes 589832 | tf_op jit(solution)/shard_map/ppermute | solution.py:98
  99.5 7.9 %collective-permute-start.26 = (bf16[128,768]{1,0:T(8,128)(2,1)S(1)}, bf16[128,768]{1,0:T(8,128)(2,1)S(1)}, u32[]{:S(2)}, u32[]{:S(2)}) collective-permute-start(bf16[128,768]{1,0:T(8,128)(2,1)S(1)} %multiply_convert_fusion.1.refs_0_), channel_id=1, source_target_pairs={{0,16},{8,24},{16,0},{24,8},{1,17},{9,25},{17,1},{25,9},{2,18},{10... | collective-permute-start | bytes 589832 | tf_op jit(solution)/shard_map/ppermute | solution.py:98
  100.5 9.8 %collective-permute-start.29 = (bf16[128,768]{1,0:T(8,128)(2,1)S(1)}, bf16[128,768]{1,0:T(8,128)(2,1)S(1)}, u32[]{:S(2)}, u32[]{:S(2)}) collective-permute-start(bf16[128,768]{1,0:T(8,128)(2,1)S(1)} %multiply_convert_fusion.1.refs_0_), channel_id=1, source_target_pairs={{0,4},{4,0},{1,5},{5,1},{2,6},{6,2},{3,7},{7,3},{8,12},{12,8},{9,1... | collective-permute-start | bytes 589832 | tf_op jit(solution)/shard_map/ppermute | solution.py:98
  101.0 9.4 %collective-permute-start.30 = (bf16[128,768]{1,0:T(8,128)(2,1)S(1)}, bf16[128,768]{1,0:T(8,128)(2,1)S(1)}, u32[]{:S(2)}, u32[]{:S(2)}) collective-permute-start(bf16[128,768]{1,0:T(8,128)(2,1)S(1)} %multiply_convert_fusion.1.refs_0_), channel_id=1, source_target_pairs={{0,20},{4,16},{8,28},{12,24},{16,4},{20,0},{24,12},{28,8},{1,21},{... | collective-permute-start | bytes 589832 | tf_op jit(solution)/shard_map/ppermute | solution.py:98
  103.1 7.8 %collective-permute-start.27 = (bf16[128,768]{1,0:T(8,128)(2,1)S(1)}, bf16[128,768]{1,0:T(8,128)(2,1)S(1)}, u32[]{:S(2)}, u32[]{:S(2)}) collective-permute-start(bf16[128,768]{1,0:T(8,128)(2,1)S(1)} %multiply_convert_fusion.1.refs_0_), channel_id=1, source_target_pairs={{0,8},{8,0},{16,24},{24,16},{1,9},{9,1},{17,25},{25,17},{2,10},{10... | collective-permute-start | bytes 589832 | tf_op jit(solution)/shard_map/ppermute | solution.py:98
  107.4 3.4 %collective-permute-start.28 = (bf16[128,768]{1,0:T(8,128)(2,1)S(1)}, bf16[128,768]{1,0:T(8,128)(2,1)S(1)}, u32[]{:S(2)}, u32[]{:S(2)}) collective-permute-start(bf16[128,768]{1,0:T(8,128)(2,1)S(1)} %collective-permute-done.26.refs_1_), channel_id=1, source_target_pairs={{0,8},{8,0},{16,24},{24,16},{1,9},{9,1},{17,25},{25,17},{2,10},{10... | collective-permute-start | bytes 589832 | tf_op jit(solution)/shard_map/ppermute | solution.py:98
  110.3 1.4 %collective-permute-start.31 = (bf16[128,768]{1,0:T(8,128)(2,1)S(1)}, bf16[128,768]{1,0:T(8,128)(2,1)S(1)}, u32[]{:S(2)}, u32[]{:S(2)}) collective-permute-start(bf16[128,768]{1,0:T(8,128)(2,1)S(1)} %collective-permute-done.29.refs_4_), channel_id=1, source_target_pairs={{0,8},{8,0},{16,24},{24,16},{1,9},{9,1},{17,25},{25,17},{2,10},{10... | collective-permute-start | bytes 589832 | tf_op jit(solution)/shard_map/ppermute | solution.py:98
  110.3 1.7 %collective-permute-start.32 = (bf16[128,768]{1,0:T(8,128)(2,1)S(1)}, bf16[128,768]{1,0:T(8,128)(2,1)S(1)}, u32[]{:S(2)}, u32[]{:S(2)}) collective-permute-start(bf16[128,768]{1,0:T(8,128)(2,1)S(1)} %collective-permute-done.30.refs_5_), channel_id=1, source_target_pairs={{0,8},{8,0},{16,24},{24,16},{1,9},{9,1},{17,25},{25,17},{2,10},{10... | collective-permute-start | bytes 589832 | tf_op jit(solution)/shard_map/ppermute | solution.py:98
  117.4 1.8 %collective-permute-start.33 = (bf16[2,192,512]{2,1,0:T(8,128)(2,1)S(1)}, bf16[2,192,512]{2,1,0:T(8,128)(2,1)S(1)}, u32[]{:S(2)}, u32[]{:S(2)}) collective-permute-start(bf16[2,192,512]{2,1,0:T(8,128)(2,1)S(1)} %get-tuple-element.42), channel_id=1, source_target_pairs={{0,8},{8,0},{16,24},{24,16},{1,9},{9,1},{17,25},{25,17},{2,10},{10... | collective-permute-start | bytes 1179656 | tf_op jit(solution)/shard_map/ppermute | solution.py:98
  119.3 7.1 %collective-permute-start.34 = (bf16[192,512]{1,0:T(8,128)(2,1)S(1)}, bf16[192,512]{1,0:T(8,128)(2,1)S(1)}, u32[]{:S(2)}, u32[]{:S(2)}) collective-permute-start(bf16[192,512]{1,0:T(8,128)(2,1)S(1)} %fusion.27), channel_id=1, source_target_pairs={{0,16},{8,24},{16,0},{24,8},{1,17},{9,25},{17,1},{25,9},{2,18},{10... | collective-permute-start | bytes 589832 | tf_op jit(solution)/shard_map/ppermute | solution.py:98

commit v20 on v19

--- a/solution.py
+++ b/solution.py
@@ -211,7 +211,7 @@
             far = rotate(after(down_same, g[0, 1]), 2)
             rows = jnp.concatenate([both, both_c, across, across_c], axis=1)
             normed = layer_norm(rows.astype(jnp.float32), gain).astype(jnp.bfloat16)
-            g[1, 1] = after(flip(after(g[0, 1], both_c), seq=1), normed)
+            g[1, 1] = after(flip(g[0, 1], seq=1), normed)
             d[0, 2] = after(far, normed)
             for k in (1, 3):
                 d[0, k] = rotate(after(down_other, d[0, 2], code, out_w), k)

time: 128 us -> 126 us (0.984)
  waiting for transfers between devices: 62.3 us -> 59.6 us
    ppermute x29, waiting for transfers between devices: 48 us -> 46 us  [flip(): return lax.ppermute(x, names if len(names) > 1 else names[0], pairs)]
where the time goes in v20:
time: 126 us; the launch traced here: 125 us
  waiting for transfers between devices  59.6 us (47%)
  starting transfers between devices  35.2 us (28%)
  matrix products  8.79 us (7%)
  other arithmetic  8.77 us (7%)
  local copies, waits for them, and re-layouts  6.58 us (5%)
  Pallas kernels  5.34 us (4%)
    ppermute x29, waiting for transfers between devices, flip(): return lax.ppermute(x, names if len(names) > 1 else names[0], pairs)  46 us
    ppermute x29, starting transfers between devices, flip(): return lax.ppermute(x, names if len(names) > 1 else names[0], pairs)  23.3 us
    ppermute x6, waiting for transfers between devices, rotate(): return lax.ppermute(x, 'dp', [(i, (i + k) % n_dp) for i in range(n_dp)])  13.6 us
    ppermute x6, starting transfers between devices, rotate(): return lax.ppermute(x, 'dp', [(i, (i + k) % n_dp) for i in range(n_dp)])  11.8 us
    pallas_call x1, Pallas kernels, per_device(): pl.pallas_call(lambda *refs: attend_kernel(*refs, heads=local_heads, mask...  5.34 us
  transfers between devices with their start and end apart: 35, of which 19 were waited for; matrix products, arithmetic and copies ran while one was open for 16% of the time, Pallas kernels for 0%

profile of v20, /device:TPU:0, one launch (start us, length us, event | category | flops | bytes accessed | tf_op | source)
XLA Modules:
  0.0 125.4 jit_solution(4527735556106331081)
XLA Ops:
  0.0 1.4 %fusion.13 = (bf16[2,192,512]{2,1,0:T(8,128)(2,1)S(1)}, bf16[2,192,512]{2,1,0:T(8,128)(2,1)S(1)}) fusion(s32[]{:T(128)S(6)} %select_n.236, bf16[1,192,1024]{2,1,0:T(8,128)(2,1)} %bitcast.92, bf16[1,192,1024]{2,1,0:T(8,128)(2,1)} %bitcast.93, s32[]{:T(128)S(6)} %select_n.238), kind=kLoop, calls=%fused_computation.29 | loop fusion | flops 1572864 | bytes 1572872 | tf_op jit(solution)/shard_map/stack | solution.py:163
  1.4 4.1 %collective-permute-start.3 = (bf16[2,192,512]{2,1,0:T(8,128)(2,1)S(1)}, bf16[2,192,512]{2,1,0:T(8,128)(2,1)S(1)}, u32[]{:S(2)}, u32[]{:S(2)}) collective-permute-start(bf16[2,192,512]{2,1,0:T(8,128)(2,1)S(1)} %get-tuple-element.51), channel_id=1, source_target_pairs={{0,2},{1,3},{2,0},{3,1},{4,6},{5,7},{6,4},{7,5},{8,10},{9,11},{10,... | collective-permute-start | bytes 1179656 | tf_op jit(solution)/shard_map/ppermute | solution.py:101
  5.5 1.5 %collective-permute-start.9 = (bf16[2,192,512]{2,1,0:T(8,128)(2,1)S(1)}, bf16[2,192,512]{2,1,0:T(8,128)(2,1)S(1)}, u32[]{:S(2)}, u32[]{:S(2)}) collective-permute-start(bf16[2,192,512]{2,1,0:T(8,128)(2,1)S(1)} %get-tuple-element.51), channel_id=1, source_target_pairs={{0,4},{4,0},{1,5},{5,1},{2,6},{6,2},{3,7},{7,3},{8,12},{12,8},{9,1... | collective-permute-start | bytes 1179656 | tf_op jit(solution)/shard_map/ppermute | solution.py:98
  7.0 1.5 %collective-permute-start.1 = (bf16[512,384]{1,0:T(8,128)(2,1)}, bf16[512,384]{1,0:T(8,128)(2,1)S(1)}, u32[]{:S(2)}, u32[]{:S(2)}) collective-permute-start(bf16[512,384]{1,0:T(8,128)(2,1)} %bitcast.94), channel_id=1, source_target_pairs={{0,16},{8,24},{16,0},{24,8},{1,17},{9,25},{17,1},{25,9},{2,18},{10... | collective-permute-start | bytes 1179656 | tf_op jit(solution)/shard_map/ppermute | solution.py:98
  8.5 1.6 %collective-permute-start = (bf16[512,384]{1,0:T(8,128)(2,1)}, bf16[512,384]{1,0:T(8,128)(2,1)}, u32[]{:S(2)}, u32[]{:S(2)}) collective-permute-start(bf16[512,384]{1,0:T(8,128)(2,1)} %bitcast.95), channel_id=1, source_target_pairs={{0,1},{1,0},{2,3},{3,2},{4,5},{5,4},{6,7},{7,6},{8,9},{9,8},{10,11... | collective-permute-start | bytes 1179656 | tf_op jit(solution)/shard_map/ppermute | solution.py:98
  10.1 1.8 %dynamic-slice_bitcast_fusion.2 = (bf16[1,192,512]{2,1,0:T(8,128)(2,1)}, bf16[1,192,512]{2,1,0:T(8,128)(2,1)}) fusion(bf16[1024,192]{0,1:T(8,128)(2,1)} %param.16, s32[]{:T(128)S(6)} %select_n.236, s32[]{:T(128)S(6)} %select_n.238), kind=kLoop, calls=%fused_computation.61 | loop fusion | bytes 786440 | tf_op jit(solution)/shard_map/dynamic_slice | solution.py:161
  13.0 0.7 fusion.30
  13.8 12.3 %collective-permute-done = bf16[512,384]{1,0:T(8,128)(2,1)} collective-permute-done((bf16[512,384]{1,0:T(8,128)(2,1)}, bf16[512,384]{1,0:T(8,128)(2,1)}, u32[]{:S(2)}, u32[]{:S(2)}) %collective-permute-start) | collective-permute-done | bytes 393248 | tf_op jit(solution)/shard_map/ppermute | solution.py:98
  27.7 1.1 copy.14
  29.0 0.8 collective-permute-start.10
  29.8 3.1 %collective-permute-start.15 = (bf16[2,192,512]{2,1,0:T(8,128)(2,1)S(1)}, bf16[2,192,512]{2,1,0:T(8,128)(2,1)S(1)}, u32[]{:S(2)}, u32[]{:S(2)}) collective-permute-start(bf16[2,192,512]{2,1,0:T(8,128)(2,1)S(1)} %get-tuple-element.26), channel_id=1, source_target_pairs={{0,3},{1,0},{2,1},{3,2},{4,7},{5,4},{6,5},{7,6},{8,11},{9,8},{10,9... | collective-permute-start | bytes 1179656 | tf_op jit(solution)/shard_map/ppermute | solution.py:101
  32.9 1.5 %collective-permute-start.7 = (bf16[384,768]{1,0:T(8,128)(2,1)S(1)}, bf16[384,768]{1,0:T(8,128)(2,1)S(1)}, u32[]{:S(2)}, u32[]{:S(2)}) collective-permute-start(bf16[384,768]{1,0:T(8,128)(2,1)S(1)} %copy-done.2), channel_id=1, source_target_pairs={{0,16},{8,24},{16,0},{24,8},{1,17},{9,25},{17,1},{25,9},{2,18},{10... | collective-permute-start | bytes 1769480 | tf_op jit(solution)/shard_map/ppermute | solution.py:98
  34.4 1.1 pad_maximum_fusion
  35.5 3.0 %collective-permute-done.2 = bf16[512,384]{1,0:T(8,128)(2,1)} collective-permute-done((bf16[512,384]{1,0:T(8,128)(2,1)}, bf16[512,384]{1,0:T(8,128)(2,1)}, u32[]{:S(2)}, u32[]{:S(2)}) %collective-permute-start.2) | collective-permute-done | bytes 393248 | tf_op jit(solution)/shard_map/ppermute | solution.py:98
  38.5 1.1 pad_maximum_fusion.1
  40.6 2.4 %collective-permute-done.10 = bf16[2,192,512]{2,1,0:T(8,128)(2,1)S(1)} collective-permute-done((bf16[2,192,512]{2,1,0:T(8,128)(2,1)S(1)}, bf16[2,192,512]{2,1,0:T(8,128)(2,1)S(1)}, u32[]{:S(2)}, u32[]{:S(2)}) %collective-permute-start.10) | collective-permute-done | bytes 393248 | tf_op jit(solution)/shard_map/ppermute | solution.py:101
  43.0 4.4 %collective-permute-done.15 = bf16[2,192,512]{2,1,0:T(8,128)(2,1)S(1)} collective-permute-done((bf16[2,192,512]{2,1,0:T(8,128)(2,1)S(1)}, bf16[2,192,512]{2,1,0:T(8,128)(2,1)S(1)}, u32[]{:S(2)}, u32[]{:S(2)}) %collective-permute-start.15) | collective-permute-done | bytes 393248 | tf_op jit(solution)/shard_map/ppermute | solution.py:101
  48.0 1.0 constant_dynamic-update-slice_fusion.13
  49.2 1.5 %collective-permute-start.17 = (bf16[2,192,512]{2,1,0:T(8,128)(2,1)S(1)}, bf16[2,192,512]{2,1,0:T(8,128)(2,1)S(1)}, u32[]{:S(2)}, u32[]{:S(2)}) collective-permute-start(bf16[2,192,512]{2,1,0:T(8,128)(2,1)S(1)} %collective-permute-done.15), channel_id=1, source_target_pairs={{0,4},{4,0},{1,5},{5,1},{2,6},{6,2},{3,7},{7,3},{8,12},{12,8},{9,1... | collective-permute-start | bytes 1179656 | tf_op jit(solution)/shard_map/ppermute | solution.py:98
  51.6 1.0 fusion.2
  52.6 1.0 fusion.4
  53.6 2.1 %collective-permute-done.11 = bf16[1,192,512]{2,1,0:T(8,128)(2,1)S(1)} collective-permute-done((bf16[1,192,512]{2,1,0:T(8,128)(2,1)}, bf16[1,192,512]{2,1,0:T(8,128)(2,1)S(1)}, u32[]{:S(2)}, u32[]{:S(2)}) %collective-permute-start.11) | collective-permute-done | bytes 196640 | tf_op jit(solution)/shard_map/ppermute | solution.py:101
  55.7 2.6 %collective-permute-start.12 = (bf16[1,192,512]{2,1,0:T(8,128)(2,1)S(1)}, bf16[1,192,512]{2,1,0:T(8,128)(2,1)S(1)}, u32[]{:S(2)}, u32[]{:S(2)}) collective-permute-start(bf16[1,192,512]{2,1,0:T(8,128)(2,1)S(1)} %copy-done.5), channel_id=1, source_target_pairs={{0,1},{1,2},{2,3},{3,0},{4,5},{5,6},{6,7},{7,4},{8,9},{9,10},{10,1... | collective-permute-start | bytes 589832 | tf_op jit(solution)/shard_map/ppermute | solution.py:101
  58.3 1.2 collective-permute-start.18
  59.7 0.8 collective-permute-start.19
  60.7 0.9 bitcast_dynamic-update-slice_fusion.4
  61.7 3.6 %collective-permute-done.12 = bf16[1,192,512]{2,1,0:T(8,128)(2,1)S(1)} collective-permute-done((bf16[1,192,512]{2,1,0:T(8,128)(2,1)S(1)}, bf16[1,192,512]{2,1,0:T(8,128)(2,1)S(1)}, u32[]{:S(2)}, u32[]{:S(2)}) %collective-permute-start.12) | collective-permute-done | bytes 196640 | tf_op jit(solution)/shard_map/ppermute | solution.py:101
  65.8 1.1 collective-permute-done.18
  67.0 0.8 collective-permute-done.17
  67.8 1.3 %collective-permute-start.21 = (bf16[1,192,512]{2,1,0:T(8,128)(2,1)S(1)}, bf16[1,192,512]{2,1,0:T(8,128)(2,1)S(1)}, u32[]{:S(2)}, u32[]{:S(2)}) collective-permute-start(bf16[1,192,512]{2,1,0:T(8,128)(2,1)S(1)} %collective-permute-done.18), channel_id=1, source_target_pairs={{0,4},{4,0},{1,5},{5,1},{2,6},{6,2},{3,7},{7,3},{8,12},{12,8},{9,1... | collective-permute-start | bytes 589832 | tf_op jit(solution)/shard_map/ppermute | solution.py:98
  69.1 2.9 %collective-permute-done.19 = bf16[1,192,512]{2,1,0:T(8,128)(2,1)S(1)} collective-permute-done((bf16[1,192,512]{2,1,0:T(8,128)(2,1)S(1)}, bf16[1,192,512]{2,1,0:T(8,128)(2,1)S(1)}, u32[]{:S(2)}, u32[]{:S(2)}) %collective-permute-start.19) | collective-permute-done | bytes 196640 | tf_op jit(solution)/shard_map/ppermute | solution.py:98
  72.7 1.8 %fusion.5 = f32[1024,512]{1,0:T(8,128)S(1)} fusion(bf16[1024,1536]{1,0:T(8,128)(2,1)S(1)} %fusion.4, bf16[2,1536,512]{2,1,0:T(8,128)(2,1)S(1)} %constant_dynamic-update-slice_fusion.11), kind=kOutput, calls=%fused_computation.10 | convolution fusion | flops 1610612736 | bytes 6815744 | tf_op jit(solution)/shard_map/dot_general | solution.py:239
  74.4 2.0 %multiply_convert_fusion = bf16[1024,512]{1,0:T(8,128)(2,1)S(1)} fusion(f32[1024,512]{1,0:T(8,128)S(1)} %fusion.5, bf16[1024,1536]{1,0:T(8,128)(2,1)S(1)} %fusion.4, bf16[2,1536,512]{2,1,0:T(8,128)(2,1)S(1)} %constant_dynamic-update-slice_fusion.11), kind=kOutput, calls=%fused_computation.7 | convolution fusion | flops 1613758464 | bytes 7864320 | tf_op jit(solution)/shard_map/dot_general | solution.py:240
  76.5 1.4 %fusion.51 = f32[768,512]{1,0:T(8,128)S(1)} fusion(bf16[1536,768]{1,0:T(8,128)(2,1)S(1)} %constant_dynamic-update-slice_fusion.5, bf16[1536,512]{1,0:T(8,128)(2,1)S(1)} %bitcast_dynamic-update-slice_fusion), kind=kOutput, calls=%fused_computation.129 | convolution fusion | flops 1207959552 | bytes 5505024 | tf_op jit(solution)/shard_map/dot_general | solution.py:245
  78.3 1.1 collective-permute-done.21
  80.6 1.6 %fusion.8 = f32[2,2,128,768]{3,2,1,0:T(8,128)S(1)} fusion(bf16[768,512,1,1]{1,0,3,2:T(8,128)(2,1)S(1)} %fusion.6, bf16[2,2,2,128,512]{4,3,2,1,0:T(8,128)(2,1)} %bitcast.98, s32[]{:T(128)S(6)} %select_n.278), kind=kOutput, calls=%fused_computation.24 | convolution fusion | flops 402653184 | bytes 2883588 | tf_op jit(solution)/shard_map/dot_general | solution.py:262
  83.2 4.9 %collective-permute-start.25 = (bf16[128,768]{1,0:T(8,128)(2,1)S(1)}, bf16[128,768]{1,0:T(8,128)(2,1)S(1)}, u32[]{:S(2)}, u32[]{:S(2)}) collective-permute-start(bf16[128,768]{1,0:T(8,128)(2,1)S(1)} %get-tuple-element.54), channel_id=1, source_target_pairs={{0,17},{1,16},{2,19},{3,18},{8,25},{9,24},{10,27},{11,26},{16,1},{... | collective-permute-start | bytes 589832 | tf_op jit(solution)/shard_map/ppermute | solution.py:98
  88.2 6.1 %collective-permute-done.23 = bf16[128,768]{1,0:T(8,128)(2,1)S(1)} collective-permute-done((bf16[128,768]{1,0:T(8,128)(2,1)S(1)}, bf16[128,768]{1,0:T(8,128)(2,1)S(1)}, u32[]{:S(2)}, u32[]{:S(2)}) %collective-permute-start.23) | collective-permute-done | bytes 196640 | tf_op jit(solution)/shard_map/ppermute | solution.py:98
  94.4 2.2 %collective-permute-done.24 = bf16[128,768]{1,0:T(8,128)(2,1)S(1)} collective-permute-done((bf16[128,768]{1,0:T(8,128)(2,1)S(1)}, bf16[128,768]{1,0:T(8,128)(2,1)S(1)}, u32[]{:S(2)}, u32[]{:S(2)}) %collective-permute-start.24) | collective-permute-done | bytes 196640 | tf_op jit(solution)/shard_map/ppermute | solution.py:98
  97.1 1.4 %collective-permute-start.26 = (bf16[128,768]{1,0:T(8,128)(2,1)S(1)}, bf16[128,768]{1,0:T(8,128)(2,1)S(1)}, u32[]{:S(2)}, u32[]{:S(2)}) collective-permute-start(bf16[128,768]{1,0:T(8,128)(2,1)S(1)} %multiply_convert_fusion.1.refs_0_), channel_id=1, source_target_pairs={{0,16},{8,24},{16,0},{24,8},{1,17},{9,25},{17,1},{25,9},{2,18},{10... | collective-permute-start | bytes 589832 | tf_op jit(solution)/shard_map/ppermute | solution.py:98
  98.8 1.9 %collective-permute-start.30 = (bf16[128,768]{1,0:T(8,128)(2,1)S(1)}, bf16[128,768]{1,0:T(8,128)(2,1)S(1)}, u32[]{:S(2)}, u32[]{:S(2)}) collective-permute-start(bf16[128,768]{1,0:T(8,128)(2,1)S(1)} %multiply_convert_fusion.1.refs_0_), channel_id=1, source_target_pairs={{0,20},{4,16},{8,28},{12,24},{16,4},{20,0},{24,12},{28,8},{1,21},{... | collective-permute-start | bytes 589832 | tf_op jit(solution)/shard_map/ppermute | solution.py:98
  100.7 4.3 %collective-permute-done.26.refs_1_ = bf16[128,768]{1,0:T(8,128)(2,1)S(1)} collective-permute-done((bf16[128,768]{1,0:T(8,128)(2,1)S(1)}, bf16[128,768]{1,0:T(8,128)(2,1)S(1)}, u32[]{:S(2)}, u32[]{:S(2)}) %collective-permute-start.26) | collective-permute-done | bytes 196640 | tf_op jit(solution)/shard_map/ppermute | solution.py:98
  105.1 3.5 %collective-permute-done.29.refs_4_ = bf16[128,768]{1,0:T(8,128)(2,1)S(1)} collective-permute-done((bf16[128,768]{1,0:T(8,128)(2,1)S(1)}, bf16[128,768]{1,0:T(8,128)(2,1)S(1)}, u32[]{:S(2)}, u32[]{:S(2)}) %collective-permute-start.29) | collective-permute-done | bytes 196640 | tf_op jit(solution)/shard_map/ppermute | solution.py:98
  109.1 0.9 collective-permute-done.31.refs_6_
  110.3 5.3 %shard_map.118 = (f32[2,192,512]{2,1,0:T(8,128)S(1)}, bf16[2,192,512]{2,1,0:T(8,128)(2,1)S(1)}) custom-call(bf16[128,768]{1,0:T(8,128)(2,1)S(1)} %multiply_convert_fusion.1.refs_0_, bf16[128,768]{1,0:T(8,128)(2,1)S(1)} %collective-permute-done.26.refs_1_, bf16[128,768]{1,0:T(8,128)(2,1)S(1)} %collective-permute-done.27.refs_2_, ...), custom_call_target="tpu_custom_call" | custom-call | flops 2516582400 | bytes 8388608 | tf_op jit(solution)/shard_map/pallas_call | solution.py:300
  115.9 1.5 %collective-permute-done.33 = bf16[2,192,512]{2,1,0:T(8,128)(2,1)S(1)} collective-permute-done((bf16[2,192,512]{2,1,0:T(8,128)(2,1)S(1)}, bf16[2,192,512]{2,1,0:T(8,128)(2,1)S(1)}, u32[]{:S(2)}, u32[]{:S(2)}) %collective-permute-start.33) | collective-permute-done | bytes 393248 | tf_op jit(solution)/shard_map/ppermute | solution.py:98
  118.2 6.4 %collective-permute-done.34 = bf16[192,512]{1,0:T(8,128)(2,1)S(1)} collective-permute-done((bf16[192,512]{1,0:T(8,128)(2,1)S(1)}, bf16[192,512]{1,0:T(8,128)(2,1)S(1)}, u32[]{:S(2)}, u32[]{:S(2)}) %collective-permute-start.34) | collective-permute-done | bytes 196640 | tf_op jit(solution)/shard_map/ppermute | solution.py:98
  124.7 0.7 fusion.26
  (125 shorter events, 11.8 us)
Async XLA Ops:
  0.0 12.4 %copy-start.10 = (s32[1,3]{1,0:T(1,128)S(1)}, s32[1,3]{1,0:T(1,128)}, u32[]{:S(2)}) copy-start(s32[1,3]{1,0:T(1,128)} %param.21) | copy-start | bytes 40
  0.0 12.6 %copy-start.9 = (s32[4]{0:T(128)S(1)}, s32[4]{0:T(128)}, u32[]{:S(2)}) copy-start(s32[4]{0:T(128)} %param.23) | copy-start | bytes 52
  0.0 12.7 %copy-start.8 = (s32[4]{0:T(128)S(1)}, s32[4]{0:T(128)}, u32[]{:S(2)}) copy-start(s32[4]{0:T(128)} %param.22) | copy-start | bytes 52
  0.0 13.7 %copy-start.6 = (f32[1536]{0:T(1024)S(1)}, f32[1536]{0:T(1024)}, u32[]{:S(2)}) copy-start(f32[1536]{0:T(1024)} %param.13) | copy-start | bytes 18436
  0.0 28.9 %copy-start.2 = (bf16[384,768]{1,0:T(8,128)(2,1)S(1)}, bf16[384,768]{1,0:T(8,128)(2,1)}, u32[]{:S(2)}) copy-start(bf16[384,768]{1,0:T(8,128)(2,1)} %param.17) | copy-start | bytes 1769476
  0.0 34.3 %copy-start.3 = (bf16[1,512,384]{2,1,0:T(8,128)(2,1)S(1)}, bf16[1,512,384]{2,1,0:T(8,128)(2,1)}, u32[]{:S(2)}) copy-start(bf16[1,512,384]{2,1,0:T(8,128)(2,1)} %param.12) | copy-start | bytes 1179652
  1.4 25.7 %collective-permute-start.3 = (bf16[2,192,512]{2,1,0:T(8,128)(2,1)S(1)}, bf16[2,192,512]{2,1,0:T(8,128)(2,1)S(1)}, u32[]{:S(2)}, u32[]{:S(2)}) collective-permute-start(bf16[2,192,512]{2,1,0:T(8,128)(2,1)S(1)} %get-tuple-element.51), channel_id=1, source_target_pairs={{0,2},{1,3},{2,0},{3,1},{4,6},{5,7},{6,4},{7,5},{8,10},{9,11},{10,... | collective-permute-start | bytes 1179656 | tf_op jit(solution)/shard_map/ppermute | solution.py:101
  5.5 23.5 %collective-permute-start.9 = (bf16[2,192,512]{2,1,0:T(8,128)(2,1)S(1)}, bf16[2,192,512]{2,1,0:T(8,128)(2,1)S(1)}, u32[]{:S(2)}, u32[]{:S(2)}) collective-permute-start(bf16[2,192,512]{2,1,0:T(8,128)(2,1)S(1)} %get-tuple-element.51), channel_id=1, source_target_pairs={{0,4},{4,0},{1,5},{5,1},{2,6},{6,2},{3,7},{7,3},{8,12},{12,8},{9,1... | collective-permute-start | bytes 1179656 | tf_op jit(solution)/shard_map/ppermute | solution.py:98
  7.0 22.0 %collective-permute-start.1 = (bf16[512,384]{1,0:T(8,128)(2,1)}, bf16[512,384]{1,0:T(8,128)(2,1)S(1)}, u32[]{:S(2)}, u32[]{:S(2)}) collective-permute-start(bf16[512,384]{1,0:T(8,128)(2,1)} %bitcast.94), channel_id=1, source_target_pairs={{0,16},{8,24},{16,0},{24,8},{1,17},{9,25},{17,1},{25,9},{2,18},{10... | collective-permute-start | bytes 1179656 | tf_op jit(solution)/shard_map/ppermute | solution.py:98
  8.5 17.6 %collective-permute-start = (bf16[512,384]{1,0:T(8,128)(2,1)}, bf16[512,384]{1,0:T(8,128)(2,1)}, u32[]{:S(2)}, u32[]{:S(2)}) collective-permute-start(bf16[512,384]{1,0:T(8,128)(2,1)} %bitcast.95), channel_id=1, source_target_pairs={{0,1},{1,0},{2,3},{3,2},{4,5},{5,4},{6,7},{7,6},{8,9},{9,8},{10,11... | collective-permute-start | bytes 1179656 | tf_op jit(solution)/shard_map/ppermute | solution.py:98
  11.9 17.1 %collective-permute-start.8 = (bf16[1,192,512]{2,1,0:T(8,128)(2,1)}, bf16[1,192,512]{2,1,0:T(8,128)(2,1)}, u32[]{:S(2)}, u32[]{:S(2)}) collective-permute-start(bf16[1,192,512]{2,1,0:T(8,128)(2,1)} %get-tuple-element.27), channel_id=1, source_target_pairs={{0,4},{4,0},{1,5},{5,1},{2,6},{6,2},{3,7},{7,3},{8,12},{12,8},{9,1... | collective-permute-start | bytes 589832 | tf_op jit(solution)/shard_map/ppermute | solution.py:98
  26.1 12.4 %collective-permute-start.2 = (bf16[512,384]{1,0:T(8,128)(2,1)}, bf16[512,384]{1,0:T(8,128)(2,1)}, u32[]{:S(2)}, u32[]{:S(2)}) collective-permute-start(bf16[512,384]{1,0:T(8,128)(2,1)} %collective-permute-done), channel_id=1, source_target_pairs={{0,16},{8,24},{16,0},{24,8},{1,17},{9,25},{17,1},{25,9},{2,18},{10... | collective-permute-start | bytes 1179656 | tf_op jit(solution)/shard_map/ppermute | solution.py:98
  27.2 12.4 %collective-permute-start.4 = (bf16[2,192,512]{2,1,0:T(8,128)(2,1)S(1)}, bf16[2,192,512]{2,1,0:T(8,128)(2,1)}, u32[]{:S(2)}, u32[]{:S(2)}) collective-permute-start(bf16[2,192,512]{2,1,0:T(8,128)(2,1)S(1)} %collective-permute-done.3), channel_id=1, source_target_pairs={{0,4},{4,0},{1,5},{5,1},{2,6},{6,2},{3,7},{7,3},{8,12},{12,8},{9,1... | collective-permute-start | bytes 1179656 | tf_op jit(solution)/shard_map/ppermute | solution.py:98
  29.0 13.9 %collective-permute-start.10 = (bf16[2,192,512]{2,1,0:T(8,128)(2,1)S(1)}, bf16[2,192,512]{2,1,0:T(8,128)(2,1)S(1)}, u32[]{:S(2)}, u32[]{:S(2)}) collective-permute-start(bf16[2,192,512]{2,1,0:T(8,128)(2,1)S(1)} %get-tuple-element.26), channel_id=1, source_target_pairs={{0,1},{1,2},{2,3},{3,0},{4,5},{5,6},{6,7},{7,4},{8,9},{9,10},{10,1... | collective-permute-start | bytes 1179656 | tf_op jit(solution)/shard_map/ppermute | solution.py:101
  29.8 17.6 %collective-permute-start.15 = (bf16[2,192,512]{2,1,0:T(8,128)(2,1)S(1)}, bf16[2,192,512]{2,1,0:T(8,128)(2,1)S(1)}, u32[]{:S(2)}, u32[]{:S(2)}) collective-permute-start(bf16[2,192,512]{2,1,0:T(8,128)(2,1)S(1)} %get-tuple-element.26), channel_id=1, source_target_pairs={{0,3},{1,0},{2,1},{3,2},{4,7},{5,4},{6,5},{7,6},{8,11},{9,8},{10,9... | collective-permute-start | bytes 1179656 | tf_op jit(solution)/shard_map/ppermute | solution.py:101
  32.9 28.8 %collective-permute-start.7 = (bf16[384,768]{1,0:T(8,128)(2,1)S(1)}, bf16[384,768]{1,0:T(8,128)(2,1)S(1)}, u32[]{:S(2)}, u32[]{:S(2)}) collective-permute-start(bf16[384,768]{1,0:T(8,128)(2,1)S(1)} %copy-done.2), channel_id=1, source_target_pairs={{0,16},{8,24},{16,0},{24,8},{1,17},{9,25},{17,1},{25,9},{2,18},{10... | collective-permute-start | bytes 1769480 | tf_op jit(solution)/shard_map/ppermute | solution.py:98
  39.6 9.6 %collective-permute-start.5 = (bf16[1024,384]{1,0:T(8,128)(2,1)S(1)}, bf16[1024,384]{1,0:T(8,128)(2,1)S(1)}, u32[]{:S(2)}, u32[]{:S(2)}) collective-permute-start(bf16[1024,384]{1,0:T(8,128)(2,1)S(1)} %pad_maximum_fusion), channel_id=1, source_target_pairs={{0,8},{8,0},{16,24},{24,16},{1,9},{9,1},{17,25},{25,17},{2,10},{10... | collective-permute-start | bytes 2359304 | tf_op jit(solution)/shard_map/ppermute | solution.py:98
  40.0 11.0 %collective-permute-start.6 = (bf16[1024,384]{1,0:T(8,128)(2,1)S(1)}, bf16[1024,384]{1,0:T(8,128)(2,1)S(1)}, u32[]{:S(2)}, u32[]{:S(2)}) collective-permute-start(bf16[1024,384]{1,0:T(8,128)(2,1)S(1)} %pad_maximum_fusion.1), channel_id=1, source_target_pairs={{0,8},{8,0},{16,24},{24,16},{1,9},{9,1},{17,25},{25,17},{2,10},{10... | collective-permute-start | bytes 2359304 | tf_op jit(solution)/shard_map/ppermute | solution.py:98
  42.9 12.8 %collective-permute-start.11 = (bf16[1,192,512]{2,1,0:T(8,128)(2,1)}, bf16[1,192,512]{2,1,0:T(8,128)(2,1)S(1)}, u32[]{:S(2)}, u32[]{:S(2)}) collective-permute-start(bf16[1,192,512]{2,1,0:T(8,128)(2,1)} %get-tuple-element.27), channel_id=1, source_target_pairs={{0,2},{1,3},{2,0},{3,1},{4,6},{5,7},{6,4},{7,5},{8,10},{9,11},{10,... | collective-permute-start | bytes 589832 | tf_op jit(solution)/shard_map/ppermute | solution.py:101
  47.4 12.3 %collective-permute-start.16 = (bf16[2,192,512]{2,1,0:T(8,128)(2,1)S(1)}, bf16[2,192,512]{2,1,0:T(8,128)(2,1)S(1)}, u32[]{:S(2)}, u32[]{:S(2)}) collective-permute-start(bf16[2,192,512]{2,1,0:T(8,128)(2,1)S(1)} %collective-permute-done.10), channel_id=1, source_target_pairs={{0,4},{4,0},{1,5},{5,1},{2,6},{6,2},{3,7},{7,3},{8,12},{12,8},{9,1... | collective-permute-start | bytes 1179656 | tf_op jit(solution)/shard_map/ppermute | solution.py:98
  49.2 18.6 %collective-permute-start.17 = (bf16[2,192,512]{2,1,0:T(8,128)(2,1)S(1)}, bf16[2,192,512]{2,1,0:T(8,128)(2,1)S(1)}, u32[]{:S(2)}, u32[]{:S(2)}) collective-permute-start(bf16[2,192,512]{2,1,0:T(8,128)(2,1)S(1)} %collective-permute-done.15), channel_id=1, source_target_pairs={{0,4},{4,0},{1,5},{5,1},{2,6},{6,2},{3,7},{7,3},{8,12},{12,8},{9,1... | collective-permute-start | bytes 1179656 | tf_op jit(solution)/shard_map/ppermute | solution.py:98
  52.6 3.1 %copy-start.5 = (bf16[1,192,512]{2,1,0:T(8,128)(2,1)S(1)}, bf16[1,192,512]{2,1,0:T(8,128)(2,1)}, u32[]{:S(2)}) copy-start(bf16[1,192,512]{2,1,0:T(8,128)(2,1)} %get-tuple-element.29) | copy-start | bytes 589828
  55.7 4.9 %copy-start.1 = (bf16[1024,192]{0,1:T(8,128)(2,1)S(1)}, bf16[1024,192]{0,1:T(8,128)(2,1)}, u32[]{:S(2)}) copy-start(bf16[1024,192]{0,1:T(8,128)(2,1)} %param.16) | copy-start | bytes 1179652
  55.7 9.6 %collective-permute-start.12 = (bf16[1,192,512]{2,1,0:T(8,128)(2,1)S(1)}, bf16[1,192,512]{2,1,0:T(8,128)(2,1)S(1)}, u32[]{:S(2)}, u32[]{:S(2)}) collective-permute-start(bf16[1,192,512]{2,1,0:T(8,128)(2,1)S(1)} %copy-done.5), channel_id=1, source_target_pairs={{0,1},{1,2},{2,3},{3,0},{4,5},{5,6},{6,7},{7,4},{8,9},{9,10},{10,1... | collective-permute-start | bytes 589832 | tf_op jit(solution)/shard_map/ppermute | solution.py:101
  58.3 8.6 %collective-permute-start.18 = (bf16[1,192,512]{2,1,0:T(8,128)(2,1)S(1)}, bf16[1,192,512]{2,1,0:T(8,128)(2,1)S(1)}, u32[]{:S(2)}, u32[]{:S(2)}) collective-permute-start(bf16[1,192,512]{2,1,0:T(8,128)(2,1)S(1)} %copy-done.5), channel_id=1, source_target_pairs={{0,3},{1,0},{2,1},{3,2},{4,7},{5,4},{6,5},{7,6},{8,11},{9,8},{10,9... | collective-permute-start | bytes 589832 | tf_op jit(solution)/shard_map/ppermute | solution.py:101
  59.7 12.3 %collective-permute-start.19 = (bf16[1,192,512]{2,1,0:T(8,128)(2,1)S(1)}, bf16[1,192,512]{2,1,0:T(8,128)(2,1)S(1)}, u32[]{:S(2)}, u32[]{:S(2)}) collective-permute-start(bf16[1,192,512]{2,1,0:T(8,128)(2,1)S(1)} %collective-permute-done.11), channel_id=1, source_target_pairs={{0,4},{4,0},{1,5},{5,1},{2,6},{6,2},{3,7},{7,3},{8,12},{12,8},{9,1... | collective-permute-start | bytes 589832 | tf_op jit(solution)/shard_map/ppermute | solution.py:98
  65.3 6.7 %collective-permute-start.13 = (bf16[384,768]{1,0:T(8,128)(2,1)S(1)}, bf16[384,768]{1,0:T(8,128)(2,1)S(1)}, u32[]{:S(2)}, u32[]{:S(2)}) collective-permute-start(bf16[384,768]{1,0:T(8,128)(2,1)S(1)} %copy-done.2), channel_id=1, source_target_pairs={{0,8},{8,0},{16,24},{24,16},{1,9},{9,1},{17,25},{25,17},{2,10},{10... | collective-permute-start | bytes 1769480 | tf_op jit(solution)/shard_map/ppermute | solution.py:98
  65.3 6.8 %collective-permute-start.14 = (bf16[384,768]{1,0:T(8,128)(2,1)S(1)}, bf16[384,768]{1,0:T(8,128)(2,1)S(1)}, u32[]{:S(2)}, u32[]{:S(2)}) collective-permute-start(bf16[384,768]{1,0:T(8,128)(2,1)S(1)} %collective-permute-done.7), channel_id=1, source_target_pairs={{0,8},{8,0},{16,24},{24,16},{1,9},{9,1},{17,25},{25,17},{2,10},{10... | collective-permute-start | bytes 1769480 | tf_op jit(solution)/shard_map/ppermute | solution.py:98
  67.0 11.0 %collective-permute-start.20 = (bf16[1,192,512]{2,1,0:T(8,128)(2,1)S(1)}, bf16[1,192,512]{2,1,0:T(8,128)(2,1)S(1)}, u32[]{:S(2)}, u32[]{:S(2)}) collective-permute-start(bf16[1,192,512]{2,1,0:T(8,128)(2,1)S(1)} %collective-permute-done.12), channel_id=1, source_target_pairs={{0,4},{4,0},{1,5},{5,1},{2,6},{6,2},{3,7},{7,3},{8,12},{12,8},{9,1... | collective-permute-start | bytes 589832 | tf_op jit(solution)/shard_map/ppermute | solution.py:98
  67.8 11.6 %collective-permute-start.21 = (bf16[1,192,512]{2,1,0:T(8,128)(2,1)S(1)}, bf16[1,192,512]{2,1,0:T(8,128)(2,1)S(1)}, u32[]{:S(2)}, u32[]{:S(2)}) collective-permute-start(bf16[1,192,512]{2,1,0:T(8,128)(2,1)S(1)} %collective-permute-done.18), channel_id=1, source_target_pairs={{0,4},{4,0},{1,5},{5,1},{2,6},{6,2},{3,7},{7,3},{8,12},{12,8},{9,1... | collective-permute-start | bytes 589832 | tf_op jit(solution)/shard_map/ppermute | solution.py:98
  76.5 3.4 %copy-start.4 = (bf16[1024,512]{1,0:T(8,128)(2,1)}, bf16[1024,512]{1,0:T(8,128)(2,1)S(1)}, u32[]{:S(2)}) copy-start(bf16[1024,512]{1,0:T(8,128)(2,1)S(1)} %multiply_convert_fusion) | copy-start | bytes 3145732
  80.5 2.4 %collective-permute-start.22 = (bf16[2,2,128,768]{3,2,1,0:T(8,128)(2,1)S(1)}, bf16[2,2,128,768]{3,2,1,0:T(8,128)(2,1)S(1)}, u32[]{:S(2)}, u32[]{:S(2)}) collective-permute-start(bf16[2,2,128,768]{3,2,1,0:T(8,128)(2,1)S(1)} %convolution_convert_fusion), channel_id=1, source_target_pairs={{0,8},{8,0},{16,24},{24,16},{1,9},{9,1},{17,25},{25,17},{2,10},{10... | collective-permute-start | bytes 2359304 | tf_op jit(solution)/shard_map/ppermute | solution.py:98
  83.0 14.0 %copy-start.7 = (f32[768]{0:T(1024)S(1)}, f32[768]{0:T(1024)}, u32[]{:S(2)}) copy-start(f32[768]{0:T(1024)} %param.18) | copy-start | bytes 9220
  83.0 27.3 %copy-start = (bf16[3,768,192]{1,2,0:T(8,128)(2,1)S(1)}, bf16[3,768,192]{1,2,0:T(8,128)(2,1)}, u32[]{:S(2)}) copy-start(bf16[3,768,192]{1,2,0:T(8,128)(2,1)} %param.19) | copy-start | bytes 2654212
  83.1 11.2 %collective-permute-start.23 = (bf16[128,768]{1,0:T(8,128)(2,1)S(1)}, bf16[128,768]{1,0:T(8,128)(2,1)S(1)}, u32[]{:S(2)}, u32[]{:S(2)}) collective-permute-start(bf16[128,768]{1,0:T(8,128)(2,1)S(1)} %get-tuple-element.53), channel_id=1, source_target_pairs={{0,16},{8,24},{16,0},{24,8},{1,17},{9,25},{17,1},{25,9},{2,18},{10... | collective-permute-start | bytes 589832 | tf_op jit(solution)/shard_map/ppermute | solution.py:98
  83.2 11.1 %collective-permute-start.25 = (bf16[128,768]{1,0:T(8,128)(2,1)S(1)}, bf16[128,768]{1,0:T(8,128)(2,1)S(1)}, u32[]{:S(2)}, u32[]{:S(2)}) collective-permute-start(bf16[128,768]{1,0:T(8,128)(2,1)S(1)} %get-tuple-element.54), channel_id=1, source_target_pairs={{0,17},{1,16},{2,19},{3,18},{8,25},{9,24},{10,27},{11,26},{16,1},{... | collective-permute-start | bytes 589832 | tf_op jit(solution)/shard_map/ppermute | solution.py:98
  88.2 8.4 %collective-permute-start.24 = (bf16[128,768]{1,0:T(8,128)(2,1)S(1)}, bf16[128,768]{1,0:T(8,128)(2,1)S(1)}, u32[]{:S(2)}, u32[]{:S(2)}) collective-permute-start(bf16[128,768]{1,0:T(8,128)(2,1)S(1)} %fusion.25), channel_id=1, source_target_pairs={{0,1},{1,0},{2,3},{3,2},{4,5},{5,4},{6,7},{7,6},{8,9},{9,8},{10,11... | collective-permute-start | bytes 589832 | tf_op jit(solution)/shard_map/ppermute | solution.py:98
  97.1 7.9 %collective-permute-start.26 = (bf16[128,768]{1,0:T(8,128)(2,1)S(1)}, bf16[128,768]{1,0:T(8,128)(2,1)S(1)}, u32[]{:S(2)}, u32[]{:S(2)}) collective-permute-start(bf16[128,768]{1,0:T(8,128)(2,1)S(1)} %multiply_convert_fusion.1.refs_0_), channel_id=1, source_target_pairs={{0,16},{8,24},{16,0},{24,8},{1,17},{9,25},{17,1},{25,9},{2,18},{10... | collective-permute-start | bytes 589832 | tf_op jit(solution)/shard_map/ppermute | solution.py:98
  98.5 10.0 %collective-permute-start.29 = (bf16[128,768]{1,0:T(8,128)(2,1)S(1)}, bf16[128,768]{1,0:T(8,128)(2,1)S(1)}, u32[]{:S(2)}, u32[]{:S(2)}) collective-permute-start(bf16[128,768]{1,0:T(8,128)(2,1)S(1)} %multiply_convert_fusion.1.refs_0_), channel_id=1, source_target_pairs={{0,4},{4,0},{1,5},{5,1},{2,6},{6,2},{3,7},{7,3},{8,12},{12,8},{9,1... | collective-permute-start | bytes 589832 | tf_op jit(solution)/shard_map/ppermute | solution.py:98
  98.8 9.8 %collective-permute-start.30 = (bf16[128,768]{1,0:T(8,128)(2,1)S(1)}, bf16[128,768]{1,0:T(8,128)(2,1)S(1)}, u32[]{:S(2)}, u32[]{:S(2)}) collective-permute-start(bf16[128,768]{1,0:T(8,128)(2,1)S(1)} %multiply_convert_fusion.1.refs_0_), channel_id=1, source_target_pairs={{0,20},{4,16},{8,28},{12,24},{16,4},{20,0},{24,12},{28,8},{1,21},{... | collective-permute-start | bytes 589832 | tf_op jit(solution)/shard_map/ppermute | solution.py:98
  100.7 8.4 %collective-permute-start.27 = (bf16[128,768]{1,0:T(8,128)(2,1)S(1)}, bf16[128,768]{1,0:T(8,128)(2,1)S(1)}, u32[]{:S(2)}, u32[]{:S(2)}) collective-permute-start(bf16[128,768]{1,0:T(8,128)(2,1)S(1)} %multiply_convert_fusion.1.refs_0_), channel_id=1, source_target_pairs={{0,8},{8,0},{16,24},{24,16},{1,9},{9,1},{17,25},{25,17},{2,10},{10... | collective-permute-start | bytes 589832 | tf_op jit(solution)/shard_map/ppermute | solution.py:98
  105.1 4.0 %collective-permute-start.28 = (bf16[128,768]{1,0:T(8,128)(2,1)S(1)}, bf16[128,768]{1,0:T(8,128)(2,1)S(1)}, u32[]{:S(2)}, u32[]{:S(2)}) collective-permute-start(bf16[128,768]{1,0:T(8,128)(2,1)S(1)} %collective-permute-done.26.refs_1_), channel_id=1, source_target_pairs={{0,8},{8,0},{16,24},{24,16},{1,9},{9,1},{17,25},{25,17},{2,10},{10... | collective-permute-start | bytes 589832 | tf_op jit(solution)/shard_map/ppermute | solution.py:98
  108.6 1.4 %collective-permute-start.31 = (bf16[128,768]{1,0:T(8,128)(2,1)S(1)}, bf16[128,768]{1,0:T(8,128)(2,1)S(1)}, u32[]{:S(2)}, u32[]{:S(2)}) collective-permute-start(bf16[128,768]{1,0:T(8,128)(2,1)S(1)} %collective-permute-done.29.refs_4_), channel_id=1, source_target_pairs={{0,8},{8,0},{16,24},{24,16},{1,9},{9,1},{17,25},{25,17},{2,10},{10... | collective-permute-start | bytes 589832 | tf_op jit(solution)/shard_map/ppermute | solution.py:98
  108.6 1.7 %collective-permute-start.32 = (bf16[128,768]{1,0:T(8,128)(2,1)S(1)}, bf16[128,768]{1,0:T(8,128)(2,1)S(1)}, u32[]{:S(2)}, u32[]{:S(2)}) collective-permute-start(bf16[128,768]{1,0:T(8,128)(2,1)S(1)} %collective-permute-done.30.refs_5_), channel_id=1, source_target_pairs={{0,8},{8,0},{16,24},{24,16},{1,9},{9,1},{17,25},{25,17},{2,10},{10... | collective-permute-start | bytes 589832 | tf_op jit(solution)/shard_map/ppermute | solution.py:98
  115.6 1.8 %collective-permute-start.33 = (bf16[2,192,512]{2,1,0:T(8,128)(2,1)S(1)}, bf16[2,192,512]{2,1,0:T(8,128)(2,1)S(1)}, u32[]{:S(2)}, u32[]{:S(2)}) collective-permute-start(bf16[2,192,512]{2,1,0:T(8,128)(2,1)S(1)} %get-tuple-element.40), channel_id=1, source_target_pairs={{0,8},{8,0},{16,24},{24,16},{1,9},{9,1},{17,25},{25,17},{2,10},{10... | collective-permute-start | bytes 1179656 | tf_op jit(solution)/shard_map/ppermute | solution.py:98
  117.6 7.1 %collective-permute-start.34 = (bf16[192,512]{1,0:T(8,128)(2,1)S(1)}, bf16[192,512]{1,0:T(8,128)(2,1)S(1)}, u32[]{:S(2)}, u32[]{:S(2)}) collective-permute-start(bf16[192,512]{1,0:T(8,128)(2,1)S(1)} %fusion.27), channel_id=1, source_target_pairs={{0,16},{8,24},{16,0},{24,8},{1,17},{9,25},{17,1},{25,9},{2,18},{10... | collective-permute-start | bytes 589832 | tf_op jit(solution)/shard_map/ppermute | solution.py:98

commit v21 on v20

--- a/solution.py
+++ b/solution.py
@@ -208,7 +208,7 @@
             across = after(jnp.concatenate([mine_x, beside_x], axis=0), g[0, 2], g[1, 2])
             both = after(jnp.concatenate([mine, beside], axis=0), across)
             both_c, across_c = flip(both, section=1), flip(across, section=1)
-            far = rotate(after(down_same, g[0, 1]), 2)
+            far = rotate(after(down_same, g[0, 1], both_c), 2)
             rows = jnp.concatenate([both, both_c, across, across_c], axis=1)
             normed = layer_norm(rows.astype(jnp.float32), gain).astype(jnp.bfloat16)
             g[1, 1] = after(flip(g[0, 1], seq=1), normed)

time: 126 us -> 129 us (1.024)
  waiting for transfers between devices: 59.6 us -> 61.1 us
  starting transfers between devices: 35.2 us -> 36.6 us
    ppermute x6, waiting for transfers between devices: 13.6 us -> 17.6 us  [rotate(): return lax.ppermute(x, 'dp', [(i, (i + k) % n_dp) for i in range(n_dp)])]
    ppermute x29, waiting for transfers between devices: 46 us -> 43.4 us  [flip(): return lax.ppermute(x, names if len(names) > 1 else names[0], pairs)]
    ppermute x6, starting transfers between devices: 11.8 us -> 13.6 us  [rotate(): return lax.ppermute(x, 'dp', [(i, (i + k) % n_dp) for i in range(n_dp)])]
  transfers between devices with their start and end apart: 35 -> 35, of which waited for: 19 -> 17; matrix products, arithmetic and copies ran while one was open for 16% -> 16% of each run, Pallas kernels for 0% -> 0%
where the time goes in v21:
time: 129 us; the launch traced here: 128 us
  waiting for transfers between devices  61.1 us (47%)
  starting transfers between devices  36.6 us (28%)
  other arithmetic  8.77 us (7%)
  matrix products  8.75 us (7%)
  local copies, waits for them, and re-layouts  6.59 us (5%)
  Pallas kernels  5.34 us (4%)
    ppermute x29, waiting for transfers between devices, flip(): return lax.ppermute(x, names if len(names) > 1 else names[0], pairs)  43.4 us
    ppermute x29, starting transfers between devices, flip(): return lax.ppermute(x, names if len(names) > 1 else names[0], pairs)  23 us
    ppermute x6, waiting for transfers between devices, rotate(): return lax.ppermute(x, 'dp', [(i, (i + k) % n_dp) for i in range(n_dp)])  17.6 us
    ppermute x6, starting transfers between devices, rotate(): return lax.ppermute(x, 'dp', [(i, (i + k) % n_dp) for i in range(n_dp)])  13.6 us
    pallas_call x1, Pallas kernels, per_device(): pl.pallas_call(lambda *refs: attend_kernel(*refs, heads=local_heads, mask...  5.34 us
  transfers between devices with their start and end apart: 35, of which 17 were waited for; matrix products, arithmetic and copies ran while one was open for 16% of the time, Pallas kernels for 0%

profile of v21, /device:TPU:0, one launch (start us, length us, event | category | flops | bytes accessed | tf_op | source)
XLA Modules:
  0.0 128.4 jit_solution(5736934474585783727)
XLA Ops:
  0.0 1.4 %fusion.13 = (bf16[2,192,512]{2,1,0:T(8,128)(2,1)S(1)}, bf16[2,192,512]{2,1,0:T(8,128)(2,1)S(1)}) fusion(s32[]{:T(128)S(6)} %select_n.236, bf16[1,192,1024]{2,1,0:T(8,128)(2,1)} %bitcast.92, bf16[1,192,1024]{2,1,0:T(8,128)(2,1)} %bitcast.93, s32[]{:T(128)S(6)} %select_n.238), kind=kLoop, calls=%fused_computation.29 | loop fusion | flops 1572864 | bytes 1572872 | tf_op jit(solution)/shard_map/stack | solution.py:163
  1.4 4.1 %collective-permute-start.3 = (bf16[2,192,512]{2,1,0:T(8,128)(2,1)S(1)}, bf16[2,192,512]{2,1,0:T(8,128)(2,1)S(1)}, u32[]{:S(2)}, u32[]{:S(2)}) collective-permute-start(bf16[2,192,512]{2,1,0:T(8,128)(2,1)S(1)} %get-tuple-element.51), channel_id=1, source_target_pairs={{0,2},{1,3},{2,0},{3,1},{4,6},{5,7},{6,4},{7,5},{8,10},{9,11},{10,... | collective-permute-start | bytes 1179656 | tf_op jit(solution)/shard_map/ppermute | solution.py:101
  5.5 1.5 %collective-permute-start.9 = (bf16[2,192,512]{2,1,0:T(8,128)(2,1)S(1)}, bf16[2,192,512]{2,1,0:T(8,128)(2,1)S(1)}, u32[]{:S(2)}, u32[]{:S(2)}) collective-permute-start(bf16[2,192,512]{2,1,0:T(8,128)(2,1)S(1)} %get-tuple-element.51), channel_id=1, source_target_pairs={{0,4},{4,0},{1,5},{5,1},{2,6},{6,2},{3,7},{7,3},{8,12},{12,8},{9,1... | collective-permute-start | bytes 1179656 | tf_op jit(solution)/shard_map/ppermute | solution.py:98
  7.0 1.5 %collective-permute-start.1 = (bf16[512,384]{1,0:T(8,128)(2,1)}, bf16[512,384]{1,0:T(8,128)(2,1)S(1)}, u32[]{:S(2)}, u32[]{:S(2)}) collective-permute-start(bf16[512,384]{1,0:T(8,128)(2,1)} %bitcast.94), channel_id=1, source_target_pairs={{0,16},{8,24},{16,0},{24,8},{1,17},{9,25},{17,1},{25,9},{2,18},{10... | collective-permute-start | bytes 1179656 | tf_op jit(solution)/shard_map/ppermute | solution.py:98
  8.5 1.6 %collective-permute-start = (bf16[512,384]{1,0:T(8,128)(2,1)}, bf16[512,384]{1,0:T(8,128)(2,1)}, u32[]{:S(2)}, u32[]{:S(2)}) collective-permute-start(bf16[512,384]{1,0:T(8,128)(2,1)} %bitcast.95), channel_id=1, source_target_pairs={{0,1},{1,0},{2,3},{3,2},{4,5},{5,4},{6,7},{7,6},{8,9},{9,8},{10,11... | collective-permute-start | bytes 1179656 | tf_op jit(solution)/shard_map/ppermute | solution.py:98
  10.1 1.8 %dynamic-slice_bitcast_fusion.2 = (bf16[1,192,512]{2,1,0:T(8,128)(2,1)}, bf16[1,192,512]{2,1,0:T(8,128)(2,1)}) fusion(bf16[1024,192]{0,1:T(8,128)(2,1)} %param.16, s32[]{:T(128)S(6)} %select_n.236, s32[]{:T(128)S(6)} %select_n.238), kind=kLoop, calls=%fused_computation.61 | loop fusion | bytes 786440 | tf_op jit(solution)/shard_map/dynamic_slice | solution.py:161
  13.0 0.7 fusion.30
  13.8 12.3 %collective-permute-done = bf16[512,384]{1,0:T(8,128)(2,1)} collective-permute-done((bf16[512,384]{1,0:T(8,128)(2,1)}, bf16[512,384]{1,0:T(8,128)(2,1)}, u32[]{:S(2)}, u32[]{:S(2)}) %collective-permute-start) | collective-permute-done | bytes 393248 | tf_op jit(solution)/shard_map/ppermute | solution.py:98
  27.7 1.1 copy.14
  29.0 0.8 collective-permute-start.10
  29.8 3.1 %collective-permute-start.15 = (bf16[2,192,512]{2,1,0:T(8,128)(2,1)S(1)}, bf16[2,192,512]{2,1,0:T(8,128)(2,1)S(1)}, u32[]{:S(2)}, u32[]{:S(2)}) collective-permute-start(bf16[2,192,512]{2,1,0:T(8,128)(2,1)S(1)} %get-tuple-element.26), channel_id=1, source_target_pairs={{0,3},{1,0},{2,1},{3,2},{4,7},{5,4},{6,5},{7,6},{8,11},{9,8},{10,9... | collective-permute-start | bytes 1179656 | tf_op jit(solution)/shard_map/ppermute | solution.py:101
  32.9 1.5 %collective-permute-start.7 = (bf16[384,768]{1,0:T(8,128)(2,1)S(1)}, bf16[384,768]{1,0:T(8,128)(2,1)S(1)}, u32[]{:S(2)}, u32[]{:S(2)}) collective-permute-start(bf16[384,768]{1,0:T(8,128)(2,1)S(1)} %copy-done.2), channel_id=1, source_target_pairs={{0,16},{8,24},{16,0},{24,8},{1,17},{9,25},{17,1},{25,9},{2,18},{10... | collective-permute-start | bytes 1769480 | tf_op jit(solution)/shard_map/ppermute | solution.py:98
  34.4 1.1 pad_maximum_fusion
  35.5 3.0 %collective-permute-done.2 = bf16[512,384]{1,0:T(8,128)(2,1)} collective-permute-done((bf16[512,384]{1,0:T(8,128)(2,1)}, bf16[512,384]{1,0:T(8,128)(2,1)}, u32[]{:S(2)}, u32[]{:S(2)}) %collective-permute-start.2) | collective-permute-done | bytes 393248 | tf_op jit(solution)/shard_map/ppermute | solution.py:98
  38.5 1.1 pad_maximum_fusion.1
  40.6 2.4 %collective-permute-done.10 = bf16[2,192,512]{2,1,0:T(8,128)(2,1)S(1)} collective-permute-done((bf16[2,192,512]{2,1,0:T(8,128)(2,1)S(1)}, bf16[2,192,512]{2,1,0:T(8,128)(2,1)S(1)}, u32[]{:S(2)}, u32[]{:S(2)}) %collective-permute-start.10) | collective-permute-done | bytes 393248 | tf_op jit(solution)/shard_map/ppermute | solution.py:101
  42.9 1.5 %collective-permute-start.16 = (bf16[2,192,512]{2,1,0:T(8,128)(2,1)S(1)}, bf16[2,192,512]{2,1,0:T(8,128)(2,1)S(1)}, u32[]{:S(2)}, u32[]{:S(2)}) collective-permute-start(bf16[2,192,512]{2,1,0:T(8,128)(2,1)S(1)} %collective-permute-done.10), channel_id=1, source_target_pairs={{0,4},{4,0},{1,5},{5,1},{2,6},{6,2},{3,7},{7,3},{8,12},{12,8},{9,1... | collective-permute-start | bytes 1179656 | tf_op jit(solution)/shard_map/ppermute | solution.py:98
  44.4 2.9 %collective-permute-done.15 = bf16[2,192,512]{2,1,0:T(8,128)(2,1)S(1)} collective-permute-done((bf16[2,192,512]{2,1,0:T(8,128)(2,1)S(1)}, bf16[2,192,512]{2,1,0:T(8,128)(2,1)S(1)}, u32[]{:S(2)}, u32[]{:S(2)}) %collective-permute-start.15) | collective-permute-done | bytes 393248 | tf_op jit(solution)/shard_map/ppermute | solution.py:101
  48.0 1.0 constant_dynamic-update-slice_fusion.13
  50.1 1.0 fusion.2
  51.1 1.8 %collective-permute-start.11 = (bf16[1,192,512]{2,1,0:T(8,128)(2,1)}, bf16[1,192,512]{2,1,0:T(8,128)(2,1)S(1)}, u32[]{:S(2)}, u32[]{:S(2)}) collective-permute-start(bf16[1,192,512]{2,1,0:T(8,128)(2,1)} %get-tuple-element.27), channel_id=1, source_target_pairs={{0,2},{1,3},{2,0},{3,1},{4,6},{5,7},{6,4},{7,5},{8,10},{9,11},{10,... | collective-permute-start | bytes 589832 | tf_op jit(solution)/shard_map/ppermute | solution.py:101
  52.9 1.0 fusion.4
  54.1 8.6 %collective-permute-done.11 = bf16[1,192,512]{2,1,0:T(8,128)(2,1)S(1)} collective-permute-done((bf16[1,192,512]{2,1,0:T(8,128)(2,1)}, bf16[1,192,512]{2,1,0:T(8,128)(2,1)S(1)}, u32[]{:S(2)}, u32[]{:S(2)}) %collective-permute-start.11) | collective-permute-done | bytes 196640 | tf_op jit(solution)/shard_map/ppermute | solution.py:101
  62.7 3.8 %collective-permute-start.18 = (bf16[1,192,512]{2,1,0:T(8,128)(2,1)S(1)}, bf16[1,192,512]{2,1,0:T(8,128)(2,1)S(1)}, u32[]{:S(2)}, u32[]{:S(2)}) collective-permute-start(bf16[1,192,512]{2,1,0:T(8,128)(2,1)S(1)} %copy-done.5), channel_id=1, source_target_pairs={{0,3},{1,0},{2,1},{3,2},{4,7},{5,4},{6,5},{7,6},{8,11},{9,8},{10,9... | collective-permute-start | bytes 589832 | tf_op jit(solution)/shard_map/ppermute | solution.py:101
  66.5 1.7 %collective-permute-start.19 = (bf16[1,192,512]{2,1,0:T(8,128)(2,1)S(1)}, bf16[1,192,512]{2,1,0:T(8,128)(2,1)S(1)}, u32[]{:S(2)}, u32[]{:S(2)}) collective-permute-start(bf16[1,192,512]{2,1,0:T(8,128)(2,1)S(1)} %collective-permute-done.11), channel_id=1, source_target_pairs={{0,4},{4,0},{1,5},{5,1},{2,6},{6,2},{3,7},{7,3},{8,12},{12,8},{9,1... | collective-permute-start | bytes 589832 | tf_op jit(solution)/shard_map/ppermute | solution.py:98
  68.4 0.9 bitcast_dynamic-update-slice_fusion.4
  69.4 2.9 %collective-permute-done.12 = bf16[1,192,512]{2,1,0:T(8,128)(2,1)S(1)} collective-permute-done((bf16[1,192,512]{2,1,0:T(8,128)(2,1)S(1)}, bf16[1,192,512]{2,1,0:T(8,128)(2,1)S(1)}, u32[]{:S(2)}, u32[]{:S(2)}) %collective-permute-start.12) | collective-permute-done | bytes 196640 | tf_op jit(solution)/shard_map/ppermute | solution.py:101
  72.8 0.9 collective-permute-done.18
  73.7 1.7 %collective-permute-start.20 = (bf16[1,192,512]{2,1,0:T(8,128)(2,1)S(1)}, bf16[1,192,512]{2,1,0:T(8,128)(2,1)S(1)}, u32[]{:S(2)}, u32[]{:S(2)}) collective-permute-start(bf16[1,192,512]{2,1,0:T(8,128)(2,1)S(1)} %collective-permute-done.12), channel_id=1, source_target_pairs={{0,4},{4,0},{1,5},{5,1},{2,6},{6,2},{3,7},{7,3},{8,12},{12,8},{9,1... | collective-permute-start | bytes 589832 | tf_op jit(solution)/shard_map/ppermute | solution.py:98
  76.5 1.8 %fusion.5 = f32[1024,512]{1,0:T(8,128)S(1)} fusion(bf16[1024,1536]{1,0:T(8,128)(2,1)S(1)} %fusion.4, bf16[2,1536,512]{2,1,0:T(8,128)(2,1)S(1)} %constant_dynamic-update-slice_fusion.11), kind=kOutput, calls=%fused_computation.10 | convolution fusion | flops 1610612736 | bytes 6815744 | tf_op jit(solution)/shard_map/dot_general | solution.py:239
  78.3 2.0 %multiply_convert_fusion = bf16[1024,512]{1,0:T(8,128)(2,1)S(1)} fusion(f32[1024,512]{1,0:T(8,128)S(1)} %fusion.5, bf16[1024,1536]{1,0:T(8,128)(2,1)S(1)} %fusion.4, bf16[2,1536,512]{2,1,0:T(8,128)(2,1)S(1)} %constant_dynamic-update-slice_fusion.11), kind=kOutput, calls=%fused_computation.7 | convolution fusion | flops 1613758464 | bytes 7864320 | tf_op jit(solution)/shard_map/dot_general | solution.py:240
  80.4 1.4 %fusion.51 = f32[768,512]{1,0:T(8,128)S(1)} fusion(bf16[1536,768]{1,0:T(8,128)(2,1)S(1)} %constant_dynamic-update-slice_fusion.5, bf16[1536,512]{1,0:T(8,128)(2,1)S(1)} %bitcast_dynamic-update-slice_fusion), kind=kOutput, calls=%fused_computation.129 | convolution fusion | flops 1207959552 | bytes 5505024 | tf_op jit(solution)/shard_map/dot_general | solution.py:245
  82.2 1.7 %collective-permute-done.21 = bf16[1,192,512]{2,1,0:T(8,128)(2,1)S(1)} collective-permute-done((bf16[1,192,512]{2,1,0:T(8,128)(2,1)S(1)}, bf16[1,192,512]{2,1,0:T(8,128)(2,1)S(1)}, u32[]{:S(2)}, u32[]{:S(2)}) %collective-permute-start.21) | collective-permute-done | bytes 196640 | tf_op jit(solution)/shard_map/ppermute | solution.py:98
  85.1 1.7 %fusion.8 = f32[2,2,128,768]{3,2,1,0:T(8,128)S(1)} fusion(bf16[768,512,1,1]{1,0,3,2:T(8,128)(2,1)S(1)} %fusion.6, bf16[2,2,2,128,512]{4,3,2,1,0:T(8,128)(2,1)} %bitcast.98, s32[]{:T(128)S(6)} %select_n.278), kind=kOutput, calls=%fused_computation.24 | convolution fusion | flops 402653184 | bytes 2883588 | tf_op jit(solution)/shard_map/dot_general | solution.py:262
  87.7 0.8 collective-permute-start.25
  88.5 2.7 %collective-permute-start.24 = (bf16[128,768]{1,0:T(8,128)(2,1)S(1)}, bf16[128,768]{1,0:T(8,128)(2,1)S(1)}, u32[]{:S(2)}, u32[]{:S(2)}) collective-permute-start(bf16[128,768]{1,0:T(8,128)(2,1)S(1)} %fusion.25), channel_id=1, source_target_pairs={{0,1},{1,0},{2,3},{3,2},{4,5},{5,4},{6,7},{7,6},{8,9},{9,8},{10,11... | collective-permute-start | bytes 589832 | tf_op jit(solution)/shard_map/ppermute | solution.py:98
  91.3 7.6 %collective-permute-done.23 = bf16[128,768]{1,0:T(8,128)(2,1)S(1)} collective-permute-done((bf16[128,768]{1,0:T(8,128)(2,1)S(1)}, bf16[128,768]{1,0:T(8,128)(2,1)S(1)}, u32[]{:S(2)}, u32[]{:S(2)}) %collective-permute-start.23) | collective-permute-done | bytes 196640 | tf_op jit(solution)/shard_map/ppermute | solution.py:98
  98.8 1.2 collective-permute-done.24
  101.0 1.7 %collective-permute-start.29 = (bf16[128,768]{1,0:T(8,128)(2,1)S(1)}, bf16[128,768]{1,0:T(8,128)(2,1)S(1)}, u32[]{:S(2)}, u32[]{:S(2)}) collective-permute-start(bf16[128,768]{1,0:T(8,128)(2,1)S(1)} %multiply_convert_fusion.1.refs_0_), channel_id=1, source_target_pairs={{0,4},{4,0},{1,5},{5,1},{2,6},{6,2},{3,7},{7,3},{8,12},{12,8},{9,1... | collective-permute-start | bytes 589832 | tf_op jit(solution)/shard_map/ppermute | solution.py:98
  102.8 1.4 %collective-permute-start.30 = (bf16[128,768]{1,0:T(8,128)(2,1)S(1)}, bf16[128,768]{1,0:T(8,128)(2,1)S(1)}, u32[]{:S(2)}, u32[]{:S(2)}) collective-permute-start(bf16[128,768]{1,0:T(8,128)(2,1)S(1)} %multiply_convert_fusion.1.refs_0_), channel_id=1, source_target_pairs={{0,20},{4,16},{8,28},{12,24},{16,4},{20,0},{24,12},{28,8},{1,21},{... | collective-permute-start | bytes 589832 | tf_op jit(solution)/shard_map/ppermute | solution.py:98
  104.2 4.3 %collective-permute-done.26.refs_1_ = bf16[128,768]{1,0:T(8,128)(2,1)S(1)} collective-permute-done((bf16[128,768]{1,0:T(8,128)(2,1)S(1)}, bf16[128,768]{1,0:T(8,128)(2,1)S(1)}, u32[]{:S(2)}, u32[]{:S(2)}) %collective-permute-start.26) | collective-permute-done | bytes 196640 | tf_op jit(solution)/shard_map/ppermute | solution.py:98
  108.5 1.8 %collective-permute-done.29.refs_4_ = bf16[128,768]{1,0:T(8,128)(2,1)S(1)} collective-permute-done((bf16[128,768]{1,0:T(8,128)(2,1)S(1)}, bf16[128,768]{1,0:T(8,128)(2,1)S(1)}, u32[]{:S(2)}, u32[]{:S(2)}) %collective-permute-start.29) | collective-permute-done | bytes 196640 | tf_op jit(solution)/shard_map/ppermute | solution.py:98
  110.4 1.5 %collective-permute-done.30.refs_5_ = bf16[128,768]{1,0:T(8,128)(2,1)S(1)} collective-permute-done((bf16[128,768]{1,0:T(8,128)(2,1)S(1)}, bf16[128,768]{1,0:T(8,128)(2,1)S(1)}, u32[]{:S(2)}, u32[]{:S(2)}) %collective-permute-start.30) | collective-permute-done | bytes 196640 | tf_op jit(solution)/shard_map/ppermute | solution.py:98
  111.9 1.4 %collective-permute-done.32.refs_7_ = bf16[128,768]{1,0:T(8,128)(2,1)S(1)} collective-permute-done((bf16[128,768]{1,0:T(8,128)(2,1)S(1)}, bf16[128,768]{1,0:T(8,128)(2,1)S(1)}, u32[]{:S(2)}, u32[]{:S(2)}) %collective-permute-start.32) | collective-permute-done | bytes 196640 | tf_op jit(solution)/shard_map/ppermute | solution.py:98
  113.3 5.3 %shard_map.118 = (f32[2,192,512]{2,1,0:T(8,128)S(1)}, bf16[2,192,512]{2,1,0:T(8,128)(2,1)S(1)}) custom-call(bf16[128,768]{1,0:T(8,128)(2,1)S(1)} %multiply_convert_fusion.1.refs_0_, bf16[128,768]{1,0:T(8,128)(2,1)S(1)} %collective-permute-done.26.refs_1_, bf16[128,768]{1,0:T(8,128)(2,1)S(1)} %collective-permute-done.27.refs_2_, ...), custom_call_target="tpu_custom_call" | custom-call | flops 2516582400 | bytes 8388608 | tf_op jit(solution)/shard_map/pallas_call | solution.py:300
  118.9 1.6 %collective-permute-done.33 = bf16[2,192,512]{2,1,0:T(8,128)(2,1)S(1)} collective-permute-done((bf16[2,192,512]{2,1,0:T(8,128)(2,1)S(1)}, bf16[2,192,512]{2,1,0:T(8,128)(2,1)S(1)}, u32[]{:S(2)}, u32[]{:S(2)}) %collective-permute-start.33) | collective-permute-done | bytes 393248 | tf_op jit(solution)/shard_map/ppermute | solution.py:98
  120.6 0.8 collective-permute-start.34
  121.4 6.2 %collective-permute-done.34 = bf16[192,512]{1,0:T(8,128)(2,1)S(1)} collective-permute-done((bf16[192,512]{1,0:T(8,128)(2,1)S(1)}, bf16[192,512]{1,0:T(8,128)(2,1)S(1)}, u32[]{:S(2)}, u32[]{:S(2)}) %collective-permute-start.34) | collective-permute-done | bytes 196640 | tf_op jit(solution)/shard_map/ppermute | solution.py:98
  (125 shorter events, 11.2 us)
Async XLA Ops:
  0.0 12.4 %copy-start.10 = (s32[1,3]{1,0:T(1,128)S(1)}, s32[1,3]{1,0:T(1,128)}, u32[]{:S(2)}) copy-start(s32[1,3]{1,0:T(1,128)} %param.21) | copy-start | bytes 40
  0.0 12.6 %copy-start.9 = (s32[4]{0:T(128)S(1)}, s32[4]{0:T(128)}, u32[]{:S(2)}) copy-start(s32[4]{0:T(128)} %param.23) | copy-start | bytes 52
  0.0 12.7 %copy-start.8 = (s32[4]{0:T(128)S(1)}, s32[4]{0:T(128)}, u32[]{:S(2)}) copy-start(s32[4]{0:T(128)} %param.22) | copy-start | bytes 52
  0.0 13.7 %copy-start.6 = (f32[1536]{0:T(1024)S(1)}, f32[1536]{0:T(1024)}, u32[]{:S(2)}) copy-start(f32[1536]{0:T(1024)} %param.13) | copy-start | bytes 18436
  0.0 28.9 %copy-start.2 = (bf16[384,768]{1,0:T(8,128)(2,1)S(1)}, bf16[384,768]{1,0:T(8,128)(2,1)}, u32[]{:S(2)}) copy-start(bf16[384,768]{1,0:T(8,128)(2,1)} %param.17) | copy-start | bytes 1769476
  0.0 34.3 %copy-start.3 = (bf16[1,512,384]{2,1,0:T(8,128)(2,1)S(1)}, bf16[1,512,384]{2,1,0:T(8,128)(2,1)}, u32[]{:S(2)}) copy-start(bf16[1,512,384]{2,1,0:T(8,128)(2,1)} %param.12) | copy-start | bytes 1179652
  1.4 25.7 %collective-permute-start.3 = (bf16[2,192,512]{2,1,0:T(8,128)(2,1)S(1)}, bf16[2,192,512]{2,1,0:T(8,128)(2,1)S(1)}, u32[]{:S(2)}, u32[]{:S(2)}) collective-permute-start(bf16[2,192,512]{2,1,0:T(8,128)(2,1)S(1)} %get-tuple-element.51), channel_id=1, source_target_pairs={{0,2},{1,3},{2,0},{3,1},{4,6},{5,7},{6,4},{7,5},{8,10},{9,11},{10,... | collective-permute-start | bytes 1179656 | tf_op jit(solution)/shard_map/ppermute | solution.py:101
  5.5 23.5 %collective-permute-start.9 = (bf16[2,192,512]{2,1,0:T(8,128)(2,1)S(1)}, bf16[2,192,512]{2,1,0:T(8,128)(2,1)S(1)}, u32[]{:S(2)}, u32[]{:S(2)}) collective-permute-start(bf16[2,192,512]{2,1,0:T(8,128)(2,1)S(1)} %get-tuple-element.51), channel_id=1, source_target_pairs={{0,4},{4,0},{1,5},{5,1},{2,6},{6,2},{3,7},{7,3},{8,12},{12,8},{9,1... | collective-permute-start | bytes 1179656 | tf_op jit(solution)/shard_map/ppermute | solution.py:98
  7.0 22.0 %collective-permute-start.1 = (bf16[512,384]{1,0:T(8,128)(2,1)}, bf16[512,384]{1,0:T(8,128)(2,1)S(1)}, u32[]{:S(2)}, u32[]{:S(2)}) collective-permute-start(bf16[512,384]{1,0:T(8,128)(2,1)} %bitcast.94), channel_id=1, source_target_pairs={{0,16},{8,24},{16,0},{24,8},{1,17},{9,25},{17,1},{25,9},{2,18},{10... | collective-permute-start | bytes 1179656 | tf_op jit(solution)/shard_map/ppermute | solution.py:98
  8.5 17.6 %collective-permute-start = (bf16[512,384]{1,0:T(8,128)(2,1)}, bf16[512,384]{1,0:T(8,128)(2,1)}, u32[]{:S(2)}, u32[]{:S(2)}) collective-permute-start(bf16[512,384]{1,0:T(8,128)(2,1)} %bitcast.95), channel_id=1, source_target_pairs={{0,1},{1,0},{2,3},{3,2},{4,5},{5,4},{6,7},{7,6},{8,9},{9,8},{10,11... | collective-permute-start | bytes 1179656 | tf_op jit(solution)/shard_map/ppermute | solution.py:98
  11.9 17.1 %collective-permute-start.8 = (bf16[1,192,512]{2,1,0:T(8,128)(2,1)}, bf16[1,192,512]{2,1,0:T(8,128)(2,1)}, u32[]{:S(2)}, u32[]{:S(2)}) collective-permute-start(bf16[1,192,512]{2,1,0:T(8,128)(2,1)} %get-tuple-element.27), channel_id=1, source_target_pairs={{0,4},{4,0},{1,5},{5,1},{2,6},{6,2},{3,7},{7,3},{8,12},{12,8},{9,1... | collective-permute-start | bytes 589832 | tf_op jit(solution)/shard_map/ppermute | solution.py:98
  26.1 12.4 %collective-permute-start.2 = (bf16[512,384]{1,0:T(8,128)(2,1)}, bf16[512,384]{1,0:T(8,128)(2,1)}, u32[]{:S(2)}, u32[]{:S(2)}) collective-permute-start(bf16[512,384]{1,0:T(8,128)(2,1)} %collective-permute-done), channel_id=1, source_target_pairs={{0,16},{8,24},{16,0},{24,8},{1,17},{9,25},{17,1},{25,9},{2,18},{10... | collective-permute-start | bytes 1179656 | tf_op jit(solution)/shard_map/ppermute | solution.py:98
  27.2 12.4 %collective-permute-start.4 = (bf16[2,192,512]{2,1,0:T(8,128)(2,1)S(1)}, bf16[2,192,512]{2,1,0:T(8,128)(2,1)}, u32[]{:S(2)}, u32[]{:S(2)}) collective-permute-start(bf16[2,192,512]{2,1,0:T(8,128)(2,1)S(1)} %collective-permute-done.3), channel_id=1, source_target_pairs={{0,4},{4,0},{1,5},{5,1},{2,6},{6,2},{3,7},{7,3},{8,12},{12,8},{9,1... | collective-permute-start | bytes 1179656 | tf_op jit(solution)/shard_map/ppermute | solution.py:98
  29.0 13.9 %collective-permute-start.10 = (bf16[2,192,512]{2,1,0:T(8,128)(2,1)S(1)}, bf16[2,192,512]{2,1,0:T(8,128)(2,1)S(1)}, u32[]{:S(2)}, u32[]{:S(2)}) collective-permute-start(bf16[2,192,512]{2,1,0:T(8,128)(2,1)S(1)} %get-tuple-element.26), channel_id=1, source_target_pairs={{0,1},{1,2},{2,3},{3,0},{4,5},{5,6},{6,7},{7,4},{8,9},{9,10},{10,1... | collective-permute-start | bytes 1179656 | tf_op jit(solution)/shard_map/ppermute | solution.py:101
  29.8 17.6 %collective-permute-start.15 = (bf16[2,192,512]{2,1,0:T(8,128)(2,1)S(1)}, bf16[2,192,512]{2,1,0:T(8,128)(2,1)S(1)}, u32[]{:S(2)}, u32[]{:S(2)}) collective-permute-start(bf16[2,192,512]{2,1,0:T(8,128)(2,1)S(1)} %get-tuple-element.26), channel_id=1, source_target_pairs={{0,3},{1,0},{2,1},{3,2},{4,7},{5,4},{6,5},{7,6},{8,11},{9,8},{10,9... | collective-permute-start | bytes 1179656 | tf_op jit(solution)/shard_map/ppermute | solution.py:101
  32.9 36.5 %collective-permute-start.7 = (bf16[384,768]{1,0:T(8,128)(2,1)S(1)}, bf16[384,768]{1,0:T(8,128)(2,1)S(1)}, u32[]{:S(2)}, u32[]{:S(2)}) collective-permute-start(bf16[384,768]{1,0:T(8,128)(2,1)S(1)} %copy-done.2), channel_id=1, source_target_pairs={{0,16},{8,24},{16,0},{24,8},{1,17},{9,25},{17,1},{25,9},{2,18},{10... | collective-permute-start | bytes 1769480 | tf_op jit(solution)/shard_map/ppermute | solution.py:98
  39.6 9.5 %collective-permute-start.5 = (bf16[1024,384]{1,0:T(8,128)(2,1)S(1)}, bf16[1024,384]{1,0:T(8,128)(2,1)S(1)}, u32[]{:S(2)}, u32[]{:S(2)}) collective-permute-start(bf16[1024,384]{1,0:T(8,128)(2,1)S(1)} %pad_maximum_fusion), channel_id=1, source_target_pairs={{0,8},{8,0},{16,24},{24,16},{1,9},{9,1},{17,25},{25,17},{2,10},{10... | collective-permute-start | bytes 2359304 | tf_op jit(solution)/shard_map/ppermute | solution.py:98
  40.0 9.5 %collective-permute-start.6 = (bf16[1024,384]{1,0:T(8,128)(2,1)S(1)}, bf16[1024,384]{1,0:T(8,128)(2,1)S(1)}, u32[]{:S(2)}, u32[]{:S(2)}) collective-permute-start(bf16[1024,384]{1,0:T(8,128)(2,1)S(1)} %pad_maximum_fusion.1), channel_id=1, source_target_pairs={{0,8},{8,0},{16,24},{24,16},{1,9},{9,1},{17,25},{25,17},{2,10},{10... | collective-permute-start | bytes 2359304 | tf_op jit(solution)/shard_map/ppermute | solution.py:98
  42.9 11.0 %collective-permute-start.16 = (bf16[2,192,512]{2,1,0:T(8,128)(2,1)S(1)}, bf16[2,192,512]{2,1,0:T(8,128)(2,1)S(1)}, u32[]{:S(2)}, u32[]{:S(2)}) collective-permute-start(bf16[2,192,512]{2,1,0:T(8,128)(2,1)S(1)} %collective-permute-done.10), channel_id=1, source_target_pairs={{0,4},{4,0},{1,5},{5,1},{2,6},{6,2},{3,7},{7,3},{8,12},{12,8},{9,1... | collective-permute-start | bytes 1179656 | tf_op jit(solution)/shard_map/ppermute | solution.py:98
  47.4 28.1 %collective-permute-start.17 = (bf16[2,192,512]{2,1,0:T(8,128)(2,1)S(1)}, bf16[2,192,512]{2,1,0:T(8,128)(2,1)S(1)}, u32[]{:S(2)}, u32[]{:S(2)}) collective-permute-start(bf16[2,192,512]{2,1,0:T(8,128)(2,1)S(1)} %collective-permute-done.15), channel_id=1, source_target_pairs={{0,4},{4,0},{1,5},{5,1},{2,6},{6,2},{3,7},{7,3},{8,12},{12,8},{9,1... | collective-permute-start | bytes 1179656 | tf_op jit(solution)/shard_map/ppermute | solution.py:98
  51.1 11.6 %collective-permute-start.11 = (bf16[1,192,512]{2,1,0:T(8,128)(2,1)}, bf16[1,192,512]{2,1,0:T(8,128)(2,1)S(1)}, u32[]{:S(2)}, u32[]{:S(2)}) collective-permute-start(bf16[1,192,512]{2,1,0:T(8,128)(2,1)} %get-tuple-element.27), channel_id=1, source_target_pairs={{0,2},{1,3},{2,0},{3,1},{4,6},{5,7},{6,4},{7,5},{8,10},{9,11},{10,... | collective-permute-start | bytes 589832 | tf_op jit(solution)/shard_map/ppermute | solution.py:101
  53.9 8.7 %copy-start.5 = (bf16[1,192,512]{2,1,0:T(8,128)(2,1)S(1)}, bf16[1,192,512]{2,1,0:T(8,128)(2,1)}, u32[]{:S(2)}) copy-start(bf16[1,192,512]{2,1,0:T(8,128)(2,1)} %get-tuple-element.29) | copy-start | bytes 589828
  54.0 14.4 %copy-start.1 = (bf16[1024,192]{0,1:T(8,128)(2,1)S(1)}, bf16[1024,192]{0,1:T(8,128)(2,1)}, u32[]{:S(2)}) copy-start(bf16[1024,192]{0,1:T(8,128)(2,1)} %param.16) | copy-start | bytes 1179652
  62.7 9.6 %collective-permute-start.12 = (bf16[1,192,512]{2,1,0:T(8,128)(2,1)S(1)}, bf16[1,192,512]{2,1,0:T(8,128)(2,1)S(1)}, u32[]{:S(2)}, u32[]{:S(2)}) collective-permute-start(bf16[1,192,512]{2,1,0:T(8,128)(2,1)S(1)} %copy-done.5), channel_id=1, source_target_pairs={{0,1},{1,2},{2,3},{3,0},{4,5},{5,6},{6,7},{7,4},{8,9},{9,10},{10,1... | collective-permute-start | bytes 589832 | tf_op jit(solution)/shard_map/ppermute | solution.py:101
  62.7 11.0 %collective-permute-start.18 = (bf16[1,192,512]{2,1,0:T(8,128)(2,1)S(1)}, bf16[1,192,512]{2,1,0:T(8,128)(2,1)S(1)}, u32[]{:S(2)}, u32[]{:S(2)}) collective-permute-start(bf16[1,192,512]{2,1,0:T(8,128)(2,1)S(1)} %copy-done.5), channel_id=1, source_target_pairs={{0,3},{1,0},{2,1},{3,2},{4,7},{5,4},{6,5},{7,6},{8,11},{9,8},{10,9... | collective-permute-start | bytes 589832 | tf_op jit(solution)/shard_map/ppermute | solution.py:101
  66.5 9.4 %collective-permute-start.19 = (bf16[1,192,512]{2,1,0:T(8,128)(2,1)S(1)}, bf16[1,192,512]{2,1,0:T(8,128)(2,1)S(1)}, u32[]{:S(2)}, u32[]{:S(2)}) collective-permute-start(bf16[1,192,512]{2,1,0:T(8,128)(2,1)S(1)} %collective-permute-done.11), channel_id=1, source_target_pairs={{0,4},{4,0},{1,5},{5,1},{2,6},{6,2},{3,7},{7,3},{8,12},{12,8},{9,1... | collective-permute-start | bytes 589832 | tf_op jit(solution)/shard_map/ppermute | solution.py:98
  72.3 3.6 %collective-permute-start.13 = (bf16[384,768]{1,0:T(8,128)(2,1)S(1)}, bf16[384,768]{1,0:T(8,128)(2,1)S(1)}, u32[]{:S(2)}, u32[]{:S(2)}) collective-permute-start(bf16[384,768]{1,0:T(8,128)(2,1)S(1)} %copy-done.2), channel_id=1, source_target_pairs={{0,8},{8,0},{16,24},{24,16},{1,9},{9,1},{17,25},{25,17},{2,10},{10... | collective-permute-start | bytes 1769480 | tf_op jit(solution)/shard_map/ppermute | solution.py:98
  72.3 3.7 %collective-permute-start.14 = (bf16[384,768]{1,0:T(8,128)(2,1)S(1)}, bf16[384,768]{1,0:T(8,128)(2,1)S(1)}, u32[]{:S(2)}, u32[]{:S(2)}) collective-permute-start(bf16[384,768]{1,0:T(8,128)(2,1)S(1)} %collective-permute-done.7), channel_id=1, source_target_pairs={{0,8},{8,0},{16,24},{24,16},{1,9},{9,1},{17,25},{25,17},{2,10},{10... | collective-permute-start | bytes 1769480 | tf_op jit(solution)/shard_map/ppermute | solution.py:98
  73.7 8.1 %collective-permute-start.20 = (bf16[1,192,512]{2,1,0:T(8,128)(2,1)S(1)}, bf16[1,192,512]{2,1,0:T(8,128)(2,1)S(1)}, u32[]{:S(2)}, u32[]{:S(2)}) collective-permute-start(bf16[1,192,512]{2,1,0:T(8,128)(2,1)S(1)} %collective-permute-done.12), channel_id=1, source_target_pairs={{0,4},{4,0},{1,5},{5,1},{2,6},{6,2},{3,7},{7,3},{8,12},{12,8},{9,1... | collective-permute-start | bytes 589832 | tf_op jit(solution)/shard_map/ppermute | solution.py:98
  75.5 8.4 %collective-permute-start.21 = (bf16[1,192,512]{2,1,0:T(8,128)(2,1)S(1)}, bf16[1,192,512]{2,1,0:T(8,128)(2,1)S(1)}, u32[]{:S(2)}, u32[]{:S(2)}) collective-permute-start(bf16[1,192,512]{2,1,0:T(8,128)(2,1)S(1)} %collective-permute-done.18), channel_id=1, source_target_pairs={{0,4},{4,0},{1,5},{5,1},{2,6},{6,2},{3,7},{7,3},{8,12},{12,8},{9,1... | collective-permute-start | bytes 589832 | tf_op jit(solution)/shard_map/ppermute | solution.py:98
  80.3 4.0 %copy-start.4 = (bf16[1024,512]{1,0:T(8,128)(2,1)}, bf16[1024,512]{1,0:T(8,128)(2,1)S(1)}, u32[]{:S(2)}) copy-start(bf16[1024,512]{1,0:T(8,128)(2,1)S(1)} %multiply_convert_fusion) | copy-start | bytes 3145732
  84.9 2.4 %collective-permute-start.22 = (bf16[2,2,128,768]{3,2,1,0:T(8,128)(2,1)S(1)}, bf16[2,2,128,768]{3,2,1,0:T(8,128)(2,1)S(1)}, u32[]{:S(2)}, u32[]{:S(2)}) collective-permute-start(bf16[2,2,128,768]{3,2,1,0:T(8,128)(2,1)S(1)} %convolution_convert_fusion), channel_id=1, source_target_pairs={{0,8},{8,0},{16,24},{24,16},{1,9},{9,1},{17,25},{25,17},{2,10},{10... | collective-permute-start | bytes 2359304 | tf_op jit(solution)/shard_map/ppermute | solution.py:98
  87.5 13.0 %copy-start.7 = (f32[768]{0:T(1024)S(1)}, f32[768]{0:T(1024)}, u32[]{:S(2)}) copy-start(f32[768]{0:T(1024)} %param.18) | copy-start | bytes 9220
  87.5 25.8 %copy-start = (bf16[3,768,192]{1,2,0:T(8,128)(2,1)S(1)}, bf16[3,768,192]{1,2,0:T(8,128)(2,1)}, u32[]{:S(2)}) copy-start(bf16[3,768,192]{1,2,0:T(8,128)(2,1)} %param.19) | copy-start | bytes 2654212
  87.6 11.2 %collective-permute-start.23 = (bf16[128,768]{1,0:T(8,128)(2,1)S(1)}, bf16[128,768]{1,0:T(8,128)(2,1)S(1)}, u32[]{:S(2)}, u32[]{:S(2)}) collective-permute-start(bf16[128,768]{1,0:T(8,128)(2,1)S(1)} %get-tuple-element.53), channel_id=1, source_target_pairs={{0,16},{8,24},{16,0},{24,8},{1,17},{9,25},{17,1},{25,9},{2,18},{10... | collective-permute-start | bytes 589832 | tf_op jit(solution)/shard_map/ppermute | solution.py:98
  87.7 11.1 %collective-permute-start.25 = (bf16[128,768]{1,0:T(8,128)(2,1)S(1)}, bf16[128,768]{1,0:T(8,128)(2,1)S(1)}, u32[]{:S(2)}, u32[]{:S(2)}) collective-permute-start(bf16[128,768]{1,0:T(8,128)(2,1)S(1)} %get-tuple-element.54), channel_id=1, source_target_pairs={{0,17},{1,16},{2,19},{3,18},{8,25},{9,24},{10,27},{11,26},{16,1},{... | collective-permute-start | bytes 589832 | tf_op jit(solution)/shard_map/ppermute | solution.py:98
  88.5 11.5 %collective-permute-start.24 = (bf16[128,768]{1,0:T(8,128)(2,1)S(1)}, bf16[128,768]{1,0:T(8,128)(2,1)S(1)}, u32[]{:S(2)}, u32[]{:S(2)}) collective-permute-start(bf16[128,768]{1,0:T(8,128)(2,1)S(1)} %fusion.25), channel_id=1, source_target_pairs={{0,1},{1,0},{2,3},{3,2},{4,5},{5,4},{6,7},{7,6},{8,9},{9,8},{10,11... | collective-permute-start | bytes 589832 | tf_op jit(solution)/shard_map/ppermute | solution.py:98
  100.6 7.9 %collective-permute-start.26 = (bf16[128,768]{1,0:T(8,128)(2,1)S(1)}, bf16[128,768]{1,0:T(8,128)(2,1)S(1)}, u32[]{:S(2)}, u32[]{:S(2)}) collective-permute-start(bf16[128,768]{1,0:T(8,128)(2,1)S(1)} %multiply_convert_fusion.1.refs_0_), channel_id=1, source_target_pairs={{0,16},{8,24},{16,0},{24,8},{1,17},{9,25},{17,1},{25,9},{2,18},{10... | collective-permute-start | bytes 589832 | tf_op jit(solution)/shard_map/ppermute | solution.py:98
  101.0 9.3 %collective-permute-start.29 = (bf16[128,768]{1,0:T(8,128)(2,1)S(1)}, bf16[128,768]{1,0:T(8,128)(2,1)S(1)}, u32[]{:S(2)}, u32[]{:S(2)}) collective-permute-start(bf16[128,768]{1,0:T(8,128)(2,1)S(1)} %multiply_convert_fusion.1.refs_0_), channel_id=1, source_target_pairs={{0,4},{4,0},{1,5},{5,1},{2,6},{6,2},{3,7},{7,3},{8,12},{12,8},{9,1... | collective-permute-start | bytes 589832 | tf_op jit(solution)/shard_map/ppermute | solution.py:98
  102.8 9.1 %collective-permute-start.30 = (bf16[128,768]{1,0:T(8,128)(2,1)S(1)}, bf16[128,768]{1,0:T(8,128)(2,1)S(1)}, u32[]{:S(2)}, u32[]{:S(2)}) collective-permute-start(bf16[128,768]{1,0:T(8,128)(2,1)S(1)} %multiply_convert_fusion.1.refs_0_), channel_id=1, source_target_pairs={{0,20},{4,16},{8,28},{12,24},{16,4},{20,0},{24,12},{28,8},{1,21},{... | collective-permute-start | bytes 589832 | tf_op jit(solution)/shard_map/ppermute | solution.py:98
  104.2 7.7 %collective-permute-start.27 = (bf16[128,768]{1,0:T(8,128)(2,1)S(1)}, bf16[128,768]{1,0:T(8,128)(2,1)S(1)}, u32[]{:S(2)}, u32[]{:S(2)}) collective-permute-start(bf16[128,768]{1,0:T(8,128)(2,1)S(1)} %multiply_convert_fusion.1.refs_0_), channel_id=1, source_target_pairs={{0,8},{8,0},{16,24},{24,16},{1,9},{9,1},{17,25},{25,17},{2,10},{10... | collective-permute-start | bytes 589832 | tf_op jit(solution)/shard_map/ppermute | solution.py:98
  108.5 3.4 %collective-permute-start.28 = (bf16[128,768]{1,0:T(8,128)(2,1)S(1)}, bf16[128,768]{1,0:T(8,128)(2,1)S(1)}, u32[]{:S(2)}, u32[]{:S(2)}) collective-permute-start(bf16[128,768]{1,0:T(8,128)(2,1)S(1)} %collective-permute-done.26.refs_1_), channel_id=1, source_target_pairs={{0,8},{8,0},{16,24},{24,16},{1,9},{9,1},{17,25},{25,17},{2,10},{10... | collective-permute-start | bytes 589832 | tf_op jit(solution)/shard_map/ppermute | solution.py:98
  110.4 1.5 %collective-permute-start.31 = (bf16[128,768]{1,0:T(8,128)(2,1)S(1)}, bf16[128,768]{1,0:T(8,128)(2,1)S(1)}, u32[]{:S(2)}, u32[]{:S(2)}) collective-permute-start(bf16[128,768]{1,0:T(8,128)(2,1)S(1)} %collective-permute-done.29.refs_4_), channel_id=1, source_target_pairs={{0,8},{8,0},{16,24},{24,16},{1,9},{9,1},{17,25},{25,17},{2,10},{10... | collective-permute-start | bytes 589832 | tf_op jit(solution)/shard_map/ppermute | solution.py:98
  111.9 1.4 %collective-permute-start.32 = (bf16[128,768]{1,0:T(8,128)(2,1)S(1)}, bf16[128,768]{1,0:T(8,128)(2,1)S(1)}, u32[]{:S(2)}, u32[]{:S(2)}) collective-permute-start(bf16[128,768]{1,0:T(8,128)(2,1)S(1)} %collective-permute-done.30.refs_5_), channel_id=1, source_target_pairs={{0,8},{8,0},{16,24},{24,16},{1,9},{9,1},{17,25},{25,17},{2,10},{10... | collective-permute-start | bytes 589832 | tf_op jit(solution)/shard_map/ppermute | solution.py:98
  118.7 1.8 %collective-permute-start.33 = (bf16[2,192,512]{2,1,0:T(8,128)(2,1)S(1)}, bf16[2,192,512]{2,1,0:T(8,128)(2,1)S(1)}, u32[]{:S(2)}, u32[]{:S(2)}) collective-permute-start(bf16[2,192,512]{2,1,0:T(8,128)(2,1)S(1)} %get-tuple-element.40), channel_id=1, source_target_pairs={{0,8},{8,0},{16,24},{24,16},{1,9},{9,1},{17,25},{25,17},{2,10},{10... | collective-permute-start | bytes 1179656 | tf_op jit(solution)/shard_map/ppermute | solution.py:98
  120.6 7.0 %collective-permute-start.34 = (bf16[192,512]{1,0:T(8,128)(2,1)S(1)}, bf16[192,512]{1,0:T(8,128)(2,1)S(1)}, u32[]{:S(2)}, u32[]{:S(2)}) collective-permute-start(bf16[192,512]{1,0:T(8,128)(2,1)S(1)} %fusion.27), channel_id=1, source_target_pairs={{0,16},{8,24},{16,0},{24,8},{1,17},{9,25},{17,1},{25,9},{2,18},{10... | collective-permute-start | bytes 589832 | tf_op jit(solution)/shard_map/ppermute | solution.py:98

commit v22 on v20

--- a/solution.py
+++ b/solution.py
@@ -205,9 +205,11 @@
             for k in (1, 3):
                 g[0, k] = rotate(after(pair_other, g[0, 2], d[1, 0], g[1, 0], mine_x), k)
             g[1, 2] = flip(g[0, 2], seq=1)
-            across = after(jnp.concatenate([mine_x, beside_x], axis=0), g[0, 2], g[1, 2])
-            both = after(jnp.concatenate([mine, beside], axis=0), across)
-            both_c, across_c = flip(both, section=1), flip(across, section=1)
+            tiles = after(
+                jnp.concatenate([mine, beside, mine_x, beside_x], axis=0), g[0, 2], g[1, 2]
+            )
+            both, across = jnp.split(tiles, 2, axis=0)
+            both_c, across_c = jnp.split(flip(tiles, section=1), 2, axis=0)
             far = rotate(after(down_same, g[0, 1]), 2)
             rows = jnp.concatenate([both, both_c, across, across_c], axis=1)
             normed = layer_norm(rows.astype(jnp.float32), gain).astype(jnp.bfloat16)

time: 126 us -> 134 us (1.063)
  waiting for transfers between devices: 59.6 us -> 66.4 us
  local copies, waits for them, and re-layouts: 6.58 us -> 10.7 us
  starting transfers between devices: 35.2 us -> 33.1 us
    ppermute x6, waiting for transfers between devices: 13.6 us -> 17.8 us  [rotate(): return lax.ppermute(x, 'dp', [(i, (i + k) % n_dp) for i in range(n_dp)])]
    ppermute x29 -> x28, waiting for transfers between devices: 46 us -> 48.6 us  [flip(): return lax.ppermute(x, names if len(names) > 1 else names[0], pairs)]
    dynamic_update_slice x14, local copies, waits for them, and re-layouts: 2.29 us -> 4.47 us  [place_rows(): whole = lax.dynamic_update_slice(whole, block, (0, row_of(y, k, rows), 0))]
    ppermute x29 -> x28, starting transfers between devices: 23.3 us -> 21.3 us  [flip(): return lax.ppermute(x, names if len(names) > 1 else names[0], pairs)]
    split x0 -> x2, local copies, waits for them, and re-layouts: none -> 1.69 us  [the longest x1 1.53 us: per_device(): both_c, across_c = jnp.split(flip(tiles, section=1), 2, axis=0)]
  transfers between devices with their start and end apart: 35 -> 34, of which waited for: 19 -> 17; matrix products, arithmetic and copies ran while one was open for 16% -> 17% of each run, Pallas kernels for 0% -> 0%
where the time goes in v22:
time: 134 us
  waiting for transfers between devices  66.4 us (50%)
  starting transfers between devices  33.1 us (25%)
  local copies, waits for them, and re-layouts  10.7 us (8%)
  matrix products  8.8 us (7%)
  other arithmetic  8.68 us (6%)
  Pallas kernels  5.34 us (4%)
    ppermute x28, waiting for transfers between devices, flip(): return lax.ppermute(x, names if len(names) > 1 else names[0], pairs)  48.6 us
    ppermute x28, starting transfers between devices, flip(): return lax.ppermute(x, names if len(names) > 1 else names[0], pairs)  21.3 us
    ppermute x6, waiting for transfers between devices, rotate(): return lax.ppermute(x, 'dp', [(i, (i + k) % n_dp) for i in range(n_dp)])  17.8 us
    ppermute x6, starting transfers between devices, rotate(): return lax.ppermute(x, 'dp', [(i, (i + k) % n_dp) for i in range(n_dp)])  11.8 us
    pallas_call x1, Pallas kernels, per_device(): pl.pallas_call(lambda *refs: attend_kernel(*refs, heads=local_heads, mask...  5.34 us
    dynamic_update_slice x14, local copies, waits for them, and re-layouts, place_rows(): whole = lax.dynamic_update_slice(whole, block, (0, row_of(y, k, rows), 0))  4.47 us
  transfers between devices with their start and end apart: 34, of which 17 were waited for; matrix products, arithmetic and copies ran while one was open for 17% of the time, Pallas kernels for 0%

profile of v22, /device:TPU:0, one launch (start us, length us, event | category | flops | bytes accessed | tf_op | source)
XLA Modules:
  0.0 133.8 jit_solution(9379976319984289100)
XLA Ops:
  0.0 2.1 %fusion.13 = (bf16[2,192,512]{2,1,0:T(8,128)(2,1)S(1)}, bf16[2,192,512]{2,1,0:T(8,128)(2,1)}) fusion(s32[]{:T(128)S(6)} %select_n.236, bf16[1,192,1024]{2,1,0:T(8,128)(2,1)} %bitcast.95, bf16[1,192,1024]{2,1,0:T(8,128)(2,1)} %bitcast.96, s32[]{:T(128)S(6)} %select_n.238), kind=kLoop, calls=%fused_computation.29 | loop fusion | flops 1572864 | bytes 1572872 | tf_op jit(solution)/shard_map/stack | solution.py:163
  2.1 4.1 %collective-permute-start.3 = (bf16[2,192,512]{2,1,0:T(8,128)(2,1)S(1)}, bf16[2,192,512]{2,1,0:T(8,128)(2,1)}, u32[]{:S(2)}, u32[]{:S(2)}) collective-permute-start(bf16[2,192,512]{2,1,0:T(8,128)(2,1)S(1)} %get-tuple-element.55), channel_id=1, source_target_pairs={{0,2},{1,3},{2,0},{3,1},{4,6},{5,7},{6,4},{7,5},{8,10},{9,11},{10,... | collective-permute-start | bytes 1179656 | tf_op jit(solution)/shard_map/ppermute | solution.py:101
  6.2 1.5 %collective-permute-start.8 = (bf16[2,192,512]{2,1,0:T(8,128)(2,1)S(1)}, bf16[2,192,512]{2,1,0:T(8,128)(2,1)}, u32[]{:S(2)}, u32[]{:S(2)}) collective-permute-start(bf16[2,192,512]{2,1,0:T(8,128)(2,1)S(1)} %get-tuple-element.55), channel_id=1, source_target_pairs={{0,4},{4,0},{1,5},{5,1},{2,6},{6,2},{3,7},{7,3},{8,12},{12,8},{9,1... | collective-permute-start | bytes 1179656 | tf_op jit(solution)/shard_map/ppermute | solution.py:98
  7.7 1.5 %collective-permute-start.1 = (bf16[512,384]{1,0:T(8,128)(2,1)}, bf16[512,384]{1,0:T(8,128)(2,1)S(1)}, u32[]{:S(2)}, u32[]{:S(2)}) collective-permute-start(bf16[512,384]{1,0:T(8,128)(2,1)} %bitcast.92), channel_id=1, source_target_pairs={{0,16},{8,24},{16,0},{24,8},{1,17},{9,25},{17,1},{25,9},{2,18},{10... | collective-permute-start | bytes 1179656 | tf_op jit(solution)/shard_map/ppermute | solution.py:98
  9.2 1.6 %collective-permute-start = (bf16[512,384]{1,0:T(8,128)(2,1)}, bf16[512,384]{1,0:T(8,128)(2,1)S(1)}, u32[]{:S(2)}, u32[]{:S(2)}) collective-permute-start(bf16[512,384]{1,0:T(8,128)(2,1)} %bitcast.93), channel_id=1, source_target_pairs={{0,1},{1,0},{2,3},{3,2},{4,5},{5,4},{6,7},{7,6},{8,9},{9,8},{10,11... | collective-permute-start | bytes 1179656 | tf_op jit(solution)/shard_map/ppermute | solution.py:98
  10.8 1.8 %dynamic-slice_bitcast_fusion.2 = (bf16[1,192,512]{2,1,0:T(8,128)(2,1)}, bf16[1,192,512]{2,1,0:T(8,128)(2,1)}) fusion(bf16[1024,192]{0,1:T(8,128)(2,1)} %param.16, s32[]{:T(128)S(6)} %select_n.236, s32[]{:T(128)S(6)} %select_n.238), kind=kLoop, calls=%fused_computation.61 | loop fusion | bytes 786440 | tf_op jit(solution)/shard_map/dynamic_slice | solution.py:161
  13.6 13.1 %collective-permute-done = bf16[512,384]{1,0:T(8,128)(2,1)S(1)} collective-permute-done((bf16[512,384]{1,0:T(8,128)(2,1)}, bf16[512,384]{1,0:T(8,128)(2,1)S(1)}, u32[]{:S(2)}, u32[]{:S(2)}) %collective-permute-start) | collective-permute-done | bytes 393248 | tf_op jit(solution)/shard_map/ppermute | solution.py:98
  28.0 7.8 %collective-permute-done.2 = bf16[512,384]{1,0:T(8,128)(2,1)S(1)} collective-permute-done((bf16[512,384]{1,0:T(8,128)(2,1)S(1)}, bf16[512,384]{1,0:T(8,128)(2,1)S(1)}, u32[]{:S(2)}, u32[]{:S(2)}) %collective-permute-start.2) | collective-permute-done | bytes 393248 | tf_op jit(solution)/shard_map/ppermute | solution.py:98
  35.8 1.2 pad_maximum_fusion.1
  37.8 0.9 constant_dynamic-update-slice_fusion.4
  38.8 3.7 %collective-permute-start.14 = (bf16[2,192,512]{2,1,0:T(8,128)(2,1)}, bf16[2,192,512]{2,1,0:T(8,128)(2,1)S(1)}, u32[]{:S(2)}, u32[]{:S(2)}) collective-permute-start(bf16[2,192,512]{2,1,0:T(8,128)(2,1)} %get-tuple-element.24), channel_id=1, source_target_pairs={{0,3},{1,0},{2,1},{3,2},{4,7},{5,4},{6,5},{7,6},{8,11},{9,8},{10,9... | collective-permute-start | bytes 1179656 | tf_op jit(solution)/shard_map/ppermute | solution.py:101
  42.6 1.1 copy.14
  43.7 1.0 collective-permute-start.6
  45.0 1.1 constant_dynamic-update-slice_fusion.11
  46.1 1.0 constant_dynamic-update-slice_fusion.10
  47.1 5.7 %collective-permute-done.9 = bf16[2,192,512]{2,1,0:T(8,128)(2,1)} collective-permute-done((bf16[2,192,512]{2,1,0:T(8,128)(2,1)}, bf16[2,192,512]{2,1,0:T(8,128)(2,1)}, u32[]{:S(2)}, u32[]{:S(2)}) %collective-permute-start.9) | collective-permute-done | bytes 393248 | tf_op jit(solution)/shard_map/ppermute | solution.py:101
  52.8 6.4 %collective-permute-done.14 = bf16[2,192,512]{2,1,0:T(8,128)(2,1)S(1)} collective-permute-done((bf16[2,192,512]{2,1,0:T(8,128)(2,1)}, bf16[2,192,512]{2,1,0:T(8,128)(2,1)S(1)}, u32[]{:S(2)}, u32[]{:S(2)}) %collective-permute-start.14) | collective-permute-done | bytes 393248 | tf_op jit(solution)/shard_map/ppermute | solution.py:101
  59.2 1.0 collective-permute-start.16
  60.2 1.0 constant_dynamic-update-slice_fusion.9
  61.5 1.5 %fusion.51 = (bf16[1024,384]{1,0:T(8,128)(2,1)S(1)}, bf16[1024,384]{1,0:T(8,128)(2,1)S(1)}) fusion(bf16[2048,384]{1,0:T(8,128)(2,1)} %collective-permute-done.5), kind=kLoop, calls=%fused_computation.125 | loop fusion | bytes 3145728 | tf_op jit(solution)/shard_map/split | solution.py:212
  63.7 1.0 fusion.2
  64.7 1.0 fusion.4
  65.7 1.8 %collective-permute-done.10 = bf16[1,192,512]{2,1,0:T(8,128)(2,1)S(1)} collective-permute-done((bf16[1,192,512]{2,1,0:T(8,128)(2,1)}, bf16[1,192,512]{2,1,0:T(8,128)(2,1)S(1)}, u32[]{:S(2)}, u32[]{:S(2)}) %collective-permute-start.10) | collective-permute-done | bytes 196640 | tf_op jit(solution)/shard_map/ppermute | solution.py:101
  67.5 3.8 %collective-permute-start.17 = (bf16[1,192,512]{2,1,0:T(8,128)(2,1)S(1)}, bf16[1,192,512]{2,1,0:T(8,128)(2,1)S(1)}, u32[]{:S(2)}, u32[]{:S(2)}) collective-permute-start(bf16[1,192,512]{2,1,0:T(8,128)(2,1)S(1)} %copy-done.9), channel_id=1, source_target_pairs={{0,3},{1,0},{2,1},{3,2},{4,7},{5,4},{6,5},{7,6},{8,11},{9,8},{10,9... | collective-permute-start | bytes 589832 | tf_op jit(solution)/shard_map/ppermute | solution.py:101
  71.5 1.3 collective-permute-start.18
  72.9 1.1 bitcast_dynamic-update-slice_fusion.4
  74.1 3.1 %collective-permute-done.11 = bf16[1,192,512]{2,1,0:T(8,128)(2,1)S(1)} collective-permute-done((bf16[1,192,512]{2,1,0:T(8,128)(2,1)S(1)}, bf16[1,192,512]{2,1,0:T(8,128)(2,1)S(1)}, u32[]{:S(2)}, u32[]{:S(2)}) %collective-permute-start.11) | collective-permute-done | bytes 196640 | tf_op jit(solution)/shard_map/ppermute | solution.py:101
  77.7 0.8 collective-permute-done.17
  78.5 1.6 %collective-permute-start.19 = (bf16[1,192,512]{2,1,0:T(8,128)(2,1)S(1)}, bf16[1,192,512]{2,1,0:T(8,128)(2,1)S(1)}, u32[]{:S(2)}, u32[]{:S(2)}) collective-permute-start(bf16[1,192,512]{2,1,0:T(8,128)(2,1)S(1)} %collective-permute-done.11), channel_id=1, source_target_pairs={{0,4},{4,0},{1,5},{5,1},{2,6},{6,2},{3,7},{7,3},{8,12},{12,8},{9,1... | collective-permute-start | bytes 589832 | tf_op jit(solution)/shard_map/ppermute | solution.py:98
  81.4 1.8 %fusion.5 = f32[1024,512]{1,0:T(8,128)S(1)} fusion(bf16[1024,1536]{1,0:T(8,128)(2,1)S(1)} %fusion.4, bf16[2,1536,512]{2,1,0:T(8,128)(2,1)S(1)} %constant_dynamic-update-slice_fusion.5), kind=kOutput, calls=%fused_computation.11 | convolution fusion | flops 1610612736 | bytes 6815744 | tf_op jit(solution)/shard_map/dot_general | solution.py:241
  83.2 2.0 %multiply_convert_fusion = bf16[1024,512]{1,0:T(8,128)(2,1)S(1)} fusion(f32[1024,512]{1,0:T(8,128)S(1)} %fusion.5, bf16[1024,1536]{1,0:T(8,128)(2,1)S(1)} %fusion.4, bf16[2,1536,512]{2,1,0:T(8,128)(2,1)S(1)} %constant_dynamic-update-slice_fusion.5), kind=kOutput, calls=%fused_computation.8 | convolution fusion | flops 1613758464 | bytes 7864320 | tf_op jit(solution)/shard_map/dot_general | solution.py:242
  85.2 1.4 %fusion.53 = f32[768,512]{1,0:T(8,128)S(1)} fusion(bf16[1536,768]{1,0:T(8,128)(2,1)S(1)} %constant_dynamic-update-slice_fusion.1, bf16[1536,512]{1,0:T(8,128)(2,1)S(1)} %bitcast_dynamic-update-slice_fusion), kind=kOutput, calls=%fused_computation.127 | convolution fusion | flops 1207959552 | bytes 5505024 | tf_op jit(solution)/shard_map/dot_general | solution.py:247
  87.0 1.7 %collective-permute-done.20 = bf16[1,192,512]{2,1,0:T(8,128)(2,1)S(1)} collective-permute-done((bf16[1,192,512]{2,1,0:T(8,128)(2,1)S(1)}, bf16[1,192,512]{2,1,0:T(8,128)(2,1)S(1)}, u32[]{:S(2)}, u32[]{:S(2)}) %collective-permute-start.20) | collective-permute-done | bytes 196640 | tf_op jit(solution)/shard_map/ppermute | solution.py:98
  90.0 1.6 %fusion.8 = f32[2,2,128,768]{3,2,1,0:T(8,128)S(1)} fusion(bf16[768,512,1,1]{1,0,3,2:T(8,128)(2,1)S(1)} %fusion.6, bf16[2,2,2,128,512]{4,3,2,1,0:T(8,128)(2,1)} %bitcast.98, s32[]{:T(128)S(6)} %select_n.278), kind=kOutput, calls=%fused_computation.24 | convolution fusion | flops 402653184 | bytes 2883588 | tf_op jit(solution)/shard_map/dot_general | solution.py:264
  92.5 1.6 %collective-permute-start.22 = (bf16[128,768]{1,0:T(8,128)(2,1)S(1)}, bf16[128,768]{1,0:T(8,128)(2,1)S(1)}, u32[]{:S(2)}, u32[]{:S(2)}) collective-permute-start(bf16[128,768]{1,0:T(8,128)(2,1)S(1)} %get-tuple-element.57), channel_id=1, source_target_pairs={{0,16},{8,24},{16,0},{24,8},{1,17},{9,25},{17,1},{25,9},{2,18},{10... | collective-permute-start | bytes 589832 | tf_op jit(solution)/shard_map/ppermute | solution.py:98
  94.1 0.9 collective-permute-start.24
  95.0 1.1 collective-permute-start.23
  96.1 7.6 %collective-permute-done.22 = bf16[128,768]{1,0:T(8,128)(2,1)S(1)} collective-permute-done((bf16[128,768]{1,0:T(8,128)(2,1)S(1)}, bf16[128,768]{1,0:T(8,128)(2,1)S(1)}, u32[]{:S(2)}, u32[]{:S(2)}) %collective-permute-start.22) | collective-permute-done | bytes 196640 | tf_op jit(solution)/shard_map/ppermute | solution.py:98
  103.7 1.2 collective-permute-done.23
  105.5 1.6 %collective-permute-start.25 = (bf16[128,768]{1,0:T(8,128)(2,1)S(1)}, bf16[128,768]{1,0:T(8,128)(2,1)S(1)}, u32[]{:S(2)}, u32[]{:S(2)}) collective-permute-start(bf16[128,768]{1,0:T(8,128)(2,1)S(1)} %multiply_convert_fusion.1.refs_0_), channel_id=1, source_target_pairs={{0,16},{8,24},{16,0},{24,8},{1,17},{9,25},{17,1},{25,9},{2,18},{10... | collective-permute-start | bytes 589832 | tf_op jit(solution)/shard_map/ppermute | solution.py:98
  107.1 1.6 %collective-permute-start.28 = (bf16[128,768]{1,0:T(8,128)(2,1)S(1)}, bf16[128,768]{1,0:T(8,128)(2,1)S(1)}, u32[]{:S(2)}, u32[]{:S(2)}) collective-permute-start(bf16[128,768]{1,0:T(8,128)(2,1)S(1)} %multiply_convert_fusion.1.refs_0_), channel_id=1, source_target_pairs={{0,4},{4,0},{1,5},{5,1},{2,6},{6,2},{3,7},{7,3},{8,12},{12,8},{9,1... | collective-permute-start | bytes 589832 | tf_op jit(solution)/shard_map/ppermute | solution.py:98
  109.1 4.2 %collective-permute-done.25.refs_1_ = bf16[128,768]{1,0:T(8,128)(2,1)S(1)} collective-permute-done((bf16[128,768]{1,0:T(8,128)(2,1)S(1)}, bf16[128,768]{1,0:T(8,128)(2,1)S(1)}, u32[]{:S(2)}, u32[]{:S(2)}) %collective-permute-start.25) | collective-permute-done | bytes 196640 | tf_op jit(solution)/shard_map/ppermute | solution.py:98
  113.2 3.7 %collective-permute-done.28.refs_4_ = bf16[128,768]{1,0:T(8,128)(2,1)S(1)} collective-permute-done((bf16[128,768]{1,0:T(8,128)(2,1)S(1)}, bf16[128,768]{1,0:T(8,128)(2,1)S(1)}, u32[]{:S(2)}, u32[]{:S(2)}) %collective-permute-start.28) | collective-permute-done | bytes 196640 | tf_op jit(solution)/shard_map/ppermute | solution.py:98
  117.5 0.9 collective-permute-done.30.refs_6_
  118.7 5.3 %shard_map.118 = (f32[2,192,512]{2,1,0:T(8,128)S(1)}, bf16[2,192,512]{2,1,0:T(8,128)(2,1)S(1)}) custom-call(bf16[128,768]{1,0:T(8,128)(2,1)S(1)} %multiply_convert_fusion.1.refs_0_, bf16[128,768]{1,0:T(8,128)(2,1)S(1)} %collective-permute-done.25.refs_1_, bf16[128,768]{1,0:T(8,128)(2,1)S(1)} %collective-permute-done.26.refs_2_, ...), custom_call_target="tpu_custom_call" | custom-call | flops 2516582400 | bytes 8388608 | tf_op jit(solution)/shard_map/pallas_call | solution.py:302
  124.3 1.5 %collective-permute-done.32 = bf16[2,192,512]{2,1,0:T(8,128)(2,1)S(1)} collective-permute-done((bf16[2,192,512]{2,1,0:T(8,128)(2,1)S(1)}, bf16[2,192,512]{2,1,0:T(8,128)(2,1)S(1)}, u32[]{:S(2)}, u32[]{:S(2)}) %collective-permute-start.32) | collective-permute-done | bytes 393248 | tf_op jit(solution)/shard_map/ppermute | solution.py:98
  126.0 1.0 collective-permute-start.33
  127.0 6.1 %collective-permute-done.33 = bf16[192,512]{1,0:T(8,128)(2,1)S(1)} collective-permute-done((bf16[192,512]{1,0:T(8,128)(2,1)S(1)}, bf16[192,512]{1,0:T(8,128)(2,1)S(1)}, u32[]{:S(2)}, u32[]{:S(2)}) %collective-permute-start.33) | collective-permute-done | bytes 196640 | tf_op jit(solution)/shard_map/ppermute | solution.py:98
  (128 shorter events, 11.7 us)
Async XLA Ops:
  0.0 35.8 %copy-start.4 = (bf16[1,512,384]{2,1,0:T(8,128)(2,1)S(1)}, bf16[1,512,384]{2,1,0:T(8,128)(2,1)}, u32[]{:S(2)}) copy-start(bf16[1,512,384]{2,1,0:T(8,128)(2,1)} %param.12) | copy-start | bytes 1179652
  0.0 13.1 %copy-start.10 = (f32[1536]{0:T(1024)S(1)}, f32[1536]{0:T(1024)}, u32[]{:S(2)}) copy-start(f32[1536]{0:T(1024)} %param.13) | copy-start | bytes 18436
  0.0 13.3 %copy-start.14 = (s32[1,3]{1,0:T(1,128)S(1)}, s32[1,3]{1,0:T(1,128)}, u32[]{:S(2)}) copy-start(s32[1,3]{1,0:T(1,128)} %param.21) | copy-start | bytes 40
  0.0 13.4 %copy-start.12 = (s32[4]{0:T(128)S(1)}, s32[4]{0:T(128)}, u32[]{:S(2)}) copy-start(s32[4]{0:T(128)} %param.22) | copy-start | bytes 52
  0.0 27.3 %copy-start.13 = (s32[4]{0:T(128)S(1)}, s32[4]{0:T(128)}, u32[]{:S(2)}) copy-start(s32[4]{0:T(128)} %param.23) | copy-start | bytes 52
  2.1 35.7 %copy-start.3 = (bf16[384,768]{1,0:T(8,128)(2,1)S(1)}, bf16[384,768]{1,0:T(8,128)(2,1)}, u32[]{:S(2)}) copy-start(bf16[384,768]{1,0:T(8,128)(2,1)} %param.17) | copy-start | bytes 1769476
  2.1 25.3 %collective-permute-start.3 = (bf16[2,192,512]{2,1,0:T(8,128)(2,1)S(1)}, bf16[2,192,512]{2,1,0:T(8,128)(2,1)}, u32[]{:S(2)}, u32[]{:S(2)}) collective-permute-start(bf16[2,192,512]{2,1,0:T(8,128)(2,1)S(1)} %get-tuple-element.55), channel_id=1, source_target_pairs={{0,2},{1,3},{2,0},{3,1},{4,6},{5,7},{6,4},{7,5},{8,10},{9,11},{10,... | collective-permute-start | bytes 1179656 | tf_op jit(solution)/shard_map/ppermute | solution.py:101
  6.2 32.5 %collective-permute-start.8 = (bf16[2,192,512]{2,1,0:T(8,128)(2,1)S(1)}, bf16[2,192,512]{2,1,0:T(8,128)(2,1)}, u32[]{:S(2)}, u32[]{:S(2)}) collective-permute-start(bf16[2,192,512]{2,1,0:T(8,128)(2,1)S(1)} %get-tuple-element.55), channel_id=1, source_target_pairs={{0,4},{4,0},{1,5},{5,1},{2,6},{6,2},{3,7},{7,3},{8,12},{12,8},{9,1... | collective-permute-start | bytes 1179656 | tf_op jit(solution)/shard_map/ppermute | solution.py:98
  7.7 20.3 %collective-permute-start.1 = (bf16[512,384]{1,0:T(8,128)(2,1)}, bf16[512,384]{1,0:T(8,128)(2,1)S(1)}, u32[]{:S(2)}, u32[]{:S(2)}) collective-permute-start(bf16[512,384]{1,0:T(8,128)(2,1)} %bitcast.92), channel_id=1, source_target_pairs={{0,16},{8,24},{16,0},{24,8},{1,17},{9,25},{17,1},{25,9},{2,18},{10... | collective-permute-start | bytes 1179656 | tf_op jit(solution)/shard_map/ppermute | solution.py:98
  9.2 17.5 %collective-permute-start = (bf16[512,384]{1,0:T(8,128)(2,1)}, bf16[512,384]{1,0:T(8,128)(2,1)S(1)}, u32[]{:S(2)}, u32[]{:S(2)}) collective-permute-start(bf16[512,384]{1,0:T(8,128)(2,1)} %bitcast.93), channel_id=1, source_target_pairs={{0,1},{1,0},{2,3},{3,2},{4,5},{5,4},{6,7},{7,6},{8,9},{9,8},{10,11... | collective-permute-start | bytes 1179656 | tf_op jit(solution)/shard_map/ppermute | solution.py:98
  12.6 26.1 %collective-permute-start.7 = (bf16[1,192,512]{2,1,0:T(8,128)(2,1)}, bf16[1,192,512]{2,1,0:T(8,128)(2,1)}, u32[]{:S(2)}, u32[]{:S(2)}) collective-permute-start(bf16[1,192,512]{2,1,0:T(8,128)(2,1)} %get-tuple-element.25), channel_id=1, source_target_pairs={{0,4},{4,0},{1,5},{5,1},{2,6},{6,2},{3,7},{7,3},{8,12},{12,8},{9,1... | collective-permute-start | bytes 589832 | tf_op jit(solution)/shard_map/ppermute | solution.py:98
  26.7 9.1 %collective-permute-start.2 = (bf16[512,384]{1,0:T(8,128)(2,1)S(1)}, bf16[512,384]{1,0:T(8,128)(2,1)S(1)}, u32[]{:S(2)}, u32[]{:S(2)}) collective-permute-start(bf16[512,384]{1,0:T(8,128)(2,1)S(1)} %collective-permute-done), channel_id=1, source_target_pairs={{0,16},{8,24},{16,0},{24,8},{1,17},{9,25},{17,1},{25,9},{2,18},{10... | collective-permute-start | bytes 1179656 | tf_op jit(solution)/shard_map/ppermute | solution.py:98
  27.4 9.5 %collective-permute-start.4 = (bf16[2,192,512]{2,1,0:T(8,128)(2,1)}, bf16[2,192,512]{2,1,0:T(8,128)(2,1)S(1)}, u32[]{:S(2)}, u32[]{:S(2)}) collective-permute-start(bf16[2,192,512]{2,1,0:T(8,128)(2,1)} %collective-permute-done.3), channel_id=1, source_target_pairs={{0,4},{4,0},{1,5},{5,1},{2,6},{6,2},{3,7},{7,3},{8,12},{12,8},{9,1... | collective-permute-start | bytes 1179656 | tf_op jit(solution)/shard_map/ppermute | solution.py:98
  36.9 1.7 %copy-start.6 = (bf16[2,192,512]{2,1,0:T(8,128)(2,1)}, bf16[2,192,512]{2,1,0:T(8,128)(2,1)S(1)}, u32[]{:S(2)}) copy-start(bf16[2,192,512]{2,1,0:T(8,128)(2,1)S(1)} %collective-permute-done.4) | copy-start | bytes 1179652
  36.9 24.6 %collective-permute-start.5 = (bf16[2048,384]{1,0:T(8,128)(2,1)S(1)}, bf16[2048,384]{1,0:T(8,128)(2,1)}, u32[]{:S(2)}, u32[]{:S(2)}) collective-permute-start(bf16[2048,384]{1,0:T(8,128)(2,1)S(1)} %pad_maximum_fusion.1), channel_id=1, source_target_pairs={{0,8},{8,0},{16,24},{24,16},{1,9},{9,1},{17,25},{25,17},{2,10},{10... | collective-permute-start | bytes 4718600 | tf_op jit(solution)/shard_map/ppermute | solution.py:98
  38.7 14.1 %collective-permute-start.9 = (bf16[2,192,512]{2,1,0:T(8,128)(2,1)}, bf16[2,192,512]{2,1,0:T(8,128)(2,1)}, u32[]{:S(2)}, u32[]{:S(2)}) collective-permute-start(bf16[2,192,512]{2,1,0:T(8,128)(2,1)} %get-tuple-element.24), channel_id=1, source_target_pairs={{0,1},{1,2},{2,3},{3,0},{4,5},{5,6},{6,7},{7,4},{8,9},{9,10},{10,1... | collective-permute-start | bytes 1179656 | tf_op jit(solution)/shard_map/ppermute | solution.py:101
  38.8 20.4 %collective-permute-start.14 = (bf16[2,192,512]{2,1,0:T(8,128)(2,1)}, bf16[2,192,512]{2,1,0:T(8,128)(2,1)S(1)}, u32[]{:S(2)}, u32[]{:S(2)}) collective-permute-start(bf16[2,192,512]{2,1,0:T(8,128)(2,1)} %get-tuple-element.24), channel_id=1, source_target_pairs={{0,3},{1,0},{2,1},{3,2},{4,7},{5,4},{6,5},{7,6},{8,11},{9,8},{10,9... | collective-permute-start | bytes 1179656 | tf_op jit(solution)/shard_map/ppermute | solution.py:101
  43.7 30.3 %collective-permute-start.6 = (bf16[384,768]{1,0:T(8,128)(2,1)S(1)}, bf16[384,768]{1,0:T(8,128)(2,1)S(1)}, u32[]{:S(2)}, u32[]{:S(2)}) collective-permute-start(bf16[384,768]{1,0:T(8,128)(2,1)S(1)} %copy-done.3), channel_id=1, source_target_pairs={{0,16},{8,24},{16,0},{24,8},{1,17},{9,25},{17,1},{25,9},{2,18},{10... | collective-permute-start | bytes 1769480 | tf_op jit(solution)/shard_map/ppermute | solution.py:98
  44.9 16.4 %copy-start.7 = (bf16[2,192,512]{2,1,0:T(8,128)(2,1)S(1)}, bf16[2,192,512]{2,1,0:T(8,128)(2,1)}, u32[]{:S(2)}) copy-start(bf16[2,192,512]{2,1,0:T(8,128)(2,1)} %copy-done.6) | copy-start | bytes 1179652
  52.8 14.7 %collective-permute-start.10 = (bf16[1,192,512]{2,1,0:T(8,128)(2,1)}, bf16[1,192,512]{2,1,0:T(8,128)(2,1)S(1)}, u32[]{:S(2)}, u32[]{:S(2)}) collective-permute-start(bf16[1,192,512]{2,1,0:T(8,128)(2,1)} %get-tuple-element.25), channel_id=1, source_target_pairs={{0,2},{1,3},{2,0},{3,1},{4,6},{5,7},{6,4},{7,5},{8,10},{9,11},{10,... | collective-permute-start | bytes 589832 | tf_op jit(solution)/shard_map/ppermute | solution.py:101
  52.8 18.7 %collective-permute-start.15 = (bf16[2,192,512]{2,1,0:T(8,128)(2,1)}, bf16[2,192,512]{2,1,0:T(8,128)(2,1)S(1)}, u32[]{:S(2)}, u32[]{:S(2)}) collective-permute-start(bf16[2,192,512]{2,1,0:T(8,128)(2,1)} %collective-permute-done.9), channel_id=1, source_target_pairs={{0,4},{4,0},{1,5},{5,1},{2,6},{6,2},{3,7},{7,3},{8,12},{12,8},{9,1... | collective-permute-start | bytes 1179656 | tf_op jit(solution)/shard_map/ppermute | solution.py:98
  59.2 20.9 %collective-permute-start.16 = (bf16[2,192,512]{2,1,0:T(8,128)(2,1)S(1)}, bf16[2,192,512]{2,1,0:T(8,128)(2,1)S(1)}, u32[]{:S(2)}, u32[]{:S(2)}) collective-permute-start(bf16[2,192,512]{2,1,0:T(8,128)(2,1)S(1)} %collective-permute-done.14), channel_id=1, source_target_pairs={{0,4},{4,0},{1,5},{5,1},{2,6},{6,2},{3,7},{7,3},{8,12},{12,8},{9,1... | collective-permute-start | bytes 1179656 | tf_op jit(solution)/shard_map/ppermute | solution.py:98
  64.7 2.8 %copy-start.9 = (bf16[1,192,512]{2,1,0:T(8,128)(2,1)S(1)}, bf16[1,192,512]{2,1,0:T(8,128)(2,1)}, u32[]{:S(2)}) copy-start(bf16[1,192,512]{2,1,0:T(8,128)(2,1)} %get-tuple-element.27) | copy-start | bytes 589828
  67.5 5.3 %copy-start.2 = (bf16[1024,192]{0,1:T(8,128)(2,1)S(1)}, bf16[1024,192]{0,1:T(8,128)(2,1)}, u32[]{:S(2)}) copy-start(bf16[1024,192]{0,1:T(8,128)(2,1)} %param.16) | copy-start | bytes 1179652
  67.5 9.6 %collective-permute-start.11 = (bf16[1,192,512]{2,1,0:T(8,128)(2,1)S(1)}, bf16[1,192,512]{2,1,0:T(8,128)(2,1)S(1)}, u32[]{:S(2)}, u32[]{:S(2)}) collective-permute-start(bf16[1,192,512]{2,1,0:T(8,128)(2,1)S(1)} %copy-done.9), channel_id=1, source_target_pairs={{0,1},{1,2},{2,3},{3,0},{4,5},{5,6},{6,7},{7,4},{8,9},{9,10},{10,1... | collective-permute-start | bytes 589832 | tf_op jit(solution)/shard_map/ppermute | solution.py:101
  67.5 11.0 %collective-permute-start.17 = (bf16[1,192,512]{2,1,0:T(8,128)(2,1)S(1)}, bf16[1,192,512]{2,1,0:T(8,128)(2,1)S(1)}, u32[]{:S(2)}, u32[]{:S(2)}) collective-permute-start(bf16[1,192,512]{2,1,0:T(8,128)(2,1)S(1)} %copy-done.9), channel_id=1, source_target_pairs={{0,3},{1,0},{2,1},{3,2},{4,7},{5,4},{6,5},{7,6},{8,11},{9,8},{10,9... | collective-permute-start | bytes 589832 | tf_op jit(solution)/shard_map/ppermute | solution.py:101
  71.5 9.2 %collective-permute-start.18 = (bf16[1,192,512]{2,1,0:T(8,128)(2,1)S(1)}, bf16[1,192,512]{2,1,0:T(8,128)(2,1)S(1)}, u32[]{:S(2)}, u32[]{:S(2)}) collective-permute-start(bf16[1,192,512]{2,1,0:T(8,128)(2,1)S(1)} %collective-permute-done.10), channel_id=1, source_target_pairs={{0,4},{4,0},{1,5},{5,1},{2,6},{6,2},{3,7},{7,3},{8,12},{12,8},{9,1... | collective-permute-start | bytes 589832 | tf_op jit(solution)/shard_map/ppermute | solution.py:98
  72.9 7.9 %copy-start.1 = (bf16[1536,768]{1,0:T(8,128)(2,1)S(1)}, bf16[1536,768]{1,0:T(8,128)(2,1)}, u32[]{:S(2)}) copy-start(bf16[1536,768]{1,0:T(8,128)(2,1)} %constant_dynamic-update-slice_fusion.4) | copy-start | bytes 7077892
  77.1 3.6 %collective-permute-start.12 = (bf16[384,768]{1,0:T(8,128)(2,1)S(1)}, bf16[384,768]{1,0:T(8,128)(2,1)S(1)}, u32[]{:S(2)}, u32[]{:S(2)}) collective-permute-start(bf16[384,768]{1,0:T(8,128)(2,1)S(1)} %copy-done.3), channel_id=1, source_target_pairs={{0,8},{8,0},{16,24},{24,16},{1,9},{9,1},{17,25},{25,17},{2,10},{10... | collective-permute-start | bytes 1769480 | tf_op jit(solution)/shard_map/ppermute | solution.py:98
  77.1 3.7 %collective-permute-start.13 = (bf16[384,768]{1,0:T(8,128)(2,1)S(1)}, bf16[384,768]{1,0:T(8,128)(2,1)S(1)}, u32[]{:S(2)}, u32[]{:S(2)}) collective-permute-start(bf16[384,768]{1,0:T(8,128)(2,1)S(1)} %collective-permute-done.6), channel_id=1, source_target_pairs={{0,8},{8,0},{16,24},{24,16},{1,9},{9,1},{17,25},{25,17},{2,10},{10... | collective-permute-start | bytes 1769480 | tf_op jit(solution)/shard_map/ppermute | solution.py:98
  78.5 8.1 %collective-permute-start.19 = (bf16[1,192,512]{2,1,0:T(8,128)(2,1)S(1)}, bf16[1,192,512]{2,1,0:T(8,128)(2,1)S(1)}, u32[]{:S(2)}, u32[]{:S(2)}) collective-permute-start(bf16[1,192,512]{2,1,0:T(8,128)(2,1)S(1)} %collective-permute-done.11), channel_id=1, source_target_pairs={{0,4},{4,0},{1,5},{5,1},{2,6},{6,2},{3,7},{7,3},{8,12},{12,8},{9,1... | collective-permute-start | bytes 589832 | tf_op jit(solution)/shard_map/ppermute | solution.py:98
  80.1 8.7 %collective-permute-start.20 = (bf16[1,192,512]{2,1,0:T(8,128)(2,1)S(1)}, bf16[1,192,512]{2,1,0:T(8,128)(2,1)S(1)}, u32[]{:S(2)}, u32[]{:S(2)}) collective-permute-start(bf16[1,192,512]{2,1,0:T(8,128)(2,1)S(1)} %collective-permute-done.17), channel_id=1, source_target_pairs={{0,4},{4,0},{1,5},{5,1},{2,6},{6,2},{3,7},{7,3},{8,12},{12,8},{9,1... | collective-permute-start | bytes 589832 | tf_op jit(solution)/shard_map/ppermute | solution.py:98
  85.2 4.0 %copy-start.8 = (bf16[1024,512]{1,0:T(8,128)(2,1)}, bf16[1024,512]{1,0:T(8,128)(2,1)S(1)}, u32[]{:S(2)}) copy-start(bf16[1024,512]{1,0:T(8,128)(2,1)S(1)} %multiply_convert_fusion) | copy-start | bytes 3145732
  89.8 2.4 %collective-permute-start.21 = (bf16[2,2,128,768]{3,2,1,0:T(8,128)(2,1)S(1)}, bf16[2,2,128,768]{3,2,1,0:T(8,128)(2,1)S(1)}, u32[]{:S(2)}, u32[]{:S(2)}) collective-permute-start(bf16[2,2,128,768]{3,2,1,0:T(8,128)(2,1)S(1)} %convolution_convert_fusion), channel_id=1, source_target_pairs={{0,8},{8,0},{16,24},{24,16},{1,9},{9,1},{17,25},{25,17},{2,10},{10... | collective-permute-start | bytes 2359304 | tf_op jit(solution)/shard_map/ppermute | solution.py:98
  92.4 13.0 %copy-start.11 = (f32[768]{0:T(1024)S(1)}, f32[768]{0:T(1024)}, u32[]{:S(2)}) copy-start(f32[768]{0:T(1024)} %param.18) | copy-start | bytes 9220
  92.4 26.3 %copy-start = (bf16[3,768,192]{1,2,0:T(8,128)(2,1)S(1)}, bf16[3,768,192]{1,2,0:T(8,128)(2,1)}, u32[]{:S(2)}) copy-start(bf16[3,768,192]{1,2,0:T(8,128)(2,1)} %param.19) | copy-start | bytes 2654212
  92.5 11.2 %collective-permute-start.22 = (bf16[128,768]{1,0:T(8,128)(2,1)S(1)}, bf16[128,768]{1,0:T(8,128)(2,1)S(1)}, u32[]{:S(2)}, u32[]{:S(2)}) collective-permute-start(bf16[128,768]{1,0:T(8,128)(2,1)S(1)} %get-tuple-element.57), channel_id=1, source_target_pairs={{0,16},{8,24},{16,0},{24,8},{1,17},{9,25},{17,1},{25,9},{2,18},{10... | collective-permute-start | bytes 589832 | tf_op jit(solution)/shard_map/ppermute | solution.py:98
  94.1 9.7 %collective-permute-start.24 = (bf16[128,768]{1,0:T(8,128)(2,1)S(1)}, bf16[128,768]{1,0:T(8,128)(2,1)S(1)}, u32[]{:S(2)}, u32[]{:S(2)}) collective-permute-start(bf16[128,768]{1,0:T(8,128)(2,1)S(1)} %get-tuple-element.58), channel_id=1, source_target_pairs={{0,17},{1,16},{2,19},{3,18},{8,25},{9,24},{10,27},{11,26},{16,1},{... | collective-permute-start | bytes 589832 | tf_op jit(solution)/shard_map/ppermute | solution.py:98
  95.0 9.9 %collective-permute-start.23 = (bf16[128,768]{1,0:T(8,128)(2,1)S(1)}, bf16[128,768]{1,0:T(8,128)(2,1)S(1)}, u32[]{:S(2)}, u32[]{:S(2)}) collective-permute-start(bf16[128,768]{1,0:T(8,128)(2,1)S(1)} %fusion.25), channel_id=1, source_target_pairs={{0,1},{1,0},{2,3},{3,2},{4,5},{5,4},{6,7},{7,6},{8,9},{9,8},{10,11... | collective-permute-start | bytes 589832 | tf_op jit(solution)/shard_map/ppermute | solution.py:98
  105.5 7.7 %collective-permute-start.25 = (bf16[128,768]{1,0:T(8,128)(2,1)S(1)}, bf16[128,768]{1,0:T(8,128)(2,1)S(1)}, u32[]{:S(2)}, u32[]{:S(2)}) collective-permute-start(bf16[128,768]{1,0:T(8,128)(2,1)S(1)} %multiply_convert_fusion.1.refs_0_), channel_id=1, source_target_pairs={{0,16},{8,24},{16,0},{24,8},{1,17},{9,25},{17,1},{25,9},{2,18},{10... | collective-permute-start | bytes 589832 | tf_op jit(solution)/shard_map/ppermute | solution.py:98
  107.1 9.9 %collective-permute-start.28 = (bf16[128,768]{1,0:T(8,128)(2,1)S(1)}, bf16[128,768]{1,0:T(8,128)(2,1)S(1)}, u32[]{:S(2)}, u32[]{:S(2)}) collective-permute-start(bf16[128,768]{1,0:T(8,128)(2,1)S(1)} %multiply_convert_fusion.1.refs_0_), channel_id=1, source_target_pairs={{0,4},{4,0},{1,5},{5,1},{2,6},{6,2},{3,7},{7,3},{8,12},{12,8},{9,1... | collective-permute-start | bytes 589832 | tf_op jit(solution)/shard_map/ppermute | solution.py:98
  108.7 8.3 %collective-permute-start.29 = (bf16[128,768]{1,0:T(8,128)(2,1)S(1)}, bf16[128,768]{1,0:T(8,128)(2,1)S(1)}, u32[]{:S(2)}, u32[]{:S(2)}) collective-permute-start(bf16[128,768]{1,0:T(8,128)(2,1)S(1)} %multiply_convert_fusion.1.refs_0_), channel_id=1, source_target_pairs={{0,20},{4,16},{8,28},{12,24},{16,4},{20,0},{24,12},{28,8},{1,21},{... | collective-permute-start | bytes 589832 | tf_op jit(solution)/shard_map/ppermute | solution.py:98
  109.1 8.4 %collective-permute-start.26 = (bf16[128,768]{1,0:T(8,128)(2,1)S(1)}, bf16[128,768]{1,0:T(8,128)(2,1)S(1)}, u32[]{:S(2)}, u32[]{:S(2)}) collective-permute-start(bf16[128,768]{1,0:T(8,128)(2,1)S(1)} %multiply_convert_fusion.1.refs_0_), channel_id=1, source_target_pairs={{0,8},{8,0},{16,24},{24,16},{1,9},{9,1},{17,25},{25,17},{2,10},{10... | collective-permute-start | bytes 589832 | tf_op jit(solution)/shard_map/ppermute | solution.py:98
  113.2 4.2 %collective-permute-start.27 = (bf16[128,768]{1,0:T(8,128)(2,1)S(1)}, bf16[128,768]{1,0:T(8,128)(2,1)S(1)}, u32[]{:S(2)}, u32[]{:S(2)}) collective-permute-start(bf16[128,768]{1,0:T(8,128)(2,1)S(1)} %collective-permute-done.25.refs_1_), channel_id=1, source_target_pairs={{0,8},{8,0},{16,24},{24,16},{1,9},{9,1},{17,25},{25,17},{2,10},{10... | collective-permute-start | bytes 589832 | tf_op jit(solution)/shard_map/ppermute | solution.py:98
  116.9 1.4 %collective-permute-start.30 = (bf16[128,768]{1,0:T(8,128)(2,1)S(1)}, bf16[128,768]{1,0:T(8,128)(2,1)S(1)}, u32[]{:S(2)}, u32[]{:S(2)}) collective-permute-start(bf16[128,768]{1,0:T(8,128)(2,1)S(1)} %collective-permute-done.28.refs_4_), channel_id=1, source_target_pairs={{0,8},{8,0},{16,24},{24,16},{1,9},{9,1},{17,25},{25,17},{2,10},{10... | collective-permute-start | bytes 589832 | tf_op jit(solution)/shard_map/ppermute | solution.py:98
  117.0 1.7 %collective-permute-start.31 = (bf16[128,768]{1,0:T(8,128)(2,1)S(1)}, bf16[128,768]{1,0:T(8,128)(2,1)S(1)}, u32[]{:S(2)}, u32[]{:S(2)}) collective-permute-start(bf16[128,768]{1,0:T(8,128)(2,1)S(1)} %collective-permute-done.29.refs_5_), channel_id=1, source_target_pairs={{0,8},{8,0},{16,24},{24,16},{1,9},{9,1},{17,25},{25,17},{2,10},{10... | collective-permute-start | bytes 589832 | tf_op jit(solution)/shard_map/ppermute | solution.py:98
  124.0 1.8 %collective-permute-start.32 = (bf16[2,192,512]{2,1,0:T(8,128)(2,1)S(1)}, bf16[2,192,512]{2,1,0:T(8,128)(2,1)S(1)}, u32[]{:S(2)}, u32[]{:S(2)}) collective-permute-start(bf16[2,192,512]{2,1,0:T(8,128)(2,1)S(1)} %get-tuple-element.38), channel_id=1, source_target_pairs={{0,8},{8,0},{16,24},{24,16},{1,9},{9,1},{17,25},{25,17},{2,10},{10... | collective-permute-start | bytes 1179656 | tf_op jit(solution)/shard_map/ppermute | solution.py:98
  126.0 7.1 %collective-permute-start.33 = (bf16[192,512]{1,0:T(8,128)(2,1)S(1)}, bf16[192,512]{1,0:T(8,128)(2,1)S(1)}, u32[]{:S(2)}, u32[]{:S(2)}) collective-permute-start(bf16[192,512]{1,0:T(8,128)(2,1)S(1)} %fusion.27), channel_id=1, source_target_pairs={{0,16},{8,24},{16,0},{24,8},{1,17},{9,25},{17,1},{25,9},{2,18},{10... | collective-permute-start | bytes 589832 | tf_op jit(solution)/shard_map/ppermute | solution.py:98
  (1 other events, 1.3 us)
